TPU v7x, 32 devices: a whole 2x2x4 slice. The times are simulated.
32 devices in a mesh: groups: 2 (over x), seq: 8 (over z, y), adapter: 2 (over core).
Axes of the slice: x: 2, y: 2, z: 4, core: 2. Of those that a mesh axis runs over, the one named last changes fastest.
Arguments:
- tokens: bfloat16 [1024, 4608], P(('groups', 'seq', 'adapter')), parts along dimension 0, may hold values from -6 to 6
- shared_up_weight: bfloat16 [4608, 36864], P(None, ('seq', 'adapter')), may hold values from -0.09375 to 0.09375
- adapter_down_factor: float32 [8, 4608, 64], P(('groups', 'adapter'), 'seq'), parts along dimension 0, may hold values from -0.09375 to 0.09375
- adapter_up_factor: float32 [8, 64, 36864], P('groups', None, ('seq', 'adapter')), parts along dimension 0, may hold values from -0.375 to 0.375
- adapter_per_block: int32 [8, 1], P('groups'), parts along dimension 0, may hold values from 0 to 3
- rows_per_block: int32 [8], P('groups'), parts along dimension 0, may hold values from 32 to 128, as said below
Outputs:
- hidden: bfloat16 [1024, 36864], P('groups', ('seq', 'adapter')), parts along dimension 0
There are 2 independent parts, one for each index of `groups`. A program takes and returns all parts, laid end to end along the dimension named above; an argument that names none is the same for every part. Nothing has to cross between parts.
Inputs may be any that keep to these rules, and one draw needn't show every extreme that they name: `adapter_per_block`: every one of the 4 adapters serves one or more blocks. `rows_per_block`: the live rows of a block stand at its start and the rest are padding; some block is full.
All inputs are finite; a program needn't handle non-finite values.
Results may differ from a plain program's by a relative error of at most 0.005.
Values may be sent and summed in bfloat16 or wider, within the bound.
No kernel may reach another device: no remote copies, remote signals or barrier semaphores. Data moves between devices by JAX's collectives and lax.ppermute only.
A program may use at most 128 MiB of HBM per device.

v0:
```python
import jax
import jax.numpy as jnp
from jax import lax
from jax.sharding import PartitionSpec as P

BLOCK = 128


exact_precision = lax.Precision.HIGHEST


def adapter_table(adapter_per_block, adapter_list):
    return (adapter_per_block[:, 0][:, None] == jnp.arange(adapter_list)[None, :]).astype(
        jnp.float32
    )


def row_adapters(row_ids, block_lookup):
    block_of = row_ids // BLOCK
    chosen = (block_of[:, None] == jnp.arange(block_lookup.shape[0])[None, :]).astype(jnp.float32)
    return jnp.dot(chosen, block_lookup, preferred_element_type=jnp.float32)


def partial_reduction(device_rows, segment_offset, width_segment, down_bank, indicator_matrix):
    columns = lax.dynamic_slice_in_dim(device_rows, segment_offset, width_segment, 1).astype(
        jnp.float32
    )
    projected = jnp.einsum("nd,adr->nar", columns, down_bank, precision=exact_precision)
    return jnp.einsum("nar,na->nr", projected, indicator_matrix, precision=exact_precision)


def finalize_output(base_output, rank_reduction, block_lookup, rows_per_block, up_bank):
    total_row_count = base_output.shape[0]
    blocks = total_row_count // BLOCK
    chosen = jnp.einsum("gp,piz->giz", block_lookup, up_bank, precision=exact_precision)
    adapter_update = jnp.einsum(
        "zyd,zdc->zyc", rank_reduction.reshape(blocks, BLOCK, -1), chosen, precision=exact_precision
    )
    adapter_update = adapter_update.reshape(total_row_count, -1)
    position = jnp.arange(total_row_count) % BLOCK
    active_rows = (position < jnp.repeat(rows_per_block, BLOCK)).astype(jnp.float32)
    return ((base_output + adapter_update) * active_rows[:, None]).astype(jnp.bfloat16)


def on_device(
    tokens,
    shared_up_weight,
    adapter_down_factor,
    adapter_up_factor,
    adapter_per_block,
    rows_per_block,
):
    adapter_list = adapter_up_factor.shape[0]
    block_lookup = adapter_table(adapter_per_block, adapter_list)
    width_segment = adapter_down_factor.shape[1]
    segment_offset = lax.axis_index("seq") * width_segment
    ff_local = shared_up_weight.shape[1]
    held_block_count = adapter_down_factor.shape[0]
    first_owned = lax.axis_index("adapter") * held_block_count
    device_rows = lax.all_gather(tokens, ("seq", "adapter"), axis=0, tiled=True)
    row_ids = jnp.arange(device_rows.shape[0])
    indicator_matrix = row_adapters(row_ids, block_lookup)
    held_blocks = lax.dynamic_slice_in_dim(indicator_matrix, first_owned, held_block_count, 1)
    base_output = jnp.dot(device_rows, shared_up_weight, preferred_element_type=jnp.float32)
    partial_output = partial_reduction(
        device_rows, segment_offset, width_segment, adapter_down_factor, held_blocks
    )
    combined = jnp.concatenate([base_output, partial_output], 1)
    rank_reduction = lax.psum(combined[:, ff_local:], ("seq", "adapter"))
    base_output = combined[:, :ff_local]
    return finalize_output(
        base_output, rank_reduction, block_lookup, rows_per_block, adapter_up_factor
    )


def solution(mesh):
    placed = (
        P(("groups", "seq", "adapter"), None),
        P(None, ("seq", "adapter")),
        P(("groups", "adapter"), "seq", None),
        P("groups", None, ("seq", "adapter")),
        P("groups", None),
        P("groups"),
    )
    return jax.shard_map(
        on_device,
        mesh=mesh,
        in_specs=placed,
        out_specs=P("groups", ("seq", "adapter")),
        check_vma=False,
    )
```

profile of v0, /device:TPU:0, one launch (start us, length us, event | category | flops | bytes accessed | tf_op | source)
XLA Modules:
  0.0 188.2 jit_solution(4126563232552571167)
XLA Ops:
  6.5 0.0 copy-start
  6.5 0.0 copy-start.1
  6.5 0.0 all-gather.2.cloned.1.call-start
  6.5 0.7 all-gather.2.cloned.1.call-update
  7.3 0.0 all-reduce.2.cloned.1.call-start
  7.3 0.9 fusion.9
  8.3 0.1 constant_dynamic-slice_fusion
  8.4 0.0 copy-done
  8.4 0.0 copy-start.3
  8.4 5.7 %fusion.4 = f32[4,64,2304]{2,0,1:T(4,128)} fusion(f32[4,64,2304]{2,1,0:T(8,128)S(1)} %copy-done, s32[4]{0:T(128)} %bitcast.30), kind=kOutput, calls=%fused_computation.5 | convolution fusion | flops 28311568 | bytes 4718608 | tf_op jit(solution)/shard_map/gp,piz->giz/dot_general | solution.py:35
  14.1 51.6 %all-gather.2.cloned.1.call-done = bf16[512,4608]{1,0:T(8,128)(2,1)} async-done(((bf16[32,4608]{1,0:T(8,128)(2,1)}), bf16[512,4608]{1,0:T(8,128)(2,1)}) %all-gather.2.cloned.1.call-update) | async-done | bytes 4718608 | tf_op jit(solution)/shard_map/all_gather | solution.py:60
  65.8 0.0 copy-done.1
  65.8 2.0 %fusion.6 = f32[512,2,64]{0,2,1:T(8,128)S(1)} fusion(f32[2,576,64]{1,2,0:T(8,128)S(1)} %copy-done.1, bf16[512,4608]{1,0:T(8,128)(2,1)} %all-gather.2.cloned.1.call-done, s32[]{:T(128)S(6)} %select_n.26), kind=kOutput, calls=%fused_computation.7 | convolution fusion | flops 452984832 | bytes 1212420 | tf_op jit(solution)/shard_map/nd,adr->nar/dot_general | solution.py:28
  67.8 0.2 copy.8
  68.0 4.3 %fusion.25 = f32[512,1,64]{2,1,0:T(1,128)} fusion(f32[512,2,64]{2,1,0:T(2,128)S(1)} %copy.8, f32[512,2,1]{1,2,0:T(1,128)S(1)} %bitcast.28), kind=kOutput, calls=%fused_computation.33 | convolution fusion | flops 786432 | bytes 397312 | tf_op jit(solution)/shard_map/nar,na->nr/dot_general | solution.py:29
  72.4 1.1 copy.10
  73.4 0.7 copy_bitcast_fusion
  74.1 0.0 all-reduce.2.cloned.1.call-update
  74.1 0.0 copy-done.3
  74.1 0.1 fusion.18
  74.2 85.5 %all-reduce.2.cloned.1.call-done = f32[4,128,64]{1,2,0:T(8,128)} async-done(((f32[4,128,64]{1,2,0:T(8,128)}), f32[4,128,64]{1,2,0:T(8,128)}) %all-reduce.2.cloned.1.call-update) | async-done | bytes 131088 | tf_op jit(solution)/shard_map/psum | solution.py:69
  159.7 6.2 %fusion.2 = f32[4,128,2304]{2,1,0:T(8,128)S(1)} fusion(f32[4,128,64]{1,2,0:T(8,128)} %all-reduce.2.cloned.1.call-done, f32[4,64,2304]{2,0,1:T(4,128)} %fusion.4), kind=kOutput, calls=%fused_computation.3 | convolution fusion | flops 905969664 | bytes 7208960 | tf_op jit(solution)/shard_map/zyd,zdc->zyc/dot_general | solution.py:36
  165.9 0.0 copy-done.2
  165.9 15.4 %fusion.1 = bf16[512,2304]{1,0:T(8,128)(2,1)} fusion(f32[512,2304]{1,0:T(8,128)S(1)} %bitcast.27, bf16[512,4608]{1,0:T(8,128)(2,1)S(1)} %copy-done.2, bf16[4608,2304]{1,0:T(8,128)(2,1)} %param.7, f32[512]{0:T(512)S(1)} %fusion.18), kind=kOutput, calls=%fused_computation.2 | convolution fusion | flops 10875174912 | bytes 33032192 | tf_op jit(solution)/shard_map/dot_general | solution.py:64
  (2 shorter events, 0.0 us)
Async XLA Ops:
  6.5 1.9 copy-start
  6.5 59.2 %copy-start.1 = (f32[2,576,64]{1,2,0:T(8,128)S(1)}, f32[2,576,64]{1,2,0:T(8,128)}, u32[]{:S(2)}) copy-start(f32[2,576,64]{1,2,0:T(8,128)} %param.8) | copy-start | bytes 884740
  6.5 59.2 %all-gather.2.cloned.1.call-start = ((), (), s32[]{:S(2)}) async-start(), calls=%async_computation | async-start | bytes 5013504 | tf_op jit(solution)/shard_map/all_gather | solution.py:60
  7.3 152.5 %all-reduce.2.cloned.1.call-start = ((), (), s32[]{:S(2)}) async-start(), calls=%async_computation.1 | async-start | bytes 262144 | tf_op jit(solution)/shard_map/psum | solution.py:69
  8.4 65.7 %copy-start.3 = (s32[4]{0:T(128)S(1)}, s32[4]{0:T(128)}, u32[]{:S(2)}) copy-start(s32[4]{0:T(128)} %param.11) | copy-start | bytes 52
  159.7 6.2 %copy-start.2 = (bf16[512,4608]{1,0:T(8,128)(2,1)S(1)}, bf16[512,4608]{1,0:T(8,128)(2,1)}, u32[]{:S(2)}) copy-start(bf16[512,4608]{1,0:T(8,128)(2,1)} %all-gather.2.cloned.1.call-done) | copy-start | bytes 14155780
Sparse Core Ops, SparseCore 0:
  9.6 56.0 all-gather.1
  74.2 85.4 all-reduce.1
where the time goes:
time: 189 us; the launch traced here: 188 us
  waiting for transfers between devices  138 us (73%)
  matrix products  34.6 us (18%)
  between operations  13.5 us (7%)
  local copies, waits for them, and re-layouts  2.1 us (1%)
    psum x1, waiting for transfers between devices, on_device(): rank_reduction = lax.psum(combined[:, ff_local:], ('seq', 'adapter'))  85.5 us
    all_gather x1, waiting for transfers between devices, on_device(): device_rows = lax.all_gather(tokens, ('seq', 'adapter'), axis=0, tiled=True)  51.6 us
    dot_general x1, matrix products, on_device(): jnp.dot(device_rows, shared_up_weight, preferred_element_type=jnp.float32)  15.4 us
    dot_general x1, matrix products, finalize_output(): jnp.einsum('zyd,zdc->zyc', rank_reduction.reshape(blocks, BLOCK, -1), cho...  6.18 us
    dot_general x1, matrix products, finalize_output(): jnp.einsum('gp,piz->giz', block_lookup, up_bank, precision=exact_precision)  5.71 us
    dot_general x1, matrix products, partial_reduction(): jnp.einsum('nar,na->nr', projected, indicator_matrix, precision=exact_pre...  4.34 us
  transfers between devices with their start and end apart: 2, of which 2 were waited for; matrix products, arithmetic and copies ran while one was open for 4% of the time, Pallas kernels for 0%

commit v1 on v0

v1 whole, which is shorter than its diff:
```python
import functools

import jax
import jax.numpy as jnp
from jax import lax
from jax.experimental import pallas as pl
from jax.experimental.pallas import tpu as pltpu
from jax.sharding import PartitionSpec as P

BLOCK = 128
AXES = ("seq", "adapter")
CHUNKS = 2


def ring_position(s, n):
    z, y = s // 2, s % 2
    return z * (1 - y) + (n - 1 - z) * y


def ring_member(pos, n):
    up = pos < n // 2
    return jnp.where(up, 2 * pos, 2 * (n - 1 - pos) + 1)


def ring_perm(n):
    at = {ring_position(s, n): s for s in range(n)}
    perm = []
    for pos in range(n):
        s = at[pos]
        perm.append((2 * s, 2 * at[(pos + 1) % n]))
        perm.append((2 * s + 1, 2 * at[(pos - 1) % n] + 1))
    return perm


def core_perm(n):
    return [(2 * s + c, 2 * s + 1 - c) for s in range(n) for c in range(2)]


def y_perm(n):
    return [(2 * s + c, 2 * (s ^ 1) + c) for s in range(n) for c in range(2)]


def z_perm(n, shift):
    nz = n // 2
    return [
        (2 * (2 * z + y) + c, 2 * (2 * ((z - shift) % nz) + y) + c)
        for z in range(nz)
        for y in range(2)
        for c in range(2)
    ]


def gather_ring(piece, n):
    ring, swap = ring_perm(n), core_perm(n)
    own, other = [], []
    for step in range(n):
        if step:
            piece = lax.ppermute(piece, AXES, ring)
        own.append(piece)
        other.append(lax.ppermute(piece, AXES, swap))
    return own + other


def piece_rows(n, rows):
    s, c = lax.axis_index("seq"), lax.axis_index("adapter")
    pos = ring_position(s, n)
    step = jnp.arange(n)
    first = []
    for core in (c, 1 - c):
        back = jnp.where(core == 0, pos - step, pos + step)
        first.append((2 * ring_member(jnp.mod(back, n), n) + core) * rows)
    return jnp.concatenate(first).astype(jnp.int32)


def shrink_piece(tokens, down, adapters, n):
    z, y, c = lax.axis_index("seq") // 2, lax.axis_index("seq") % 2, lax.axis_index("adapter")
    nz, rows = n // 2, tokens.shape[0]
    held, width, rank = down.shape
    half = rank // 2
    both = lax.ppermute(tokens, AXES, core_perm(n))
    chip_rows = jnp.where(c == 0, jnp.stack([tokens, both]), jnp.stack([both, tokens])).reshape(2 * rows, -1)
    factor = jnp.swapaxes(down, 1, 2).astype(jnp.bfloat16).reshape(held, 2, half, width)
    mine = lax.dynamic_index_in_dim(factor, c, 1, False)
    theirs = lax.ppermute(lax.dynamic_index_in_dim(factor, 1 - c, 1, False), AXES, core_perm(n))
    every = jnp.where(c == 0, jnp.stack([mine, theirs]), jnp.stack([theirs, mine])).reshape(2 * held, half, width)
    per_block = BLOCK // (2 * rows)
    parts = []
    for shift in range(nz):
        seat = jnp.mod(z - shift, nz)
        pick = lax.dynamic_index_in_dim(every, adapters[2 * seat // per_block], 0, False)
        parts.append(lax.ppermute(pick, AXES, z_perm(n, shift)) if shift else pick)
    mine = jnp.stack(parts)
    theirs = lax.ppermute(mine, AXES, y_perm(n))
    factor = jnp.where(y == 0, jnp.stack([mine, theirs], 1), jnp.stack([theirs, mine], 1))
    turned = lax.dynamic_slice_in_dim(
        jnp.concatenate([chip_rows, chip_rows], 1), z * 2 * width, n * width, 1
    ).reshape(2 * rows, nz, 2, width)
    shrink = jnp.einsum("tzyk,zyrk->tr", turned, factor, preferred_element_type=jnp.float32)
    high = shrink.astype(jnp.bfloat16)
    low = (shrink - high.astype(jnp.float32)).astype(jnp.bfloat16)
    return jnp.concatenate([high[:rows], high[rows:], low[:rows], low[rows:]], 1)


def collect(first, pieces, held, sems):
    copies = []
    for i, piece in enumerate(pieces):
        rows = piece.shape[0]
        place = held.at[pl.ds(pl.multiple_of(first[i], rows), rows), :]
        copies.append(pltpu.make_async_copy(piece, place, sems.at[i]))
    for copy in copies:
        copy.start()
    for copy in copies:
        copy.wait()


def first_kernel(count, first, *refs):
    pieces, (w_ref, out_ref, held, sems) = refs[:count], refs[count:]

    @pl.when(pl.program_id(0) == 0)
    def _():
        collect(first, pieces, held, sems)

    out_ref[...] = jnp.dot(held[...], w_ref[...], preferred_element_type=jnp.float32)


def last_kernel(count, first, adapters, live, *refs):
    pieces, (w_ref, base_ref, up_ref, out_ref, held, shrink, sems) = refs[:count], refs[count:]
    depth, rows = w_ref.shape[0], pieces[0].shape[0]
    half = shrink.shape[1] // 4

    @pl.when(pl.program_id(0) == 0)
    def _():
        collect(first, pieces, held, sems)
        for start in range(0, shrink.shape[0], 2 * rows):
            zero = held[start : start + rows, depth:]
            one = held[start + rows : start + 2 * rows, depth:]
            for core in range(2):
                a, b = core * half, (2 + core) * half
                shrink[start + core * rows : start + (core + 1) * rows, :] = jnp.concatenate(
                    [zero[:, a : a + half], one[:, a : a + half], zero[:, b : b + half], one[:, b : b + half]], 1
                )

    total = base_ref[...] + jnp.dot(held[:, :depth], w_ref[...], preferred_element_type=jnp.float32)
    for block in range(shrink.shape[0] // BLOCK):
        at = slice(block * BLOCK, (block + 1) * BLOCK)
        factor = up_ref[adapters[block]].astype(jnp.bfloat16)
        delta = jnp.dot(shrink[at, :], jnp.concatenate([factor, factor], 0), preferred_element_type=jnp.float32)
        on = lax.broadcasted_iota(jnp.int32, delta.shape, 0) < live[block]
        out_ref[at, :] = jnp.where(on, total[at] + delta, 0.0).astype(out_ref.dtype)


def matmul_first(first, pieces, weight, chunk, columns):
    count, (rows, depth) = len(pieces), pieces[0].shape
    total, width = rows * count, weight.shape[1]
    return pl.pallas_call(
        functools.partial(first_kernel, count),
        out_shape=jax.ShapeDtypeStruct((total, width), jnp.float32),
        grid_spec=pltpu.PrefetchScalarGridSpec(
            num_scalar_prefetch=1,
            grid=(width // columns,),
            in_specs=[pl.BlockSpec(memory_space=pl.ANY)] * count
            + [pl.BlockSpec((depth, columns), lambda j, *_: (chunk, j))],
            out_specs=pl.BlockSpec((total, columns), lambda j, *_: (0, j)),
            scratch_shapes=[pltpu.VMEM((total, depth), jnp.bfloat16), pltpu.SemaphoreType.DMA((count,))],
        ),
        compiler_params=pltpu.CompilerParams(vmem_limit_bytes=40 << 20),
        cost_estimate=pl.CostEstimate(
            flops=2 * total * depth * width, bytes_accessed=2 * depth * width + 4 * total * width, transcendentals=0
        ),
    )(first, *pieces, weight)


def matmul_last(first, adapters, live, pieces, weight, chunk, base, up, columns):
    count, (rows, wide) = len(pieces), pieces[0].shape
    total, width = rows * count, weight.shape[1]
    rank = up.shape[1]
    depth = wide - 2 * rank
    return pl.pallas_call(
        functools.partial(last_kernel, count),
        out_shape=jax.ShapeDtypeStruct((total, width), jnp.bfloat16),
        grid_spec=pltpu.PrefetchScalarGridSpec(
            num_scalar_prefetch=3,
            grid=(width // columns,),
            in_specs=[pl.BlockSpec(memory_space=pl.ANY)] * count
            + [
                pl.BlockSpec((depth, columns), lambda j, *_: (chunk, j)),
                pl.BlockSpec((total, columns), lambda j, *_: (0, j)),
                pl.BlockSpec((up.shape[0], rank, columns), lambda j, *_: (0, 0, j)),
            ],
            out_specs=pl.BlockSpec((total, columns), lambda j, *_: (0, j)),
            scratch_shapes=[
                pltpu.VMEM((total, wide), jnp.bfloat16),
                pltpu.VMEM((total, 2 * rank), jnp.bfloat16),
                pltpu.SemaphoreType.DMA((count,)),
            ],
        ),
        compiler_params=pltpu.CompilerParams(vmem_limit_bytes=40 << 20),
        cost_estimate=pl.CostEstimate(
            flops=2 * total * depth * width, bytes_accessed=2 * depth * width + 6 * total * width, transcendentals=0
        ),
    )(first, adapters, live, *pieces, weight, base, up)


def on_device(n, tokens, weight, down, up, adapter_per_block, rows_per_block):
    rows = tokens.shape[0]
    adapters = adapter_per_block[:, 0]
    columns = 256 if weight.shape[1] % 256 == 0 else weight.shape[1]
    depth = tokens.shape[1] // CHUNKS
    first = piece_rows(n, rows)
    early = gather_ring(tokens[:, :depth], n)
    shrink = shrink_piece(tokens, down, adapters, n)
    late = gather_ring(jnp.concatenate([tokens[:, depth:], shrink], 1), n)
    base = matmul_first(first, early, weight, 0, columns)
    return matmul_last(first, adapters, rows_per_block, late, weight, 1, base, up, columns)


def solution(mesh):
    placed = (
        P(("groups", "seq", "adapter"), None),
        P(None, ("seq", "adapter")),
        P(("groups", "adapter"), "seq", None),
        P("groups", None, ("seq", "adapter")),
        P("groups", None),
        P("groups"),
    )
    return jax.shard_map(
        functools.partial(on_device, mesh.shape["seq"]),
        mesh=mesh,
        in_specs=placed,
        out_specs=P("groups", ("seq", "adapter")),
        check_vma=False,
    )
```

time: 189 us -> 97.1 us (0.51)
  waiting for transfers between devices: 138 us -> 35.3 us
  matrix products: 34.6 us -> 0.33 us
  Pallas kernels: 0 us -> 31.3 us
  starting transfers between devices: 0.04 us -> 18 us
  between operations: 13.5 us -> 7.57 us
    psum x1 -> x0, waiting for transfers between devices: 85.5 us -> none  [on_device(): rank_reduction = lax.psum(combined[:, ff_local:], ('seq', 'adapter'))]
    all_gather x1 -> x0, waiting for transfers between devices: 51.6 us -> none  [on_device(): device_rows = lax.all_gather(tokens, ('seq', 'adapter'), axis=0, tiled=True)]
    ppermute x0 -> x36, waiting for transfers between devices: none -> 35.3 us  [the longest x14 29.5 us: gather_ring(): piece = lax.ppermute(piece, AXES, ring)]
    dot_general x6 -> x1, matrix products: 34.6 us -> 0.33 us  [shrink_piece(): jnp.einsum('tzyk,zyrk->tr', turned, factor, preferred_element_type=jnp.fl...]
    pallas_call x0 -> x2, Pallas kernels: none -> 31.3 us  [the longest x1 16.4 us: matmul_last(): pl.pallas_call(functools.partial(last_kernel, count), out_shape=jax.Shape...]
    ppermute x0 -> x36, starting transfers between devices: none -> 18 us  [the longest x3 6.99 us: shrink_piece(): parts.append(lax.ppermute(pick, AXES, z_perm(n, shift)) if shift else pick)]
  transfers between devices with their start and end apart: 2 -> 36, of which waited for: 2 -> 15; matrix products, arithmetic and copies ran while one was open for 4% -> 3% of each run, Pallas kernels for 0% -> 15%
where the time goes in v1:
time: 97.1 us; the launch traced here: 96.4 us
  waiting for transfers between devices  35.3 us (36%)
  Pallas kernels  31.3 us (32%)
  starting transfers between devices  18 us (19%)
  between operations  7.57 us (8%)
  local copies, waits for them, and re-layouts  2.28 us (2%)
  other arithmetic  1.58 us (2%)
    ppermute x14, waiting for transfers between devices, gather_ring(): piece = lax.ppermute(piece, AXES, ring)  29.5 us
    pallas_call x1, Pallas kernels, matmul_last(): pl.pallas_call(functools.partial(last_kernel, count), out_shape=jax.Shape...  16.4 us
    pallas_call x1, Pallas kernels, matmul_first(): pl.pallas_call(functools.partial(first_kernel, count), out_shape=jax.Shap...  14.9 us
    ppermute x3, starting transfers between devices, shrink_piece(): parts.append(lax.ppermute(pick, AXES, z_perm(n, shift)) if shift else pick)  6.99 us
    ppermute x14, starting transfers between devices, gather_ring(): piece = lax.ppermute(piece, AXES, ring)  4.85 us
    ppermute x16, starting transfers between devices, gather_ring(): other.append(lax.ppermute(piece, AXES, swap))  4.44 us
    ppermute x1, waiting for transfers between devices, shrink_piece(): theirs = lax.ppermute(mine, AXES, y_perm(n))  3.43 us
    ppermute x3, waiting for transfers between devices, shrink_piece(): parts.append(lax.ppermute(pick, AXES, z_perm(n, shift)) if shift else pick)  2.33 us
  transfers between devices with their start and end apart: 36, of which 15 were waited for; matrix products, arithmetic and copies ran while one was open for 3% of the time, Pallas kernels for 15%

profile of v1, /device:TPU:0, one launch (start us, length us, event | category | flops | bytes accessed | tf_op | source)
XLA Modules:
  0.0 96.4 jit_solution(2246998166156578488)
XLA Ops:
  0.0 1.0 %convert_element_type.15 = bf16[2,576,64]{1,2,0:T(8,128)(2,1)S(1)} convert(f32[2,576,64]{1,2,0:T(8,128)} %param.8) | non-fusion elementwise | flops 73728 | bytes 442368 | tf_op jit(solution)/shard_map/convert_element_type | solution.py:82
  1.7 1.4 %constant_dynamic-slice_fusion.4 = (s32[1,1]{0,1:T(1,128)}, s32[1,1]{0,1:T(1,128)}, s32[1,1]{0,1:T(1,128)}, s32[1,1]{0,1:T(1,128)}) fusion(s32[4,1]{0,1:T(1,128)} %param.10, s32[]{:T(128)S(6)} %select_n.162, s32[]{:T(128)S(6)} %select_n.166, s32[]{:T(128)S(6)} %select_n.174, s32[]{:T(128)S(6)} %select_n.170), kind=kLoop, calls=%fused_computation.25 | loop fusion | bytes 48 | tf_op jit(solution)/shard_map/dynamic_slice | solution.py:90
  10.6 3.1 %collective-permute-start.4 = (bf16[32,576]{1,0:T(8,128)(2,1)S(1)}, bf16[32,576]{1,0:T(8,128)(2,1)S(1)}, u32[]{:S(2)}, u32[]{:S(2)}) collective-permute-start(bf16[32,576]{1,0:T(8,128)(2,1)S(1)} %get-tuple-element.12), channel_id=1, source_target_pairs={{0,4},{1,5},{2,6},{3,7},{4,8},{5,9},{6,10},{7,11},{8,12},{9,13},{1... | collective-permute-start | bytes 110600 | tf_op jit(solution)/shard_map/ppermute | solution.py:91
  13.7 2.6 %collective-permute-start.3 = (bf16[32,576]{1,0:T(8,128)(2,1)S(1)}, bf16[32,576]{1,0:T(8,128)(2,1)S(1)}, u32[]{:S(2)}, u32[]{:S(2)}) collective-permute-start(bf16[32,576]{1,0:T(8,128)(2,1)S(1)} %get-tuple-element.13), channel_id=1, source_target_pairs={{0,8},{1,9},{2,10},{3,11},{4,12},{5,13},{6,14},{7,15},{8,0},{9,1},... | collective-permute-start | bytes 110600 | tf_op jit(solution)/shard_map/ppermute | solution.py:91
  16.3 1.3 %collective-permute-start.2 = (bf16[32,576]{1,0:T(8,128)(2,1)S(1)}, bf16[32,576]{1,0:T(8,128)(2,1)S(1)}, u32[]{:S(2)}, u32[]{:S(2)}) collective-permute-start(bf16[32,576]{1,0:T(8,128)(2,1)S(1)} %get-tuple-element.14), channel_id=1, source_target_pairs={{0,12},{1,13},{2,14},{3,15},{4,0},{5,1},{6,2},{7,3},{8,4},{9,5},{1... | collective-permute-start | bytes 110600 | tf_op jit(solution)/shard_map/ppermute | solution.py:91
  18.4 1.3 %collective-permute-done.3 = bf16[32,576]{1,0:T(8,128)(2,1)S(1)} collective-permute-done((bf16[32,576]{1,0:T(8,128)(2,1)S(1)}, bf16[32,576]{1,0:T(8,128)(2,1)S(1)}, u32[]{:S(2)}, u32[]{:S(2)}) %collective-permute-start.3) | collective-permute-done | bytes 36896 | tf_op jit(solution)/shard_map/ppermute | solution.py:91
  19.7 1.0 %collective-permute-done.2 = bf16[32,576]{1,0:T(8,128)(2,1)S(1)} collective-permute-done((bf16[32,576]{1,0:T(8,128)(2,1)S(1)}, bf16[32,576]{1,0:T(8,128)(2,1)S(1)}, u32[]{:S(2)}, u32[]{:S(2)}) %collective-permute-start.2) | collective-permute-done | bytes 36896 | tf_op jit(solution)/shard_map/ppermute | solution.py:91
  20.7 1.1 %collective-permute-start.5 = (bf16[4,32,576]{2,1,0:T(8,128)(2,1)S(1)}, bf16[4,32,576]{2,1,0:T(8,128)(2,1)S(1)}, u32[]{:S(2)}, u32[]{:S(2)}) collective-permute-start(bf16[4,32,576]{2,1,0:T(8,128)(2,1)S(1)} %get-tuple-element.10), channel_id=1, source_target_pairs={{0,2},{1,3},{2,0},{3,1},{4,6},{5,7},{6,4},{7,5},{8,10},{9,11},{10,... | collective-permute-start | bytes 442376 | tf_op jit(solution)/shard_map/ppermute | solution.py:93
  22.9 3.4 %collective-permute-done.5 = bf16[4,32,576]{2,1,0:T(8,128)(2,1)S(1)} collective-permute-done((bf16[4,32,576]{2,1,0:T(8,128)(2,1)S(1)}, bf16[4,32,576]{2,1,0:T(8,128)(2,1)S(1)}, u32[]{:S(2)}, u32[]{:S(2)}) %collective-permute-start.5) | collective-permute-done | bytes 147488 | tf_op jit(solution)/shard_map/ppermute | solution.py:93
  27.1 0.9 collective-permute-start.22
  28.0 4.1 %collective-permute-done.6.refs_1_ = bf16[32,2432]{1,0:T(8,128)(2,1)S(1)} collective-permute-done((bf16[32,2432]{1,0:T(8,128)(2,1)S(1)}, bf16[32,2432]{1,0:T(8,128)(2,1)S(1)}, u32[]{:S(2)}, u32[]{:S(2)}) %collective-permute-start.6) | collective-permute-done | bytes 155680 | tf_op jit(solution)/shard_map/ppermute | solution.py:58
  32.3 1.3 %collective-permute-done.22.refs_2_ = bf16[32,2304]{1,0:T(8,128)(2,1)S(1)} collective-permute-done((bf16[32,2304]{1,0:T(8,128)(2,1)S(1)}, bf16[32,2304]{1,0:T(8,128)(2,1)S(1)}, u32[]{:S(2)}, u32[]{:S(2)}) %collective-permute-start.22) | collective-permute-done | bytes 147488 | tf_op jit(solution)/shard_map/ppermute | solution.py:58
  33.9 3.4 %collective-permute-done.7.refs_2_ = bf16[32,2432]{1,0:T(8,128)(2,1)S(1)} collective-permute-done((bf16[32,2432]{1,0:T(8,128)(2,1)S(1)}, bf16[32,2432]{1,0:T(8,128)(2,1)S(1)}, u32[]{:S(2)}, u32[]{:S(2)}) %collective-permute-start.7) | collective-permute-done | bytes 155680 | tf_op jit(solution)/shard_map/ppermute | solution.py:58
  37.6 1.3 %collective-permute-done.23.refs_3_ = bf16[32,2304]{1,0:T(8,128)(2,1)S(1)} collective-permute-done((bf16[32,2304]{1,0:T(8,128)(2,1)S(1)}, bf16[32,2304]{1,0:T(8,128)(2,1)S(1)}, u32[]{:S(2)}, u32[]{:S(2)}) %collective-permute-start.23) | collective-permute-done | bytes 147488 | tf_op jit(solution)/shard_map/ppermute | solution.py:58
  39.1 3.4 %collective-permute-done.8.refs_3_ = bf16[32,2432]{1,0:T(8,128)(2,1)S(1)} collective-permute-done((bf16[32,2432]{1,0:T(8,128)(2,1)S(1)}, bf16[32,2432]{1,0:T(8,128)(2,1)S(1)}, u32[]{:S(2)}, u32[]{:S(2)}) %collective-permute-start.8) | collective-permute-done | bytes 155680 | tf_op jit(solution)/shard_map/ppermute | solution.py:58
  42.8 1.3 %collective-permute-done.24.refs_4_ = bf16[32,2304]{1,0:T(8,128)(2,1)S(1)} collective-permute-done((bf16[32,2304]{1,0:T(8,128)(2,1)S(1)}, bf16[32,2304]{1,0:T(8,128)(2,1)S(1)}, u32[]{:S(2)}, u32[]{:S(2)}) %collective-permute-start.24) | collective-permute-done | bytes 147488 | tf_op jit(solution)/shard_map/ppermute | solution.py:58
  44.4 3.4 %collective-permute-done.9.refs_4_ = bf16[32,2432]{1,0:T(8,128)(2,1)S(1)} collective-permute-done((bf16[32,2432]{1,0:T(8,128)(2,1)S(1)}, bf16[32,2432]{1,0:T(8,128)(2,1)S(1)}, u32[]{:S(2)}, u32[]{:S(2)}) %collective-permute-start.9) | collective-permute-done | bytes 155680 | tf_op jit(solution)/shard_map/ppermute | solution.py:58
  49.6 0.9 collective-permute-start.14
  50.5 2.5 %collective-permute-done.10.refs_5_ = bf16[32,2432]{1,0:T(8,128)(2,1)S(1)} collective-permute-done((bf16[32,2432]{1,0:T(8,128)(2,1)S(1)}, bf16[32,2432]{1,0:T(8,128)(2,1)S(1)}, u32[]{:S(2)}, u32[]{:S(2)}) %collective-permute-start.10) | collective-permute-done | bytes 155680 | tf_op jit(solution)/shard_map/ppermute | solution.py:58
  55.8 4.0 %collective-permute-done.27.refs_7_ = bf16[32,2304]{1,0:T(8,128)(2,1)S(1)} collective-permute-done((bf16[32,2304]{1,0:T(8,128)(2,1)S(1)}, bf16[32,2304]{1,0:T(8,128)(2,1)S(1)}, u32[]{:S(2)}, u32[]{:S(2)}) %collective-permute-start.27) | collective-permute-done | bytes 147488 | tf_op jit(solution)/shard_map/ppermute | solution.py:58
  60.2 0.9 collective-permute-start.16
  61.7 3.4 %collective-permute-done.12.refs_7_ = bf16[32,2432]{1,0:T(8,128)(2,1)S(1)} collective-permute-done((bf16[32,2432]{1,0:T(8,128)(2,1)S(1)}, bf16[32,2432]{1,0:T(8,128)(2,1)S(1)}, u32[]{:S(2)}, u32[]{:S(2)}) %collective-permute-start.12) | collective-permute-done | bytes 155680 | tf_op jit(solution)/shard_map/ppermute | solution.py:58
  65.0 14.9 %shard_map.64.refs_17_ = f32[512,2304]{1,0:T(8,128)S(1)} custom-call(s32[16]{0:T(128)S(1)} %pad_add_fusion.first, bf16[32,2304]{1,0:T(8,128)(2,1)S(1)} %get-tuple-element.7.refs_0_, bf16[32,2304]{1,0:T(8,128)(2,1)S(1)} %collective-permute-done.21.refs_1_, bf16[32,2304]{1,0:T(8,128)(2,1)S(1)} %collective-permute-done.22.refs_2_, ...), custom_call_target="tpu_custom_call" | custom-call | flops 5435817984 | bytes 15335424 | tf_op jit(solution)/shard_map/pallas_call | solution.py:155
  80.0 16.4 %shard_map.65 = bf16[512,2304]{1,0:T(8,128)(2,1)} custom-call(s32[16]{0:T(128)S(1)} %pad_add_fusion.first, s32[4]{0:T(128)S(1)} %bitcast.33, s32[4]{0:T(128)S(1)} %copy-done.2, bf16[32,2432]{1,0:T(8,128)(2,1)S(1)} %concatenate.11.refs_0_, bf16[32,2432]{1,0:T(8,128)(2,1)S(1)} %collective-permute-done.6.refs_1_, ...), custom_call_target="tpu_custom_call" | custom-call | flops 5435817984 | bytes 17694720 | tf_op jit(solution)/shard_map/pallas_call | solution.py:178
  (73 shorter events, 10.5 us)
Async XLA Ops:
  1.1 9.4 %collective-permute-start.1 = (bf16[2,32,576]{2,1,0:T(8,128)(2,1)S(1)}, bf16[2,32,576]{2,1,0:T(8,128)(2,1)S(1)}, u32[]{:S(2)}, u32[]{:S(2)}) collective-permute-start(bf16[2,32,576]{2,1,0:T(8,128)(2,1)S(1)} %get-tuple-element.16), channel_id=1, source_target_pairs={{0,1},{1,0},{2,3},{3,2},{4,5},{5,4},{6,7},{7,6},{8,9},{9,8},{10,11... | collective-permute-start | bytes 221192 | tf_op jit(solution)/shard_map/ppermute | solution.py:84
  1.6 20.3 %collective-permute-start = (bf16[32,4608]{1,0:T(8,128)(2,1)}, bf16[32,4608]{1,0:T(8,128)(2,1)S(1)}, u32[]{:S(2)}, u32[]{:S(2)}) collective-permute-start(bf16[32,4608]{1,0:T(8,128)(2,1)} %param.6), channel_id=1, source_target_pairs={{0,1},{1,0},{2,3},{3,2},{4,5},{5,4},{6,7},{7,6},{8,9},{9,8},{10,11... | collective-permute-start | bytes 884744 | tf_op jit(solution)/shard_map/ppermute | solution.py:80
  10.6 7.8 %collective-permute-start.4 = (bf16[32,576]{1,0:T(8,128)(2,1)S(1)}, bf16[32,576]{1,0:T(8,128)(2,1)S(1)}, u32[]{:S(2)}, u32[]{:S(2)}) collective-permute-start(bf16[32,576]{1,0:T(8,128)(2,1)S(1)} %get-tuple-element.12), channel_id=1, source_target_pairs={{0,4},{1,5},{2,6},{3,7},{4,8},{5,9},{6,10},{7,11},{8,12},{9,13},{1... | collective-permute-start | bytes 110600 | tf_op jit(solution)/shard_map/ppermute | solution.py:91
  13.7 6.0 %collective-permute-start.3 = (bf16[32,576]{1,0:T(8,128)(2,1)S(1)}, bf16[32,576]{1,0:T(8,128)(2,1)S(1)}, u32[]{:S(2)}, u32[]{:S(2)}) collective-permute-start(bf16[32,576]{1,0:T(8,128)(2,1)S(1)} %get-tuple-element.13), channel_id=1, source_target_pairs={{0,8},{1,9},{2,10},{3,11},{4,12},{5,13},{6,14},{7,15},{8,0},{9,1},... | collective-permute-start | bytes 110600 | tf_op jit(solution)/shard_map/ppermute | solution.py:91
  17.6 9.5 %collective-permute-start.21 = (bf16[32,2304]{1,0:T(8,128)(2,1)S(1)}, bf16[32,2304]{1,0:T(8,128)(2,1)S(1)}, u32[]{:S(2)}, u32[]{:S(2)}) collective-permute-start(bf16[32,2304]{1,0:T(8,128)(2,1)S(1)} %get-tuple-element.7.refs_0_), channel_id=1, source_target_pairs={{0,4},{1,3},{4,8},{5,1},{8,12},{9,5},{12,14},{13,9},{14,10},{15,13... | collective-permute-start | bytes 442376 | tf_op jit(solution)/shard_map/ppermute | solution.py:58
  20.7 5.6 %collective-permute-start.5 = (bf16[4,32,576]{2,1,0:T(8,128)(2,1)S(1)}, bf16[4,32,576]{2,1,0:T(8,128)(2,1)S(1)}, u32[]{:S(2)}, u32[]{:S(2)}) collective-permute-start(bf16[4,32,576]{2,1,0:T(8,128)(2,1)S(1)} %get-tuple-element.10), channel_id=1, source_target_pairs={{0,2},{1,3},{2,0},{3,1},{4,6},{5,7},{6,4},{7,5},{8,10},{9,11},{10,... | collective-permute-start | bytes 442376 | tf_op jit(solution)/shard_map/ppermute | solution.py:93
  26.8 5.3 %collective-permute-start.6 = (bf16[32,2432]{1,0:T(8,128)(2,1)S(1)}, bf16[32,2432]{1,0:T(8,128)(2,1)S(1)}, u32[]{:S(2)}, u32[]{:S(2)}) collective-permute-start(bf16[32,2432]{1,0:T(8,128)(2,1)S(1)} %concatenate.11.refs_0_), channel_id=1, source_target_pairs={{0,4},{1,3},{4,8},{5,1},{8,12},{9,5},{12,14},{13,9},{14,10},{15,13... | collective-permute-start | bytes 466952 | tf_op jit(solution)/shard_map/ppermute | solution.py:58
  27.1 6.5 %collective-permute-start.22 = (bf16[32,2304]{1,0:T(8,128)(2,1)S(1)}, bf16[32,2304]{1,0:T(8,128)(2,1)S(1)}, u32[]{:S(2)}, u32[]{:S(2)}) collective-permute-start(bf16[32,2304]{1,0:T(8,128)(2,1)S(1)} %collective-permute-done.21.refs_1_), channel_id=1, source_target_pairs={{0,4},{1,3},{4,8},{5,1},{8,12},{9,5},{12,14},{13,9},{14,10},{15,13... | collective-permute-start | bytes 442376 | tf_op jit(solution)/shard_map/ppermute | solution.py:58
  32.1 5.2 %collective-permute-start.7 = (bf16[32,2432]{1,0:T(8,128)(2,1)S(1)}, bf16[32,2432]{1,0:T(8,128)(2,1)S(1)}, u32[]{:S(2)}, u32[]{:S(2)}) collective-permute-start(bf16[32,2432]{1,0:T(8,128)(2,1)S(1)} %collective-permute-done.6.refs_1_), channel_id=1, source_target_pairs={{0,4},{1,3},{4,8},{5,1},{8,12},{9,5},{12,14},{13,9},{14,10},{15,13... | collective-permute-start | bytes 466952 | tf_op jit(solution)/shard_map/ppermute | solution.py:58
  33.6 5.2 %collective-permute-start.23 = (bf16[32,2304]{1,0:T(8,128)(2,1)S(1)}, bf16[32,2304]{1,0:T(8,128)(2,1)S(1)}, u32[]{:S(2)}, u32[]{:S(2)}) collective-permute-start(bf16[32,2304]{1,0:T(8,128)(2,1)S(1)} %collective-permute-done.22.refs_2_), channel_id=1, source_target_pairs={{0,4},{1,3},{4,8},{5,1},{8,12},{9,5},{12,14},{13,9},{14,10},{15,13... | collective-permute-start | bytes 442376 | tf_op jit(solution)/shard_map/ppermute | solution.py:58
  37.3 5.2 %collective-permute-start.8 = (bf16[32,2432]{1,0:T(8,128)(2,1)S(1)}, bf16[32,2432]{1,0:T(8,128)(2,1)S(1)}, u32[]{:S(2)}, u32[]{:S(2)}) collective-permute-start(bf16[32,2432]{1,0:T(8,128)(2,1)S(1)} %collective-permute-done.7.refs_2_), channel_id=1, source_target_pairs={{0,4},{1,3},{4,8},{5,1},{8,12},{9,5},{12,14},{13,9},{14,10},{15,13... | collective-permute-start | bytes 466952 | tf_op jit(solution)/shard_map/ppermute | solution.py:58
  42.8 5.7 %collective-permute-start.28 = (bf16[32,2304]{1,0:T(8,128)(2,1)S(1)}, bf16[32,2304]{1,0:T(8,128)(2,1)S(1)}, u32[]{:S(2)}, u32[]{:S(2)}) collective-permute-start(bf16[32,2304]{1,0:T(8,128)(2,1)S(1)} %get-tuple-element.7.refs_0_), channel_id=1, source_target_pairs={{0,1},{1,0},{2,3},{3,2},{4,5},{5,4},{6,7},{7,6},{8,9},{9,8},{10,11... | collective-permute-start | bytes 442376 | tf_op jit(solution)/shard_map/ppermute | solution.py:60
  48.0 5.2 %collective-permute-start.13 = (bf16[32,2432]{1,0:T(8,128)(2,1)S(1)}, bf16[32,2432]{1,0:T(8,128)(2,1)S(1)}, u32[]{:S(2)}, u32[]{:S(2)}) collective-permute-start(bf16[32,2432]{1,0:T(8,128)(2,1)S(1)} %concatenate.11.refs_0_), channel_id=1, source_target_pairs={{0,1},{1,0},{2,3},{3,2},{4,5},{5,4},{6,7},{7,6},{8,9},{9,8},{10,11... | collective-permute-start | bytes 466952 | tf_op jit(solution)/shard_map/ppermute | solution.py:60
  49.6 5.7 %collective-permute-start.14 = (bf16[32,2432]{1,0:T(8,128)(2,1)S(1)}, bf16[32,2432]{1,0:T(8,128)(2,1)S(1)}, u32[]{:S(2)}, u32[]{:S(2)}) collective-permute-start(bf16[32,2432]{1,0:T(8,128)(2,1)S(1)} %collective-permute-done.6.refs_1_), channel_id=1, source_target_pairs={{0,1},{1,0},{2,3},{3,2},{4,5},{5,4},{6,7},{7,6},{8,9},{9,8},{10,11... | collective-permute-start | bytes 466952 | tf_op jit(solution)/shard_map/ppermute | solution.py:60
  53.0 6.8 %collective-permute-start.11 = (bf16[32,2432]{1,0:T(8,128)(2,1)S(1)}, bf16[32,2432]{1,0:T(8,128)(2,1)S(1)}, u32[]{:S(2)}, u32[]{:S(2)}) collective-permute-start(bf16[32,2432]{1,0:T(8,128)(2,1)S(1)} %collective-permute-done.10.refs_5_), channel_id=1, source_target_pairs={{0,4},{1,3},{4,8},{5,1},{8,12},{9,5},{12,14},{13,9},{14,10},{15,13... | collective-permute-start | bytes 466952 | tf_op jit(solution)/shard_map/ppermute | solution.py:58
  54.8 5.3 %collective-permute-start.15 = (bf16[32,2432]{1,0:T(8,128)(2,1)S(1)}, bf16[32,2432]{1,0:T(8,128)(2,1)S(1)}, u32[]{:S(2)}, u32[]{:S(2)}) collective-permute-start(bf16[32,2432]{1,0:T(8,128)(2,1)S(1)} %collective-permute-done.7.refs_2_), channel_id=1, source_target_pairs={{0,1},{1,0},{2,3},{3,2},{4,5},{5,4},{6,7},{7,6},{8,9},{9,8},{10,11... | collective-permute-start | bytes 466952 | tf_op jit(solution)/shard_map/ppermute | solution.py:60
  55.3 5.7 %collective-permute-start.33 = (bf16[32,2304]{1,0:T(8,128)(2,1)S(1)}, bf16[32,2304]{1,0:T(8,128)(2,1)S(1)}, u32[]{:S(2)}, u32[]{:S(2)}) collective-permute-start(bf16[32,2304]{1,0:T(8,128)(2,1)S(1)} %collective-permute-done.25.refs_5_), channel_id=1, source_target_pairs={{0,1},{1,0},{2,3},{3,2},{4,5},{5,4},{6,7},{7,6},{8,9},{9,8},{10,11... | collective-permute-start | bytes 442376 | tf_op jit(solution)/shard_map/ppermute | solution.py:60
  55.4 5.8 %collective-permute-start.34 = (bf16[32,2304]{1,0:T(8,128)(2,1)S(1)}, bf16[32,2304]{1,0:T(8,128)(2,1)S(1)}, u32[]{:S(2)}, u32[]{:S(2)}) collective-permute-start(bf16[32,2304]{1,0:T(8,128)(2,1)S(1)} %collective-permute-done.26.refs_6_), channel_id=1, source_target_pairs={{0,1},{1,0},{2,3},{3,2},{4,5},{5,4},{6,7},{7,6},{8,9},{9,8},{10,11... | collective-permute-start | bytes 442376 | tf_op jit(solution)/shard_map/ppermute | solution.py:60
  59.8 5.2 %collective-permute-start.12 = (bf16[32,2432]{1,0:T(8,128)(2,1)S(1)}, bf16[32,2432]{1,0:T(8,128)(2,1)S(1)}, u32[]{:S(2)}, u32[]{:S(2)}) collective-permute-start(bf16[32,2432]{1,0:T(8,128)(2,1)S(1)} %collective-permute-done.11.refs_6_), channel_id=1, source_target_pairs={{0,4},{1,3},{4,8},{5,1},{8,12},{9,5},{12,14},{13,9},{14,10},{15,13... | collective-permute-start | bytes 466952 | tf_op jit(solution)/shard_map/ppermute | solution.py:58
  60.2 19.8 %collective-permute-start.16 = (bf16[32,2432]{1,0:T(8,128)(2,1)S(1)}, bf16[32,2432]{1,0:T(8,128)(2,1)S(1)}, u32[]{:S(2)}, u32[]{:S(2)}) collective-permute-start(bf16[32,2432]{1,0:T(8,128)(2,1)S(1)} %collective-permute-done.8.refs_3_), channel_id=1, source_target_pairs={{0,1},{1,0},{2,3},{3,2},{4,5},{5,4},{6,7},{7,6},{8,9},{9,8},{10,11... | collective-permute-start | bytes 466952 | tf_op jit(solution)/shard_map/ppermute | solution.py:60
  61.1 18.9 %collective-permute-start.17 = (bf16[32,2432]{1,0:T(8,128)(2,1)S(1)}, bf16[32,2432]{1,0:T(8,128)(2,1)S(1)}, u32[]{:S(2)}, u32[]{:S(2)}) collective-permute-start(bf16[32,2432]{1,0:T(8,128)(2,1)S(1)} %collective-permute-done.9.refs_4_), channel_id=1, source_target_pairs={{0,1},{1,0},{2,3},{3,2},{4,5},{5,4},{6,7},{7,6},{8,9},{9,8},{10,11... | collective-permute-start | bytes 466952 | tf_op jit(solution)/shard_map/ppermute | solution.py:60
  61.2 18.8 %collective-permute-start.18 = (bf16[32,2432]{1,0:T(8,128)(2,1)S(1)}, bf16[32,2432]{1,0:T(8,128)(2,1)S(1)}, u32[]{:S(2)}, u32[]{:S(2)}) collective-permute-start(bf16[32,2432]{1,0:T(8,128)(2,1)S(1)} %collective-permute-done.10.refs_5_), channel_id=1, source_target_pairs={{0,1},{1,0},{2,3},{3,2},{4,5},{5,4},{6,7},{7,6},{8,9},{9,8},{10,11... | collective-permute-start | bytes 466952 | tf_op jit(solution)/shard_map/ppermute | solution.py:60
  61.6 18.4 %collective-permute-start.19 = (bf16[32,2432]{1,0:T(8,128)(2,1)S(1)}, bf16[32,2432]{1,0:T(8,128)(2,1)S(1)}, u32[]{:S(2)}, u32[]{:S(2)}) collective-permute-start(bf16[32,2432]{1,0:T(8,128)(2,1)S(1)} %collective-permute-done.11.refs_6_), channel_id=1, source_target_pairs={{0,1},{1,0},{2,3},{3,2},{4,5},{5,4},{6,7},{7,6},{8,9},{9,8},{10,11... | collective-permute-start | bytes 466952 | tf_op jit(solution)/shard_map/ppermute | solution.py:60
  65.0 14.9 %collective-permute-start.20 = (bf16[32,2432]{1,0:T(8,128)(2,1)S(1)}, bf16[32,2432]{1,0:T(8,128)(2,1)S(1)}, u32[]{:S(2)}, u32[]{:S(2)}) collective-permute-start(bf16[32,2432]{1,0:T(8,128)(2,1)S(1)} %collective-permute-done.12.refs_7_), channel_id=1, source_target_pairs={{0,1},{1,0},{2,3},{3,2},{4,5},{5,4},{6,7},{7,6},{8,9},{9,8},{10,11... | collective-permute-start | bytes 466952 | tf_op jit(solution)/shard_map/ppermute | solution.py:60
  (16 other events, 119.9 us)

commit v2 on v0

v2 whole, which is shorter than its diff:
```python
import functools

import jax
import jax.numpy as jnp
import numpy as np
from jax import lax
from jax.experimental import pallas as pl
from jax.experimental.pallas import tpu as pltpu
from jax.sharding import PartitionSpec as P

BLOCK = 128
AXES = ("seq", "adapter")
CHUNKS = 2


def ring_order(n):
    return [2 * z for z in range(n // 2)] + [2 * z + 1 for z in reversed(range(n // 2))]


def ring_distances(n):
    steps = [0]
    for hop in range(1, n // 2):
        steps += [-hop, hop]
    return steps + [n // 2]


def ring_perm(n, way):
    order = ring_order(n)
    return [(2 * s + c, 2 * order[(pos + way) % n] + c) for pos, s in enumerate(order) for c in range(2)]


def flip_perm(n, y, c):
    return [(2 * s + k, 2 * (s ^ y) + (k ^ c)) for s in range(n) for k in range(2)]


def z_perm(n, shift):
    nz = n // 2
    return [
        (2 * (2 * z + y) + c, 2 * (2 * ((z - shift) % nz) + y) + c)
        for z in range(nz)
        for y in range(2)
        for c in range(2)
    ]


def device_table(n):
    order, nz = ring_order(n), n // 2
    place = {s: pos for pos, s in enumerate(order)}
    table = np.zeros((2 * n, 3, n), np.int32)
    for s in range(n):
        for c in range(2):
            for i, distance in enumerate(ring_distances(n)):
                chip = order[(place[s] + distance) % n]
                table[2 * s + c, 0, i] = chip
                for core in range(2):
                    turn = (chip // 2 - s // 2) % nz
                    table[2 * s + c, 1 + core, i] = 4 * turn + 2 * ((chip ^ s) & 1) + (core ^ c)
    return table.reshape(2 * n, -1)


def gather_ring(chunks, n):
    ahead, back = ring_perm(n, 1), ring_perm(n, -1)
    swap = flip_perm(n, 0, 1)
    own = [[x] for x in chunks]
    other = [[lax.ppermute(x, AXES, swap)] for x in chunks]
    up, down = list(chunks), list(chunks)
    for hop in range(1, n // 2):
        for k in range(len(chunks)):
            up[k] = lax.ppermute(up[k], AXES, ahead)
            down[k] = lax.ppermute(down[k], AXES, back)
        for k in range(len(chunks)):
            own[k] += [up[k], down[k]]
            other[k] += [lax.ppermute(x, AXES, swap) for x in (up[k], down[k])]
    for k in range(len(chunks)):
        end = lax.ppermute(*((down[k], AXES, back) if k % 2 else (up[k], AXES, ahead)))
        own[k].append(end)
        other[k].append(lax.ppermute(end, AXES, swap))
    return own, other


def pick_kernel(n, blocks_apart, adapters, place, keep, keep_far, give, give_far, *outs):
    nz, held = n // 2, keep.shape[0]
    s, c = place[0], place[1]
    z, y = s >> 1, s & 1
    for shift, out in enumerate(outs):
        seat = z - shift
        seat = jnp.where(seat < 0, seat + nz, seat)
        adapter = adapters[(seat * 2 * blocks_apart) // BLOCK]
        for index in range(held):

            @pl.when(adapter == c * held + index)
            def _():
                out[y] = keep[index]
                out[1 - y] = keep_far[index]

            @pl.when(adapter == (1 - c) * held + index)
            def _():
                out[y] = give[index]
                out[1 - y] = give_far[index]


def split_kernel(place, down_ref, keep, give):
    half = keep.shape[1]
    c = place[1]
    for ref, core in ((keep, c), (give, 1 - c)):
        ref[...] = down_ref[:, pl.ds(pl.multiple_of(core * half, half), half), :].astype(jnp.bfloat16)


def whole(count):
    return [pl.BlockSpec(memory_space=pltpu.VMEM)] * count


def small_call(kernel, scalars, arrays, outs):
    return pl.pallas_call(
        kernel,
        out_shape=[jax.ShapeDtypeStruct(shape, jnp.bfloat16) for shape in outs],
        in_specs=[pl.BlockSpec(memory_space=pltpu.SMEM)] * len(scalars) + whole(len(arrays)),
        out_specs=whole(len(outs)),
    )(*scalars, *arrays)


def spread_shrink(own, other, down, adapters, place, n):
    z, c = lax.axis_index("seq") >> 1, lax.axis_index("adapter")
    nz, rows = n // 2, own[0].shape[0]
    held, width, rank = down.shape
    half = rank // 2
    part = (held, half, width)
    keep, give = small_call(split_kernel, [place], [jnp.swapaxes(down, 1, 2)], [part, part])
    keep_far = lax.ppermute(keep, AXES, flip_perm(n, 1, 0))
    give_near = lax.ppermute(give, AXES, flip_perm(n, 0, 1))
    give_far = lax.ppermute(give, AXES, flip_perm(n, 1, 1))
    picks = small_call(
        functools.partial(pick_kernel, n, 2 * rows),
        [adapters, place],
        [keep, keep_far, give_near, give_far],
        [(2, half, width)] * nz,
    )
    factor = jnp.stack(
        [picks[0]] + [lax.ppermute(picks[shift], AXES, z_perm(n, shift)) for shift in range(1, nz)]
    )
    mine, theirs = jnp.concatenate(own, 1), jnp.concatenate(other, 1)
    chip_rows = jnp.where(c == 0, jnp.stack([mine, theirs]), jnp.stack([theirs, mine])).reshape(2 * rows, -1)
    turned = lax.dynamic_slice_in_dim(
        jnp.concatenate([chip_rows, chip_rows], 1), z * 2 * width, n * width, 1
    ).reshape(2 * rows, nz, 2, width)
    shrink = jnp.einsum("tzyk,zyrk->tr", turned, factor, preferred_element_type=jnp.float32)
    high = shrink.astype(jnp.bfloat16)
    low = (shrink - high.astype(jnp.float32)).astype(jnp.bfloat16)
    piece = jnp.concatenate([high[:rows], high[rows:], low[:rows], low[rows:]], 1)
    near = jnp.concatenate(
        [piece] + [lax.ppermute(piece, AXES, flip_perm(n, y, c)) for y, c in ((0, 1), (1, 0), (1, 1))], 0
    )
    return [near] + [lax.ppermute(near, AXES, z_perm(n, shift)) for shift in range(1, nz)]


def rows_kernel(layout, table, place, adapters, live, *refs):
    n, begin, entries, chunks, aliased = layout
    count = 2 * entries * chunks
    pieces, refs = refs[:count], refs[count:]
    parts, refs = refs[: n // 2], refs[n // 2 :]
    w_ref, up_ref = refs[:2]
    out_ref, held, near, shrink, block, in_sems, out_sems = refs[2 + aliased :]
    rows, depth = pieces[0].shape
    chip, (_, columns) = 2 * rows, w_ref.shape
    half = near.shape[1] // 4
    step = pl.program_id(0)
    c = place[1]

    @pl.when(step == 0)
    def _():
        copies = []
        for i in range(entries):
            for k in range(chunks):
                for far in range(2):
                    at = (i * chunks + k) * 2 + far
                    core = 1 - c if far else c
                    row = pl.multiple_of(i * chip + core * rows, rows)
                    to = held.at[pl.ds(row, rows), pl.ds(k * depth, depth)]
                    copies.append(pltpu.make_async_copy(pieces[at], to, in_sems.at[at]))
        for copy in copies:
            copy.start()
        for j, part in enumerate(parts):
            near[j * 4 * rows : (j + 1) * 4 * rows, :] = part[...]
        for i in range(entries):
            zero, one = (
                near[pl.ds(pl.multiple_of(table[(1 + core) * n + begin + i] * rows, rows), rows), :]
                for core in range(2)
            )
            for core in range(2):
                a, b = core * half, (2 + core) * half
                shrink[i * chip + core * rows : i * chip + (core + 1) * rows, :] = jnp.concatenate(
                    [zero[:, a : a + half], one[:, a : a + half], zero[:, b : b + half], one[:, b : b + half]], 1
                )
        for copy in copies:
            copy.wait()

    def outgoing(j, i):
        to = out_ref.at[pl.ds(pl.multiple_of(table[begin + i] * chip, chip), chip), pl.ds(j * columns, columns)]
        return pltpu.make_async_copy(block.at[j, pl.ds(i * chip, chip), :], to, out_sems.at[j, i])

    tile = jnp.dot(held[...], w_ref[...], preferred_element_type=jnp.float32)
    for i in range(entries):
        first = table[begin + i] * chip
        of_block = first // BLOCK
        factor = up_ref[adapters[of_block]].astype(jnp.bfloat16)
        at = slice(i * chip, (i + 1) * chip)
        delta = jnp.dot(
            shrink[at, :], jnp.concatenate([factor, factor], 0), preferred_element_type=jnp.float32
        )
        row = lax.broadcasted_iota(jnp.int32, delta.shape, 0) + (first - of_block * BLOCK)
        block[step, at, :] = jnp.where(row < live[of_block], tile[at] + delta, 0.0).astype(out_ref.dtype)
    for j in range(block.shape[0]):

        @pl.when(step == j)
        def _():
            for i in range(entries):
                outgoing(j, i).start()

    @pl.when(step == block.shape[0] - 1)
    def _():
        for j in range(block.shape[0]):
            for i in range(entries):
                outgoing(j, i).wait()


def rows_matmul(n, begin, own, other, parts, scalars, weight, up, into):
    chunks, entries = len(own), len(own[0])
    pieces = [x[k][i] for i in range(entries) for k in range(chunks) for x in (own, other)]
    rows, depth = pieces[0].shape
    total, width = 2 * rows * entries, weight.shape[1]
    columns = 768 if width % 768 == 0 else width
    held, rank = up.shape[:2]
    aliased = [] if into is None else [into]
    operands = [*scalars, *pieces, *parts, weight, up, *aliased]
    return pl.pallas_call(
        functools.partial(rows_kernel, (n, begin, entries, chunks, len(aliased))),
        out_shape=jax.ShapeDtypeStruct((2 * n * rows, width), jnp.bfloat16),
        grid_spec=pltpu.PrefetchScalarGridSpec(
            num_scalar_prefetch=len(scalars),
            grid=(width // columns,),
            in_specs=[pl.BlockSpec(memory_space=pl.ANY)] * len(pieces)
            + whole(len(parts))
            + [
                pl.BlockSpec((weight.shape[0], columns), lambda j, *_: (0, j)),
                pl.BlockSpec((held, rank, columns), lambda j, *_: (0, 0, j)),
            ]
            + [pl.BlockSpec(memory_space=pl.ANY)] * len(aliased),
            out_specs=pl.BlockSpec(memory_space=pl.ANY),
            scratch_shapes=[
                pltpu.VMEM((total, chunks * depth), jnp.bfloat16),
                pltpu.VMEM((2 * n * rows, 2 * rank), jnp.bfloat16),
                pltpu.VMEM((total, 2 * rank), jnp.bfloat16),
                pltpu.VMEM((width // columns, total, columns), jnp.bfloat16),
                pltpu.SemaphoreType.DMA((len(pieces),)),
                pltpu.SemaphoreType.DMA((width // columns, entries)),
            ],
        ),
        input_output_aliases={len(operands) - 1: 0} if aliased else {},
        compiler_params=pltpu.CompilerParams(vmem_limit_bytes=44 << 20),
        cost_estimate=pl.CostEstimate(
            flops=2 * total * chunks * depth * width,
            bytes_accessed=2 * chunks * depth * width + 2 * total * width,
            transcendentals=0,
        ),
    )(*operands)


def on_device(n, tokens, weight, down, up, adapter_per_block, rows_per_block):
    depth = tokens.shape[1] // CHUNKS
    adapters = adapter_per_block[:, 0]
    device = lax.axis_index(AXES)
    table = lax.dynamic_index_in_dim(jnp.asarray(device_table(n)), device, 0, False)
    place = jnp.stack([device >> 1, device & 1]).astype(jnp.int32)
    own, other = gather_ring([tokens[:, k * depth : (k + 1) * depth] for k in range(CHUNKS)], n)
    parts = spread_shrink([x[0] for x in own], [x[0] for x in other], down, adapters, place, n)
    scalars = (table, place, adapters, rows_per_block)
    cut = 1 + 2 * (n // 2 - 2)
    out = None
    for begin, end in ((0, cut), (cut, n)):
        out = rows_matmul(
            n, begin, [x[begin:end] for x in own], [x[begin:end] for x in other], parts, scalars, weight, up, out
        )
    return out


def solution(mesh):
    placed = (
        P(("groups", "seq", "adapter"), None),
        P(None, ("seq", "adapter")),
        P(("groups", "adapter"), "seq", None),
        P("groups", None, ("seq", "adapter")),
        P("groups", None),
        P("groups"),
    )
    return jax.shard_map(
        functools.partial(on_device, mesh.shape["seq"]),
        mesh=mesh,
        in_specs=placed,
        out_specs=P("groups", ("seq", "adapter")),
        check_vma=False,
    )
```

time: 189 us -> 113 us (0.60)
  waiting for transfers between devices: 138 us -> 20.8 us
  starting transfers between devices: 0.04 us -> 35.1 us
  matrix products: 34.6 us -> 1.61 us
  Pallas kernels: 0 us -> 32.2 us
  local copies, waits for them, and re-layouts: 2.1 us -> 21.7 us
  between operations: 13.5 us -> 0.22 us
    psum x1 -> x0, waiting for transfers between devices: 85.5 us -> none  [on_device(): rank_reduction = lax.psum(combined[:, ff_local:], ('seq', 'adapter'))]
    all_gather x1 -> x0, waiting for transfers between devices: 51.6 us -> none  [on_device(): device_rows = lax.all_gather(tokens, ('seq', 'adapter'), axis=0, tiled=True)]
    ppermute x0 -> x42, starting transfers between devices: none -> 35.1 us  [the longest x6 7.73 us: gather_ring(): up[k] = lax.ppermute(up[k], AXES, ahead)]
    dot_general x6 -> x1, matrix products: 34.6 us -> 1.61 us  [spread_shrink(): jnp.einsum('tzyk,zyrk->tr', turned, factor, preferred_element_type=jnp.fl...]
    pallas_call x0 -> x4, Pallas kernels: none -> 32.2 us  [the longest x2 28.6 us: rows_matmul(): pl.pallas_call(functools.partial(rows_kernel, (n, begin, entries, chunks,...]
    ppermute x0 -> x42, waiting for transfers between devices: none -> 20.8 us  [the longest x3 13.4 us: spread_shrink(): lax.ppermute(near, AXES, z_perm(n, shift))]
    unnamed x8 -> x68, local copies, waits for them, and re-layouts: 0.02 us -> 18.5 us
  transfers between devices with their start and end apart: 2 -> 42, of which waited for: 2 -> 7; matrix products, arithmetic and copies ran while one was open for 4% -> 4% of each run, Pallas kernels for 0% -> 17%
where the time goes in v2:
time: 113 us
  starting transfers between devices  35.1 us (31%)
  Pallas kernels  32.2 us (28%)
  local copies, waits for them, and re-layouts  21.7 us (19%)
  waiting for transfers between devices  20.8 us (18%)
  matrix products  1.61 us (1%)
  other arithmetic  1.19 us (1%)
    pallas_call x2, Pallas kernels, rows_matmul(): pl.pallas_call(functools.partial(rows_kernel, (n, begin, entries, chunks,...  28.6 us
    unnamed x68, local copies, waits for them, and re-layouts  18.5 us
    ppermute x3, waiting for transfers between devices, spread_shrink(): lax.ppermute(near, AXES, z_perm(n, shift))  13.4 us
    ppermute x6, starting transfers between devices, gather_ring(): up[k] = lax.ppermute(up[k], AXES, ahead)  7.73 us
    ppermute x3, starting transfers between devices, spread_shrink(): lax.ppermute(picks[shift], AXES, z_perm(n, shift))  7.21 us
    ppermute x6, starting transfers between devices, gather_ring(): down[k] = lax.ppermute(down[k], AXES, back)  5.67 us
    ppermute x3, starting transfers between devices, spread_shrink(): lax.ppermute(near, AXES, z_perm(n, shift))  4.67 us
    pallas_call x2, Pallas kernels, small_call(): pl.pallas_call(kernel, out_shape=[jax.ShapeDtypeStruct(shape, jnp.bfloat1...  3.56 us
  transfers between devices with their start and end apart: 42, of which 7 were waited for; matrix products, arithmetic and copies ran while one was open for 4% of the time, Pallas kernels for 17%

profile of v2, /device:TPU:0, one launch (start us, length us, event | category | flops | bytes accessed | tf_op | source)
XLA Modules:
  0.0 112.8 jit_solution(15965822330645901725)
XLA Ops:
  2.3 1.7 %shard_map.73 = (bf16[2,32,576]{2,1,0:T(8,128)(2,1)}, bf16[2,32,576]{2,1,0:T(8,128)(2,1)}) custom-call(s32[2]{0:T(128)} %pad_add_fusion.place, f32[2,64,576]{2,1,0:T(8,128)} %bitcast.23), custom_call_target="tpu_custom_call" | custom-call | tf_op jit(solution)/shard_map/pallas_call | solution.py:114
  3.9 2.9 %collective-permute-start.22 = (bf16[2,32,576]{2,1,0:T(8,128)(2,1)}, bf16[2,32,576]{2,1,0:T(8,128)(2,1)S(1)}, u32[]{:S(2)}, u32[]{:S(2)}) collective-permute-start(bf16[2,32,576]{2,1,0:T(8,128)(2,1)} %get-tuple-element.11.keep), channel_id=1, source_target_pairs={{0,2},{1,3},{2,0},{3,1},{4,6},{5,7},{6,4},{7,5},{8,10},{9,11},{10,... | collective-permute-start | bytes 221192 | tf_op jit(solution)/shard_map/ppermute | solution.py:129
  7.0 3.0 %collective-permute-done.22.keep_far = bf16[2,32,576]{2,1,0:T(8,128)(2,1)S(1)} collective-permute-done((bf16[2,32,576]{2,1,0:T(8,128)(2,1)}, bf16[2,32,576]{2,1,0:T(8,128)(2,1)S(1)}, u32[]{:S(2)}, u32[]{:S(2)}) %collective-permute-start.22) | collective-permute-done | bytes 73760 | tf_op jit(solution)/shard_map/ppermute | solution.py:129
  10.0 1.6 %collective-permute-start = (bf16[32,2304]{1,0:T(8,128)(2,1)S(1)}, bf16[32,2304]{1,0:T(8,128)(2,1)S(1)}, u32[]{:S(2)}, u32[]{:S(2)}) collective-permute-start(bf16[32,2304]{1,0:T(8,128)(2,1)S(1)} %get-tuple-element.20.refs_0_), channel_id=1, source_target_pairs={{0,4},{1,5},{4,8},{5,9},{8,12},{9,13},{12,14},{13,15},{14,10},{15,... | collective-permute-start | bytes 442376 | tf_op jit(solution)/shard_map/ppermute | solution.py:69
  11.6 1.6 %collective-permute-start.4 = (bf16[32,2304]{1,0:T(8,128)(2,1)S(1)}, bf16[32,2304]{1,0:T(8,128)(2,1)S(1)}, u32[]{:S(2)}, u32[]{:S(2)}) collective-permute-start(bf16[32,2304]{1,0:T(8,128)(2,1)S(1)} %get-tuple-element.19.refs_2_), channel_id=1, source_target_pairs={{0,4},{1,5},{4,8},{5,9},{8,12},{9,13},{12,14},{13,15},{14,10},{15,... | collective-permute-start | bytes 442376 | tf_op jit(solution)/shard_map/ppermute | solution.py:69
  13.8 1.9 %shard_map.74 = (bf16[2,32,576]{2,1,0:T(8,128)(2,1)}, bf16[2,32,576]{2,1,0:T(8,128)(2,1)}, bf16[2,32,576]{2,1,0:T(8,128)(2,1)}, bf16[2,32,576]{2,1,0:T(8,128)(2,1)}) custom-call(s32[4]{0:T(128)} %bitcast.18, s32[2]{0:T(128)} %pad_add_fusion.place, bf16[2,32,576]{2,1,0:T(8,128)(2,1)} %get-tuple-element.11.keep, bf16[2,32,576]{2,1,0:T(8,128)(2,1)} %copy-done.27, ...), custom_call_target="tpu_custom_call" | custom-call | tf_op jit(solution)/shard_map/pallas_call | solution.py:114
  15.7 3.4 %collective-permute-start.26 = (bf16[2,32,576]{2,1,0:T(8,128)(2,1)}, bf16[2,32,576]{2,1,0:T(8,128)(2,1)S(1)}, u32[]{:S(2)}, u32[]{:S(2)}) collective-permute-start(bf16[2,32,576]{2,1,0:T(8,128)(2,1)} %get-tuple-element.15), channel_id=1, source_target_pairs={{0,8},{1,9},{2,10},{3,11},{4,12},{5,13},{6,14},{7,15},{8,0},{9,1},... | collective-permute-start | bytes 221192 | tf_op jit(solution)/shard_map/ppermute | solution.py:139
  19.6 3.4 %collective-permute-start.25 = (bf16[2,32,576]{2,1,0:T(8,128)(2,1)}, bf16[2,32,576]{2,1,0:T(8,128)(2,1)S(1)}, u32[]{:S(2)}, u32[]{:S(2)}) collective-permute-start(bf16[2,32,576]{2,1,0:T(8,128)(2,1)} %get-tuple-element.14), channel_id=1, source_target_pairs={{0,12},{1,13},{2,14},{3,15},{4,0},{5,1},{6,2},{7,3},{8,4},{9,5},{1... | collective-permute-start | bytes 221192 | tf_op jit(solution)/shard_map/ppermute | solution.py:139
  23.4 1.5 %reshape.8 = bf16[64,4,2,576]{3,2,1,0:T(2,128)(2,1)} reshape(bf16[64,4608]{1,0:T(8,128)(2,1)S(1)} %fusion.1) | data formatting | bytes 1179648 | tf_op jit(solution)/shard_map/reshape | solution.py:145
  24.8 1.7 %collective-permute-start.8 = (bf16[32,2304]{1,0:T(8,128)(2,1)S(1)}, bf16[32,2304]{1,0:T(8,128)(2,1)S(1)}, u32[]{:S(2)}, u32[]{:S(2)}) collective-permute-start(bf16[32,2304]{1,0:T(8,128)(2,1)S(1)} %get-tuple-element.20.refs_0_), channel_id=1, source_target_pairs={{0,2},{1,3},{4,0},{5,1},{8,4},{9,5},{12,8},{13,9},{14,12},{15,13},... | collective-permute-start | bytes 442376 | tf_op jit(solution)/shard_map/ppermute | solution.py:70
  27.2 1.6 %subtract_convert_fusion = (bf16[64,32]{1,0:T(8,128)(2,1)S(1)}, bf16[64,32]{1,0:T(8,128)(2,1)S(1)}) fusion(bf16[64,4,2,576]{3,2,1,0:T(2,128)(2,1)} %reshape.8, bf16[1,2,32,576]{3,2,1,0:T(8,128)(2,1)} %bitcast.26, bf16[1,2,32,576]{3,2,1,0:T(8,128)(2,1)} %bitcast.25, bf16[1,2,32,576]{3,2,1,0:T(8,128)(2,1)} %bitcast.27, bf16[1,2,32,576]{3,2,1,0:T(8,128)(2,1)S(1)} %bitcast.24), kind=kOutput, calls=%fused_computation.10 | convolution fusion | flops 19324928 | bytes 892928 | tf_op jit(solution)/shard_map/tzyk,zyrk->tr/dot_general | solution.py:146
  30.9 2.0 %collective-permute-start.1 = (bf16[32,2304]{1,0:T(8,128)(2,1)S(1)}, bf16[32,2304]{1,0:T(8,128)(2,1)S(1)}, u32[]{:S(2)}, u32[]{:S(2)}) collective-permute-start(bf16[32,2304]{1,0:T(8,128)(2,1)S(1)} %collective-permute-done.refs_4_), channel_id=1, source_target_pairs={{0,4},{1,5},{4,8},{5,9},{8,12},{9,13},{12,14},{13,15},{14,10},{15,... | collective-permute-start | bytes 442376 | tf_op jit(solution)/shard_map/ppermute | solution.py:69
  33.6 1.3 %collective-permute-start.9 = (bf16[32,2304]{1,0:T(8,128)(2,1)S(1)}, bf16[32,2304]{1,0:T(8,128)(2,1)}, u32[]{:S(2)}, u32[]{:S(2)}) collective-permute-start(bf16[32,2304]{1,0:T(8,128)(2,1)S(1)} %collective-permute-done.8.refs_8_), channel_id=1, source_target_pairs={{0,2},{1,3},{4,0},{5,1},{8,4},{9,5},{12,8},{13,9},{14,12},{15,13},... | collective-permute-start | bytes 442376 | tf_op jit(solution)/shard_map/ppermute | solution.py:70
  35.4 2.4 %collective-permute-start.31 = (bf16[128,128]{1,0:T(8,128)(2,1)S(1)}, bf16[128,128]{1,0:T(8,128)(2,1)S(1)}, u32[]{:S(2)}, u32[]{:S(2)}) collective-permute-start(bf16[128,128]{1,0:T(8,128)(2,1)S(1)} %pad_maximum_fusion.1.refs_20_.refs_12_), channel_id=1, source_target_pairs={{0,12},{1,13},{2,14},{3,15},{4,0},{5,1},{6,2},{7,3},{8,4},{9,5},{1... | collective-permute-start | bytes 98312 | tf_op jit(solution)/shard_map/ppermute | solution.py:153
  37.9 5.1 %collective-permute-done.31.refs_21_.refs_13_ = bf16[128,128]{1,0:T(8,128)(2,1)S(1)} collective-permute-done((bf16[128,128]{1,0:T(8,128)(2,1)S(1)}, bf16[128,128]{1,0:T(8,128)(2,1)S(1)}, u32[]{:S(2)}, u32[]{:S(2)}) %collective-permute-start.31) | collective-permute-done | bytes 32800 | tf_op jit(solution)/shard_map/ppermute | solution.py:153
  44.0 3.8 %collective-permute-done.32.refs_22_.refs_14_ = bf16[128,128]{1,0:T(8,128)(2,1)S(1)} collective-permute-done((bf16[128,128]{1,0:T(8,128)(2,1)S(1)}, bf16[128,128]{1,0:T(8,128)(2,1)S(1)}, u32[]{:S(2)}, u32[]{:S(2)}) %collective-permute-start.32) | collective-permute-done | bytes 32800 | tf_op jit(solution)/shard_map/ppermute | solution.py:153
  47.8 1.2 %collective-permute-start.33 = (bf16[128,128]{1,0:T(8,128)(2,1)S(1)}, bf16[128,128]{1,0:T(8,128)(2,1)S(1)}, u32[]{:S(2)}, u32[]{:S(2)}) collective-permute-start(bf16[128,128]{1,0:T(8,128)(2,1)S(1)} %pad_maximum_fusion.1.refs_20_.refs_12_), channel_id=1, source_target_pairs={{0,4},{1,5},{2,6},{3,7},{4,8},{5,9},{6,10},{7,11},{8,12},{9,13},{1... | collective-permute-start | bytes 98312 | tf_op jit(solution)/shard_map/ppermute | solution.py:153
  49.0 4.5 %collective-permute-done.33.refs_23_.refs_15_ = bf16[128,128]{1,0:T(8,128)(2,1)S(1)} collective-permute-done((bf16[128,128]{1,0:T(8,128)(2,1)S(1)}, bf16[128,128]{1,0:T(8,128)(2,1)S(1)}, u32[]{:S(2)}, u32[]{:S(2)}) %collective-permute-start.33) | collective-permute-done | bytes 32800 | tf_op jit(solution)/shard_map/ppermute | solution.py:153
  59.1 2.0 %collective-permute-start.14 = (bf16[32,2304]{1,0:T(8,128)(2,1)S(1)}, bf16[32,2304]{1,0:T(8,128)(2,1)}, u32[]{:S(2)}, u32[]{:S(2)}) collective-permute-start(bf16[32,2304]{1,0:T(8,128)(2,1)S(1)} %collective-permute-done.13.refs_18_), channel_id=1, source_target_pairs={{0,2},{1,3},{4,0},{5,1},{8,4},{9,5},{12,8},{13,9},{14,12},{15,13},... | collective-permute-start | bytes 442376 | tf_op jit(solution)/shard_map/ppermute | solution.py:70
  63.9 1.9 %collective-permute-start.6 = (bf16[32,2304]{1,0:T(8,128)(2,1)}, bf16[32,2304]{1,0:T(8,128)(2,1)}, u32[]{:S(2)}, u32[]{:S(2)}) collective-permute-start(bf16[32,2304]{1,0:T(8,128)(2,1)} %collective-permute-done.5.refs_14_), channel_id=1, source_target_pairs={{0,4},{1,5},{4,8},{5,9},{8,12},{9,13},{12,14},{13,15},{14,10},{15,... | collective-permute-start | bytes 442376 | tf_op jit(solution)/shard_map/ppermute | solution.py:69
  66.0 1.9 %collective-permute-start.18 = (bf16[32,2304]{1,0:T(8,128)(2,1)}, bf16[32,2304]{1,0:T(8,128)(2,1)}, u32[]{:S(2)}, u32[]{:S(2)}) collective-permute-start(bf16[32,2304]{1,0:T(8,128)(2,1)} %collective-permute-done.14.refs_6_), channel_id=1, source_target_pairs={{0,2},{1,3},{4,0},{5,1},{8,4},{9,5},{12,8},{13,9},{14,12},{15,13},... | collective-permute-start | bytes 442376 | tf_op jit(solution)/shard_map/ppermute | solution.py:75
  70.9 2.6 %collective-permute-done.16.refs_8_ = bf16[32,2304]{1,0:T(8,128)(2,1)} collective-permute-done((bf16[32,2304]{1,0:T(8,128)(2,1)}, bf16[32,2304]{1,0:T(8,128)(2,1)}, u32[]{:S(2)}, u32[]{:S(2)}) %collective-permute-start.16) | collective-permute-done | bytes 147488 | tf_op jit(solution)/shard_map/ppermute | solution.py:75
  84.1 15.2 %shard_map.75.refs_18_ = bf16[512,2304]{1,0:T(8,128)(2,1)} custom-call(s32[24]{0:T(128)S(1)} %fusion.3.table, s32[2]{0:T(128)S(1)} %copy-done.23, s32[4]{0:T(128)S(1)} %bitcast.19, s32[4]{0:T(128)S(1)} %copy-done.25, bf16[32,2304]{1,0:T(8,128)(2,1)S(1)} %get-tuple-element.20.refs_0_, bf16[32,2304]{1,0:T(8,128)(2,1)S(1)} %collective-permute-done.20.refs_1_, ...), custom_call_target="tpu_custom_call" | custom-call | flops 6794772480 | bytes 22708224 | tf_op jit(solution)/shard_map/pallas_call | solution.py:235
  99.4 13.4 %shard_map.76 = bf16[512,2304]{1,0:T(8,128)(2,1)} custom-call(s32[24]{0:T(128)S(1)} %fusion.3.table, s32[2]{0:T(128)S(1)} %copy-done.23, s32[4]{0:T(128)S(1)} %bitcast.20, s32[4]{0:T(128)S(1)} %copy-done.25, bf16[32,2304]{1,0:T(8,128)(2,1)} %collective-permute-done.2.refs_0_, ...), custom_call_target="tpu_custom_call", output_to_operand_aliasing={{}: (22, {})} | custom-call | flops 4076863488 | bytes 22118400 | tf_op jit(solution)/shard_map/pallas_call | solution.py:235
  (143 shorter events, 31.2 us)
Async XLA Ops:
  1.1 18.1 %collective-permute-start.20 = (bf16[32,2304]{1,0:T(8,128)(2,1)S(1)}, bf16[32,2304]{1,0:T(8,128)(2,1)S(1)}, u32[]{:S(2)}, u32[]{:S(2)}) collective-permute-start(bf16[32,2304]{1,0:T(8,128)(2,1)S(1)} %get-tuple-element.20.refs_0_), channel_id=1, source_target_pairs={{0,1},{1,0},{2,3},{3,2},{4,5},{5,4},{6,7},{7,6},{8,9},{9,8},{10,11... | collective-permute-start | bytes 442376 | tf_op jit(solution)/shard_map/ppermute | solution.py:65
  1.6 18.0 %collective-permute-start.21 = (bf16[32,2304]{1,0:T(8,128)(2,1)S(1)}, bf16[32,2304]{1,0:T(8,128)(2,1)S(1)}, u32[]{:S(2)}, u32[]{:S(2)}) collective-permute-start(bf16[32,2304]{1,0:T(8,128)(2,1)S(1)} %get-tuple-element.19.refs_2_), channel_id=1, source_target_pairs={{0,1},{1,0},{2,3},{3,2},{4,5},{5,4},{6,7},{7,6},{8,9},{9,8},{10,11... | collective-permute-start | bytes 442376 | tf_op jit(solution)/shard_map/ppermute | solution.py:65
  10.0 19.0 %collective-permute-start = (bf16[32,2304]{1,0:T(8,128)(2,1)S(1)}, bf16[32,2304]{1,0:T(8,128)(2,1)S(1)}, u32[]{:S(2)}, u32[]{:S(2)}) collective-permute-start(bf16[32,2304]{1,0:T(8,128)(2,1)S(1)} %get-tuple-element.20.refs_0_), channel_id=1, source_target_pairs={{0,4},{1,5},{4,8},{5,9},{8,12},{9,13},{12,14},{13,15},{14,10},{15,... | collective-permute-start | bytes 442376 | tf_op jit(solution)/shard_map/ppermute | solution.py:69
  11.6 18.2 %collective-permute-start.4 = (bf16[32,2304]{1,0:T(8,128)(2,1)S(1)}, bf16[32,2304]{1,0:T(8,128)(2,1)S(1)}, u32[]{:S(2)}, u32[]{:S(2)}) collective-permute-start(bf16[32,2304]{1,0:T(8,128)(2,1)S(1)} %get-tuple-element.19.refs_2_), channel_id=1, source_target_pairs={{0,4},{1,5},{4,8},{5,9},{8,12},{9,13},{12,14},{13,15},{14,10},{15,... | collective-permute-start | bytes 442376 | tf_op jit(solution)/shard_map/ppermute | solution.py:69
  15.7 9.1 %collective-permute-start.26 = (bf16[2,32,576]{2,1,0:T(8,128)(2,1)}, bf16[2,32,576]{2,1,0:T(8,128)(2,1)S(1)}, u32[]{:S(2)}, u32[]{:S(2)}) collective-permute-start(bf16[2,32,576]{2,1,0:T(8,128)(2,1)} %get-tuple-element.15), channel_id=1, source_target_pairs={{0,8},{1,9},{2,10},{3,11},{4,12},{5,13},{6,14},{7,15},{8,0},{9,1},... | collective-permute-start | bytes 221192 | tf_op jit(solution)/shard_map/ppermute | solution.py:139
  19.1 7.4 %collective-permute-start.27 = (bf16[2,32,576]{2,1,0:T(8,128)(2,1)}, bf16[2,32,576]{2,1,0:T(8,128)(2,1)S(1)}, u32[]{:S(2)}, u32[]{:S(2)}) collective-permute-start(bf16[2,32,576]{2,1,0:T(8,128)(2,1)} %get-tuple-element.16), channel_id=1, source_target_pairs={{0,4},{1,5},{2,6},{3,7},{4,8},{5,9},{6,10},{7,11},{8,12},{9,13},{1... | collective-permute-start | bytes 221192 | tf_op jit(solution)/shard_map/ppermute | solution.py:139
  19.6 7.0 %collective-permute-start.25 = (bf16[2,32,576]{2,1,0:T(8,128)(2,1)}, bf16[2,32,576]{2,1,0:T(8,128)(2,1)S(1)}, u32[]{:S(2)}, u32[]{:S(2)}) collective-permute-start(bf16[2,32,576]{2,1,0:T(8,128)(2,1)} %get-tuple-element.14), channel_id=1, source_target_pairs={{0,12},{1,13},{2,14},{3,15},{4,0},{5,1},{6,2},{7,3},{8,4},{9,5},{1... | collective-permute-start | bytes 221192 | tf_op jit(solution)/shard_map/ppermute | solution.py:139
  30.9 22.7 %collective-permute-start.1 = (bf16[32,2304]{1,0:T(8,128)(2,1)S(1)}, bf16[32,2304]{1,0:T(8,128)(2,1)S(1)}, u32[]{:S(2)}, u32[]{:S(2)}) collective-permute-start(bf16[32,2304]{1,0:T(8,128)(2,1)S(1)} %collective-permute-done.refs_4_), channel_id=1, source_target_pairs={{0,4},{1,5},{4,8},{5,9},{8,12},{9,13},{12,14},{13,15},{14,10},{15,... | collective-permute-start | bytes 442376 | tf_op jit(solution)/shard_map/ppermute | solution.py:69
  32.8 21.2 %collective-permute-start.5 = (bf16[32,2304]{1,0:T(8,128)(2,1)S(1)}, bf16[32,2304]{1,0:T(8,128)(2,1)}, u32[]{:S(2)}, u32[]{:S(2)}) collective-permute-start(bf16[32,2304]{1,0:T(8,128)(2,1)S(1)} %collective-permute-done.4.refs_6_), channel_id=1, source_target_pairs={{0,4},{1,5},{4,8},{5,9},{8,12},{9,13},{12,14},{13,15},{14,10},{15,... | collective-permute-start | bytes 442376 | tf_op jit(solution)/shard_map/ppermute | solution.py:69
  33.6 20.5 %collective-permute-start.9 = (bf16[32,2304]{1,0:T(8,128)(2,1)S(1)}, bf16[32,2304]{1,0:T(8,128)(2,1)}, u32[]{:S(2)}, u32[]{:S(2)}) collective-permute-start(bf16[32,2304]{1,0:T(8,128)(2,1)S(1)} %collective-permute-done.8.refs_8_), channel_id=1, source_target_pairs={{0,2},{1,3},{4,0},{5,1},{8,4},{9,5},{12,8},{13,9},{14,12},{15,13},... | collective-permute-start | bytes 442376 | tf_op jit(solution)/shard_map/ppermute | solution.py:70
  34.9 20.3 %collective-permute-start.13 = (bf16[32,2304]{1,0:T(8,128)(2,1)S(1)}, bf16[32,2304]{1,0:T(8,128)(2,1)S(1)}, u32[]{:S(2)}, u32[]{:S(2)}) collective-permute-start(bf16[32,2304]{1,0:T(8,128)(2,1)S(1)} %collective-permute-done.12.refs_10_), channel_id=1, source_target_pairs={{0,2},{1,3},{4,0},{5,1},{8,4},{9,5},{12,8},{13,9},{14,12},{15,13},... | collective-permute-start | bytes 442376 | tf_op jit(solution)/shard_map/ppermute | solution.py:70
  35.4 7.6 %collective-permute-start.31 = (bf16[128,128]{1,0:T(8,128)(2,1)S(1)}, bf16[128,128]{1,0:T(8,128)(2,1)S(1)}, u32[]{:S(2)}, u32[]{:S(2)}) collective-permute-start(bf16[128,128]{1,0:T(8,128)(2,1)S(1)} %pad_maximum_fusion.1.refs_20_.refs_12_), channel_id=1, source_target_pairs={{0,12},{1,13},{2,14},{3,15},{4,0},{5,1},{6,2},{7,3},{8,4},{9,5},{1... | collective-permute-start | bytes 98312 | tf_op jit(solution)/shard_map/ppermute | solution.py:153
  56.0 6.5 %collective-permute-start.39 = (bf16[32,2304]{1,0:T(8,128)(2,1)}, bf16[32,2304]{1,0:T(8,128)(2,1)S(1)}, u32[]{:S(2)}, u32[]{:S(2)}) collective-permute-start(bf16[32,2304]{1,0:T(8,128)(2,1)} %collective-permute-done.5.refs_14_), channel_id=1, source_target_pairs={{0,1},{1,0},{2,3},{3,2},{4,5},{5,4},{6,7},{7,6},{8,9},{9,8},{10,11... | collective-permute-start | bytes 442376 | tf_op jit(solution)/shard_map/ppermute | solution.py:73
  57.8 8.0 %collective-permute-start.2 = (bf16[32,2304]{1,0:T(8,128)(2,1)S(1)}, bf16[32,2304]{1,0:T(8,128)(2,1)}, u32[]{:S(2)}, u32[]{:S(2)}) collective-permute-start(bf16[32,2304]{1,0:T(8,128)(2,1)S(1)} %collective-permute-done.1.refs_12_), channel_id=1, source_target_pairs={{0,4},{1,5},{4,8},{5,9},{8,12},{9,13},{12,14},{13,15},{14,10},{15,... | collective-permute-start | bytes 442376 | tf_op jit(solution)/shard_map/ppermute | solution.py:69
  59.1 6.9 %collective-permute-start.14 = (bf16[32,2304]{1,0:T(8,128)(2,1)S(1)}, bf16[32,2304]{1,0:T(8,128)(2,1)}, u32[]{:S(2)}, u32[]{:S(2)}) collective-permute-start(bf16[32,2304]{1,0:T(8,128)(2,1)S(1)} %collective-permute-done.13.refs_18_), channel_id=1, source_target_pairs={{0,2},{1,3},{4,0},{5,1},{8,4},{9,5},{12,8},{13,9},{14,12},{15,13},... | collective-permute-start | bytes 442376 | tf_op jit(solution)/shard_map/ppermute | solution.py:70
  63.1 7.0 %collective-permute-start.10 = (bf16[32,2304]{1,0:T(8,128)(2,1)}, bf16[32,2304]{1,0:T(8,128)(2,1)}, u32[]{:S(2)}, u32[]{:S(2)}) collective-permute-start(bf16[32,2304]{1,0:T(8,128)(2,1)} %collective-permute-done.9.refs_16_), channel_id=1, source_target_pairs={{0,2},{1,3},{4,0},{5,1},{8,4},{9,5},{12,8},{13,9},{14,12},{15,13},... | collective-permute-start | bytes 442376 | tf_op jit(solution)/shard_map/ppermute | solution.py:70
  63.9 7.0 %collective-permute-start.6 = (bf16[32,2304]{1,0:T(8,128)(2,1)}, bf16[32,2304]{1,0:T(8,128)(2,1)}, u32[]{:S(2)}, u32[]{:S(2)}) collective-permute-start(bf16[32,2304]{1,0:T(8,128)(2,1)} %collective-permute-done.5.refs_14_), channel_id=1, source_target_pairs={{0,4},{1,5},{4,8},{5,9},{8,12},{9,13},{12,14},{13,15},{14,10},{15,... | collective-permute-start | bytes 442376 | tf_op jit(solution)/shard_map/ppermute | solution.py:69
  65.8 7.7 %collective-permute-start.16 = (bf16[32,2304]{1,0:T(8,128)(2,1)}, bf16[32,2304]{1,0:T(8,128)(2,1)}, u32[]{:S(2)}, u32[]{:S(2)}) collective-permute-start(bf16[32,2304]{1,0:T(8,128)(2,1)} %collective-permute-done.2.refs_0_), channel_id=1, source_target_pairs={{0,4},{1,5},{4,8},{5,9},{8,12},{9,13},{12,14},{13,15},{14,10},{15,... | collective-permute-start | bytes 442376 | tf_op jit(solution)/shard_map/ppermute | solution.py:75
  66.0 7.6 %collective-permute-start.18 = (bf16[32,2304]{1,0:T(8,128)(2,1)}, bf16[32,2304]{1,0:T(8,128)(2,1)}, u32[]{:S(2)}, u32[]{:S(2)}) collective-permute-start(bf16[32,2304]{1,0:T(8,128)(2,1)} %collective-permute-done.14.refs_6_), channel_id=1, source_target_pairs={{0,2},{1,3},{4,0},{5,1},{8,4},{9,5},{12,8},{13,9},{14,12},{15,13},... | collective-permute-start | bytes 442376 | tf_op jit(solution)/shard_map/ppermute | solution.py:75
  70.1 29.3 %collective-permute-start.3 = (bf16[32,2304]{1,0:T(8,128)(2,1)}, bf16[32,2304]{1,0:T(8,128)(2,1)S(1)}, u32[]{:S(2)}, u32[]{:S(2)}) collective-permute-start(bf16[32,2304]{1,0:T(8,128)(2,1)} %collective-permute-done.2.refs_0_), channel_id=1, source_target_pairs={{0,1},{1,0},{2,3},{3,2},{4,5},{5,4},{6,7},{7,6},{8,9},{9,8},{10,11... | collective-permute-start | bytes 442376 | tf_op jit(solution)/shard_map/ppermute | solution.py:73
  70.9 28.5 %collective-permute-start.11 = (bf16[32,2304]{1,0:T(8,128)(2,1)}, bf16[32,2304]{1,0:T(8,128)(2,1)S(1)}, u32[]{:S(2)}, u32[]{:S(2)}) collective-permute-start(bf16[32,2304]{1,0:T(8,128)(2,1)} %collective-permute-done.10.refs_4_), channel_id=1, source_target_pairs={{0,1},{1,0},{2,3},{3,2},{4,5},{5,4},{6,7},{7,6},{8,9},{9,8},{10,11... | collective-permute-start | bytes 442376 | tf_op jit(solution)/shard_map/ppermute | solution.py:73
  73.5 25.9 %collective-permute-start.7 = (bf16[32,2304]{1,0:T(8,128)(2,1)}, bf16[32,2304]{1,0:T(8,128)(2,1)S(1)}, u32[]{:S(2)}, u32[]{:S(2)}) collective-permute-start(bf16[32,2304]{1,0:T(8,128)(2,1)} %collective-permute-done.6.refs_2_), channel_id=1, source_target_pairs={{0,1},{1,0},{2,3},{3,2},{4,5},{5,4},{6,7},{7,6},{8,9},{9,8},{10,11... | collective-permute-start | bytes 442376 | tf_op jit(solution)/shard_map/ppermute | solution.py:73
  73.5 25.9 %collective-permute-start.17 = (bf16[32,2304]{1,0:T(8,128)(2,1)}, bf16[32,2304]{1,0:T(8,128)(2,1)S(1)}, u32[]{:S(2)}, u32[]{:S(2)}) collective-permute-start(bf16[32,2304]{1,0:T(8,128)(2,1)} %collective-permute-done.16.refs_8_), channel_id=1, source_target_pairs={{0,1},{1,0},{2,3},{3,2},{4,5},{5,4},{6,7},{7,6},{8,9},{9,8},{10,11... | collective-permute-start | bytes 442376 | tf_op jit(solution)/shard_map/ppermute | solution.py:77
  74.0 25.4 %collective-permute-start.19 = (bf16[32,2304]{1,0:T(8,128)(2,1)}, bf16[32,2304]{1,0:T(8,128)(2,1)S(1)}, u32[]{:S(2)}, u32[]{:S(2)}) collective-permute-start(bf16[32,2304]{1,0:T(8,128)(2,1)} %collective-permute-done.18.refs_10_), channel_id=1, source_target_pairs={{0,1},{1,0},{2,3},{3,2},{4,5},{5,4},{6,7},{7,6},{8,9},{9,8},{10,11... | collective-permute-start | bytes 442376 | tf_op jit(solution)/shard_map/ppermute | solution.py:77
  (52 other events, 332.1 us)

commit v3 on v2

v3 whole, which is shorter than its diff:
```python
import functools

import jax
import jax.numpy as jnp
import numpy as np
from jax import lax
from jax.experimental import pallas as pl
from jax.experimental.pallas import tpu as pltpu
from jax.sharding import PartitionSpec as P

BLOCK = 128
AXES = ("seq", "adapter")
CHUNKS = 2


def ring_order(n):
    return [2 * z for z in range(n // 2)] + [2 * z + 1 for z in reversed(range(n // 2))]


def ring_distances(n):
    steps = [0]
    for hop in range(1, n // 2):
        steps += [-hop, hop]
    return steps + [n // 2]


def ring_perm(n, way):
    order = ring_order(n)
    return [(2 * s + c, 2 * order[(pos + way) % n] + c) for pos, s in enumerate(order) for c in range(2)]


def flip_perm(n, y, c):
    return [(2 * s + k, 2 * (s ^ y) + (k ^ c)) for s in range(n) for k in range(2)]


def z_perm(n, shift):
    nz = n // 2
    return [
        (2 * (2 * z + y) + c, 2 * (2 * ((z - shift) % nz) + y) + c)
        for z in range(nz)
        for y in range(2)
        for c in range(2)
    ]


def device_table(n):
    order, nz = ring_order(n), n // 2
    place = {s: pos for pos, s in enumerate(order)}
    table = np.zeros((2 * n, 3, n), np.int32)
    for s in range(n):
        for c in range(2):
            for i, distance in enumerate(ring_distances(n)):
                chip = order[(place[s] + distance) % n]
                table[2 * s + c, 0, i] = chip
                for core in range(2):
                    turn = (chip // 2 - s // 2) % nz
                    table[2 * s + c, 1 + core, i] = 4 * turn + 2 * ((chip ^ s) & 1) + (core ^ c)
    return table.reshape(2 * n, -1)


def gather_ring(chunks, n):
    ahead, back = ring_perm(n, 1), ring_perm(n, -1)
    swap = flip_perm(n, 0, 1)
    own = [[x] for x in chunks]
    other = [[lax.ppermute(x, AXES, swap)] for x in chunks]
    up, down = list(chunks), list(chunks)
    for hop in range(1, n // 2):
        for k in range(len(chunks)):
            up[k] = lax.ppermute(up[k], AXES, ahead)
            down[k] = lax.ppermute(down[k], AXES, back)
        for k in range(len(chunks)):
            own[k] += [up[k], down[k]]
            other[k] += [lax.ppermute(x, AXES, swap) for x in (up[k], down[k])]
    for k in range(len(chunks)):
        end = lax.ppermute(*((down[k], AXES, back) if k % 2 else (up[k], AXES, ahead)))
        own[k].append(end)
        other[k].append(lax.ppermute(end, AXES, swap))
    return own, other


def pick_kernel(n, blocks_apart, adapters, place, keep, keep_far, give, give_far, *outs):
    nz, held = n // 2, keep.shape[0]
    s, c = place[0], place[1]
    z, y = s >> 1, s & 1
    for shift, out in enumerate(outs):
        seat = z - shift
        seat = jnp.where(seat < 0, seat + nz, seat)
        adapter = adapters[(seat * 2 * blocks_apart) // BLOCK]
        for index in range(held):

            @pl.when(adapter == c * held + index)
            def _():
                out[y] = keep[index]
                out[1 - y] = keep_far[index]

            @pl.when(adapter == (1 - c) * held + index)
            def _():
                out[y] = give[index]
                out[1 - y] = give_far[index]


def split_kernel(place, down_ref, keep, give):
    half = keep.shape[1]
    c = place[1]
    for ref, core in ((keep, c), (give, 1 - c)):
        ref[...] = down_ref[:, pl.ds(pl.multiple_of(core * half, half), half), :].astype(jnp.bfloat16)


def whole(count):
    return [pl.BlockSpec(memory_space=pltpu.VMEM)] * count


def in_vmem(arrays):
    return [pltpu.with_memory_space_constraint(x, pltpu.VMEM) for x in arrays]


def call(kernel, scalars, arrays, after, outs, scratch=(), limit=8, flops=0):
    operands = len(scalars) + len(arrays)

    def body(*refs):
        kernel(*refs[:operands], *refs[operands + len(after) :])

    return pl.pallas_call(
        body,
        out_shape=[pltpu.VMEM(shape, dtype) for shape, dtype in outs],
        in_specs=[pl.BlockSpec(memory_space=pltpu.SMEM)] * len(scalars)
        + whole(len(arrays))
        + [pl.BlockSpec(memory_space=pl.ANY)] * len(after),
        out_specs=whole(len(outs)),
        scratch_shapes=list(scratch),
        compiler_params=pltpu.CompilerParams(vmem_limit_bytes=limit << 20),
        cost_estimate=pl.CostEstimate(flops=flops, bytes_accessed=0, transcendentals=0),
    )(*scalars, *in_vmem(arrays), *after)


def assemble(place, pieces, held, entries):
    rows, depth = pieces[0].shape
    chunks = held.shape[1] // depth
    c = place[1]
    for i in range(entries):
        for k in range(chunks):
            for far in range(2):
                core = 1 - c if far else c
                row = pl.multiple_of(i * 2 * rows + core * rows, rows)
                held[pl.ds(row, rows), k * depth : (k + 1) * depth] = pieces[(i * chunks + k) * 2 + far][...]


def shrink_kernel(nz, count, place, *refs):
    parts, pieces, (out, held, turned, factor) = refs[:nz], refs[nz : nz + count], refs[nz + count :]
    rows, half = out.shape[0], factor.shape[0]
    z = place[0] >> 1
    assemble(place, pieces, held, 1)
    for j, part in enumerate(parts):
        turned[j] = part[...]
    width = turned.shape[3]
    for at in range(nz):
        turn = jnp.where(at < z, at - z + nz, at - z)
        for y in range(2):
            first = (2 * at + y) * width
            factor[:, first : first + width] = turned[turn, y]
    shrink = lax.dot_general(
        held[...], factor[...], (((1,), (1,)), ((), ())), preferred_element_type=jnp.float32
    )
    high = shrink.astype(jnp.bfloat16)
    low = (shrink - high.astype(jnp.float32)).astype(jnp.bfloat16)
    out[...] = jnp.concatenate([high[:rows], high[rows:], low[:rows], low[rows:]], 1)


class Shrink:
    def __init__(self, down, place, n):
        self.n, self.place = n, place
        held, self.width, rank = down.shape
        self.half = rank // 2
        part = ((held, self.half, self.width), jnp.bfloat16)
        keep, give = call(split_kernel, [place], [jnp.swapaxes(down, 1, 2)], [], [part, part])
        self.factors = [keep] + [
            lax.ppermute(x, AXES, flip_perm(n, y, c)) for x, y, c in ((keep, 1, 0), (give, 0, 1), (give, 1, 1))
        ]

    def pick(self, adapters, rows, after):
        nz = self.n // 2
        self.picks = call(
            functools.partial(pick_kernel, self.n, 2 * rows),
            [adapters, self.place],
            self.factors,
            after,
            [((2, self.half, self.width), jnp.bfloat16)] * nz,
        )
        self.parts = [self.picks[0]] + [
            lax.ppermute(self.picks[shift], AXES, z_perm(self.n, shift)) for shift in range(1, nz)
        ]

    def multiply(self, pieces, after):
        n, rows = self.n, pieces[0].shape[0]
        (self.piece,) = call(
            functools.partial(shrink_kernel, n // 2, len(pieces)),
            [self.place],
            [*self.parts, *pieces],
            after,
            [((rows, 4 * self.half), jnp.bfloat16)],
            [
                pltpu.VMEM((2 * rows, n * self.width), jnp.bfloat16),
                pltpu.VMEM((n // 2, 2, self.half, self.width), jnp.bfloat16),
                pltpu.VMEM((self.half, n * self.width), jnp.bfloat16),
            ],
        )
        self.near = jnp.concatenate(
            [self.piece]
            + [lax.ppermute(self.piece, AXES, flip_perm(n, y, c)) for y, c in ((0, 1), (1, 0), (1, 1))],
            0,
        )
        return [self.near] + [lax.ppermute(self.near, AXES, z_perm(n, shift)) for shift in range(1, n // 2)]


def load_kernel(w_ref, up_ref, w_out, up_out, held, sems):
    parts = sems.shape[0] - 1
    depth, rank = w_ref.shape[0] // parts, up_ref.shape[1]
    copies = [
        pltpu.make_async_copy(
            w_ref.at[pl.ds(k * depth, depth), :], w_out.at[pl.ds(k * depth, depth), :], sems.at[k]
        )
        for k in range(parts)
    ]
    copies = [pltpu.make_async_copy(up_ref, held, sems.at[parts])] + copies
    for copy in copies:
        copy.start()
    copies[0].wait()
    for adapter in range(up_ref.shape[0]):
        factor = held[adapter].astype(jnp.bfloat16)
        up_out[adapter, :rank, :] = factor
        up_out[adapter, rank:, :] = factor
    for copy in copies[1:]:
        copy.wait()


def load(weight, up):
    adapters, rank, width = up.shape
    return pl.pallas_call(
        load_kernel,
        out_shape=[
            pltpu.VMEM(weight.shape, weight.dtype),
            pltpu.VMEM((adapters, 2 * rank, width), jnp.bfloat16),
        ],
        in_specs=[pl.BlockSpec(memory_space=pltpu.HBM)] * 2,
        out_specs=whole(2),
        scratch_shapes=[pltpu.VMEM(up.shape, up.dtype), pltpu.SemaphoreType.DMA((9,))],
        compiler_params=pltpu.CompilerParams(vmem_limit_bytes=8 << 20),
        cost_estimate=pl.CostEstimate(
            flops=0, bytes_accessed=2 * weight.size + 4 * up.size, transcendentals=0
        ),
    )(*(pltpu.with_memory_space_constraint(x, pltpu.HBM) for x in (weight, up)))


def tile_width(width):
    return 768 if width % 768 == 0 else width


def base_kernel(entries, count, place, *refs):
    pieces, w_ref, (base, held) = refs[:count], refs[count], refs[count + 1 :]
    assemble(place, pieces, held, entries)
    width = w_ref.shape[1]
    columns = tile_width(width)
    for j in range(0, width, columns):
        at = slice(j, j + columns)
        base[:, at] = jnp.dot(held[...], w_ref[:, at], preferred_element_type=jnp.float32)


def base_rows(pieces, entries, weight, place, after):
    rows, depth = pieces[0].shape
    total = 2 * rows * entries
    shape = (total, weight.shape[1])
    (base,) = call(
        functools.partial(base_kernel, entries, len(pieces)),
        [place],
        [*pieces, weight],
        after,
        [(shape, jnp.float32)],
        [pltpu.VMEM((total, weight.shape[0]), jnp.bfloat16)],
        limit=8,
        flops=2 * total * weight.size,
    )
    return base


def collect_shrink(n, begin, entries, table, parts, near, shrink):
    rows = near.shape[0] // (2 * n)
    half = near.shape[1] // 4
    for j, part in enumerate(parts):
        near[j * 4 * rows : (j + 1) * 4 * rows, :] = part[...]
    for i in range(entries):
        zero, one = (
            near[pl.ds(pl.multiple_of(table[(1 + core) * n + begin + i] * rows, rows), rows), :]
            for core in range(2)
        )
        for core in range(2):
            a, b = core * half, (2 + core) * half
            first = (2 * i + core) * rows
            shrink[first : first + rows, :] = jnp.concatenate(
                [zero[:, a : a + half], one[:, a : a + half], zero[:, b : b + half], one[:, b : b + half]], 1
            )


def finish_chip(first, adapters, live, base, shrink, up_ref, at):
    of_block = first // BLOCK
    delta = jnp.dot(shrink, up_ref[adapters[of_block], :, at], preferred_element_type=jnp.float32)
    row = lax.broadcasted_iota(jnp.int32, delta.shape, 0) + (first - of_block * BLOCK)
    return jnp.where(row < live[of_block], base + delta, 0.0).astype(jnp.bfloat16)


def finish_kernel(n, counts, table, place, adapters, live, *refs):
    base_count, part_count = counts
    bases, refs = refs[:base_count], refs[base_count:]
    parts, refs = refs[:part_count], refs[part_count:]
    up_ref, out_ref, near, shrink, block, sems = refs
    chip = 2 * near.shape[0] // (2 * n)
    entries = shrink.shape[0] // chip
    collect_shrink(n, 0, entries, table, parts, near, shrink)
    width = up_ref.shape[2]
    columns = tile_width(width)
    copies = []
    for j in range(width // columns):
        at = slice(j * columns, (j + 1) * columns)
        i = 0
        for base in bases:
            for k in range(base.shape[0] // chip):
                first = table[i] * chip
                rows = slice(i * chip, (i + 1) * chip)
                block[j, rows, :] = finish_chip(
                    first, adapters, live, base[k * chip : (k + 1) * chip, at], shrink[rows, :], up_ref, at
                )
                copies.append(
                    pltpu.make_async_copy(
                        block.at[j, pl.ds(i * chip, chip), :],
                        out_ref.at[pl.ds(pl.multiple_of(first, chip), chip), pl.ds(j * columns, columns)],
                        sems.at[j, i],
                    )
                )
                copies[-1].start()
                i += 1
    for copy in copies:
        copy.wait()


def last_kernel(n, counts, table, place, adapters, live, *refs):
    piece_count, part_count = counts
    pieces, refs = refs[:piece_count], refs[piece_count:]
    parts, refs = refs[:part_count], refs[part_count:]
    w_ref, up_ref, _, out_ref, held, near, shrink, block, sems = refs
    chip = held.shape[0]
    assemble(place, pieces, held, 1)
    collect_shrink(n, n - 1, 1, table, parts, near, shrink)
    width = up_ref.shape[2]
    columns = tile_width(width)
    first = table[n - 1] * chip
    copies = []
    for j in range(width // columns):
        at = slice(j * columns, (j + 1) * columns)
        base = jnp.dot(held[...], w_ref[:, at], preferred_element_type=jnp.float32)
        block[j] = finish_chip(first, adapters, live, base, shrink[...], up_ref, at)
        copies.append(
            pltpu.make_async_copy(
                block.at[j],
                out_ref.at[pl.ds(pl.multiple_of(first, chip), chip), pl.ds(j * columns, columns)],
                sems.at[j],
            )
        )
        copies[-1].start()
    for copy in copies:
        copy.wait()


def finish(kernel, n, counts, scalars, arrays, into, total, rows, up, held, flops):
    _, wide, width = up.shape
    columns = tile_width(width)
    tiles = width // columns
    sems = (tiles,) if held else (tiles, n - 1)
    return pl.pallas_call(
        functools.partial(kernel, n, counts),
        out_shape=jax.ShapeDtypeStruct((total, width), jnp.bfloat16),
        in_specs=[pl.BlockSpec(memory_space=pltpu.SMEM)] * len(scalars)
        + whole(len(arrays))
        + [pl.BlockSpec(memory_space=pl.ANY)] * len(into),
        out_specs=pl.BlockSpec(memory_space=pl.ANY),
        scratch_shapes=held
        + [
            pltpu.VMEM((total, wide), jnp.bfloat16),
            pltpu.VMEM((rows, wide), jnp.bfloat16),
            pltpu.VMEM((tiles, rows, columns), jnp.bfloat16),
            pltpu.SemaphoreType.DMA(sems),
        ],
        input_output_aliases={len(scalars) + len(arrays): 0} if into else {},
        compiler_params=pltpu.CompilerParams(vmem_limit_bytes=12 << 20),
        cost_estimate=pl.CostEstimate(flops=flops, bytes_accessed=2 * rows * width, transcendentals=0),
    )(*scalars, *in_vmem(arrays), *into)


def on_device(n, tokens, weight, down, up, adapter_per_block, rows_per_block):
    rows = tokens.shape[0]
    chip, total = 2 * rows, 2 * n * rows
    depth = tokens.shape[1] // CHUNKS
    adapters = adapter_per_block[:, 0]
    device = lax.axis_index(AXES)
    table = lax.dynamic_index_in_dim(jnp.asarray(device_table(n)), device, 0, False)
    place = jnp.stack([device >> 1, device & 1]).astype(jnp.int32)
    own, other = gather_ring([tokens[:, k * depth : (k + 1) * depth] for k in range(CHUNKS)], n)
    shrink = Shrink(down, place, n)
    weight, up = load(weight, up)

    def pieces(begin, end):
        return [x[k][i] for i in range(begin, end) for k in range(CHUNKS) for x in (own, other)]

    def arrived(hop):
        return [x[i] for x in own for i in range(2 * hop - 1, min(2 * hop + 1, n))]

    shrink.pick(adapters, rows, [*arrived(1), weight])
    bases = [base_rows(pieces(0, 1), 1, weight, place, [shrink.picks[0]])]
    parts = shrink.multiply(pieces(0, 1), [*arrived(2), *bases])
    for hop in range(1, n // 2):
        after = {1: [shrink.piece], 2: [shrink.near, *arrived(3)]}.get(hop, [])
        after.append(bases[-1])
        bases.append(base_rows(pieces(2 * hop - 1, 2 * hop + 1), 2, weight, place, after))
    scalars = (table, place, adapters, rows_per_block)
    out = finish(
        finish_kernel, n, (len(bases), len(parts)), scalars, [*bases, *parts, up],
        [], total, total - chip, up, [], 0,
    )
    last = pieces(n - 1, n)
    return finish(
        last_kernel, n, (len(last), len(parts)), scalars, [*last, *parts, weight, up],
        [out], total, chip, up, [pltpu.VMEM((chip, weight.shape[0]), jnp.bfloat16)], 2 * chip * weight.size,
    )


def solution(mesh):
    placed = (
        P(("groups", "seq", "adapter"), None),
        P(None, ("seq", "adapter")),
        P(("groups", "adapter"), "seq", None),
        P("groups", None, ("seq", "adapter")),
        P("groups", None),
        P("groups"),
    )
    return jax.shard_map(
        functools.partial(on_device, mesh.shape["seq"]),
        mesh=mesh,
        in_specs=placed,
        out_specs=P("groups", ("seq", "adapter")),
        check_vma=False,
    )
```

time: 113 us -> 102 us (0.903)
  starting transfers between devices: 35.1 us -> 30 us
  local copies, waits for them, and re-layouts: 21.7 us -> 18.5 us
  matrix products: 1.61 us -> 0 us
    ppermute x12, starting transfers between devices: 16.9 us -> 11.3 us  [the longest x3 5.62 us: pick(): lax.ppermute(self.picks[shift], AXES, z_perm(self.n, shift))]
    ppermute x6, waiting for transfers between devices: 0.89 us -> 4.6 us  [gather_ring(): down[k] = lax.ppermute(down[k], AXES, back)]
    ppermute x2, waiting for transfers between devices: 2.59 us -> 0.01 us  [gather_ring(): lax.ppermute(*((down[k], AXES, back) if k % 2 else (up[k], AXES, ahead)))]
    unnamed x68 -> x44, local copies, waits for them, and re-layouts: 18.5 us -> 16.8 us
    dot_general x1 -> x0, matrix products: 1.61 us -> none  [spread_shrink(): jnp.einsum('tzyk,zyrk->tr', turned, factor, preferred_element_type=jnp.fl...]
    ppermute x12, starting transfers between devices: 1.61 us -> 3.17 us  [gather_ring(): other[k] += [lax.ppermute(x, AXES, swap) for x in (up[k], down[k])]]
    reshape x1 -> x0, local copies, waits for them, and re-layouts: 1.46 us -> none  [spread_shrink(): turned = lax.dynamic_slice_in_dim(jnp.concatenate([chip_rows, chip_rows],...]
    ppermute x12, waiting for transfers between devices: 16.4 us -> 15 us  [the longest x3 6.43 us: multiply(): lax.ppermute(self.piece, AXES, flip_perm(n, y, c))]
  transfers between devices with their start and end apart: 42 -> 42, of which waited for: 7 -> 8; matrix products, arithmetic and copies ran while one was open for 4% -> 1% of each run, Pallas kernels for 17% -> 28%
where the time goes in v3:
time: 102 us
  Pallas kernels  32.8 us (32%)
  starting transfers between devices  30 us (29%)
  waiting for transfers between devices  19.7 us (19%)
  local copies, waits for them, and re-layouts  18.5 us (18%)
    pallas_call x7, Pallas kernels, call(): pl.pallas_call(body, out_shape=[pltpu.VMEM(shape, dtype) for shape, dtype...  18.3 us
    unnamed x44, local copies, waits for them, and re-layouts  16.8 us
    ppermute x6, starting transfers between devices, gather_ring(): up[k] = lax.ppermute(up[k], AXES, ahead)  8.2 us
    pallas_call x1, Pallas kernels, load(): pl.pallas_call(load_kernel, out_shape=[pltpu.VMEM(weight.shape, weight.dt...  7.87 us
    pallas_call x2, Pallas kernels, finish(): pl.pallas_call(functools.partial(kernel, n, counts), out_shape=jax.ShapeD...  6.59 us
    ppermute x3, waiting for transfers between devices, multiply(): lax.ppermute(self.piece, AXES, flip_perm(n, y, c))  6.43 us
    ppermute x3, waiting for transfers between devices, pick(): lax.ppermute(self.picks[shift], AXES, z_perm(self.n, shift))  5.65 us
    ppermute x3, starting transfers between devices, pick(): lax.ppermute(self.picks[shift], AXES, z_perm(self.n, shift))  5.62 us
  transfers between devices with their start and end apart: 42, of which 8 were waited for; matrix products, arithmetic and copies ran while one was open for 1% of the time, Pallas kernels for 28%

profile of v3, /device:TPU:0, one launch (start us, length us, event | category | flops | bytes accessed | tf_op | source)
XLA Modules:
  0.0 101.5 jit_solution(352260811745395842)
XLA Ops:
  1.0 3.1 %collective-permute-start = (bf16[32,2304]{1,0:T(8,128)(2,1)S(1)}, bf16[32,2304]{1,0:T(8,128)(2,1)S(1)}, u32[]{:S(2)}, u32[]{:S(2)}) collective-permute-start(bf16[32,2304]{1,0:T(8,128)(2,1)S(1)} %get-tuple-element.22.refs_1_.refs_5_), channel_id=1, source_target_pairs={{0,4},{1,5},{4,8},{5,9},{8,12},{9,13},{12,14},{13,15},{14,10},{15,... | collective-permute-start | bytes 442376 | tf_op jit(solution)/shard_map/ppermute | solution.py:69
  5.9 2.0 %collective-permute-start.12 = (bf16[2,32,576]{2,1,0:T(8,128)(2,1)S(1)}, bf16[2,32,576]{2,1,0:T(8,128)(2,1)S(1)}, u32[]{:S(2)}, u32[]{:S(2)}) collective-permute-start(bf16[2,32,576]{2,1,0:T(8,128)(2,1)S(1)} %get-tuple-element.14), channel_id=1, source_target_pairs={{0,3},{1,2},{2,1},{3,0},{4,7},{5,6},{6,5},{7,4},{8,11},{9,10},{10,... | collective-permute-start | bytes 221192 | tf_op jit(solution)/shard_map/ppermute | solution.py:177
  8.0 2.9 %collective-permute-done.10.refs_3_ = bf16[2,32,576]{2,1,0:T(8,128)(2,1)S(1)} collective-permute-done((bf16[2,32,576]{2,1,0:T(8,128)(2,1)S(1)}, bf16[2,32,576]{2,1,0:T(8,128)(2,1)S(1)}, u32[]{:S(2)}, u32[]{:S(2)}) %collective-permute-start.10) | collective-permute-done | bytes 73760 | tf_op jit(solution)/shard_map/ppermute | solution.py:177
  10.9 1.6 %collective-permute-start.14 = (bf16[32,2304]{1,0:T(8,128)(2,1)S(1)}, bf16[32,2304]{1,0:T(8,128)(2,1)S(1)}, u32[]{:S(2)}, u32[]{:S(2)}) collective-permute-start(bf16[32,2304]{1,0:T(8,128)(2,1)S(1)} %get-tuple-element.21.refs_3_.refs_7_), channel_id=1, source_target_pairs={{0,4},{1,5},{4,8},{5,9},{8,12},{9,13},{12,14},{13,15},{14,10},{15,... | collective-permute-start | bytes 442376 | tf_op jit(solution)/shard_map/ppermute | solution.py:69
  14.6 1.6 %collective-permute-start.1 = (bf16[32,2304]{1,0:T(8,128)(2,1)S(1)}, bf16[32,2304]{1,0:T(8,128)(2,1)}, u32[]{:S(2)}, u32[]{:S(2)}) collective-permute-start(bf16[32,2304]{1,0:T(8,128)(2,1)S(1)} %collective-permute-done.refs_6_.refs_1_), channel_id=1, source_target_pairs={{0,4},{1,5},{4,8},{5,9},{8,12},{9,13},{12,14},{13,15},{14,10},{15,... | collective-permute-start | bytes 442376 | tf_op jit(solution)/shard_map/ppermute | solution.py:69
  16.7 7.9 %shard_map.74 = (bf16[4608,2304]{1,0:T(8,128)(2,1)S(1)}, bf16[4,128,2304]{2,1,0:T(8,128)(2,1)S(1)}) custom-call(bf16[4608,2304]{1,0:T(8,128)(2,1)} %w_ref.1, f32[4,64,2304]{2,1,0:T(8,128)} %up_ref.1), custom_call_target="tpu_custom_call" | custom-call | bytes 23592960 | tf_op jit(solution)/shard_map/pallas_call | solution.py:238
  25.3 5.0 %collective-permute-start.15 = (bf16[2,32,576]{2,1,0:T(8,128)(2,1)S(1)}, bf16[2,32,576]{2,1,0:T(8,128)(2,1)S(1)}, u32[]{:S(2)}, u32[]{:S(2)}) collective-permute-start(bf16[2,32,576]{2,1,0:T(8,128)(2,1)S(1)} %get-tuple-element.17), channel_id=1, source_target_pairs={{0,12},{1,13},{2,14},{3,15},{4,0},{5,1},{6,2},{7,3},{8,4},{9,5},{1... | collective-permute-start | bytes 221192 | tf_op jit(solution)/shard_map/ppermute | solution.py:190
  30.9 2.1 %collective-permute-done.15.refs_2_ = bf16[2,32,576]{2,1,0:T(8,128)(2,1)S(1)} collective-permute-done((bf16[2,32,576]{2,1,0:T(8,128)(2,1)S(1)}, bf16[2,32,576]{2,1,0:T(8,128)(2,1)S(1)}, u32[]{:S(2)}, u32[]{:S(2)}) %collective-permute-start.15) | collective-permute-done | bytes 73760 | tf_op jit(solution)/shard_map/ppermute | solution.py:190
  33.8 3.5 %collective-permute-done.16.refs_3_ = bf16[2,32,576]{2,1,0:T(8,128)(2,1)S(1)} collective-permute-done((bf16[2,32,576]{2,1,0:T(8,128)(2,1)S(1)}, bf16[2,32,576]{2,1,0:T(8,128)(2,1)S(1)}, u32[]{:S(2)}, u32[]{:S(2)}) %collective-permute-start.16) | collective-permute-done | bytes 73760 | tf_op jit(solution)/shard_map/ppermute | solution.py:190
  39.1 3.4 %collective-permute-done.6.refs_12_.refs_7_ = bf16[32,2304]{1,0:T(8,128)(2,1)} collective-permute-done((bf16[32,2304]{1,0:T(8,128)(2,1)S(1)}, bf16[32,2304]{1,0:T(8,128)(2,1)}, u32[]{:S(2)}, u32[]{:S(2)}) %collective-permute-start.6) | collective-permute-done | bytes 147488 | tf_op jit(solution)/shard_map/ppermute | solution.py:70
  43.2 2.0 %collective-permute-start.7 = (bf16[32,2304]{1,0:T(8,128)(2,1)}, bf16[32,2304]{1,0:T(8,128)(2,1)}, u32[]{:S(2)}, u32[]{:S(2)}) collective-permute-start(bf16[32,2304]{1,0:T(8,128)(2,1)} %collective-permute-done.6.refs_12_.refs_7_), channel_id=1, source_target_pairs={{0,2},{1,3},{4,0},{5,1},{8,4},{9,5},{12,8},{13,9},{14,12},{15,13},... | collective-permute-start | bytes 442376 | tf_op jit(solution)/shard_map/ppermute | solution.py:70
  47.3 1.3 %collective-permute-start.37 = (bf16[32,2304]{1,0:T(8,128)(2,1)}, bf16[32,2304]{1,0:T(8,128)(2,1)}, u32[]{:S(2)}, u32[]{:S(2)}) collective-permute-start(bf16[32,2304]{1,0:T(8,128)(2,1)} %collective-permute-done.21.refs_11_.refs_3_), channel_id=1, source_target_pairs={{0,4},{1,5},{4,8},{5,9},{8,12},{9,13},{12,14},{13,15},{14,10},{15,... | collective-permute-start | bytes 442376 | tf_op jit(solution)/shard_map/ppermute | solution.py:69
  48.6 4.3 %shard_map.76.refs_13_.refs_11_.refs_0_ = f32[64,2304]{1,0:T(8,128)S(1)} custom-call(s32[2]{0:T(128)S(1)} %pad_add_fusion.refs_0_.refs_1_.place, bf16[32,2304]{1,0:T(8,128)(2,1)S(1)} %get-tuple-element.22.refs_1_.refs_5_, bf16[32,2304]{1,0:T(8,128)(2,1)S(1)} %collective-permute-done.18.refs_2_.refs_6_, ...), custom_call_target="tpu_custom_call" | custom-call | flops 1358954496 | tf_op jit(solution)/shard_map/pallas_call | solution.py:123
  54.6 1.2 %collective-permute-done.22 = bf16[32,128]{1,0:T(8,128)(2,1)S(1)} collective-permute-done((bf16[32,128]{1,0:T(8,128)(2,1)S(1)}, bf16[32,128]{1,0:T(8,128)(2,1)S(1)}, u32[]{:S(2)}, u32[]{:S(2)}) %collective-permute-start.22) | collective-permute-done | bytes 8224 | tf_op jit(solution)/shard_map/ppermute | solution.py:209
  56.5 2.9 %collective-permute-done.23 = bf16[32,128]{1,0:T(8,128)(2,1)S(1)} collective-permute-done((bf16[32,128]{1,0:T(8,128)(2,1)S(1)}, bf16[32,128]{1,0:T(8,128)(2,1)S(1)}, u32[]{:S(2)}, u32[]{:S(2)}) %collective-permute-start.23) | collective-permute-done | bytes 8224 | tf_op jit(solution)/shard_map/ppermute | solution.py:209
  60.1 2.4 %collective-permute-done.24 = bf16[32,128]{1,0:T(8,128)(2,1)S(1)} collective-permute-done((bf16[32,128]{1,0:T(8,128)(2,1)S(1)}, bf16[32,128]{1,0:T(8,128)(2,1)S(1)}, u32[]{:S(2)}, u32[]{:S(2)}) %collective-permute-start.24) | collective-permute-done | bytes 8224 | tf_op jit(solution)/shard_map/ppermute | solution.py:209
  63.7 7.0 %copy-done.1 = bf16[4608,2304]{1,0:T(8,128)(2,1)S(1)} copy-done((bf16[4608,2304]{1,0:T(8,128)(2,1)S(1)}, bf16[4608,2304]{1,0:T(8,128)(2,1)}, u32[]{:S(2)}) %copy-start.1) | copy-done | bytes 21233688
  76.2 3.5 %shard_map.78.refs_15_.refs_1_ = f32[128,2304]{1,0:T(8,128)S(1)} custom-call(s32[2]{0:T(128)S(1)} %pad_add_fusion.refs_0_.refs_1_.place, bf16[32,2304]{1,0:T(8,128)(2,1)S(1)} %collective-permute-done.refs_6_.refs_1_, bf16[32,2304]{1,0:T(8,128)(2,1)S(1)} %copy-done.9, bf16[32,2304]{1,0:T(8,128)(2,1)S(1)} %copy-done.4, bf16[32,2304]{1,0:T(8,128)(2,1)S(1)} %copy-done.11, ...), custom_call_target="tpu_custom_call" | custom-call | flops 2717908992 | tf_op jit(solution)/shard_map/pallas_call | solution.py:123
  80.3 1.7 %collective-permute-start.8 = (bf16[32,2304]{1,0:T(8,128)(2,1)}, bf16[32,2304]{1,0:T(8,128)(2,1)S(1)}, u32[]{:S(2)}, u32[]{:S(2)}) collective-permute-start(bf16[32,2304]{1,0:T(8,128)(2,1)} %collective-permute-done.7.refs_14_.refs_7_), channel_id=1, source_target_pairs={{0,2},{1,3},{4,0},{5,1},{8,4},{9,5},{12,8},{13,9},{14,12},{15,13},... | collective-permute-start | bytes 442376 | tf_op jit(solution)/shard_map/ppermute | solution.py:75
  83.3 4.1 %shard_map.79.refs_10_.refs_2_ = f32[128,2304]{1,0:T(8,128)S(1)} custom-call(s32[2]{0:T(128)S(1)} %pad_add_fusion.refs_0_.refs_1_.place, bf16[32,2304]{1,0:T(8,128)(2,1)} %collective-permute-done.1.refs_9_.refs_1_, bf16[32,2304]{1,0:T(8,128)(2,1)S(1)} %collective-permute-done.32.refs_2_, bf16[32,2304]{1,0:T(8,128)(2,1)} %collective-permute-done.21.refs_11_.refs_3_, ...), custom_call_target="tpu_custom_call" | custom-call | flops 2717908992 | tf_op jit(solution)/shard_map/pallas_call | solution.py:123
  88.9 1.2 %collective-permute-start.27 = (bf16[128,128]{1,0:T(8,128)(2,1)S(1)}, bf16[128,128]{1,0:T(8,128)(2,1)S(1)}, u32[]{:S(2)}, u32[]{:S(2)}) collective-permute-start(bf16[128,128]{1,0:T(8,128)(2,1)S(1)} %pad_maximum_fusion.refs_10_.refs_4_), channel_id=1, source_target_pairs={{0,4},{1,5},{2,6},{3,7},{4,8},{5,9},{6,10},{7,11},{8,12},{9,13},{1... | collective-permute-start | bytes 98312 | tf_op jit(solution)/shard_map/ppermute | solution.py:212
  90.6 4.1 %shard_map.80.refs_3_ = f32[128,2304]{1,0:T(8,128)S(1)} custom-call(s32[2]{0:T(128)S(1)} %pad_add_fusion.refs_0_.refs_1_.place, bf16[32,2304]{1,0:T(8,128)(2,1)} %collective-permute-done.2.refs_11_.refs_1_, bf16[32,2304]{1,0:T(8,128)(2,1)S(1)} %collective-permute-done.38.refs_2_, bf16[32,2304]{1,0:T(8,128)(2,1)} %collective-permute-done.37.refs_13_.refs_3_, ...), custom_call_target="tpu_custom_call" | custom-call | flops 2717908992 | tf_op jit(solution)/shard_map/pallas_call | solution.py:123
  94.8 2.3 %shard_map.81.refs_10_ = bf16[512,2304]{1,0:T(8,128)(2,1)} custom-call(s32[24]{0:T(128)S(1)} %dynamic-slice_bitcast_fusion.table, s32[2]{0:T(128)S(1)} %pad_add_fusion.refs_0_.refs_1_.place, s32[4]{0:T(128)S(1)} %bitcast.8, s32[4]{0:T(128)S(1)} %copy-done.17, f32[64,2304]{1,0:T(8,128)S(1)} %shard_map.76.refs_13_.refs_11_.refs_0_, ...), custom_call_target="tpu_custom_call" | custom-call | bytes 2064384 | tf_op jit(solution)/shard_map/pallas_call | solution.py:377
  97.1 4.3 %shard_map.82 = bf16[512,2304]{1,0:T(8,128)(2,1)} custom-call(s32[24]{0:T(128)S(1)} %dynamic-slice_bitcast_fusion.table, s32[2]{0:T(128)S(1)} %pad_add_fusion.refs_0_.refs_1_.place, s32[4]{0:T(128)S(1)} %bitcast.9, s32[4]{0:T(128)S(1)} %copy-done.17, bf16[32,2304]{1,0:T(8,128)(2,1)S(1)} %collective-permute-done.3.refs_0_, ...), custom_call_target="tpu_custom_call", output_to_operand_aliasing={{}: (14, {})} | custom-call | flops 1358954496 | bytes 294912 | tf_op jit(solution)/shard_map/pallas_call | solution.py:377
  (118 shorter events, 25.6 us)
Async XLA Ops:
  1.0 11.9 %collective-permute-start = (bf16[32,2304]{1,0:T(8,128)(2,1)S(1)}, bf16[32,2304]{1,0:T(8,128)(2,1)S(1)}, u32[]{:S(2)}, u32[]{:S(2)}) collective-permute-start(bf16[32,2304]{1,0:T(8,128)(2,1)S(1)} %get-tuple-element.22.refs_1_.refs_5_), channel_id=1, source_target_pairs={{0,4},{1,5},{4,8},{5,9},{8,12},{9,13},{12,14},{13,15},{14,10},{15,... | collective-permute-start | bytes 442376 | tf_op jit(solution)/shard_map/ppermute | solution.py:69
  12.5 12.1 %collective-permute-start.5 = (bf16[32,2304]{1,0:T(8,128)(2,1)S(1)}, bf16[32,2304]{1,0:T(8,128)(2,1)S(1)}, u32[]{:S(2)}, u32[]{:S(2)}) collective-permute-start(bf16[32,2304]{1,0:T(8,128)(2,1)S(1)} %get-tuple-element.21.refs_3_.refs_7_), channel_id=1, source_target_pairs={{0,2},{1,3},{4,0},{5,1},{8,4},{9,5},{12,8},{13,9},{14,12},{15,13},... | collective-permute-start | bytes 442376 | tf_op jit(solution)/shard_map/ppermute | solution.py:70
  12.9 17.3 %collective-permute-start.18 = (bf16[32,2304]{1,0:T(8,128)(2,1)S(1)}, bf16[32,2304]{1,0:T(8,128)(2,1)S(1)}, u32[]{:S(2)}, u32[]{:S(2)}) collective-permute-start(bf16[32,2304]{1,0:T(8,128)(2,1)S(1)} %get-tuple-element.22.refs_1_.refs_5_), channel_id=1, source_target_pairs={{0,1},{1,0},{2,3},{3,2},{4,5},{5,4},{6,7},{7,6},{8,9},{9,8},{10,11... | collective-permute-start | bytes 442376 | tf_op jit(solution)/shard_map/ppermute | solution.py:65
  13.0 17.3 %collective-permute-start.19 = (bf16[32,2304]{1,0:T(8,128)(2,1)S(1)}, bf16[32,2304]{1,0:T(8,128)(2,1)S(1)}, u32[]{:S(2)}, u32[]{:S(2)}) collective-permute-start(bf16[32,2304]{1,0:T(8,128)(2,1)S(1)} %get-tuple-element.21.refs_3_.refs_7_), channel_id=1, source_target_pairs={{0,1},{1,0},{2,3},{3,2},{4,5},{5,4},{6,7},{7,6},{8,9},{9,8},{10,11... | collective-permute-start | bytes 442376 | tf_op jit(solution)/shard_map/ppermute | solution.py:65
  14.6 23.4 %collective-permute-start.1 = (bf16[32,2304]{1,0:T(8,128)(2,1)S(1)}, bf16[32,2304]{1,0:T(8,128)(2,1)}, u32[]{:S(2)}, u32[]{:S(2)}) collective-permute-start(bf16[32,2304]{1,0:T(8,128)(2,1)S(1)} %collective-permute-done.refs_6_.refs_1_), channel_id=1, source_target_pairs={{0,4},{1,5},{4,8},{5,9},{8,12},{9,13},{12,14},{13,15},{14,10},{15,... | collective-permute-start | bytes 442376 | tf_op jit(solution)/shard_map/ppermute | solution.py:69
  16.2 22.4 %collective-permute-start.20 = (bf16[32,2304]{1,0:T(8,128)(2,1)S(1)}, bf16[32,2304]{1,0:T(8,128)(2,1)}, u32[]{:S(2)}, u32[]{:S(2)}) collective-permute-start(bf16[32,2304]{1,0:T(8,128)(2,1)S(1)} %collective-permute-done.13.refs_7_.refs_5_), channel_id=1, source_target_pairs={{0,2},{1,3},{4,0},{5,1},{8,4},{9,5},{12,8},{13,9},{14,12},{15,13},... | collective-permute-start | bytes 442376 | tf_op jit(solution)/shard_map/ppermute | solution.py:70
  25.3 7.8 %collective-permute-start.15 = (bf16[2,32,576]{2,1,0:T(8,128)(2,1)S(1)}, bf16[2,32,576]{2,1,0:T(8,128)(2,1)S(1)}, u32[]{:S(2)}, u32[]{:S(2)}) collective-permute-start(bf16[2,32,576]{2,1,0:T(8,128)(2,1)S(1)} %get-tuple-element.17), channel_id=1, source_target_pairs={{0,12},{1,13},{2,14},{3,15},{4,0},{5,1},{6,2},{7,3},{8,4},{9,5},{1... | collective-permute-start | bytes 221192 | tf_op jit(solution)/shard_map/ppermute | solution.py:190
  30.3 7.8 %collective-permute-start.17 = (bf16[2,32,576]{2,1,0:T(8,128)(2,1)S(1)}, bf16[2,32,576]{2,1,0:T(8,128)(2,1)S(1)}, u32[]{:S(2)}, u32[]{:S(2)}) collective-permute-start(bf16[2,32,576]{2,1,0:T(8,128)(2,1)S(1)} %get-tuple-element.19), channel_id=1, source_target_pairs={{0,4},{1,5},{2,6},{3,7},{4,8},{5,9},{6,10},{7,11},{8,12},{9,13},{1... | collective-permute-start | bytes 221192 | tf_op jit(solution)/shard_map/ppermute | solution.py:190
  38.1 7.2 %collective-permute-start.29 = (bf16[32,2304]{1,0:T(8,128)(2,1)S(1)}, bf16[32,2304]{1,0:T(8,128)(2,1)S(1)}, u32[]{:S(2)}, u32[]{:S(2)}) collective-permute-start(bf16[32,2304]{1,0:T(8,128)(2,1)S(1)} %collective-permute-done.14.refs_8_.refs_3_), channel_id=1, source_target_pairs={{0,1},{1,0},{2,3},{3,2},{4,5},{5,4},{6,7},{7,6},{8,9},{9,8},{10,11... | collective-permute-start | bytes 442376 | tf_op jit(solution)/shard_map/ppermute | solution.py:73
  38.6 8.1 %collective-permute-start.30 = (bf16[32,2304]{1,0:T(8,128)(2,1)S(1)}, bf16[32,2304]{1,0:T(8,128)(2,1)S(1)}, u32[]{:S(2)}, u32[]{:S(2)}) collective-permute-start(bf16[32,2304]{1,0:T(8,128)(2,1)S(1)} %collective-permute-done.13.refs_7_.refs_5_), channel_id=1, source_target_pairs={{0,1},{1,0},{2,3},{3,2},{4,5},{5,4},{6,7},{7,6},{8,9},{9,8},{10,11... | collective-permute-start | bytes 442376 | tf_op jit(solution)/shard_map/ppermute | solution.py:73
  38.7 15.3 %collective-permute-start.31 = (bf16[32,2304]{1,0:T(8,128)(2,1)S(1)}, bf16[32,2304]{1,0:T(8,128)(2,1)S(1)}, u32[]{:S(2)}, u32[]{:S(2)}) collective-permute-start(bf16[32,2304]{1,0:T(8,128)(2,1)S(1)} %collective-permute-done.5.refs_9_.refs_7_), channel_id=1, source_target_pairs={{0,1},{1,0},{2,3},{3,2},{4,5},{5,4},{6,7},{7,6},{8,9},{9,8},{10,11... | collective-permute-start | bytes 442376 | tf_op jit(solution)/shard_map/ppermute | solution.py:73
  42.5 20.0 %collective-permute-start.2 = (bf16[32,2304]{1,0:T(8,128)(2,1)}, bf16[32,2304]{1,0:T(8,128)(2,1)}, u32[]{:S(2)}, u32[]{:S(2)}) collective-permute-start(bf16[32,2304]{1,0:T(8,128)(2,1)} %collective-permute-done.1.refs_9_.refs_1_), channel_id=1, source_target_pairs={{0,4},{1,5},{4,8},{5,9},{8,12},{9,13},{12,14},{13,15},{14,10},{15,... | collective-permute-start | bytes 442376 | tf_op jit(solution)/shard_map/ppermute | solution.py:69
  43.2 19.8 %collective-permute-start.7 = (bf16[32,2304]{1,0:T(8,128)(2,1)}, bf16[32,2304]{1,0:T(8,128)(2,1)}, u32[]{:S(2)}, u32[]{:S(2)}) collective-permute-start(bf16[32,2304]{1,0:T(8,128)(2,1)} %collective-permute-done.6.refs_12_.refs_7_), channel_id=1, source_target_pairs={{0,2},{1,3},{4,0},{5,1},{8,4},{9,5},{12,8},{13,9},{14,12},{15,13},... | collective-permute-start | bytes 442376 | tf_op jit(solution)/shard_map/ppermute | solution.py:70
  45.9 17.2 %collective-permute-start.36 = (bf16[32,2304]{1,0:T(8,128)(2,1)}, bf16[32,2304]{1,0:T(8,128)(2,1)}, u32[]{:S(2)}, u32[]{:S(2)}) collective-permute-start(bf16[32,2304]{1,0:T(8,128)(2,1)} %collective-permute-done.20.refs_10_.refs_5_), channel_id=1, source_target_pairs={{0,2},{1,3},{4,0},{5,1},{8,4},{9,5},{12,8},{13,9},{14,12},{15,13},... | collective-permute-start | bytes 442376 | tf_op jit(solution)/shard_map/ppermute | solution.py:70
  47.3 16.2 %collective-permute-start.37 = (bf16[32,2304]{1,0:T(8,128)(2,1)}, bf16[32,2304]{1,0:T(8,128)(2,1)}, u32[]{:S(2)}, u32[]{:S(2)}) collective-permute-start(bf16[32,2304]{1,0:T(8,128)(2,1)} %collective-permute-done.21.refs_11_.refs_3_), channel_id=1, source_target_pairs={{0,4},{1,5},{4,8},{5,9},{8,12},{9,13},{12,14},{13,15},{14,10},{15,... | collective-permute-start | bytes 442376 | tf_op jit(solution)/shard_map/ppermute | solution.py:69
  62.5 17.2 %collective-permute-start.32 = (bf16[32,2304]{1,0:T(8,128)(2,1)}, bf16[32,2304]{1,0:T(8,128)(2,1)S(1)}, u32[]{:S(2)}, u32[]{:S(2)}) collective-permute-start(bf16[32,2304]{1,0:T(8,128)(2,1)} %collective-permute-done.1.refs_9_.refs_1_), channel_id=1, source_target_pairs={{0,1},{1,0},{2,3},{3,2},{4,5},{5,4},{6,7},{7,6},{8,9},{9,8},{10,11... | collective-permute-start | bytes 442376 | tf_op jit(solution)/shard_map/ppermute | solution.py:73
  62.5 17.3 %collective-permute-start.33 = (bf16[32,2304]{1,0:T(8,128)(2,1)}, bf16[32,2304]{1,0:T(8,128)(2,1)S(1)}, u32[]{:S(2)}, u32[]{:S(2)}) collective-permute-start(bf16[32,2304]{1,0:T(8,128)(2,1)} %collective-permute-done.21.refs_11_.refs_3_), channel_id=1, source_target_pairs={{0,1},{1,0},{2,3},{3,2},{4,5},{5,4},{6,7},{7,6},{8,9},{9,8},{10,11... | collective-permute-start | bytes 442376 | tf_op jit(solution)/shard_map/ppermute | solution.py:73
  63.0 17.3 %collective-permute-start.34 = (bf16[32,2304]{1,0:T(8,128)(2,1)}, bf16[32,2304]{1,0:T(8,128)(2,1)S(1)}, u32[]{:S(2)}, u32[]{:S(2)}) collective-permute-start(bf16[32,2304]{1,0:T(8,128)(2,1)} %collective-permute-done.20.refs_10_.refs_5_), channel_id=1, source_target_pairs={{0,1},{1,0},{2,3},{3,2},{4,5},{5,4},{6,7},{7,6},{8,9},{9,8},{10,11... | collective-permute-start | bytes 442376 | tf_op jit(solution)/shard_map/ppermute | solution.py:73
  63.1 19.0 %collective-permute-start.35 = (bf16[32,2304]{1,0:T(8,128)(2,1)}, bf16[32,2304]{1,0:T(8,128)(2,1)S(1)}, u32[]{:S(2)}, u32[]{:S(2)}) collective-permute-start(bf16[32,2304]{1,0:T(8,128)(2,1)} %collective-permute-done.6.refs_12_.refs_7_), channel_id=1, source_target_pairs={{0,1},{1,0},{2,3},{3,2},{4,5},{5,4},{6,7},{7,6},{8,9},{9,8},{10,11... | collective-permute-start | bytes 442376 | tf_op jit(solution)/shard_map/ppermute | solution.py:73
  63.6 18.5 %collective-permute-start.38 = (bf16[32,2304]{1,0:T(8,128)(2,1)}, bf16[32,2304]{1,0:T(8,128)(2,1)S(1)}, u32[]{:S(2)}, u32[]{:S(2)}) collective-permute-start(bf16[32,2304]{1,0:T(8,128)(2,1)} %collective-permute-done.2.refs_11_.refs_1_), channel_id=1, source_target_pairs={{0,1},{1,0},{2,3},{3,2},{4,5},{5,4},{6,7},{7,6},{8,9},{9,8},{10,11... | collective-permute-start | bytes 442376 | tf_op jit(solution)/shard_map/ppermute | solution.py:73
  79.8 10.3 %collective-permute-start.3 = (bf16[32,2304]{1,0:T(8,128)(2,1)}, bf16[32,2304]{1,0:T(8,128)(2,1)S(1)}, u32[]{:S(2)}, u32[]{:S(2)}) collective-permute-start(bf16[32,2304]{1,0:T(8,128)(2,1)} %collective-permute-done.2.refs_11_.refs_1_), channel_id=1, source_target_pairs={{0,4},{1,5},{4,8},{5,9},{8,12},{9,13},{12,14},{13,15},{14,10},{15,... | collective-permute-start | bytes 442376 | tf_op jit(solution)/shard_map/ppermute | solution.py:75
  79.8 7.6 %collective-permute-start.41 = (bf16[32,2304]{1,0:T(8,128)(2,1)}, bf16[32,2304]{1,0:T(8,128)(2,1)S(1)}, u32[]{:S(2)}, u32[]{:S(2)}) collective-permute-start(bf16[32,2304]{1,0:T(8,128)(2,1)} %collective-permute-done.7.refs_14_.refs_7_), channel_id=1, source_target_pairs={{0,1},{1,0},{2,3},{3,2},{4,5},{5,4},{6,7},{7,6},{8,9},{9,8},{10,11... | collective-permute-start | bytes 442376 | tf_op jit(solution)/shard_map/ppermute | solution.py:73
  80.3 9.8 %collective-permute-start.8 = (bf16[32,2304]{1,0:T(8,128)(2,1)}, bf16[32,2304]{1,0:T(8,128)(2,1)S(1)}, u32[]{:S(2)}, u32[]{:S(2)}) collective-permute-start(bf16[32,2304]{1,0:T(8,128)(2,1)} %collective-permute-done.7.refs_14_.refs_7_), channel_id=1, source_target_pairs={{0,2},{1,3},{4,0},{5,1},{8,4},{9,5},{12,8},{13,9},{14,12},{15,13},... | collective-permute-start | bytes 442376 | tf_op jit(solution)/shard_map/ppermute | solution.py:75
  87.4 7.3 %collective-permute-start.25 = (bf16[128,128]{1,0:T(8,128)(2,1)S(1)}, bf16[128,128]{1,0:T(8,128)(2,1)S(1)}, u32[]{:S(2)}, u32[]{:S(2)}) collective-permute-start(bf16[128,128]{1,0:T(8,128)(2,1)S(1)} %pad_maximum_fusion.refs_10_.refs_4_), channel_id=1, source_target_pairs={{0,12},{1,13},{2,14},{3,15},{4,0},{5,1},{6,2},{7,3},{8,4},{9,5},{1... | collective-permute-start | bytes 98312 | tf_op jit(solution)/shard_map/ppermute | solution.py:212
  (40 other events, 223.7 us)

commit v4 on v0

v4 whole, which is shorter than its diff:
```python
import functools

import jax
import jax.numpy as jnp
from jax import lax
from jax.experimental import pallas as pl
from jax.experimental.pallas import tpu as pltpu
from jax.sharding import PartitionSpec as P

BLOCK = 128
AXES = ("seq", "adapter")
CHUNKS = 2


def ring_perm(n, way):
    order = [2 * z for z in range(n // 2)] + [2 * z + 1 for z in reversed(range(n // 2))]
    return [(2 * s + c, 2 * order[(pos + way) % n] + c) for pos, s in enumerate(order) for c in range(2)]


def swap_cores(x, n):
    return lax.ppermute(x, AXES, [(2 * s + c, 2 * s + 1 - c) for s in range(n) for c in range(2)])


def chip_at(distance, n):
    s = lax.axis_index("seq")
    z = s >> 1
    pos = jnp.where(s & 1 == 0, z, n - 1 - z) + distance
    pos = jnp.where(pos >= n, pos - n, pos)
    pos = jnp.where(pos < 0, pos + n, pos)
    return jnp.where(pos < n // 2, 2 * pos, 2 * (n - 1 - pos) + 1)


def hop_distances(hop, n):
    if hop == 0:
        return [0]
    return [-hop, hop] if hop < n // 2 else [hop]


class Ring:
    def __init__(self, chunks, n):
        self.n, self.up, self.down = n, list(chunks), list(chunks)

    def hop(self, hop, after=()):
        n = self.n
        if hop < n // 2:
            self.up = [lax.ppermute(x, AXES, ring_perm(n, 1)) for x in self.up]
            self.down = [lax.ppermute(x, AXES, ring_perm(n, -1)) for x in self.down]
            pieces = self.up + self.down
        else:
            pieces = [
                lax.ppermute((self.down if k % 2 else self.up)[k], AXES, ring_perm(n, -1 if k % 2 else 1))
                for k in range(CHUNKS)
            ]
        rows, depth = pieces[0].shape
        (joined,) = call(
            join_kernel, [], pieces, list(after), [((rows * len(pieces), depth), pieces[0].dtype)]
        )
        return joined


def join_kernel(*refs):
    *pieces, out = refs
    rows = pieces[0].shape[0]
    for i, piece in enumerate(pieces):
        out[i * rows : (i + 1) * rows, :] = piece[...]


def whole(count):
    return [pl.BlockSpec(memory_space=pltpu.VMEM)] * count


def in_vmem(arrays):
    return [pltpu.with_memory_space_constraint(x, pltpu.VMEM) for x in arrays]


def call(kernel, scalars, arrays, after, outs, scratch=(), limit=8, flops=0):
    operands = len(scalars) + len(arrays)

    def body(*refs):
        kernel(*refs[:operands], *refs[operands + len(after) :])

    return pl.pallas_call(
        body,
        out_shape=[pltpu.VMEM(shape, dtype) for shape, dtype in outs],
        in_specs=[pl.BlockSpec(memory_space=pltpu.SMEM)] * len(scalars)
        + whole(len(arrays))
        + [pl.BlockSpec(memory_space=pl.ANY)] * len(after),
        out_specs=whole(len(outs)),
        scratch_shapes=list(scratch),
        compiler_params=pltpu.CompilerParams(vmem_limit_bytes=limit << 20),
        cost_estimate=pl.CostEstimate(flops=flops, bytes_accessed=0, transcendentals=0),
    )(*scalars, *in_vmem(arrays), *after)


def split_kernel(down_ref, keep, give):
    half = keep.shape[1]
    c = lax.axis_index("adapter")
    for ref, core in ((keep, c), (give, 1 - c)):
        ref[...] = down_ref[:, pl.ds(pl.multiple_of(core * half, half), half), :].astype(jnp.bfloat16)


def pick_kernel(chip_rows, adapters, keep, give, out):
    held = keep.shape[0]
    c = lax.axis_index("adapter")
    for s in range(out.shape[0]):
        adapter = adapters[s * chip_rows // BLOCK]
        for index in range(held):

            @pl.when(adapter == c * held + index)
            def _():
                out[s] = keep[index]

            @pl.when(adapter == (1 - c) * held + index)
            def _():
                out[s] = give[index]


def shrink_kernel(own, other, parts, out, held, factor):
    rows, width = own.shape[0], parts.shape[2]
    c = lax.axis_index("adapter")
    for ref, core in ((own, c), (other, 1 - c)):
        held[pl.ds(pl.multiple_of(core * rows, rows), rows), :] = ref[...]
    for s in range(parts.shape[0]):
        factor[:, s * width : (s + 1) * width] = parts[s]
    shrink = lax.dot_general(
        held[...], factor[...], (((1,), (1,)), ((), ())), preferred_element_type=jnp.float32
    )
    high = shrink.astype(jnp.bfloat16)
    low = (shrink - high.astype(jnp.float32)).astype(jnp.bfloat16)
    piece = jnp.concatenate([high[:rows], high[rows:], low[:rows], low[rows:]], 1)
    for device in range(out.shape[0]):
        out[device] = piece


def load_kernel(w_ref, up_ref, w_out, up_out, held, sems):
    parts = sems.shape[0] - 1
    depth, rank = w_ref.shape[0] // parts, up_ref.shape[1]
    copies = [pltpu.make_async_copy(up_ref, held, sems.at[parts])] + [
        pltpu.make_async_copy(
            w_ref.at[pl.ds(k * depth, depth), :], w_out.at[pl.ds(k * depth, depth), :], sems.at[k]
        )
        for k in range(parts)
    ]
    for copy in copies:
        copy.start()
    copies[0].wait()
    for adapter in range(up_ref.shape[0]):
        factor = held[adapter].astype(jnp.bfloat16)
        up_out[adapter, :rank, :] = factor
        up_out[adapter, rank:, :] = factor
    for copy in copies[1:]:
        copy.wait()


def load(weight, up):
    adapters, rank, width = up.shape
    return pl.pallas_call(
        load_kernel,
        out_shape=[
            pltpu.VMEM(weight.shape, weight.dtype),
            pltpu.VMEM((adapters, 2 * rank, width), jnp.bfloat16),
        ],
        in_specs=[pl.BlockSpec(memory_space=pltpu.HBM)] * 2,
        out_specs=whole(2),
        scratch_shapes=[pltpu.VMEM(up.shape, up.dtype), pltpu.SemaphoreType.DMA((9,))],
        compiler_params=pltpu.CompilerParams(vmem_limit_bytes=8 << 20),
        cost_estimate=pl.CostEstimate(
            flops=0, bytes_accessed=2 * weight.size + 4 * up.size, transcendentals=0
        ),
    )(*(pltpu.with_memory_space_constraint(x, pltpu.HBM) for x in (weight, up)))


def assemble(pairs, rows, held):
    width = held.shape[1]
    c = lax.axis_index("adapter")
    first = 0
    for pair in pairs:
        depth = pair[0].shape[1]
        chunks = width // depth
        for chip in range(pair[0].shape[0] // (rows * chunks)):
            for k in range(chunks):
                at = (chip * chunks + k) * rows
                for ref, core in zip(pair, (c, 1 - c)):
                    row = pl.multiple_of(first + core * rows, rows)
                    held[pl.ds(row, rows), k * depth : (k + 1) * depth] = ref[at : at + rows, :]
            first += 2 * rows


def tile_width(width):
    return 768 if width % 768 == 0 else width


def base_kernel(rows, *refs):
    *pairs, w_ref, base, held = refs
    assemble(list(zip(pairs[::2], pairs[1::2])), rows, held)
    width = w_ref.shape[1]
    columns = tile_width(width)
    for j in range(0, width, columns):
        at = slice(j, j + columns)
        base[:, at] = jnp.dot(held[...], w_ref[:, at], preferred_element_type=jnp.float32)


def base_rows(pairs, chips, rows, weight, after):
    total = 2 * rows * chips
    (base,) = call(
        functools.partial(base_kernel, rows),
        [],
        [x for pair in pairs for x in pair] + [weight],
        after,
        [((total, weight.shape[1]), jnp.float32)],
        [pltpu.VMEM((total, weight.shape[0]), jnp.bfloat16)],
        flops=2 * total * weight.size,
    )
    return base


def finish_tile(distances, n, adapters, live, spread, up_ref, out_ref, block, sems, j, base_of):
    rows = spread.shape[1]
    half = spread.shape[2] // 4
    chip_rows, columns = 2 * rows, block.shape[2]
    at = slice(j * columns, (j + 1) * columns)
    copies = []
    for i, distance in enumerate(distances):
        chip = chip_at(distance, n)
        zero, one = spread[2 * chip], spread[2 * chip + 1]
        shrink = jnp.concatenate(
            [
                jnp.concatenate([x[:, a : a + half] for a in (k * half, (2 + k) * half) for x in (zero, one)], 1)
                for k in range(2)
            ],
            0,
        )
        first = chip * chip_rows
        of_block = first // BLOCK
        delta = jnp.dot(shrink, up_ref[adapters[of_block], :, at], preferred_element_type=jnp.float32)
        row = lax.broadcasted_iota(jnp.int32, delta.shape, 0) + (first - of_block * BLOCK)
        place = slice(i * chip_rows, (i + 1) * chip_rows)
        total = jnp.where(row < live[of_block], base_of(i) + delta, 0.0)
        block[j, place, :] = total.astype(out_ref.dtype)
        copies.append(
            pltpu.make_async_copy(
                block.at[j, pl.ds(i * chip_rows, chip_rows), :],
                out_ref.at[pl.ds(pl.multiple_of(first, chip_rows), chip_rows), pl.ds(j * columns, columns)],
                sems.at[j, i],
            )
        )
        copies[-1].start()
    return copies


def finish_kernel(distances, n, adapters, live, *refs):
    *bases, spread, up_ref, out_ref, block, sems = refs
    chip_rows = 2 * spread.shape[1]
    place = [(base, k * chip_rows) for base in bases for k in range(base.shape[0] // chip_rows)]
    copies = []
    for j in range(block.shape[0]):
        columns = slice(j * block.shape[2], (j + 1) * block.shape[2])

        def base_of(i):
            base, row = place[i]
            return base[row : row + chip_rows, columns]

        copies += finish_tile(distances, n, adapters, live, spread, up_ref, out_ref, block, sems, j, base_of)
    for copy in copies:
        copy.wait()


def last_kernel(distances, n, adapters, live, *refs):
    *pairs, spread, w_ref, up_ref, _, out_ref, block, sems, held = refs
    rows = spread.shape[1]
    assemble(list(zip(pairs[::2], pairs[1::2])), rows, held)
    copies = []
    for j in range(block.shape[0]):
        columns = slice(j * block.shape[2], (j + 1) * block.shape[2])
        base = jnp.dot(held[...], w_ref[:, columns], preferred_element_type=jnp.float32)

        def base_of(i):
            return base[2 * i * rows : 2 * (i + 1) * rows]

        copies += finish_tile(distances, n, adapters, live, spread, up_ref, out_ref, block, sems, j, base_of)
    for copy in copies:
        copy.wait()


def finish(kernel, distances, n, scalars, arrays, others, into, rows, width, scratch=(), flops=0):
    columns = tile_width(width)
    total = 2 * rows * len(distances)
    operands = len(scalars) + len(arrays)

    def body(*refs):
        refs = refs[:operands] + refs[operands + len(others) :]
        kernel(distances, n, *refs)

    return pl.pallas_call(
        body,
        out_shape=jax.ShapeDtypeStruct((2 * n * rows, width), jnp.bfloat16),
        in_specs=[pl.BlockSpec(memory_space=pltpu.SMEM)] * len(scalars)
        + whole(len(arrays))
        + [pl.BlockSpec(memory_space=pl.ANY)] * (len(others) + len(into)),
        out_specs=pl.BlockSpec(memory_space=pl.ANY),
        scratch_shapes=[
            pltpu.VMEM((width // columns, total, columns), jnp.bfloat16),
            pltpu.SemaphoreType.DMA((width // columns, len(distances))),
            *scratch,
        ],
        input_output_aliases={operands + len(others): 0} if into else {},
        compiler_params=pltpu.CompilerParams(vmem_limit_bytes=12 << 20),
        cost_estimate=pl.CostEstimate(flops=flops, bytes_accessed=2 * total * width, transcendentals=0),
    )(*scalars, *in_vmem(arrays), *others, *into)


def on_device(n, tokens, weight, down, up, adapter_per_block, rows_per_block):
    rows, features = tokens.shape
    depth = features // CHUNKS
    held, width, rank = down.shape
    half, last = rank // 2, n // 2
    adapters = adapter_per_block[:, 0]
    ring = Ring([tokens[:, k * depth : (k + 1) * depth] for k in range(CHUNKS)], n)
    part = ((held, half, width), jnp.bfloat16)
    keep, give = call(split_kernel, [], [jnp.swapaxes(down, 1, 2)], [], [part, part])
    give = swap_cores(give, n)
    weight, up = load(weight, up)
    arrived = [tokens, ring.hop(1, [weight])]
    pairs = [(x, swap_cores(x, n)) for x in arrived]

    (picks,) = call(
        functools.partial(pick_kernel, 2 * rows),
        [adapters],
        [keep, give],
        [arrived[1]],
        [((n, half, width), jnp.bfloat16)],
    )
    parts = lax.all_to_all(picks, "seq", 0, 0, tiled=True)
    arrived.append(ring.hop(2, [picks]))
    bases = [base_rows(pairs, 3, rows, weight, [picks])]
    (spread,) = call(
        shrink_kernel,
        [],
        [*pairs[0], parts],
        [arrived[2], *bases],
        [((2 * n, rows, 2 * rank), jnp.bfloat16)],
        [pltpu.VMEM((2 * rows, features), jnp.bfloat16), pltpu.VMEM((half, features), jnp.bfloat16)],
    )
    done = spread
    spread = lax.all_to_all(spread, AXES, 0, 0, tiled=True)
    for hop in range(3, last + 1):
        pairs.append((arrived[hop - 1], swap_cores(arrived[hop - 1], n)))
        arrived.append(ring.hop(hop, [done, *bases[-1:]]))
        if hop < last:
            bases.append(base_rows(pairs[-1:], 2, rows, weight, [arrived[hop], bases[-1]]))
        done = spread
    pairs.append((arrived[last], swap_cores(arrived[last], n)))
    early = [d for hop in range(last - 1) for d in hop_distances(hop, n)]
    late = hop_distances(last - 1, n) + hop_distances(last, n)
    scalars = [adapters, rows_per_block]
    out = finish(
        finish_kernel, early, n, scalars, [*bases, spread, up], [arrived[last]], [], rows, weight.shape[1]
    )
    return finish(
        last_kernel,
        late,
        n,
        scalars,
        [*pairs[last - 1], *pairs[last], spread, weight, up],
        [],
        [out],
        rows,
        weight.shape[1],
        [pltpu.VMEM((2 * rows * len(late), features), jnp.bfloat16)],
        4 * rows * len(late) * weight.size,
    )


def solution(mesh):
    placed = (
        P(("groups", "seq", "adapter"), None),
        P(None, ("seq", "adapter")),
        P(("groups", "adapter"), "seq", None),
        P("groups", None, ("seq", "adapter")),
        P("groups", None),
        P("groups"),
    )
    return jax.shard_map(
        functools.partial(on_device, mesh.shape["seq"]),
        mesh=mesh,
        in_specs=placed,
        out_specs=P("groups", ("seq", "adapter")),
        check_vma=False,
    )
```

time: 189 us -> 102 us (0.54)
  waiting for transfers between devices: 138 us -> 5.48 us
  matrix products: 34.6 us -> 0 us
  Pallas kernels: 0 us -> 33.4 us
  local copies, waits for them, and re-layouts: 2.1 us -> 34.2 us
  starting transfers between devices: 0.04 us -> 27.4 us
  between operations: 13.5 us -> 0.4 us
    psum x1 -> x0, waiting for transfers between devices: 85.5 us -> none  [on_device(): rank_reduction = lax.psum(combined[:, ff_local:], ('seq', 'adapter'))]
    all_gather x1 -> x0, waiting for transfers between devices: 51.6 us -> none  [on_device(): device_rows = lax.all_gather(tokens, ('seq', 'adapter'), axis=0, tiled=True)]
    dot_general x6 -> x0, matrix products: 34.6 us -> none  [the longest x1 15.4 us: on_device(): jnp.dot(device_rows, shared_up_weight, preferred_element_type=jnp.float32)]
    pallas_call x0 -> x12, Pallas kernels: none -> 33.4 us  [the longest x9 16.3 us: call(): pl.pallas_call(body, out_shape=[pltpu.VMEM(shape, dtype) for shape, dtype...]
    unnamed x8 -> x26, local copies, waits for them, and re-layouts: 0.02 us -> 33.2 us
    ppermute x0 -> x20, starting transfers between devices: none -> 16.4 us  [the longest x6 12.5 us: hop(): self.down = [lax.ppermute(x, AXES, ring_perm(n, -1)) for x in self.down]]
    all_to_all x0 -> x2, starting transfers between devices: none -> 11 us  [the longest x1 6.12 us: on_device(): spread = lax.all_to_all(spread, AXES, 0, 0, tiled=True)]
    ppermute x0 -> x20, waiting for transfers between devices: none -> 5.47 us  [the longest x6 2.98 us: hop(): self.down = [lax.ppermute(x, AXES, ring_perm(n, -1)) for x in self.down]]
  transfers between devices with their start and end apart: 2 -> 22, of which waited for: 2 -> 4; matrix products, arithmetic and copies ran while one was open for 4% -> 0% of each run, Pallas kernels for 0% -> 26%
where the time goes in v4:
time: 102 us; the launch traced here: 101 us
  local copies, waits for them, and re-layouts  34.2 us (34%)
  Pallas kernels  33.4 us (33%)
  starting transfers between devices  27.4 us (27%)
  waiting for transfers between devices  5.48 us (5%)
    unnamed x26, local copies, waits for them, and re-layouts  33.2 us
    pallas_call x9, Pallas kernels, call(): pl.pallas_call(body, out_shape=[pltpu.VMEM(shape, dtype) for shape, dtype...  16.3 us
    ppermute x6, starting transfers between devices, hop(): self.down = [lax.ppermute(x, AXES, ring_perm(n, -1)) for x in self.down]  12.5 us
    pallas_call x2, Pallas kernels, finish(): pl.pallas_call(body, out_shape=jax.ShapeDtypeStruct((2 * n * rows, width)...  9.25 us
    pallas_call x1, Pallas kernels, load(): pl.pallas_call(load_kernel, out_shape=[pltpu.VMEM(weight.shape, weight.dt...  7.87 us
    all_to_all x1, starting transfers between devices, on_device(): spread = lax.all_to_all(spread, AXES, 0, 0, tiled=True)  6.12 us
    all_to_all x1, starting transfers between devices, on_device(): parts = lax.all_to_all(picks, 'seq', 0, 0, tiled=True)  4.89 us
    ppermute x6, waiting for transfers between devices, hop(): self.down = [lax.ppermute(x, AXES, ring_perm(n, -1)) for x in self.down]  2.98 us
  transfers between devices with their start and end apart: 22, of which 4 were waited for; matrix products, arithmetic and copies ran while one was open for 0% of the time, Pallas kernels for 26%

profile of v4, /device:TPU:0, one launch (start us, length us, event | category | flops | bytes accessed | tf_op | source)
XLA Modules:
  0.0 100.9 jit_solution(8879421853775644000)
XLA Ops:
  1.0 3.0 %collective-permute-start.9 = (bf16[32,2304]{1,0:T(8,128)(2,1)S(1)}, bf16[32,2304]{1,0:T(8,128)(2,1)S(1)}, u32[]{:S(2)}, u32[]{:S(2)}) collective-permute-start(bf16[32,2304]{1,0:T(8,128)(2,1)S(1)} %get-tuple-element.13), channel_id=1, source_target_pairs={{0,2},{1,3},{4,0},{5,1},{8,4},{9,5},{12,8},{13,9},{14,12},{15,13},... | collective-permute-start | bytes 442376 | tf_op jit(solution)/shard_map/ppermute | solution.py:47
  4.1 1.9 %collective-permute-start.6 = (bf16[32,2304]{1,0:T(8,128)(2,1)S(1)}, bf16[32,2304]{1,0:T(8,128)(2,1)S(1)}, u32[]{:S(2)}, u32[]{:S(2)}) collective-permute-start(bf16[32,2304]{1,0:T(8,128)(2,1)S(1)} %get-tuple-element.14), channel_id=1, source_target_pairs={{0,2},{1,3},{4,0},{5,1},{8,4},{9,5},{12,8},{13,9},{14,12},{15,13},... | collective-permute-start | bytes 442376 | tf_op jit(solution)/shard_map/ppermute | solution.py:47
  6.2 7.9 %shard_map.65 = (bf16[4608,2304]{1,0:T(8,128)(2,1)S(1)}, bf16[4,128,2304]{2,1,0:T(8,128)(2,1)S(1)}) custom-call(bf16[4608,2304]{1,0:T(8,128)(2,1)} %w_ref.1, f32[4,64,2304]{2,1,0:T(8,128)} %up_ref.1), custom_call_target="tpu_custom_call" | custom-call | bytes 23592960 | tf_op jit(solution)/shard_map/pallas_call | solution.py:157
  15.6 7.1 %copy-done = bf16[4608,2304]{1,0:T(8,128)(2,1)} copy-done((bf16[4608,2304]{1,0:T(8,128)(2,1)}, bf16[4608,2304]{1,0:T(8,128)(2,1)S(1)}, u32[]{:S(2)}) %copy-start) | copy-done | bytes 21233688
  22.7 1.9 %collective-permute-start.10 = (bf16[32,2304]{1,0:T(8,128)(2,1)S(1)}, bf16[32,2304]{1,0:T(8,128)(2,1)}, u32[]{:S(2)}, u32[]{:S(2)}) collective-permute-start(bf16[32,2304]{1,0:T(8,128)(2,1)S(1)} %collective-permute-done.9.refs_3_), channel_id=1, source_target_pairs={{0,2},{1,3},{4,0},{5,1},{8,4},{9,5},{12,8},{13,9},{14,12},{15,13},... | collective-permute-start | bytes 442376 | tf_op jit(solution)/shard_map/ppermute | solution.py:47
  25.3 1.7 %collective-permute-start.7 = (bf16[32,2304]{1,0:T(8,128)(2,1)S(1)}, bf16[32,2304]{1,0:T(8,128)(2,1)}, u32[]{:S(2)}, u32[]{:S(2)}) collective-permute-start(bf16[32,2304]{1,0:T(8,128)(2,1)S(1)} %collective-permute-done.6.refs_2_), channel_id=1, source_target_pairs={{0,2},{1,3},{4,0},{5,1},{8,4},{9,5},{12,8},{13,9},{14,12},{15,13},... | collective-permute-start | bytes 442376 | tf_op jit(solution)/shard_map/ppermute | solution.py:47
  27.3 2.2 %collective-permute-done.10.refs_3_ = bf16[32,2304]{1,0:T(8,128)(2,1)} collective-permute-done((bf16[32,2304]{1,0:T(8,128)(2,1)S(1)}, bf16[32,2304]{1,0:T(8,128)(2,1)}, u32[]{:S(2)}, u32[]{:S(2)}) %collective-permute-start.10) | collective-permute-done | bytes 147488 | tf_op jit(solution)/shard_map/ppermute | solution.py:47
  29.6 1.5 %shard_map.67.refs_4_.refs_5_ = bf16[8,32,576]{2,1,0:T(8,128)(2,1)} custom-call(s32[4]{0:T(128)S(1)} %bitcast.3, bf16[2,32,576]{2,1,0:T(8,128)(2,1)S(1)} %get-tuple-element.9.refs_1_, bf16[2,32,576]{2,1,0:T(8,128)(2,1)S(1)} %collective-permute-done.13.refs_2_, bf16[128,2304]{1,0:T(8,128)(2,1)S(1)} %shard_map.66.refs_3_.refs_2_), custom_call_target="tpu_custom_call" | custom-call | tf_op jit(solution)/shard_map/pallas_call | solution.py:82
  32.5 1.8 %collective-permute-done.1.refs_0_ = bf16[32,2304]{1,0:T(8,128)(2,1)} collective-permute-done((bf16[32,2304]{1,0:T(8,128)(2,1)S(1)}, bf16[32,2304]{1,0:T(8,128)(2,1)}, u32[]{:S(2)}, u32[]{:S(2)}) %collective-permute-start.1) | collective-permute-done | bytes 147488 | tf_op jit(solution)/shard_map/ppermute | solution.py:46
  35.5 4.9 %all-to-all-start = ((bf16[8,32,576]{2,1,0:T(8,128)(2,1)}), bf16[8,32,576]{2,1,0:T(8,128)(2,1)}, u32[]{:S(2)}, u32[]{:S(2)}) async-start(bf16[8,32,576]{2,1,0:T(8,128)(2,1)} %shard_map.67.refs_4_.refs_5_), calls=%async_computation | async-start | bytes 655360 | tf_op jit(solution)/shard_map/all_to_all | solution.py:333
  40.4 2.0 %collective-permute-start.11 = (bf16[32,2304]{1,0:T(8,128)(2,1)}, bf16[32,2304]{1,0:T(8,128)(2,1)}, u32[]{:S(2)}, u32[]{:S(2)}) collective-permute-start(bf16[32,2304]{1,0:T(8,128)(2,1)} %collective-permute-done.10.refs_3_), channel_id=1, source_target_pairs={{0,2},{1,3},{4,0},{5,1},{8,4},{9,5},{12,8},{13,9},{14,12},{15,13},... | collective-permute-start | bytes 442376 | tf_op jit(solution)/shard_map/ppermute | solution.py:47
  42.5 2.0 %collective-permute-start.8 = (bf16[32,2304]{1,0:T(8,128)(2,1)}, bf16[32,2304]{1,0:T(8,128)(2,1)}, u32[]{:S(2)}, u32[]{:S(2)}) collective-permute-start(bf16[32,2304]{1,0:T(8,128)(2,1)} %collective-permute-done.7.refs_2_), channel_id=1, source_target_pairs={{0,2},{1,3},{4,0},{5,1},{8,4},{9,5},{12,8},{13,9},{14,12},{15,13},... | collective-permute-start | bytes 442376 | tf_op jit(solution)/shard_map/ppermute | solution.py:47
  45.3 7.0 %copy-done.1 = bf16[4608,2304]{1,0:T(8,128)(2,1)S(1)} copy-done((bf16[4608,2304]{1,0:T(8,128)(2,1)S(1)}, bf16[4608,2304]{1,0:T(8,128)(2,1)}, u32[]{:S(2)}) %copy-start.1) | copy-done | bytes 21233688
  53.4 4.4 %shard_map.69.refs_4_.refs_5_.refs_2_ = f32[192,2304]{1,0:T(8,128)S(1)} custom-call(bf16[32,4608]{1,0:T(8,128)(2,1)S(1)} %copy-done.7, bf16[32,4608]{1,0:T(8,128)(2,1)S(1)} %collective-permute-done.12.refs_1_, bf16[128,2304]{1,0:T(8,128)(2,1)S(1)} %shard_map.66.refs_3_.refs_2_, bf16[128,2304]{1,0:T(8,128)(2,1)S(1)} %copy-done.9, ...), custom_call_target="tpu_custom_call" | custom-call | flops 4076863488 | tf_op jit(solution)/shard_map/pallas_call | solution.py:82
  57.8 2.1 %shard_map.70.refs_4_ = bf16[16,32,128]{2,1,0:T(8,128)(2,1)} custom-call(bf16[32,4608]{1,0:T(8,128)(2,1)S(1)} %copy-done.7, bf16[32,4608]{1,0:T(8,128)(2,1)S(1)} %collective-permute-done.12.refs_1_, bf16[8,32,576]{2,1,0:T(8,128)(2,1)} %all-to-all-done.refs_2_, bf16[128,2304]{1,0:T(8,128)(2,1)S(1)} %shard_map.68.refs_3_.refs_0_, ...), custom_call_target="tpu_custom_call" | custom-call | tf_op jit(solution)/shard_map/pallas_call | solution.py:82
  59.9 2.0 %shard_map.71.refs_3_.refs_2_ = bf16[128,2304]{1,0:T(8,128)(2,1)} custom-call(bf16[32,2304]{1,0:T(8,128)(2,1)} %collective-permute-done.2.refs_0_, bf16[32,2304]{1,0:T(8,128)(2,1)} %collective-permute-done.5.refs_1_, bf16[32,2304]{1,0:T(8,128)(2,1)} %collective-permute-done.8.refs_2_, bf16[32,2304]{1,0:T(8,128)(2,1)} %collective-permute-done.11.refs_3_, ...), custom_call_target="tpu_custom_call" | custom-call | tf_op jit(solution)/shard_map/pallas_call | solution.py:82
  62.0 2.0 %collective-permute-start.17 = (bf16[32,2304]{1,0:T(8,128)(2,1)}, bf16[32,2304]{1,0:T(8,128)(2,1)}, u32[]{:S(2)}, u32[]{:S(2)}) collective-permute-start(bf16[32,2304]{1,0:T(8,128)(2,1)} %collective-permute-done.11.refs_3_), channel_id=1, source_target_pairs={{0,2},{1,3},{4,0},{5,1},{8,4},{9,5},{12,8},{13,9},{14,12},{15,13},... | collective-permute-start | bytes 442376 | tf_op jit(solution)/shard_map/ppermute | solution.py:51
  64.0 6.1 %all-to-all-start.1 = ((bf16[16,32,128]{2,1,0:T(8,128)(2,1)}), bf16[16,32,128]{2,1,0:T(8,128)(2,1)}, u32[]{:S(2)}, u32[]{:S(2)}) async-start(bf16[16,32,128]{2,1,0:T(8,128)(2,1)} %shard_map.70.refs_4_), calls=%async_computation.1 | async-start | bytes 262144 | tf_op jit(solution)/shard_map/all_to_all | solution.py:345
  70.1 7.0 %copy-done.2 = bf16[4608,2304]{1,0:T(8,128)(2,1)S(1)} copy-done((bf16[4608,2304]{1,0:T(8,128)(2,1)S(1)}, bf16[4608,2304]{1,0:T(8,128)(2,1)}, u32[]{:S(2)}) %copy-start.2) | copy-done | bytes 21233688
  77.2 4.1 %shard_map.72.refs_3_ = f32[128,2304]{1,0:T(8,128)S(1)} custom-call(bf16[128,2304]{1,0:T(8,128)(2,1)S(1)} %shard_map.68.refs_3_.refs_0_, bf16[128,2304]{1,0:T(8,128)(2,1)} %collective-permute-done.18.refs_1_, bf16[4608,2304]{1,0:T(8,128)(2,1)S(1)} %copy-done.2, bf16[128,2304]{1,0:T(8,128)(2,1)} %shard_map.71.refs_3_.refs_2_, ...), custom_call_target="tpu_custom_call" | custom-call | flops 2717908992 | tf_op jit(solution)/shard_map/pallas_call | solution.py:82
  82.8 1.7 %copy-done.5 = bf16[4,128,2304]{2,1,0:T(8,128)(2,1)S(1)} copy-done((bf16[4,128,2304]{2,1,0:T(8,128)(2,1)S(1)}, bf16[4,128,2304]{2,1,0:T(8,128)(2,1)}, u32[]{:S(2)}) %copy-start.5) | copy-done | bytes 2359320
  84.4 2.5 %shard_map.74.refs_9_ = bf16[512,2304]{1,0:T(8,128)(2,1)} custom-call(s32[4]{0:T(128)S(1)} %bitcast.4, s32[4]{0:T(128)S(1)} %copy-done.12, f32[192,2304]{1,0:T(8,128)S(1)} %shard_map.69.refs_4_.refs_5_.refs_2_, f32[128,2304]{1,0:T(8,128)S(1)} %shard_map.72.refs_3_, bf16[16,32,128]{2,1,0:T(8,128)(2,1)} %all-to-all-done.1.refs_2_.refs_4_.refs_6_, ...), custom_call_target="tpu_custom_call" | custom-call | bytes 1474560 | tf_op jit(solution)/shard_map/pallas_call | solution.py:294
  87.0 7.0 %copy-done.3 = bf16[4608,2304]{1,0:T(8,128)(2,1)S(1)} copy-done((bf16[4608,2304]{1,0:T(8,128)(2,1)S(1)}, bf16[4608,2304]{1,0:T(8,128)(2,1)}, u32[]{:S(2)}) %copy-start.3) | copy-done | bytes 21233688
  94.1 6.7 %shard_map.75 = bf16[512,2304]{1,0:T(8,128)(2,1)} custom-call(s32[4]{0:T(128)S(1)} %bitcast.5, s32[4]{0:T(128)S(1)} %copy-done.12, bf16[128,2304]{1,0:T(8,128)(2,1)} %shard_map.71.refs_3_.refs_2_, bf16[128,2304]{1,0:T(8,128)(2,1)} %collective-permute-done.15.refs_3_, bf16[64,2304]{1,0:T(8,128)(2,1)S(1)} %shard_map.73.refs_6_.refs_4_, ...), custom_call_target="tpu_custom_call", output_to_operand_aliasing={{}: (9, {})} | custom-call | flops 4076863488 | bytes 884736 | tf_op jit(solution)/shard_map/pallas_call | solution.py:294
  (59 shorter events, 9.9 us)
Async XLA Ops:
  1.0 14.5 %collective-permute-start.9 = (bf16[32,2304]{1,0:T(8,128)(2,1)S(1)}, bf16[32,2304]{1,0:T(8,128)(2,1)S(1)}, u32[]{:S(2)}, u32[]{:S(2)}) collective-permute-start(bf16[32,2304]{1,0:T(8,128)(2,1)S(1)} %get-tuple-element.13), channel_id=1, source_target_pairs={{0,2},{1,3},{4,0},{5,1},{8,4},{9,5},{12,8},{13,9},{14,12},{15,13},... | collective-permute-start | bytes 442376 | tf_op jit(solution)/shard_map/ppermute | solution.py:47
  4.0 11.5 %collective-permute-start.3 = (bf16[32,2304]{1,0:T(8,128)(2,1)S(1)}, bf16[32,2304]{1,0:T(8,128)(2,1)S(1)}, u32[]{:S(2)}, u32[]{:S(2)}) collective-permute-start(bf16[32,2304]{1,0:T(8,128)(2,1)S(1)} %get-tuple-element.13), channel_id=1, source_target_pairs={{0,4},{1,5},{4,8},{5,9},{8,12},{9,13},{12,14},{13,15},{14,10},{15,... | collective-permute-start | bytes 442376 | tf_op jit(solution)/shard_map/ppermute | solution.py:46
  4.1 11.4 %collective-permute-start.6 = (bf16[32,2304]{1,0:T(8,128)(2,1)S(1)}, bf16[32,2304]{1,0:T(8,128)(2,1)S(1)}, u32[]{:S(2)}, u32[]{:S(2)}) collective-permute-start(bf16[32,2304]{1,0:T(8,128)(2,1)S(1)} %get-tuple-element.14), channel_id=1, source_target_pairs={{0,2},{1,3},{4,0},{5,1},{8,4},{9,5},{12,8},{13,9},{14,12},{15,13},... | collective-permute-start | bytes 442376 | tf_op jit(solution)/shard_map/ppermute | solution.py:47
  6.1 9.5 %collective-permute-start = (bf16[32,2304]{1,0:T(8,128)(2,1)S(1)}, bf16[32,2304]{1,0:T(8,128)(2,1)S(1)}, u32[]{:S(2)}, u32[]{:S(2)}) collective-permute-start(bf16[32,2304]{1,0:T(8,128)(2,1)S(1)} %get-tuple-element.14), channel_id=1, source_target_pairs={{0,4},{1,5},{4,8},{5,9},{8,12},{9,13},{12,14},{13,15},{14,10},{15,... | collective-permute-start | bytes 442376 | tf_op jit(solution)/shard_map/ppermute | solution.py:46
  15.5 14.0 %copy-start.7 = (bf16[32,4608]{1,0:T(8,128)(2,1)S(1)}, bf16[32,4608]{1,0:T(8,128)(2,1)}, u32[]{:S(2)}) copy-start(bf16[32,4608]{1,0:T(8,128)(2,1)} %refs_0_.3) | copy-start | bytes 884740
  15.5 14.0 %copy-start.11 = (s32[4,1]{0,1:T(1,128)S(1)}, s32[4,1]{0,1:T(1,128)}, u32[]{:S(2)}) copy-start(s32[4,1]{0,1:T(1,128)} %param.10) | copy-start | bytes 52
  22.7 21.7 %collective-permute-start.14 = (bf16[128,2304]{1,0:T(8,128)(2,1)S(1)}, bf16[128,2304]{1,0:T(8,128)(2,1)S(1)}, u32[]{:S(2)}, u32[]{:S(2)}) collective-permute-start(bf16[128,2304]{1,0:T(8,128)(2,1)S(1)} %shard_map.66.refs_3_.refs_2_), channel_id=1, source_target_pairs={{0,1},{1,0},{2,3},{3,2},{4,5},{5,4},{6,7},{7,6},{8,9},{9,8},{10,11... | collective-permute-start | bytes 1769480 | tf_op jit(solution)/shard_map/ppermute | solution.py:21
  22.7 6.8 %collective-permute-start.10 = (bf16[32,2304]{1,0:T(8,128)(2,1)S(1)}, bf16[32,2304]{1,0:T(8,128)(2,1)}, u32[]{:S(2)}, u32[]{:S(2)}) collective-permute-start(bf16[32,2304]{1,0:T(8,128)(2,1)S(1)} %collective-permute-done.9.refs_3_), channel_id=1, source_target_pairs={{0,2},{1,3},{4,0},{5,1},{8,4},{9,5},{12,8},{13,9},{14,12},{15,13},... | collective-permute-start | bytes 442376 | tf_op jit(solution)/shard_map/ppermute | solution.py:47
  24.7 2.3 %collective-permute-start.13 = (bf16[2,32,576]{2,1,0:T(8,128)(2,1)S(1)}, bf16[2,32,576]{2,1,0:T(8,128)(2,1)S(1)}, u32[]{:S(2)}, u32[]{:S(2)}) collective-permute-start(bf16[2,32,576]{2,1,0:T(8,128)(2,1)S(1)} %get-tuple-element.10), channel_id=1, source_target_pairs={{0,1},{1,0},{2,3},{3,2},{4,5},{5,4},{6,7},{7,6},{8,9},{9,8},{10,11... | collective-permute-start | bytes 221192 | tf_op jit(solution)/shard_map/ppermute | solution.py:21
  25.0 6.8 %collective-permute-start.4 = (bf16[32,2304]{1,0:T(8,128)(2,1)S(1)}, bf16[32,2304]{1,0:T(8,128)(2,1)}, u32[]{:S(2)}, u32[]{:S(2)}) collective-permute-start(bf16[32,2304]{1,0:T(8,128)(2,1)S(1)} %collective-permute-done.3.refs_1_), channel_id=1, source_target_pairs={{0,4},{1,5},{4,8},{5,9},{8,12},{9,13},{12,14},{13,15},{14,10},{15,... | collective-permute-start | bytes 442376 | tf_op jit(solution)/shard_map/ppermute | solution.py:46
  25.3 7.2 %collective-permute-start.7 = (bf16[32,2304]{1,0:T(8,128)(2,1)S(1)}, bf16[32,2304]{1,0:T(8,128)(2,1)}, u32[]{:S(2)}, u32[]{:S(2)}) collective-permute-start(bf16[32,2304]{1,0:T(8,128)(2,1)S(1)} %collective-permute-done.6.refs_2_), channel_id=1, source_target_pairs={{0,2},{1,3},{4,0},{5,1},{8,4},{9,5},{12,8},{13,9},{14,12},{15,13},... | collective-permute-start | bytes 442376 | tf_op jit(solution)/shard_map/ppermute | solution.py:47
  27.0 7.3 %collective-permute-start.1 = (bf16[32,2304]{1,0:T(8,128)(2,1)S(1)}, bf16[32,2304]{1,0:T(8,128)(2,1)}, u32[]{:S(2)}, u32[]{:S(2)}) collective-permute-start(bf16[32,2304]{1,0:T(8,128)(2,1)S(1)} %collective-permute-done.refs_0_), channel_id=1, source_target_pairs={{0,4},{1,5},{4,8},{5,9},{8,12},{9,13},{12,14},{13,15},{14,10},{15,... | collective-permute-start | bytes 442376 | tf_op jit(solution)/shard_map/ppermute | solution.py:46
  29.6 12.9 %collective-permute-start.12 = (bf16[32,4608]{1,0:T(8,128)(2,1)S(1)}, bf16[32,4608]{1,0:T(8,128)(2,1)S(1)}, u32[]{:S(2)}, u32[]{:S(2)}) collective-permute-start(bf16[32,4608]{1,0:T(8,128)(2,1)S(1)} %copy-done.7), channel_id=1, source_target_pairs={{0,1},{1,0},{2,3},{3,2},{4,5},{5,4},{6,7},{7,6},{8,9},{9,8},{10,11... | collective-permute-start | bytes 884744 | tf_op jit(solution)/shard_map/ppermute | solution.py:21
  35.4 34.7 %collective-permute-start.18 = (bf16[128,2304]{1,0:T(8,128)(2,1)S(1)}, bf16[128,2304]{1,0:T(8,128)(2,1)}, u32[]{:S(2)}, u32[]{:S(2)}) collective-permute-start(bf16[128,2304]{1,0:T(8,128)(2,1)S(1)} %shard_map.68.refs_3_.refs_0_), channel_id=1, source_target_pairs={{0,1},{1,0},{2,3},{3,2},{4,5},{5,4},{6,7},{7,6},{8,9},{9,8},{10,11... | collective-permute-start | bytes 1769480 | tf_op jit(solution)/shard_map/ppermute | solution.py:21
  35.5 22.3 %all-to-all-start = ((bf16[8,32,576]{2,1,0:T(8,128)(2,1)}), bf16[8,32,576]{2,1,0:T(8,128)(2,1)}, u32[]{:S(2)}, u32[]{:S(2)}) async-start(bf16[8,32,576]{2,1,0:T(8,128)(2,1)} %shard_map.67.refs_4_.refs_5_), calls=%async_computation | async-start | bytes 655360 | tf_op jit(solution)/shard_map/all_to_all | solution.py:333
  40.4 19.5 %collective-permute-start.11 = (bf16[32,2304]{1,0:T(8,128)(2,1)}, bf16[32,2304]{1,0:T(8,128)(2,1)}, u32[]{:S(2)}, u32[]{:S(2)}) collective-permute-start(bf16[32,2304]{1,0:T(8,128)(2,1)} %collective-permute-done.10.refs_3_), channel_id=1, source_target_pairs={{0,2},{1,3},{4,0},{5,1},{8,4},{9,5},{12,8},{13,9},{14,12},{15,13},... | collective-permute-start | bytes 442376 | tf_op jit(solution)/shard_map/ppermute | solution.py:47
  42.4 17.5 %collective-permute-start.5 = (bf16[32,2304]{1,0:T(8,128)(2,1)}, bf16[32,2304]{1,0:T(8,128)(2,1)}, u32[]{:S(2)}, u32[]{:S(2)}) collective-permute-start(bf16[32,2304]{1,0:T(8,128)(2,1)} %collective-permute-done.4.refs_1_), channel_id=1, source_target_pairs={{0,4},{1,5},{4,8},{5,9},{8,12},{9,13},{12,14},{13,15},{14,10},{15,... | collective-permute-start | bytes 442376 | tf_op jit(solution)/shard_map/ppermute | solution.py:46
  42.5 17.4 %collective-permute-start.8 = (bf16[32,2304]{1,0:T(8,128)(2,1)}, bf16[32,2304]{1,0:T(8,128)(2,1)}, u32[]{:S(2)}, u32[]{:S(2)}) collective-permute-start(bf16[32,2304]{1,0:T(8,128)(2,1)} %collective-permute-done.7.refs_2_), channel_id=1, source_target_pairs={{0,2},{1,3},{4,0},{5,1},{8,4},{9,5},{12,8},{13,9},{14,12},{15,13},... | collective-permute-start | bytes 442376 | tf_op jit(solution)/shard_map/ppermute | solution.py:47
  45.3 14.6 %collective-permute-start.2 = (bf16[32,2304]{1,0:T(8,128)(2,1)}, bf16[32,2304]{1,0:T(8,128)(2,1)}, u32[]{:S(2)}, u32[]{:S(2)}) collective-permute-start(bf16[32,2304]{1,0:T(8,128)(2,1)} %collective-permute-done.1.refs_0_), channel_id=1, source_target_pairs={{0,4},{1,5},{4,8},{5,9},{8,12},{9,13},{12,14},{13,15},{14,10},{15,... | collective-permute-start | bytes 442376 | tf_op jit(solution)/shard_map/ppermute | solution.py:46
  61.9 25.1 %collective-permute-start.15 = (bf16[128,2304]{1,0:T(8,128)(2,1)}, bf16[128,2304]{1,0:T(8,128)(2,1)}, u32[]{:S(2)}, u32[]{:S(2)}) collective-permute-start(bf16[128,2304]{1,0:T(8,128)(2,1)} %shard_map.71.refs_3_.refs_2_), channel_id=1, source_target_pairs={{0,1},{1,0},{2,3},{3,2},{4,5},{5,4},{6,7},{7,6},{8,9},{9,8},{10,11... | collective-permute-start | bytes 1769480 | tf_op jit(solution)/shard_map/ppermute | solution.py:21
  62.0 19.4 %collective-permute-start.17 = (bf16[32,2304]{1,0:T(8,128)(2,1)}, bf16[32,2304]{1,0:T(8,128)(2,1)}, u32[]{:S(2)}, u32[]{:S(2)}) collective-permute-start(bf16[32,2304]{1,0:T(8,128)(2,1)} %collective-permute-done.11.refs_3_), channel_id=1, source_target_pairs={{0,2},{1,3},{4,0},{5,1},{8,4},{9,5},{12,8},{13,9},{14,12},{15,13},... | collective-permute-start | bytes 442376 | tf_op jit(solution)/shard_map/ppermute | solution.py:51
  63.9 17.4 %collective-permute-start.16 = (bf16[32,2304]{1,0:T(8,128)(2,1)}, bf16[32,2304]{1,0:T(8,128)(2,1)}, u32[]{:S(2)}, u32[]{:S(2)}) collective-permute-start(bf16[32,2304]{1,0:T(8,128)(2,1)} %collective-permute-done.2.refs_0_), channel_id=1, source_target_pairs={{0,4},{1,5},{4,8},{5,9},{8,12},{9,13},{12,14},{13,15},{14,10},{15,... | collective-permute-start | bytes 442376 | tf_op jit(solution)/shard_map/ppermute | solution.py:51
  64.0 17.3 %all-to-all-start.1 = ((bf16[16,32,128]{2,1,0:T(8,128)(2,1)}), bf16[16,32,128]{2,1,0:T(8,128)(2,1)}, u32[]{:S(2)}, u32[]{:S(2)}) async-start(bf16[16,32,128]{2,1,0:T(8,128)(2,1)} %shard_map.70.refs_4_), calls=%async_computation.1 | async-start | bytes 262144 | tf_op jit(solution)/shard_map/all_to_all | solution.py:345
  82.3 4.7 %collective-permute-start.19 = (bf16[64,2304]{1,0:T(8,128)(2,1)S(1)}, bf16[64,2304]{1,0:T(8,128)(2,1)S(1)}, u32[]{:S(2)}, u32[]{:S(2)}) collective-permute-start(bf16[64,2304]{1,0:T(8,128)(2,1)S(1)} %shard_map.73.refs_6_.refs_4_), channel_id=1, source_target_pairs={{0,1},{1,0},{2,3},{3,2},{4,5},{5,4},{6,7},{7,6},{8,9},{9,8},{10,11... | collective-permute-start | bytes 884744 | tf_op jit(solution)/shard_map/ppermute | solution.py:21
  (11 other events, 50.7 us)

commit v5 on v0

v5 whole, which is shorter than its diff:
```python
import functools

import jax
import jax.numpy as jnp
from jax import lax
from jax.experimental import pallas as pl
from jax.experimental.pallas import tpu as pltpu
from jax.sharding import PartitionSpec as P

BLOCK = 128
AXES = ("seq", "adapter")
CHUNKS = 2


def ring_perm(n, way):
    order = [2 * z for z in range(n // 2)] + [2 * z + 1 for z in reversed(range(n // 2))]
    return [(2 * s + c, 2 * order[(pos + way) % n] + c) for pos, s in enumerate(order) for c in range(2)]


def swap_cores(x, n):
    return lax.ppermute(x, AXES, [(2 * s + c, 2 * s + 1 - c) for s in range(n) for c in range(2)])


def chip_at(distance, n):
    s = lax.axis_index("seq")
    z = s >> 1
    pos = jnp.where(s & 1 == 0, z, n - 1 - z) + distance
    pos = jnp.where(pos >= n, pos - n, pos)
    pos = jnp.where(pos < 0, pos + n, pos)
    return jnp.where(pos < n // 2, 2 * pos, 2 * (n - 1 - pos) + 1)


def y_perm(n):
    return [(2 * s + c, 2 * (s ^ 1) + c) for s in range(n) for c in range(2)]


def z_perm(n, shift):
    nz = n // 2
    return [
        (2 * (2 * z + y) + c, 2 * (2 * ((z - shift) % nz) + y) + c)
        for z in range(nz)
        for y in range(2)
        for c in range(2)
    ]


def hop_distances(hop, n):
    if hop == 0:
        return [0]
    return [-hop, hop] if hop < n // 2 else [hop]


class Ring:
    def __init__(self, chunks, n):
        self.n, self.up, self.down = n, list(chunks), list(chunks)

    def hop(self, hop):
        n = self.n
        if hop < n // 2:
            self.up = [lax.ppermute(x, AXES, ring_perm(n, 1)) for x in self.up]
            self.down = [lax.ppermute(x, AXES, ring_perm(n, -1)) for x in self.down]
            return self.up + self.down
        return [
            lax.ppermute((self.down if k % 2 else self.up)[k], AXES, ring_perm(n, -1 if k % 2 else 1))
            for k in range(CHUNKS)
        ]


def join_kernel(*refs):
    *pieces, out = refs
    rows = pieces[0].shape[0]
    for i, piece in enumerate(pieces):
        out[i * rows : (i + 1) * rows, :] = piece[...]


def join(pieces, after):
    rows, depth = pieces[0].shape
    (joined,) = call(join_kernel, [], pieces, after, [((rows * len(pieces), depth), pieces[0].dtype)])
    return joined


def whole(count):
    return [pl.BlockSpec(memory_space=pltpu.VMEM)] * count


def in_vmem(arrays):
    return [pltpu.with_memory_space_constraint(x, pltpu.VMEM) for x in arrays]


def call(kernel, scalars, arrays, after, outs, scratch=(), limit=8, flops=0):
    operands = len(scalars) + len(arrays)

    def body(*refs):
        kernel(*refs[:operands], *refs[operands + len(after) :])

    return pl.pallas_call(
        body,
        out_shape=[pltpu.VMEM(shape, dtype) for shape, dtype in outs],
        in_specs=[pl.BlockSpec(memory_space=pltpu.SMEM)] * len(scalars)
        + whole(len(arrays))
        + [pl.BlockSpec(memory_space=pl.ANY)] * len(after),
        out_specs=whole(len(outs)),
        scratch_shapes=list(scratch),
        compiler_params=pltpu.CompilerParams(vmem_limit_bytes=limit << 20),
        cost_estimate=pl.CostEstimate(flops=flops, bytes_accessed=0, transcendentals=0),
    )(*scalars, *in_vmem(arrays), *after)


class Window:
    def __init__(self, n, width, depth):
        self.width, self.depth = width, depth
        self.size = -(-(width + max(s * width % 128 for s in range(n))) // 128) * 128
        for s in range(n):
            start = s * width // 128 * 128
            assert start // depth == (start + self.size - 1) // depth

    def start(self, chip):
        return (chip * self.width) >> 7 << 7

    def shift(self, chip):
        return chip * self.width - self.start(chip)


def prepare_kernel(n, window, distances, tokens, down, factor, *sends):
    s = lax.axis_index("seq")
    zeros = jnp.zeros((down.shape[1], window.size - window.width), jnp.float32)
    for index in range(down.shape[0]):
        wide = jnp.concatenate([down[index], zeros], 1)
        factor[index] = pltpu.roll(wide, window.shift(s), 1).astype(jnp.bfloat16)
    for distance, send in zip(distances, sends):
        start = pl.multiple_of(window.start(chip_at(distance, n)), 128)
        send[...] = tokens[:, pl.ds(start, window.size)]


def pack(parts, out):
    chips, rows, rank = parts.shape
    for t in range(chips):
        i, k = t % (chips // 2), t // (chips // 2)
        out[i * rows : (i + 1) * rows, k * rank : (k + 1) * rank] = parts[t].astype(out.dtype)


def partial_kernel(n, window, groups, opposite, adapters, *refs):
    *pieces, factor, other, received, total, rounded, parts = refs
    s, c = lax.axis_index("seq"), lax.axis_index("adapter")
    rows, held = received.shape[0], factor.shape[0]
    start = window.start(s)
    chunk = jnp.where(start >= window.depth, 1, 0)
    inside = pl.multiple_of(start - chunk * window.depth, 128)
    found = []
    for piece, distances in zip(pieces, groups):
        for i, distance in enumerate(distances):
            row = pl.multiple_of((i * CHUNKS + chunk) * rows, rows)
            found.append((distance, piece[pl.ds(row, rows), pl.ds(inside, window.size)]))
    for distance, x in [*found, (opposite, received[...])]:
        chip = chip_at(distance, n)
        adapter = adapters[chip * 2 * rows // BLOCK]
        index = lax.rem(adapter, held)
        mine = (adapter >= c * held) & (adapter < (c + 1) * held)
        weights = jnp.where(mine, factor[index], other[index])
        parts[chip] = lax.dot_general(x, weights, (((1,), (1,)), ((), ())), preferred_element_type=jnp.float32)
    pack(parts, total)
    rounded[...] = total[...].astype(jnp.bfloat16)


def add_kernel(total, *refs):
    *received, out, rounded = refs
    value = total[...]
    for x in received:
        value += x[...].astype(jnp.float32)
    out[...] = value
    rounded[...] = value.astype(jnp.bfloat16)


def load_kernel(chunk, w_ref, *refs):
    *up_refs, sems = refs
    w_out = up_refs.pop(1 if len(up_refs) > 1 else 0)
    parts = sems.shape[0] - 1
    depth = w_out.shape[0] // parts
    first = chunk * w_out.shape[0]
    copies = [
        pltpu.make_async_copy(
            w_ref.at[pl.ds(first + k * depth, depth), :], w_out.at[pl.ds(k * depth, depth), :], sems.at[k]
        )
        for k in range(parts)
    ]
    if up_refs:
        up_ref, up_out, held = up_refs
        up_copy = pltpu.make_async_copy(up_ref, held, sems.at[parts])
        up_copy.start()
    for copy in copies:
        copy.start()
    if up_refs:
        up_copy.wait()
        up_out[...] = held[...].astype(jnp.bfloat16)
    for copy in copies:
        copy.wait()


def load(weight, chunk, up=None):
    depth, width = weight.shape[0] // CHUNKS, weight.shape[1]
    ups = [] if up is None else [up]
    return pl.pallas_call(
        functools.partial(load_kernel, chunk),
        out_shape=[pltpu.VMEM((depth, width), weight.dtype)] + [pltpu.VMEM(x.shape, jnp.bfloat16) for x in ups],
        in_specs=[pl.BlockSpec(memory_space=pltpu.HBM)] * (1 + len(ups)),
        out_specs=whole(1 + len(ups)),
        scratch_shapes=[pltpu.VMEM(x.shape, x.dtype) for x in ups] + [pltpu.SemaphoreType.DMA((5,))],
        compiler_params=pltpu.CompilerParams(vmem_limit_bytes=8 << 20),
        cost_estimate=pl.CostEstimate(flops=0, bytes_accessed=2 * depth * width, transcendentals=0),
    )(*(pltpu.with_memory_space_constraint(x, pltpu.HBM) for x in [weight, *ups]))


def assemble(pairs, rows, held):
    width = held.shape[1]
    c = lax.axis_index("adapter")
    first = 0
    for pair in pairs:
        depth = pair[0].shape[1]
        chunks = width // depth
        for chip in range(pair[0].shape[0] // (rows * chunks)):
            for k in range(chunks):
                at = (chip * chunks + k) * rows
                for ref, core in zip(pair, (c, 1 - c)):
                    row = pl.multiple_of(first + core * rows, rows)
                    held[pl.ds(row, rows), k * depth : (k + 1) * depth] = ref[at : at + rows, :]
            first += 2 * rows


def tile_width(width):
    return 768 if width % 768 == 0 else width


def multiply(held, weights, at):
    depth = weights[0].shape[0]
    return sum(
        jnp.dot(held[:, k * depth : (k + 1) * depth], w[:, at], preferred_element_type=jnp.float32)
        for k, w in enumerate(weights)
    )


def base_kernel(rows, count, *refs):
    pairs, weights, (base, held) = refs[:count], refs[count : count + CHUNKS], refs[count + CHUNKS :]
    assemble(list(zip(pairs[::2], pairs[1::2])), rows, held)
    width = base.shape[1]
    columns = tile_width(width)
    for j in range(0, width, columns):
        at = slice(j, j + columns)
        base[:, at] = multiply(held, weights, at)


def base_rows(pairs, chips, rows, weights, after):
    total, depth, width = 2 * rows * chips, CHUNKS * weights[0].shape[0], weights[0].shape[1]
    arrays = [x for pair in pairs for x in pair]
    (base,) = call(
        functools.partial(base_kernel, rows, len(arrays)),
        [],
        arrays + weights,
        after,
        [((total, width), jnp.float32)],
        [pltpu.VMEM((total, depth), jnp.bfloat16)],
        limit=8 + (2 * total * depth >> 20),
        flops=2 * total * depth * width,
    )
    return base


def finish_kernel(n, rows, groups, adapters, live, *refs):
    *bases, own, other, up_ref, out_ref, shrink, block, sems = refs
    c = lax.axis_index("adapter")
    chip_rows, rank = 2 * rows, up_ref.shape[1]
    tiles, _, columns = block.shape
    for t in range(n):
        i, k = t % (n // 2), t // (n // 2)
        for ref, core in ((own, c), (other, 1 - c)):
            part = ref[i * rows : (i + 1) * rows, k * rank : (k + 1) * rank]
            shrink[t, pl.ds(pl.multiple_of(core * rows, rows), rows), :] = part.astype(jnp.bfloat16)
    places = [
        (distance, base, i * chip_rows)
        for base, distances in zip(bases, groups)
        for i, distance in enumerate(distances)
    ]
    copies = []
    for j in range(tiles):
        at = slice(j * columns, (j + 1) * columns)
        for i, (distance, base, row) in enumerate(places):
            chip = chip_at(distance, n)
            first = chip * chip_rows
            of_block = first // BLOCK
            delta = jnp.dot(shrink[chip], up_ref[adapters[of_block], :, at], preferred_element_type=jnp.float32)
            index = lax.broadcasted_iota(jnp.int32, delta.shape, 0) + (first - of_block * BLOCK)
            total = jnp.where(index < live[of_block], base[row : row + chip_rows, at] + delta, 0.0)
            place = pl.ds(i * chip_rows, chip_rows)
            block[j, place, :] = total.astype(out_ref.dtype)
            copies.append(
                pltpu.make_async_copy(
                    block.at[j, place, :],
                    out_ref.at[pl.ds(pl.multiple_of(first, chip_rows), chip_rows), pl.ds(j * columns, columns)],
                    sems.at[j, i],
                )
            )
            copies[-1].start()
    for copy in copies:
        copy.wait()


def finish(n, rows, groups, scalars, bases, own, other, up):
    rank, width = up.shape[1:]
    total, columns = 2 * n * rows, tile_width(width)
    arrays = [*bases, own, other, up]
    return pl.pallas_call(
        functools.partial(finish_kernel, n, rows, groups),
        out_shape=jax.ShapeDtypeStruct((total, width), jnp.bfloat16),
        in_specs=[pl.BlockSpec(memory_space=pltpu.SMEM)] * len(scalars) + whole(len(arrays)),
        out_specs=pl.BlockSpec(memory_space=pl.ANY),
        scratch_shapes=[
            pltpu.VMEM((n, 2 * rows, rank), jnp.bfloat16),
            pltpu.VMEM((width // columns, total, columns), jnp.bfloat16),
            pltpu.SemaphoreType.DMA((width // columns, n)),
        ],
        compiler_params=pltpu.CompilerParams(vmem_limit_bytes=8 << 20),
        cost_estimate=pl.CostEstimate(
            flops=2 * total * rank * width, bytes_accessed=2 * total * width, transcendentals=0
        ),
    )(*scalars, *in_vmem(arrays))


def on_device(n, tokens, weight, down, up, adapter_per_block, rows_per_block):
    rows, features = tokens.shape
    depth = features // CHUNKS
    held, width, rank = down.shape
    last = n // 2
    adapters = adapter_per_block[:, 0]
    window = Window(n, width, depth)
    early = [d for hop in range(last - 1) for d in hop_distances(hop, n)]
    late = hop_distances(last - 1, n)

    chunks = [tokens[:, k * depth : (k + 1) * depth] for k in range(CHUNKS)]
    ring = Ring(chunks, n)
    factor, send = call(
        functools.partial(prepare_kernel, n, window, [last]),
        [],
        [tokens, jnp.swapaxes(down, 1, 2)],
        [],
        [((held, rank, window.size), jnp.bfloat16), ((rows, window.size), jnp.bfloat16)],
    )
    received = lax.ppermute(send, AXES, ring_perm(n, last))
    other_factor = swap_cores(factor, n)
    weights, (last_weight, up) = [load(weight, k)[0] for k in range(CHUNKS - 1)], load(weight, CHUNKS - 1, up)
    weights.append(last_weight)

    pieces = chunks + [x for hop in range(1, last - 1) for x in ring.hop(hop)]
    near = join(pieces, [*weights, received, other_factor])
    far = join(ring.hop(last - 1), [])
    half = (n // 2 * rows, 2 * rank)
    sums = [(half, jnp.float32), (half, jnp.bfloat16)]
    total, rounded = call(
        functools.partial(partial_kernel, n, window, [early, late], last),
        [adapters],
        [near, far, factor, other_factor, received],
        [],
        sums,
        [pltpu.VMEM((n, rows, rank), jnp.float32)],
    )
    bases = [base_rows([(near, swap_cores(near, n))], len(early), rows, weights, [rounded])]
    total, rounded = call(add_kernel, [], [total, lax.ppermute(rounded, AXES, y_perm(n))], [], sums)
    final = join(ring.hop(last), [*bases, rounded])
    total, rounded = call(
        add_kernel,
        [],
        [total] + [lax.ppermute(rounded, AXES, z_perm(n, shift)) for shift in range(1, n // 2)],
        [final],
        sums,
    )
    pairs = [(x, swap_cores(x, n)) for x in (far, final)]
    bases.append(base_rows(pairs, len(late) + 1, rows, weights, [rounded]))
    return finish(
        n,
        rows,
        [early, late + [last]],
        [adapters, rows_per_block],
        bases,
        total,
        swap_cores(rounded, n),
        up,
    )


def solution(mesh):
    placed = (
        P(("groups", "seq", "adapter"), None),
        P(None, ("seq", "adapter")),
        P(("groups", "adapter"), "seq", None),
        P("groups", None, ("seq", "adapter")),
        P("groups", None),
        P("groups"),
    )
    return jax.shard_map(
        functools.partial(on_device, mesh.shape["seq"]),
        mesh=mesh,
        in_specs=placed,
        out_specs=P("groups", ("seq", "adapter")),
        check_vma=False,
    )
```

time: 189 us -> 69.1 us (0.37)
  waiting for transfers between devices: 138 us -> 15 us
  matrix products: 34.6 us -> 0 us
  starting transfers between devices: 0.04 us -> 26.4 us
  Pallas kernels: 0 us -> 24.1 us
  between operations: 13.5 us -> 0.41 us
    psum x1 -> x0, waiting for transfers between devices: 85.5 us -> none  [on_device(): rank_reduction = lax.psum(combined[:, ff_local:], ('seq', 'adapter'))]
    all_gather x1 -> x0, waiting for transfers between devices: 51.6 us -> none  [on_device(): device_rows = lax.all_gather(tokens, ('seq', 'adapter'), axis=0, tiled=True)]
    dot_general x6 -> x0, matrix products: 34.6 us -> none  [the longest x1 15.4 us: on_device(): jnp.dot(device_rows, shared_up_weight, preferred_element_type=jnp.float32)]
    ppermute x0 -> x24, starting transfers between devices: none -> 26.4 us  [the longest x6 8.43 us: hop(): self.up = [lax.ppermute(x, AXES, ring_perm(n, 1)) for x in self.up]]
    pallas_call x0 -> x12, Pallas kernels: none -> 24.1 us  [the longest x9 12.8 us: call(): pl.pallas_call(body, out_shape=[pltpu.VMEM(shape, dtype) for shape, dtype...]
    ppermute x0 -> x24, waiting for transfers between devices: none -> 15 us  [the longest x6 5.5 us: hop(): self.up = [lax.ppermute(x, AXES, ring_perm(n, 1)) for x in self.up]]
    unnamed x8, local copies, waits for them, and re-layouts: 0.02 us -> 1.95 us
  transfers between devices with their start and end apart: 2 -> 24, of which waited for: 2 -> 7; matrix products, arithmetic and copies ran while one was open for 4% -> 0% of each run, Pallas kernels for 0% -> 31%
where the time goes in v5:
time: 69.1 us; the launch traced here: 68.9 us
  starting transfers between devices  26.4 us (38%)
  Pallas kernels  24.1 us (35%)
  waiting for transfers between devices  15 us (22%)
  local copies, waits for them, and re-layouts  2.95 us (4%)
    pallas_call x9, Pallas kernels, call(): pl.pallas_call(body, out_shape=[pltpu.VMEM(shape, dtype) for shape, dtype...  12.8 us
    pallas_call x2, Pallas kernels, load(): pl.pallas_call(functools.partial(load_kernel, chunk), out_shape=[pltpu.VM...  8.96 us
    ppermute x6, starting transfers between devices, hop(): self.up = [lax.ppermute(x, AXES, ring_perm(n, 1)) for x in self.up]  8.43 us
    ppermute x6, starting transfers between devices, hop(): self.down = [lax.ppermute(x, AXES, ring_perm(n, -1)) for x in self.down]  5.82 us
    ppermute x6, waiting for transfers between devices, hop(): self.up = [lax.ppermute(x, AXES, ring_perm(n, 1)) for x in self.up]  5.5 us
    ppermute x1, starting transfers between devices, on_device(): received = lax.ppermute(send, AXES, ring_perm(n, last))  5.04 us
    ppermute x3, starting transfers between devices, on_device(): lax.ppermute(rounded, AXES, z_perm(n, shift))  4.43 us
    ppermute x3, waiting for transfers between devices, on_device(): lax.ppermute(rounded, AXES, z_perm(n, shift))  4.19 us
  transfers between devices with their start and end apart: 24, of which 7 were waited for; matrix products, arithmetic and copies ran while one was open for 0% of the time, Pallas kernels for 31%

profile of v5, /device:TPU:0, one launch (start us, length us, event | category | flops | bytes accessed | tf_op | source)
XLA Modules:
  0.0 68.9 jit_solution(5814597574599469196)
XLA Ops:
  0.0 1.0 %fusion = (bf16[32,2304]{1,0:T(8,128)(2,1)S(1)}, bf16[32,2304]{1,0:T(8,128)(2,1)S(1)}) fusion(bf16[32,4608]{1,0:T(8,128)(2,1)} %refs_0_.3), kind=kLoop, calls=%fused_computation | loop fusion | bytes 589824 | tf_op jit(solution)/shard_map/slice | solution.py:337
  1.0 3.1 %collective-permute-start = (bf16[32,2304]{1,0:T(8,128)(2,1)S(1)}, bf16[32,2304]{1,0:T(8,128)(2,1)S(1)}, u32[]{:S(2)}, u32[]{:S(2)}) collective-permute-start(bf16[32,2304]{1,0:T(8,128)(2,1)S(1)} %get-tuple-element.26.refs_0_), channel_id=1, source_target_pairs={{0,4},{1,5},{4,8},{5,9},{8,12},{9,13},{12,14},{13,15},{14,10},{15,... | collective-permute-start | bytes 442376 | tf_op jit(solution)/shard_map/ppermute | solution.py:60
  4.1 1.6 %collective-permute-start.1 = (bf16[32,2304]{1,0:T(8,128)(2,1)S(1)}, bf16[32,2304]{1,0:T(8,128)(2,1)S(1)}, u32[]{:S(2)}, u32[]{:S(2)}) collective-permute-start(bf16[32,2304]{1,0:T(8,128)(2,1)S(1)} %get-tuple-element.25.refs_1_), channel_id=1, source_target_pairs={{0,4},{1,5},{4,8},{5,9},{8,12},{9,13},{12,14},{13,15},{14,10},{15,... | collective-permute-start | bytes 442376 | tf_op jit(solution)/shard_map/ppermute | solution.py:60
  8.2 5.0 %collective-permute-start.8 = (bf16[32,640]{1,0:T(8,128)(2,1)S(1)}, bf16[32,640]{1,0:T(8,128)(2,1)S(1)}, u32[]{:S(2)}, u32[]{:S(2)}) collective-permute-start(bf16[32,640]{1,0:T(8,128)(2,1)S(1)} %get-tuple-element.16), channel_id=1, source_target_pairs={{0,14},{1,15},{4,10},{5,11},{8,6},{9,7},{12,2},{13,3},{14,0},{15,1... | collective-permute-start | bytes 122888 | tf_op jit(solution)/shard_map/ppermute | solution.py:346
  13.3 2.0 %collective-permute-done.8.refs_12_.refs_5_ = bf16[32,640]{1,0:T(8,128)(2,1)S(1)} collective-permute-done((bf16[32,640]{1,0:T(8,128)(2,1)S(1)}, bf16[32,640]{1,0:T(8,128)(2,1)S(1)}, u32[]{:S(2)}, u32[]{:S(2)}) %collective-permute-start.8) | collective-permute-done | bytes 40992 | tf_op jit(solution)/shard_map/ppermute | solution.py:346
  15.3 1.7 %collective-permute-start.5 = (bf16[32,2304]{1,0:T(8,128)(2,1)S(1)}, bf16[32,2304]{1,0:T(8,128)(2,1)S(1)}, u32[]{:S(2)}, u32[]{:S(2)}) collective-permute-start(bf16[32,2304]{1,0:T(8,128)(2,1)S(1)} %collective-permute-done.1.refs_3_), channel_id=1, source_target_pairs={{0,4},{1,5},{4,8},{5,9},{8,12},{9,13},{12,14},{13,15},{14,10},{15,... | collective-permute-start | bytes 442376 | tf_op jit(solution)/shard_map/ppermute | solution.py:60
  17.0 1.3 %collective-permute-start.6 = (bf16[32,2304]{1,0:T(8,128)(2,1)S(1)}, bf16[32,2304]{1,0:T(8,128)(2,1)S(1)}, u32[]{:S(2)}, u32[]{:S(2)}) collective-permute-start(bf16[32,2304]{1,0:T(8,128)(2,1)S(1)} %collective-permute-done.2.refs_4_), channel_id=1, source_target_pairs={{0,2},{1,3},{4,0},{5,1},{8,4},{9,5},{12,8},{13,9},{14,12},{15,13},... | collective-permute-start | bytes 442376 | tf_op jit(solution)/shard_map/ppermute | solution.py:61
  18.3 2.0 %collective-permute-start.7 = (bf16[32,2304]{1,0:T(8,128)(2,1)S(1)}, bf16[32,2304]{1,0:T(8,128)(2,1)S(1)}, u32[]{:S(2)}, u32[]{:S(2)}) collective-permute-start(bf16[32,2304]{1,0:T(8,128)(2,1)S(1)} %collective-permute-done.3.refs_5_), channel_id=1, source_target_pairs={{0,2},{1,3},{4,0},{5,1},{8,4},{9,5},{12,8},{13,9},{14,12},{15,13},... | collective-permute-start | bytes 442376 | tf_op jit(solution)/shard_map/ppermute | solution.py:61
  20.3 4.1 %shard_map.64.refs_10_.refs_2_.refs_4_ = bf16[2304,2304]{1,0:T(8,128)(2,1)S(1)} custom-call(bf16[4608,2304]{1,0:T(8,128)(2,1)} %w_ref.3), custom_call_target="tpu_custom_call" | custom-call | bytes 10616832 | tf_op jit(solution)/shard_map/pallas_call | solution.py:202
  24.4 4.8 %shard_map.65 = (bf16[2304,2304]{1,0:T(8,128)(2,1)S(1)}, bf16[4,64,2304]{2,1,0:T(8,128)(2,1)S(1)}) custom-call(bf16[4608,2304]{1,0:T(8,128)(2,1)} %w_ref.3, f32[4,64,2304]{2,1,0:T(8,128)} %refs_0_.2), custom_call_target="tpu_custom_call" | custom-call | bytes 10616832 | tf_op jit(solution)/shard_map/pallas_call | solution.py:202
  29.6 1.9 %collective-permute-start.12 = (bf16[32,2304]{1,0:T(8,128)(2,1)S(1)}, bf16[32,2304]{1,0:T(8,128)(2,1)S(1)}, u32[]{:S(2)}, u32[]{:S(2)}) collective-permute-start(bf16[32,2304]{1,0:T(8,128)(2,1)S(1)} %collective-permute-done.5.refs_7_), channel_id=1, source_target_pairs={{0,4},{1,5},{4,8},{5,9},{8,12},{9,13},{12,14},{13,15},{14,10},{15,... | collective-permute-start | bytes 442376 | tf_op jit(solution)/shard_map/ppermute | solution.py:60
  31.7 2.0 %collective-permute-start.14 = (bf16[32,2304]{1,0:T(8,128)(2,1)S(1)}, bf16[32,2304]{1,0:T(8,128)(2,1)S(1)}, u32[]{:S(2)}, u32[]{:S(2)}) collective-permute-start(bf16[32,2304]{1,0:T(8,128)(2,1)S(1)} %collective-permute-done.7.refs_9_), channel_id=1, source_target_pairs={{0,2},{1,3},{4,0},{5,1},{8,4},{9,5},{12,8},{13,9},{14,12},{15,13},... | collective-permute-start | bytes 442376 | tf_op jit(solution)/shard_map/ppermute | solution.py:61
  33.6 2.6 %collective-permute-done.11.refs_0_ = bf16[32,2304]{1,0:T(8,128)(2,1)S(1)} collective-permute-done((bf16[32,2304]{1,0:T(8,128)(2,1)S(1)}, bf16[32,2304]{1,0:T(8,128)(2,1)S(1)}, u32[]{:S(2)}, u32[]{:S(2)}) %collective-permute-start.11) | collective-permute-done | bytes 147488 | tf_op jit(solution)/shard_map/ppermute | solution.py:60
  36.3 2.9 %collective-permute-done.12.refs_1_ = bf16[32,2304]{1,0:T(8,128)(2,1)S(1)} collective-permute-done((bf16[32,2304]{1,0:T(8,128)(2,1)S(1)}, bf16[32,2304]{1,0:T(8,128)(2,1)S(1)}, u32[]{:S(2)}, u32[]{:S(2)}) %collective-permute-start.12) | collective-permute-done | bytes 147488 | tf_op jit(solution)/shard_map/ppermute | solution.py:60
  39.1 1.4 %collective-permute-done.14.refs_3_ = bf16[32,2304]{1,0:T(8,128)(2,1)S(1)} collective-permute-done((bf16[32,2304]{1,0:T(8,128)(2,1)S(1)}, bf16[32,2304]{1,0:T(8,128)(2,1)S(1)}, u32[]{:S(2)}, u32[]{:S(2)}) %collective-permute-start.14) | collective-permute-done | bytes 147488 | tf_op jit(solution)/shard_map/ppermute | solution.py:61
  42.0 1.8 %collective-permute-start.16 = (bf16[32,2304]{1,0:T(8,128)(2,1)S(1)}, bf16[32,2304]{1,0:T(8,128)(2,1)S(1)}, u32[]{:S(2)}, u32[]{:S(2)}) collective-permute-start(bf16[32,2304]{1,0:T(8,128)(2,1)S(1)} %collective-permute-done.11.refs_0_), channel_id=1, source_target_pairs={{0,4},{1,5},{4,8},{5,9},{8,12},{9,13},{12,14},{13,15},{14,10},{15,... | collective-permute-start | bytes 442376 | tf_op jit(solution)/shard_map/ppermute | solution.py:64
  44.0 1.9 %collective-permute-done.18.refs_1_ = bf16[128,128]{1,0:T(8,128)(2,1)S(1)} collective-permute-done((bf16[128,128]{1,0:T(8,128)(2,1)S(1)}, bf16[128,128]{1,0:T(8,128)(2,1)S(1)}, u32[]{:S(2)}, u32[]{:S(2)}) %collective-permute-start.18) | collective-permute-done | bytes 32800 | tf_op jit(solution)/shard_map/ppermute | solution.py:365
  46.0 7.1 %shard_map.70.refs_2_.refs_0_ = f32[320,2304]{1,0:T(8,128)S(1)} custom-call(bf16[320,2304]{1,0:T(8,128)(2,1)S(1)} %shard_map.67.refs_1_.refs_0_, bf16[320,2304]{1,0:T(8,128)(2,1)S(1)} %collective-permute-done.10.refs_1_, bf16[2304,2304]{1,0:T(8,128)(2,1)S(1)} %shard_map.64.refs_10_.refs_2_.refs_4_, ...), custom_call_target="tpu_custom_call" | custom-call | flops 6794772480 | tf_op jit(solution)/shard_map/pallas_call | solution.py:96
  53.2 2.1 %collective-permute-start.20 = (bf16[128,128]{1,0:T(8,128)(2,1)S(1)}, bf16[128,128]{1,0:T(8,128)(2,1)S(1)}, u32[]{:S(2)}, u32[]{:S(2)}) collective-permute-start(bf16[128,128]{1,0:T(8,128)(2,1)S(1)} %get-tuple-element.20.refs_3_), channel_id=1, source_target_pairs={{0,12},{1,13},{2,14},{3,15},{4,0},{5,1},{6,2},{7,3},{8,4},{9,5},{1... | collective-permute-start | bytes 98312 | tf_op jit(solution)/shard_map/ppermute | solution.py:370
  56.1 1.5 %collective-permute-start.22 = (bf16[128,128]{1,0:T(8,128)(2,1)S(1)}, bf16[128,128]{1,0:T(8,128)(2,1)S(1)}, u32[]{:S(2)}, u32[]{:S(2)}) collective-permute-start(bf16[128,128]{1,0:T(8,128)(2,1)S(1)} %get-tuple-element.20.refs_3_), channel_id=1, source_target_pairs={{0,4},{1,5},{2,6},{3,7},{4,8},{5,9},{6,10},{7,11},{8,12},{9,13},{1... | collective-permute-start | bytes 98312 | tf_op jit(solution)/shard_map/ppermute | solution.py:370
  57.6 2.5 %collective-permute-done.21.refs_2_ = bf16[128,128]{1,0:T(8,128)(2,1)S(1)} collective-permute-done((bf16[128,128]{1,0:T(8,128)(2,1)S(1)}, bf16[128,128]{1,0:T(8,128)(2,1)S(1)}, u32[]{:S(2)}, u32[]{:S(2)}) %collective-permute-start.21) | collective-permute-done | bytes 32800 | tf_op jit(solution)/shard_map/ppermute | solution.py:370
  60.2 1.7 %collective-permute-done.22.refs_3_ = bf16[128,128]{1,0:T(8,128)(2,1)S(1)} collective-permute-done((bf16[128,128]{1,0:T(8,128)(2,1)S(1)}, bf16[128,128]{1,0:T(8,128)(2,1)S(1)}, u32[]{:S(2)}, u32[]{:S(2)}) %collective-permute-start.22) | collective-permute-done | bytes 32800 | tf_op jit(solution)/shard_map/ppermute | solution.py:370
  62.0 4.3 %shard_map.74.refs_1_ = f32[192,2304]{1,0:T(8,128)S(1)} custom-call(bf16[128,2304]{1,0:T(8,128)(2,1)S(1)} %shard_map.68.refs_2_.refs_0_, bf16[128,2304]{1,0:T(8,128)(2,1)S(1)} %collective-permute-done.15.refs_1_, bf16[64,2304]{1,0:T(8,128)(2,1)S(1)} %shard_map.72.refs_4_.refs_2_, bf16[64,2304]{1,0:T(8,128)(2,1)S(1)} %collective-permute-done.19.refs_3_, ...), custom_call_target="tpu_custom_call" | custom-call | flops 4076863488 | tf_op jit(solution)/shard_map/pallas_call | solution.py:96
  66.3 2.4 %shard_map.75 = bf16[512,2304]{1,0:T(8,128)(2,1)} custom-call(s32[4]{0:T(128)S(1)} %bitcast.4, s32[4]{0:T(128)S(1)} %copy-done.3, f32[320,2304]{1,0:T(8,128)S(1)} %shard_map.70.refs_2_.refs_0_, f32[192,2304]{1,0:T(8,128)S(1)} %shard_map.74.refs_1_, f32[128,128]{1,0:T(8,128)S(1)} %get-tuple-element.23.refs_2_, ...), custom_call_target="tpu_custom_call" | custom-call | flops 150994944 | bytes 2359296 | tf_op jit(solution)/shard_map/pallas_call | solution.py:310
  (45 shorter events, 5.7 us)
Async XLA Ops:
  1.0 14.3 %collective-permute-start = (bf16[32,2304]{1,0:T(8,128)(2,1)S(1)}, bf16[32,2304]{1,0:T(8,128)(2,1)S(1)}, u32[]{:S(2)}, u32[]{:S(2)}) collective-permute-start(bf16[32,2304]{1,0:T(8,128)(2,1)S(1)} %get-tuple-element.26.refs_0_), channel_id=1, source_target_pairs={{0,4},{1,5},{4,8},{5,9},{8,12},{9,13},{12,14},{13,15},{14,10},{15,... | collective-permute-start | bytes 442376 | tf_op jit(solution)/shard_map/ppermute | solution.py:60
  4.1 11.2 %collective-permute-start.1 = (bf16[32,2304]{1,0:T(8,128)(2,1)S(1)}, bf16[32,2304]{1,0:T(8,128)(2,1)S(1)}, u32[]{:S(2)}, u32[]{:S(2)}) collective-permute-start(bf16[32,2304]{1,0:T(8,128)(2,1)S(1)} %get-tuple-element.25.refs_1_), channel_id=1, source_target_pairs={{0,4},{1,5},{4,8},{5,9},{8,12},{9,13},{12,14},{13,15},{14,10},{15,... | collective-permute-start | bytes 442376 | tf_op jit(solution)/shard_map/ppermute | solution.py:60
  5.7 11.4 %collective-permute-start.2 = (bf16[32,2304]{1,0:T(8,128)(2,1)S(1)}, bf16[32,2304]{1,0:T(8,128)(2,1)S(1)}, u32[]{:S(2)}, u32[]{:S(2)}) collective-permute-start(bf16[32,2304]{1,0:T(8,128)(2,1)S(1)} %get-tuple-element.26.refs_0_), channel_id=1, source_target_pairs={{0,2},{1,3},{4,0},{5,1},{8,4},{9,5},{12,8},{13,9},{14,12},{15,13},... | collective-permute-start | bytes 442376 | tf_op jit(solution)/shard_map/ppermute | solution.py:61
  6.1 12.2 %collective-permute-start.3 = (bf16[32,2304]{1,0:T(8,128)(2,1)S(1)}, bf16[32,2304]{1,0:T(8,128)(2,1)S(1)}, u32[]{:S(2)}, u32[]{:S(2)}) collective-permute-start(bf16[32,2304]{1,0:T(8,128)(2,1)S(1)} %get-tuple-element.25.refs_1_), channel_id=1, source_target_pairs={{0,2},{1,3},{4,0},{5,1},{8,4},{9,5},{12,8},{13,9},{14,12},{15,13},... | collective-permute-start | bytes 442376 | tf_op jit(solution)/shard_map/ppermute | solution.py:61
  8.2 7.0 %collective-permute-start.8 = (bf16[32,640]{1,0:T(8,128)(2,1)S(1)}, bf16[32,640]{1,0:T(8,128)(2,1)S(1)}, u32[]{:S(2)}, u32[]{:S(2)}) collective-permute-start(bf16[32,640]{1,0:T(8,128)(2,1)S(1)} %get-tuple-element.16), channel_id=1, source_target_pairs={{0,14},{1,15},{4,10},{5,11},{8,6},{9,7},{12,2},{13,3},{14,0},{15,1... | collective-permute-start | bytes 122888 | tf_op jit(solution)/shard_map/ppermute | solution.py:346
  15.3 14.0 %collective-permute-start.9 = (bf16[2,64,640]{2,1,0:T(8,128)(2,1)S(1)}, bf16[2,64,640]{2,1,0:T(8,128)(2,1)S(1)}, u32[]{:S(2)}, u32[]{:S(2)}) collective-permute-start(bf16[2,64,640]{2,1,0:T(8,128)(2,1)S(1)} %get-tuple-element.17.refs_3_), channel_id=1, source_target_pairs={{0,1},{1,0},{2,3},{3,2},{4,5},{5,4},{6,7},{7,6},{8,9},{9,8},{10,11... | collective-permute-start | bytes 491528 | tf_op jit(solution)/shard_map/ppermute | solution.py:21
  15.3 14.0 %collective-permute-start.4 = (bf16[32,2304]{1,0:T(8,128)(2,1)S(1)}, bf16[32,2304]{1,0:T(8,128)(2,1)S(1)}, u32[]{:S(2)}, u32[]{:S(2)}) collective-permute-start(bf16[32,2304]{1,0:T(8,128)(2,1)S(1)} %collective-permute-done.refs_2_), channel_id=1, source_target_pairs={{0,4},{1,5},{4,8},{5,9},{8,12},{9,13},{12,14},{13,15},{14,10},{15,... | collective-permute-start | bytes 442376 | tf_op jit(solution)/shard_map/ppermute | solution.py:60
  15.3 14.0 %collective-permute-start.5 = (bf16[32,2304]{1,0:T(8,128)(2,1)S(1)}, bf16[32,2304]{1,0:T(8,128)(2,1)S(1)}, u32[]{:S(2)}, u32[]{:S(2)}) collective-permute-start(bf16[32,2304]{1,0:T(8,128)(2,1)S(1)} %collective-permute-done.1.refs_3_), channel_id=1, source_target_pairs={{0,4},{1,5},{4,8},{5,9},{8,12},{9,13},{12,14},{13,15},{14,10},{15,... | collective-permute-start | bytes 442376 | tf_op jit(solution)/shard_map/ppermute | solution.py:60
  17.0 12.2 %collective-permute-start.6 = (bf16[32,2304]{1,0:T(8,128)(2,1)S(1)}, bf16[32,2304]{1,0:T(8,128)(2,1)S(1)}, u32[]{:S(2)}, u32[]{:S(2)}) collective-permute-start(bf16[32,2304]{1,0:T(8,128)(2,1)S(1)} %collective-permute-done.2.refs_4_), channel_id=1, source_target_pairs={{0,2},{1,3},{4,0},{5,1},{8,4},{9,5},{12,8},{13,9},{14,12},{15,13},... | collective-permute-start | bytes 442376 | tf_op jit(solution)/shard_map/ppermute | solution.py:61
  18.3 11.0 %collective-permute-start.7 = (bf16[32,2304]{1,0:T(8,128)(2,1)S(1)}, bf16[32,2304]{1,0:T(8,128)(2,1)S(1)}, u32[]{:S(2)}, u32[]{:S(2)}) collective-permute-start(bf16[32,2304]{1,0:T(8,128)(2,1)S(1)} %collective-permute-done.3.refs_5_), channel_id=1, source_target_pairs={{0,2},{1,3},{4,0},{5,1},{8,4},{9,5},{12,8},{13,9},{14,12},{15,13},... | collective-permute-start | bytes 442376 | tf_op jit(solution)/shard_map/ppermute | solution.py:61
  29.4 16.5 %collective-permute-start.10 = (bf16[320,2304]{1,0:T(8,128)(2,1)S(1)}, bf16[320,2304]{1,0:T(8,128)(2,1)S(1)}, u32[]{:S(2)}, u32[]{:S(2)}) collective-permute-start(bf16[320,2304]{1,0:T(8,128)(2,1)S(1)} %shard_map.67.refs_1_.refs_0_), channel_id=1, source_target_pairs={{0,1},{1,0},{2,3},{3,2},{4,5},{5,4},{6,7},{7,6},{8,9},{9,8},{10,11... | collective-permute-start | bytes 4423688 | tf_op jit(solution)/shard_map/ppermute | solution.py:21
  29.5 6.8 %collective-permute-start.11 = (bf16[32,2304]{1,0:T(8,128)(2,1)S(1)}, bf16[32,2304]{1,0:T(8,128)(2,1)S(1)}, u32[]{:S(2)}, u32[]{:S(2)}) collective-permute-start(bf16[32,2304]{1,0:T(8,128)(2,1)S(1)} %collective-permute-done.4.refs_6_), channel_id=1, source_target_pairs={{0,4},{1,5},{4,8},{5,9},{8,12},{9,13},{12,14},{13,15},{14,10},{15,... | collective-permute-start | bytes 442376 | tf_op jit(solution)/shard_map/ppermute | solution.py:60
  29.6 9.5 %collective-permute-start.12 = (bf16[32,2304]{1,0:T(8,128)(2,1)S(1)}, bf16[32,2304]{1,0:T(8,128)(2,1)S(1)}, u32[]{:S(2)}, u32[]{:S(2)}) collective-permute-start(bf16[32,2304]{1,0:T(8,128)(2,1)S(1)} %collective-permute-done.5.refs_7_), channel_id=1, source_target_pairs={{0,4},{1,5},{4,8},{5,9},{8,12},{9,13},{12,14},{13,15},{14,10},{15,... | collective-permute-start | bytes 442376 | tf_op jit(solution)/shard_map/ppermute | solution.py:60
  31.5 7.6 %collective-permute-start.13 = (bf16[32,2304]{1,0:T(8,128)(2,1)S(1)}, bf16[32,2304]{1,0:T(8,128)(2,1)S(1)}, u32[]{:S(2)}, u32[]{:S(2)}) collective-permute-start(bf16[32,2304]{1,0:T(8,128)(2,1)S(1)} %collective-permute-done.6.refs_8_), channel_id=1, source_target_pairs={{0,2},{1,3},{4,0},{5,1},{8,4},{9,5},{12,8},{13,9},{14,12},{15,13},... | collective-permute-start | bytes 442376 | tf_op jit(solution)/shard_map/ppermute | solution.py:61
  31.7 8.9 %collective-permute-start.14 = (bf16[32,2304]{1,0:T(8,128)(2,1)S(1)}, bf16[32,2304]{1,0:T(8,128)(2,1)S(1)}, u32[]{:S(2)}, u32[]{:S(2)}) collective-permute-start(bf16[32,2304]{1,0:T(8,128)(2,1)S(1)} %collective-permute-done.7.refs_9_), channel_id=1, source_target_pairs={{0,2},{1,3},{4,0},{5,1},{8,4},{9,5},{12,8},{13,9},{14,12},{15,13},... | collective-permute-start | bytes 442376 | tf_op jit(solution)/shard_map/ppermute | solution.py:61
  41.6 4.3 %collective-permute-start.18 = (bf16[128,128]{1,0:T(8,128)(2,1)S(1)}, bf16[128,128]{1,0:T(8,128)(2,1)S(1)}, u32[]{:S(2)}, u32[]{:S(2)}) collective-permute-start(bf16[128,128]{1,0:T(8,128)(2,1)S(1)} %get-tuple-element.18.refs_4_), channel_id=1, source_target_pairs={{0,2},{1,3},{2,0},{3,1},{4,6},{5,7},{6,4},{7,5},{8,10},{9,11},{10,... | collective-permute-start | bytes 98312 | tf_op jit(solution)/shard_map/ppermute | solution.py:365
  42.0 19.9 %collective-permute-start.15 = (bf16[128,2304]{1,0:T(8,128)(2,1)S(1)}, bf16[128,2304]{1,0:T(8,128)(2,1)S(1)}, u32[]{:S(2)}, u32[]{:S(2)}) collective-permute-start(bf16[128,2304]{1,0:T(8,128)(2,1)S(1)} %shard_map.68.refs_2_.refs_0_), channel_id=1, source_target_pairs={{0,1},{1,0},{2,3},{3,2},{4,5},{5,4},{6,7},{7,6},{8,9},{9,8},{10,11... | collective-permute-start | bytes 1769480 | tf_op jit(solution)/shard_map/ppermute | solution.py:21
  42.0 11.1 %collective-permute-start.16 = (bf16[32,2304]{1,0:T(8,128)(2,1)S(1)}, bf16[32,2304]{1,0:T(8,128)(2,1)S(1)}, u32[]{:S(2)}, u32[]{:S(2)}) collective-permute-start(bf16[32,2304]{1,0:T(8,128)(2,1)S(1)} %collective-permute-done.11.refs_0_), channel_id=1, source_target_pairs={{0,4},{1,5},{4,8},{5,9},{8,12},{9,13},{12,14},{13,15},{14,10},{15,... | collective-permute-start | bytes 442376 | tf_op jit(solution)/shard_map/ppermute | solution.py:64
  43.8 9.3 %collective-permute-start.17 = (bf16[32,2304]{1,0:T(8,128)(2,1)S(1)}, bf16[32,2304]{1,0:T(8,128)(2,1)S(1)}, u32[]{:S(2)}, u32[]{:S(2)}) collective-permute-start(bf16[32,2304]{1,0:T(8,128)(2,1)S(1)} %collective-permute-done.14.refs_3_), channel_id=1, source_target_pairs={{0,2},{1,3},{4,0},{5,1},{8,4},{9,5},{12,8},{13,9},{14,12},{15,13},... | collective-permute-start | bytes 442376 | tf_op jit(solution)/shard_map/ppermute | solution.py:64
  53.1 8.8 %collective-permute-start.19 = (bf16[64,2304]{1,0:T(8,128)(2,1)S(1)}, bf16[64,2304]{1,0:T(8,128)(2,1)S(1)}, u32[]{:S(2)}, u32[]{:S(2)}) collective-permute-start(bf16[64,2304]{1,0:T(8,128)(2,1)S(1)} %shard_map.72.refs_4_.refs_2_), channel_id=1, source_target_pairs={{0,1},{1,0},{2,3},{3,2},{4,5},{5,4},{6,7},{7,6},{8,9},{9,8},{10,11... | collective-permute-start | bytes 884744 | tf_op jit(solution)/shard_map/ppermute | solution.py:21
  53.2 4.4 %collective-permute-start.20 = (bf16[128,128]{1,0:T(8,128)(2,1)S(1)}, bf16[128,128]{1,0:T(8,128)(2,1)S(1)}, u32[]{:S(2)}, u32[]{:S(2)}) collective-permute-start(bf16[128,128]{1,0:T(8,128)(2,1)S(1)} %get-tuple-element.20.refs_3_), channel_id=1, source_target_pairs={{0,12},{1,13},{2,14},{3,15},{4,0},{5,1},{6,2},{7,3},{8,4},{9,5},{1... | collective-permute-start | bytes 98312 | tf_op jit(solution)/shard_map/ppermute | solution.py:370
  55.4 4.8 %collective-permute-start.21 = (bf16[128,128]{1,0:T(8,128)(2,1)S(1)}, bf16[128,128]{1,0:T(8,128)(2,1)S(1)}, u32[]{:S(2)}, u32[]{:S(2)}) collective-permute-start(bf16[128,128]{1,0:T(8,128)(2,1)S(1)} %get-tuple-element.20.refs_3_), channel_id=1, source_target_pairs={{0,8},{1,9},{2,10},{3,11},{4,12},{5,13},{6,14},{7,15},{8,0},{9,1},... | collective-permute-start | bytes 98312 | tf_op jit(solution)/shard_map/ppermute | solution.py:370
  56.1 5.7 %collective-permute-start.22 = (bf16[128,128]{1,0:T(8,128)(2,1)S(1)}, bf16[128,128]{1,0:T(8,128)(2,1)S(1)}, u32[]{:S(2)}, u32[]{:S(2)}) collective-permute-start(bf16[128,128]{1,0:T(8,128)(2,1)S(1)} %get-tuple-element.20.refs_3_), channel_id=1, source_target_pairs={{0,4},{1,5},{2,6},{3,7},{4,8},{5,9},{6,10},{7,11},{8,12},{9,13},{1... | collective-permute-start | bytes 98312 | tf_op jit(solution)/shard_map/ppermute | solution.py:370
  61.9 4.4 %collective-permute-start.23 = (bf16[128,128]{1,0:T(8,128)(2,1)S(1)}, bf16[128,128]{1,0:T(8,128)(2,1)S(1)}, u32[]{:S(2)}, u32[]{:S(2)}) collective-permute-start(bf16[128,128]{1,0:T(8,128)(2,1)S(1)} %get-tuple-element.22.refs_6_), channel_id=1, source_target_pairs={{0,1},{1,0},{2,3},{3,2},{4,5},{5,4},{6,7},{7,6},{8,9},{9,8},{10,11... | collective-permute-start | bytes 98312 | tf_op jit(solution)/shard_map/ppermute | solution.py:21
  (4 other events, 17.7 us)

commit v6 on v5

--- a/solution.py
+++ b/solution.py
@@ -12,9 +12,10 @@
 CHUNKS = 2
 
 
-def ring_perm(n, way):
+def ring_perm(n, way, other_way=None):
     order = [2 * z for z in range(n // 2)] + [2 * z + 1 for z in reversed(range(n // 2))]
-    return [(2 * s + c, 2 * order[(pos + way) % n] + c) for pos, s in enumerate(order) for c in range(2)]
+    ways = (way, way if other_way is None else other_way)
+    return [(2 * s + c, 2 * order[(pos + ways[c]) % n] + c) for pos, s in enumerate(order) for c in range(2)]
 
 
 def swap_cores(x, n):
@@ -50,33 +51,31 @@
     return [-hop, hop] if hop < n // 2 else [hop]
 
 
-class Ring:
-    def __init__(self, chunks, n):
-        self.n, self.up, self.down = n, list(chunks), list(chunks)
-
-    def hop(self, hop):
-        n = self.n
-        if hop < n // 2:
-            self.up = [lax.ppermute(x, AXES, ring_perm(n, 1)) for x in self.up]
-            self.down = [lax.ppermute(x, AXES, ring_perm(n, -1)) for x in self.down]
-            return self.up + self.down
-        return [
-            lax.ppermute((self.down if k % 2 else self.up)[k], AXES, ring_perm(n, -1 if k % 2 else 1))
-            for k in range(CHUNKS)
-        ]
-
-
-def join_kernel(*refs):
-    *pieces, out = refs
-    rows = pieces[0].shape[0]
-    for i, piece in enumerate(pieces):
-        out[i * rows : (i + 1) * rows, :] = piece[...]
-
-
-def join(pieces, after):
-    rows, depth = pieces[0].shape
-    (joined,) = call(join_kernel, [], pieces, after, [((rows * len(pieces), depth), pieces[0].dtype)])
-    return joined
+def ring_hop(up, down, n):
+    return [lax.ppermute(x, AXES, ring_perm(n, 1)) for x in up], [lax.ppermute(x, AXES, ring_perm(n, -1)) for x in down]
+
+
+def join_kernel(turned, *refs):
+    *pieces, out = refs[:-1] if turned else refs
+    first = 0
+    for piece in pieces:
+        out[first : first + piece.shape[0], :] = piece[...]
+        first += piece.shape[0]
+    if turned:
+        c = lax.axis_index("adapter")
+        rows = pieces[-1].shape[0]
+        for core, begin in enumerate((len(pieces) - 2 * CHUNKS, len(pieces) - CHUNKS)):
+
+            @pl.when(c == core)
+            def _():
+                for i, piece in enumerate(pieces[begin : begin + CHUNKS]):
+                    refs[-1][i * rows : (i + 1) * rows, :] = piece[...]
+
+
+def join(pieces, after, turned=False):
+    (rows, depth), dtype = pieces[-1].shape, pieces[-1].dtype
+    outs = [((sum(x.shape[0] for x in pieces), depth), dtype)] + [((CHUNKS * rows, depth), dtype)] * turned
+    return call(functools.partial(join_kernel, turned), [], pieces, after, outs)
 
 
 def whole(count):
@@ -132,6 +131,22 @@
         send[...] = tokens[:, pl.ds(start, window.size)]
 
 
+def near_kernel(tokens, behind, ahead, factor, out, *chunks):
+    held, rank, size = factor.shape
+    rows, depth = chunks[0].shape
+    for i, ref in enumerate((tokens, behind, ahead)):
+        for k in range(CHUNKS):
+            piece = ref[:, k * depth : (k + 1) * depth]
+            at = (i * CHUNKS + k) * rows
+            out[at : at + rows, :] = piece
+            if i:
+                chunks[(i - 1) * CHUNKS + k][...] = piece
+    first = 3 * CHUNKS * rows
+    out[first:, :] = jnp.zeros((rank, depth), out.dtype)
+    for index in range(held):
+        out[first:, index * size : (index + 1) * size] = factor[index]
+
+
 def pack(parts, out):
     chips, rows, rank = parts.shape
     for t in range(chips):
@@ -139,10 +154,12 @@
         out[i * rows : (i + 1) * rows, k * rank : (k + 1) * rank] = parts[t].astype(out.dtype)
 
 
-def partial_kernel(n, window, groups, opposite, adapters, *refs):
-    *pieces, factor, other, received, total, rounded, parts = refs
+def partial_kernel(n, window, groups, far, adapters, *refs):
+    *pieces, factor, other, total, rounded, parts = refs
+    pieces, received = pieces[: len(groups)], pieces[len(groups) :]
     s, c = lax.axis_index("seq"), lax.axis_index("adapter")
-    rows, held = received.shape[0], factor.shape[0]
+    rows, size = received[0].shape
+    held, rank, _ = factor.shape
     start = window.start(s)
     chunk = jnp.where(start >= window.depth, 1, 0)
     inside = pl.multiple_of(start - chunk * window.depth, 128)
@@ -150,13 +167,16 @@
     for piece, distances in zip(pieces, groups):
         for i, distance in enumerate(distances):
             row = pl.multiple_of((i * CHUNKS + chunk) * rows, rows)
-            found.append((distance, piece[pl.ds(row, rows), pl.ds(inside, window.size)]))
-    for distance, x in [*found, (opposite, received[...])]:
+            found.append((distance, piece[pl.ds(row, rows), pl.ds(inside, size)]))
+    found += [(distance, x[...]) for distance, x in zip(far, received)]
+    below = other.shape[0] - rank
+    for distance, x in found:
         chip = chip_at(distance, n)
         adapter = adapters[chip * 2 * rows // BLOCK]
         index = lax.rem(adapter, held)
         mine = (adapter >= c * held) & (adapter < (c + 1) * held)
-        weights = jnp.where(mine, factor[index], other[index])
+        theirs = other[below:, pl.ds(pl.multiple_of(index * size, 128), size)]
+        weights = jnp.where(mine, factor[index], theirs)
         parts[chip] = lax.dot_general(x, weights, (((1,), (1,)), ((), ())), preferred_element_type=jnp.float32)
     pack(parts, total)
     rounded[...] = total[...].astype(jnp.bfloat16)
@@ -210,16 +230,14 @@
     )(*(pltpu.with_memory_space_constraint(x, pltpu.HBM) for x in [weight, *ups]))
 
 
-def assemble(pairs, rows, held):
-    width = held.shape[1]
+def assemble(pairs, counts, rows, held):
     c = lax.axis_index("adapter")
     first = 0
-    for pair in pairs:
+    for pair, (begin, end) in zip(pairs, counts):
         depth = pair[0].shape[1]
-        chunks = width // depth
-        for chip in range(pair[0].shape[0] // (rows * chunks)):
-            for k in range(chunks):
-                at = (chip * chunks + k) * rows
+        for chip in range(begin, end):
+            for k in range(CHUNKS):
+                at = (chip * CHUNKS + k) * rows
                 for ref, core in zip(pair, (c, 1 - c)):
                     row = pl.multiple_of(first + core * rows, rows)
                     held[pl.ds(row, rows), k * depth : (k + 1) * depth] = ref[at : at + rows, :]
@@ -238,9 +256,10 @@
     )
 
 
-def base_kernel(rows, count, *refs):
+def base_kernel(rows, counts, *refs):
+    count = 2 * len(counts)
     pairs, weights, (base, held) = refs[:count], refs[count : count + CHUNKS], refs[count + CHUNKS :]
-    assemble(list(zip(pairs[::2], pairs[1::2])), rows, held)
+    assemble(list(zip(pairs[::2], pairs[1::2])), counts, rows, held)
     width = base.shape[1]
     columns = tile_width(width)
     for j in range(0, width, columns):
@@ -248,11 +267,12 @@
         base[:, at] = multiply(held, weights, at)
 
 
-def base_rows(pairs, chips, rows, weights, after):
+def base_rows(pairs, counts, rows, weights, after):
+    chips = sum(end - begin for begin, end in counts)
     total, depth, width = 2 * rows * chips, CHUNKS * weights[0].shape[0], weights[0].shape[1]
     arrays = [x for pair in pairs for x in pair]
     (base,) = call(
-        functools.partial(base_kernel, rows, len(arrays)),
+        functools.partial(base_kernel, rows, counts),
         [],
         arrays + weights,
         after,
@@ -331,52 +351,73 @@
     last = n // 2
     adapters = adapter_per_block[:, 0]
     window = Window(n, width, depth)
-    early = [d for hop in range(last - 1) for d in hop_distances(hop, n)]
-    late = hop_distances(last - 1, n)
-
-    chunks = [tokens[:, k * depth : (k + 1) * depth] for k in range(CHUNKS)]
-    ring = Ring(chunks, n)
-    factor, send = call(
-        functools.partial(prepare_kernel, n, window, [last]),
-        [],
-        [tokens, jnp.swapaxes(down, 1, 2)],
-        [],
-        [((held, rank, window.size), jnp.bfloat16), ((rows, window.size), jnp.bfloat16)],
-    )
-    received = lax.ppermute(send, AXES, ring_perm(n, last))
-    other_factor = swap_cores(factor, n)
-    weights, (last_weight, up) = [load(weight, k)[0] for k in range(CHUNKS - 1)], load(weight, CHUNKS - 1, up)
-    weights.append(last_weight)
-
-    pieces = chunks + [x for hop in range(1, last - 1) for x in ring.hop(hop)]
-    near = join(pieces, [*weights, received, other_factor])
-    far = join(ring.hop(last - 1), [])
+    near, mid, far = ([d for hop in hops for d in hop_distances(hop, n)] for hops in ((0, 1), range(2, last - 1), [last - 1]))
     half = (n // 2 * rows, 2 * rank)
     sums = [(half, jnp.float32), (half, jnp.bfloat16)]
+
+    (behind,), (ahead,) = ring_hop([tokens], [tokens], n)
+    ends = far + [last]
+    columns = ((rows, window.size), jnp.bfloat16)
+    factor, *sends = call(
+        functools.partial(prepare_kernel, n, window, ends),
+        [],
+        [tokens, jnp.swapaxes(down, 1, 2)],
+        [],
+        [((held, rank, window.size), jnp.bfloat16)] + [columns] * len(ends),
+    )
+    received = [lax.ppermute(x, AXES, ring_perm(n, d)) for d, x in zip(ends, sends)]
+    come_from = [-d for d in far] + [last]
+    weights = [load(weight, k)[0] for k in range(CHUNKS - 1)]
+    piece = ((rows, depth), jnp.bfloat16)
+    near_rows, *chunks = call(
+        near_kernel,
+        [],
+        [tokens, behind, ahead, factor],
+        [*weights, *received],
+        [((3 * CHUNKS * rows + rank, depth), jnp.bfloat16)] + [piece] * (2 * CHUNKS),
+    )
+
+    up_way, down_way = chunks[:CHUNKS], chunks[CHUNKS:]
+    near_pair = (near_rows, swap_cores(near_rows, n))
+    last_weight, up = load(weight, CHUNKS - 1, up)
+    weights.append(last_weight)
+    arrived = []
+    for _ in range(2, last - 1):
+        up_way, down_way = ring_hop(up_way, down_way, n)
+        arrived += up_way + down_way
+    (mid_rows,) = join(arrived, [last_weight])
+
     total, rounded = call(
-        functools.partial(partial_kernel, n, window, [early, late], last),
+        functools.partial(partial_kernel, n, window, [near, mid], come_from),
         [adapters],
-        [near, far, factor, other_factor, received],
+        [near_rows, mid_rows, *received, factor, near_pair[1]],
         [],
         sums,
         [pltpu.VMEM((n, rows, rank), jnp.float32)],
     )
-    bases = [base_rows([(near, swap_cores(near, n))], len(early), rows, weights, [rounded])]
     total, rounded = call(add_kernel, [], [total, lax.ppermute(rounded, AXES, y_perm(n))], [], sums)
-    final = join(ring.hop(last), [*bases, rounded])
+    bases = [base_rows([near_pair], [(0, len(near))], rows, weights, [mid_rows])]
+    up_way, down_way = ring_hop(up_way, down_way, n)
+    far_rows, turned = join([mid_rows, *up_way, *down_way], [*bases, rounded], True)
+
+    far_pair = (far_rows, swap_cores(far_rows, n))
     total, rounded = call(
         add_kernel,
         [],
         [total] + [lax.ppermute(rounded, AXES, z_perm(n, shift)) for shift in range(1, n // 2)],
-        [final],
+        [],
         sums,
     )
-    pairs = [(x, swap_cores(x, n)) for x in (far, final)]
-    bases.append(base_rows(pairs, len(late) + 1, rows, weights, [rounded]))
+    (last_rows,) = join([lax.ppermute(turned, AXES, ring_perm(n, 1, -1))], [rounded])
+
+    cut = len(mid)
+    bases.append(base_rows([far_pair], [(0, cut)], rows, weights, [last_rows]))
+    pairs = [far_pair, (last_rows, swap_cores(last_rows, n))]
+    bases.append(base_rows(pairs, [(cut, cut + len(far)), (0, 1)], rows, weights, [bases[-1]]))
     return finish(
         n,
         rows,
-        [early, late + [last]],
+        [near, mid, far + [last]],
         [adapters, rows_per_block],
         bases,
         total,

time: 69.1 us -> 57.4 us (0.83)
  waiting for transfers between devices: 15 us -> 2.33 us
  starting transfers between devices: 26.4 us -> 27.5 us
    ppermute x15 -> x14, waiting for transfers between devices: 8.92 us -> 0.07 us  [the longest x5 0.04 us: ring_hop(): lax.ppermute(x, AXES, ring_perm(n, 1))]
    ppermute x3, waiting for transfers between devices: 4.19 us -> 2.25 us  [on_device(): lax.ppermute(rounded, AXES, z_perm(n, shift))]
    ppermute x1, waiting for transfers between devices: 1.91 us -> 0.01 us  [on_device(): lax.ppermute(rounded, AXES, y_perm(n))]
    ppermute x3, starting transfers between devices: 4.43 us -> 5.72 us  [on_device(): lax.ppermute(rounded, AXES, z_perm(n, shift))]
    slice x1 -> x0, local copies, waits for them, and re-layouts: 1 us -> none  [on_device(): chunks = [tokens[:, k * depth:(k + 1) * depth] for k in range(CHUNKS)]]
    ppermute x15 -> x14, starting transfers between devices: 21.3 us -> 20.5 us  [the longest x5 9.78 us: ring_hop(): lax.ppermute(x, AXES, ring_perm(n, -1))]
    pallas_call x9 -> x11, Pallas kernels: 12.8 us -> 13.1 us  [call(): pl.pallas_call(body, out_shape=[pltpu.VMEM(shape, dtype) for shape, dtype...]
  transfers between devices with their start and end apart: 24 -> 22, of which waited for: 7 -> 3; matrix products, arithmetic and copies ran while one was open for 0% -> 0% of each run, Pallas kernels for 31% -> 38%
where the time goes in v6:
time: 57.4 us; the launch traced here: 57.3 us
  starting transfers between devices  27.5 us (48%)
  Pallas kernels  24.5 us (43%)
  local copies, waits for them, and re-layouts  2.59 us (5%)
  waiting for transfers between devices  2.33 us (4%)
    pallas_call x11, Pallas kernels, call(): pl.pallas_call(body, out_shape=[pltpu.VMEM(shape, dtype) for shape, dtype...  13.1 us
    ppermute x5, starting transfers between devices, ring_hop(): lax.ppermute(x, AXES, ring_perm(n, -1))  9.78 us
    pallas_call x2, Pallas kernels, load(): pl.pallas_call(functools.partial(load_kernel, chunk), out_shape=[pltpu.VM...  8.95 us
    ppermute x3, starting transfers between devices, on_device(): lax.ppermute(x, AXES, ring_perm(n, d))  8.87 us
    ppermute x3, starting transfers between devices, on_device(): lax.ppermute(rounded, AXES, z_perm(n, shift))  5.72 us
    unnamed x8, local copies, waits for them, and re-layouts  2.59 us
    pallas_call x1, Pallas kernels, finish(): pl.pallas_call(functools.partial(finish_kernel, n, rows, groups), out_sha...  2.41 us
    ppermute x3, waiting for transfers between devices, on_device(): lax.ppermute(rounded, AXES, z_perm(n, shift))  2.25 us
  transfers between devices with their start and end apart: 22, of which 3 were waited for; matrix products, arithmetic and copies ran while one was open for 0% of the time, Pallas kernels for 38%

profile of v6, /device:TPU:0, one launch (start us, length us, event | category | flops | bytes accessed | tf_op | source)
XLA Modules:
  0.0 57.3 jit_solution(2256785618826798895)
XLA Ops:
  0.0 3.0 %collective-permute-start.1 = (bf16[32,4608]{1,0:T(8,128)(2,1)}, bf16[32,4608]{1,0:T(8,128)(2,1)S(1)}, u32[]{:S(2)}, u32[]{:S(2)}) collective-permute-start(bf16[32,4608]{1,0:T(8,128)(2,1)} %refs_0_.4), channel_id=1, source_target_pairs={{0,2},{1,3},{4,0},{5,1},{8,4},{9,5},{12,8},{13,9},{14,12},{15,13},... | collective-permute-start | bytes 884744 | tf_op jit(solution)/shard_map/ppermute | solution.py:55
  3.0 1.0 %copy-done = bf16[32,4608]{1,0:T(8,128)(2,1)S(1)} copy-done((bf16[32,4608]{1,0:T(8,128)(2,1)S(1)}, bf16[32,4608]{1,0:T(8,128)(2,1)}, u32[]{:S(2)}) %copy-start) | copy-done | bytes 294936
  4.0 1.0 %copy-done.1 = f32[2,576,64]{1,2,0:T(8,128)S(1)} copy-done((f32[2,576,64]{1,2,0:T(8,128)S(1)}, f32[2,576,64]{1,2,0:T(8,128)}, u32[]{:S(2)}) %copy-start.1) | copy-done | bytes 294936
  5.2 4.0 %collective-permute-start.2 = (bf16[32,640]{1,0:T(8,128)(2,1)S(1)}, bf16[32,640]{1,0:T(8,128)(2,1)S(1)}, u32[]{:S(2)}, u32[]{:S(2)}) collective-permute-start(bf16[32,640]{1,0:T(8,128)(2,1)S(1)} %get-tuple-element.25), channel_id=1, source_target_pairs={{0,10},{1,11},{4,6},{5,7},{8,2},{9,3},{12,0},{13,1},{14,4},{15,5},... | collective-permute-start | bytes 122888 | tf_op jit(solution)/shard_map/ppermute | solution.py:368
  9.3 4.7 %collective-permute-start.4 = (bf16[32,640]{1,0:T(8,128)(2,1)S(1)}, bf16[32,640]{1,0:T(8,128)(2,1)S(1)}, u32[]{:S(2)}, u32[]{:S(2)}) collective-permute-start(bf16[32,640]{1,0:T(8,128)(2,1)S(1)} %get-tuple-element.27), channel_id=1, source_target_pairs={{0,14},{1,15},{4,10},{5,11},{8,6},{9,7},{12,2},{13,3},{14,0},{15,1... | collective-permute-start | bytes 122888 | tf_op jit(solution)/shard_map/ppermute | solution.py:368
  14.0 4.1 %shard_map.65.refs_4_.refs_2_ = bf16[2304,2304]{1,0:T(8,128)(2,1)S(1)} custom-call(bf16[4608,2304]{1,0:T(8,128)(2,1)} %w_ref.3), custom_call_target="tpu_custom_call" | custom-call | bytes 10616832 | tf_op jit(solution)/shard_map/pallas_call | solution.py:222
  19.0 1.9 %collective-permute-start.8 = (bf16[32,2304]{1,0:T(8,128)(2,1)S(1)}, bf16[32,2304]{1,0:T(8,128)(2,1)S(1)}, u32[]{:S(2)}, u32[]{:S(2)}) collective-permute-start(bf16[32,2304]{1,0:T(8,128)(2,1)S(1)} %get-tuple-element.32), channel_id=1, source_target_pairs={{0,2},{1,3},{4,0},{5,1},{8,4},{9,5},{12,8},{13,9},{14,12},{15,13},... | collective-permute-start | bytes 442376 | tf_op jit(solution)/shard_map/ppermute | solution.py:55
  20.9 1.6 %collective-permute-start.9 = (bf16[32,2304]{1,0:T(8,128)(2,1)S(1)}, bf16[32,2304]{1,0:T(8,128)(2,1)S(1)}, u32[]{:S(2)}, u32[]{:S(2)}) collective-permute-start(bf16[32,2304]{1,0:T(8,128)(2,1)S(1)} %get-tuple-element.33), channel_id=1, source_target_pairs={{0,2},{1,3},{4,0},{5,1},{8,4},{9,5},{12,8},{13,9},{14,12},{15,13},... | collective-permute-start | bytes 442376 | tf_op jit(solution)/shard_map/ppermute | solution.py:55
  22.6 4.8 %shard_map.67 = (bf16[2304,2304]{1,0:T(8,128)(2,1)S(1)}, bf16[4,64,2304]{2,1,0:T(8,128)(2,1)S(1)}) custom-call(bf16[4608,2304]{1,0:T(8,128)(2,1)} %w_ref.3, f32[4,64,2304]{2,1,0:T(8,128)} %refs_0_.5), custom_call_target="tpu_custom_call" | custom-call | bytes 10616832 | tf_op jit(solution)/shard_map/pallas_call | solution.py:222
  28.3 1.6 %collective-permute-start.12 = (bf16[32,2304]{1,0:T(8,128)(2,1)S(1)}, bf16[32,2304]{1,0:T(8,128)(2,1)S(1)}, u32[]{:S(2)}, u32[]{:S(2)}) collective-permute-start(bf16[32,2304]{1,0:T(8,128)(2,1)S(1)} %collective-permute-done.8.refs_2_), channel_id=1, source_target_pairs={{0,2},{1,3},{4,0},{5,1},{8,4},{9,5},{12,8},{13,9},{14,12},{15,13},... | collective-permute-start | bytes 442376 | tf_op jit(solution)/shard_map/ppermute | solution.py:55
  29.9 1.6 %collective-permute-start.13 = (bf16[32,2304]{1,0:T(8,128)(2,1)S(1)}, bf16[32,2304]{1,0:T(8,128)(2,1)S(1)}, u32[]{:S(2)}, u32[]{:S(2)}) collective-permute-start(bf16[32,2304]{1,0:T(8,128)(2,1)S(1)} %collective-permute-done.9.refs_3_), channel_id=1, source_target_pairs={{0,2},{1,3},{4,0},{5,1},{8,4},{9,5},{12,8},{13,9},{14,12},{15,13},... | collective-permute-start | bytes 442376 | tf_op jit(solution)/shard_map/ppermute | solution.py:55
  31.6 0.6 %copy-done.2 = s32[4,1]{0,1:T(1,128)S(1)} copy-done((s32[4,1]{0,1:T(1,128)S(1)}, s32[4,1]{0,1:T(1,128)}, u32[]{:S(2)}) %copy-start.2) | copy-done | bytes 40
  32.2 1.0 %shard_map.70 = (f32[128,128]{1,0:T(8,128)S(1)}, bf16[128,128]{1,0:T(8,128)(2,1)S(1)}) custom-call(s32[4]{0:T(128)S(1)} %bitcast.3, bf16[256,2304]{1,0:T(8,128)(2,1)S(1)} %get-tuple-element.28.refs_0_.refs_1_, bf16[128,2304]{1,0:T(8,128)(2,1)S(1)} %shard_map.68.refs_4_.refs_2_.refs_0_, bf16[32,640]{1,0:T(8,128)(2,1)S(1)} %collective-permute-done.2.refs_5_.refs_3_, ...), custom_call_target="tpu_custom_call" | custom-call | tf_op jit(solution)/shard_map/pallas_call | solution.py:95
  33.2 0.6 collective-permute-start.14
  33.8 4.3 %shard_map.69.refs_5_.refs_0_ = f32[192,2304]{1,0:T(8,128)S(1)} custom-call(bf16[256,2304]{1,0:T(8,128)(2,1)S(1)} %get-tuple-element.28.refs_0_.refs_1_, bf16[256,2304]{1,0:T(8,128)(2,1)S(1)} %collective-permute-done.5.refs_1_.refs_7_, bf16[2304,2304]{1,0:T(8,128)(2,1)S(1)} %shard_map.65.refs_4_.refs_2_, ...), custom_call_target="tpu_custom_call" | custom-call | flops 4076863488 | tf_op jit(solution)/shard_map/pallas_call | solution.py:95
  38.7 1.7 %collective-permute-start.19 = (bf16[128,128]{1,0:T(8,128)(2,1)S(1)}, bf16[128,128]{1,0:T(8,128)(2,1)S(1)}, u32[]{:S(2)}, u32[]{:S(2)}) collective-permute-start(bf16[128,128]{1,0:T(8,128)(2,1)S(1)} %get-tuple-element.36.refs_6_), channel_id=1, source_target_pairs={{0,4},{1,5},{2,6},{3,7},{4,8},{5,9},{6,10},{7,11},{8,12},{9,13},{1... | collective-permute-start | bytes 98312 | tf_op jit(solution)/shard_map/ppermute | solution.py:407
  40.5 1.6 %collective-permute-start.18 = (bf16[128,128]{1,0:T(8,128)(2,1)S(1)}, bf16[128,128]{1,0:T(8,128)(2,1)S(1)}, u32[]{:S(2)}, u32[]{:S(2)}) collective-permute-start(bf16[128,128]{1,0:T(8,128)(2,1)S(1)} %get-tuple-element.36.refs_6_), channel_id=1, source_target_pairs={{0,8},{1,9},{2,10},{3,11},{4,12},{5,13},{6,14},{7,15},{8,0},{9,1},... | collective-permute-start | bytes 98312 | tf_op jit(solution)/shard_map/ppermute | solution.py:407
  42.0 2.4 %collective-permute-start.17 = (bf16[128,128]{1,0:T(8,128)(2,1)S(1)}, bf16[128,128]{1,0:T(8,128)(2,1)S(1)}, u32[]{:S(2)}, u32[]{:S(2)}) collective-permute-start(bf16[128,128]{1,0:T(8,128)(2,1)S(1)} %get-tuple-element.36.refs_6_), channel_id=1, source_target_pairs={{0,12},{1,13},{2,14},{3,15},{4,0},{5,1},{6,2},{7,3},{8,4},{9,5},{1... | collective-permute-start | bytes 98312 | tf_op jit(solution)/shard_map/ppermute | solution.py:407
  44.5 0.5 collective-permute-done.19.refs_3_
  45.0 0.6 collective-permute-done.18.refs_2_
  45.5 1.2 %collective-permute-done.17.refs_1_ = bf16[128,128]{1,0:T(8,128)(2,1)S(1)} collective-permute-done((bf16[128,128]{1,0:T(8,128)(2,1)S(1)}, bf16[128,128]{1,0:T(8,128)(2,1)S(1)}, u32[]{:S(2)}, u32[]{:S(2)}) %collective-permute-start.17) | collective-permute-done | bytes 32800 | tf_op jit(solution)/shard_map/ppermute | solution.py:407
  47.4 3.0 %shard_map.75.refs_6_.refs_1_ = f32[128,2304]{1,0:T(8,128)S(1)} custom-call(bf16[256,2304]{1,0:T(8,128)(2,1)S(1)} %get-tuple-element.37.refs_0_, bf16[256,2304]{1,0:T(8,128)(2,1)S(1)} %collective-permute-done.15.refs_1_, bf16[2304,2304]{1,0:T(8,128)(2,1)S(1)} %shard_map.65.refs_4_.refs_2_, bf16[2304,2304]{1,0:T(8,128)(2,1)S(1)} %get-tuple-element.29.refs_4_.refs_3_.refs_5_, ...), custom_call_target="tpu_custom_call" | custom-call | flops 2717908992 | tf_op jit(solution)/shard_map/pallas_call | solution.py:95
  50.4 4.3 %shard_map.76.refs_2_ = f32[192,2304]{1,0:T(8,128)S(1)} custom-call(bf16[256,2304]{1,0:T(8,128)(2,1)S(1)} %get-tuple-element.37.refs_0_, bf16[256,2304]{1,0:T(8,128)(2,1)S(1)} %collective-permute-done.15.refs_1_, bf16[64,2304]{1,0:T(8,128)(2,1)S(1)} %shard_map.74.refs_4_.refs_2_, bf16[64,2304]{1,0:T(8,128)(2,1)S(1)} %collective-permute-done.20.refs_3_, ...), custom_call_target="tpu_custom_call" | custom-call | flops 4076863488 | tf_op jit(solution)/shard_map/pallas_call | solution.py:95
  54.7 2.4 %shard_map.77 = bf16[512,2304]{1,0:T(8,128)(2,1)} custom-call(s32[4]{0:T(128)S(1)} %bitcast.4, s32[4]{0:T(128)S(1)} %copy-done.3, f32[192,2304]{1,0:T(8,128)S(1)} %shard_map.69.refs_5_.refs_0_, f32[128,2304]{1,0:T(8,128)S(1)} %shard_map.75.refs_6_.refs_1_, f32[192,2304]{1,0:T(8,128)S(1)} %shard_map.76.refs_2_, f32[128,128]{1,0:T(8,128)S(1)} %get-tuple-element.41.refs_3_, ...), custom_call_target="tpu_custom_call" | custom-call | flops 150994944 | bytes 2359296 | tf_op jit(solution)/shard_map/pallas_call | solution.py:330
  (42 shorter events, 3.2 us)
Async XLA Ops:
  0.0 18.2 %collective-permute-start.1 = (bf16[32,4608]{1,0:T(8,128)(2,1)}, bf16[32,4608]{1,0:T(8,128)(2,1)S(1)}, u32[]{:S(2)}, u32[]{:S(2)}) collective-permute-start(bf16[32,4608]{1,0:T(8,128)(2,1)} %refs_0_.4), channel_id=1, source_target_pairs={{0,2},{1,3},{4,0},{5,1},{8,4},{9,5},{12,8},{13,9},{14,12},{15,13},... | collective-permute-start | bytes 884744 | tf_op jit(solution)/shard_map/ppermute | solution.py:55
  3.0 15.3 %collective-permute-start = (bf16[32,4608]{1,0:T(8,128)(2,1)}, bf16[32,4608]{1,0:T(8,128)(2,1)S(1)}, u32[]{:S(2)}, u32[]{:S(2)}) collective-permute-start(bf16[32,4608]{1,0:T(8,128)(2,1)} %refs_0_.4), channel_id=1, source_target_pairs={{0,4},{1,5},{4,8},{5,9},{8,12},{9,13},{12,14},{13,15},{14,10},{15,... | collective-permute-start | bytes 884744 | tf_op jit(solution)/shard_map/ppermute | solution.py:55
  3.0 1.0 %copy-start = (bf16[32,4608]{1,0:T(8,128)(2,1)S(1)}, bf16[32,4608]{1,0:T(8,128)(2,1)}, u32[]{:S(2)}) copy-start(bf16[32,4608]{1,0:T(8,128)(2,1)} %refs_0_.4) | copy-start | bytes 884740
  5.2 13.0 %collective-permute-start.2 = (bf16[32,640]{1,0:T(8,128)(2,1)S(1)}, bf16[32,640]{1,0:T(8,128)(2,1)S(1)}, u32[]{:S(2)}, u32[]{:S(2)}) collective-permute-start(bf16[32,640]{1,0:T(8,128)(2,1)S(1)} %get-tuple-element.25), channel_id=1, source_target_pairs={{0,10},{1,11},{4,6},{5,7},{8,2},{9,3},{12,0},{13,1},{14,4},{15,5},... | collective-permute-start | bytes 122888 | tf_op jit(solution)/shard_map/ppermute | solution.py:368
  9.2 9.0 %collective-permute-start.3 = (bf16[32,640]{1,0:T(8,128)(2,1)S(1)}, bf16[32,640]{1,0:T(8,128)(2,1)S(1)}, u32[]{:S(2)}, u32[]{:S(2)}) collective-permute-start(bf16[32,640]{1,0:T(8,128)(2,1)S(1)} %get-tuple-element.26), channel_id=1, source_target_pairs={{0,12},{1,13},{4,14},{5,15},{8,10},{9,11},{12,6},{13,7},{14,2},{15... | collective-permute-start | bytes 122888 | tf_op jit(solution)/shard_map/ppermute | solution.py:368
  9.3 8.9 %collective-permute-start.4 = (bf16[32,640]{1,0:T(8,128)(2,1)S(1)}, bf16[32,640]{1,0:T(8,128)(2,1)S(1)}, u32[]{:S(2)}, u32[]{:S(2)}) collective-permute-start(bf16[32,640]{1,0:T(8,128)(2,1)S(1)} %get-tuple-element.27), channel_id=1, source_target_pairs={{0,14},{1,15},{4,10},{5,11},{8,6},{9,7},{12,2},{13,3},{14,0},{15,1... | collective-permute-start | bytes 122888 | tf_op jit(solution)/shard_map/ppermute | solution.py:368
  18.4 13.2 %collective-permute-start.5 = (bf16[256,2304]{1,0:T(8,128)(2,1)S(1)}, bf16[256,2304]{1,0:T(8,128)(2,1)S(1)}, u32[]{:S(2)}, u32[]{:S(2)}) collective-permute-start(bf16[256,2304]{1,0:T(8,128)(2,1)S(1)} %get-tuple-element.28.refs_0_.refs_1_), channel_id=1, source_target_pairs={{0,1},{1,0},{2,3},{3,2},{4,5},{5,4},{6,7},{7,6},{8,9},{9,8},{10,11... | collective-permute-start | bytes 3538952 | tf_op jit(solution)/shard_map/ppermute | solution.py:22
  18.5 8.9 %collective-permute-start.6 = (bf16[32,2304]{1,0:T(8,128)(2,1)S(1)}, bf16[32,2304]{1,0:T(8,128)(2,1)S(1)}, u32[]{:S(2)}, u32[]{:S(2)}) collective-permute-start(bf16[32,2304]{1,0:T(8,128)(2,1)S(1)} %get-tuple-element.30), channel_id=1, source_target_pairs={{0,4},{1,5},{4,8},{5,9},{8,12},{9,13},{12,14},{13,15},{14,10},{15,... | collective-permute-start | bytes 442376 | tf_op jit(solution)/shard_map/ppermute | solution.py:55
  18.9 9.0 %collective-permute-start.7 = (bf16[32,2304]{1,0:T(8,128)(2,1)S(1)}, bf16[32,2304]{1,0:T(8,128)(2,1)S(1)}, u32[]{:S(2)}, u32[]{:S(2)}) collective-permute-start(bf16[32,2304]{1,0:T(8,128)(2,1)S(1)} %get-tuple-element.31), channel_id=1, source_target_pairs={{0,4},{1,5},{4,8},{5,9},{8,12},{9,13},{12,14},{13,15},{14,10},{15,... | collective-permute-start | bytes 442376 | tf_op jit(solution)/shard_map/ppermute | solution.py:55
  19.0 9.3 %collective-permute-start.8 = (bf16[32,2304]{1,0:T(8,128)(2,1)S(1)}, bf16[32,2304]{1,0:T(8,128)(2,1)S(1)}, u32[]{:S(2)}, u32[]{:S(2)}) collective-permute-start(bf16[32,2304]{1,0:T(8,128)(2,1)S(1)} %get-tuple-element.32), channel_id=1, source_target_pairs={{0,2},{1,3},{4,0},{5,1},{8,4},{9,5},{12,8},{13,9},{14,12},{15,13},... | collective-permute-start | bytes 442376 | tf_op jit(solution)/shard_map/ppermute | solution.py:55
  20.9 9.0 %collective-permute-start.9 = (bf16[32,2304]{1,0:T(8,128)(2,1)S(1)}, bf16[32,2304]{1,0:T(8,128)(2,1)S(1)}, u32[]{:S(2)}, u32[]{:S(2)}) collective-permute-start(bf16[32,2304]{1,0:T(8,128)(2,1)S(1)} %get-tuple-element.33), channel_id=1, source_target_pairs={{0,2},{1,3},{4,0},{5,1},{8,4},{9,5},{12,8},{13,9},{14,12},{15,13},... | collective-permute-start | bytes 442376 | tf_op jit(solution)/shard_map/ppermute | solution.py:55
  27.4 10.7 %collective-permute-start.10 = (bf16[32,2304]{1,0:T(8,128)(2,1)S(1)}, bf16[32,2304]{1,0:T(8,128)(2,1)S(1)}, u32[]{:S(2)}, u32[]{:S(2)}) collective-permute-start(bf16[32,2304]{1,0:T(8,128)(2,1)S(1)} %collective-permute-done.6.refs_0_), channel_id=1, source_target_pairs={{0,4},{1,5},{4,8},{5,9},{8,12},{9,13},{12,14},{13,15},{14,10},{15,... | collective-permute-start | bytes 442376 | tf_op jit(solution)/shard_map/ppermute | solution.py:55
  27.9 10.3 %collective-permute-start.11 = (bf16[32,2304]{1,0:T(8,128)(2,1)S(1)}, bf16[32,2304]{1,0:T(8,128)(2,1)S(1)}, u32[]{:S(2)}, u32[]{:S(2)}) collective-permute-start(bf16[32,2304]{1,0:T(8,128)(2,1)S(1)} %collective-permute-done.7.refs_1_), channel_id=1, source_target_pairs={{0,4},{1,5},{4,8},{5,9},{8,12},{9,13},{12,14},{13,15},{14,10},{15,... | collective-permute-start | bytes 442376 | tf_op jit(solution)/shard_map/ppermute | solution.py:55
  28.3 9.9 %collective-permute-start.12 = (bf16[32,2304]{1,0:T(8,128)(2,1)S(1)}, bf16[32,2304]{1,0:T(8,128)(2,1)S(1)}, u32[]{:S(2)}, u32[]{:S(2)}) collective-permute-start(bf16[32,2304]{1,0:T(8,128)(2,1)S(1)} %collective-permute-done.8.refs_2_), channel_id=1, source_target_pairs={{0,2},{1,3},{4,0},{5,1},{8,4},{9,5},{12,8},{13,9},{14,12},{15,13},... | collective-permute-start | bytes 442376 | tf_op jit(solution)/shard_map/ppermute | solution.py:55
  29.9 8.3 %collective-permute-start.13 = (bf16[32,2304]{1,0:T(8,128)(2,1)S(1)}, bf16[32,2304]{1,0:T(8,128)(2,1)S(1)}, u32[]{:S(2)}, u32[]{:S(2)}) collective-permute-start(bf16[32,2304]{1,0:T(8,128)(2,1)S(1)} %collective-permute-done.9.refs_3_), channel_id=1, source_target_pairs={{0,2},{1,3},{4,0},{5,1},{8,4},{9,5},{12,8},{13,9},{14,12},{15,13},... | collective-permute-start | bytes 442376 | tf_op jit(solution)/shard_map/ppermute | solution.py:55
  33.2 4.9 %collective-permute-start.14 = (bf16[128,128]{1,0:T(8,128)(2,1)S(1)}, bf16[128,128]{1,0:T(8,128)(2,1)S(1)}, u32[]{:S(2)}, u32[]{:S(2)}) collective-permute-start(bf16[128,128]{1,0:T(8,128)(2,1)S(1)} %get-tuple-element.35), channel_id=1, source_target_pairs={{0,2},{1,3},{2,0},{3,1},{4,6},{5,7},{6,4},{7,5},{8,10},{9,11},{10,... | collective-permute-start | bytes 98312 | tf_op jit(solution)/shard_map/ppermute | solution.py:398
  38.3 9.1 %collective-permute-start.15 = (bf16[256,2304]{1,0:T(8,128)(2,1)S(1)}, bf16[256,2304]{1,0:T(8,128)(2,1)S(1)}, u32[]{:S(2)}, u32[]{:S(2)}) collective-permute-start(bf16[256,2304]{1,0:T(8,128)(2,1)S(1)} %get-tuple-element.37.refs_0_), channel_id=1, source_target_pairs={{0,1},{1,0},{2,3},{3,2},{4,5},{5,4},{6,7},{7,6},{8,9},{9,8},{10,11... | collective-permute-start | bytes 3538952 | tf_op jit(solution)/shard_map/ppermute | solution.py:22
  38.4 8.4 %collective-permute-start.16 = (bf16[64,2304]{1,0:T(8,128)(2,1)S(1)}, bf16[64,2304]{1,0:T(8,128)(2,1)S(1)}, u32[]{:S(2)}, u32[]{:S(2)}) collective-permute-start(bf16[64,2304]{1,0:T(8,128)(2,1)S(1)} %get-tuple-element.38), channel_id=1, source_target_pairs={{0,4},{1,3},{4,8},{5,1},{8,12},{9,5},{12,14},{13,9},{14,10},{15,13... | collective-permute-start | bytes 884744 | tf_op jit(solution)/shard_map/ppermute | solution.py:411
  38.7 6.2 %collective-permute-start.19 = (bf16[128,128]{1,0:T(8,128)(2,1)S(1)}, bf16[128,128]{1,0:T(8,128)(2,1)S(1)}, u32[]{:S(2)}, u32[]{:S(2)}) collective-permute-start(bf16[128,128]{1,0:T(8,128)(2,1)S(1)} %get-tuple-element.36.refs_6_), channel_id=1, source_target_pairs={{0,4},{1,5},{2,6},{3,7},{4,8},{5,9},{6,10},{7,11},{8,12},{9,13},{1... | collective-permute-start | bytes 98312 | tf_op jit(solution)/shard_map/ppermute | solution.py:407
  40.5 5.1 %collective-permute-start.18 = (bf16[128,128]{1,0:T(8,128)(2,1)S(1)}, bf16[128,128]{1,0:T(8,128)(2,1)S(1)}, u32[]{:S(2)}, u32[]{:S(2)}) collective-permute-start(bf16[128,128]{1,0:T(8,128)(2,1)S(1)} %get-tuple-element.36.refs_6_), channel_id=1, source_target_pairs={{0,8},{1,9},{2,10},{3,11},{4,12},{5,13},{6,14},{7,15},{8,0},{9,1},... | collective-permute-start | bytes 98312 | tf_op jit(solution)/shard_map/ppermute | solution.py:407
  42.0 4.7 %collective-permute-start.17 = (bf16[128,128]{1,0:T(8,128)(2,1)S(1)}, bf16[128,128]{1,0:T(8,128)(2,1)S(1)}, u32[]{:S(2)}, u32[]{:S(2)}) collective-permute-start(bf16[128,128]{1,0:T(8,128)(2,1)S(1)} %get-tuple-element.36.refs_6_), channel_id=1, source_target_pairs={{0,12},{1,13},{2,14},{3,15},{4,0},{5,1},{6,2},{7,3},{8,4},{9,5},{1... | collective-permute-start | bytes 98312 | tf_op jit(solution)/shard_map/ppermute | solution.py:407
  46.8 3.6 %collective-permute-start.20 = (bf16[64,2304]{1,0:T(8,128)(2,1)S(1)}, bf16[64,2304]{1,0:T(8,128)(2,1)S(1)}, u32[]{:S(2)}, u32[]{:S(2)}) collective-permute-start(bf16[64,2304]{1,0:T(8,128)(2,1)S(1)} %shard_map.74.refs_4_.refs_2_), channel_id=1, source_target_pairs={{0,1},{1,0},{2,3},{3,2},{4,5},{5,4},{6,7},{7,6},{8,9},{9,8},{10,11... | collective-permute-start | bytes 884744 | tf_op jit(solution)/shard_map/ppermute | solution.py:22
  47.0 7.7 %collective-permute-start.21 = (bf16[128,128]{1,0:T(8,128)(2,1)S(1)}, bf16[128,128]{1,0:T(8,128)(2,1)S(1)}, u32[]{:S(2)}, u32[]{:S(2)}) collective-permute-start(bf16[128,128]{1,0:T(8,128)(2,1)S(1)} %get-tuple-element.40.refs_1_), channel_id=1, source_target_pairs={{0,1},{1,0},{2,3},{3,2},{4,5},{5,4},{6,7},{7,6},{8,9},{9,8},{10,11... | collective-permute-start | bytes 98312 | tf_op jit(solution)/shard_map/ppermute | solution.py:22
  50.3 4.3 %copy-start.3 = (s32[4]{0:T(128)S(1)}, s32[4]{0:T(128)}, u32[]{:S(2)}) copy-start(s32[4]{0:T(128)} %live.1) | copy-start | bytes 52
  (2 other events, 1.6 us)

commit v7 on v6

v7 whole, which is shorter than its diff:
```python
import functools

import jax
import jax.numpy as jnp
from jax import lax
from jax.experimental import pallas as pl
from jax.experimental.pallas import tpu as pltpu
from jax.sharding import PartitionSpec as P

BLOCK = 128
AXES = ("seq", "adapter")
CHUNKS = 2


def ring_perm(n, way, other_way=None):
    order = [2 * z for z in range(n // 2)] + [2 * z + 1 for z in reversed(range(n // 2))]
    ways = (way, way if other_way is None else other_way)
    return [(2 * s + c, 2 * order[(pos + ways[c]) % n] + c) for pos, s in enumerate(order) for c in range(2)]


def swap_cores(x, n):
    return lax.ppermute(x, AXES, [(2 * s + c, 2 * s + 1 - c) for s in range(n) for c in range(2)])


def chip_at(distance, n):
    s = lax.axis_index("seq")
    z = s >> 1
    pos = jnp.where(s & 1 == 0, z, n - 1 - z) + distance
    pos = jnp.where(pos >= n, pos - n, pos)
    pos = jnp.where(pos < 0, pos + n, pos)
    return jnp.where(pos < n // 2, 2 * pos, 2 * (n - 1 - pos) + 1)


def y_perm(n):
    return [(2 * s + c, 2 * (s ^ 1) + c) for s in range(n) for c in range(2)]


def z_perm(n, shift):
    nz = n // 2
    return [
        (2 * (2 * z + y) + c, 2 * (2 * ((z - shift) % nz) + y) + c)
        for z in range(nz)
        for y in range(2)
        for c in range(2)
    ]


def hop_distances(hop, n):
    if hop == 0:
        return [0]
    return [-hop, hop] if hop < n // 2 else [hop]


def ring_hop(up, down, n):
    return [lax.ppermute(x, AXES, ring_perm(n, 1)) for x in up], [lax.ppermute(x, AXES, ring_perm(n, -1)) for x in down]


def join_kernel(ways, *refs):
    count = len(refs) - 1 - (2 * CHUNKS if ways == 2 else ways)
    pieces, out, on = refs[:count], refs[count], refs[count + 1 :]
    first = 0
    for piece in pieces:
        out[first : first + piece.shape[0], :] = piece[...]
        first += piece.shape[0]
    arrived = pieces[len(pieces) - 2 * CHUNKS :]
    if ways == 2:
        for piece, ref in zip(arrived, on):
            ref[...] = piece[...]
    if ways == 1:
        c = lax.axis_index("adapter")
        rows = arrived[0].shape[0]
        for core in range(2):

            @pl.when(c == core)
            def _():
                for i, piece in enumerate(arrived[core * CHUNKS : (core + 1) * CHUNKS]):
                    on[0][i * rows : (i + 1) * rows, :] = piece[...]


def join(pieces, after, ways=0):
    (rows, depth), dtype = pieces[-1].shape, pieces[-1].dtype
    on = {0: [], 1: [CHUNKS * rows], 2: [rows] * 2 * CHUNKS}[ways]
    outs = [((count, depth), dtype) for count in [sum(x.shape[0] for x in pieces), *on]]
    return call(functools.partial(join_kernel, ways), pieces, after, outs)


def whole(count):
    return [pl.BlockSpec(memory_space=pltpu.VMEM)] * count


def in_vmem(arrays):
    return [pltpu.with_memory_space_constraint(x, pltpu.VMEM) for x in arrays]


def call(kernel, arrays, after, outs, scratch=(), limit=8, flops=0, outside=()):
    operands = len(arrays) + len(outside)

    def body(*refs):
        kernel(*refs[:operands], *refs[operands + len(after) :])

    return pl.pallas_call(
        body,
        out_shape=[pltpu.VMEM(shape, dtype) for shape, dtype in outs],
        in_specs=whole(len(arrays)) + [pl.BlockSpec(memory_space=pl.ANY)] * (len(outside) + len(after)),
        out_specs=whole(len(outs)),
        scratch_shapes=list(scratch),
        compiler_params=pltpu.CompilerParams(vmem_limit_bytes=limit << 20),
        cost_estimate=pl.CostEstimate(flops=flops, bytes_accessed=0, transcendentals=0),
    )(*in_vmem(arrays), *outside, *after)


class Window:
    def __init__(self, n, width, depth):
        self.width, self.depth = width, depth
        self.size = -(-(width + max(s * width % 128 for s in range(n))) // 128) * 128
        for s in range(n):
            start = s * width // 128 * 128
            assert start // depth == (start + self.size - 1) // depth

    def start(self, chip):
        return (chip * self.width) >> 7 << 7

    def shift(self, chip):
        return chip * self.width - self.start(chip)


def near_kernel(tokens, behind, ahead, factor, out, *chunks):
    held, rank, size = factor.shape
    rows, depth = chunks[0].shape
    for i, ref in enumerate((tokens, behind, ahead)):
        for k in range(CHUNKS):
            piece = ref[:, k * depth : (k + 1) * depth]
            at = (i * CHUNKS + k) * rows
            out[at : at + rows, :] = piece
            if i:
                chunks[(i - 1) * CHUNKS + k][...] = piece
    first = 3 * CHUNKS * rows
    out[first:, :] = jnp.zeros((rank, depth), out.dtype)
    for index in range(held):
        out[first:, index * size : (index + 1) * size] = factor[index]


def pack(parts, out):
    chips, rows, rank = parts.shape
    for t in range(chips):
        i, k = t % (chips // 2), t // (chips // 2)
        out[i * rows : (i + 1) * rows, k * rank : (k + 1) * rank] = parts[t].astype(out.dtype)


def partial_kernel(n, window, groups, far, *refs):
    *pieces, factor, other, adapters_ref, total, rounded, adapters, x, products, parts, sem = refs
    lookup = pltpu.make_async_copy(adapters_ref, adapters, sem)
    lookup.start()
    pieces, received = pieces[: len(groups)], pieces[len(groups) :]
    s, c = lax.axis_index("seq"), lax.axis_index("adapter")
    rows, size = received[0].shape
    held, rank, _ = factor.shape
    start = window.start(s)
    chunk = jnp.where(start >= window.depth, 1, 0)
    inside = pl.multiple_of(start - chunk * window.depth, 128)
    order = []
    for piece, distances in zip(pieces, groups):
        for i, distance in enumerate(distances):
            row = pl.multiple_of((i * CHUNKS + chunk) * rows, rows)
            x[len(order) * rows : (len(order) + 1) * rows, :] = piece[pl.ds(row, rows), pl.ds(inside, size)]
            order.append(distance)
    for piece, distance in zip(received, far):
        x[len(order) * rows : (len(order) + 1) * rows, :] = piece[...]
        order.append(distance)
    below = other.shape[0] - rank
    for index in range(held):
        theirs = other[below:, index * size : (index + 1) * size]
        for core, weights in ((c, factor[index]), (1 - c, theirs)):
            products[core * held + index] = lax.dot_general(
                x[...], weights, (((1,), (1,)), ((), ())), preferred_element_type=jnp.float32
            )
    lookup.wait()
    for i, distance in enumerate(order):
        chip = chip_at(distance, n)
        parts[chip] = products[adapters[chip * 2 * rows // BLOCK], i * rows : (i + 1) * rows, :]
    pack(parts, total)
    rounded[...] = total[...].astype(jnp.bfloat16)


def add_kernel(total, *refs):
    *received, out, rounded = refs
    value = total[...]
    for x in received:
        value += x[...].astype(jnp.float32)
    out[...] = value
    rounded[...] = value.astype(jnp.bfloat16)


def weight_copies(first, w_ref, w_out, sems):
    parts = sems.shape[0]
    depth = w_out.shape[0] // parts
    return [
        pltpu.make_async_copy(
            w_ref.at[pl.ds(first + k * depth, depth), :], w_out.at[pl.ds(k * depth, depth), :], sems.at[k]
        )
        for k in range(parts)
    ]


def first_load_kernel(n, window, distances, w_ref, tokens_ref, down_ref, w_out, factor, *refs):
    *sends, tokens, down, sems, small_sems = refs
    copies = weight_copies(0, w_ref, w_out, sems)
    small = [
        pltpu.make_async_copy(source, to, small_sems.at[k])
        for k, (source, to) in enumerate(((tokens_ref, tokens), (down_ref, down)))
    ]
    for copy in small + copies:
        copy.start()
    for copy in small:
        copy.wait()
    zeros = jnp.zeros((down.shape[1], window.size - window.width), jnp.float32)
    for index in range(down.shape[0]):
        wide = jnp.concatenate([down[index], zeros], 1)
        factor[index] = pltpu.roll(wide, window.shift(lax.axis_index("seq")), 1).astype(jnp.bfloat16)
    for distance, send in zip(distances, sends):
        start = pl.multiple_of(window.start(chip_at(distance, n)), 128)
        send[...] = tokens[:, pl.ds(start, window.size)]
    for copy in copies:
        copy.wait()


def second_load_kernel(first, w_ref, up_ref, w_out, up_out, held, sems, up_sem):
    copies = weight_copies(first, w_ref, w_out, sems)
    up_copy = pltpu.make_async_copy(up_ref, held, up_sem)
    up_copy.start()
    for copy in copies:
        copy.start()
    up_copy.wait()
    up_out[...] = held[...].astype(jnp.bfloat16)
    for copy in copies:
        copy.wait()


def load(kernel, arrays, after, outs, scratch):
    operands = len(arrays)

    def body(*refs):
        kernel(*refs[:operands], *refs[operands + len(after) :])

    return pl.pallas_call(
        body,
        out_shape=[pltpu.VMEM(shape, jnp.bfloat16) for shape in outs],
        in_specs=[pl.BlockSpec(memory_space=pltpu.HBM)] * operands
        + [pl.BlockSpec(memory_space=pl.ANY)] * len(after),
        out_specs=whole(len(outs)),
        scratch_shapes=scratch,
        compiler_params=pltpu.CompilerParams(vmem_limit_bytes=8 << 20),
        cost_estimate=pl.CostEstimate(
            flops=0, bytes_accessed=2 * outs[0][0] * outs[0][1], transcendentals=0
        ),
    )(*(pltpu.with_memory_space_constraint(x, pltpu.HBM) for x in arrays), *after)


def assemble(pairs, counts, rows, held):
    c = lax.axis_index("adapter")
    first = 0
    for pair, (begin, end) in zip(pairs, counts):
        depth = pair[0].shape[1]
        for chip in range(begin, end):
            for k in range(CHUNKS):
                at = (chip * CHUNKS + k) * rows
                for ref, core in zip(pair, (c, 1 - c)):
                    row = pl.multiple_of(first + core * rows, rows)
                    held[pl.ds(row, rows), k * depth : (k + 1) * depth] = ref[at : at + rows, :]
            first += 2 * rows


def tile_width(width):
    return 768 if width % 768 == 0 else width


def multiply(held, weights, at):
    total, first = 0.0, 0
    for w in weights:
        columns = held[:, first : first + w.shape[0]]
        total += jnp.dot(columns, w[:, at], preferred_element_type=jnp.float32)
        first += w.shape[0]
    return total


def base_kernel(rows, counts, *refs):
    count = 2 * len(counts)
    pairs, weights, (base, held) = refs[:count], refs[count:-2], refs[-2:]
    assemble(list(zip(pairs[::2], pairs[1::2])), counts, rows, held)
    width = base.shape[1]
    columns = tile_width(width)
    for j in range(0, width, columns):
        at = slice(j, j + columns)
        base[:, at] = multiply(held, weights, at)


def base_rows(pairs, counts, rows, weights, after):
    chips = sum(end - begin for begin, end in counts)
    total, depth, width = 2 * rows * chips, sum(w.shape[0] for w in weights), weights[0].shape[1]
    arrays = [x for pair in pairs for x in pair]
    (base,) = call(
        functools.partial(base_kernel, rows, counts),
        arrays + weights,
        after,
        [((total, width), jnp.float32)],
        [pltpu.VMEM((total, depth), jnp.bfloat16)],
        limit=8 + (2 * total * depth >> 20),
        flops=2 * total * depth * width,
    )
    return base


def finish_kernel(n, rows, groups, skipped, adapters, live, *refs):
    *bases, own, other, up_ref = refs[: len(groups) + 3]
    out_ref, *token, shrink, block, sems = refs[len(groups) + 3 + skipped :]
    for ref in token:
        ref[...] = jnp.zeros_like(ref)
    c = lax.axis_index("adapter")
    chip_rows, rank = 2 * rows, up_ref.shape[1]
    tiles, _, columns = block.shape
    for t in range(n):
        i, k = t % (n // 2), t // (n // 2)
        for ref, core in ((own, c), (other, 1 - c)):
            part = ref[i * rows : (i + 1) * rows, k * rank : (k + 1) * rank]
            shrink[t, pl.ds(pl.multiple_of(core * rows, rows), rows), :] = part.astype(jnp.bfloat16)
    places = [
        (distance, base, i * chip_rows)
        for base, distances in zip(bases, groups)
        for i, distance in enumerate(distances)
    ]
    copies = []
    for j in range(tiles):
        at = slice(j * columns, (j + 1) * columns)
        for i, (distance, base, row) in enumerate(places):
            chip = chip_at(distance, n)
            first = chip * chip_rows
            of_block = first // BLOCK
            delta = jnp.dot(shrink[chip], up_ref[adapters[of_block], :, at], preferred_element_type=jnp.float32)
            index = lax.broadcasted_iota(jnp.int32, delta.shape, 0) + (first - of_block * BLOCK)
            total = jnp.where(index < live[of_block], base[row : row + chip_rows, at] + delta, 0.0)
            place = pl.ds(i * chip_rows, chip_rows)
            block[j, place, :] = total.astype(out_ref.dtype)
            copies.append(
                pltpu.make_async_copy(
                    block.at[j, place, :],
                    out_ref.at[pl.ds(pl.multiple_of(first, chip_rows), chip_rows), pl.ds(j * columns, columns)],
                    sems.at[j, i],
                )
            )
            copies[-1].start()
    for copy in copies:
        copy.wait()


def finish(n, rows, groups, scalars, bases, own, other, up, into):
    rank, width = up.shape[1:]
    count = sum(len(group) for group in groups)
    total, columns = 2 * rows * count, tile_width(width)
    arrays = [*bases, own, other, up]
    token = [] if into else [pltpu.VMEM((8, 128), jnp.float32)]
    return pl.pallas_call(
        functools.partial(finish_kernel, n, rows, groups, len(into)),
        out_shape=[jax.ShapeDtypeStruct((2 * n * rows, width), jnp.bfloat16)] + token,
        in_specs=[pl.BlockSpec(memory_space=pltpu.SMEM)] * len(scalars)
        + whole(len(arrays))
        + [pl.BlockSpec(memory_space=pl.ANY)] * len(into),
        out_specs=[pl.BlockSpec(memory_space=pl.ANY)] + whole(len(token)),
        scratch_shapes=[
            pltpu.VMEM((n, 2 * rows, rank), jnp.bfloat16),
            pltpu.VMEM((width // columns, total, columns), jnp.bfloat16),
            pltpu.SemaphoreType.DMA((width // columns, count)),
        ],
        input_output_aliases={len(scalars) + len(arrays): 0} if into else {},
        compiler_params=pltpu.CompilerParams(vmem_limit_bytes=8 << 20),
        cost_estimate=pl.CostEstimate(
            flops=2 * total * rank * width, bytes_accessed=2 * total * width, transcendentals=0
        ),
    )(*scalars, *in_vmem(arrays), *into)


def on_device(n, tokens, weight, down, up, adapter_per_block, rows_per_block):
    rows, features = tokens.shape
    depth = features // CHUNKS
    held, width, rank = down.shape
    last = n // 2
    adapters = adapter_per_block[:, 0]
    window = Window(n, width, depth)
    near, mid, far = ([d for hop in hops for d in hop_distances(hop, n)] for hops in ((0, 1), range(2, last - 1), [last - 1]))
    half = (n // 2 * rows, 2 * rank)
    sums = [(half, jnp.float32), (half, jnp.bfloat16)]

    (behind,), (ahead,) = ring_hop([tokens], [tokens], n)
    ends = far + [last]
    cut = features * 3 // 5 // 256 * 256
    weights, factor, *sends = load(
        functools.partial(first_load_kernel, n, window, ends),
        [weight, tokens, jnp.swapaxes(down, 1, 2)],
        [],
        [(cut, weight.shape[1]), (held, rank, window.size)] + [(rows, window.size)] * len(ends),
        [
            pltpu.VMEM(tokens.shape, tokens.dtype),
            pltpu.VMEM((held, rank, width), down.dtype),
            pltpu.SemaphoreType.DMA((4,)),
            pltpu.SemaphoreType.DMA((2,)),
        ],
    )
    received = [lax.ppermute(x, AXES, ring_perm(n, d)) for d, x in zip(ends, sends)]
    come_from = [-d for d in far] + [last]
    piece = ((rows, depth), jnp.bfloat16)
    near_rows, *chunks = call(
        near_kernel,
        [tokens, behind, ahead, factor],
        received,
        [((3 * CHUNKS * rows + rank, depth), jnp.bfloat16)] + [piece] * (2 * CHUNKS),
    )

    up_way, down_way = chunks[:CHUNKS], chunks[CHUNKS:]
    near_pair = (near_rows, swap_cores(near_rows, n))
    other_weights, up = load(
        functools.partial(second_load_kernel, cut),
        [weight, up],
        [near_rows],
        [(features - cut, weight.shape[1]), up.shape],
        [pltpu.VMEM(up.shape, up.dtype), pltpu.SemaphoreType.DMA((4,)), pltpu.SemaphoreType.DMA],
    )
    weights = [weights, other_weights]
    arrived = []
    for _ in range(2, last - 1):
        up_way, down_way = ring_hop(up_way, down_way, n)
        arrived += up_way + down_way
    mid_rows, *chunks = join(arrived, [other_weights], 2)
    up_way, down_way = chunks[:CHUNKS], chunks[CHUNKS:]

    total, rounded = call(
        functools.partial(partial_kernel, n, window, [near, mid], come_from),
        [near_rows, mid_rows, *received, factor, near_pair[1]],
        [],
        sums,
        [
            pltpu.SMEM(adapters.shape, jnp.int32),
            pltpu.VMEM((n * rows, window.size), jnp.bfloat16),
            pltpu.VMEM((2 * held, n * rows, rank), jnp.float32),
            pltpu.VMEM((n, rows, rank), jnp.float32),
            pltpu.SemaphoreType.DMA,
        ],
        outside=[adapters],
    )
    total, rounded = call(add_kernel, [total, lax.ppermute(rounded, AXES, y_perm(n))], [], sums)
    up_way, down_way = ring_hop(up_way, down_way, n)
    far_rows, turned = join([mid_rows, *up_way, *down_way], [rounded], 1)

    far_pair = (far_rows, swap_cores(far_rows, n))
    bases = [base_rows([near_pair], [(0, len(near))], rows, weights, [far_rows])]
    total, rounded = call(
        add_kernel,
        [total] + [lax.ppermute(rounded, AXES, z_perm(n, shift)) for shift in range(1, n // 2)],
        [],
        sums,
    )
    (last_rows,) = join([lax.ppermute(turned, AXES, ring_perm(n, 1, -1))], [rounded, *bases])

    count = len(mid)
    bases.append(base_rows([far_pair], [(0, count)], rows, weights, [last_rows]))
    scalars = [adapters, rows_per_block]
    sums = [total, swap_cores(rounded, n)]
    out, token = finish(n, rows, [near, mid], scalars, bases, *sums, up, [])
    pairs = [far_pair, (last_rows, swap_cores(last_rows, n))]
    bases = [base_rows(pairs, [(count, count + len(far)), (0, 1)], rows, weights, [token])]
    return finish(n, rows, [far + [last]], scalars, bases, *sums, up, [out])[0]


def solution(mesh):
    placed = (
        P(("groups", "seq", "adapter"), None),
        P(None, ("seq", "adapter")),
        P(("groups", "adapter"), "seq", None),
        P("groups", None, ("seq", "adapter")),
        P("groups", None),
        P("groups"),
    )
    return jax.shard_map(
        functools.partial(on_device, mesh.shape["seq"]),
        mesh=mesh,
        in_specs=placed,
        out_specs=P("groups", ("seq", "adapter")),
        check_vma=False,
    )
```

time: 57.4 us -> 63.7 us (1.11)
  waiting for transfers between devices: 2.33 us -> 10.5 us
  local copies, waits for them, and re-layouts: 2.59 us -> 0.01 us
  Pallas kernels: 24.5 us -> 25.8 us
  starting transfers between devices: 27.5 us -> 26.8 us
    ppermute x5, starting transfers between devices: 1.42 us -> 6.96 us  [ring_hop(): lax.ppermute(x, AXES, ring_perm(n, 1))]
    ppermute x5, starting transfers between devices: 9.78 us -> 4.27 us  [ring_hop(): lax.ppermute(x, AXES, ring_perm(n, -1))]
    ppermute x1, waiting for transfers between devices: 0.01 us -> 3.97 us  [on_device(): lax.ppermute(rounded, AXES, y_perm(n))]
    unnamed x8 -> x6, local copies, waits for them, and re-layouts: 2.59 us -> 0.01 us
    ppermute x5, waiting for transfers between devices: 0.01 us -> 2.57 us  [ring_hop(): lax.ppermute(x, AXES, ring_perm(n, -1))]
    ppermute x3, waiting for transfers between devices: 0.01 us -> 2.41 us  [on_device(): lax.ppermute(x, AXES, ring_perm(n, d))]
    ppermute x3, waiting for transfers between devices: 2.25 us -> 0.01 us  [on_device(): lax.ppermute(rounded, AXES, z_perm(n, shift))]
    pallas_call x3 -> x4, Pallas kernels: 11.4 us -> 13 us  [the longest x2 9.17 us: load(): pl.pallas_call(body, out_shape=[pltpu.VMEM(shape, jnp.bfloat16) for shape...]
  transfers between devices with their start and end apart: 22 -> 22, of which waited for: 3 -> 7; matrix products, arithmetic and copies ran while one was open for 0% -> 0% of each run, Pallas kernels for 38% -> 31%
where the time goes in v7:
time: 63.7 us; the launch traced here: 63.5 us
  starting transfers between devices  26.8 us (42%)
  Pallas kernels  25.8 us (41%)
  waiting for transfers between devices  10.5 us (16%)
    pallas_call x10, Pallas kernels, call(): pl.pallas_call(body, out_shape=[pltpu.VMEM(shape, dtype) for shape, dtype...  12.8 us
    pallas_call x2, Pallas kernels, load(): pl.pallas_call(body, out_shape=[pltpu.VMEM(shape, jnp.bfloat16) for shape...  9.17 us
    ppermute x3, starting transfers between devices, on_device(): lax.ppermute(x, AXES, ring_perm(n, d))  8.88 us
    ppermute x5, starting transfers between devices, ring_hop(): lax.ppermute(x, AXES, ring_perm(n, 1))  6.96 us
    ppermute x3, starting transfers between devices, on_device(): lax.ppermute(rounded, AXES, z_perm(n, shift))  4.3 us
    ppermute x5, starting transfers between devices, ring_hop(): lax.ppermute(x, AXES, ring_perm(n, -1))  4.27 us
    ppermute x1, waiting for transfers between devices, on_device(): lax.ppermute(rounded, AXES, y_perm(n))  3.97 us
    pallas_call x2, Pallas kernels, finish(): pl.pallas_call(functools.partial(finish_kernel, n, rows, groups, len(into...  3.83 us
  transfers between devices with their start and end apart: 22, of which 7 were waited for; matrix products, arithmetic and copies ran while one was open for 0% of the time, Pallas kernels for 31%

profile of v7, /device:TPU:0, one launch (start us, length us, event | category | flops | bytes accessed | tf_op | source)
XLA Modules:
  0.0 63.5 jit_solution(14478964395109735592)
XLA Ops:
  0.0 3.0 %collective-permute-start = (bf16[32,4608]{1,0:T(8,128)(2,1)}, bf16[32,4608]{1,0:T(8,128)(2,1)S(1)}, u32[]{:S(2)}, u32[]{:S(2)}) collective-permute-start(bf16[32,4608]{1,0:T(8,128)(2,1)} %refs_0_.4), channel_id=1, source_target_pairs={{0,4},{1,5},{4,8},{5,9},{8,12},{9,13},{12,14},{13,15},{14,10},{15,... | collective-permute-start | bytes 884744 | tf_op jit(solution)/shard_map/ppermute | solution.py:55
  3.0 4.7 %shard_map.64 = (bf16[2560,2304]{1,0:T(8,128)(2,1)S(1)}, bf16[2,64,640]{2,1,0:T(8,128)(2,1)S(1)}, bf16[32,640]{1,0:T(8,128)(2,1)S(1)}, bf16[32,640]{1,0:T(8,128)(2,1)S(1)}, bf16[32,640]{1,0:T(8,128)(2,1)S(1)}) custom-call(bf16[4608,2304]{1,0:T(8,128)(2,1)} %refs_0_.5, bf16[32,4608]{1,0:T(8,128)(2,1)} %refs_0_.4, f32[2,64,576]{2,1,0:T(8,128)} %bitcast.5), custom_call_target="tpu_custom_call" | custom-call | bytes 11796480 | tf_op jit(solution)/shard_map/pallas_call | solution.py:245
  7.7 4.0 %collective-permute-start.2 = (bf16[32,640]{1,0:T(8,128)(2,1)S(1)}, bf16[32,640]{1,0:T(8,128)(2,1)S(1)}, u32[]{:S(2)}, u32[]{:S(2)}) collective-permute-start(bf16[32,640]{1,0:T(8,128)(2,1)S(1)} %get-tuple-element.33), channel_id=1, source_target_pairs={{0,10},{1,11},{4,6},{5,7},{8,2},{9,3},{12,0},{13,1},{14,4},{15,5},... | collective-permute-start | bytes 122888 | tf_op jit(solution)/shard_map/ppermute | solution.py:407
  11.9 4.7 %collective-permute-start.4 = (bf16[32,640]{1,0:T(8,128)(2,1)S(1)}, bf16[32,640]{1,0:T(8,128)(2,1)S(1)}, u32[]{:S(2)}, u32[]{:S(2)}) collective-permute-start(bf16[32,640]{1,0:T(8,128)(2,1)S(1)} %get-tuple-element.35), channel_id=1, source_target_pairs={{0,14},{1,15},{4,10},{5,11},{8,6},{9,7},{12,2},{13,3},{14,0},{15,1... | collective-permute-start | bytes 122888 | tf_op jit(solution)/shard_map/ppermute | solution.py:407
  16.6 1.0 %collective-permute-done.3.refs_5_.refs_3_ = bf16[32,640]{1,0:T(8,128)(2,1)S(1)} collective-permute-done((bf16[32,640]{1,0:T(8,128)(2,1)S(1)}, bf16[32,640]{1,0:T(8,128)(2,1)S(1)}, u32[]{:S(2)}, u32[]{:S(2)}) %collective-permute-start.3) | collective-permute-done | bytes 40992 | tf_op jit(solution)/shard_map/ppermute | solution.py:407
  17.6 1.5 %collective-permute-done.4.refs_6_.refs_4_ = bf16[32,640]{1,0:T(8,128)(2,1)S(1)} collective-permute-done((bf16[32,640]{1,0:T(8,128)(2,1)S(1)}, bf16[32,640]{1,0:T(8,128)(2,1)S(1)}, u32[]{:S(2)}, u32[]{:S(2)}) %collective-permute-start.4) | collective-permute-done | bytes 40992 | tf_op jit(solution)/shard_map/ppermute | solution.py:407
  19.4 2.0 %collective-permute-start.7 = (bf16[32,2304]{1,0:T(8,128)(2,1)S(1)}, bf16[32,2304]{1,0:T(8,128)(2,1)S(1)}, u32[]{:S(2)}, u32[]{:S(2)}) collective-permute-start(bf16[32,2304]{1,0:T(8,128)(2,1)S(1)} %get-tuple-element.38), channel_id=1, source_target_pairs={{0,2},{1,3},{4,0},{5,1},{8,4},{9,5},{12,8},{13,9},{14,12},{15,13},... | collective-permute-start | bytes 442376 | tf_op jit(solution)/shard_map/ppermute | solution.py:55
  21.4 1.9 %collective-permute-start.8 = (bf16[32,2304]{1,0:T(8,128)(2,1)S(1)}, bf16[32,2304]{1,0:T(8,128)(2,1)S(1)}, u32[]{:S(2)}, u32[]{:S(2)}) collective-permute-start(bf16[32,2304]{1,0:T(8,128)(2,1)S(1)} %get-tuple-element.39), channel_id=1, source_target_pairs={{0,2},{1,3},{4,0},{5,1},{8,4},{9,5},{12,8},{13,9},{14,12},{15,13},... | collective-permute-start | bytes 442376 | tf_op jit(solution)/shard_map/ppermute | solution.py:55
  23.4 4.5 %shard_map.66 = (bf16[2048,2304]{1,0:T(8,128)(2,1)S(1)}, bf16[4,64,2304]{2,1,0:T(8,128)(2,1)S(1)}) custom-call(bf16[4608,2304]{1,0:T(8,128)(2,1)} %refs_0_.5, f32[4,64,2304]{2,1,0:T(8,128)} %refs_1_.3, bf16[256,2304]{1,0:T(8,128)(2,1)S(1)} %get-tuple-element.40.refs_2_.refs_0_), custom_call_target="tpu_custom_call" | custom-call | bytes 9437184 | tf_op jit(solution)/shard_map/pallas_call | solution.py:245
  27.9 0.8 %collective-permute-done.6.refs_1_ = bf16[32,2304]{1,0:T(8,128)(2,1)S(1)} collective-permute-done((bf16[32,2304]{1,0:T(8,128)(2,1)S(1)}, bf16[32,2304]{1,0:T(8,128)(2,1)S(1)}, u32[]{:S(2)}, u32[]{:S(2)}) %collective-permute-start.6) | collective-permute-done | bytes 147488 | tf_op jit(solution)/shard_map/ppermute | solution.py:55
  28.7 2.1 %collective-permute-done.8.refs_3_ = bf16[32,2304]{1,0:T(8,128)(2,1)S(1)} collective-permute-done((bf16[32,2304]{1,0:T(8,128)(2,1)S(1)}, bf16[32,2304]{1,0:T(8,128)(2,1)S(1)}, u32[]{:S(2)}, u32[]{:S(2)}) %collective-permute-start.8) | collective-permute-done | bytes 147488 | tf_op jit(solution)/shard_map/ppermute | solution.py:55
  30.9 1.8 %collective-permute-start.10 = (bf16[32,2304]{1,0:T(8,128)(2,1)S(1)}, bf16[32,2304]{1,0:T(8,128)(2,1)S(1)}, u32[]{:S(2)}, u32[]{:S(2)}) collective-permute-start(bf16[32,2304]{1,0:T(8,128)(2,1)S(1)} %get-tuple-element.44), channel_id=1, source_target_pairs={{0,4},{1,5},{4,8},{5,9},{8,12},{9,13},{12,14},{13,15},{14,10},{15,... | collective-permute-start | bytes 442376 | tf_op jit(solution)/shard_map/ppermute | solution.py:55
  33.0 2.0 %collective-permute-start.9 = (bf16[32,2304]{1,0:T(8,128)(2,1)S(1)}, bf16[32,2304]{1,0:T(8,128)(2,1)S(1)}, u32[]{:S(2)}, u32[]{:S(2)}) collective-permute-start(bf16[32,2304]{1,0:T(8,128)(2,1)S(1)} %get-tuple-element.43), channel_id=1, source_target_pairs={{0,4},{1,5},{4,8},{5,9},{8,12},{9,13},{12,14},{13,15},{14,10},{15,... | collective-permute-start | bytes 442376 | tf_op jit(solution)/shard_map/ppermute | solution.py:55
  35.0 0.8 %shard_map.68 = (f32[128,128]{1,0:T(8,128)S(1)}, bf16[128,128]{1,0:T(8,128)(2,1)S(1)}) custom-call(bf16[256,2304]{1,0:T(8,128)(2,1)S(1)} %get-tuple-element.40.refs_2_.refs_0_, bf16[128,2304]{1,0:T(8,128)(2,1)S(1)} %get-tuple-element.42.refs_1_.refs_0_, bf16[32,640]{1,0:T(8,128)(2,1)S(1)} %collective-permute-done.2.refs_4_.refs_2_, ...), custom_call_target="tpu_custom_call" | custom-call | tf_op jit(solution)/shard_map/pallas_call | solution.py:101
  35.9 4.0 %collective-permute-done.14.refs_1_ = bf16[128,128]{1,0:T(8,128)(2,1)S(1)} collective-permute-done((bf16[128,128]{1,0:T(8,128)(2,1)S(1)}, bf16[128,128]{1,0:T(8,128)(2,1)S(1)}, u32[]{:S(2)}, u32[]{:S(2)}) %collective-permute-start.14) | collective-permute-done | bytes 32800 | tf_op jit(solution)/shard_map/ppermute | solution.py:448
  40.5 2.4 %collective-permute-start.17 = (bf16[128,128]{1,0:T(8,128)(2,1)S(1)}, bf16[128,128]{1,0:T(8,128)(2,1)S(1)}, u32[]{:S(2)}, u32[]{:S(2)}) collective-permute-start(bf16[128,128]{1,0:T(8,128)(2,1)S(1)} %get-tuple-element.49.refs_5_), channel_id=1, source_target_pairs={{0,12},{1,13},{2,14},{3,15},{4,0},{5,1},{6,2},{7,3},{8,4},{9,5},{1... | collective-permute-start | bytes 98312 | tf_op jit(solution)/shard_map/ppermute | solution.py:456
  43.6 1.3 %collective-permute-start.19 = (bf16[128,128]{1,0:T(8,128)(2,1)S(1)}, bf16[128,128]{1,0:T(8,128)(2,1)S(1)}, u32[]{:S(2)}, u32[]{:S(2)}) collective-permute-start(bf16[128,128]{1,0:T(8,128)(2,1)S(1)} %get-tuple-element.49.refs_5_), channel_id=1, source_target_pairs={{0,4},{1,5},{2,6},{3,7},{4,8},{5,9},{6,10},{7,11},{8,12},{9,13},{1... | collective-permute-start | bytes 98312 | tf_op jit(solution)/shard_map/ppermute | solution.py:456
  44.8 1.6 %collective-permute-start.16 = (bf16[64,2304]{1,0:T(8,128)(2,1)S(1)}, bf16[64,2304]{1,0:T(8,128)(2,1)S(1)}, u32[]{:S(2)}, u32[]{:S(2)}) collective-permute-start(bf16[64,2304]{1,0:T(8,128)(2,1)S(1)} %get-tuple-element.51), channel_id=1, source_target_pairs={{0,4},{1,3},{4,8},{5,1},{8,12},{9,5},{12,14},{13,9},{14,10},{15,13... | collective-permute-start | bytes 884744 | tf_op jit(solution)/shard_map/ppermute | solution.py:460
  46.5 4.3 %shard_map.72.refs_2_.refs_0_ = f32[192,2304]{1,0:T(8,128)S(1)} custom-call(bf16[256,2304]{1,0:T(8,128)(2,1)S(1)} %get-tuple-element.40.refs_2_.refs_0_, bf16[256,2304]{1,0:T(8,128)(2,1)S(1)} %collective-permute-done.13.refs_6_.refs_1_, bf16[2560,2304]{1,0:T(8,128)(2,1)S(1)} %get-tuple-element.54.refs_2_.refs_4_, ...), custom_call_target="tpu_custom_call" | custom-call | flops 4076863488 | tf_op jit(solution)/shard_map/pallas_call | solution.py:101
  50.8 0.7 %collective-permute-done.16.refs_0_ = bf16[64,2304]{1,0:T(8,128)(2,1)S(1)} collective-permute-done((bf16[64,2304]{1,0:T(8,128)(2,1)S(1)}, bf16[64,2304]{1,0:T(8,128)(2,1)S(1)}, u32[]{:S(2)}, u32[]{:S(2)}) %collective-permute-start.16) | collective-permute-done | bytes 294944 | tf_op jit(solution)/shard_map/ppermute | solution.py:460
  52.2 3.0 %shard_map.74.refs_1_ = f32[128,2304]{1,0:T(8,128)S(1)} custom-call(bf16[256,2304]{1,0:T(8,128)(2,1)S(1)} %get-tuple-element.50.refs_4_.refs_0_, bf16[256,2304]{1,0:T(8,128)(2,1)S(1)} %collective-permute-done.15.refs_1_, bf16[2560,2304]{1,0:T(8,128)(2,1)S(1)} %get-tuple-element.54.refs_2_.refs_4_, ...), custom_call_target="tpu_custom_call" | custom-call | flops 2717908992 | tf_op jit(solution)/shard_map/pallas_call | solution.py:101
  55.2 2.0 %shard_map.75 = (bf16[512,2304]{1,0:T(8,128)(2,1)}, f32[8,128]{1,0:T(8,128)S(1)}) custom-call(s32[4]{0:T(128)S(1)} %bitcast.3, s32[4]{0:T(128)S(1)} %copy-done.2, f32[192,2304]{1,0:T(8,128)S(1)} %shard_map.72.refs_2_.refs_0_, f32[128,2304]{1,0:T(8,128)S(1)} %shard_map.74.refs_1_, f32[128,128]{1,0:T(8,128)S(1)} %get-tuple-element.55.refs_2_.refs_1_, ...), custom_call_target="tpu_custom_call" | custom-call | flops 94371840 | bytes 1474560 | tf_op jit(solution)/shard_map/pallas_call | solution.py:361
  57.2 4.3 %shard_map.76.refs_0_ = f32[192,2304]{1,0:T(8,128)S(1)} custom-call(bf16[256,2304]{1,0:T(8,128)(2,1)S(1)} %get-tuple-element.50.refs_4_.refs_0_, bf16[256,2304]{1,0:T(8,128)(2,1)S(1)} %collective-permute-done.15.refs_1_, bf16[64,2304]{1,0:T(8,128)(2,1)S(1)} %shard_map.73.refs_4_.refs_2_, bf16[64,2304]{1,0:T(8,128)(2,1)S(1)} %collective-permute-done.20.refs_3_, ...), custom_call_target="tpu_custom_call" | custom-call | flops 4076863488 | tf_op jit(solution)/shard_map/pallas_call | solution.py:101
  61.6 1.8 %shard_map.77 = bf16[512,2304]{1,0:T(8,128)(2,1)} custom-call(s32[4]{0:T(128)S(1)} %bitcast.4, s32[4]{0:T(128)S(1)} %copy-done.2, f32[192,2304]{1,0:T(8,128)S(1)} %shard_map.76.refs_0_, f32[128,128]{1,0:T(8,128)S(1)} %get-tuple-element.55.refs_2_.refs_1_, ...), custom_call_target="tpu_custom_call", output_to_operand_aliasing={{}: (6, {})} | custom-call | flops 56623104 | bytes 884736 | tf_op jit(solution)/shard_map/pallas_call | solution.py:361
  (40 shorter events, 2.8 us)
Async XLA Ops:
  0.0 19.0 %collective-permute-start = (bf16[32,4608]{1,0:T(8,128)(2,1)}, bf16[32,4608]{1,0:T(8,128)(2,1)S(1)}, u32[]{:S(2)}, u32[]{:S(2)}) collective-permute-start(bf16[32,4608]{1,0:T(8,128)(2,1)} %refs_0_.4), channel_id=1, source_target_pairs={{0,4},{1,5},{4,8},{5,9},{8,12},{9,13},{12,14},{13,15},{14,10},{15,... | collective-permute-start | bytes 884744 | tf_op jit(solution)/shard_map/ppermute | solution.py:55
  3.0 16.0 %collective-permute-start.1 = (bf16[32,4608]{1,0:T(8,128)(2,1)}, bf16[32,4608]{1,0:T(8,128)(2,1)S(1)}, u32[]{:S(2)}, u32[]{:S(2)}) collective-permute-start(bf16[32,4608]{1,0:T(8,128)(2,1)} %refs_0_.4), channel_id=1, source_target_pairs={{0,2},{1,3},{4,0},{5,1},{8,4},{9,5},{12,8},{13,9},{14,12},{15,13},... | collective-permute-start | bytes 884744 | tf_op jit(solution)/shard_map/ppermute | solution.py:55
  3.0 16.0 %copy-start = (bf16[32,4608]{1,0:T(8,128)(2,1)S(1)}, bf16[32,4608]{1,0:T(8,128)(2,1)}, u32[]{:S(2)}) copy-start(bf16[32,4608]{1,0:T(8,128)(2,1)} %refs_0_.4) | copy-start | bytes 884740
  7.7 8.9 %collective-permute-start.2 = (bf16[32,640]{1,0:T(8,128)(2,1)S(1)}, bf16[32,640]{1,0:T(8,128)(2,1)S(1)}, u32[]{:S(2)}, u32[]{:S(2)}) collective-permute-start(bf16[32,640]{1,0:T(8,128)(2,1)S(1)} %get-tuple-element.33), channel_id=1, source_target_pairs={{0,10},{1,11},{4,6},{5,7},{8,2},{9,3},{12,0},{13,1},{14,4},{15,5},... | collective-permute-start | bytes 122888 | tf_op jit(solution)/shard_map/ppermute | solution.py:407
  11.8 5.8 %collective-permute-start.3 = (bf16[32,640]{1,0:T(8,128)(2,1)S(1)}, bf16[32,640]{1,0:T(8,128)(2,1)S(1)}, u32[]{:S(2)}, u32[]{:S(2)}) collective-permute-start(bf16[32,640]{1,0:T(8,128)(2,1)S(1)} %get-tuple-element.34), channel_id=1, source_target_pairs={{0,12},{1,13},{4,14},{5,15},{8,10},{9,11},{12,6},{13,7},{14,2},{15... | collective-permute-start | bytes 122888 | tf_op jit(solution)/shard_map/ppermute | solution.py:407
  11.9 7.1 %collective-permute-start.4 = (bf16[32,640]{1,0:T(8,128)(2,1)S(1)}, bf16[32,640]{1,0:T(8,128)(2,1)S(1)}, u32[]{:S(2)}, u32[]{:S(2)}) collective-permute-start(bf16[32,640]{1,0:T(8,128)(2,1)S(1)} %get-tuple-element.35), channel_id=1, source_target_pairs={{0,14},{1,15},{4,10},{5,11},{8,6},{9,7},{12,2},{13,3},{14,0},{15,1... | collective-permute-start | bytes 122888 | tf_op jit(solution)/shard_map/ppermute | solution.py:407
  19.2 15.8 %collective-permute-start.13 = (bf16[256,2304]{1,0:T(8,128)(2,1)S(1)}, bf16[256,2304]{1,0:T(8,128)(2,1)S(1)}, u32[]{:S(2)}, u32[]{:S(2)}) collective-permute-start(bf16[256,2304]{1,0:T(8,128)(2,1)S(1)} %get-tuple-element.40.refs_2_.refs_0_), channel_id=1, source_target_pairs={{0,1},{1,0},{2,3},{3,2},{4,5},{5,4},{6,7},{7,6},{8,9},{9,8},{10,11... | collective-permute-start | bytes 3538952 | tf_op jit(solution)/shard_map/ppermute | solution.py:22
  19.3 8.6 %collective-permute-start.5 = (bf16[32,2304]{1,0:T(8,128)(2,1)S(1)}, bf16[32,2304]{1,0:T(8,128)(2,1)S(1)}, u32[]{:S(2)}, u32[]{:S(2)}) collective-permute-start(bf16[32,2304]{1,0:T(8,128)(2,1)S(1)} %get-tuple-element.36), channel_id=1, source_target_pairs={{0,4},{1,5},{4,8},{5,9},{8,12},{9,13},{12,14},{13,15},{14,10},{15,... | collective-permute-start | bytes 442376 | tf_op jit(solution)/shard_map/ppermute | solution.py:55
  19.3 9.3 %collective-permute-start.6 = (bf16[32,2304]{1,0:T(8,128)(2,1)S(1)}, bf16[32,2304]{1,0:T(8,128)(2,1)S(1)}, u32[]{:S(2)}, u32[]{:S(2)}) collective-permute-start(bf16[32,2304]{1,0:T(8,128)(2,1)S(1)} %get-tuple-element.37), channel_id=1, source_target_pairs={{0,4},{1,5},{4,8},{5,9},{8,12},{9,13},{12,14},{13,15},{14,10},{15,... | collective-permute-start | bytes 442376 | tf_op jit(solution)/shard_map/ppermute | solution.py:55
  19.4 9.3 %collective-permute-start.7 = (bf16[32,2304]{1,0:T(8,128)(2,1)S(1)}, bf16[32,2304]{1,0:T(8,128)(2,1)S(1)}, u32[]{:S(2)}, u32[]{:S(2)}) collective-permute-start(bf16[32,2304]{1,0:T(8,128)(2,1)S(1)} %get-tuple-element.38), channel_id=1, source_target_pairs={{0,2},{1,3},{4,0},{5,1},{8,4},{9,5},{12,8},{13,9},{14,12},{15,13},... | collective-permute-start | bytes 442376 | tf_op jit(solution)/shard_map/ppermute | solution.py:55
  21.4 9.4 %collective-permute-start.8 = (bf16[32,2304]{1,0:T(8,128)(2,1)S(1)}, bf16[32,2304]{1,0:T(8,128)(2,1)S(1)}, u32[]{:S(2)}, u32[]{:S(2)}) collective-permute-start(bf16[32,2304]{1,0:T(8,128)(2,1)S(1)} %get-tuple-element.39), channel_id=1, source_target_pairs={{0,2},{1,3},{4,0},{5,1},{8,4},{9,5},{12,8},{13,9},{14,12},{15,13},... | collective-permute-start | bytes 442376 | tf_op jit(solution)/shard_map/ppermute | solution.py:55
  30.8 4.2 %copy-start.1 = (s32[4,1]{0,1:T(1,128)S(1)}, s32[4,1]{0,1:T(1,128)}, u32[]{:S(2)}) copy-start(s32[4,1]{0,1:T(1,128)} %param.10) | copy-start | bytes 52
  30.9 9.0 %collective-permute-start.10 = (bf16[32,2304]{1,0:T(8,128)(2,1)S(1)}, bf16[32,2304]{1,0:T(8,128)(2,1)S(1)}, u32[]{:S(2)}, u32[]{:S(2)}) collective-permute-start(bf16[32,2304]{1,0:T(8,128)(2,1)S(1)} %get-tuple-element.44), channel_id=1, source_target_pairs={{0,4},{1,5},{4,8},{5,9},{8,12},{9,13},{12,14},{13,15},{14,10},{15,... | collective-permute-start | bytes 442376 | tf_op jit(solution)/shard_map/ppermute | solution.py:55
  32.7 7.2 %collective-permute-start.11 = (bf16[32,2304]{1,0:T(8,128)(2,1)S(1)}, bf16[32,2304]{1,0:T(8,128)(2,1)S(1)}, u32[]{:S(2)}, u32[]{:S(2)}) collective-permute-start(bf16[32,2304]{1,0:T(8,128)(2,1)S(1)} %get-tuple-element.45), channel_id=1, source_target_pairs={{0,2},{1,3},{4,0},{5,1},{8,4},{9,5},{12,8},{13,9},{14,12},{15,13},... | collective-permute-start | bytes 442376 | tf_op jit(solution)/shard_map/ppermute | solution.py:55
  33.0 7.4 %collective-permute-start.12 = (bf16[32,2304]{1,0:T(8,128)(2,1)S(1)}, bf16[32,2304]{1,0:T(8,128)(2,1)S(1)}, u32[]{:S(2)}, u32[]{:S(2)}) collective-permute-start(bf16[32,2304]{1,0:T(8,128)(2,1)S(1)} %get-tuple-element.46), channel_id=1, source_target_pairs={{0,2},{1,3},{4,0},{5,1},{8,4},{9,5},{12,8},{13,9},{14,12},{15,13},... | collective-permute-start | bytes 442376 | tf_op jit(solution)/shard_map/ppermute | solution.py:55
  33.0 7.3 %collective-permute-start.9 = (bf16[32,2304]{1,0:T(8,128)(2,1)S(1)}, bf16[32,2304]{1,0:T(8,128)(2,1)S(1)}, u32[]{:S(2)}, u32[]{:S(2)}) collective-permute-start(bf16[32,2304]{1,0:T(8,128)(2,1)S(1)} %get-tuple-element.43), channel_id=1, source_target_pairs={{0,4},{1,5},{4,8},{5,9},{8,12},{9,13},{12,14},{13,15},{14,10},{15,... | collective-permute-start | bytes 442376 | tf_op jit(solution)/shard_map/ppermute | solution.py:55
  35.8 4.1 %collective-permute-start.14 = (bf16[128,128]{1,0:T(8,128)(2,1)S(1)}, bf16[128,128]{1,0:T(8,128)(2,1)S(1)}, u32[]{:S(2)}, u32[]{:S(2)}) collective-permute-start(bf16[128,128]{1,0:T(8,128)(2,1)S(1)} %get-tuple-element.48), channel_id=1, source_target_pairs={{0,2},{1,3},{2,0},{3,1},{4,6},{5,7},{6,4},{7,5},{8,10},{9,11},{10,... | collective-permute-start | bytes 98312 | tf_op jit(solution)/shard_map/ppermute | solution.py:448
  40.5 11.7 %collective-permute-start.15 = (bf16[256,2304]{1,0:T(8,128)(2,1)S(1)}, bf16[256,2304]{1,0:T(8,128)(2,1)S(1)}, u32[]{:S(2)}, u32[]{:S(2)}) collective-permute-start(bf16[256,2304]{1,0:T(8,128)(2,1)S(1)} %get-tuple-element.50.refs_4_.refs_0_), channel_id=1, source_target_pairs={{0,1},{1,0},{2,3},{3,2},{4,5},{5,4},{6,7},{7,6},{8,9},{9,8},{10,11... | collective-permute-start | bytes 3538952 | tf_op jit(solution)/shard_map/ppermute | solution.py:22
  40.5 10.2 %collective-permute-start.17 = (bf16[128,128]{1,0:T(8,128)(2,1)S(1)}, bf16[128,128]{1,0:T(8,128)(2,1)S(1)}, u32[]{:S(2)}, u32[]{:S(2)}) collective-permute-start(bf16[128,128]{1,0:T(8,128)(2,1)S(1)} %get-tuple-element.49.refs_5_), channel_id=1, source_target_pairs={{0,12},{1,13},{2,14},{3,15},{4,0},{5,1},{6,2},{7,3},{8,4},{9,5},{1... | collective-permute-start | bytes 98312 | tf_op jit(solution)/shard_map/ppermute | solution.py:456
  43.0 7.8 %collective-permute-start.18 = (bf16[128,128]{1,0:T(8,128)(2,1)S(1)}, bf16[128,128]{1,0:T(8,128)(2,1)S(1)}, u32[]{:S(2)}, u32[]{:S(2)}) collective-permute-start(bf16[128,128]{1,0:T(8,128)(2,1)S(1)} %get-tuple-element.49.refs_5_), channel_id=1, source_target_pairs={{0,8},{1,9},{2,10},{3,11},{4,12},{5,13},{6,14},{7,15},{8,0},{9,1},... | collective-permute-start | bytes 98312 | tf_op jit(solution)/shard_map/ppermute | solution.py:456
  43.6 7.2 %collective-permute-start.19 = (bf16[128,128]{1,0:T(8,128)(2,1)S(1)}, bf16[128,128]{1,0:T(8,128)(2,1)S(1)}, u32[]{:S(2)}, u32[]{:S(2)}) collective-permute-start(bf16[128,128]{1,0:T(8,128)(2,1)S(1)} %get-tuple-element.49.refs_5_), channel_id=1, source_target_pairs={{0,4},{1,5},{2,6},{3,7},{4,8},{5,9},{6,10},{7,11},{8,12},{9,13},{1... | collective-permute-start | bytes 98312 | tf_op jit(solution)/shard_map/ppermute | solution.py:456
  44.8 6.7 %collective-permute-start.16 = (bf16[64,2304]{1,0:T(8,128)(2,1)S(1)}, bf16[64,2304]{1,0:T(8,128)(2,1)S(1)}, u32[]{:S(2)}, u32[]{:S(2)}) collective-permute-start(bf16[64,2304]{1,0:T(8,128)(2,1)S(1)} %get-tuple-element.51), channel_id=1, source_target_pairs={{0,4},{1,3},{4,8},{5,1},{8,12},{9,5},{12,14},{13,9},{14,10},{15,13... | collective-permute-start | bytes 884744 | tf_op jit(solution)/shard_map/ppermute | solution.py:460
  51.6 5.6 %collective-permute-start.20 = (bf16[64,2304]{1,0:T(8,128)(2,1)S(1)}, bf16[64,2304]{1,0:T(8,128)(2,1)S(1)}, u32[]{:S(2)}, u32[]{:S(2)}) collective-permute-start(bf16[64,2304]{1,0:T(8,128)(2,1)S(1)} %shard_map.73.refs_4_.refs_2_), channel_id=1, source_target_pairs={{0,1},{1,0},{2,3},{3,2},{4,5},{5,4},{6,7},{7,6},{8,9},{9,8},{10,11... | collective-permute-start | bytes 884744 | tf_op jit(solution)/shard_map/ppermute | solution.py:22
  51.7 3.5 %collective-permute-start.21 = (bf16[128,128]{1,0:T(8,128)(2,1)S(1)}, bf16[128,128]{1,0:T(8,128)(2,1)S(1)}, u32[]{:S(2)}, u32[]{:S(2)}) collective-permute-start(bf16[128,128]{1,0:T(8,128)(2,1)S(1)} %get-tuple-element.53.refs_1_), channel_id=1, source_target_pairs={{0,1},{1,0},{2,3},{3,2},{4,5},{5,4},{6,7},{7,6},{8,9},{9,8},{10,11... | collective-permute-start | bytes 98312 | tf_op jit(solution)/shard_map/ppermute | solution.py:22
  (1 other events, 3.6 us)

commit v8 on v7

--- a/solution.py
+++ b/solution.py
@@ -202,66 +202,125 @@
     ]
 
 
-def first_load_kernel(n, window, distances, w_ref, tokens_ref, down_ref, w_out, factor, *refs):
-    *sends, tokens, down, sems, small_sems = refs
-    copies = weight_copies(0, w_ref, w_out, sems)
-    small = [
-        pltpu.make_async_copy(source, to, small_sems.at[k])
+def prepare_kernel(n, window, distances, tokens_ref, down_ref, factor, *refs):
+    *sends, tokens, down, sems = refs
+    copies = [
+        pltpu.make_async_copy(source, to, sems.at[k])
         for k, (source, to) in enumerate(((tokens_ref, tokens), (down_ref, down)))
     ]
-    for copy in small + copies:
+    for copy in copies:
         copy.start()
-    for copy in small:
-        copy.wait()
+    copies[0].wait()
+    for distance, send in zip(distances, sends):
+        start = pl.multiple_of(window.start(chip_at(distance, n)), 128)
+        send[...] = tokens[:, pl.ds(start, window.size)]
+    copies[1].wait()
     zeros = jnp.zeros((down.shape[1], window.size - window.width), jnp.float32)
     for index in range(down.shape[0]):
         wide = jnp.concatenate([down[index], zeros], 1)
         factor[index] = pltpu.roll(wide, window.shift(lax.axis_index("seq")), 1).astype(jnp.bfloat16)
-    for distance, send in zip(distances, sends):
-        start = pl.multiple_of(window.start(chip_at(distance, n)), 128)
-        send[...] = tokens[:, pl.ds(start, window.size)]
+
+
+def first_load_kernel(w_ref, w_out, sems):
+    copies = weight_copies(0, w_ref, w_out, sems)
+    for copy in copies:
+        copy.start()
     for copy in copies:
         copy.wait()
 
 
-def second_load_kernel(first, w_ref, up_ref, w_out, up_out, held, sems, up_sem):
+def second_load_kernel(chips, rows, w_ref, up_ref, first_w, near, w_out, up_out, base, up, held, sems, up_sem):
+    first, parts = first_w.shape[0], sems.shape[0]
     copies = weight_copies(first, w_ref, w_out, sems)
-    up_copy = pltpu.make_async_copy(up_ref, held, up_sem)
+    up_copy = pltpu.make_async_copy(up_ref, up, up_sem)
     up_copy.start()
     for copy in copies:
         copy.start()
+    assemble_core(near, chips, rows, held)
+    base[...] = jnp.dot(held[:, :first], first_w[...], preferred_element_type=jnp.float32)
     up_copy.wait()
-    up_out[...] = held[...].astype(jnp.bfloat16)
-    for copy in copies:
+    up_out[...] = up[...].astype(jnp.bfloat16)
+    deep = w_out.shape[0] // parts
+    for k, copy in enumerate(copies):
         copy.wait()
-
-
-def load(kernel, arrays, after, outs, scratch):
-    operands = len(arrays)
+        columns = held[:, first + k * deep : first + (k + 1) * deep]
+        weight = w_out[k * deep : (k + 1) * deep, :]
+        base[...] += jnp.dot(columns, weight, preferred_element_type=jnp.float32)
+
+
+def assemble_core(ref, chips, rows, held):
+    depth = ref.shape[1]
+    for i in range(chips):
+        for k in range(CHUNKS):
+            at = (i * CHUNKS + k) * rows
+            held[i * rows : (i + 1) * rows, k * depth : (k + 1) * depth] = ref[at : at + rows, :]
+
+
+def core_kernel(rows, ref, *refs):
+    *weights, base, held = refs
+    assemble_core(ref, base.shape[0] // rows, rows, held)
+    columns = tile_width(base.shape[1])
+    for j in range(0, base.shape[1], columns):
+        at = slice(j, j + columns)
+        base[:, at] = multiply(held, weights, at)
+
+
+def both_kernel(rows, ref, mine, *refs):
+    *weights, base, held = refs
+    chips = mine.shape[0] // rows
+    c = lax.axis_index("adapter")
+    assemble_core(ref, chips, rows, held)
+    columns = tile_width(base.shape[1])
+    for j in range(0, base.shape[1], columns):
+        at = slice(j, j + columns)
+        tile = multiply(held, weights, at)
+        for i in range(chips):
+            here = slice(i * rows, (i + 1) * rows)
+            for core, value in ((c, mine[here, at]), (1 - c, tile[here])):
+                base[pl.ds(pl.multiple_of((2 * i + core) * rows, rows), rows), at] = value
+
+
+def core_rows(ref, chips, rows, weights, after, mine=None):
+    total, depth, width = rows * chips, sum(w.shape[0] for w in weights), weights[0].shape[1]
+    (base,) = call(
+        functools.partial(core_kernel if mine is None else both_kernel, rows),
+        [ref] + ([] if mine is None else [mine]) + weights,
+        after,
+        [((total if mine is None else 2 * total, width), jnp.float32)],
+        [pltpu.VMEM((total, depth), jnp.bfloat16)],
+        limit=8 + (2 * total * depth >> 20),
+        flops=2 * total * depth * width,
+    )
+    return base
+
+
+def load(kernel, arrays, after, outs, scratch, inside=(), flops=0):
+    operands = len(arrays) + len(inside)
 
     def body(*refs):
         kernel(*refs[:operands], *refs[operands + len(after) :])
 
     return pl.pallas_call(
         body,
-        out_shape=[pltpu.VMEM(shape, jnp.bfloat16) for shape in outs],
-        in_specs=[pl.BlockSpec(memory_space=pltpu.HBM)] * operands
+        out_shape=[pltpu.VMEM(shape, dtype) for shape, dtype in outs],
+        in_specs=[pl.BlockSpec(memory_space=pltpu.HBM)] * len(arrays)
+        + whole(len(inside))
         + [pl.BlockSpec(memory_space=pl.ANY)] * len(after),
         out_specs=whole(len(outs)),
         scratch_shapes=scratch,
         compiler_params=pltpu.CompilerParams(vmem_limit_bytes=8 << 20),
         cost_estimate=pl.CostEstimate(
-            flops=0, bytes_accessed=2 * outs[0][0] * outs[0][1], transcendentals=0
+            flops=flops, bytes_accessed=2 * outs[0][0][0] * outs[0][0][1], transcendentals=0
         ),
-    )(*(pltpu.with_memory_space_constraint(x, pltpu.HBM) for x in arrays), *after)
+    )(*(pltpu.with_memory_space_constraint(x, pltpu.HBM) for x in arrays), *in_vmem(inside), *after)
 
 
 def assemble(pairs, counts, rows, held):
     c = lax.axis_index("adapter")
     first = 0
-    for pair, (begin, end) in zip(pairs, counts):
+    for pair, chips in zip(pairs, counts):
         depth = pair[0].shape[1]
-        for chip in range(begin, end):
+        for chip in range(chips):
             for k in range(CHUNKS):
                 at = (chip * CHUNKS + k) * rows
                 for ref, core in zip(pair, (c, 1 - c)):
@@ -295,7 +354,7 @@
 
 
 def base_rows(pairs, counts, rows, weights, after):
-    chips = sum(end - begin for begin, end in counts)
+    chips = sum(counts)
     total, depth, width = 2 * rows * chips, sum(w.shape[0] for w in weights), weights[0].shape[1]
     arrays = [x for pair in pairs for x in pair]
     (base,) = call(
@@ -310,11 +369,9 @@
     return base
 
 
-def finish_kernel(n, rows, groups, skipped, adapters, live, *refs):
+def finish_kernel(n, rows, groups, adapters, live, *refs):
     *bases, own, other, up_ref = refs[: len(groups) + 3]
-    out_ref, *token, shrink, block, sems = refs[len(groups) + 3 + skipped :]
-    for ref in token:
-        ref[...] = jnp.zeros_like(ref)
+    out_ref, shrink, block, sems = refs[len(groups) + 3 :]
     c = lax.axis_index("adapter")
     chip_rows, rank = 2 * rows, up_ref.shape[1]
     tiles, _, columns = block.shape
@@ -352,30 +409,25 @@
         copy.wait()
 
 
-def finish(n, rows, groups, scalars, bases, own, other, up, into):
+def finish(n, rows, groups, scalars, bases, own, other, up):
     rank, width = up.shape[1:]
-    count = sum(len(group) for group in groups)
-    total, columns = 2 * rows * count, tile_width(width)
+    total, columns = 2 * n * rows, tile_width(width)
     arrays = [*bases, own, other, up]
-    token = [] if into else [pltpu.VMEM((8, 128), jnp.float32)]
     return pl.pallas_call(
-        functools.partial(finish_kernel, n, rows, groups, len(into)),
-        out_shape=[jax.ShapeDtypeStruct((2 * n * rows, width), jnp.bfloat16)] + token,
-        in_specs=[pl.BlockSpec(memory_space=pltpu.SMEM)] * len(scalars)
-        + whole(len(arrays))
-        + [pl.BlockSpec(memory_space=pl.ANY)] * len(into),
-        out_specs=[pl.BlockSpec(memory_space=pl.ANY)] + whole(len(token)),
+        functools.partial(finish_kernel, n, rows, groups),
+        out_shape=jax.ShapeDtypeStruct((total, width), jnp.bfloat16),
+        in_specs=[pl.BlockSpec(memory_space=pltpu.SMEM)] * len(scalars) + whole(len(arrays)),
+        out_specs=pl.BlockSpec(memory_space=pl.ANY),
         scratch_shapes=[
             pltpu.VMEM((n, 2 * rows, rank), jnp.bfloat16),
             pltpu.VMEM((width // columns, total, columns), jnp.bfloat16),
-            pltpu.SemaphoreType.DMA((width // columns, count)),
+            pltpu.SemaphoreType.DMA((width // columns, n)),
         ],
-        input_output_aliases={len(scalars) + len(arrays): 0} if into else {},
         compiler_params=pltpu.CompilerParams(vmem_limit_bytes=8 << 20),
         cost_estimate=pl.CostEstimate(
             flops=2 * total * rank * width, bytes_accessed=2 * total * width, transcendentals=0
         ),
-    )(*scalars, *in_vmem(arrays), *into)
+    )(*scalars, *in_vmem(arrays))
 
 
 def on_device(n, tokens, weight, down, up, adapter_per_block, rows_per_block):
@@ -391,82 +443,100 @@
 
     (behind,), (ahead,) = ring_hop([tokens], [tokens], n)
     ends = far + [last]
-    cut = features * 3 // 5 // 256 * 256
-    weights, factor, *sends = load(
-        functools.partial(first_load_kernel, n, window, ends),
-        [weight, tokens, jnp.swapaxes(down, 1, 2)],
+    bf16 = jnp.bfloat16
+    factor, *sends = load(
+        functools.partial(prepare_kernel, n, window, ends),
+        [tokens, jnp.swapaxes(down, 1, 2)],
         [],
-        [(cut, weight.shape[1]), (held, rank, window.size)] + [(rows, window.size)] * len(ends),
+        [((held, rank, window.size), bf16)] + [((rows, window.size), bf16)] * len(ends),
         [
             pltpu.VMEM(tokens.shape, tokens.dtype),
             pltpu.VMEM((held, rank, width), down.dtype),
-            pltpu.SemaphoreType.DMA((4,)),
             pltpu.SemaphoreType.DMA((2,)),
         ],
     )
     received = [lax.ppermute(x, AXES, ring_perm(n, d)) for d, x in zip(ends, sends)]
     come_from = [-d for d in far] + [last]
-    piece = ((rows, depth), jnp.bfloat16)
+    cut, hidden = features * 3 // 5 // 256 * 256, weight.shape[1]
+    (first_weight,) = load(
+        first_load_kernel, [weight], [], [((cut, hidden), bf16)], [pltpu.SemaphoreType.DMA((4,))]
+    )
+    piece = ((rows, depth), bf16)
     near_rows, *chunks = call(
         near_kernel,
         [tokens, behind, ahead, factor],
-        received,
-        [((3 * CHUNKS * rows + rank, depth), jnp.bfloat16)] + [piece] * (2 * CHUNKS),
+        [first_weight, *received],
+        [((len(near) * CHUNKS * rows + rank, depth), bf16)] + [piece] * (2 * CHUNKS),
     )
 
     up_way, down_way = chunks[:CHUNKS], chunks[CHUNKS:]
-    near_pair = (near_rows, swap_cores(near_rows, n))
-    other_weights, up = load(
-        functools.partial(second_load_kernel, cut),
+    near_swapped = swap_cores(near_rows, n)
+    own = len(near) * rows
+    other_weight, up, mine = load(
+        functools.partial(second_load_kernel, len(near), rows),
         [weight, up],
-        [near_rows],
-        [(features - cut, weight.shape[1]), up.shape],
-        [pltpu.VMEM(up.shape, up.dtype), pltpu.SemaphoreType.DMA((4,)), pltpu.SemaphoreType.DMA],
-    )
-    weights = [weights, other_weights]
+        [],
+        [((features - cut, hidden), bf16), (up.shape, bf16), ((own, hidden), jnp.float32)],
+        [
+            pltpu.VMEM(up.shape, up.dtype),
+            pltpu.VMEM((own, features), bf16),
+            pltpu.SemaphoreType.DMA((4,)),
+            pltpu.SemaphoreType.DMA,
+        ],
+        [first_weight, near_rows],
+        2 * own * features * hidden,
+    )
+    weights = [first_weight, other_weight]
     arrived = []
     for _ in range(2, last - 1):
         up_way, down_way = ring_hop(up_way, down_way, n)
         arrived += up_way + down_way
-    mid_rows, *chunks = join(arrived, [other_weights], 2)
+    mid_rows, *chunks = join(arrived, [other_weight], 2)
     up_way, down_way = chunks[:CHUNKS], chunks[CHUNKS:]
 
     total, rounded = call(
         functools.partial(partial_kernel, n, window, [near, mid], come_from),
-        [near_rows, mid_rows, *received, factor, near_pair[1]],
+        [near_rows, mid_rows, *received, factor, near_swapped],
         [],
         sums,
         [
             pltpu.SMEM(adapters.shape, jnp.int32),
-            pltpu.VMEM((n * rows, window.size), jnp.bfloat16),
+            pltpu.VMEM((n * rows, window.size), bf16),
             pltpu.VMEM((2 * held, n * rows, rank), jnp.float32),
             pltpu.VMEM((n, rows, rank), jnp.float32),
             pltpu.SemaphoreType.DMA,
         ],
         outside=[adapters],
     )
+    bases = [core_rows(near_swapped, len(near), rows, weights, [rounded], mine)]
     total, rounded = call(add_kernel, [total, lax.ppermute(rounded, AXES, y_perm(n))], [], sums)
     up_way, down_way = ring_hop(up_way, down_way, n)
-    far_rows, turned = join([mid_rows, *up_way, *down_way], [rounded], 1)
-
-    far_pair = (far_rows, swap_cores(far_rows, n))
-    bases = [base_rows([near_pair], [(0, len(near))], rows, weights, [far_rows])]
+    late_rows, turned = join([mid_rows, *up_way, *down_way], [rounded, *bases], 1)
+
+    late = mid + far
+    late_swapped = swap_cores(late_rows, n)
+    mine = core_rows(late_rows, len(late), rows, weights, [])
     total, rounded = call(
         add_kernel,
         [total] + [lax.ppermute(rounded, AXES, z_perm(n, shift)) for shift in range(1, n // 2)],
         [],
         sums,
     )
-    (last_rows,) = join([lax.ppermute(turned, AXES, ring_perm(n, 1, -1))], [rounded, *bases])
-
-    count = len(mid)
-    bases.append(base_rows([far_pair], [(0, count)], rows, weights, [last_rows]))
-    scalars = [adapters, rows_per_block]
-    sums = [total, swap_cores(rounded, n)]
-    out, token = finish(n, rows, [near, mid], scalars, bases, *sums, up, [])
-    pairs = [far_pair, (last_rows, swap_cores(last_rows, n))]
-    bases = [base_rows(pairs, [(count, count + len(far)), (0, 1)], rows, weights, [token])]
-    return finish(n, rows, [far + [last]], scalars, bases, *sums, up, [out])[0]
+    (last_rows,) = join([lax.ppermute(turned, AXES, ring_perm(n, 1, -1))], [rounded, mine])
+
+    bases.append(core_rows(late_swapped, len(late), rows, weights, [last_rows], mine))
+    last_pair = (last_rows, swap_cores(last_rows, n))
+    bases.append(base_rows([last_pair], [1], rows, weights, bases[-1:]))
+    return finish(
+        n,
+        rows,
+        [near, late, [last]],
+        [adapters, rows_per_block],
+        bases,
+        total,
+        swap_cores(rounded, n),
+        up,
+    )
 
 
 def solution(mesh):

time: 63.7 us -> 58.1 us (0.912)
  waiting for transfers between devices: 10.5 us -> 2.59 us
  Pallas kernels: 25.8 us -> 28.1 us
    ppermute x1, waiting for transfers between devices: 3.97 us -> 0.01 us  [on_device(): lax.ppermute(rounded, AXES, y_perm(n))]
    ppermute x3, waiting for transfers between devices: 2.41 us -> 0.01 us  [on_device(): lax.ppermute(x, AXES, ring_perm(n, d))]
    ppermute x5, waiting for transfers between devices: 2.57 us -> 0.78 us  [ring_hop(): lax.ppermute(x, AXES, ring_perm(n, -1))]
    ppermute x3, waiting for transfers between devices: 0.01 us -> 1.78 us  [on_device(): lax.ppermute(rounded, AXES, z_perm(n, shift))]
    pallas_call x10 -> x11, Pallas kernels: 12.8 us -> 14.3 us  [call(): pl.pallas_call(body, out_shape=[pltpu.VMEM(shape, dtype) for shape, dtype...]
    ppermute x1, starting transfers between devices: 0.1 us -> 1 us  [on_device(): lax.ppermute(rounded, AXES, y_perm(n))]
    pallas_call x4, Pallas kernels: 13 us -> 13.8 us  [the longest x3 11.4 us: load(): pl.pallas_call(body, out_shape=[pltpu.VMEM(shape, dtype) for shape, dtype...]
    ppermute x5, waiting for transfers between devices: 0.82 us -> 0.01 us  [ring_hop(): lax.ppermute(x, AXES, ring_perm(n, 1))]
  transfers between devices with their start and end apart: 22 -> 22, of which waited for: 7 -> 3; matrix products, arithmetic and copies ran while one was open for 0% -> 0% of each run, Pallas kernels for 31% -> 44%
where the time goes in v8:
time: 58.1 us; the launch traced here: 58 us
  Pallas kernels  28.1 us (48%)
  starting transfers between devices  26.8 us (46%)
  waiting for transfers between devices  2.59 us (4%)
    pallas_call x11, Pallas kernels, call(): pl.pallas_call(body, out_shape=[pltpu.VMEM(shape, dtype) for shape, dtype...  14.3 us
    pallas_call x3, Pallas kernels, load(): pl.pallas_call(body, out_shape=[pltpu.VMEM(shape, dtype) for shape, dtype...  11.4 us
    ppermute x3, starting transfers between devices, on_device(): lax.ppermute(x, AXES, ring_perm(n, d))  8.88 us
    ppermute x5, starting transfers between devices, ring_hop(): lax.ppermute(x, AXES, ring_perm(n, 1))  6.99 us
    ppermute x5, starting transfers between devices, ring_hop(): lax.ppermute(x, AXES, ring_perm(n, -1))  4.24 us
    ppermute x3, starting transfers between devices, on_device(): lax.ppermute(rounded, AXES, z_perm(n, shift))  3.58 us
    pallas_call x1, Pallas kernels, finish(): pl.pallas_call(functools.partial(finish_kernel, n, rows, groups), out_sha...  2.41 us
    ppermute x3, waiting for transfers between devices, on_device(): lax.ppermute(rounded, AXES, z_perm(n, shift))  1.78 us
  transfers between devices with their start and end apart: 22, of which 3 were waited for; matrix products, arithmetic and copies ran while one was open for 0% of the time, Pallas kernels for 44%

profile of v8, /device:TPU:0, one launch (start us, length us, event | category | flops | bytes accessed | tf_op | source)
XLA Modules:
  0.0 58.0 jit_solution(4692517428300077439)
XLA Ops:
  0.0 3.0 %collective-permute-start = (bf16[32,4608]{1,0:T(8,128)(2,1)}, bf16[32,4608]{1,0:T(8,128)(2,1)S(1)}, u32[]{:S(2)}, u32[]{:S(2)}) collective-permute-start(bf16[32,4608]{1,0:T(8,128)(2,1)} %refs_0_.6), channel_id=1, source_target_pairs={{0,4},{1,5},{4,8},{5,9},{8,12},{9,13},{12,14},{13,15},{14,10},{15,... | collective-permute-start | bytes 884744 | tf_op jit(solution)/shard_map/ppermute | solution.py:55
  3.0 1.2 %shard_map.64 = (bf16[2,64,640]{2,1,0:T(8,128)(2,1)S(1)}, bf16[32,640]{1,0:T(8,128)(2,1)S(1)}, bf16[32,640]{1,0:T(8,128)(2,1)S(1)}, bf16[32,640]{1,0:T(8,128)(2,1)S(1)}) custom-call(bf16[32,4608]{1,0:T(8,128)(2,1)} %refs_0_.6, f32[2,64,576]{2,1,0:T(8,128)} %bitcast.4), custom_call_target="tpu_custom_call" | custom-call | bytes 256 | tf_op jit(solution)/shard_map/pallas_call | solution.py:303
  4.3 4.0 %collective-permute-start.2 = (bf16[32,640]{1,0:T(8,128)(2,1)S(1)}, bf16[32,640]{1,0:T(8,128)(2,1)S(1)}, u32[]{:S(2)}, u32[]{:S(2)}) collective-permute-start(bf16[32,640]{1,0:T(8,128)(2,1)S(1)} %get-tuple-element.31), channel_id=1, source_target_pairs={{0,10},{1,11},{4,6},{5,7},{8,2},{9,3},{12,0},{13,1},{14,4},{15,5},... | collective-permute-start | bytes 122888 | tf_op jit(solution)/shard_map/ppermute | solution.py:458
  8.4 4.7 %collective-permute-start.4 = (bf16[32,640]{1,0:T(8,128)(2,1)S(1)}, bf16[32,640]{1,0:T(8,128)(2,1)S(1)}, u32[]{:S(2)}, u32[]{:S(2)}) collective-permute-start(bf16[32,640]{1,0:T(8,128)(2,1)S(1)} %get-tuple-element.33), channel_id=1, source_target_pairs={{0,14},{1,15},{4,10},{5,11},{8,6},{9,7},{12,2},{13,3},{14,0},{15,1... | collective-permute-start | bytes 122888 | tf_op jit(solution)/shard_map/ppermute | solution.py:458
  13.1 4.5 %shard_map.65.refs_4_.refs_2_.refs_1_ = bf16[2560,2304]{1,0:T(8,128)(2,1)S(1)} custom-call(bf16[4608,2304]{1,0:T(8,128)(2,1)} %refs_0_.7), custom_call_target="tpu_custom_call" | custom-call | bytes 11796480 | tf_op jit(solution)/shard_map/pallas_call | solution.py:303
  18.0 1.4 %collective-permute-start.7 = (bf16[32,2304]{1,0:T(8,128)(2,1)S(1)}, bf16[32,2304]{1,0:T(8,128)(2,1)S(1)}, u32[]{:S(2)}, u32[]{:S(2)}) collective-permute-start(bf16[32,2304]{1,0:T(8,128)(2,1)S(1)} %get-tuple-element.38), channel_id=1, source_target_pairs={{0,4},{1,5},{4,8},{5,9},{8,12},{9,13},{12,14},{13,15},{14,10},{15,... | collective-permute-start | bytes 442376 | tf_op jit(solution)/shard_map/ppermute | solution.py:55
  19.4 0.7 %collective-permute-start.8 = (bf16[32,2304]{1,0:T(8,128)(2,1)S(1)}, bf16[32,2304]{1,0:T(8,128)(2,1)S(1)}, u32[]{:S(2)}, u32[]{:S(2)}) collective-permute-start(bf16[32,2304]{1,0:T(8,128)(2,1)S(1)} %get-tuple-element.39), channel_id=1, source_target_pairs={{0,2},{1,3},{4,0},{5,1},{8,4},{9,5},{12,8},{13,9},{14,12},{15,13},... | collective-permute-start | bytes 442376 | tf_op jit(solution)/shard_map/ppermute | solution.py:55
  20.1 1.9 %collective-permute-start.9 = (bf16[32,2304]{1,0:T(8,128)(2,1)S(1)}, bf16[32,2304]{1,0:T(8,128)(2,1)S(1)}, u32[]{:S(2)}, u32[]{:S(2)}) collective-permute-start(bf16[32,2304]{1,0:T(8,128)(2,1)S(1)} %get-tuple-element.40), channel_id=1, source_target_pairs={{0,2},{1,3},{4,0},{5,1},{8,4},{9,5},{12,8},{13,9},{14,12},{15,13},... | collective-permute-start | bytes 442376 | tf_op jit(solution)/shard_map/ppermute | solution.py:55
  22.0 5.7 %shard_map.67 = (bf16[2048,2304]{1,0:T(8,128)(2,1)S(1)}, bf16[4,64,2304]{2,1,0:T(8,128)(2,1)S(1)}, f32[96,2304]{1,0:T(8,128)S(1)}) custom-call(bf16[4608,2304]{1,0:T(8,128)(2,1)} %refs_0_.7, f32[4,64,2304]{2,1,0:T(8,128)} %refs_1_.1, bf16[2560,2304]{1,0:T(8,128)(2,1)S(1)} %shard_map.65.refs_4_.refs_2_.refs_1_, ...), custom_call_target="tpu_custom_call" | custom-call | flops 2038431744 | bytes 9437184 | tf_op jit(solution)/shard_map/pallas_call | solution.py:303
  28.2 1.1 %collective-permute-start.10 = (bf16[32,2304]{1,0:T(8,128)(2,1)S(1)}, bf16[32,2304]{1,0:T(8,128)(2,1)S(1)}, u32[]{:S(2)}, u32[]{:S(2)}) collective-permute-start(bf16[32,2304]{1,0:T(8,128)(2,1)S(1)} %get-tuple-element.43), channel_id=1, source_target_pairs={{0,4},{1,5},{4,8},{5,9},{8,12},{9,13},{12,14},{13,15},{14,10},{15,... | collective-permute-start | bytes 442376 | tf_op jit(solution)/shard_map/ppermute | solution.py:55
  29.3 1.4 %collective-permute-start.11 = (bf16[32,2304]{1,0:T(8,128)(2,1)S(1)}, bf16[32,2304]{1,0:T(8,128)(2,1)S(1)}, u32[]{:S(2)}, u32[]{:S(2)}) collective-permute-start(bf16[32,2304]{1,0:T(8,128)(2,1)S(1)} %get-tuple-element.44), channel_id=1, source_target_pairs={{0,4},{1,5},{4,8},{5,9},{8,12},{9,13},{12,14},{13,15},{14,10},{15,... | collective-permute-start | bytes 442376 | tf_op jit(solution)/shard_map/ppermute | solution.py:55
  30.7 0.6 %collective-permute-start.12 = (bf16[32,2304]{1,0:T(8,128)(2,1)S(1)}, bf16[32,2304]{1,0:T(8,128)(2,1)S(1)}, u32[]{:S(2)}, u32[]{:S(2)}) collective-permute-start(bf16[32,2304]{1,0:T(8,128)(2,1)S(1)} %get-tuple-element.45), channel_id=1, source_target_pairs={{0,2},{1,3},{4,0},{5,1},{8,4},{9,5},{12,8},{13,9},{14,12},{15,13},... | collective-permute-start | bytes 442376 | tf_op jit(solution)/shard_map/ppermute | solution.py:55
  31.4 1.0 %collective-permute-start.13 = (bf16[32,2304]{1,0:T(8,128)(2,1)S(1)}, bf16[32,2304]{1,0:T(8,128)(2,1)S(1)}, u32[]{:S(2)}, u32[]{:S(2)}) collective-permute-start(bf16[32,2304]{1,0:T(8,128)(2,1)S(1)} %get-tuple-element.46), channel_id=1, source_target_pairs={{0,2},{1,3},{4,0},{5,1},{8,4},{9,5},{12,8},{13,9},{14,12},{15,13},... | collective-permute-start | bytes 442376 | tf_op jit(solution)/shard_map/ppermute | solution.py:55
  32.3 0.8 %shard_map.69 = (f32[128,128]{1,0:T(8,128)S(1)}, bf16[128,128]{1,0:T(8,128)(2,1)S(1)}) custom-call(bf16[256,2304]{1,0:T(8,128)(2,1)S(1)} %get-tuple-element.34.refs_3_.refs_0_, bf16[128,2304]{1,0:T(8,128)(2,1)S(1)} %get-tuple-element.41.refs_1_.refs_0_, bf16[32,640]{1,0:T(8,128)(2,1)S(1)} %collective-permute-done.2.refs_5_.refs_2_, ...), custom_call_target="tpu_custom_call" | custom-call | tf_op jit(solution)/shard_map/pallas_call | solution.py:101
  33.2 1.0 %collective-permute-start.14 = (bf16[128,128]{1,0:T(8,128)(2,1)S(1)}, bf16[128,128]{1,0:T(8,128)(2,1)S(1)}, u32[]{:S(2)}, u32[]{:S(2)}) collective-permute-start(bf16[128,128]{1,0:T(8,128)(2,1)S(1)} %get-tuple-element.42.refs_4_), channel_id=1, source_target_pairs={{0,2},{1,3},{2,0},{3,1},{4,6},{5,7},{6,4},{7,5},{8,10},{9,11},{10,... | collective-permute-start | bytes 98312 | tf_op jit(solution)/shard_map/ppermute | solution.py:512
  34.2 3.5 %shard_map.70.refs_6_.refs_0_ = f32[192,2304]{1,0:T(8,128)S(1)} custom-call(bf16[256,2304]{1,0:T(8,128)(2,1)S(1)} %collective-permute-done.5.refs_6_.refs_0_, f32[96,2304]{1,0:T(8,128)S(1)} %get-tuple-element.35.refs_1_, bf16[2560,2304]{1,0:T(8,128)(2,1)S(1)} %shard_map.65.refs_4_.refs_2_.refs_1_, ...), custom_call_target="tpu_custom_call" | custom-call | flops 2038431744 | tf_op jit(solution)/shard_map/pallas_call | solution.py:101
  38.3 1.4 %collective-permute-start.16 = (bf16[64,2304]{1,0:T(8,128)(2,1)S(1)}, bf16[64,2304]{1,0:T(8,128)(2,1)S(1)}, u32[]{:S(2)}, u32[]{:S(2)}) collective-permute-start(bf16[64,2304]{1,0:T(8,128)(2,1)S(1)} %get-tuple-element.50), channel_id=1, source_target_pairs={{0,4},{1,3},{4,8},{5,1},{8,12},{9,5},{12,14},{13,9},{14,10},{15,13... | collective-permute-start | bytes 884744 | tf_op jit(solution)/shard_map/ppermute | solution.py:525
  39.7 1.7 %collective-permute-start.17 = (bf16[128,128]{1,0:T(8,128)(2,1)S(1)}, bf16[128,128]{1,0:T(8,128)(2,1)S(1)}, u32[]{:S(2)}, u32[]{:S(2)}) collective-permute-start(bf16[128,128]{1,0:T(8,128)(2,1)S(1)} %get-tuple-element.48.refs_5_), channel_id=1, source_target_pairs={{0,12},{1,13},{2,14},{3,15},{4,0},{5,1},{6,2},{7,3},{8,4},{9,5},{1... | collective-permute-start | bytes 98312 | tf_op jit(solution)/shard_map/ppermute | solution.py:521
  41.7 1.6 %collective-permute-start.19 = (bf16[128,128]{1,0:T(8,128)(2,1)S(1)}, bf16[128,128]{1,0:T(8,128)(2,1)S(1)}, u32[]{:S(2)}, u32[]{:S(2)}) collective-permute-start(bf16[128,128]{1,0:T(8,128)(2,1)S(1)} %get-tuple-element.48.refs_5_), channel_id=1, source_target_pairs={{0,4},{1,5},{2,6},{3,7},{4,8},{5,9},{6,10},{7,11},{8,12},{9,13},{1... | collective-permute-start | bytes 98312 | tf_op jit(solution)/shard_map/ppermute | solution.py:521
  43.3 2.9 %shard_map.73.refs_2_.refs_1_ = f32[128,2304]{1,0:T(8,128)S(1)} custom-call(bf16[256,2304]{1,0:T(8,128)(2,1)S(1)} %get-tuple-element.49.refs_0_, bf16[2560,2304]{1,0:T(8,128)(2,1)S(1)} %shard_map.65.refs_4_.refs_2_.refs_1_, bf16[2048,2304]{1,0:T(8,128)(2,1)S(1)} %get-tuple-element.36.refs_4_.refs_3_.refs_2_), custom_call_target="tpu_custom_call" | custom-call | flops 2717908992 | tf_op jit(solution)/shard_map/pallas_call | solution.py:101
  46.2 1.8 %collective-permute-done.18.refs_2_ = bf16[128,128]{1,0:T(8,128)(2,1)S(1)} collective-permute-done((bf16[128,128]{1,0:T(8,128)(2,1)S(1)}, bf16[128,128]{1,0:T(8,128)(2,1)S(1)}, u32[]{:S(2)}, u32[]{:S(2)}) %collective-permute-start.18) | collective-permute-done | bytes 32800 | tf_op jit(solution)/shard_map/ppermute | solution.py:521
  48.6 2.9 %shard_map.76.refs_4_.refs_1_ = f32[256,2304]{1,0:T(8,128)S(1)} custom-call(bf16[256,2304]{1,0:T(8,128)(2,1)S(1)} %collective-permute-done.15.refs_0_, f32[128,2304]{1,0:T(8,128)S(1)} %shard_map.73.refs_2_.refs_1_, bf16[2560,2304]{1,0:T(8,128)(2,1)S(1)} %shard_map.65.refs_4_.refs_2_.refs_1_, ...), custom_call_target="tpu_custom_call" | custom-call | flops 2717908992 | tf_op jit(solution)/shard_map/pallas_call | solution.py:101
  51.6 3.8 %shard_map.77.refs_2_ = f32[64,2304]{1,0:T(8,128)S(1)} custom-call(bf16[64,2304]{1,0:T(8,128)(2,1)S(1)} %shard_map.75.refs_4_.refs_0_, bf16[64,2304]{1,0:T(8,128)(2,1)S(1)} %collective-permute-done.20.refs_1_, bf16[2560,2304]{1,0:T(8,128)(2,1)S(1)} %shard_map.65.refs_4_.refs_2_.refs_1_, bf16[2048,2304]{1,0:T(8,128)(2,1)S(1)} %get-tuple-element.36.refs_4_.refs_3_.refs_2_, ...), custom_call_target="tpu_custom_call" | custom-call | flops 1358954496 | tf_op jit(solution)/shard_map/pallas_call | solution.py:101
  55.4 2.4 %shard_map.78 = bf16[512,2304]{1,0:T(8,128)(2,1)} custom-call(s32[4]{0:T(128)S(1)} %bitcast.3, s32[4]{0:T(128)S(1)} %copy-done.2, f32[192,2304]{1,0:T(8,128)S(1)} %shard_map.70.refs_6_.refs_0_, f32[256,2304]{1,0:T(8,128)S(1)} %shard_map.76.refs_4_.refs_1_, f32[64,2304]{1,0:T(8,128)S(1)} %shard_map.77.refs_2_, f32[128,128]{1,0:T(8,128)S(1)} %get-tuple-element.53.refs_3_, ...), custom_call_target="tpu_custom_call" | custom-call | flops 150994944 | bytes 2359296 | tf_op jit(solution)/shard_map/pallas_call | solution.py:416
  (41 shorter events, 2.3 us)
Async XLA Ops:
  0.0 17.7 %collective-permute-start = (bf16[32,4608]{1,0:T(8,128)(2,1)}, bf16[32,4608]{1,0:T(8,128)(2,1)S(1)}, u32[]{:S(2)}, u32[]{:S(2)}) collective-permute-start(bf16[32,4608]{1,0:T(8,128)(2,1)} %refs_0_.6), channel_id=1, source_target_pairs={{0,4},{1,5},{4,8},{5,9},{8,12},{9,13},{12,14},{13,15},{14,10},{15,... | collective-permute-start | bytes 884744 | tf_op jit(solution)/shard_map/ppermute | solution.py:55
  3.0 14.6 %collective-permute-start.1 = (bf16[32,4608]{1,0:T(8,128)(2,1)}, bf16[32,4608]{1,0:T(8,128)(2,1)S(1)}, u32[]{:S(2)}, u32[]{:S(2)}) collective-permute-start(bf16[32,4608]{1,0:T(8,128)(2,1)} %refs_0_.6), channel_id=1, source_target_pairs={{0,2},{1,3},{4,0},{5,1},{8,4},{9,5},{12,8},{13,9},{14,12},{15,13},... | collective-permute-start | bytes 884744 | tf_op jit(solution)/shard_map/ppermute | solution.py:55
  4.3 13.4 %collective-permute-start.2 = (bf16[32,640]{1,0:T(8,128)(2,1)S(1)}, bf16[32,640]{1,0:T(8,128)(2,1)S(1)}, u32[]{:S(2)}, u32[]{:S(2)}) collective-permute-start(bf16[32,640]{1,0:T(8,128)(2,1)S(1)} %get-tuple-element.31), channel_id=1, source_target_pairs={{0,10},{1,11},{4,6},{5,7},{8,2},{9,3},{12,0},{13,1},{14,4},{15,5},... | collective-permute-start | bytes 122888 | tf_op jit(solution)/shard_map/ppermute | solution.py:458
  8.3 9.3 %collective-permute-start.3 = (bf16[32,640]{1,0:T(8,128)(2,1)S(1)}, bf16[32,640]{1,0:T(8,128)(2,1)S(1)}, u32[]{:S(2)}, u32[]{:S(2)}) collective-permute-start(bf16[32,640]{1,0:T(8,128)(2,1)S(1)} %get-tuple-element.32), channel_id=1, source_target_pairs={{0,12},{1,13},{4,14},{5,15},{8,10},{9,11},{12,6},{13,7},{14,2},{15... | collective-permute-start | bytes 122888 | tf_op jit(solution)/shard_map/ppermute | solution.py:458
  8.4 9.2 %copy-start = (bf16[32,4608]{1,0:T(8,128)(2,1)S(1)}, bf16[32,4608]{1,0:T(8,128)(2,1)}, u32[]{:S(2)}) copy-start(bf16[32,4608]{1,0:T(8,128)(2,1)} %refs_0_.6) | copy-start | bytes 884740
  8.4 9.2 %collective-permute-start.4 = (bf16[32,640]{1,0:T(8,128)(2,1)S(1)}, bf16[32,640]{1,0:T(8,128)(2,1)S(1)}, u32[]{:S(2)}, u32[]{:S(2)}) collective-permute-start(bf16[32,640]{1,0:T(8,128)(2,1)S(1)} %get-tuple-element.33), channel_id=1, source_target_pairs={{0,14},{1,15},{4,10},{5,11},{8,6},{9,7},{12,2},{13,3},{14,0},{15,1... | collective-permute-start | bytes 122888 | tf_op jit(solution)/shard_map/ppermute | solution.py:458
  17.8 14.5 %collective-permute-start.5 = (bf16[256,2304]{1,0:T(8,128)(2,1)S(1)}, bf16[256,2304]{1,0:T(8,128)(2,1)S(1)}, u32[]{:S(2)}, u32[]{:S(2)}) collective-permute-start(bf16[256,2304]{1,0:T(8,128)(2,1)S(1)} %get-tuple-element.34.refs_3_.refs_0_), channel_id=1, source_target_pairs={{0,1},{1,0},{2,3},{3,2},{4,5},{5,4},{6,7},{7,6},{8,9},{9,8},{10,11... | collective-permute-start | bytes 3538952 | tf_op jit(solution)/shard_map/ppermute | solution.py:22
  17.9 9.8 %collective-permute-start.6 = (bf16[32,2304]{1,0:T(8,128)(2,1)S(1)}, bf16[32,2304]{1,0:T(8,128)(2,1)S(1)}, u32[]{:S(2)}, u32[]{:S(2)}) collective-permute-start(bf16[32,2304]{1,0:T(8,128)(2,1)S(1)} %get-tuple-element.37), channel_id=1, source_target_pairs={{0,4},{1,5},{4,8},{5,9},{8,12},{9,13},{12,14},{13,15},{14,10},{15,... | collective-permute-start | bytes 442376 | tf_op jit(solution)/shard_map/ppermute | solution.py:55
  18.0 9.8 %collective-permute-start.7 = (bf16[32,2304]{1,0:T(8,128)(2,1)S(1)}, bf16[32,2304]{1,0:T(8,128)(2,1)S(1)}, u32[]{:S(2)}, u32[]{:S(2)}) collective-permute-start(bf16[32,2304]{1,0:T(8,128)(2,1)S(1)} %get-tuple-element.38), channel_id=1, source_target_pairs={{0,4},{1,5},{4,8},{5,9},{8,12},{9,13},{12,14},{13,15},{14,10},{15,... | collective-permute-start | bytes 442376 | tf_op jit(solution)/shard_map/ppermute | solution.py:55
  19.4 8.4 %collective-permute-start.8 = (bf16[32,2304]{1,0:T(8,128)(2,1)S(1)}, bf16[32,2304]{1,0:T(8,128)(2,1)S(1)}, u32[]{:S(2)}, u32[]{:S(2)}) collective-permute-start(bf16[32,2304]{1,0:T(8,128)(2,1)S(1)} %get-tuple-element.39), channel_id=1, source_target_pairs={{0,2},{1,3},{4,0},{5,1},{8,4},{9,5},{12,8},{13,9},{14,12},{15,13},... | collective-permute-start | bytes 442376 | tf_op jit(solution)/shard_map/ppermute | solution.py:55
  20.1 8.1 %collective-permute-start.9 = (bf16[32,2304]{1,0:T(8,128)(2,1)S(1)}, bf16[32,2304]{1,0:T(8,128)(2,1)S(1)}, u32[]{:S(2)}, u32[]{:S(2)}) collective-permute-start(bf16[32,2304]{1,0:T(8,128)(2,1)S(1)} %get-tuple-element.40), channel_id=1, source_target_pairs={{0,2},{1,3},{4,0},{5,1},{8,4},{9,5},{12,8},{13,9},{14,12},{15,13},... | collective-permute-start | bytes 442376 | tf_op jit(solution)/shard_map/ppermute | solution.py:55
  28.2 4.2 %copy-start.1 = (s32[4,1]{0,1:T(1,128)S(1)}, s32[4,1]{0,1:T(1,128)}, u32[]{:S(2)}) copy-start(s32[4,1]{0,1:T(1,128)} %param.10) | copy-start | bytes 52
  28.2 9.5 %collective-permute-start.10 = (bf16[32,2304]{1,0:T(8,128)(2,1)S(1)}, bf16[32,2304]{1,0:T(8,128)(2,1)S(1)}, u32[]{:S(2)}, u32[]{:S(2)}) collective-permute-start(bf16[32,2304]{1,0:T(8,128)(2,1)S(1)} %get-tuple-element.43), channel_id=1, source_target_pairs={{0,4},{1,5},{4,8},{5,9},{8,12},{9,13},{12,14},{13,15},{14,10},{15,... | collective-permute-start | bytes 442376 | tf_op jit(solution)/shard_map/ppermute | solution.py:55
  29.3 8.4 %collective-permute-start.11 = (bf16[32,2304]{1,0:T(8,128)(2,1)S(1)}, bf16[32,2304]{1,0:T(8,128)(2,1)S(1)}, u32[]{:S(2)}, u32[]{:S(2)}) collective-permute-start(bf16[32,2304]{1,0:T(8,128)(2,1)S(1)} %get-tuple-element.44), channel_id=1, source_target_pairs={{0,4},{1,5},{4,8},{5,9},{8,12},{9,13},{12,14},{13,15},{14,10},{15,... | collective-permute-start | bytes 442376 | tf_op jit(solution)/shard_map/ppermute | solution.py:55
  30.7 7.0 %collective-permute-start.12 = (bf16[32,2304]{1,0:T(8,128)(2,1)S(1)}, bf16[32,2304]{1,0:T(8,128)(2,1)S(1)}, u32[]{:S(2)}, u32[]{:S(2)}) collective-permute-start(bf16[32,2304]{1,0:T(8,128)(2,1)S(1)} %get-tuple-element.45), channel_id=1, source_target_pairs={{0,2},{1,3},{4,0},{5,1},{8,4},{9,5},{12,8},{13,9},{14,12},{15,13},... | collective-permute-start | bytes 442376 | tf_op jit(solution)/shard_map/ppermute | solution.py:55
  31.4 6.8 %collective-permute-start.13 = (bf16[32,2304]{1,0:T(8,128)(2,1)S(1)}, bf16[32,2304]{1,0:T(8,128)(2,1)S(1)}, u32[]{:S(2)}, u32[]{:S(2)}) collective-permute-start(bf16[32,2304]{1,0:T(8,128)(2,1)S(1)} %get-tuple-element.46), channel_id=1, source_target_pairs={{0,2},{1,3},{4,0},{5,1},{8,4},{9,5},{12,8},{13,9},{14,12},{15,13},... | collective-permute-start | bytes 442376 | tf_op jit(solution)/shard_map/ppermute | solution.py:55
  33.2 4.5 %collective-permute-start.14 = (bf16[128,128]{1,0:T(8,128)(2,1)S(1)}, bf16[128,128]{1,0:T(8,128)(2,1)S(1)}, u32[]{:S(2)}, u32[]{:S(2)}) collective-permute-start(bf16[128,128]{1,0:T(8,128)(2,1)S(1)} %get-tuple-element.42.refs_4_), channel_id=1, source_target_pairs={{0,2},{1,3},{2,0},{3,1},{4,6},{5,7},{6,4},{7,5},{8,10},{9,11},{10,... | collective-permute-start | bytes 98312 | tf_op jit(solution)/shard_map/ppermute | solution.py:512
  38.2 10.4 %collective-permute-start.15 = (bf16[256,2304]{1,0:T(8,128)(2,1)S(1)}, bf16[256,2304]{1,0:T(8,128)(2,1)S(1)}, u32[]{:S(2)}, u32[]{:S(2)}) collective-permute-start(bf16[256,2304]{1,0:T(8,128)(2,1)S(1)} %get-tuple-element.49.refs_0_), channel_id=1, source_target_pairs={{0,1},{1,0},{2,3},{3,2},{4,5},{5,4},{6,7},{7,6},{8,9},{9,8},{10,11... | collective-permute-start | bytes 3538952 | tf_op jit(solution)/shard_map/ppermute | solution.py:22
  38.3 9.7 %collective-permute-start.16 = (bf16[64,2304]{1,0:T(8,128)(2,1)S(1)}, bf16[64,2304]{1,0:T(8,128)(2,1)S(1)}, u32[]{:S(2)}, u32[]{:S(2)}) collective-permute-start(bf16[64,2304]{1,0:T(8,128)(2,1)S(1)} %get-tuple-element.50), channel_id=1, source_target_pairs={{0,4},{1,3},{4,8},{5,1},{8,12},{9,5},{12,14},{13,9},{14,10},{15,13... | collective-permute-start | bytes 884744 | tf_op jit(solution)/shard_map/ppermute | solution.py:525
  39.7 6.5 %collective-permute-start.17 = (bf16[128,128]{1,0:T(8,128)(2,1)S(1)}, bf16[128,128]{1,0:T(8,128)(2,1)S(1)}, u32[]{:S(2)}, u32[]{:S(2)}) collective-permute-start(bf16[128,128]{1,0:T(8,128)(2,1)S(1)} %get-tuple-element.48.refs_5_), channel_id=1, source_target_pairs={{0,12},{1,13},{2,14},{3,15},{4,0},{5,1},{6,2},{7,3},{8,4},{9,5},{1... | collective-permute-start | bytes 98312 | tf_op jit(solution)/shard_map/ppermute | solution.py:521
  41.5 6.5 %collective-permute-start.18 = (bf16[128,128]{1,0:T(8,128)(2,1)S(1)}, bf16[128,128]{1,0:T(8,128)(2,1)S(1)}, u32[]{:S(2)}, u32[]{:S(2)}) collective-permute-start(bf16[128,128]{1,0:T(8,128)(2,1)S(1)} %get-tuple-element.48.refs_5_), channel_id=1, source_target_pairs={{0,8},{1,9},{2,10},{3,11},{4,12},{5,13},{6,14},{7,15},{8,0},{9,1},... | collective-permute-start | bytes 98312 | tf_op jit(solution)/shard_map/ppermute | solution.py:521
  41.7 6.3 %collective-permute-start.19 = (bf16[128,128]{1,0:T(8,128)(2,1)S(1)}, bf16[128,128]{1,0:T(8,128)(2,1)S(1)}, u32[]{:S(2)}, u32[]{:S(2)}) collective-permute-start(bf16[128,128]{1,0:T(8,128)(2,1)S(1)} %get-tuple-element.48.refs_5_), channel_id=1, source_target_pairs={{0,4},{1,5},{2,6},{3,7},{4,8},{5,9},{6,10},{7,11},{8,12},{9,13},{1... | collective-permute-start | bytes 98312 | tf_op jit(solution)/shard_map/ppermute | solution.py:521
  48.1 3.5 %collective-permute-start.20 = (bf16[64,2304]{1,0:T(8,128)(2,1)S(1)}, bf16[64,2304]{1,0:T(8,128)(2,1)S(1)}, u32[]{:S(2)}, u32[]{:S(2)}) collective-permute-start(bf16[64,2304]{1,0:T(8,128)(2,1)S(1)} %shard_map.75.refs_4_.refs_0_), channel_id=1, source_target_pairs={{0,1},{1,0},{2,3},{3,2},{4,5},{5,4},{6,7},{7,6},{8,9},{9,8},{10,11... | collective-permute-start | bytes 884744 | tf_op jit(solution)/shard_map/ppermute | solution.py:22
  48.2 7.2 %collective-permute-start.21 = (bf16[128,128]{1,0:T(8,128)(2,1)S(1)}, bf16[128,128]{1,0:T(8,128)(2,1)S(1)}, u32[]{:S(2)}, u32[]{:S(2)}) collective-permute-start(bf16[128,128]{1,0:T(8,128)(2,1)S(1)} %get-tuple-element.52.refs_1_), channel_id=1, source_target_pairs={{0,1},{1,0},{2,3},{3,2},{4,5},{5,4},{6,7},{7,6},{8,9},{9,8},{10,11... | collective-permute-start | bytes 98312 | tf_op jit(solution)/shard_map/ppermute | solution.py:22
  (1 other events, 3.8 us)

commit v9 on v8

--- a/solution.py
+++ b/solution.py
@@ -248,6 +248,10 @@
         base[...] += jnp.dot(columns, weight, preferred_element_type=jnp.float32)
 
 
+def full_rows(rows):
+    return max(rows, 128)
+
+
 def assemble_core(ref, chips, rows, held):
     depth = ref.shape[1]
     for i in range(chips):
@@ -262,12 +266,12 @@
     columns = tile_width(base.shape[1])
     for j in range(0, base.shape[1], columns):
         at = slice(j, j + columns)
-        base[:, at] = multiply(held, weights, at)
+        base[:, at] = multiply(held, weights, at)[: base.shape[0]]
 
 
 def both_kernel(rows, ref, mine, *refs):
     *weights, base, held = refs
-    chips = mine.shape[0] // rows
+    chips = base.shape[0] // (2 * rows)
     c = lax.axis_index("adapter")
     assemble_core(ref, chips, rows, held)
     columns = tile_width(base.shape[1])
@@ -287,7 +291,7 @@
         [ref] + ([] if mine is None else [mine]) + weights,
         after,
         [((total if mine is None else 2 * total, width), jnp.float32)],
-        [pltpu.VMEM((total, depth), jnp.bfloat16)],
+        [pltpu.VMEM((full_rows(total), depth), jnp.bfloat16)],
         limit=8 + (2 * total * depth >> 20),
         flops=2 * total * depth * width,
     )
@@ -350,7 +354,7 @@
     columns = tile_width(width)
     for j in range(0, width, columns):
         at = slice(j, j + columns)
-        base[:, at] = multiply(held, weights, at)
+        base[:, at] = multiply(held, weights, at)[: base.shape[0]]
 
 
 def base_rows(pairs, counts, rows, weights, after):
@@ -362,7 +366,7 @@
         arrays + weights,
         after,
         [((total, width), jnp.float32)],
-        [pltpu.VMEM((total, depth), jnp.bfloat16)],
+        [pltpu.VMEM((full_rows(total), depth), jnp.bfloat16)],
         limit=8 + (2 * total * depth >> 20),
         flops=2 * total * depth * width,
     )
@@ -476,10 +480,10 @@
         functools.partial(second_load_kernel, len(near), rows),
         [weight, up],
         [],
-        [((features - cut, hidden), bf16), (up.shape, bf16), ((own, hidden), jnp.float32)],
+        [((features - cut, hidden), bf16), (up.shape, bf16), ((full_rows(own), hidden), jnp.float32)],
         [
             pltpu.VMEM(up.shape, up.dtype),
-            pltpu.VMEM((own, features), bf16),
+            pltpu.VMEM((full_rows(own), features), bf16),
             pltpu.SemaphoreType.DMA((4,)),
             pltpu.SemaphoreType.DMA,
         ],

time: 58.1 us -> 56.9 us (0.979)
  Pallas kernels: 28.1 us -> 26.9 us
    pallas_call x11, Pallas kernels: 14.3 us -> 12.9 us  [call(): pl.pallas_call(body, out_shape=[pltpu.VMEM(shape, dtype) for shape, dtype...]
  transfers between devices with their start and end apart: 22 -> 22, of which waited for: 3 -> 3; matrix products, arithmetic and copies ran while one was open for 0% -> 0% of each run, Pallas kernels for 44% -> 43%
where the time goes in v9:
time: 56.9 us; the launch traced here: 56.8 us
  Pallas kernels  26.9 us (47%)
  starting transfers between devices  26.8 us (47%)
  waiting for transfers between devices  2.6 us (5%)
    pallas_call x11, Pallas kernels, call(): pl.pallas_call(body, out_shape=[pltpu.VMEM(shape, dtype) for shape, dtype...  12.9 us
    pallas_call x3, Pallas kernels, load(): pl.pallas_call(body, out_shape=[pltpu.VMEM(shape, dtype) for shape, dtype...  11.6 us
    ppermute x3, starting transfers between devices, on_device(): lax.ppermute(x, AXES, ring_perm(n, d))  8.88 us
    ppermute x5, starting transfers between devices, ring_hop(): lax.ppermute(x, AXES, ring_perm(n, 1))  6.99 us
    ppermute x5, starting transfers between devices, ring_hop(): lax.ppermute(x, AXES, ring_perm(n, -1))  4.24 us
    ppermute x3, starting transfers between devices, on_device(): lax.ppermute(rounded, AXES, z_perm(n, shift))  4.14 us
    pallas_call x1, Pallas kernels, finish(): pl.pallas_call(functools.partial(finish_kernel, n, rows, groups), out_sha...  2.41 us
    ppermute x3, waiting for transfers between devices, on_device(): lax.ppermute(rounded, AXES, z_perm(n, shift))  1.39 us
  transfers between devices with their start and end apart: 22, of which 3 were waited for; matrix products, arithmetic and copies ran while one was open for 0% of the time, Pallas kernels for 43%

profile of v9, /device:TPU:0, one launch (start us, length us, event | category | flops | bytes accessed | tf_op | source)
XLA Modules:
  0.0 56.8 jit_solution(15051407142404154231)
XLA Ops:
  0.0 3.0 %collective-permute-start = (bf16[32,4608]{1,0:T(8,128)(2,1)}, bf16[32,4608]{1,0:T(8,128)(2,1)S(1)}, u32[]{:S(2)}, u32[]{:S(2)}) collective-permute-start(bf16[32,4608]{1,0:T(8,128)(2,1)} %refs_0_.6), channel_id=1, source_target_pairs={{0,4},{1,5},{4,8},{5,9},{8,12},{9,13},{12,14},{13,15},{14,10},{15,... | collective-permute-start | bytes 884744 | tf_op jit(solution)/shard_map/ppermute | solution.py:55
  3.0 1.2 %shard_map.64 = (bf16[2,64,640]{2,1,0:T(8,128)(2,1)S(1)}, bf16[32,640]{1,0:T(8,128)(2,1)S(1)}, bf16[32,640]{1,0:T(8,128)(2,1)S(1)}, bf16[32,640]{1,0:T(8,128)(2,1)S(1)}) custom-call(bf16[32,4608]{1,0:T(8,128)(2,1)} %refs_0_.6, f32[2,64,576]{2,1,0:T(8,128)} %bitcast.4), custom_call_target="tpu_custom_call" | custom-call | bytes 256 | tf_op jit(solution)/shard_map/pallas_call | solution.py:307
  4.3 4.0 %collective-permute-start.2 = (bf16[32,640]{1,0:T(8,128)(2,1)S(1)}, bf16[32,640]{1,0:T(8,128)(2,1)S(1)}, u32[]{:S(2)}, u32[]{:S(2)}) collective-permute-start(bf16[32,640]{1,0:T(8,128)(2,1)S(1)} %get-tuple-element.31), channel_id=1, source_target_pairs={{0,10},{1,11},{4,6},{5,7},{8,2},{9,3},{12,0},{13,1},{14,4},{15,5},... | collective-permute-start | bytes 122888 | tf_op jit(solution)/shard_map/ppermute | solution.py:462
  8.4 4.7 %collective-permute-start.4 = (bf16[32,640]{1,0:T(8,128)(2,1)S(1)}, bf16[32,640]{1,0:T(8,128)(2,1)S(1)}, u32[]{:S(2)}, u32[]{:S(2)}) collective-permute-start(bf16[32,640]{1,0:T(8,128)(2,1)S(1)} %get-tuple-element.33), channel_id=1, source_target_pairs={{0,14},{1,15},{4,10},{5,11},{8,6},{9,7},{12,2},{13,3},{14,0},{15,1... | collective-permute-start | bytes 122888 | tf_op jit(solution)/shard_map/ppermute | solution.py:462
  13.1 4.5 %shard_map.65.refs_4_.refs_2_.refs_1_ = bf16[2560,2304]{1,0:T(8,128)(2,1)S(1)} custom-call(bf16[4608,2304]{1,0:T(8,128)(2,1)} %refs_0_.7), custom_call_target="tpu_custom_call" | custom-call | bytes 11796480 | tf_op jit(solution)/shard_map/pallas_call | solution.py:307
  18.0 1.4 %collective-permute-start.7 = (bf16[32,2304]{1,0:T(8,128)(2,1)S(1)}, bf16[32,2304]{1,0:T(8,128)(2,1)S(1)}, u32[]{:S(2)}, u32[]{:S(2)}) collective-permute-start(bf16[32,2304]{1,0:T(8,128)(2,1)S(1)} %get-tuple-element.38), channel_id=1, source_target_pairs={{0,4},{1,5},{4,8},{5,9},{8,12},{9,13},{12,14},{13,15},{14,10},{15,... | collective-permute-start | bytes 442376 | tf_op jit(solution)/shard_map/ppermute | solution.py:55
  19.4 0.7 %collective-permute-start.8 = (bf16[32,2304]{1,0:T(8,128)(2,1)S(1)}, bf16[32,2304]{1,0:T(8,128)(2,1)S(1)}, u32[]{:S(2)}, u32[]{:S(2)}) collective-permute-start(bf16[32,2304]{1,0:T(8,128)(2,1)S(1)} %get-tuple-element.39), channel_id=1, source_target_pairs={{0,2},{1,3},{4,0},{5,1},{8,4},{9,5},{12,8},{13,9},{14,12},{15,13},... | collective-permute-start | bytes 442376 | tf_op jit(solution)/shard_map/ppermute | solution.py:55
  20.1 1.9 %collective-permute-start.9 = (bf16[32,2304]{1,0:T(8,128)(2,1)S(1)}, bf16[32,2304]{1,0:T(8,128)(2,1)S(1)}, u32[]{:S(2)}, u32[]{:S(2)}) collective-permute-start(bf16[32,2304]{1,0:T(8,128)(2,1)S(1)} %get-tuple-element.40), channel_id=1, source_target_pairs={{0,2},{1,3},{4,0},{5,1},{8,4},{9,5},{12,8},{13,9},{14,12},{15,13},... | collective-permute-start | bytes 442376 | tf_op jit(solution)/shard_map/ppermute | solution.py:55
  22.0 5.9 %shard_map.67 = (bf16[2048,2304]{1,0:T(8,128)(2,1)S(1)}, bf16[4,64,2304]{2,1,0:T(8,128)(2,1)S(1)}, f32[128,2304]{1,0:T(8,128)S(1)}) custom-call(bf16[4608,2304]{1,0:T(8,128)(2,1)} %refs_0_.7, f32[4,64,2304]{2,1,0:T(8,128)} %refs_1_.1, bf16[2560,2304]{1,0:T(8,128)(2,1)S(1)} %shard_map.65.refs_4_.refs_2_.refs_1_, ...), custom_call_target="tpu_custom_call" | custom-call | flops 2038431744 | bytes 9437184 | tf_op jit(solution)/shard_map/pallas_call | solution.py:307
  28.2 1.1 %collective-permute-start.10 = (bf16[32,2304]{1,0:T(8,128)(2,1)S(1)}, bf16[32,2304]{1,0:T(8,128)(2,1)S(1)}, u32[]{:S(2)}, u32[]{:S(2)}) collective-permute-start(bf16[32,2304]{1,0:T(8,128)(2,1)S(1)} %get-tuple-element.43), channel_id=1, source_target_pairs={{0,4},{1,5},{4,8},{5,9},{8,12},{9,13},{12,14},{13,15},{14,10},{15,... | collective-permute-start | bytes 442376 | tf_op jit(solution)/shard_map/ppermute | solution.py:55
  29.3 1.4 %collective-permute-start.11 = (bf16[32,2304]{1,0:T(8,128)(2,1)S(1)}, bf16[32,2304]{1,0:T(8,128)(2,1)S(1)}, u32[]{:S(2)}, u32[]{:S(2)}) collective-permute-start(bf16[32,2304]{1,0:T(8,128)(2,1)S(1)} %get-tuple-element.44), channel_id=1, source_target_pairs={{0,4},{1,5},{4,8},{5,9},{8,12},{9,13},{12,14},{13,15},{14,10},{15,... | collective-permute-start | bytes 442376 | tf_op jit(solution)/shard_map/ppermute | solution.py:55
  31.4 1.0 %collective-permute-start.13 = (bf16[32,2304]{1,0:T(8,128)(2,1)S(1)}, bf16[32,2304]{1,0:T(8,128)(2,1)S(1)}, u32[]{:S(2)}, u32[]{:S(2)}) collective-permute-start(bf16[32,2304]{1,0:T(8,128)(2,1)S(1)} %get-tuple-element.46), channel_id=1, source_target_pairs={{0,2},{1,3},{4,0},{5,1},{8,4},{9,5},{12,8},{13,9},{14,12},{15,13},... | collective-permute-start | bytes 442376 | tf_op jit(solution)/shard_map/ppermute | solution.py:55
  32.3 0.8 %shard_map.69 = (f32[128,128]{1,0:T(8,128)S(1)}, bf16[128,128]{1,0:T(8,128)(2,1)S(1)}) custom-call(bf16[256,2304]{1,0:T(8,128)(2,1)S(1)} %get-tuple-element.34.refs_3_.refs_0_, bf16[128,2304]{1,0:T(8,128)(2,1)S(1)} %get-tuple-element.41.refs_1_.refs_0_, bf16[32,640]{1,0:T(8,128)(2,1)S(1)} %collective-permute-done.2.refs_5_.refs_2_, ...), custom_call_target="tpu_custom_call" | custom-call | tf_op jit(solution)/shard_map/pallas_call | solution.py:101
  33.2 1.0 %collective-permute-start.14 = (bf16[128,128]{1,0:T(8,128)(2,1)S(1)}, bf16[128,128]{1,0:T(8,128)(2,1)S(1)}, u32[]{:S(2)}, u32[]{:S(2)}) collective-permute-start(bf16[128,128]{1,0:T(8,128)(2,1)S(1)} %get-tuple-element.42.refs_4_), channel_id=1, source_target_pairs={{0,2},{1,3},{2,0},{3,1},{4,6},{5,7},{6,4},{7,5},{8,10},{9,11},{10,... | collective-permute-start | bytes 98312 | tf_op jit(solution)/shard_map/ppermute | solution.py:516
  34.2 3.0 %shard_map.70.refs_6_.refs_0_ = f32[192,2304]{1,0:T(8,128)S(1)} custom-call(bf16[256,2304]{1,0:T(8,128)(2,1)S(1)} %collective-permute-done.5.refs_6_.refs_0_, f32[128,2304]{1,0:T(8,128)S(1)} %get-tuple-element.35.refs_1_, bf16[2560,2304]{1,0:T(8,128)(2,1)S(1)} %shard_map.65.refs_4_.refs_2_.refs_1_, ...), custom_call_target="tpu_custom_call" | custom-call | flops 2038431744 | tf_op jit(solution)/shard_map/pallas_call | solution.py:101
  37.2 0.9 %collective-permute-done.13.refs_4_ = bf16[32,2304]{1,0:T(8,128)(2,1)S(1)} collective-permute-done((bf16[32,2304]{1,0:T(8,128)(2,1)S(1)}, bf16[32,2304]{1,0:T(8,128)(2,1)S(1)}, u32[]{:S(2)}, u32[]{:S(2)}) %collective-permute-start.13) | collective-permute-done | bytes 147488 | tf_op jit(solution)/shard_map/ppermute | solution.py:55
  38.3 0.9 %collective-permute-start.16 = (bf16[64,2304]{1,0:T(8,128)(2,1)S(1)}, bf16[64,2304]{1,0:T(8,128)(2,1)S(1)}, u32[]{:S(2)}, u32[]{:S(2)}) collective-permute-start(bf16[64,2304]{1,0:T(8,128)(2,1)S(1)} %get-tuple-element.50), channel_id=1, source_target_pairs={{0,4},{1,3},{4,8},{5,1},{8,12},{9,5},{12,14},{13,9},{14,10},{15,13... | collective-permute-start | bytes 884744 | tf_op jit(solution)/shard_map/ppermute | solution.py:529
  39.2 2.3 %collective-permute-start.17 = (bf16[128,128]{1,0:T(8,128)(2,1)S(1)}, bf16[128,128]{1,0:T(8,128)(2,1)S(1)}, u32[]{:S(2)}, u32[]{:S(2)}) collective-permute-start(bf16[128,128]{1,0:T(8,128)(2,1)S(1)} %get-tuple-element.48.refs_5_), channel_id=1, source_target_pairs={{0,12},{1,13},{2,14},{3,15},{4,0},{5,1},{6,2},{7,3},{8,4},{9,5},{1... | collective-permute-start | bytes 98312 | tf_op jit(solution)/shard_map/ppermute | solution.py:525
  41.5 1.8 %collective-permute-start.19 = (bf16[128,128]{1,0:T(8,128)(2,1)S(1)}, bf16[128,128]{1,0:T(8,128)(2,1)S(1)}, u32[]{:S(2)}, u32[]{:S(2)}) collective-permute-start(bf16[128,128]{1,0:T(8,128)(2,1)S(1)} %get-tuple-element.48.refs_5_), channel_id=1, source_target_pairs={{0,4},{1,5},{2,6},{3,7},{4,8},{5,9},{6,10},{7,11},{8,12},{9,13},{1... | collective-permute-start | bytes 98312 | tf_op jit(solution)/shard_map/ppermute | solution.py:525
  43.3 2.9 %shard_map.73.refs_2_.refs_1_ = f32[128,2304]{1,0:T(8,128)S(1)} custom-call(bf16[256,2304]{1,0:T(8,128)(2,1)S(1)} %get-tuple-element.49.refs_0_, bf16[2560,2304]{1,0:T(8,128)(2,1)S(1)} %shard_map.65.refs_4_.refs_2_.refs_1_, bf16[2048,2304]{1,0:T(8,128)(2,1)S(1)} %get-tuple-element.36.refs_4_.refs_3_.refs_2_), custom_call_target="tpu_custom_call" | custom-call | flops 2717908992 | tf_op jit(solution)/shard_map/pallas_call | solution.py:101
  46.2 1.4 %collective-permute-done.18.refs_2_ = bf16[128,128]{1,0:T(8,128)(2,1)S(1)} collective-permute-done((bf16[128,128]{1,0:T(8,128)(2,1)S(1)}, bf16[128,128]{1,0:T(8,128)(2,1)S(1)}, u32[]{:S(2)}, u32[]{:S(2)}) %collective-permute-start.18) | collective-permute-done | bytes 32800 | tf_op jit(solution)/shard_map/ppermute | solution.py:525
  48.3 2.9 %shard_map.76.refs_4_.refs_1_ = f32[256,2304]{1,0:T(8,128)S(1)} custom-call(bf16[256,2304]{1,0:T(8,128)(2,1)S(1)} %collective-permute-done.15.refs_0_, f32[128,2304]{1,0:T(8,128)S(1)} %shard_map.73.refs_2_.refs_1_, bf16[2560,2304]{1,0:T(8,128)(2,1)S(1)} %shard_map.65.refs_4_.refs_2_.refs_1_, ...), custom_call_target="tpu_custom_call" | custom-call | flops 2717908992 | tf_op jit(solution)/shard_map/pallas_call | solution.py:101
  51.2 2.9 %shard_map.77.refs_2_ = f32[64,2304]{1,0:T(8,128)S(1)} custom-call(bf16[64,2304]{1,0:T(8,128)(2,1)S(1)} %shard_map.75.refs_4_.refs_0_, bf16[64,2304]{1,0:T(8,128)(2,1)S(1)} %collective-permute-done.20.refs_1_, bf16[2560,2304]{1,0:T(8,128)(2,1)S(1)} %shard_map.65.refs_4_.refs_2_.refs_1_, bf16[2048,2304]{1,0:T(8,128)(2,1)S(1)} %get-tuple-element.36.refs_4_.refs_3_.refs_2_, ...), custom_call_target="tpu_custom_call" | custom-call | flops 1358954496 | tf_op jit(solution)/shard_map/pallas_call | solution.py:101
  54.2 2.4 %shard_map.78 = bf16[512,2304]{1,0:T(8,128)(2,1)} custom-call(s32[4]{0:T(128)S(1)} %bitcast.3, s32[4]{0:T(128)S(1)} %copy-done.2, f32[192,2304]{1,0:T(8,128)S(1)} %shard_map.70.refs_6_.refs_0_, f32[256,2304]{1,0:T(8,128)S(1)} %shard_map.76.refs_4_.refs_1_, f32[64,2304]{1,0:T(8,128)S(1)} %shard_map.77.refs_2_, f32[128,128]{1,0:T(8,128)S(1)} %get-tuple-element.53.refs_3_, ...), custom_call_target="tpu_custom_call" | custom-call | flops 150994944 | bytes 2359296 | tf_op jit(solution)/shard_map/pallas_call | solution.py:420
  (41 shorter events, 2.2 us)
Async XLA Ops:
  0.0 17.7 %collective-permute-start = (bf16[32,4608]{1,0:T(8,128)(2,1)}, bf16[32,4608]{1,0:T(8,128)(2,1)S(1)}, u32[]{:S(2)}, u32[]{:S(2)}) collective-permute-start(bf16[32,4608]{1,0:T(8,128)(2,1)} %refs_0_.6), channel_id=1, source_target_pairs={{0,4},{1,5},{4,8},{5,9},{8,12},{9,13},{12,14},{13,15},{14,10},{15,... | collective-permute-start | bytes 884744 | tf_op jit(solution)/shard_map/ppermute | solution.py:55
  3.0 14.6 %collective-permute-start.1 = (bf16[32,4608]{1,0:T(8,128)(2,1)}, bf16[32,4608]{1,0:T(8,128)(2,1)S(1)}, u32[]{:S(2)}, u32[]{:S(2)}) collective-permute-start(bf16[32,4608]{1,0:T(8,128)(2,1)} %refs_0_.6), channel_id=1, source_target_pairs={{0,2},{1,3},{4,0},{5,1},{8,4},{9,5},{12,8},{13,9},{14,12},{15,13},... | collective-permute-start | bytes 884744 | tf_op jit(solution)/shard_map/ppermute | solution.py:55
  4.3 13.4 %collective-permute-start.2 = (bf16[32,640]{1,0:T(8,128)(2,1)S(1)}, bf16[32,640]{1,0:T(8,128)(2,1)S(1)}, u32[]{:S(2)}, u32[]{:S(2)}) collective-permute-start(bf16[32,640]{1,0:T(8,128)(2,1)S(1)} %get-tuple-element.31), channel_id=1, source_target_pairs={{0,10},{1,11},{4,6},{5,7},{8,2},{9,3},{12,0},{13,1},{14,4},{15,5},... | collective-permute-start | bytes 122888 | tf_op jit(solution)/shard_map/ppermute | solution.py:462
  8.3 9.3 %collective-permute-start.3 = (bf16[32,640]{1,0:T(8,128)(2,1)S(1)}, bf16[32,640]{1,0:T(8,128)(2,1)S(1)}, u32[]{:S(2)}, u32[]{:S(2)}) collective-permute-start(bf16[32,640]{1,0:T(8,128)(2,1)S(1)} %get-tuple-element.32), channel_id=1, source_target_pairs={{0,12},{1,13},{4,14},{5,15},{8,10},{9,11},{12,6},{13,7},{14,2},{15... | collective-permute-start | bytes 122888 | tf_op jit(solution)/shard_map/ppermute | solution.py:462
  8.4 9.2 %copy-start = (bf16[32,4608]{1,0:T(8,128)(2,1)S(1)}, bf16[32,4608]{1,0:T(8,128)(2,1)}, u32[]{:S(2)}) copy-start(bf16[32,4608]{1,0:T(8,128)(2,1)} %refs_0_.6) | copy-start | bytes 884740
  8.4 9.2 %collective-permute-start.4 = (bf16[32,640]{1,0:T(8,128)(2,1)S(1)}, bf16[32,640]{1,0:T(8,128)(2,1)S(1)}, u32[]{:S(2)}, u32[]{:S(2)}) collective-permute-start(bf16[32,640]{1,0:T(8,128)(2,1)S(1)} %get-tuple-element.33), channel_id=1, source_target_pairs={{0,14},{1,15},{4,10},{5,11},{8,6},{9,7},{12,2},{13,3},{14,0},{15,1... | collective-permute-start | bytes 122888 | tf_op jit(solution)/shard_map/ppermute | solution.py:462
  17.8 14.5 %collective-permute-start.5 = (bf16[256,2304]{1,0:T(8,128)(2,1)S(1)}, bf16[256,2304]{1,0:T(8,128)(2,1)S(1)}, u32[]{:S(2)}, u32[]{:S(2)}) collective-permute-start(bf16[256,2304]{1,0:T(8,128)(2,1)S(1)} %get-tuple-element.34.refs_3_.refs_0_), channel_id=1, source_target_pairs={{0,1},{1,0},{2,3},{3,2},{4,5},{5,4},{6,7},{7,6},{8,9},{9,8},{10,11... | collective-permute-start | bytes 3538952 | tf_op jit(solution)/shard_map/ppermute | solution.py:22
  17.9 10.0 %collective-permute-start.6 = (bf16[32,2304]{1,0:T(8,128)(2,1)S(1)}, bf16[32,2304]{1,0:T(8,128)(2,1)S(1)}, u32[]{:S(2)}, u32[]{:S(2)}) collective-permute-start(bf16[32,2304]{1,0:T(8,128)(2,1)S(1)} %get-tuple-element.37), channel_id=1, source_target_pairs={{0,4},{1,5},{4,8},{5,9},{8,12},{9,13},{12,14},{13,15},{14,10},{15,... | collective-permute-start | bytes 442376 | tf_op jit(solution)/shard_map/ppermute | solution.py:55
  18.0 10.0 %collective-permute-start.7 = (bf16[32,2304]{1,0:T(8,128)(2,1)S(1)}, bf16[32,2304]{1,0:T(8,128)(2,1)S(1)}, u32[]{:S(2)}, u32[]{:S(2)}) collective-permute-start(bf16[32,2304]{1,0:T(8,128)(2,1)S(1)} %get-tuple-element.38), channel_id=1, source_target_pairs={{0,4},{1,5},{4,8},{5,9},{8,12},{9,13},{12,14},{13,15},{14,10},{15,... | collective-permute-start | bytes 442376 | tf_op jit(solution)/shard_map/ppermute | solution.py:55
  19.4 8.6 %collective-permute-start.8 = (bf16[32,2304]{1,0:T(8,128)(2,1)S(1)}, bf16[32,2304]{1,0:T(8,128)(2,1)S(1)}, u32[]{:S(2)}, u32[]{:S(2)}) collective-permute-start(bf16[32,2304]{1,0:T(8,128)(2,1)S(1)} %get-tuple-element.39), channel_id=1, source_target_pairs={{0,2},{1,3},{4,0},{5,1},{8,4},{9,5},{12,8},{13,9},{14,12},{15,13},... | collective-permute-start | bytes 442376 | tf_op jit(solution)/shard_map/ppermute | solution.py:55
  20.1 8.1 %collective-permute-start.9 = (bf16[32,2304]{1,0:T(8,128)(2,1)S(1)}, bf16[32,2304]{1,0:T(8,128)(2,1)S(1)}, u32[]{:S(2)}, u32[]{:S(2)}) collective-permute-start(bf16[32,2304]{1,0:T(8,128)(2,1)S(1)} %get-tuple-element.40), channel_id=1, source_target_pairs={{0,2},{1,3},{4,0},{5,1},{8,4},{9,5},{12,8},{13,9},{14,12},{15,13},... | collective-permute-start | bytes 442376 | tf_op jit(solution)/shard_map/ppermute | solution.py:55
  28.2 4.2 %copy-start.1 = (s32[4,1]{0,1:T(1,128)S(1)}, s32[4,1]{0,1:T(1,128)}, u32[]{:S(2)}) copy-start(s32[4,1]{0,1:T(1,128)} %param.10) | copy-start | bytes 52
  28.2 8.9 %collective-permute-start.10 = (bf16[32,2304]{1,0:T(8,128)(2,1)S(1)}, bf16[32,2304]{1,0:T(8,128)(2,1)S(1)}, u32[]{:S(2)}, u32[]{:S(2)}) collective-permute-start(bf16[32,2304]{1,0:T(8,128)(2,1)S(1)} %get-tuple-element.43), channel_id=1, source_target_pairs={{0,4},{1,5},{4,8},{5,9},{8,12},{9,13},{12,14},{13,15},{14,10},{15,... | collective-permute-start | bytes 442376 | tf_op jit(solution)/shard_map/ppermute | solution.py:55
  29.3 7.8 %collective-permute-start.11 = (bf16[32,2304]{1,0:T(8,128)(2,1)S(1)}, bf16[32,2304]{1,0:T(8,128)(2,1)S(1)}, u32[]{:S(2)}, u32[]{:S(2)}) collective-permute-start(bf16[32,2304]{1,0:T(8,128)(2,1)S(1)} %get-tuple-element.44), channel_id=1, source_target_pairs={{0,4},{1,5},{4,8},{5,9},{8,12},{9,13},{12,14},{13,15},{14,10},{15,... | collective-permute-start | bytes 442376 | tf_op jit(solution)/shard_map/ppermute | solution.py:55
  30.7 6.4 %collective-permute-start.12 = (bf16[32,2304]{1,0:T(8,128)(2,1)S(1)}, bf16[32,2304]{1,0:T(8,128)(2,1)S(1)}, u32[]{:S(2)}, u32[]{:S(2)}) collective-permute-start(bf16[32,2304]{1,0:T(8,128)(2,1)S(1)} %get-tuple-element.45), channel_id=1, source_target_pairs={{0,2},{1,3},{4,0},{5,1},{8,4},{9,5},{12,8},{13,9},{14,12},{15,13},... | collective-permute-start | bytes 442376 | tf_op jit(solution)/shard_map/ppermute | solution.py:55
  31.4 6.8 %collective-permute-start.13 = (bf16[32,2304]{1,0:T(8,128)(2,1)S(1)}, bf16[32,2304]{1,0:T(8,128)(2,1)S(1)}, u32[]{:S(2)}, u32[]{:S(2)}) collective-permute-start(bf16[32,2304]{1,0:T(8,128)(2,1)S(1)} %get-tuple-element.46), channel_id=1, source_target_pairs={{0,2},{1,3},{4,0},{5,1},{8,4},{9,5},{12,8},{13,9},{14,12},{15,13},... | collective-permute-start | bytes 442376 | tf_op jit(solution)/shard_map/ppermute | solution.py:55
  33.2 4.0 %collective-permute-start.14 = (bf16[128,128]{1,0:T(8,128)(2,1)S(1)}, bf16[128,128]{1,0:T(8,128)(2,1)S(1)}, u32[]{:S(2)}, u32[]{:S(2)}) collective-permute-start(bf16[128,128]{1,0:T(8,128)(2,1)S(1)} %get-tuple-element.42.refs_4_), channel_id=1, source_target_pairs={{0,2},{1,3},{2,0},{3,1},{4,6},{5,7},{6,4},{7,5},{8,10},{9,11},{10,... | collective-permute-start | bytes 98312 | tf_op jit(solution)/shard_map/ppermute | solution.py:516
  38.2 10.0 %collective-permute-start.15 = (bf16[256,2304]{1,0:T(8,128)(2,1)S(1)}, bf16[256,2304]{1,0:T(8,128)(2,1)S(1)}, u32[]{:S(2)}, u32[]{:S(2)}) collective-permute-start(bf16[256,2304]{1,0:T(8,128)(2,1)S(1)} %get-tuple-element.49.refs_0_), channel_id=1, source_target_pairs={{0,1},{1,0},{2,3},{3,2},{4,5},{5,4},{6,7},{7,6},{8,9},{9,8},{10,11... | collective-permute-start | bytes 3538952 | tf_op jit(solution)/shard_map/ppermute | solution.py:22
  38.3 9.3 %collective-permute-start.16 = (bf16[64,2304]{1,0:T(8,128)(2,1)S(1)}, bf16[64,2304]{1,0:T(8,128)(2,1)S(1)}, u32[]{:S(2)}, u32[]{:S(2)}) collective-permute-start(bf16[64,2304]{1,0:T(8,128)(2,1)S(1)} %get-tuple-element.50), channel_id=1, source_target_pairs={{0,4},{1,3},{4,8},{5,1},{8,12},{9,5},{12,14},{13,9},{14,10},{15,13... | collective-permute-start | bytes 884744 | tf_op jit(solution)/shard_map/ppermute | solution.py:529
  39.2 7.1 %collective-permute-start.17 = (bf16[128,128]{1,0:T(8,128)(2,1)S(1)}, bf16[128,128]{1,0:T(8,128)(2,1)S(1)}, u32[]{:S(2)}, u32[]{:S(2)}) collective-permute-start(bf16[128,128]{1,0:T(8,128)(2,1)S(1)} %get-tuple-element.48.refs_5_), channel_id=1, source_target_pairs={{0,12},{1,13},{2,14},{3,15},{4,0},{5,1},{6,2},{7,3},{8,4},{9,5},{1... | collective-permute-start | bytes 98312 | tf_op jit(solution)/shard_map/ppermute | solution.py:525
  41.5 6.1 %collective-permute-start.18 = (bf16[128,128]{1,0:T(8,128)(2,1)S(1)}, bf16[128,128]{1,0:T(8,128)(2,1)S(1)}, u32[]{:S(2)}, u32[]{:S(2)}) collective-permute-start(bf16[128,128]{1,0:T(8,128)(2,1)S(1)} %get-tuple-element.48.refs_5_), channel_id=1, source_target_pairs={{0,8},{1,9},{2,10},{3,11},{4,12},{5,13},{6,14},{7,15},{8,0},{9,1},... | collective-permute-start | bytes 98312 | tf_op jit(solution)/shard_map/ppermute | solution.py:525
  41.5 6.1 %collective-permute-start.19 = (bf16[128,128]{1,0:T(8,128)(2,1)S(1)}, bf16[128,128]{1,0:T(8,128)(2,1)S(1)}, u32[]{:S(2)}, u32[]{:S(2)}) collective-permute-start(bf16[128,128]{1,0:T(8,128)(2,1)S(1)} %get-tuple-element.48.refs_5_), channel_id=1, source_target_pairs={{0,4},{1,5},{2,6},{3,7},{4,8},{5,9},{6,10},{7,11},{8,12},{9,13},{1... | collective-permute-start | bytes 98312 | tf_op jit(solution)/shard_map/ppermute | solution.py:525
  47.7 3.5 %collective-permute-start.20 = (bf16[64,2304]{1,0:T(8,128)(2,1)S(1)}, bf16[64,2304]{1,0:T(8,128)(2,1)S(1)}, u32[]{:S(2)}, u32[]{:S(2)}) collective-permute-start(bf16[64,2304]{1,0:T(8,128)(2,1)S(1)} %shard_map.75.refs_4_.refs_0_), channel_id=1, source_target_pairs={{0,1},{1,0},{2,3},{3,2},{4,5},{5,4},{6,7},{7,6},{8,9},{9,8},{10,11... | collective-permute-start | bytes 884744 | tf_op jit(solution)/shard_map/ppermute | solution.py:22
  47.8 6.4 %collective-permute-start.21 = (bf16[128,128]{1,0:T(8,128)(2,1)S(1)}, bf16[128,128]{1,0:T(8,128)(2,1)S(1)}, u32[]{:S(2)}, u32[]{:S(2)}) collective-permute-start(bf16[128,128]{1,0:T(8,128)(2,1)S(1)} %get-tuple-element.52.refs_1_), channel_id=1, source_target_pairs={{0,1},{1,0},{2,3},{3,2},{4,5},{5,4},{6,7},{7,6},{8,9},{9,8},{10,11... | collective-permute-start | bytes 98312 | tf_op jit(solution)/shard_map/ppermute | solution.py:22
  (1 other events, 3.0 us)

commit v10 on v9

--- a/solution.py
+++ b/solution.py
@@ -56,16 +56,13 @@
 
 
 def join_kernel(ways, *refs):
-    count = len(refs) - 1 - (2 * CHUNKS if ways == 2 else ways)
+    count = len(refs) - 1 - ways
     pieces, out, on = refs[:count], refs[count], refs[count + 1 :]
     first = 0
     for piece in pieces:
         out[first : first + piece.shape[0], :] = piece[...]
         first += piece.shape[0]
     arrived = pieces[len(pieces) - 2 * CHUNKS :]
-    if ways == 2:
-        for piece, ref in zip(arrived, on):
-            ref[...] = piece[...]
     if ways == 1:
         c = lax.axis_index("adapter")
         rows = arrived[0].shape[0]
@@ -79,7 +76,7 @@
 
 def join(pieces, after, ways=0):
     (rows, depth), dtype = pieces[-1].shape, pieces[-1].dtype
-    on = {0: [], 1: [CHUNKS * rows], 2: [rows] * 2 * CHUNKS}[ways]
+    on = [CHUNKS * rows] * ways
     outs = [((count, depth), dtype) for count in [sum(x.shape[0] for x in pieces), *on]]
     return call(functools.partial(join_kernel, ways), pieces, after, outs)
 
@@ -191,17 +188,6 @@
     rounded[...] = value.astype(jnp.bfloat16)
 
 
-def weight_copies(first, w_ref, w_out, sems):
-    parts = sems.shape[0]
-    depth = w_out.shape[0] // parts
-    return [
-        pltpu.make_async_copy(
-            w_ref.at[pl.ds(first + k * depth, depth), :], w_out.at[pl.ds(k * depth, depth), :], sems.at[k]
-        )
-        for k in range(parts)
-    ]
-
-
 def prepare_kernel(n, window, distances, tokens_ref, down_ref, factor, *refs):
     *sends, tokens, down, sems = refs
     copies = [
@@ -221,33 +207,6 @@
         factor[index] = pltpu.roll(wide, window.shift(lax.axis_index("seq")), 1).astype(jnp.bfloat16)
 
 
-def first_load_kernel(w_ref, w_out, sems):
-    copies = weight_copies(0, w_ref, w_out, sems)
-    for copy in copies:
-        copy.start()
-    for copy in copies:
-        copy.wait()
-
-
-def second_load_kernel(chips, rows, w_ref, up_ref, first_w, near, w_out, up_out, base, up, held, sems, up_sem):
-    first, parts = first_w.shape[0], sems.shape[0]
-    copies = weight_copies(first, w_ref, w_out, sems)
-    up_copy = pltpu.make_async_copy(up_ref, up, up_sem)
-    up_copy.start()
-    for copy in copies:
-        copy.start()
-    assemble_core(near, chips, rows, held)
-    base[...] = jnp.dot(held[:, :first], first_w[...], preferred_element_type=jnp.float32)
-    up_copy.wait()
-    up_out[...] = up[...].astype(jnp.bfloat16)
-    deep = w_out.shape[0] // parts
-    for k, copy in enumerate(copies):
-        copy.wait()
-        columns = held[:, first + k * deep : first + (k + 1) * deep]
-        weight = w_out[k * deep : (k + 1) * deep, :]
-        base[...] += jnp.dot(columns, weight, preferred_element_type=jnp.float32)
-
-
 def full_rows(rows):
     return max(rows, 128)
 
@@ -298,25 +257,29 @@
     return base
 
 
-def load(kernel, arrays, after, outs, scratch, inside=(), flops=0):
-    operands = len(arrays) + len(inside)
+def cast_kernel(source, out):
+    out[...] = source[...].astype(out.dtype)
+
+
+def in_hbm(arrays):
+    return [pltpu.with_memory_space_constraint(x, pltpu.HBM) for x in arrays]
+
+
+def prepare(kernel, arrays, later, outs, scratch):
+    operands = len(arrays)
 
     def body(*refs):
-        kernel(*refs[:operands], *refs[operands + len(after) :])
+        kernel(*refs[:operands], *refs[operands + len(later) :])
 
     return pl.pallas_call(
         body,
         out_shape=[pltpu.VMEM(shape, dtype) for shape, dtype in outs],
-        in_specs=[pl.BlockSpec(memory_space=pltpu.HBM)] * len(arrays)
-        + whole(len(inside))
-        + [pl.BlockSpec(memory_space=pl.ANY)] * len(after),
+        in_specs=[pl.BlockSpec(memory_space=pltpu.HBM)] * (operands + len(later)),
         out_specs=whole(len(outs)),
         scratch_shapes=scratch,
         compiler_params=pltpu.CompilerParams(vmem_limit_bytes=8 << 20),
-        cost_estimate=pl.CostEstimate(
-            flops=flops, bytes_accessed=2 * outs[0][0][0] * outs[0][0][1], transcendentals=0
-        ),
-    )(*(pltpu.with_memory_space_constraint(x, pltpu.HBM) for x in arrays), *in_vmem(inside), *after)
+        cost_estimate=pl.CostEstimate(flops=0, bytes_accessed=0, transcendentals=0),
+    )(*in_hbm(arrays), *in_hbm(later))
 
 
 def assemble(pairs, counts, rows, held):
@@ -448,10 +411,10 @@
     (behind,), (ahead,) = ring_hop([tokens], [tokens], n)
     ends = far + [last]
     bf16 = jnp.bfloat16
-    factor, *sends = load(
+    factor, *sends = prepare(
         functools.partial(prepare_kernel, n, window, ends),
         [tokens, jnp.swapaxes(down, 1, 2)],
-        [],
+        [weight, up],
         [((held, rank, window.size), bf16)] + [((rows, window.size), bf16)] * len(ends),
         [
             pltpu.VMEM(tokens.shape, tokens.dtype),
@@ -461,42 +424,24 @@
     )
     received = [lax.ppermute(x, AXES, ring_perm(n, d)) for d, x in zip(ends, sends)]
     come_from = [-d for d in far] + [last]
-    cut, hidden = features * 3 // 5 // 256 * 256, weight.shape[1]
-    (first_weight,) = load(
-        first_load_kernel, [weight], [], [((cut, hidden), bf16)], [pltpu.SemaphoreType.DMA((4,))]
-    )
     piece = ((rows, depth), bf16)
     near_rows, *chunks = call(
         near_kernel,
         [tokens, behind, ahead, factor],
-        [first_weight, *received],
+        received,
         [((len(near) * CHUNKS * rows + rank, depth), bf16)] + [piece] * (2 * CHUNKS),
     )
 
     up_way, down_way = chunks[:CHUNKS], chunks[CHUNKS:]
+    weights = [weight]
     near_swapped = swap_cores(near_rows, n)
-    own = len(near) * rows
-    other_weight, up, mine = load(
-        functools.partial(second_load_kernel, len(near), rows),
-        [weight, up],
-        [],
-        [((features - cut, hidden), bf16), (up.shape, bf16), ((full_rows(own), hidden), jnp.float32)],
-        [
-            pltpu.VMEM(up.shape, up.dtype),
-            pltpu.VMEM((full_rows(own), features), bf16),
-            pltpu.SemaphoreType.DMA((4,)),
-            pltpu.SemaphoreType.DMA,
-        ],
-        [first_weight, near_rows],
-        2 * own * features * hidden,
-    )
-    weights = [first_weight, other_weight]
+    mine = core_rows(near_rows, len(near), rows, weights, [])
+    (up,) = call(cast_kernel, [up], [mine], [(up.shape, bf16)])
     arrived = []
     for _ in range(2, last - 1):
         up_way, down_way = ring_hop(up_way, down_way, n)
         arrived += up_way + down_way
-    mid_rows, *chunks = join(arrived, [other_weight], 2)
-    up_way, down_way = chunks[:CHUNKS], chunks[CHUNKS:]
+    (mid_rows,) = join(arrived, [mine, up])
 
     total, rounded = call(
         functools.partial(partial_kernel, n, window, [near, mid], come_from),

time: 56.9 us -> 55.2 us (0.970)
  Pallas kernels: 26.9 us -> 19.7 us
  waiting for transfers between devices: 2.6 us -> 7.54 us
  starting transfers between devices: 26.8 us -> 27.4 us
    pallas_call x3 -> x1, Pallas kernels: 11.6 us -> 1.38 us  [prepare(): pl.pallas_call(body, out_shape=[pltpu.VMEM(shape, dtype) for shape, dtype...]
    ppermute x3, waiting for transfers between devices: 0.01 us -> 4.33 us  [on_device(): lax.ppermute(x, AXES, ring_perm(n, d))]
    ppermute x5, starting transfers between devices: 6.99 us -> 3.42 us  [ring_hop(): lax.ppermute(x, AXES, ring_perm(n, 1))]
    pallas_call x11 -> x13, Pallas kernels: 12.9 us -> 15.9 us  [call(): pl.pallas_call(body, out_shape=[pltpu.VMEM(shape, dtype) for shape, dtype...]
    ppermute x5, starting transfers between devices: 4.24 us -> 7.04 us  [ring_hop(): lax.ppermute(x, AXES, ring_perm(n, -1))]
    ppermute x3, starting transfers between devices: 4.14 us -> 5.91 us  [on_device(): lax.ppermute(rounded, AXES, z_perm(n, shift))]
    ppermute x3, waiting for transfers between devices: 1.39 us -> 0.01 us  [on_device(): lax.ppermute(rounded, AXES, z_perm(n, shift))]
    ppermute x5, waiting for transfers between devices: 0.01 us -> 1.35 us  [ring_hop(): lax.ppermute(x, AXES, ring_perm(n, 1))]
  transfers between devices with their start and end apart: 22 -> 22, of which waited for: 3 -> 5; matrix products, arithmetic and copies ran while one was open for 0% -> 0% of each run, Pallas kernels for 43% -> 31%
where the time goes in v10:
time: 55.2 us; the launch traced here: 55.1 us
  starting transfers between devices  27.4 us (50%)
  Pallas kernels  19.7 us (36%)
  waiting for transfers between devices  7.54 us (14%)
    pallas_call x13, Pallas kernels, call(): pl.pallas_call(body, out_shape=[pltpu.VMEM(shape, dtype) for shape, dtype...  15.9 us
    ppermute x3, starting transfers between devices, on_device(): lax.ppermute(x, AXES, ring_perm(n, d))  8.88 us
    ppermute x5, starting transfers between devices, ring_hop(): lax.ppermute(x, AXES, ring_perm(n, -1))  7.04 us
    ppermute x3, starting transfers between devices, on_device(): lax.ppermute(rounded, AXES, z_perm(n, shift))  5.91 us
    ppermute x3, waiting for transfers between devices, on_device(): lax.ppermute(x, AXES, ring_perm(n, d))  4.33 us
    ppermute x5, starting transfers between devices, ring_hop(): lax.ppermute(x, AXES, ring_perm(n, 1))  3.42 us
    pallas_call x1, Pallas kernels, finish(): pl.pallas_call(functools.partial(finish_kernel, n, rows, groups), out_sha...  2.41 us
    pallas_call x1, Pallas kernels, prepare(): pl.pallas_call(body, out_shape=[pltpu.VMEM(shape, dtype) for shape, dtype...  1.38 us
  transfers between devices with their start and end apart: 22, of which 5 were waited for; matrix products, arithmetic and copies ran while one was open for 0% of the time, Pallas kernels for 31%

profile of v10, /device:TPU:0, one launch (start us, length us, event | category | flops | bytes accessed | tf_op | source)
XLA Modules:
  0.0 55.1 jit_solution(17833992977019191406)
XLA Ops:
  0.0 3.0 %collective-permute-start.1 = (bf16[32,4608]{1,0:T(8,128)(2,1)}, bf16[32,4608]{1,0:T(8,128)(2,1)S(1)}, u32[]{:S(2)}, u32[]{:S(2)}) collective-permute-start(bf16[32,4608]{1,0:T(8,128)(2,1)} %refs_0_.4), channel_id=1, source_target_pairs={{0,2},{1,3},{4,0},{5,1},{8,4},{9,5},{12,8},{13,9},{14,12},{15,13},... | collective-permute-start | bytes 884744 | tf_op jit(solution)/shard_map/ppermute | solution.py:55
  3.0 1.4 %shard_map.64 = (bf16[2,64,640]{2,1,0:T(8,128)(2,1)S(1)}, bf16[32,640]{1,0:T(8,128)(2,1)S(1)}, bf16[32,640]{1,0:T(8,128)(2,1)S(1)}, bf16[32,640]{1,0:T(8,128)(2,1)S(1)}) custom-call(bf16[32,4608]{1,0:T(8,128)(2,1)} %refs_0_.4, f32[2,64,576]{2,1,0:T(8,128)} %bitcast.4, bf16[4608,2304]{1,0:T(8,128)(2,1)} %refs_2_.7, f32[4,64,2304]{2,1,0:T(8,128)} %refs_0_.5), custom_call_target="tpu_custom_call" | custom-call | tf_op jit(solution)/shard_map/pallas_call | solution.py:274
  4.4 4.0 %collective-permute-start.2 = (bf16[32,640]{1,0:T(8,128)(2,1)S(1)}, bf16[32,640]{1,0:T(8,128)(2,1)S(1)}, u32[]{:S(2)}, u32[]{:S(2)}) collective-permute-start(bf16[32,640]{1,0:T(8,128)(2,1)S(1)} %get-tuple-element.23), channel_id=1, source_target_pairs={{0,10},{1,11},{4,6},{5,7},{8,2},{9,3},{12,0},{13,1},{14,4},{15,5},... | collective-permute-start | bytes 122888 | tf_op jit(solution)/shard_map/ppermute | solution.py:425
  8.6 4.7 %collective-permute-start.4 = (bf16[32,640]{1,0:T(8,128)(2,1)S(1)}, bf16[32,640]{1,0:T(8,128)(2,1)S(1)}, u32[]{:S(2)}, u32[]{:S(2)}) collective-permute-start(bf16[32,640]{1,0:T(8,128)(2,1)S(1)} %get-tuple-element.25), channel_id=1, source_target_pairs={{0,14},{1,15},{4,10},{5,11},{8,6},{9,7},{12,2},{13,3},{14,0},{15,1... | collective-permute-start | bytes 122888 | tf_op jit(solution)/shard_map/ppermute | solution.py:425
  13.3 1.0 %collective-permute-done.2.refs_4_.refs_2_ = bf16[32,640]{1,0:T(8,128)(2,1)S(1)} collective-permute-done((bf16[32,640]{1,0:T(8,128)(2,1)S(1)}, bf16[32,640]{1,0:T(8,128)(2,1)S(1)}, u32[]{:S(2)}, u32[]{:S(2)}) %collective-permute-start.2) | collective-permute-done | bytes 40992 | tf_op jit(solution)/shard_map/ppermute | solution.py:425
  14.3 3.3 %collective-permute-done.3.refs_5_.refs_3_ = bf16[32,640]{1,0:T(8,128)(2,1)S(1)} collective-permute-done((bf16[32,640]{1,0:T(8,128)(2,1)S(1)}, bf16[32,640]{1,0:T(8,128)(2,1)S(1)}, u32[]{:S(2)}, u32[]{:S(2)}) %collective-permute-start.3) | collective-permute-done | bytes 40992 | tf_op jit(solution)/shard_map/ppermute | solution.py:425
  17.9 1.0 %collective-permute-start.6 = (bf16[32,2304]{1,0:T(8,128)(2,1)S(1)}, bf16[32,2304]{1,0:T(8,128)(2,1)S(1)}, u32[]{:S(2)}, u32[]{:S(2)}) collective-permute-start(bf16[32,2304]{1,0:T(8,128)(2,1)S(1)} %get-tuple-element.27), channel_id=1, source_target_pairs={{0,4},{1,5},{4,8},{5,9},{8,12},{9,13},{12,14},{13,15},{14,10},{15,... | collective-permute-start | bytes 442376 | tf_op jit(solution)/shard_map/ppermute | solution.py:55
  19.2 1.7 %collective-permute-start.8 = (bf16[32,2304]{1,0:T(8,128)(2,1)S(1)}, bf16[32,2304]{1,0:T(8,128)(2,1)S(1)}, u32[]{:S(2)}, u32[]{:S(2)}) collective-permute-start(bf16[32,2304]{1,0:T(8,128)(2,1)S(1)} %get-tuple-element.29), channel_id=1, source_target_pairs={{0,2},{1,3},{4,0},{5,1},{8,4},{9,5},{12,8},{13,9},{14,12},{15,13},... | collective-permute-start | bytes 442376 | tf_op jit(solution)/shard_map/ppermute | solution.py:55
  20.9 1.0 %collective-permute-start.9 = (bf16[32,2304]{1,0:T(8,128)(2,1)S(1)}, bf16[32,2304]{1,0:T(8,128)(2,1)S(1)}, u32[]{:S(2)}, u32[]{:S(2)}) collective-permute-start(bf16[32,2304]{1,0:T(8,128)(2,1)S(1)} %get-tuple-element.30), channel_id=1, source_target_pairs={{0,2},{1,3},{4,0},{5,1},{8,4},{9,5},{12,8},{13,9},{14,12},{15,13},... | collective-permute-start | bytes 442376 | tf_op jit(solution)/shard_map/ppermute | solution.py:55
  22.0 2.9 %shard_map.66.refs_1_.refs_4_ = f32[96,2304]{1,0:T(8,128)S(1)} custom-call(bf16[256,2304]{1,0:T(8,128)(2,1)S(1)} %get-tuple-element.26.refs_0_, bf16[4608,2304]{1,0:T(8,128)(2,1)S(1)} %copy-done), custom_call_target="tpu_custom_call" | custom-call | flops 2038431744 | tf_op jit(solution)/shard_map/pallas_call | solution.py:98
  25.1 1.0 %collective-permute-start.10 = (bf16[32,2304]{1,0:T(8,128)(2,1)S(1)}, bf16[32,2304]{1,0:T(8,128)(2,1)S(1)}, u32[]{:S(2)}, u32[]{:S(2)}) collective-permute-start(bf16[32,2304]{1,0:T(8,128)(2,1)S(1)} %collective-permute-done.6.refs_0_), channel_id=1, source_target_pairs={{0,4},{1,5},{4,8},{5,9},{8,12},{9,13},{12,14},{13,15},{14,10},{15,... | collective-permute-start | bytes 442376 | tf_op jit(solution)/shard_map/ppermute | solution.py:55
  26.1 1.3 %collective-permute-done.7.refs_1_ = bf16[32,2304]{1,0:T(8,128)(2,1)S(1)} collective-permute-done((bf16[32,2304]{1,0:T(8,128)(2,1)S(1)}, bf16[32,2304]{1,0:T(8,128)(2,1)S(1)}, u32[]{:S(2)}, u32[]{:S(2)}) %collective-permute-start.7) | collective-permute-done | bytes 147488 | tf_op jit(solution)/shard_map/ppermute | solution.py:55
  27.4 1.0 %collective-permute-start.11 = (bf16[32,2304]{1,0:T(8,128)(2,1)S(1)}, bf16[32,2304]{1,0:T(8,128)(2,1)S(1)}, u32[]{:S(2)}, u32[]{:S(2)}) collective-permute-start(bf16[32,2304]{1,0:T(8,128)(2,1)S(1)} %collective-permute-done.7.refs_1_), channel_id=1, source_target_pairs={{0,4},{1,5},{4,8},{5,9},{8,12},{9,13},{12,14},{13,15},{14,10},{15,... | collective-permute-start | bytes 442376 | tf_op jit(solution)/shard_map/ppermute | solution.py:55
  28.4 1.0 %collective-permute-start.12 = (bf16[32,2304]{1,0:T(8,128)(2,1)S(1)}, bf16[32,2304]{1,0:T(8,128)(2,1)S(1)}, u32[]{:S(2)}, u32[]{:S(2)}) collective-permute-start(bf16[32,2304]{1,0:T(8,128)(2,1)S(1)} %collective-permute-done.8.refs_2_), channel_id=1, source_target_pairs={{0,2},{1,3},{4,0},{5,1},{8,4},{9,5},{12,8},{13,9},{14,12},{15,13},... | collective-permute-start | bytes 442376 | tf_op jit(solution)/shard_map/ppermute | solution.py:55
  30.6 1.1 %collective-permute-start.14 = (bf16[128,128]{1,0:T(8,128)(2,1)S(1)}, bf16[128,128]{1,0:T(8,128)(2,1)S(1)}, u32[]{:S(2)}, u32[]{:S(2)}) collective-permute-start(bf16[128,128]{1,0:T(8,128)(2,1)S(1)} %get-tuple-element.31.refs_3_), channel_id=1, source_target_pairs={{0,2},{1,3},{2,0},{3,1},{4,6},{5,7},{6,4},{7,5},{8,10},{9,11},{10,... | collective-permute-start | bytes 98312 | tf_op jit(solution)/shard_map/ppermute | solution.py:461
  31.7 3.0 %shard_map.70.refs_6_.refs_0_ = f32[192,2304]{1,0:T(8,128)S(1)} custom-call(bf16[256,2304]{1,0:T(8,128)(2,1)S(1)} %collective-permute-done.5.refs_6_.refs_0_, f32[96,2304]{1,0:T(8,128)S(1)} %shard_map.66.refs_1_.refs_4_, bf16[4608,2304]{1,0:T(8,128)(2,1)S(1)} %copy-done, bf16[128,128]{1,0:T(8,128)(2,1)S(1)} %get-tuple-element.31.refs_3_), custom_call_target="tpu_custom_call" | custom-call | flops 2038431744 | tf_op jit(solution)/shard_map/pallas_call | solution.py:98
  34.7 1.1 %collective-permute-done.14.refs_1_ = bf16[128,128]{1,0:T(8,128)(2,1)S(1)} collective-permute-done((bf16[128,128]{1,0:T(8,128)(2,1)S(1)}, bf16[128,128]{1,0:T(8,128)(2,1)S(1)}, u32[]{:S(2)}, u32[]{:S(2)}) %collective-permute-start.14) | collective-permute-done | bytes 32800 | tf_op jit(solution)/shard_map/ppermute | solution.py:461
  37.1 1.4 %collective-permute-start.19 = (bf16[128,128]{1,0:T(8,128)(2,1)S(1)}, bf16[128,128]{1,0:T(8,128)(2,1)S(1)}, u32[]{:S(2)}, u32[]{:S(2)}) collective-permute-start(bf16[128,128]{1,0:T(8,128)(2,1)S(1)} %get-tuple-element.33.refs_5_), channel_id=1, source_target_pairs={{0,4},{1,5},{2,6},{3,7},{4,8},{5,9},{6,10},{7,11},{8,12},{9,13},{1... | collective-permute-start | bytes 98312 | tf_op jit(solution)/shard_map/ppermute | solution.py:470
  38.4 1.7 %collective-permute-start.18 = (bf16[128,128]{1,0:T(8,128)(2,1)S(1)}, bf16[128,128]{1,0:T(8,128)(2,1)S(1)}, u32[]{:S(2)}, u32[]{:S(2)}) collective-permute-start(bf16[128,128]{1,0:T(8,128)(2,1)S(1)} %get-tuple-element.33.refs_5_), channel_id=1, source_target_pairs={{0,8},{1,9},{2,10},{3,11},{4,12},{5,13},{6,14},{7,15},{8,0},{9,1},... | collective-permute-start | bytes 98312 | tf_op jit(solution)/shard_map/ppermute | solution.py:470
  40.1 2.8 %collective-permute-start.17 = (bf16[128,128]{1,0:T(8,128)(2,1)S(1)}, bf16[128,128]{1,0:T(8,128)(2,1)S(1)}, u32[]{:S(2)}, u32[]{:S(2)}) collective-permute-start(bf16[128,128]{1,0:T(8,128)(2,1)S(1)} %get-tuple-element.33.refs_5_), channel_id=1, source_target_pairs={{0,12},{1,13},{2,14},{3,15},{4,0},{5,1},{6,2},{7,3},{8,4},{9,5},{1... | collective-permute-start | bytes 98312 | tf_op jit(solution)/shard_map/ppermute | solution.py:470
  43.0 2.9 %shard_map.73.refs_2_.refs_1_ = f32[128,2304]{1,0:T(8,128)S(1)} custom-call(bf16[256,2304]{1,0:T(8,128)(2,1)S(1)} %get-tuple-element.34.refs_0_, bf16[4608,2304]{1,0:T(8,128)(2,1)S(1)} %copy-done), custom_call_target="tpu_custom_call" | custom-call | flops 2717908992 | tf_op jit(solution)/shard_map/pallas_call | solution.py:98
  46.6 2.9 %shard_map.76.refs_3_.refs_1_ = f32[256,2304]{1,0:T(8,128)S(1)} custom-call(bf16[256,2304]{1,0:T(8,128)(2,1)S(1)} %collective-permute-done.15.refs_0_, f32[128,2304]{1,0:T(8,128)S(1)} %shard_map.73.refs_2_.refs_1_, bf16[4608,2304]{1,0:T(8,128)(2,1)S(1)} %copy-done, bf16[64,2304]{1,0:T(8,128)(2,1)S(1)} %shard_map.75.refs_3_.refs_0_), custom_call_target="tpu_custom_call" | custom-call | flops 2717908992 | tf_op jit(solution)/shard_map/pallas_call | solution.py:98
  49.5 3.0 %shard_map.77.refs_2_ = f32[64,2304]{1,0:T(8,128)S(1)} custom-call(bf16[64,2304]{1,0:T(8,128)(2,1)S(1)} %shard_map.75.refs_3_.refs_0_, bf16[64,2304]{1,0:T(8,128)(2,1)S(1)} %collective-permute-done.20.refs_1_, bf16[4608,2304]{1,0:T(8,128)(2,1)S(1)} %copy-done, f32[256,2304]{1,0:T(8,128)S(1)} %shard_map.76.refs_3_.refs_1_), custom_call_target="tpu_custom_call" | custom-call | flops 1358954496 | tf_op jit(solution)/shard_map/pallas_call | solution.py:98
  52.5 2.4 %shard_map.78 = bf16[512,2304]{1,0:T(8,128)(2,1)} custom-call(s32[4]{0:T(128)S(1)} %bitcast.3, s32[4]{0:T(128)S(1)} %copy-done.4, f32[192,2304]{1,0:T(8,128)S(1)} %shard_map.70.refs_6_.refs_0_, f32[256,2304]{1,0:T(8,128)S(1)} %shard_map.76.refs_3_.refs_1_, f32[64,2304]{1,0:T(8,128)S(1)} %shard_map.77.refs_2_, f32[128,128]{1,0:T(8,128)S(1)} %get-tuple-element.38.refs_3_, ...), custom_call_target="tpu_custom_call" | custom-call | flops 150994944 | bytes 2359296 | tf_op jit(solution)/shard_map/pallas_call | solution.py:383
  (45 shorter events, 3.8 us)
Async XLA Ops:
  0.0 17.6 %collective-permute-start.1 = (bf16[32,4608]{1,0:T(8,128)(2,1)}, bf16[32,4608]{1,0:T(8,128)(2,1)S(1)}, u32[]{:S(2)}, u32[]{:S(2)}) collective-permute-start(bf16[32,4608]{1,0:T(8,128)(2,1)} %refs_0_.4), channel_id=1, source_target_pairs={{0,2},{1,3},{4,0},{5,1},{8,4},{9,5},{12,8},{13,9},{14,12},{15,13},... | collective-permute-start | bytes 884744 | tf_op jit(solution)/shard_map/ppermute | solution.py:55
  3.0 14.7 %collective-permute-start = (bf16[32,4608]{1,0:T(8,128)(2,1)}, bf16[32,4608]{1,0:T(8,128)(2,1)S(1)}, u32[]{:S(2)}, u32[]{:S(2)}) collective-permute-start(bf16[32,4608]{1,0:T(8,128)(2,1)} %refs_0_.4), channel_id=1, source_target_pairs={{0,4},{1,5},{4,8},{5,9},{8,12},{9,13},{12,14},{13,15},{14,10},{15,... | collective-permute-start | bytes 884744 | tf_op jit(solution)/shard_map/ppermute | solution.py:55
  3.0 14.6 %copy-start.2 = (bf16[32,4608]{1,0:T(8,128)(2,1)S(1)}, bf16[32,4608]{1,0:T(8,128)(2,1)}, u32[]{:S(2)}) copy-start(bf16[32,4608]{1,0:T(8,128)(2,1)} %refs_0_.4) | copy-start | bytes 884740
  3.0 18.9 %copy-start = (bf16[4608,2304]{1,0:T(8,128)(2,1)S(1)}, bf16[4608,2304]{1,0:T(8,128)(2,1)}, u32[]{:S(2)}) copy-start(bf16[4608,2304]{1,0:T(8,128)(2,1)} %refs_2_.7) | copy-start | bytes 63700996
  4.4 9.9 %collective-permute-start.2 = (bf16[32,640]{1,0:T(8,128)(2,1)S(1)}, bf16[32,640]{1,0:T(8,128)(2,1)S(1)}, u32[]{:S(2)}, u32[]{:S(2)}) collective-permute-start(bf16[32,640]{1,0:T(8,128)(2,1)S(1)} %get-tuple-element.23), channel_id=1, source_target_pairs={{0,10},{1,11},{4,6},{5,7},{8,2},{9,3},{12,0},{13,1},{14,4},{15,5},... | collective-permute-start | bytes 122888 | tf_op jit(solution)/shard_map/ppermute | solution.py:425
  8.5 9.2 %collective-permute-start.3 = (bf16[32,640]{1,0:T(8,128)(2,1)S(1)}, bf16[32,640]{1,0:T(8,128)(2,1)S(1)}, u32[]{:S(2)}, u32[]{:S(2)}) collective-permute-start(bf16[32,640]{1,0:T(8,128)(2,1)S(1)} %get-tuple-element.24), channel_id=1, source_target_pairs={{0,12},{1,13},{4,14},{5,15},{8,10},{9,11},{12,6},{13,7},{14,2},{15... | collective-permute-start | bytes 122888 | tf_op jit(solution)/shard_map/ppermute | solution.py:425
  8.6 9.0 %collective-permute-start.4 = (bf16[32,640]{1,0:T(8,128)(2,1)S(1)}, bf16[32,640]{1,0:T(8,128)(2,1)S(1)}, u32[]{:S(2)}, u32[]{:S(2)}) collective-permute-start(bf16[32,640]{1,0:T(8,128)(2,1)S(1)} %get-tuple-element.25), channel_id=1, source_target_pairs={{0,14},{1,15},{4,10},{5,11},{8,6},{9,7},{12,2},{13,3},{14,0},{15,1... | collective-permute-start | bytes 122888 | tf_op jit(solution)/shard_map/ppermute | solution.py:425
  17.8 12.0 %collective-permute-start.5 = (bf16[256,2304]{1,0:T(8,128)(2,1)S(1)}, bf16[256,2304]{1,0:T(8,128)(2,1)S(1)}, u32[]{:S(2)}, u32[]{:S(2)}) collective-permute-start(bf16[256,2304]{1,0:T(8,128)(2,1)S(1)} %get-tuple-element.26.refs_0_), channel_id=1, source_target_pairs={{0,1},{1,0},{2,3},{3,2},{4,5},{5,4},{6,7},{7,6},{8,9},{9,8},{10,11... | collective-permute-start | bytes 3538952 | tf_op jit(solution)/shard_map/ppermute | solution.py:22
  17.9 7.2 %collective-permute-start.6 = (bf16[32,2304]{1,0:T(8,128)(2,1)S(1)}, bf16[32,2304]{1,0:T(8,128)(2,1)S(1)}, u32[]{:S(2)}, u32[]{:S(2)}) collective-permute-start(bf16[32,2304]{1,0:T(8,128)(2,1)S(1)} %get-tuple-element.27), channel_id=1, source_target_pairs={{0,4},{1,5},{4,8},{5,9},{8,12},{9,13},{12,14},{13,15},{14,10},{15,... | collective-permute-start | bytes 442376 | tf_op jit(solution)/shard_map/ppermute | solution.py:55
  18.9 8.5 %collective-permute-start.7 = (bf16[32,2304]{1,0:T(8,128)(2,1)S(1)}, bf16[32,2304]{1,0:T(8,128)(2,1)S(1)}, u32[]{:S(2)}, u32[]{:S(2)}) collective-permute-start(bf16[32,2304]{1,0:T(8,128)(2,1)S(1)} %get-tuple-element.28), channel_id=1, source_target_pairs={{0,4},{1,5},{4,8},{5,9},{8,12},{9,13},{12,14},{13,15},{14,10},{15,... | collective-permute-start | bytes 442376 | tf_op jit(solution)/shard_map/ppermute | solution.py:55
  19.2 9.3 %collective-permute-start.8 = (bf16[32,2304]{1,0:T(8,128)(2,1)S(1)}, bf16[32,2304]{1,0:T(8,128)(2,1)S(1)}, u32[]{:S(2)}, u32[]{:S(2)}) collective-permute-start(bf16[32,2304]{1,0:T(8,128)(2,1)S(1)} %get-tuple-element.29), channel_id=1, source_target_pairs={{0,2},{1,3},{4,0},{5,1},{8,4},{9,5},{12,8},{13,9},{14,12},{15,13},... | collective-permute-start | bytes 442376 | tf_op jit(solution)/shard_map/ppermute | solution.py:55
  20.9 8.5 %collective-permute-start.9 = (bf16[32,2304]{1,0:T(8,128)(2,1)S(1)}, bf16[32,2304]{1,0:T(8,128)(2,1)S(1)}, u32[]{:S(2)}, u32[]{:S(2)}) collective-permute-start(bf16[32,2304]{1,0:T(8,128)(2,1)S(1)} %get-tuple-element.30), channel_id=1, source_target_pairs={{0,2},{1,3},{4,0},{5,1},{8,4},{9,5},{12,8},{13,9},{14,12},{15,13},... | collective-permute-start | bytes 442376 | tf_op jit(solution)/shard_map/ppermute | solution.py:55
  25.1 10.8 %collective-permute-start.10 = (bf16[32,2304]{1,0:T(8,128)(2,1)S(1)}, bf16[32,2304]{1,0:T(8,128)(2,1)S(1)}, u32[]{:S(2)}, u32[]{:S(2)}) collective-permute-start(bf16[32,2304]{1,0:T(8,128)(2,1)S(1)} %collective-permute-done.6.refs_0_), channel_id=1, source_target_pairs={{0,4},{1,5},{4,8},{5,9},{8,12},{9,13},{12,14},{13,15},{14,10},{15,... | collective-permute-start | bytes 442376 | tf_op jit(solution)/shard_map/ppermute | solution.py:55
  27.4 8.4 %collective-permute-start.11 = (bf16[32,2304]{1,0:T(8,128)(2,1)S(1)}, bf16[32,2304]{1,0:T(8,128)(2,1)S(1)}, u32[]{:S(2)}, u32[]{:S(2)}) collective-permute-start(bf16[32,2304]{1,0:T(8,128)(2,1)S(1)} %collective-permute-done.7.refs_1_), channel_id=1, source_target_pairs={{0,4},{1,5},{4,8},{5,9},{8,12},{9,13},{12,14},{13,15},{14,10},{15,... | collective-permute-start | bytes 442376 | tf_op jit(solution)/shard_map/ppermute | solution.py:55
  28.4 7.4 %collective-permute-start.12 = (bf16[32,2304]{1,0:T(8,128)(2,1)S(1)}, bf16[32,2304]{1,0:T(8,128)(2,1)S(1)}, u32[]{:S(2)}, u32[]{:S(2)}) collective-permute-start(bf16[32,2304]{1,0:T(8,128)(2,1)S(1)} %collective-permute-done.8.refs_2_), channel_id=1, source_target_pairs={{0,2},{1,3},{4,0},{5,1},{8,4},{9,5},{12,8},{13,9},{14,12},{15,13},... | collective-permute-start | bytes 442376 | tf_op jit(solution)/shard_map/ppermute | solution.py:55
  29.5 7.1 %collective-permute-start.13 = (bf16[32,2304]{1,0:T(8,128)(2,1)S(1)}, bf16[32,2304]{1,0:T(8,128)(2,1)S(1)}, u32[]{:S(2)}, u32[]{:S(2)}) collective-permute-start(bf16[32,2304]{1,0:T(8,128)(2,1)S(1)} %collective-permute-done.9.refs_3_), channel_id=1, source_target_pairs={{0,2},{1,3},{4,0},{5,1},{8,4},{9,5},{12,8},{13,9},{14,12},{15,13},... | collective-permute-start | bytes 442376 | tf_op jit(solution)/shard_map/ppermute | solution.py:55
  30.6 5.2 %collective-permute-start.14 = (bf16[128,128]{1,0:T(8,128)(2,1)S(1)}, bf16[128,128]{1,0:T(8,128)(2,1)S(1)}, u32[]{:S(2)}, u32[]{:S(2)}) collective-permute-start(bf16[128,128]{1,0:T(8,128)(2,1)S(1)} %get-tuple-element.31.refs_3_), channel_id=1, source_target_pairs={{0,2},{1,3},{2,0},{3,1},{4,6},{5,7},{6,4},{7,5},{8,10},{9,11},{10,... | collective-permute-start | bytes 98312 | tf_op jit(solution)/shard_map/ppermute | solution.py:461
  36.7 9.9 %collective-permute-start.15 = (bf16[256,2304]{1,0:T(8,128)(2,1)S(1)}, bf16[256,2304]{1,0:T(8,128)(2,1)S(1)}, u32[]{:S(2)}, u32[]{:S(2)}) collective-permute-start(bf16[256,2304]{1,0:T(8,128)(2,1)S(1)} %get-tuple-element.34.refs_0_), channel_id=1, source_target_pairs={{0,1},{1,0},{2,3},{3,2},{4,5},{5,4},{6,7},{7,6},{8,9},{9,8},{10,11... | collective-permute-start | bytes 3538952 | tf_op jit(solution)/shard_map/ppermute | solution.py:22
  36.7 9.2 %collective-permute-start.16 = (bf16[64,2304]{1,0:T(8,128)(2,1)S(1)}, bf16[64,2304]{1,0:T(8,128)(2,1)S(1)}, u32[]{:S(2)}, u32[]{:S(2)}) collective-permute-start(bf16[64,2304]{1,0:T(8,128)(2,1)S(1)} %get-tuple-element.35), channel_id=1, source_target_pairs={{0,4},{1,3},{4,8},{5,1},{8,12},{9,5},{12,14},{13,9},{14,10},{15,13... | collective-permute-start | bytes 884744 | tf_op jit(solution)/shard_map/ppermute | solution.py:474
  37.1 8.8 %collective-permute-start.19 = (bf16[128,128]{1,0:T(8,128)(2,1)S(1)}, bf16[128,128]{1,0:T(8,128)(2,1)S(1)}, u32[]{:S(2)}, u32[]{:S(2)}) collective-permute-start(bf16[128,128]{1,0:T(8,128)(2,1)S(1)} %get-tuple-element.33.refs_5_), channel_id=1, source_target_pairs={{0,4},{1,5},{2,6},{3,7},{4,8},{5,9},{6,10},{7,11},{8,12},{9,13},{1... | collective-permute-start | bytes 98312 | tf_op jit(solution)/shard_map/ppermute | solution.py:470
  38.4 7.5 %collective-permute-start.18 = (bf16[128,128]{1,0:T(8,128)(2,1)S(1)}, bf16[128,128]{1,0:T(8,128)(2,1)S(1)}, u32[]{:S(2)}, u32[]{:S(2)}) collective-permute-start(bf16[128,128]{1,0:T(8,128)(2,1)S(1)} %get-tuple-element.33.refs_5_), channel_id=1, source_target_pairs={{0,8},{1,9},{2,10},{3,11},{4,12},{5,13},{6,14},{7,15},{8,0},{9,1},... | collective-permute-start | bytes 98312 | tf_op jit(solution)/shard_map/ppermute | solution.py:470
  40.1 5.8 %collective-permute-start.17 = (bf16[128,128]{1,0:T(8,128)(2,1)S(1)}, bf16[128,128]{1,0:T(8,128)(2,1)S(1)}, u32[]{:S(2)}, u32[]{:S(2)}) collective-permute-start(bf16[128,128]{1,0:T(8,128)(2,1)S(1)} %get-tuple-element.33.refs_5_), channel_id=1, source_target_pairs={{0,12},{1,13},{2,14},{3,15},{4,0},{5,1},{6,2},{7,3},{8,4},{9,5},{1... | collective-permute-start | bytes 98312 | tf_op jit(solution)/shard_map/ppermute | solution.py:470
  46.0 3.5 %collective-permute-start.20 = (bf16[64,2304]{1,0:T(8,128)(2,1)S(1)}, bf16[64,2304]{1,0:T(8,128)(2,1)S(1)}, u32[]{:S(2)}, u32[]{:S(2)}) collective-permute-start(bf16[64,2304]{1,0:T(8,128)(2,1)S(1)} %shard_map.75.refs_3_.refs_0_), channel_id=1, source_target_pairs={{0,1},{1,0},{2,3},{3,2},{4,5},{5,4},{6,7},{7,6},{8,9},{9,8},{10,11... | collective-permute-start | bytes 884744 | tf_op jit(solution)/shard_map/ppermute | solution.py:22
  46.1 6.4 %collective-permute-start.21 = (bf16[128,128]{1,0:T(8,128)(2,1)S(1)}, bf16[128,128]{1,0:T(8,128)(2,1)S(1)}, u32[]{:S(2)}, u32[]{:S(2)}) collective-permute-start(bf16[128,128]{1,0:T(8,128)(2,1)S(1)} %get-tuple-element.37.refs_1_), channel_id=1, source_target_pairs={{0,1},{1,0},{2,3},{3,2},{4,5},{5,4},{6,7},{7,6},{8,9},{9,8},{10,11... | collective-permute-start | bytes 98312 | tf_op jit(solution)/shard_map/ppermute | solution.py:22
  (3 other events, 10.7 us)

commit v11 on v10

--- a/solution.py
+++ b/solution.py
@@ -188,23 +188,21 @@
     rounded[...] = value.astype(jnp.bfloat16)
 
 
-def prepare_kernel(n, window, distances, tokens_ref, down_ref, factor, *refs):
-    *sends, tokens, down, sems = refs
-    copies = [
-        pltpu.make_async_copy(source, to, sems.at[k])
-        for k, (source, to) in enumerate(((tokens_ref, tokens), (down_ref, down)))
-    ]
+def prepare_kernel(n, window, distances, tokens, down_ref, factor, *refs):
+    *sends, down, sems = refs
+    copies = [pltpu.make_async_copy(down_ref, down, sems.at[0])]
+    for k, (distance, send) in enumerate(zip(distances, sends)):
+        start = pl.multiple_of(window.start(chip_at(distance, n)), 128)
+        copies.append(pltpu.make_async_copy(tokens.at[:, pl.ds(start, window.size)], send, sems.at[1 + k]))
     for copy in copies:
         copy.start()
     copies[0].wait()
-    for distance, send in zip(distances, sends):
-        start = pl.multiple_of(window.start(chip_at(distance, n)), 128)
-        send[...] = tokens[:, pl.ds(start, window.size)]
-    copies[1].wait()
     zeros = jnp.zeros((down.shape[1], window.size - window.width), jnp.float32)
     for index in range(down.shape[0]):
         wide = jnp.concatenate([down[index], zeros], 1)
         factor[index] = pltpu.roll(wide, window.shift(lax.axis_index("seq")), 1).astype(jnp.bfloat16)
+    for copy in copies[1:]:
+        copy.wait()
 
 
 def full_rows(rows):
@@ -309,39 +307,21 @@
     return total
 
 
-def base_kernel(rows, counts, *refs):
-    count = 2 * len(counts)
-    pairs, weights, (base, held) = refs[:count], refs[count:-2], refs[-2:]
-    assemble(list(zip(pairs[::2], pairs[1::2])), counts, rows, held)
-    width = base.shape[1]
-    columns = tile_width(width)
-    for j in range(0, width, columns):
-        at = slice(j, j + columns)
-        base[:, at] = multiply(held, weights, at)[: base.shape[0]]
-
-
-def base_rows(pairs, counts, rows, weights, after):
-    chips = sum(counts)
-    total, depth, width = 2 * rows * chips, sum(w.shape[0] for w in weights), weights[0].shape[1]
-    arrays = [x for pair in pairs for x in pair]
-    (base,) = call(
-        functools.partial(base_kernel, rows, counts),
-        arrays + weights,
-        after,
-        [((total, width), jnp.float32)],
-        [pltpu.VMEM((full_rows(total), depth), jnp.bfloat16)],
-        limit=8 + (2 * total * depth >> 20),
-        flops=2 * total * depth * width,
-    )
-    return base
-
-
-def finish_kernel(n, rows, groups, adapters, live, *refs):
-    *bases, own, other, up_ref = refs[: len(groups) + 3]
-    out_ref, shrink, block, sems = refs[len(groups) + 3 :]
+def finish_kernel(n, rows, groups, skipped, *refs):
+    count = len(groups) - 1
+    bases, refs = refs[:count], refs[count:]
+    mine, others, weight, own, other, up_ref, adapters_ref, live_ref = refs[:8]
+    out_ref, held, shrink, block, adapters, live, sems, small_sems = refs[8 + skipped :]
+    lookups = [
+        pltpu.make_async_copy(source, to, small_sems.at[k])
+        for k, (source, to) in enumerate(((adapters_ref, adapters), (live_ref, live)))
+    ]
+    for lookup in lookups:
+        lookup.start()
     c = lax.axis_index("adapter")
     chip_rows, rank = 2 * rows, up_ref.shape[1]
     tiles, _, columns = block.shape
+    assemble([(mine, others)], [1], rows, held)
     for t in range(n):
         i, k = t % (n // 2), t // (n // 2)
         for ref, core in ((own, c), (other, 1 - c)):
@@ -349,21 +329,24 @@
             shrink[t, pl.ds(pl.multiple_of(core * rows, rows), rows), :] = part.astype(jnp.bfloat16)
     places = [
         (distance, base, i * chip_rows)
-        for base, distances in zip(bases, groups)
+        for base, distances in zip([*bases, None], groups)
         for i, distance in enumerate(distances)
     ]
+    for lookup in lookups:
+        lookup.wait()
     copies = []
     for j in range(tiles):
         at = slice(j * columns, (j + 1) * columns)
+        last = multiply(held, [weight], at)
         for i, (distance, base, row) in enumerate(places):
             chip = chip_at(distance, n)
             first = chip * chip_rows
             of_block = first // BLOCK
             delta = jnp.dot(shrink[chip], up_ref[adapters[of_block], :, at], preferred_element_type=jnp.float32)
             index = lax.broadcasted_iota(jnp.int32, delta.shape, 0) + (first - of_block * BLOCK)
-            total = jnp.where(index < live[of_block], base[row : row + chip_rows, at] + delta, 0.0)
+            value = last[:chip_rows] if base is None else base[row : row + chip_rows, at]
             place = pl.ds(i * chip_rows, chip_rows)
-            block[j, place, :] = total.astype(out_ref.dtype)
+            block[j, place, :] = jnp.where(index < live[of_block], value + delta, 0.0).astype(out_ref.dtype)
             copies.append(
                 pltpu.make_async_copy(
                     block.at[j, place, :],
@@ -376,25 +359,29 @@
         copy.wait()
 
 
-def finish(n, rows, groups, scalars, bases, own, other, up):
-    rank, width = up.shape[1:]
+def finish(n, rows, groups, lookups, bases, last_pair, weight, sums, up, after):
+    (rank, width), depth = up.shape[1:], weight.shape[0]
     total, columns = 2 * n * rows, tile_width(width)
-    arrays = [*bases, own, other, up]
+    arrays = [*bases, *last_pair, weight, *sums, up]
+    held = full_rows(2 * rows)
     return pl.pallas_call(
-        functools.partial(finish_kernel, n, rows, groups),
+        functools.partial(finish_kernel, n, rows, groups, len(after)),
         out_shape=jax.ShapeDtypeStruct((total, width), jnp.bfloat16),
-        in_specs=[pl.BlockSpec(memory_space=pltpu.SMEM)] * len(scalars) + whole(len(arrays)),
+        in_specs=whole(len(arrays)) + [pl.BlockSpec(memory_space=pl.ANY)] * (len(lookups) + len(after)),
         out_specs=pl.BlockSpec(memory_space=pl.ANY),
         scratch_shapes=[
+            pltpu.VMEM((held, depth), jnp.bfloat16),
             pltpu.VMEM((n, 2 * rows, rank), jnp.bfloat16),
             pltpu.VMEM((width // columns, total, columns), jnp.bfloat16),
+            *(pltpu.SMEM(x.shape, x.dtype) for x in lookups),
             pltpu.SemaphoreType.DMA((width // columns, n)),
+            pltpu.SemaphoreType.DMA((len(lookups),)),
         ],
-        compiler_params=pltpu.CompilerParams(vmem_limit_bytes=8 << 20),
+        compiler_params=pltpu.CompilerParams(vmem_limit_bytes=10 << 20),
         cost_estimate=pl.CostEstimate(
-            flops=2 * total * rank * width, bytes_accessed=2 * total * width, transcendentals=0
+            flops=2 * held * depth * width, bytes_accessed=2 * total * width, transcendentals=0
         ),
-    )(*scalars, *in_vmem(arrays))
+    )(*in_vmem(arrays), *lookups, *after)
 
 
 def on_device(n, tokens, weight, down, up, adapter_per_block, rows_per_block):
@@ -417,9 +404,8 @@
         [weight, up],
         [((held, rank, window.size), bf16)] + [((rows, window.size), bf16)] * len(ends),
         [
-            pltpu.VMEM(tokens.shape, tokens.dtype),
             pltpu.VMEM((held, rank, width), down.dtype),
-            pltpu.SemaphoreType.DMA((2,)),
+            pltpu.SemaphoreType.DMA((1 + len(ends),)),
         ],
     )
     received = [lax.ppermute(x, AXES, ring_perm(n, d)) for d, x in zip(ends, sends)]
@@ -475,16 +461,17 @@
 
     bases.append(core_rows(late_swapped, len(late), rows, weights, [last_rows], mine))
     last_pair = (last_rows, swap_cores(last_rows, n))
-    bases.append(base_rows([last_pair], [1], rows, weights, bases[-1:]))
     return finish(
         n,
         rows,
         [near, late, [last]],
         [adapters, rows_per_block],
         bases,
-        total,
-        swap_cores(rounded, n),
+        last_pair,
+        weight,
+        [total, swap_cores(rounded, n)],
         up,
+        [],
     )
 
 

time: 55.2 us -> 55.1 us (level)
    pallas_call x1, Pallas kernels: 2.41 us -> 5.23 us  [finish(): pl.pallas_call(functools.partial(finish_kernel, n, rows, groups, len(afte...]
    pallas_call x13 -> x12, Pallas kernels: 15.9 us -> 13.1 us  [call(): pl.pallas_call(body, out_shape=[pltpu.VMEM(shape, dtype) for shape, dtype...]
  transfers between devices with their start and end apart: 22 -> 22, of which waited for: 5 -> 5; matrix products, arithmetic and copies ran while one was open for 0% -> 0% of each run, Pallas kernels for 31% -> 26%
where the time goes in v11:
time: 55.1 us; the launch traced here: 55 us
  starting transfers between devices  27.4 us (50%)
  Pallas kernels  19.7 us (36%)
  waiting for transfers between devices  7.44 us (14%)
    pallas_call x12, Pallas kernels, call(): pl.pallas_call(body, out_shape=[pltpu.VMEM(shape, dtype) for shape, dtype...  13.1 us
    ppermute x3, starting transfers between devices, on_device(): lax.ppermute(x, AXES, ring_perm(n, d))  8.88 us
    ppermute x5, starting transfers between devices, ring_hop(): lax.ppermute(x, AXES, ring_perm(n, -1))  7.11 us
    ppermute x3, starting transfers between devices, on_device(): lax.ppermute(rounded, AXES, z_perm(n, shift))  5.84 us
    pallas_call x1, Pallas kernels, finish(): pl.pallas_call(functools.partial(finish_kernel, n, rows, groups, len(afte...  5.23 us
    ppermute x3, waiting for transfers between devices, on_device(): lax.ppermute(x, AXES, ring_perm(n, d))  4.39 us
    ppermute x5, starting transfers between devices, ring_hop(): lax.ppermute(x, AXES, ring_perm(n, 1))  3.42 us
    pallas_call x1, Pallas kernels, prepare(): pl.pallas_call(body, out_shape=[pltpu.VMEM(shape, dtype) for shape, dtype...  1.31 us
  transfers between devices with their start and end apart: 22, of which 5 were waited for; matrix products, arithmetic and copies ran while one was open for 0% of the time, Pallas kernels for 26%

profile of v11, /device:TPU:0, one launch (start us, length us, event | category | flops | bytes accessed | tf_op | source)
XLA Modules:
  0.0 55.0 jit_solution(17358722941396702848)
XLA Ops:
  0.0 3.0 %collective-permute-start.1 = (bf16[32,4608]{1,0:T(8,128)(2,1)}, bf16[32,4608]{1,0:T(8,128)(2,1)S(1)}, u32[]{:S(2)}, u32[]{:S(2)}) collective-permute-start(bf16[32,4608]{1,0:T(8,128)(2,1)} %refs_0_.4), channel_id=1, source_target_pairs={{0,2},{1,3},{4,0},{5,1},{8,4},{9,5},{12,8},{13,9},{14,12},{15,13},... | collective-permute-start | bytes 884744 | tf_op jit(solution)/shard_map/ppermute | solution.py:55
  3.0 1.3 %shard_map.64 = (bf16[2,64,640]{2,1,0:T(8,128)(2,1)S(1)}, bf16[32,640]{1,0:T(8,128)(2,1)S(1)}, bf16[32,640]{1,0:T(8,128)(2,1)S(1)}, bf16[32,640]{1,0:T(8,128)(2,1)S(1)}) custom-call(bf16[32,4608]{1,0:T(8,128)(2,1)} %refs_0_.4, f32[2,64,576]{2,1,0:T(8,128)} %bitcast.4, bf16[4608,2304]{1,0:T(8,128)(2,1)} %refs_4_.1, f32[4,64,2304]{2,1,0:T(8,128)} %refs_0_.5), custom_call_target="tpu_custom_call" | custom-call | tf_op jit(solution)/shard_map/pallas_call | solution.py:272
  4.3 4.0 %collective-permute-start.2 = (bf16[32,640]{1,0:T(8,128)(2,1)S(1)}, bf16[32,640]{1,0:T(8,128)(2,1)S(1)}, u32[]{:S(2)}, u32[]{:S(2)}) collective-permute-start(bf16[32,640]{1,0:T(8,128)(2,1)S(1)} %get-tuple-element.23), channel_id=1, source_target_pairs={{0,10},{1,11},{4,6},{5,7},{8,2},{9,3},{12,0},{13,1},{14,4},{15,5},... | collective-permute-start | bytes 122888 | tf_op jit(solution)/shard_map/ppermute | solution.py:411
  8.5 4.7 %collective-permute-start.4 = (bf16[32,640]{1,0:T(8,128)(2,1)S(1)}, bf16[32,640]{1,0:T(8,128)(2,1)S(1)}, u32[]{:S(2)}, u32[]{:S(2)}) collective-permute-start(bf16[32,640]{1,0:T(8,128)(2,1)S(1)} %get-tuple-element.25), channel_id=1, source_target_pairs={{0,14},{1,15},{4,10},{5,11},{8,6},{9,7},{12,2},{13,3},{14,0},{15,1... | collective-permute-start | bytes 122888 | tf_op jit(solution)/shard_map/ppermute | solution.py:411
  13.2 1.1 %collective-permute-done.2.refs_4_.refs_2_ = bf16[32,640]{1,0:T(8,128)(2,1)S(1)} collective-permute-done((bf16[32,640]{1,0:T(8,128)(2,1)S(1)}, bf16[32,640]{1,0:T(8,128)(2,1)S(1)}, u32[]{:S(2)}, u32[]{:S(2)}) %collective-permute-start.2) | collective-permute-done | bytes 40992 | tf_op jit(solution)/shard_map/ppermute | solution.py:411
  14.3 3.3 %collective-permute-done.3.refs_5_.refs_3_ = bf16[32,640]{1,0:T(8,128)(2,1)S(1)} collective-permute-done((bf16[32,640]{1,0:T(8,128)(2,1)S(1)}, bf16[32,640]{1,0:T(8,128)(2,1)S(1)}, u32[]{:S(2)}, u32[]{:S(2)}) %collective-permute-start.3) | collective-permute-done | bytes 40992 | tf_op jit(solution)/shard_map/ppermute | solution.py:411
  17.9 1.0 %collective-permute-start.6 = (bf16[32,2304]{1,0:T(8,128)(2,1)S(1)}, bf16[32,2304]{1,0:T(8,128)(2,1)S(1)}, u32[]{:S(2)}, u32[]{:S(2)}) collective-permute-start(bf16[32,2304]{1,0:T(8,128)(2,1)S(1)} %get-tuple-element.27), channel_id=1, source_target_pairs={{0,4},{1,5},{4,8},{5,9},{8,12},{9,13},{12,14},{13,15},{14,10},{15,... | collective-permute-start | bytes 442376 | tf_op jit(solution)/shard_map/ppermute | solution.py:55
  19.2 1.7 %collective-permute-start.8 = (bf16[32,2304]{1,0:T(8,128)(2,1)S(1)}, bf16[32,2304]{1,0:T(8,128)(2,1)S(1)}, u32[]{:S(2)}, u32[]{:S(2)}) collective-permute-start(bf16[32,2304]{1,0:T(8,128)(2,1)S(1)} %get-tuple-element.29), channel_id=1, source_target_pairs={{0,2},{1,3},{4,0},{5,1},{8,4},{9,5},{12,8},{13,9},{14,12},{15,13},... | collective-permute-start | bytes 442376 | tf_op jit(solution)/shard_map/ppermute | solution.py:55
  20.9 1.0 %collective-permute-start.9 = (bf16[32,2304]{1,0:T(8,128)(2,1)S(1)}, bf16[32,2304]{1,0:T(8,128)(2,1)S(1)}, u32[]{:S(2)}, u32[]{:S(2)}) collective-permute-start(bf16[32,2304]{1,0:T(8,128)(2,1)S(1)} %get-tuple-element.30), channel_id=1, source_target_pairs={{0,2},{1,3},{4,0},{5,1},{8,4},{9,5},{12,8},{13,9},{14,12},{15,13},... | collective-permute-start | bytes 442376 | tf_op jit(solution)/shard_map/ppermute | solution.py:55
  22.0 3.0 %shard_map.66.refs_1_.refs_4_ = f32[96,2304]{1,0:T(8,128)S(1)} custom-call(bf16[256,2304]{1,0:T(8,128)(2,1)S(1)} %get-tuple-element.26.refs_0_, bf16[4608,2304]{1,0:T(8,128)(2,1)S(1)} %copy-done), custom_call_target="tpu_custom_call" | custom-call | flops 2038431744 | tf_op jit(solution)/shard_map/pallas_call | solution.py:98
  25.1 1.0 %collective-permute-start.10 = (bf16[32,2304]{1,0:T(8,128)(2,1)S(1)}, bf16[32,2304]{1,0:T(8,128)(2,1)S(1)}, u32[]{:S(2)}, u32[]{:S(2)}) collective-permute-start(bf16[32,2304]{1,0:T(8,128)(2,1)S(1)} %collective-permute-done.6.refs_0_), channel_id=1, source_target_pairs={{0,4},{1,5},{4,8},{5,9},{8,12},{9,13},{12,14},{13,15},{14,10},{15,... | collective-permute-start | bytes 442376 | tf_op jit(solution)/shard_map/ppermute | solution.py:55
  26.2 1.2 %collective-permute-done.7.refs_1_ = bf16[32,2304]{1,0:T(8,128)(2,1)S(1)} collective-permute-done((bf16[32,2304]{1,0:T(8,128)(2,1)S(1)}, bf16[32,2304]{1,0:T(8,128)(2,1)S(1)}, u32[]{:S(2)}, u32[]{:S(2)}) %collective-permute-start.7) | collective-permute-done | bytes 147488 | tf_op jit(solution)/shard_map/ppermute | solution.py:55
  27.4 1.0 %collective-permute-start.11 = (bf16[32,2304]{1,0:T(8,128)(2,1)S(1)}, bf16[32,2304]{1,0:T(8,128)(2,1)S(1)}, u32[]{:S(2)}, u32[]{:S(2)}) collective-permute-start(bf16[32,2304]{1,0:T(8,128)(2,1)S(1)} %collective-permute-done.7.refs_1_), channel_id=1, source_target_pairs={{0,4},{1,5},{4,8},{5,9},{8,12},{9,13},{12,14},{13,15},{14,10},{15,... | collective-permute-start | bytes 442376 | tf_op jit(solution)/shard_map/ppermute | solution.py:55
  28.4 1.0 %collective-permute-start.12 = (bf16[32,2304]{1,0:T(8,128)(2,1)S(1)}, bf16[32,2304]{1,0:T(8,128)(2,1)S(1)}, u32[]{:S(2)}, u32[]{:S(2)}) collective-permute-start(bf16[32,2304]{1,0:T(8,128)(2,1)S(1)} %collective-permute-done.8.refs_2_), channel_id=1, source_target_pairs={{0,2},{1,3},{4,0},{5,1},{8,4},{9,5},{12,8},{13,9},{14,12},{15,13},... | collective-permute-start | bytes 442376 | tf_op jit(solution)/shard_map/ppermute | solution.py:55
  29.8 0.8 %shard_map.69 = (f32[128,128]{1,0:T(8,128)S(1)}, bf16[128,128]{1,0:T(8,128)(2,1)S(1)}) custom-call(bf16[256,2304]{1,0:T(8,128)(2,1)S(1)} %get-tuple-element.26.refs_0_, bf16[128,2304]{1,0:T(8,128)(2,1)S(1)} %shard_map.68.refs_1_.refs_0_, bf16[32,640]{1,0:T(8,128)(2,1)S(1)} %collective-permute-done.2.refs_4_.refs_2_, ...), custom_call_target="tpu_custom_call" | custom-call | tf_op jit(solution)/shard_map/pallas_call | solution.py:98
  30.6 1.1 %collective-permute-start.14 = (bf16[128,128]{1,0:T(8,128)(2,1)S(1)}, bf16[128,128]{1,0:T(8,128)(2,1)S(1)}, u32[]{:S(2)}, u32[]{:S(2)}) collective-permute-start(bf16[128,128]{1,0:T(8,128)(2,1)S(1)} %get-tuple-element.31.refs_3_), channel_id=1, source_target_pairs={{0,2},{1,3},{2,0},{3,1},{4,6},{5,7},{6,4},{7,5},{8,10},{9,11},{10,... | collective-permute-start | bytes 98312 | tf_op jit(solution)/shard_map/ppermute | solution.py:447
  31.7 3.0 %shard_map.70.refs_6_.refs_0_ = f32[192,2304]{1,0:T(8,128)S(1)} custom-call(bf16[256,2304]{1,0:T(8,128)(2,1)S(1)} %collective-permute-done.5.refs_6_.refs_0_, f32[96,2304]{1,0:T(8,128)S(1)} %shard_map.66.refs_1_.refs_4_, bf16[4608,2304]{1,0:T(8,128)(2,1)S(1)} %copy-done, bf16[128,128]{1,0:T(8,128)(2,1)S(1)} %get-tuple-element.31.refs_3_), custom_call_target="tpu_custom_call" | custom-call | flops 2038431744 | tf_op jit(solution)/shard_map/pallas_call | solution.py:98
  34.7 1.1 %collective-permute-done.14.refs_1_ = bf16[128,128]{1,0:T(8,128)(2,1)S(1)} collective-permute-done((bf16[128,128]{1,0:T(8,128)(2,1)S(1)}, bf16[128,128]{1,0:T(8,128)(2,1)S(1)}, u32[]{:S(2)}, u32[]{:S(2)}) %collective-permute-start.14) | collective-permute-done | bytes 32800 | tf_op jit(solution)/shard_map/ppermute | solution.py:447
  37.1 1.3 %collective-permute-start.19 = (bf16[128,128]{1,0:T(8,128)(2,1)S(1)}, bf16[128,128]{1,0:T(8,128)(2,1)S(1)}, u32[]{:S(2)}, u32[]{:S(2)}) collective-permute-start(bf16[128,128]{1,0:T(8,128)(2,1)S(1)} %get-tuple-element.33.refs_5_), channel_id=1, source_target_pairs={{0,4},{1,5},{2,6},{3,7},{4,8},{5,9},{6,10},{7,11},{8,12},{9,13},{1... | collective-permute-start | bytes 98312 | tf_op jit(solution)/shard_map/ppermute | solution.py:456
  38.4 1.7 %collective-permute-start.18 = (bf16[128,128]{1,0:T(8,128)(2,1)S(1)}, bf16[128,128]{1,0:T(8,128)(2,1)S(1)}, u32[]{:S(2)}, u32[]{:S(2)}) collective-permute-start(bf16[128,128]{1,0:T(8,128)(2,1)S(1)} %get-tuple-element.33.refs_5_), channel_id=1, source_target_pairs={{0,8},{1,9},{2,10},{3,11},{4,12},{5,13},{6,14},{7,15},{8,0},{9,1},... | collective-permute-start | bytes 98312 | tf_op jit(solution)/shard_map/ppermute | solution.py:456
  40.1 2.8 %collective-permute-start.17 = (bf16[128,128]{1,0:T(8,128)(2,1)S(1)}, bf16[128,128]{1,0:T(8,128)(2,1)S(1)}, u32[]{:S(2)}, u32[]{:S(2)}) collective-permute-start(bf16[128,128]{1,0:T(8,128)(2,1)S(1)} %get-tuple-element.33.refs_5_), channel_id=1, source_target_pairs={{0,12},{1,13},{2,14},{3,15},{4,0},{5,1},{6,2},{7,3},{8,4},{9,5},{1... | collective-permute-start | bytes 98312 | tf_op jit(solution)/shard_map/ppermute | solution.py:456
  42.9 2.9 %shard_map.73.refs_2_.refs_1_ = f32[128,2304]{1,0:T(8,128)S(1)} custom-call(bf16[256,2304]{1,0:T(8,128)(2,1)S(1)} %get-tuple-element.34.refs_0_, bf16[4608,2304]{1,0:T(8,128)(2,1)S(1)} %copy-done), custom_call_target="tpu_custom_call" | custom-call | flops 2717908992 | tf_op jit(solution)/shard_map/pallas_call | solution.py:98
  46.6 3.0 %shard_map.76.refs_1_ = f32[256,2304]{1,0:T(8,128)S(1)} custom-call(bf16[256,2304]{1,0:T(8,128)(2,1)S(1)} %collective-permute-done.15.refs_0_, f32[128,2304]{1,0:T(8,128)S(1)} %shard_map.73.refs_2_.refs_1_, bf16[4608,2304]{1,0:T(8,128)(2,1)S(1)} %copy-done, bf16[64,2304]{1,0:T(8,128)(2,1)S(1)} %shard_map.75.refs_3_.refs_2_), custom_call_target="tpu_custom_call" | custom-call | flops 2717908992 | tf_op jit(solution)/shard_map/pallas_call | solution.py:98
  49.6 5.2 %shard_map.77 = bf16[512,2304]{1,0:T(8,128)(2,1)} custom-call(f32[192,2304]{1,0:T(8,128)S(1)} %shard_map.70.refs_6_.refs_0_, f32[256,2304]{1,0:T(8,128)S(1)} %shard_map.76.refs_1_, bf16[64,2304]{1,0:T(8,128)(2,1)S(1)} %shard_map.75.refs_3_.refs_2_, bf16[64,2304]{1,0:T(8,128)(2,1)S(1)} %collective-permute-done.20.refs_3_, bf16[4608,2304]{1,0:T(8,128)(2,1)S(1)} %copy-done, ...), custom_call_target="tpu_custom_call" | custom-call | flops 2717908992 | bytes 2359296 | tf_op jit(solution)/shard_map/pallas_call | solution.py:367
  (44 shorter events, 3.0 us)
Async XLA Ops:
  0.0 17.6 %collective-permute-start.1 = (bf16[32,4608]{1,0:T(8,128)(2,1)}, bf16[32,4608]{1,0:T(8,128)(2,1)S(1)}, u32[]{:S(2)}, u32[]{:S(2)}) collective-permute-start(bf16[32,4608]{1,0:T(8,128)(2,1)} %refs_0_.4), channel_id=1, source_target_pairs={{0,2},{1,3},{4,0},{5,1},{8,4},{9,5},{12,8},{13,9},{14,12},{15,13},... | collective-permute-start | bytes 884744 | tf_op jit(solution)/shard_map/ppermute | solution.py:55
  3.0 14.7 %collective-permute-start = (bf16[32,4608]{1,0:T(8,128)(2,1)}, bf16[32,4608]{1,0:T(8,128)(2,1)S(1)}, u32[]{:S(2)}, u32[]{:S(2)}) collective-permute-start(bf16[32,4608]{1,0:T(8,128)(2,1)} %refs_0_.4), channel_id=1, source_target_pairs={{0,4},{1,5},{4,8},{5,9},{8,12},{9,13},{12,14},{13,15},{14,10},{15,... | collective-permute-start | bytes 884744 | tf_op jit(solution)/shard_map/ppermute | solution.py:55
  3.0 14.6 %copy-start.2 = (bf16[32,4608]{1,0:T(8,128)(2,1)S(1)}, bf16[32,4608]{1,0:T(8,128)(2,1)}, u32[]{:S(2)}) copy-start(bf16[32,4608]{1,0:T(8,128)(2,1)} %refs_0_.4) | copy-start | bytes 884740
  3.0 18.9 %copy-start = (bf16[4608,2304]{1,0:T(8,128)(2,1)S(1)}, bf16[4608,2304]{1,0:T(8,128)(2,1)}, u32[]{:S(2)}) copy-start(bf16[4608,2304]{1,0:T(8,128)(2,1)} %refs_4_.1) | copy-start | bytes 63700996
  4.3 9.9 %collective-permute-start.2 = (bf16[32,640]{1,0:T(8,128)(2,1)S(1)}, bf16[32,640]{1,0:T(8,128)(2,1)S(1)}, u32[]{:S(2)}, u32[]{:S(2)}) collective-permute-start(bf16[32,640]{1,0:T(8,128)(2,1)S(1)} %get-tuple-element.23), channel_id=1, source_target_pairs={{0,10},{1,11},{4,6},{5,7},{8,2},{9,3},{12,0},{13,1},{14,4},{15,5},... | collective-permute-start | bytes 122888 | tf_op jit(solution)/shard_map/ppermute | solution.py:411
  8.4 9.2 %collective-permute-start.3 = (bf16[32,640]{1,0:T(8,128)(2,1)S(1)}, bf16[32,640]{1,0:T(8,128)(2,1)S(1)}, u32[]{:S(2)}, u32[]{:S(2)}) collective-permute-start(bf16[32,640]{1,0:T(8,128)(2,1)S(1)} %get-tuple-element.24), channel_id=1, source_target_pairs={{0,12},{1,13},{4,14},{5,15},{8,10},{9,11},{12,6},{13,7},{14,2},{15... | collective-permute-start | bytes 122888 | tf_op jit(solution)/shard_map/ppermute | solution.py:411
  8.5 9.1 %collective-permute-start.4 = (bf16[32,640]{1,0:T(8,128)(2,1)S(1)}, bf16[32,640]{1,0:T(8,128)(2,1)S(1)}, u32[]{:S(2)}, u32[]{:S(2)}) collective-permute-start(bf16[32,640]{1,0:T(8,128)(2,1)S(1)} %get-tuple-element.25), channel_id=1, source_target_pairs={{0,14},{1,15},{4,10},{5,11},{8,6},{9,7},{12,2},{13,3},{14,0},{15,1... | collective-permute-start | bytes 122888 | tf_op jit(solution)/shard_map/ppermute | solution.py:411
  17.8 12.0 %collective-permute-start.5 = (bf16[256,2304]{1,0:T(8,128)(2,1)S(1)}, bf16[256,2304]{1,0:T(8,128)(2,1)S(1)}, u32[]{:S(2)}, u32[]{:S(2)}) collective-permute-start(bf16[256,2304]{1,0:T(8,128)(2,1)S(1)} %get-tuple-element.26.refs_0_), channel_id=1, source_target_pairs={{0,1},{1,0},{2,3},{3,2},{4,5},{5,4},{6,7},{7,6},{8,9},{9,8},{10,11... | collective-permute-start | bytes 3538952 | tf_op jit(solution)/shard_map/ppermute | solution.py:22
  17.9 7.3 %collective-permute-start.6 = (bf16[32,2304]{1,0:T(8,128)(2,1)S(1)}, bf16[32,2304]{1,0:T(8,128)(2,1)S(1)}, u32[]{:S(2)}, u32[]{:S(2)}) collective-permute-start(bf16[32,2304]{1,0:T(8,128)(2,1)S(1)} %get-tuple-element.27), channel_id=1, source_target_pairs={{0,4},{1,5},{4,8},{5,9},{8,12},{9,13},{12,14},{13,15},{14,10},{15,... | collective-permute-start | bytes 442376 | tf_op jit(solution)/shard_map/ppermute | solution.py:55
  18.9 8.5 %collective-permute-start.7 = (bf16[32,2304]{1,0:T(8,128)(2,1)S(1)}, bf16[32,2304]{1,0:T(8,128)(2,1)S(1)}, u32[]{:S(2)}, u32[]{:S(2)}) collective-permute-start(bf16[32,2304]{1,0:T(8,128)(2,1)S(1)} %get-tuple-element.28), channel_id=1, source_target_pairs={{0,4},{1,5},{4,8},{5,9},{8,12},{9,13},{12,14},{13,15},{14,10},{15,... | collective-permute-start | bytes 442376 | tf_op jit(solution)/shard_map/ppermute | solution.py:55
  19.2 9.2 %collective-permute-start.8 = (bf16[32,2304]{1,0:T(8,128)(2,1)S(1)}, bf16[32,2304]{1,0:T(8,128)(2,1)S(1)}, u32[]{:S(2)}, u32[]{:S(2)}) collective-permute-start(bf16[32,2304]{1,0:T(8,128)(2,1)S(1)} %get-tuple-element.29), channel_id=1, source_target_pairs={{0,2},{1,3},{4,0},{5,1},{8,4},{9,5},{12,8},{13,9},{14,12},{15,13},... | collective-permute-start | bytes 442376 | tf_op jit(solution)/shard_map/ppermute | solution.py:55
  20.9 8.5 %collective-permute-start.9 = (bf16[32,2304]{1,0:T(8,128)(2,1)S(1)}, bf16[32,2304]{1,0:T(8,128)(2,1)S(1)}, u32[]{:S(2)}, u32[]{:S(2)}) collective-permute-start(bf16[32,2304]{1,0:T(8,128)(2,1)S(1)} %get-tuple-element.30), channel_id=1, source_target_pairs={{0,2},{1,3},{4,0},{5,1},{8,4},{9,5},{12,8},{13,9},{14,12},{15,13},... | collective-permute-start | bytes 442376 | tf_op jit(solution)/shard_map/ppermute | solution.py:55
  25.1 10.7 %collective-permute-start.10 = (bf16[32,2304]{1,0:T(8,128)(2,1)S(1)}, bf16[32,2304]{1,0:T(8,128)(2,1)S(1)}, u32[]{:S(2)}, u32[]{:S(2)}) collective-permute-start(bf16[32,2304]{1,0:T(8,128)(2,1)S(1)} %collective-permute-done.6.refs_0_), channel_id=1, source_target_pairs={{0,4},{1,5},{4,8},{5,9},{8,12},{9,13},{12,14},{13,15},{14,10},{15,... | collective-permute-start | bytes 442376 | tf_op jit(solution)/shard_map/ppermute | solution.py:55
  27.4 8.5 %collective-permute-start.11 = (bf16[32,2304]{1,0:T(8,128)(2,1)S(1)}, bf16[32,2304]{1,0:T(8,128)(2,1)S(1)}, u32[]{:S(2)}, u32[]{:S(2)}) collective-permute-start(bf16[32,2304]{1,0:T(8,128)(2,1)S(1)} %collective-permute-done.7.refs_1_), channel_id=1, source_target_pairs={{0,4},{1,5},{4,8},{5,9},{8,12},{9,13},{12,14},{13,15},{14,10},{15,... | collective-permute-start | bytes 442376 | tf_op jit(solution)/shard_map/ppermute | solution.py:55
  28.4 7.5 %collective-permute-start.12 = (bf16[32,2304]{1,0:T(8,128)(2,1)S(1)}, bf16[32,2304]{1,0:T(8,128)(2,1)S(1)}, u32[]{:S(2)}, u32[]{:S(2)}) collective-permute-start(bf16[32,2304]{1,0:T(8,128)(2,1)S(1)} %collective-permute-done.8.refs_2_), channel_id=1, source_target_pairs={{0,2},{1,3},{4,0},{5,1},{8,4},{9,5},{12,8},{13,9},{14,12},{15,13},... | collective-permute-start | bytes 442376 | tf_op jit(solution)/shard_map/ppermute | solution.py:55
  29.4 7.2 %collective-permute-start.13 = (bf16[32,2304]{1,0:T(8,128)(2,1)S(1)}, bf16[32,2304]{1,0:T(8,128)(2,1)S(1)}, u32[]{:S(2)}, u32[]{:S(2)}) collective-permute-start(bf16[32,2304]{1,0:T(8,128)(2,1)S(1)} %collective-permute-done.9.refs_3_), channel_id=1, source_target_pairs={{0,2},{1,3},{4,0},{5,1},{8,4},{9,5},{12,8},{13,9},{14,12},{15,13},... | collective-permute-start | bytes 442376 | tf_op jit(solution)/shard_map/ppermute | solution.py:55
  30.6 5.2 %collective-permute-start.14 = (bf16[128,128]{1,0:T(8,128)(2,1)S(1)}, bf16[128,128]{1,0:T(8,128)(2,1)S(1)}, u32[]{:S(2)}, u32[]{:S(2)}) collective-permute-start(bf16[128,128]{1,0:T(8,128)(2,1)S(1)} %get-tuple-element.31.refs_3_), channel_id=1, source_target_pairs={{0,2},{1,3},{2,0},{3,1},{4,6},{5,7},{6,4},{7,5},{8,10},{9,11},{10,... | collective-permute-start | bytes 98312 | tf_op jit(solution)/shard_map/ppermute | solution.py:447
  36.7 9.9 %collective-permute-start.15 = (bf16[256,2304]{1,0:T(8,128)(2,1)S(1)}, bf16[256,2304]{1,0:T(8,128)(2,1)S(1)}, u32[]{:S(2)}, u32[]{:S(2)}) collective-permute-start(bf16[256,2304]{1,0:T(8,128)(2,1)S(1)} %get-tuple-element.34.refs_0_), channel_id=1, source_target_pairs={{0,1},{1,0},{2,3},{3,2},{4,5},{5,4},{6,7},{7,6},{8,9},{9,8},{10,11... | collective-permute-start | bytes 3538952 | tf_op jit(solution)/shard_map/ppermute | solution.py:22
  36.7 9.2 %collective-permute-start.16 = (bf16[64,2304]{1,0:T(8,128)(2,1)S(1)}, bf16[64,2304]{1,0:T(8,128)(2,1)S(1)}, u32[]{:S(2)}, u32[]{:S(2)}) collective-permute-start(bf16[64,2304]{1,0:T(8,128)(2,1)S(1)} %get-tuple-element.35), channel_id=1, source_target_pairs={{0,4},{1,3},{4,8},{5,1},{8,12},{9,5},{12,14},{13,9},{14,10},{15,13... | collective-permute-start | bytes 884744 | tf_op jit(solution)/shard_map/ppermute | solution.py:460
  37.1 8.8 %collective-permute-start.19 = (bf16[128,128]{1,0:T(8,128)(2,1)S(1)}, bf16[128,128]{1,0:T(8,128)(2,1)S(1)}, u32[]{:S(2)}, u32[]{:S(2)}) collective-permute-start(bf16[128,128]{1,0:T(8,128)(2,1)S(1)} %get-tuple-element.33.refs_5_), channel_id=1, source_target_pairs={{0,4},{1,5},{2,6},{3,7},{4,8},{5,9},{6,10},{7,11},{8,12},{9,13},{1... | collective-permute-start | bytes 98312 | tf_op jit(solution)/shard_map/ppermute | solution.py:456
  38.4 7.5 %collective-permute-start.18 = (bf16[128,128]{1,0:T(8,128)(2,1)S(1)}, bf16[128,128]{1,0:T(8,128)(2,1)S(1)}, u32[]{:S(2)}, u32[]{:S(2)}) collective-permute-start(bf16[128,128]{1,0:T(8,128)(2,1)S(1)} %get-tuple-element.33.refs_5_), channel_id=1, source_target_pairs={{0,8},{1,9},{2,10},{3,11},{4,12},{5,13},{6,14},{7,15},{8,0},{9,1},... | collective-permute-start | bytes 98312 | tf_op jit(solution)/shard_map/ppermute | solution.py:456
  40.1 5.8 %collective-permute-start.17 = (bf16[128,128]{1,0:T(8,128)(2,1)S(1)}, bf16[128,128]{1,0:T(8,128)(2,1)S(1)}, u32[]{:S(2)}, u32[]{:S(2)}) collective-permute-start(bf16[128,128]{1,0:T(8,128)(2,1)S(1)} %get-tuple-element.33.refs_5_), channel_id=1, source_target_pairs={{0,12},{1,13},{2,14},{3,15},{4,0},{5,1},{6,2},{7,3},{8,4},{9,5},{1... | collective-permute-start | bytes 98312 | tf_op jit(solution)/shard_map/ppermute | solution.py:456
  46.0 3.6 %collective-permute-start.20 = (bf16[64,2304]{1,0:T(8,128)(2,1)S(1)}, bf16[64,2304]{1,0:T(8,128)(2,1)S(1)}, u32[]{:S(2)}, u32[]{:S(2)}) collective-permute-start(bf16[64,2304]{1,0:T(8,128)(2,1)S(1)} %shard_map.75.refs_3_.refs_2_), channel_id=1, source_target_pairs={{0,1},{1,0},{2,3},{3,2},{4,5},{5,4},{6,7},{7,6},{8,9},{9,8},{10,11... | collective-permute-start | bytes 884744 | tf_op jit(solution)/shard_map/ppermute | solution.py:22
  46.1 3.5 %collective-permute-start.21 = (bf16[128,128]{1,0:T(8,128)(2,1)S(1)}, bf16[128,128]{1,0:T(8,128)(2,1)S(1)}, u32[]{:S(2)}, u32[]{:S(2)}) collective-permute-start(bf16[128,128]{1,0:T(8,128)(2,1)S(1)} %get-tuple-element.37.refs_1_), channel_id=1, source_target_pairs={{0,1},{1,0},{2,3},{3,2},{4,5},{5,4},{6,7},{7,6},{8,9},{9,8},{10,11... | collective-permute-start | bytes 98312 | tf_op jit(solution)/shard_map/ppermute | solution.py:22
  (3 other events, 11.3 us)

commit v12 on v11

--- a/solution.py
+++ b/solution.py
@@ -209,12 +209,20 @@
     return max(rows, 128)
 
 
-def assemble_core(ref, chips, rows, held):
+def assemble_core(ref, chips, rows, held, skip=0, first=0):
     depth = ref.shape[1]
     for i in range(chips):
         for k in range(CHUNKS):
-            at = (i * CHUNKS + k) * rows
-            held[i * rows : (i + 1) * rows, k * depth : (k + 1) * depth] = ref[at : at + rows, :]
+            at = ((skip + i) * CHUNKS + k) * rows
+            held[first + i * rows : first + (i + 1) * rows, k * depth : (k + 1) * depth] = ref[at : at + rows, :]
+
+
+def interleave(rows, chips, mine, others, base, at):
+    c = lax.axis_index("adapter")
+    for i in range(chips):
+        here = slice(i * rows, (i + 1) * rows)
+        for core, value in ((c, mine[here]), (1 - c, others[here])):
+            base[pl.ds(pl.multiple_of((2 * i + core) * rows, rows), rows), at] = value
 
 
 def core_kernel(rows, ref, *refs):
@@ -226,33 +234,38 @@
         base[:, at] = multiply(held, weights, at)[: base.shape[0]]
 
 
-def both_kernel(rows, ref, mine, *refs):
-    *weights, base, held = refs
-    chips = base.shape[0] // (2 * rows)
-    c = lax.axis_index("adapter")
-    assemble_core(ref, chips, rows, held)
+def near_base_kernel(rows, near, mid, swapped, mine, mid_rows, weight, base, mid_base, held):
+    assemble_core(swapped, near, rows, held)
+    assemble_core(mid_rows, mid, rows, held, 0, near * rows)
     columns = tile_width(base.shape[1])
     for j in range(0, base.shape[1], columns):
         at = slice(j, j + columns)
-        tile = multiply(held, weights, at)
-        for i in range(chips):
-            here = slice(i * rows, (i + 1) * rows)
-            for core, value in ((c, mine[here, at]), (1 - c, tile[here])):
-                base[pl.ds(pl.multiple_of((2 * i + core) * rows, rows), rows), at] = value
-
-
-def core_rows(ref, chips, rows, weights, after, mine=None):
-    total, depth, width = rows * chips, sum(w.shape[0] for w in weights), weights[0].shape[1]
-    (base,) = call(
-        functools.partial(core_kernel if mine is None else both_kernel, rows),
-        [ref] + ([] if mine is None else [mine]) + weights,
+        tile = multiply(held, [weight], at)
+        interleave(rows, near, mine[: near * rows, at], tile, base, at)
+        mid_base[:, at] = tile[near * rows : (near + mid) * rows]
+
+
+def late_base_kernel(rows, mid, far, swapped, mine, weight, base, far_base, held):
+    assemble_core(swapped, mid + far, rows, held)
+    columns = tile_width(base.shape[1])
+    for j in range(0, base.shape[1], columns):
+        at = slice(j, j + columns)
+        tile = multiply(held, [weight], at)
+        interleave(rows, mid, mine[:, at], tile, base, at)
+        far_base[:, at] = tile[mid * rows : (mid + far) * rows]
+
+
+def product(kernel, arrays, weight, after, total, outs):
+    (depth, width), total = weight.shape, full_rows(total)
+    return call(
+        kernel,
+        [*arrays, weight],
         after,
-        [((total if mine is None else 2 * total, width), jnp.float32)],
-        [pltpu.VMEM((full_rows(total), depth), jnp.bfloat16)],
+        [((rows, width), jnp.float32) for rows in outs],
+        [pltpu.VMEM((total, depth), jnp.bfloat16)],
         limit=8 + (2 * total * depth >> 20),
         flops=2 * total * depth * width,
     )
-    return base
 
 
 def cast_kernel(source, out):
@@ -307,11 +320,9 @@
     return total
 
 
-def finish_kernel(n, rows, groups, skipped, *refs):
-    count = len(groups) - 1
-    bases, refs = refs[:count], refs[count:]
-    mine, others, weight, own, other, up_ref, adapters_ref, live_ref = refs[:8]
-    out_ref, held, shrink, block, adapters, live, sems, small_sems = refs[8 + skipped :]
+def finish_kernel(n, rows, groups, *refs):
+    near_base, mid_base, far_base, late_rows, mine, others, weight, own, other, up_ref = refs[:10]
+    adapters_ref, live_ref, out_ref, held, shrink, far_rows, block, adapters, live, sems, small_sems = refs[10:]
     lookups = [
         pltpu.make_async_copy(source, to, small_sems.at[k])
         for k, (source, to) in enumerate(((adapters_ref, adapters), (live_ref, live)))
@@ -321,57 +332,89 @@
     c = lax.axis_index("adapter")
     chip_rows, rank = 2 * rows, up_ref.shape[1]
     tiles, _, columns = block.shape
+    _, mid, far, _ = (len(group) for group in groups)
     assemble([(mine, others)], [1], rows, held)
+    assemble_core(late_rows, far, rows, held, mid, chip_rows)
     for t in range(n):
         i, k = t % (n // 2), t // (n // 2)
         for ref, core in ((own, c), (other, 1 - c)):
             part = ref[i * rows : (i + 1) * rows, k * rank : (k + 1) * rank]
             shrink[t, pl.ds(pl.multiple_of(core * rows, rows), rows), :] = part.astype(jnp.bfloat16)
-    places = [
-        (distance, base, i * chip_rows)
-        for base, distances in zip([*bases, None], groups)
-        for i, distance in enumerate(distances)
-    ]
     for lookup in lookups:
         lookup.wait()
+    early = [(base, i) for base, group in ((near_base, groups[0]), (mid_base, groups[1])) for i in range(len(group))]
+    sources = [distance for group in groups for distance in group]
     copies = []
-    for j in range(tiles):
+
+    def put(j, which, value_of):
         at = slice(j * columns, (j + 1) * columns)
-        last = multiply(held, [weight], at)
-        for i, (distance, base, row) in enumerate(places):
-            chip = chip_at(distance, n)
-            first = chip * chip_rows
+        for i in which:
+            first = chip_at(sources[i], n) * chip_rows
             of_block = first // BLOCK
-            delta = jnp.dot(shrink[chip], up_ref[adapters[of_block], :, at], preferred_element_type=jnp.float32)
+            delta = jnp.dot(
+                shrink[chip_at(sources[i], n)],
+                up_ref[adapters[of_block], :, at],
+                preferred_element_type=jnp.float32,
+            )
             index = lax.broadcasted_iota(jnp.int32, delta.shape, 0) + (first - of_block * BLOCK)
-            value = last[:chip_rows] if base is None else base[row : row + chip_rows, at]
-            place = pl.ds(i * chip_rows, chip_rows)
-            block[j, place, :] = jnp.where(index < live[of_block], value + delta, 0.0).astype(out_ref.dtype)
+            value = jnp.where(index < live[of_block], value_of(i, at) + delta, 0.0)
+            block[j, i * chip_rows : (i + 1) * chip_rows, :] = value.astype(out_ref.dtype)
+
+    def send(j, which):
+        for i in which:
+            first = pl.multiple_of(chip_at(sources[i], n) * chip_rows, chip_rows)
             copies.append(
                 pltpu.make_async_copy(
-                    block.at[j, place, :],
-                    out_ref.at[pl.ds(pl.multiple_of(first, chip_rows), chip_rows), pl.ds(j * columns, columns)],
+                    block.at[j, pl.ds(i * chip_rows, chip_rows), :],
+                    out_ref.at[pl.ds(first, chip_rows), pl.ds(j * columns, columns)],
                     sems.at[j, i],
                 )
             )
             copies[-1].start()
+
+    def early_value(i, at):
+        base, k = early[i]
+        return base[k * chip_rows : (k + 1) * chip_rows, at]
+
+    begun, rest = range(len(early)), range(len(early), n)
+    tile = None
+    for j in range(tiles + 1):
+        done, tile = tile, multiply(held, [weight], slice(j * columns, (j + 1) * columns)) if j < tiles else None
+        if j < tiles:
+            put(j, begun, early_value)
+        if done is not None:
+            at = slice((j - 1) * columns, j * columns)
+            own_far = done[chip_rows : chip_rows + far * rows]
+            interleave(rows, far, own_far, far_base[:, at], far_rows, slice(0, columns))
+
+            def rest_value(i, at, done=done):
+                k = i - len(early)
+                return far_rows[k * chip_rows : (k + 1) * chip_rows, :] if k < far else done[:chip_rows]
+
+            put(j - 1, rest, rest_value)
+        if j < tiles:
+            send(j, begun)
+        if done is not None:
+            send(j - 1, rest)
     for copy in copies:
         copy.wait()
 
 
-def finish(n, rows, groups, lookups, bases, last_pair, weight, sums, up, after):
+def finish(n, rows, groups, lookups, bases, late, weight, sums, up):
     (rank, width), depth = up.shape[1:], weight.shape[0]
     total, columns = 2 * n * rows, tile_width(width)
-    arrays = [*bases, *last_pair, weight, *sums, up]
-    held = full_rows(2 * rows)
+    arrays = [*bases, *late, weight, *sums, up]
+    far = len(groups[2])
+    held = full_rows((2 + far) * rows)
     return pl.pallas_call(
-        functools.partial(finish_kernel, n, rows, groups, len(after)),
+        functools.partial(finish_kernel, n, rows, groups),
         out_shape=jax.ShapeDtypeStruct((total, width), jnp.bfloat16),
-        in_specs=whole(len(arrays)) + [pl.BlockSpec(memory_space=pl.ANY)] * (len(lookups) + len(after)),
+        in_specs=whole(len(arrays)) + [pl.BlockSpec(memory_space=pl.ANY)] * len(lookups),
         out_specs=pl.BlockSpec(memory_space=pl.ANY),
         scratch_shapes=[
             pltpu.VMEM((held, depth), jnp.bfloat16),
             pltpu.VMEM((n, 2 * rows, rank), jnp.bfloat16),
+            pltpu.VMEM((2 * far * rows, columns), jnp.float32),
             pltpu.VMEM((width // columns, total, columns), jnp.bfloat16),
             *(pltpu.SMEM(x.shape, x.dtype) for x in lookups),
             pltpu.SemaphoreType.DMA((width // columns, n)),
@@ -381,7 +424,7 @@
         cost_estimate=pl.CostEstimate(
             flops=2 * held * depth * width, bytes_accessed=2 * total * width, transcendentals=0
         ),
-    )(*in_vmem(arrays), *lookups, *after)
+    )(*in_vmem(arrays), *lookups)
 
 
 def on_device(n, tokens, weight, down, up, adapter_per_block, rows_per_block):
@@ -419,9 +462,9 @@
     )
 
     up_way, down_way = chunks[:CHUNKS], chunks[CHUNKS:]
-    weights = [weight]
     near_swapped = swap_cores(near_rows, n)
-    mine = core_rows(near_rows, len(near), rows, weights, [])
+    own = len(near) * rows
+    (mine,) = product(functools.partial(core_kernel, rows), [near_rows], weight, [], own, [own])
     (up,) = call(cast_kernel, [up], [mine], [(up.shape, bf16)])
     arrived = []
     for _ in range(2, last - 1):
@@ -443,35 +486,47 @@
         ],
         outside=[adapters],
     )
-    bases = [core_rows(near_swapped, len(near), rows, weights, [rounded], mine)]
+    near_base, mine = product(
+        functools.partial(near_base_kernel, rows, len(near), len(mid)),
+        [near_swapped, mine, mid_rows],
+        weight,
+        [rounded],
+        own + len(mid) * rows,
+        [2 * own, len(mid) * rows],
+    )
     total, rounded = call(add_kernel, [total, lax.ppermute(rounded, AXES, y_perm(n))], [], sums)
     up_way, down_way = ring_hop(up_way, down_way, n)
-    late_rows, turned = join([mid_rows, *up_way, *down_way], [rounded, *bases], 1)
-
-    late = mid + far
+    late_rows, turned = join([mid_rows, *up_way, *down_way], [rounded, near_base], 1)
+
     late_swapped = swap_cores(late_rows, n)
-    mine = core_rows(late_rows, len(late), rows, weights, [])
     total, rounded = call(
         add_kernel,
         [total] + [lax.ppermute(rounded, AXES, z_perm(n, shift)) for shift in range(1, n // 2)],
         [],
         sums,
     )
-    (last_rows,) = join([lax.ppermute(turned, AXES, ring_perm(n, 1, -1))], [rounded, mine])
-
-    bases.append(core_rows(late_swapped, len(late), rows, weights, [last_rows], mine))
+    (last_rows,) = join([lax.ppermute(turned, AXES, ring_perm(n, 1, -1))], [rounded])
     last_pair = (last_rows, swap_cores(last_rows, n))
+
+    late = len(mid) + len(far)
+    mid_base, far_base = product(
+        functools.partial(late_base_kernel, rows, len(mid), len(far)),
+        [late_swapped, mine],
+        weight,
+        [last_rows],
+        late * rows,
+        [2 * len(mid) * rows, len(far) * rows],
+    )
     return finish(
         n,
         rows,
-        [near, late, [last]],
+        [near, mid, far, [last]],
         [adapters, rows_per_block],
-        bases,
-        last_pair,
+        [near_base, mid_base, far_base],
+        [late_rows, *last_pair],
         weight,
         [total, swap_cores(rounded, n)],
         up,
-        [],
     )
 
 

time: 55.1 us -> 54.6 us (level)
  Pallas kernels: 19.7 us -> 17.8 us
  waiting for transfers between devices: 7.44 us -> 8.82 us
    pallas_call x12 -> x11, Pallas kernels: 13.1 us -> 10.9 us  [call(): pl.pallas_call(body, out_shape=[pltpu.VMEM(shape, dtype) for shape, dtype...]
    ppermute x3, waiting for transfers between devices: 0.01 us -> 2.06 us  [on_device(): lax.ppermute(rounded, AXES, z_perm(n, shift))]
    ppermute x1, waiting for transfers between devices: 1.11 us -> 0.44 us  [on_device(): lax.ppermute(rounded, AXES, y_perm(n))]
  transfers between devices with their start and end apart: 22 -> 22, of which waited for: 5 -> 8; matrix products, arithmetic and copies ran while one was open for 0% -> 0% of each run, Pallas kernels for 26% -> 22%
where the time goes in v12:
time: 54.6 us; the launch traced here: 54.4 us
  starting transfers between devices  27.4 us (50%)
  Pallas kernels  17.8 us (33%)
  waiting for transfers between devices  8.82 us (16%)
    pallas_call x11, Pallas kernels, call(): pl.pallas_call(body, out_shape=[pltpu.VMEM(shape, dtype) for shape, dtype...  10.9 us
    ppermute x3, starting transfers between devices, on_device(): lax.ppermute(x, AXES, ring_perm(n, d))  8.88 us
    ppermute x5, starting transfers between devices, ring_hop(): lax.ppermute(x, AXES, ring_perm(n, -1))  7.11 us
    ppermute x3, starting transfers between devices, on_device(): lax.ppermute(rounded, AXES, z_perm(n, shift))  5.84 us
    pallas_call x1, Pallas kernels, finish(): pl.pallas_call(functools.partial(finish_kernel, n, rows, groups), out_sha...  5.66 us
    ppermute x3, waiting for transfers between devices, on_device(): lax.ppermute(x, AXES, ring_perm(n, d))  4.39 us
    ppermute x5, starting transfers between devices, ring_hop(): lax.ppermute(x, AXES, ring_perm(n, 1))  3.42 us
    ppermute x3, waiting for transfers between devices, on_device(): lax.ppermute(rounded, AXES, z_perm(n, shift))  2.06 us
  transfers between devices with their start and end apart: 22, of which 8 were waited for; matrix products, arithmetic and copies ran while one was open for 0% of the time, Pallas kernels for 22%

profile of v12, /device:TPU:0, one launch (start us, length us, event | category | flops | bytes accessed | tf_op | source)
XLA Modules:
  0.0 54.4 jit_solution(18304404106972502802)
XLA Ops:
  0.0 3.0 %collective-permute-start.1 = (bf16[32,4608]{1,0:T(8,128)(2,1)}, bf16[32,4608]{1,0:T(8,128)(2,1)S(1)}, u32[]{:S(2)}, u32[]{:S(2)}) collective-permute-start(bf16[32,4608]{1,0:T(8,128)(2,1)} %refs_0_.4), channel_id=1, source_target_pairs={{0,2},{1,3},{4,0},{5,1},{8,4},{9,5},{12,8},{13,9},{14,12},{15,13},... | collective-permute-start | bytes 884744 | tf_op jit(solution)/shard_map/ppermute | solution.py:55
  3.0 1.3 %shard_map.64 = (bf16[2,64,640]{2,1,0:T(8,128)(2,1)S(1)}, bf16[32,640]{1,0:T(8,128)(2,1)S(1)}, bf16[32,640]{1,0:T(8,128)(2,1)S(1)}, bf16[32,640]{1,0:T(8,128)(2,1)S(1)}) custom-call(bf16[32,4608]{1,0:T(8,128)(2,1)} %refs_0_.4, f32[2,64,576]{2,1,0:T(8,128)} %bitcast.4, bf16[4608,2304]{1,0:T(8,128)(2,1)} %refs_6_.1, f32[4,64,2304]{2,1,0:T(8,128)} %refs_0_.5), custom_call_target="tpu_custom_call" | custom-call | tf_op jit(solution)/shard_map/pallas_call | solution.py:285
  4.3 4.0 %collective-permute-start.2 = (bf16[32,640]{1,0:T(8,128)(2,1)S(1)}, bf16[32,640]{1,0:T(8,128)(2,1)S(1)}, u32[]{:S(2)}, u32[]{:S(2)}) collective-permute-start(bf16[32,640]{1,0:T(8,128)(2,1)S(1)} %get-tuple-element.27), channel_id=1, source_target_pairs={{0,10},{1,11},{4,6},{5,7},{8,2},{9,3},{12,0},{13,1},{14,4},{15,5},... | collective-permute-start | bytes 122888 | tf_op jit(solution)/shard_map/ppermute | solution.py:454
  8.5 4.7 %collective-permute-start.4 = (bf16[32,640]{1,0:T(8,128)(2,1)S(1)}, bf16[32,640]{1,0:T(8,128)(2,1)S(1)}, u32[]{:S(2)}, u32[]{:S(2)}) collective-permute-start(bf16[32,640]{1,0:T(8,128)(2,1)S(1)} %get-tuple-element.29), channel_id=1, source_target_pairs={{0,14},{1,15},{4,10},{5,11},{8,6},{9,7},{12,2},{13,3},{14,0},{15,1... | collective-permute-start | bytes 122888 | tf_op jit(solution)/shard_map/ppermute | solution.py:454
  13.2 1.1 %collective-permute-done.2.refs_4_.refs_2_ = bf16[32,640]{1,0:T(8,128)(2,1)S(1)} collective-permute-done((bf16[32,640]{1,0:T(8,128)(2,1)S(1)}, bf16[32,640]{1,0:T(8,128)(2,1)S(1)}, u32[]{:S(2)}, u32[]{:S(2)}) %collective-permute-start.2) | collective-permute-done | bytes 40992 | tf_op jit(solution)/shard_map/ppermute | solution.py:454
  14.3 3.3 %collective-permute-done.3.refs_5_.refs_3_ = bf16[32,640]{1,0:T(8,128)(2,1)S(1)} collective-permute-done((bf16[32,640]{1,0:T(8,128)(2,1)S(1)}, bf16[32,640]{1,0:T(8,128)(2,1)S(1)}, u32[]{:S(2)}, u32[]{:S(2)}) %collective-permute-start.3) | collective-permute-done | bytes 40992 | tf_op jit(solution)/shard_map/ppermute | solution.py:454
  17.9 1.0 %collective-permute-start.6 = (bf16[32,2304]{1,0:T(8,128)(2,1)S(1)}, bf16[32,2304]{1,0:T(8,128)(2,1)S(1)}, u32[]{:S(2)}, u32[]{:S(2)}) collective-permute-start(bf16[32,2304]{1,0:T(8,128)(2,1)S(1)} %get-tuple-element.31), channel_id=1, source_target_pairs={{0,4},{1,5},{4,8},{5,9},{8,12},{9,13},{12,14},{13,15},{14,10},{15,... | collective-permute-start | bytes 442376 | tf_op jit(solution)/shard_map/ppermute | solution.py:55
  19.2 1.7 %collective-permute-start.8 = (bf16[32,2304]{1,0:T(8,128)(2,1)S(1)}, bf16[32,2304]{1,0:T(8,128)(2,1)S(1)}, u32[]{:S(2)}, u32[]{:S(2)}) collective-permute-start(bf16[32,2304]{1,0:T(8,128)(2,1)S(1)} %get-tuple-element.33), channel_id=1, source_target_pairs={{0,2},{1,3},{4,0},{5,1},{8,4},{9,5},{12,8},{13,9},{14,12},{15,13},... | collective-permute-start | bytes 442376 | tf_op jit(solution)/shard_map/ppermute | solution.py:55
  20.9 1.0 %collective-permute-start.9 = (bf16[32,2304]{1,0:T(8,128)(2,1)S(1)}, bf16[32,2304]{1,0:T(8,128)(2,1)S(1)}, u32[]{:S(2)}, u32[]{:S(2)}) collective-permute-start(bf16[32,2304]{1,0:T(8,128)(2,1)S(1)} %get-tuple-element.34), channel_id=1, source_target_pairs={{0,2},{1,3},{4,0},{5,1},{8,4},{9,5},{12,8},{13,9},{14,12},{15,13},... | collective-permute-start | bytes 442376 | tf_op jit(solution)/shard_map/ppermute | solution.py:55
  22.0 3.0 %shard_map.66.refs_1_.refs_4_ = f32[96,2304]{1,0:T(8,128)S(1)} custom-call(bf16[256,2304]{1,0:T(8,128)(2,1)S(1)} %get-tuple-element.30.refs_0_, bf16[4608,2304]{1,0:T(8,128)(2,1)S(1)} %copy-done), custom_call_target="tpu_custom_call" | custom-call | flops 2717908992 | tf_op jit(solution)/shard_map/pallas_call | solution.py:98
  25.1 1.0 %collective-permute-start.10 = (bf16[32,2304]{1,0:T(8,128)(2,1)S(1)}, bf16[32,2304]{1,0:T(8,128)(2,1)S(1)}, u32[]{:S(2)}, u32[]{:S(2)}) collective-permute-start(bf16[32,2304]{1,0:T(8,128)(2,1)S(1)} %collective-permute-done.6.refs_0_), channel_id=1, source_target_pairs={{0,4},{1,5},{4,8},{5,9},{8,12},{9,13},{12,14},{13,15},{14,10},{15,... | collective-permute-start | bytes 442376 | tf_op jit(solution)/shard_map/ppermute | solution.py:55
  26.2 1.2 %collective-permute-done.7.refs_1_ = bf16[32,2304]{1,0:T(8,128)(2,1)S(1)} collective-permute-done((bf16[32,2304]{1,0:T(8,128)(2,1)S(1)}, bf16[32,2304]{1,0:T(8,128)(2,1)S(1)}, u32[]{:S(2)}, u32[]{:S(2)}) %collective-permute-start.7) | collective-permute-done | bytes 147488 | tf_op jit(solution)/shard_map/ppermute | solution.py:55
  27.4 1.0 %collective-permute-start.11 = (bf16[32,2304]{1,0:T(8,128)(2,1)S(1)}, bf16[32,2304]{1,0:T(8,128)(2,1)S(1)}, u32[]{:S(2)}, u32[]{:S(2)}) collective-permute-start(bf16[32,2304]{1,0:T(8,128)(2,1)S(1)} %collective-permute-done.7.refs_1_), channel_id=1, source_target_pairs={{0,4},{1,5},{4,8},{5,9},{8,12},{9,13},{12,14},{13,15},{14,10},{15,... | collective-permute-start | bytes 442376 | tf_op jit(solution)/shard_map/ppermute | solution.py:55
  28.4 1.0 %collective-permute-start.12 = (bf16[32,2304]{1,0:T(8,128)(2,1)S(1)}, bf16[32,2304]{1,0:T(8,128)(2,1)S(1)}, u32[]{:S(2)}, u32[]{:S(2)}) collective-permute-start(bf16[32,2304]{1,0:T(8,128)(2,1)S(1)} %collective-permute-done.8.refs_2_), channel_id=1, source_target_pairs={{0,2},{1,3},{4,0},{5,1},{8,4},{9,5},{12,8},{13,9},{14,12},{15,13},... | collective-permute-start | bytes 442376 | tf_op jit(solution)/shard_map/ppermute | solution.py:55
  29.8 0.8 %shard_map.69 = (f32[128,128]{1,0:T(8,128)S(1)}, bf16[128,128]{1,0:T(8,128)(2,1)S(1)}) custom-call(bf16[256,2304]{1,0:T(8,128)(2,1)S(1)} %get-tuple-element.30.refs_0_, bf16[128,2304]{1,0:T(8,128)(2,1)S(1)} %shard_map.68.refs_1_.refs_2_.refs_0_, bf16[32,640]{1,0:T(8,128)(2,1)S(1)} %collective-permute-done.2.refs_4_.refs_2_, ...), custom_call_target="tpu_custom_call" | custom-call | tf_op jit(solution)/shard_map/pallas_call | solution.py:98
  30.6 1.1 %collective-permute-start.14 = (bf16[128,128]{1,0:T(8,128)(2,1)S(1)}, bf16[128,128]{1,0:T(8,128)(2,1)S(1)}, u32[]{:S(2)}, u32[]{:S(2)}) collective-permute-start(bf16[128,128]{1,0:T(8,128)(2,1)S(1)} %get-tuple-element.35.refs_4_), channel_id=1, source_target_pairs={{0,2},{1,3},{2,0},{3,1},{4,6},{5,7},{6,4},{7,5},{8,10},{9,11},{10,... | collective-permute-start | bytes 98312 | tf_op jit(solution)/shard_map/ppermute | solution.py:497
  31.7 3.7 %shard_map.70 = (f32[192,2304]{1,0:T(8,128)S(1)}, f32[64,2304]{1,0:T(8,128)S(1)}) custom-call(bf16[256,2304]{1,0:T(8,128)(2,1)S(1)} %collective-permute-done.5.refs_6_.refs_0_, f32[96,2304]{1,0:T(8,128)S(1)} %shard_map.66.refs_1_.refs_4_, bf16[128,2304]{1,0:T(8,128)(2,1)S(1)} %shard_map.68.refs_1_.refs_2_.refs_0_, bf16[4608,2304]{1,0:T(8,128)(2,1)S(1)} %copy-done, ...), custom_call_target="tpu_custom_call" | custom-call | flops 3397386240 | tf_op jit(solution)/shard_map/pallas_call | solution.py:98
  35.9 0.7 %collective-permute-done.13.refs_4_ = bf16[32,2304]{1,0:T(8,128)(2,1)S(1)} collective-permute-done((bf16[32,2304]{1,0:T(8,128)(2,1)S(1)}, bf16[32,2304]{1,0:T(8,128)(2,1)S(1)}, u32[]{:S(2)}, u32[]{:S(2)}) %collective-permute-start.13) | collective-permute-done | bytes 147488 | tf_op jit(solution)/shard_map/ppermute | solution.py:55
  37.1 1.3 %collective-permute-start.19 = (bf16[128,128]{1,0:T(8,128)(2,1)S(1)}, bf16[128,128]{1,0:T(8,128)(2,1)S(1)}, u32[]{:S(2)}, u32[]{:S(2)}) collective-permute-start(bf16[128,128]{1,0:T(8,128)(2,1)S(1)} %get-tuple-element.38.refs_5_), channel_id=1, source_target_pairs={{0,4},{1,5},{2,6},{3,7},{4,8},{5,9},{6,10},{7,11},{8,12},{9,13},{1... | collective-permute-start | bytes 98312 | tf_op jit(solution)/shard_map/ppermute | solution.py:504
  38.4 1.7 %collective-permute-start.18 = (bf16[128,128]{1,0:T(8,128)(2,1)S(1)}, bf16[128,128]{1,0:T(8,128)(2,1)S(1)}, u32[]{:S(2)}, u32[]{:S(2)}) collective-permute-start(bf16[128,128]{1,0:T(8,128)(2,1)S(1)} %get-tuple-element.38.refs_5_), channel_id=1, source_target_pairs={{0,8},{1,9},{2,10},{3,11},{4,12},{5,13},{6,14},{7,15},{8,0},{9,1},... | collective-permute-start | bytes 98312 | tf_op jit(solution)/shard_map/ppermute | solution.py:504
  40.1 2.8 %collective-permute-start.17 = (bf16[128,128]{1,0:T(8,128)(2,1)S(1)}, bf16[128,128]{1,0:T(8,128)(2,1)S(1)}, u32[]{:S(2)}, u32[]{:S(2)}) collective-permute-start(bf16[128,128]{1,0:T(8,128)(2,1)S(1)} %get-tuple-element.38.refs_5_), channel_id=1, source_target_pairs={{0,12},{1,13},{2,14},{3,15},{4,0},{5,1},{6,2},{7,3},{8,4},{9,5},{1... | collective-permute-start | bytes 98312 | tf_op jit(solution)/shard_map/ppermute | solution.py:504
  43.9 1.1 %collective-permute-done.17.refs_1_ = bf16[128,128]{1,0:T(8,128)(2,1)S(1)} collective-permute-done((bf16[128,128]{1,0:T(8,128)(2,1)S(1)}, bf16[128,128]{1,0:T(8,128)(2,1)S(1)}, u32[]{:S(2)}, u32[]{:S(2)}) %collective-permute-start.17) | collective-permute-done | bytes 32800 | tf_op jit(solution)/shard_map/ppermute | solution.py:504
  45.6 3.0 %shard_map.75 = (f32[128,2304]{1,0:T(8,128)S(1)}, f32[64,2304]{1,0:T(8,128)S(1)}) custom-call(bf16[256,2304]{1,0:T(8,128)(2,1)S(1)} %collective-permute-done.15.refs_0_, f32[64,2304]{1,0:T(8,128)S(1)} %get-tuple-element.40.refs_1_, bf16[4608,2304]{1,0:T(8,128)(2,1)S(1)} %copy-done, bf16[64,2304]{1,0:T(8,128)(2,1)S(1)} %shard_map.74.refs_3_.refs_4_), custom_call_target="tpu_custom_call" | custom-call | flops 2717908992 | tf_op jit(solution)/shard_map/pallas_call | solution.py:98
  48.6 5.7 %shard_map.76 = bf16[512,2304]{1,0:T(8,128)(2,1)} custom-call(f32[192,2304]{1,0:T(8,128)S(1)} %get-tuple-element.36.refs_6_.refs_0_, f32[128,2304]{1,0:T(8,128)S(1)} %get-tuple-element.44.refs_1_, f32[64,2304]{1,0:T(8,128)S(1)} %get-tuple-element.45.refs_2_, bf16[256,2304]{1,0:T(8,128)(2,1)S(1)} %get-tuple-element.39.refs_3_, ...), custom_call_target="tpu_custom_call" | custom-call | flops 2717908992 | bytes 2359296 | tf_op jit(solution)/shard_map/pallas_call | solution.py:409
  (43 shorter events, 3.7 us)
Async XLA Ops:
  0.0 17.6 %collective-permute-start.1 = (bf16[32,4608]{1,0:T(8,128)(2,1)}, bf16[32,4608]{1,0:T(8,128)(2,1)S(1)}, u32[]{:S(2)}, u32[]{:S(2)}) collective-permute-start(bf16[32,4608]{1,0:T(8,128)(2,1)} %refs_0_.4), channel_id=1, source_target_pairs={{0,2},{1,3},{4,0},{5,1},{8,4},{9,5},{12,8},{13,9},{14,12},{15,13},... | collective-permute-start | bytes 884744 | tf_op jit(solution)/shard_map/ppermute | solution.py:55
  3.0 14.7 %collective-permute-start = (bf16[32,4608]{1,0:T(8,128)(2,1)}, bf16[32,4608]{1,0:T(8,128)(2,1)S(1)}, u32[]{:S(2)}, u32[]{:S(2)}) collective-permute-start(bf16[32,4608]{1,0:T(8,128)(2,1)} %refs_0_.4), channel_id=1, source_target_pairs={{0,4},{1,5},{4,8},{5,9},{8,12},{9,13},{12,14},{13,15},{14,10},{15,... | collective-permute-start | bytes 884744 | tf_op jit(solution)/shard_map/ppermute | solution.py:55
  3.0 14.6 %copy-start.2 = (bf16[32,4608]{1,0:T(8,128)(2,1)S(1)}, bf16[32,4608]{1,0:T(8,128)(2,1)}, u32[]{:S(2)}) copy-start(bf16[32,4608]{1,0:T(8,128)(2,1)} %refs_0_.4) | copy-start | bytes 884740
  3.0 18.9 %copy-start = (bf16[4608,2304]{1,0:T(8,128)(2,1)S(1)}, bf16[4608,2304]{1,0:T(8,128)(2,1)}, u32[]{:S(2)}) copy-start(bf16[4608,2304]{1,0:T(8,128)(2,1)} %refs_6_.1) | copy-start | bytes 63700996
  4.3 9.9 %collective-permute-start.2 = (bf16[32,640]{1,0:T(8,128)(2,1)S(1)}, bf16[32,640]{1,0:T(8,128)(2,1)S(1)}, u32[]{:S(2)}, u32[]{:S(2)}) collective-permute-start(bf16[32,640]{1,0:T(8,128)(2,1)S(1)} %get-tuple-element.27), channel_id=1, source_target_pairs={{0,10},{1,11},{4,6},{5,7},{8,2},{9,3},{12,0},{13,1},{14,4},{15,5},... | collective-permute-start | bytes 122888 | tf_op jit(solution)/shard_map/ppermute | solution.py:454
  8.4 9.2 %collective-permute-start.3 = (bf16[32,640]{1,0:T(8,128)(2,1)S(1)}, bf16[32,640]{1,0:T(8,128)(2,1)S(1)}, u32[]{:S(2)}, u32[]{:S(2)}) collective-permute-start(bf16[32,640]{1,0:T(8,128)(2,1)S(1)} %get-tuple-element.28), channel_id=1, source_target_pairs={{0,12},{1,13},{4,14},{5,15},{8,10},{9,11},{12,6},{13,7},{14,2},{15... | collective-permute-start | bytes 122888 | tf_op jit(solution)/shard_map/ppermute | solution.py:454
  8.5 9.1 %collective-permute-start.4 = (bf16[32,640]{1,0:T(8,128)(2,1)S(1)}, bf16[32,640]{1,0:T(8,128)(2,1)S(1)}, u32[]{:S(2)}, u32[]{:S(2)}) collective-permute-start(bf16[32,640]{1,0:T(8,128)(2,1)S(1)} %get-tuple-element.29), channel_id=1, source_target_pairs={{0,14},{1,15},{4,10},{5,11},{8,6},{9,7},{12,2},{13,3},{14,0},{15,1... | collective-permute-start | bytes 122888 | tf_op jit(solution)/shard_map/ppermute | solution.py:454
  17.8 12.0 %collective-permute-start.5 = (bf16[256,2304]{1,0:T(8,128)(2,1)S(1)}, bf16[256,2304]{1,0:T(8,128)(2,1)S(1)}, u32[]{:S(2)}, u32[]{:S(2)}) collective-permute-start(bf16[256,2304]{1,0:T(8,128)(2,1)S(1)} %get-tuple-element.30.refs_0_), channel_id=1, source_target_pairs={{0,1},{1,0},{2,3},{3,2},{4,5},{5,4},{6,7},{7,6},{8,9},{9,8},{10,11... | collective-permute-start | bytes 3538952 | tf_op jit(solution)/shard_map/ppermute | solution.py:22
  17.9 7.3 %collective-permute-start.6 = (bf16[32,2304]{1,0:T(8,128)(2,1)S(1)}, bf16[32,2304]{1,0:T(8,128)(2,1)S(1)}, u32[]{:S(2)}, u32[]{:S(2)}) collective-permute-start(bf16[32,2304]{1,0:T(8,128)(2,1)S(1)} %get-tuple-element.31), channel_id=1, source_target_pairs={{0,4},{1,5},{4,8},{5,9},{8,12},{9,13},{12,14},{13,15},{14,10},{15,... | collective-permute-start | bytes 442376 | tf_op jit(solution)/shard_map/ppermute | solution.py:55
  18.9 8.5 %collective-permute-start.7 = (bf16[32,2304]{1,0:T(8,128)(2,1)S(1)}, bf16[32,2304]{1,0:T(8,128)(2,1)S(1)}, u32[]{:S(2)}, u32[]{:S(2)}) collective-permute-start(bf16[32,2304]{1,0:T(8,128)(2,1)S(1)} %get-tuple-element.32), channel_id=1, source_target_pairs={{0,4},{1,5},{4,8},{5,9},{8,12},{9,13},{12,14},{13,15},{14,10},{15,... | collective-permute-start | bytes 442376 | tf_op jit(solution)/shard_map/ppermute | solution.py:55
  19.2 9.2 %collective-permute-start.8 = (bf16[32,2304]{1,0:T(8,128)(2,1)S(1)}, bf16[32,2304]{1,0:T(8,128)(2,1)S(1)}, u32[]{:S(2)}, u32[]{:S(2)}) collective-permute-start(bf16[32,2304]{1,0:T(8,128)(2,1)S(1)} %get-tuple-element.33), channel_id=1, source_target_pairs={{0,2},{1,3},{4,0},{5,1},{8,4},{9,5},{12,8},{13,9},{14,12},{15,13},... | collective-permute-start | bytes 442376 | tf_op jit(solution)/shard_map/ppermute | solution.py:55
  20.9 8.5 %collective-permute-start.9 = (bf16[32,2304]{1,0:T(8,128)(2,1)S(1)}, bf16[32,2304]{1,0:T(8,128)(2,1)S(1)}, u32[]{:S(2)}, u32[]{:S(2)}) collective-permute-start(bf16[32,2304]{1,0:T(8,128)(2,1)S(1)} %get-tuple-element.34), channel_id=1, source_target_pairs={{0,2},{1,3},{4,0},{5,1},{8,4},{9,5},{12,8},{13,9},{14,12},{15,13},... | collective-permute-start | bytes 442376 | tf_op jit(solution)/shard_map/ppermute | solution.py:55
  25.1 10.7 %collective-permute-start.10 = (bf16[32,2304]{1,0:T(8,128)(2,1)S(1)}, bf16[32,2304]{1,0:T(8,128)(2,1)S(1)}, u32[]{:S(2)}, u32[]{:S(2)}) collective-permute-start(bf16[32,2304]{1,0:T(8,128)(2,1)S(1)} %collective-permute-done.6.refs_0_), channel_id=1, source_target_pairs={{0,4},{1,5},{4,8},{5,9},{8,12},{9,13},{12,14},{13,15},{14,10},{15,... | collective-permute-start | bytes 442376 | tf_op jit(solution)/shard_map/ppermute | solution.py:55
  27.4 8.5 %collective-permute-start.11 = (bf16[32,2304]{1,0:T(8,128)(2,1)S(1)}, bf16[32,2304]{1,0:T(8,128)(2,1)S(1)}, u32[]{:S(2)}, u32[]{:S(2)}) collective-permute-start(bf16[32,2304]{1,0:T(8,128)(2,1)S(1)} %collective-permute-done.7.refs_1_), channel_id=1, source_target_pairs={{0,4},{1,5},{4,8},{5,9},{8,12},{9,13},{12,14},{13,15},{14,10},{15,... | collective-permute-start | bytes 442376 | tf_op jit(solution)/shard_map/ppermute | solution.py:55
  28.4 7.5 %collective-permute-start.12 = (bf16[32,2304]{1,0:T(8,128)(2,1)S(1)}, bf16[32,2304]{1,0:T(8,128)(2,1)S(1)}, u32[]{:S(2)}, u32[]{:S(2)}) collective-permute-start(bf16[32,2304]{1,0:T(8,128)(2,1)S(1)} %collective-permute-done.8.refs_2_), channel_id=1, source_target_pairs={{0,2},{1,3},{4,0},{5,1},{8,4},{9,5},{12,8},{13,9},{14,12},{15,13},... | collective-permute-start | bytes 442376 | tf_op jit(solution)/shard_map/ppermute | solution.py:55
  29.4 7.2 %collective-permute-start.13 = (bf16[32,2304]{1,0:T(8,128)(2,1)S(1)}, bf16[32,2304]{1,0:T(8,128)(2,1)S(1)}, u32[]{:S(2)}, u32[]{:S(2)}) collective-permute-start(bf16[32,2304]{1,0:T(8,128)(2,1)S(1)} %collective-permute-done.9.refs_3_), channel_id=1, source_target_pairs={{0,2},{1,3},{4,0},{5,1},{8,4},{9,5},{12,8},{13,9},{14,12},{15,13},... | collective-permute-start | bytes 442376 | tf_op jit(solution)/shard_map/ppermute | solution.py:55
  30.6 5.2 %collective-permute-start.14 = (bf16[128,128]{1,0:T(8,128)(2,1)S(1)}, bf16[128,128]{1,0:T(8,128)(2,1)S(1)}, u32[]{:S(2)}, u32[]{:S(2)}) collective-permute-start(bf16[128,128]{1,0:T(8,128)(2,1)S(1)} %get-tuple-element.35.refs_4_), channel_id=1, source_target_pairs={{0,2},{1,3},{2,0},{3,1},{4,6},{5,7},{6,4},{7,5},{8,10},{9,11},{10,... | collective-permute-start | bytes 98312 | tf_op jit(solution)/shard_map/ppermute | solution.py:497
  36.7 9.0 %collective-permute-start.15 = (bf16[256,2304]{1,0:T(8,128)(2,1)S(1)}, bf16[256,2304]{1,0:T(8,128)(2,1)S(1)}, u32[]{:S(2)}, u32[]{:S(2)}) collective-permute-start(bf16[256,2304]{1,0:T(8,128)(2,1)S(1)} %get-tuple-element.39.refs_3_), channel_id=1, source_target_pairs={{0,1},{1,0},{2,3},{3,2},{4,5},{5,4},{6,7},{7,6},{8,9},{9,8},{10,11... | collective-permute-start | bytes 3538952 | tf_op jit(solution)/shard_map/ppermute | solution.py:22
  36.7 8.3 %collective-permute-start.16 = (bf16[64,2304]{1,0:T(8,128)(2,1)S(1)}, bf16[64,2304]{1,0:T(8,128)(2,1)S(1)}, u32[]{:S(2)}, u32[]{:S(2)}) collective-permute-start(bf16[64,2304]{1,0:T(8,128)(2,1)S(1)} %get-tuple-element.41), channel_id=1, source_target_pairs={{0,4},{1,3},{4,8},{5,1},{8,12},{9,5},{12,14},{13,9},{14,10},{15,13... | collective-permute-start | bytes 884744 | tf_op jit(solution)/shard_map/ppermute | solution.py:508
  37.1 6.2 %collective-permute-start.19 = (bf16[128,128]{1,0:T(8,128)(2,1)S(1)}, bf16[128,128]{1,0:T(8,128)(2,1)S(1)}, u32[]{:S(2)}, u32[]{:S(2)}) collective-permute-start(bf16[128,128]{1,0:T(8,128)(2,1)S(1)} %get-tuple-element.38.refs_5_), channel_id=1, source_target_pairs={{0,4},{1,5},{2,6},{3,7},{4,8},{5,9},{6,10},{7,11},{8,12},{9,13},{1... | collective-permute-start | bytes 98312 | tf_op jit(solution)/shard_map/ppermute | solution.py:504
  38.4 5.5 %collective-permute-start.18 = (bf16[128,128]{1,0:T(8,128)(2,1)S(1)}, bf16[128,128]{1,0:T(8,128)(2,1)S(1)}, u32[]{:S(2)}, u32[]{:S(2)}) collective-permute-start(bf16[128,128]{1,0:T(8,128)(2,1)S(1)} %get-tuple-element.38.refs_5_), channel_id=1, source_target_pairs={{0,8},{1,9},{2,10},{3,11},{4,12},{5,13},{6,14},{7,15},{8,0},{9,1},... | collective-permute-start | bytes 98312 | tf_op jit(solution)/shard_map/ppermute | solution.py:504
  40.1 4.9 %collective-permute-start.17 = (bf16[128,128]{1,0:T(8,128)(2,1)S(1)}, bf16[128,128]{1,0:T(8,128)(2,1)S(1)}, u32[]{:S(2)}, u32[]{:S(2)}) collective-permute-start(bf16[128,128]{1,0:T(8,128)(2,1)S(1)} %get-tuple-element.38.refs_5_), channel_id=1, source_target_pairs={{0,12},{1,13},{2,14},{3,15},{4,0},{5,1},{6,2},{7,3},{8,4},{9,5},{1... | collective-permute-start | bytes 98312 | tf_op jit(solution)/shard_map/ppermute | solution.py:504
  45.0 3.6 %collective-permute-start.20 = (bf16[64,2304]{1,0:T(8,128)(2,1)S(1)}, bf16[64,2304]{1,0:T(8,128)(2,1)S(1)}, u32[]{:S(2)}, u32[]{:S(2)}) collective-permute-start(bf16[64,2304]{1,0:T(8,128)(2,1)S(1)} %shard_map.74.refs_3_.refs_4_), channel_id=1, source_target_pairs={{0,1},{1,0},{2,3},{3,2},{4,5},{5,4},{6,7},{7,6},{8,9},{9,8},{10,11... | collective-permute-start | bytes 884744 | tf_op jit(solution)/shard_map/ppermute | solution.py:22
  45.2 3.4 %collective-permute-start.21 = (bf16[128,128]{1,0:T(8,128)(2,1)S(1)}, bf16[128,128]{1,0:T(8,128)(2,1)S(1)}, u32[]{:S(2)}, u32[]{:S(2)}) collective-permute-start(bf16[128,128]{1,0:T(8,128)(2,1)S(1)} %get-tuple-element.43.refs_1_), channel_id=1, source_target_pairs={{0,1},{1,0},{2,3},{3,2},{4,5},{5,4},{6,7},{7,6},{8,9},{9,8},{10,11... | collective-permute-start | bytes 98312 | tf_op jit(solution)/shard_map/ppermute | solution.py:22
  (3 other events, 10.7 us)

commit v13 on v11

--- a/solution.py
+++ b/solution.py
@@ -327,34 +327,43 @@
         for ref, core in ((own, c), (other, 1 - c)):
             part = ref[i * rows : (i + 1) * rows, k * rank : (k + 1) * rank]
             shrink[t, pl.ds(pl.multiple_of(core * rows, rows), rows), :] = part.astype(jnp.bfloat16)
-    places = [
-        (distance, base, i * chip_rows)
-        for base, distances in zip([*bases, None], groups)
-        for i, distance in enumerate(distances)
+    early = [
+        (base, i * chip_rows) for base, group in zip(bases, groups) for i in range(len(group))
     ]
+    sources = [distance for group in groups for distance in group]
     for lookup in lookups:
         lookup.wait()
     copies = []
+
+    def put(j, i, value):
+        at = slice(j * columns, (j + 1) * columns)
+        chip = chip_at(sources[i], n)
+        first = chip * chip_rows
+        of_block = first // BLOCK
+        delta = jnp.dot(shrink[chip], up_ref[adapters[of_block], :, at], preferred_element_type=jnp.float32)
+        index = lax.broadcasted_iota(jnp.int32, delta.shape, 0) + (first - of_block * BLOCK)
+        value = jnp.where(index < live[of_block], value + delta, 0.0)
+        block[j, i * chip_rows : (i + 1) * chip_rows, :] = value.astype(out_ref.dtype)
+
+    def send(j, i):
+        first = pl.multiple_of(chip_at(sources[i], n) * chip_rows, chip_rows)
+        copies.append(
+            pltpu.make_async_copy(
+                block.at[j, pl.ds(i * chip_rows, chip_rows), :],
+                out_ref.at[pl.ds(first, chip_rows), pl.ds(j * columns, columns)],
+                sems.at[j, i],
+            )
+        )
+        copies[-1].start()
+
     for j in range(tiles):
         at = slice(j * columns, (j + 1) * columns)
-        last = multiply(held, [weight], at)
-        for i, (distance, base, row) in enumerate(places):
-            chip = chip_at(distance, n)
-            first = chip * chip_rows
-            of_block = first // BLOCK
-            delta = jnp.dot(shrink[chip], up_ref[adapters[of_block], :, at], preferred_element_type=jnp.float32)
-            index = lax.broadcasted_iota(jnp.int32, delta.shape, 0) + (first - of_block * BLOCK)
-            value = last[:chip_rows] if base is None else base[row : row + chip_rows, at]
-            place = pl.ds(i * chip_rows, chip_rows)
-            block[j, place, :] = jnp.where(index < live[of_block], value + delta, 0.0).astype(out_ref.dtype)
-            copies.append(
-                pltpu.make_async_copy(
-                    block.at[j, place, :],
-                    out_ref.at[pl.ds(pl.multiple_of(first, chip_rows), chip_rows), pl.ds(j * columns, columns)],
-                    sems.at[j, i],
-                )
-            )
-            copies[-1].start()
+        tile = multiply(held, [weight], at)
+        for i, (base, row) in enumerate(early):
+            put(j, i, base[row : row + chip_rows, at])
+        put(j, n - 1, tile[:chip_rows])
+        for i in range(n):
+            send(j, i)
     for copy in copies:
         copy.wait()
 

time: 55.1 us -> 55.3 us (level)
  no operation moved by 1% of the time
where the time goes in v13:
time: 55.3 us; the launch traced here: 55.2 us
  starting transfers between devices  27.4 us (50%)
  Pallas kernels  19.9 us (36%)
  waiting for transfers between devices  7.44 us (13%)
    pallas_call x12, Pallas kernels, call(): pl.pallas_call(body, out_shape=[pltpu.VMEM(shape, dtype) for shape, dtype...  13.1 us
    ppermute x3, starting transfers between devices, on_device(): lax.ppermute(x, AXES, ring_perm(n, d))  8.88 us
    ppermute x5, starting transfers between devices, ring_hop(): lax.ppermute(x, AXES, ring_perm(n, -1))  7.11 us
    ppermute x3, starting transfers between devices, on_device(): lax.ppermute(rounded, AXES, z_perm(n, shift))  5.84 us
    pallas_call x1, Pallas kernels, finish(): pl.pallas_call(functools.partial(finish_kernel, n, rows, groups, len(afte...  5.44 us
    ppermute x3, waiting for transfers between devices, on_device(): lax.ppermute(x, AXES, ring_perm(n, d))  4.39 us
    ppermute x5, starting transfers between devices, ring_hop(): lax.ppermute(x, AXES, ring_perm(n, 1))  3.42 us
    pallas_call x1, Pallas kernels, prepare(): pl.pallas_call(body, out_shape=[pltpu.VMEM(shape, dtype) for shape, dtype...  1.31 us
  transfers between devices with their start and end apart: 22, of which 5 were waited for; matrix products, arithmetic and copies ran while one was open for 0% of the time, Pallas kernels for 26%

profile of v13, /device:TPU:0, one launch (start us, length us, event | category | flops | bytes accessed | tf_op | source)
XLA Modules:
  0.0 55.2 jit_solution(7335601010328903502)
XLA Ops:
  0.0 3.0 %collective-permute-start.1 = (bf16[32,4608]{1,0:T(8,128)(2,1)}, bf16[32,4608]{1,0:T(8,128)(2,1)S(1)}, u32[]{:S(2)}, u32[]{:S(2)}) collective-permute-start(bf16[32,4608]{1,0:T(8,128)(2,1)} %refs_0_.4), channel_id=1, source_target_pairs={{0,2},{1,3},{4,0},{5,1},{8,4},{9,5},{12,8},{13,9},{14,12},{15,13},... | collective-permute-start | bytes 884744 | tf_op jit(solution)/shard_map/ppermute | solution.py:55
  3.0 1.3 %shard_map.64 = (bf16[2,64,640]{2,1,0:T(8,128)(2,1)S(1)}, bf16[32,640]{1,0:T(8,128)(2,1)S(1)}, bf16[32,640]{1,0:T(8,128)(2,1)S(1)}, bf16[32,640]{1,0:T(8,128)(2,1)S(1)}) custom-call(bf16[32,4608]{1,0:T(8,128)(2,1)} %refs_0_.4, f32[2,64,576]{2,1,0:T(8,128)} %bitcast.4, bf16[4608,2304]{1,0:T(8,128)(2,1)} %refs_4_.1, f32[4,64,2304]{2,1,0:T(8,128)} %refs_0_.5), custom_call_target="tpu_custom_call" | custom-call | tf_op jit(solution)/shard_map/pallas_call | solution.py:272
  4.3 4.0 %collective-permute-start.2 = (bf16[32,640]{1,0:T(8,128)(2,1)S(1)}, bf16[32,640]{1,0:T(8,128)(2,1)S(1)}, u32[]{:S(2)}, u32[]{:S(2)}) collective-permute-start(bf16[32,640]{1,0:T(8,128)(2,1)S(1)} %get-tuple-element.23), channel_id=1, source_target_pairs={{0,10},{1,11},{4,6},{5,7},{8,2},{9,3},{12,0},{13,1},{14,4},{15,5},... | collective-permute-start | bytes 122888 | tf_op jit(solution)/shard_map/ppermute | solution.py:420
  8.5 4.7 %collective-permute-start.4 = (bf16[32,640]{1,0:T(8,128)(2,1)S(1)}, bf16[32,640]{1,0:T(8,128)(2,1)S(1)}, u32[]{:S(2)}, u32[]{:S(2)}) collective-permute-start(bf16[32,640]{1,0:T(8,128)(2,1)S(1)} %get-tuple-element.25), channel_id=1, source_target_pairs={{0,14},{1,15},{4,10},{5,11},{8,6},{9,7},{12,2},{13,3},{14,0},{15,1... | collective-permute-start | bytes 122888 | tf_op jit(solution)/shard_map/ppermute | solution.py:420
  13.2 1.1 %collective-permute-done.2.refs_4_.refs_2_ = bf16[32,640]{1,0:T(8,128)(2,1)S(1)} collective-permute-done((bf16[32,640]{1,0:T(8,128)(2,1)S(1)}, bf16[32,640]{1,0:T(8,128)(2,1)S(1)}, u32[]{:S(2)}, u32[]{:S(2)}) %collective-permute-start.2) | collective-permute-done | bytes 40992 | tf_op jit(solution)/shard_map/ppermute | solution.py:420
  14.3 3.3 %collective-permute-done.3.refs_5_.refs_3_ = bf16[32,640]{1,0:T(8,128)(2,1)S(1)} collective-permute-done((bf16[32,640]{1,0:T(8,128)(2,1)S(1)}, bf16[32,640]{1,0:T(8,128)(2,1)S(1)}, u32[]{:S(2)}, u32[]{:S(2)}) %collective-permute-start.3) | collective-permute-done | bytes 40992 | tf_op jit(solution)/shard_map/ppermute | solution.py:420
  17.9 1.0 %collective-permute-start.6 = (bf16[32,2304]{1,0:T(8,128)(2,1)S(1)}, bf16[32,2304]{1,0:T(8,128)(2,1)S(1)}, u32[]{:S(2)}, u32[]{:S(2)}) collective-permute-start(bf16[32,2304]{1,0:T(8,128)(2,1)S(1)} %get-tuple-element.27), channel_id=1, source_target_pairs={{0,4},{1,5},{4,8},{5,9},{8,12},{9,13},{12,14},{13,15},{14,10},{15,... | collective-permute-start | bytes 442376 | tf_op jit(solution)/shard_map/ppermute | solution.py:55
  19.2 1.7 %collective-permute-start.8 = (bf16[32,2304]{1,0:T(8,128)(2,1)S(1)}, bf16[32,2304]{1,0:T(8,128)(2,1)S(1)}, u32[]{:S(2)}, u32[]{:S(2)}) collective-permute-start(bf16[32,2304]{1,0:T(8,128)(2,1)S(1)} %get-tuple-element.29), channel_id=1, source_target_pairs={{0,2},{1,3},{4,0},{5,1},{8,4},{9,5},{12,8},{13,9},{14,12},{15,13},... | collective-permute-start | bytes 442376 | tf_op jit(solution)/shard_map/ppermute | solution.py:55
  20.9 1.0 %collective-permute-start.9 = (bf16[32,2304]{1,0:T(8,128)(2,1)S(1)}, bf16[32,2304]{1,0:T(8,128)(2,1)S(1)}, u32[]{:S(2)}, u32[]{:S(2)}) collective-permute-start(bf16[32,2304]{1,0:T(8,128)(2,1)S(1)} %get-tuple-element.30), channel_id=1, source_target_pairs={{0,2},{1,3},{4,0},{5,1},{8,4},{9,5},{12,8},{13,9},{14,12},{15,13},... | collective-permute-start | bytes 442376 | tf_op jit(solution)/shard_map/ppermute | solution.py:55
  22.0 3.0 %shard_map.66.refs_1_.refs_4_ = f32[96,2304]{1,0:T(8,128)S(1)} custom-call(bf16[256,2304]{1,0:T(8,128)(2,1)S(1)} %get-tuple-element.26.refs_0_, bf16[4608,2304]{1,0:T(8,128)(2,1)S(1)} %copy-done), custom_call_target="tpu_custom_call" | custom-call | flops 2038431744 | tf_op jit(solution)/shard_map/pallas_call | solution.py:98
  25.1 1.0 %collective-permute-start.10 = (bf16[32,2304]{1,0:T(8,128)(2,1)S(1)}, bf16[32,2304]{1,0:T(8,128)(2,1)S(1)}, u32[]{:S(2)}, u32[]{:S(2)}) collective-permute-start(bf16[32,2304]{1,0:T(8,128)(2,1)S(1)} %collective-permute-done.6.refs_0_), channel_id=1, source_target_pairs={{0,4},{1,5},{4,8},{5,9},{8,12},{9,13},{12,14},{13,15},{14,10},{15,... | collective-permute-start | bytes 442376 | tf_op jit(solution)/shard_map/ppermute | solution.py:55
  26.2 1.2 %collective-permute-done.7.refs_1_ = bf16[32,2304]{1,0:T(8,128)(2,1)S(1)} collective-permute-done((bf16[32,2304]{1,0:T(8,128)(2,1)S(1)}, bf16[32,2304]{1,0:T(8,128)(2,1)S(1)}, u32[]{:S(2)}, u32[]{:S(2)}) %collective-permute-start.7) | collective-permute-done | bytes 147488 | tf_op jit(solution)/shard_map/ppermute | solution.py:55
  27.4 1.0 %collective-permute-start.11 = (bf16[32,2304]{1,0:T(8,128)(2,1)S(1)}, bf16[32,2304]{1,0:T(8,128)(2,1)S(1)}, u32[]{:S(2)}, u32[]{:S(2)}) collective-permute-start(bf16[32,2304]{1,0:T(8,128)(2,1)S(1)} %collective-permute-done.7.refs_1_), channel_id=1, source_target_pairs={{0,4},{1,5},{4,8},{5,9},{8,12},{9,13},{12,14},{13,15},{14,10},{15,... | collective-permute-start | bytes 442376 | tf_op jit(solution)/shard_map/ppermute | solution.py:55
  28.4 1.0 %collective-permute-start.12 = (bf16[32,2304]{1,0:T(8,128)(2,1)S(1)}, bf16[32,2304]{1,0:T(8,128)(2,1)S(1)}, u32[]{:S(2)}, u32[]{:S(2)}) collective-permute-start(bf16[32,2304]{1,0:T(8,128)(2,1)S(1)} %collective-permute-done.8.refs_2_), channel_id=1, source_target_pairs={{0,2},{1,3},{4,0},{5,1},{8,4},{9,5},{12,8},{13,9},{14,12},{15,13},... | collective-permute-start | bytes 442376 | tf_op jit(solution)/shard_map/ppermute | solution.py:55
  29.8 0.8 %shard_map.69 = (f32[128,128]{1,0:T(8,128)S(1)}, bf16[128,128]{1,0:T(8,128)(2,1)S(1)}) custom-call(bf16[256,2304]{1,0:T(8,128)(2,1)S(1)} %get-tuple-element.26.refs_0_, bf16[128,2304]{1,0:T(8,128)(2,1)S(1)} %shard_map.68.refs_1_.refs_0_, bf16[32,640]{1,0:T(8,128)(2,1)S(1)} %collective-permute-done.2.refs_4_.refs_2_, ...), custom_call_target="tpu_custom_call" | custom-call | tf_op jit(solution)/shard_map/pallas_call | solution.py:98
  30.6 1.1 %collective-permute-start.14 = (bf16[128,128]{1,0:T(8,128)(2,1)S(1)}, bf16[128,128]{1,0:T(8,128)(2,1)S(1)}, u32[]{:S(2)}, u32[]{:S(2)}) collective-permute-start(bf16[128,128]{1,0:T(8,128)(2,1)S(1)} %get-tuple-element.31.refs_3_), channel_id=1, source_target_pairs={{0,2},{1,3},{2,0},{3,1},{4,6},{5,7},{6,4},{7,5},{8,10},{9,11},{10,... | collective-permute-start | bytes 98312 | tf_op jit(solution)/shard_map/ppermute | solution.py:456
  31.7 3.0 %shard_map.70.refs_6_.refs_0_ = f32[192,2304]{1,0:T(8,128)S(1)} custom-call(bf16[256,2304]{1,0:T(8,128)(2,1)S(1)} %collective-permute-done.5.refs_6_.refs_0_, f32[96,2304]{1,0:T(8,128)S(1)} %shard_map.66.refs_1_.refs_4_, bf16[4608,2304]{1,0:T(8,128)(2,1)S(1)} %copy-done, bf16[128,128]{1,0:T(8,128)(2,1)S(1)} %get-tuple-element.31.refs_3_), custom_call_target="tpu_custom_call" | custom-call | flops 2038431744 | tf_op jit(solution)/shard_map/pallas_call | solution.py:98
  34.7 1.1 %collective-permute-done.14.refs_1_ = bf16[128,128]{1,0:T(8,128)(2,1)S(1)} collective-permute-done((bf16[128,128]{1,0:T(8,128)(2,1)S(1)}, bf16[128,128]{1,0:T(8,128)(2,1)S(1)}, u32[]{:S(2)}, u32[]{:S(2)}) %collective-permute-start.14) | collective-permute-done | bytes 32800 | tf_op jit(solution)/shard_map/ppermute | solution.py:456
  37.1 1.3 %collective-permute-start.19 = (bf16[128,128]{1,0:T(8,128)(2,1)S(1)}, bf16[128,128]{1,0:T(8,128)(2,1)S(1)}, u32[]{:S(2)}, u32[]{:S(2)}) collective-permute-start(bf16[128,128]{1,0:T(8,128)(2,1)S(1)} %get-tuple-element.33.refs_5_), channel_id=1, source_target_pairs={{0,4},{1,5},{2,6},{3,7},{4,8},{5,9},{6,10},{7,11},{8,12},{9,13},{1... | collective-permute-start | bytes 98312 | tf_op jit(solution)/shard_map/ppermute | solution.py:465
  38.4 1.7 %collective-permute-start.18 = (bf16[128,128]{1,0:T(8,128)(2,1)S(1)}, bf16[128,128]{1,0:T(8,128)(2,1)S(1)}, u32[]{:S(2)}, u32[]{:S(2)}) collective-permute-start(bf16[128,128]{1,0:T(8,128)(2,1)S(1)} %get-tuple-element.33.refs_5_), channel_id=1, source_target_pairs={{0,8},{1,9},{2,10},{3,11},{4,12},{5,13},{6,14},{7,15},{8,0},{9,1},... | collective-permute-start | bytes 98312 | tf_op jit(solution)/shard_map/ppermute | solution.py:465
  40.1 2.8 %collective-permute-start.17 = (bf16[128,128]{1,0:T(8,128)(2,1)S(1)}, bf16[128,128]{1,0:T(8,128)(2,1)S(1)}, u32[]{:S(2)}, u32[]{:S(2)}) collective-permute-start(bf16[128,128]{1,0:T(8,128)(2,1)S(1)} %get-tuple-element.33.refs_5_), channel_id=1, source_target_pairs={{0,12},{1,13},{2,14},{3,15},{4,0},{5,1},{6,2},{7,3},{8,4},{9,5},{1... | collective-permute-start | bytes 98312 | tf_op jit(solution)/shard_map/ppermute | solution.py:465
  42.9 2.9 %shard_map.73.refs_2_.refs_1_ = f32[128,2304]{1,0:T(8,128)S(1)} custom-call(bf16[256,2304]{1,0:T(8,128)(2,1)S(1)} %get-tuple-element.34.refs_0_, bf16[4608,2304]{1,0:T(8,128)(2,1)S(1)} %copy-done), custom_call_target="tpu_custom_call" | custom-call | flops 2717908992 | tf_op jit(solution)/shard_map/pallas_call | solution.py:98
  46.6 3.0 %shard_map.76.refs_1_ = f32[256,2304]{1,0:T(8,128)S(1)} custom-call(bf16[256,2304]{1,0:T(8,128)(2,1)S(1)} %collective-permute-done.15.refs_0_, f32[128,2304]{1,0:T(8,128)S(1)} %shard_map.73.refs_2_.refs_1_, bf16[4608,2304]{1,0:T(8,128)(2,1)S(1)} %copy-done, bf16[64,2304]{1,0:T(8,128)(2,1)S(1)} %shard_map.75.refs_3_.refs_2_), custom_call_target="tpu_custom_call" | custom-call | flops 2717908992 | tf_op jit(solution)/shard_map/pallas_call | solution.py:98
  49.6 5.4 %shard_map.77 = bf16[512,2304]{1,0:T(8,128)(2,1)} custom-call(f32[192,2304]{1,0:T(8,128)S(1)} %shard_map.70.refs_6_.refs_0_, f32[256,2304]{1,0:T(8,128)S(1)} %shard_map.76.refs_1_, bf16[64,2304]{1,0:T(8,128)(2,1)S(1)} %shard_map.75.refs_3_.refs_2_, bf16[64,2304]{1,0:T(8,128)(2,1)S(1)} %collective-permute-done.20.refs_3_, bf16[4608,2304]{1,0:T(8,128)(2,1)S(1)} %copy-done, ...), custom_call_target="tpu_custom_call" | custom-call | flops 2717908992 | bytes 2359296 | tf_op jit(solution)/shard_map/pallas_call | solution.py:376
  (44 shorter events, 3.0 us)
Async XLA Ops:
  0.0 17.6 %collective-permute-start.1 = (bf16[32,4608]{1,0:T(8,128)(2,1)}, bf16[32,4608]{1,0:T(8,128)(2,1)S(1)}, u32[]{:S(2)}, u32[]{:S(2)}) collective-permute-start(bf16[32,4608]{1,0:T(8,128)(2,1)} %refs_0_.4), channel_id=1, source_target_pairs={{0,2},{1,3},{4,0},{5,1},{8,4},{9,5},{12,8},{13,9},{14,12},{15,13},... | collective-permute-start | bytes 884744 | tf_op jit(solution)/shard_map/ppermute | solution.py:55
  3.0 14.7 %collective-permute-start = (bf16[32,4608]{1,0:T(8,128)(2,1)}, bf16[32,4608]{1,0:T(8,128)(2,1)S(1)}, u32[]{:S(2)}, u32[]{:S(2)}) collective-permute-start(bf16[32,4608]{1,0:T(8,128)(2,1)} %refs_0_.4), channel_id=1, source_target_pairs={{0,4},{1,5},{4,8},{5,9},{8,12},{9,13},{12,14},{13,15},{14,10},{15,... | collective-permute-start | bytes 884744 | tf_op jit(solution)/shard_map/ppermute | solution.py:55
  3.0 14.6 %copy-start.2 = (bf16[32,4608]{1,0:T(8,128)(2,1)S(1)}, bf16[32,4608]{1,0:T(8,128)(2,1)}, u32[]{:S(2)}) copy-start(bf16[32,4608]{1,0:T(8,128)(2,1)} %refs_0_.4) | copy-start | bytes 884740
  3.0 18.9 %copy-start = (bf16[4608,2304]{1,0:T(8,128)(2,1)S(1)}, bf16[4608,2304]{1,0:T(8,128)(2,1)}, u32[]{:S(2)}) copy-start(bf16[4608,2304]{1,0:T(8,128)(2,1)} %refs_4_.1) | copy-start | bytes 63700996
  4.3 9.9 %collective-permute-start.2 = (bf16[32,640]{1,0:T(8,128)(2,1)S(1)}, bf16[32,640]{1,0:T(8,128)(2,1)S(1)}, u32[]{:S(2)}, u32[]{:S(2)}) collective-permute-start(bf16[32,640]{1,0:T(8,128)(2,1)S(1)} %get-tuple-element.23), channel_id=1, source_target_pairs={{0,10},{1,11},{4,6},{5,7},{8,2},{9,3},{12,0},{13,1},{14,4},{15,5},... | collective-permute-start | bytes 122888 | tf_op jit(solution)/shard_map/ppermute | solution.py:420
  8.4 9.2 %collective-permute-start.3 = (bf16[32,640]{1,0:T(8,128)(2,1)S(1)}, bf16[32,640]{1,0:T(8,128)(2,1)S(1)}, u32[]{:S(2)}, u32[]{:S(2)}) collective-permute-start(bf16[32,640]{1,0:T(8,128)(2,1)S(1)} %get-tuple-element.24), channel_id=1, source_target_pairs={{0,12},{1,13},{4,14},{5,15},{8,10},{9,11},{12,6},{13,7},{14,2},{15... | collective-permute-start | bytes 122888 | tf_op jit(solution)/shard_map/ppermute | solution.py:420
  8.5 9.1 %collective-permute-start.4 = (bf16[32,640]{1,0:T(8,128)(2,1)S(1)}, bf16[32,640]{1,0:T(8,128)(2,1)S(1)}, u32[]{:S(2)}, u32[]{:S(2)}) collective-permute-start(bf16[32,640]{1,0:T(8,128)(2,1)S(1)} %get-tuple-element.25), channel_id=1, source_target_pairs={{0,14},{1,15},{4,10},{5,11},{8,6},{9,7},{12,2},{13,3},{14,0},{15,1... | collective-permute-start | bytes 122888 | tf_op jit(solution)/shard_map/ppermute | solution.py:420
  17.8 12.0 %collective-permute-start.5 = (bf16[256,2304]{1,0:T(8,128)(2,1)S(1)}, bf16[256,2304]{1,0:T(8,128)(2,1)S(1)}, u32[]{:S(2)}, u32[]{:S(2)}) collective-permute-start(bf16[256,2304]{1,0:T(8,128)(2,1)S(1)} %get-tuple-element.26.refs_0_), channel_id=1, source_target_pairs={{0,1},{1,0},{2,3},{3,2},{4,5},{5,4},{6,7},{7,6},{8,9},{9,8},{10,11... | collective-permute-start | bytes 3538952 | tf_op jit(solution)/shard_map/ppermute | solution.py:22
  17.9 7.3 %collective-permute-start.6 = (bf16[32,2304]{1,0:T(8,128)(2,1)S(1)}, bf16[32,2304]{1,0:T(8,128)(2,1)S(1)}, u32[]{:S(2)}, u32[]{:S(2)}) collective-permute-start(bf16[32,2304]{1,0:T(8,128)(2,1)S(1)} %get-tuple-element.27), channel_id=1, source_target_pairs={{0,4},{1,5},{4,8},{5,9},{8,12},{9,13},{12,14},{13,15},{14,10},{15,... | collective-permute-start | bytes 442376 | tf_op jit(solution)/shard_map/ppermute | solution.py:55
  18.9 8.5 %collective-permute-start.7 = (bf16[32,2304]{1,0:T(8,128)(2,1)S(1)}, bf16[32,2304]{1,0:T(8,128)(2,1)S(1)}, u32[]{:S(2)}, u32[]{:S(2)}) collective-permute-start(bf16[32,2304]{1,0:T(8,128)(2,1)S(1)} %get-tuple-element.28), channel_id=1, source_target_pairs={{0,4},{1,5},{4,8},{5,9},{8,12},{9,13},{12,14},{13,15},{14,10},{15,... | collective-permute-start | bytes 442376 | tf_op jit(solution)/shard_map/ppermute | solution.py:55
  19.2 9.2 %collective-permute-start.8 = (bf16[32,2304]{1,0:T(8,128)(2,1)S(1)}, bf16[32,2304]{1,0:T(8,128)(2,1)S(1)}, u32[]{:S(2)}, u32[]{:S(2)}) collective-permute-start(bf16[32,2304]{1,0:T(8,128)(2,1)S(1)} %get-tuple-element.29), channel_id=1, source_target_pairs={{0,2},{1,3},{4,0},{5,1},{8,4},{9,5},{12,8},{13,9},{14,12},{15,13},... | collective-permute-start | bytes 442376 | tf_op jit(solution)/shard_map/ppermute | solution.py:55
  20.9 8.5 %collective-permute-start.9 = (bf16[32,2304]{1,0:T(8,128)(2,1)S(1)}, bf16[32,2304]{1,0:T(8,128)(2,1)S(1)}, u32[]{:S(2)}, u32[]{:S(2)}) collective-permute-start(bf16[32,2304]{1,0:T(8,128)(2,1)S(1)} %get-tuple-element.30), channel_id=1, source_target_pairs={{0,2},{1,3},{4,0},{5,1},{8,4},{9,5},{12,8},{13,9},{14,12},{15,13},... | collective-permute-start | bytes 442376 | tf_op jit(solution)/shard_map/ppermute | solution.py:55
  25.1 10.7 %collective-permute-start.10 = (bf16[32,2304]{1,0:T(8,128)(2,1)S(1)}, bf16[32,2304]{1,0:T(8,128)(2,1)S(1)}, u32[]{:S(2)}, u32[]{:S(2)}) collective-permute-start(bf16[32,2304]{1,0:T(8,128)(2,1)S(1)} %collective-permute-done.6.refs_0_), channel_id=1, source_target_pairs={{0,4},{1,5},{4,8},{5,9},{8,12},{9,13},{12,14},{13,15},{14,10},{15,... | collective-permute-start | bytes 442376 | tf_op jit(solution)/shard_map/ppermute | solution.py:55
  27.4 8.5 %collective-permute-start.11 = (bf16[32,2304]{1,0:T(8,128)(2,1)S(1)}, bf16[32,2304]{1,0:T(8,128)(2,1)S(1)}, u32[]{:S(2)}, u32[]{:S(2)}) collective-permute-start(bf16[32,2304]{1,0:T(8,128)(2,1)S(1)} %collective-permute-done.7.refs_1_), channel_id=1, source_target_pairs={{0,4},{1,5},{4,8},{5,9},{8,12},{9,13},{12,14},{13,15},{14,10},{15,... | collective-permute-start | bytes 442376 | tf_op jit(solution)/shard_map/ppermute | solution.py:55
  28.4 7.5 %collective-permute-start.12 = (bf16[32,2304]{1,0:T(8,128)(2,1)S(1)}, bf16[32,2304]{1,0:T(8,128)(2,1)S(1)}, u32[]{:S(2)}, u32[]{:S(2)}) collective-permute-start(bf16[32,2304]{1,0:T(8,128)(2,1)S(1)} %collective-permute-done.8.refs_2_), channel_id=1, source_target_pairs={{0,2},{1,3},{4,0},{5,1},{8,4},{9,5},{12,8},{13,9},{14,12},{15,13},... | collective-permute-start | bytes 442376 | tf_op jit(solution)/shard_map/ppermute | solution.py:55
  29.4 7.2 %collective-permute-start.13 = (bf16[32,2304]{1,0:T(8,128)(2,1)S(1)}, bf16[32,2304]{1,0:T(8,128)(2,1)S(1)}, u32[]{:S(2)}, u32[]{:S(2)}) collective-permute-start(bf16[32,2304]{1,0:T(8,128)(2,1)S(1)} %collective-permute-done.9.refs_3_), channel_id=1, source_target_pairs={{0,2},{1,3},{4,0},{5,1},{8,4},{9,5},{12,8},{13,9},{14,12},{15,13},... | collective-permute-start | bytes 442376 | tf_op jit(solution)/shard_map/ppermute | solution.py:55
  30.6 5.2 %collective-permute-start.14 = (bf16[128,128]{1,0:T(8,128)(2,1)S(1)}, bf16[128,128]{1,0:T(8,128)(2,1)S(1)}, u32[]{:S(2)}, u32[]{:S(2)}) collective-permute-start(bf16[128,128]{1,0:T(8,128)(2,1)S(1)} %get-tuple-element.31.refs_3_), channel_id=1, source_target_pairs={{0,2},{1,3},{2,0},{3,1},{4,6},{5,7},{6,4},{7,5},{8,10},{9,11},{10,... | collective-permute-start | bytes 98312 | tf_op jit(solution)/shard_map/ppermute | solution.py:456
  36.7 9.9 %collective-permute-start.15 = (bf16[256,2304]{1,0:T(8,128)(2,1)S(1)}, bf16[256,2304]{1,0:T(8,128)(2,1)S(1)}, u32[]{:S(2)}, u32[]{:S(2)}) collective-permute-start(bf16[256,2304]{1,0:T(8,128)(2,1)S(1)} %get-tuple-element.34.refs_0_), channel_id=1, source_target_pairs={{0,1},{1,0},{2,3},{3,2},{4,5},{5,4},{6,7},{7,6},{8,9},{9,8},{10,11... | collective-permute-start | bytes 3538952 | tf_op jit(solution)/shard_map/ppermute | solution.py:22
  36.7 9.2 %collective-permute-start.16 = (bf16[64,2304]{1,0:T(8,128)(2,1)S(1)}, bf16[64,2304]{1,0:T(8,128)(2,1)S(1)}, u32[]{:S(2)}, u32[]{:S(2)}) collective-permute-start(bf16[64,2304]{1,0:T(8,128)(2,1)S(1)} %get-tuple-element.35), channel_id=1, source_target_pairs={{0,4},{1,3},{4,8},{5,1},{8,12},{9,5},{12,14},{13,9},{14,10},{15,13... | collective-permute-start | bytes 884744 | tf_op jit(solution)/shard_map/ppermute | solution.py:469
  37.1 8.8 %collective-permute-start.19 = (bf16[128,128]{1,0:T(8,128)(2,1)S(1)}, bf16[128,128]{1,0:T(8,128)(2,1)S(1)}, u32[]{:S(2)}, u32[]{:S(2)}) collective-permute-start(bf16[128,128]{1,0:T(8,128)(2,1)S(1)} %get-tuple-element.33.refs_5_), channel_id=1, source_target_pairs={{0,4},{1,5},{2,6},{3,7},{4,8},{5,9},{6,10},{7,11},{8,12},{9,13},{1... | collective-permute-start | bytes 98312 | tf_op jit(solution)/shard_map/ppermute | solution.py:465
  38.4 7.5 %collective-permute-start.18 = (bf16[128,128]{1,0:T(8,128)(2,1)S(1)}, bf16[128,128]{1,0:T(8,128)(2,1)S(1)}, u32[]{:S(2)}, u32[]{:S(2)}) collective-permute-start(bf16[128,128]{1,0:T(8,128)(2,1)S(1)} %get-tuple-element.33.refs_5_), channel_id=1, source_target_pairs={{0,8},{1,9},{2,10},{3,11},{4,12},{5,13},{6,14},{7,15},{8,0},{9,1},... | collective-permute-start | bytes 98312 | tf_op jit(solution)/shard_map/ppermute | solution.py:465
  40.1 5.8 %collective-permute-start.17 = (bf16[128,128]{1,0:T(8,128)(2,1)S(1)}, bf16[128,128]{1,0:T(8,128)(2,1)S(1)}, u32[]{:S(2)}, u32[]{:S(2)}) collective-permute-start(bf16[128,128]{1,0:T(8,128)(2,1)S(1)} %get-tuple-element.33.refs_5_), channel_id=1, source_target_pairs={{0,12},{1,13},{2,14},{3,15},{4,0},{5,1},{6,2},{7,3},{8,4},{9,5},{1... | collective-permute-start | bytes 98312 | tf_op jit(solution)/shard_map/ppermute | solution.py:465
  46.0 3.6 %collective-permute-start.20 = (bf16[64,2304]{1,0:T(8,128)(2,1)S(1)}, bf16[64,2304]{1,0:T(8,128)(2,1)S(1)}, u32[]{:S(2)}, u32[]{:S(2)}) collective-permute-start(bf16[64,2304]{1,0:T(8,128)(2,1)S(1)} %shard_map.75.refs_3_.refs_2_), channel_id=1, source_target_pairs={{0,1},{1,0},{2,3},{3,2},{4,5},{5,4},{6,7},{7,6},{8,9},{9,8},{10,11... | collective-permute-start | bytes 884744 | tf_op jit(solution)/shard_map/ppermute | solution.py:22
  46.1 3.5 %collective-permute-start.21 = (bf16[128,128]{1,0:T(8,128)(2,1)S(1)}, bf16[128,128]{1,0:T(8,128)(2,1)S(1)}, u32[]{:S(2)}, u32[]{:S(2)}) collective-permute-start(bf16[128,128]{1,0:T(8,128)(2,1)S(1)} %get-tuple-element.37.refs_1_), channel_id=1, source_target_pairs={{0,1},{1,0},{2,3},{3,2},{4,5},{5,4},{6,7},{7,6},{8,9},{9,8},{10,11... | collective-permute-start | bytes 98312 | tf_op jit(solution)/shard_map/ppermute | solution.py:22
  (3 other events, 11.3 us)

commit v14 on v11

--- a/solution.py
+++ b/solution.py
@@ -145,7 +145,7 @@
 
 
 def partial_kernel(n, window, groups, far, *refs):
-    *pieces, factor, other, adapters_ref, total, rounded, adapters, x, products, parts, sem = refs
+    *pieces, factor, other, adapters_ref, total, rounded, adapters, x, stacked, products, parts, sem = refs
     lookup = pltpu.make_async_copy(adapters_ref, adapters, sem)
     lookup.start()
     pieces, received = pieces[: len(groups)], pieces[len(groups) :]
@@ -168,13 +168,19 @@
     for index in range(held):
         theirs = other[below:, index * size : (index + 1) * size]
         for core, weights in ((c, factor[index]), (1 - c, theirs)):
-            products[core * held + index] = lax.dot_general(
-                x[...], weights, (((1,), (1,)), ((), ())), preferred_element_type=jnp.float32
-            )
+            at = pl.multiple_of((core * held + index) * rank, rank)
+            stacked[pl.ds(at, rank), :] = weights
+    products[...] = lax.dot_general(
+        x[...], stacked[...], (((1,), (1,)), ((), ())), preferred_element_type=jnp.float32
+    )
     lookup.wait()
     for i, distance in enumerate(order):
         chip = chip_at(distance, n)
-        parts[chip] = products[adapters[chip * 2 * rows // BLOCK], i * rows : (i + 1) * rows, :]
+        adapter = adapters[chip * 2 * rows // BLOCK]
+        value = products[i * rows : (i + 1) * rows, :rank]
+        for k in range(1, 2 * held):
+            value = jnp.where(adapter == k, products[i * rows : (i + 1) * rows, k * rank : (k + 1) * rank], value)
+        parts[chip] = value
     pack(parts, total)
     rounded[...] = total[...].astype(jnp.bfloat16)
 
@@ -256,7 +262,9 @@
 
 
 def cast_kernel(source, out):
-    out[...] = source[...].astype(out.dtype)
+    rank = source.shape[1]
+    for adapter in range(source.shape[0]):
+        out[adapter * rank : (adapter + 1) * rank, :] = source[adapter].astype(out.dtype)
 
 
 def in_hbm(arrays):
@@ -311,7 +319,7 @@
     count = len(groups) - 1
     bases, refs = refs[:count], refs[count:]
     mine, others, weight, own, other, up_ref, adapters_ref, live_ref = refs[:8]
-    out_ref, held, shrink, block, adapters, live, sems, small_sems = refs[8 + skipped :]
+    out_ref, held, shrink, spread, block, adapters, live, sems, small_sems = refs[8 + skipped :]
     lookups = [
         pltpu.make_async_copy(source, to, small_sems.at[k])
         for k, (source, to) in enumerate(((adapters_ref, adapters), (live_ref, live)))
@@ -319,7 +327,7 @@
     for lookup in lookups:
         lookup.start()
     c = lax.axis_index("adapter")
-    chip_rows, rank = 2 * rows, up_ref.shape[1]
+    chip_rows, rank = 2 * rows, own.shape[1] // 2
     tiles, _, columns = block.shape
     assemble([(mine, others)], [1], rows, held)
     for t in range(n):
@@ -334,33 +342,44 @@
     ]
     for lookup in lookups:
         lookup.wait()
+    for i, (distance, _, _) in enumerate(places):
+        chip = chip_at(distance, n)
+        adapter = adapters[chip * chip_rows // BLOCK]
+        value = shrink[chip]
+        for k in range(up_ref.shape[0] // rank):
+            spread[i * chip_rows : (i + 1) * chip_rows, k * rank : (k + 1) * rank] = jnp.where(
+                adapter == k, value, jnp.zeros_like(value)
+            )
     copies = []
     for j in range(tiles):
         at = slice(j * columns, (j + 1) * columns)
         last = multiply(held, [weight], at)
-        for i, (distance, base, row) in enumerate(places):
-            chip = chip_at(distance, n)
-            first = chip * chip_rows
-            of_block = first // BLOCK
-            delta = jnp.dot(shrink[chip], up_ref[adapters[of_block], :, at], preferred_element_type=jnp.float32)
-            index = lax.broadcasted_iota(jnp.int32, delta.shape, 0) + (first - of_block * BLOCK)
-            value = last[:chip_rows] if base is None else base[row : row + chip_rows, at]
-            place = pl.ds(i * chip_rows, chip_rows)
-            block[j, place, :] = jnp.where(index < live[of_block], value + delta, 0.0).astype(out_ref.dtype)
-            copies.append(
-                pltpu.make_async_copy(
-                    block.at[j, place, :],
-                    out_ref.at[pl.ds(pl.multiple_of(first, chip_rows), chip_rows), pl.ds(j * columns, columns)],
-                    sems.at[j, i],
+        for pair in range(0, n, 2):
+            both = slice(pair * chip_rows, (pair + 2) * chip_rows)
+            deltas = jnp.dot(spread[both, :], up_ref[:, at], preferred_element_type=jnp.float32)
+            for i in (pair, pair + 1):
+                distance, base, row = places[i]
+                first = chip_at(distance, n) * chip_rows
+                of_block = first // BLOCK
+                delta = deltas[(i - pair) * chip_rows : (i - pair + 1) * chip_rows]
+                index = lax.broadcasted_iota(jnp.int32, delta.shape, 0) + (first - of_block * BLOCK)
+                value = last[:chip_rows] if base is None else base[row : row + chip_rows, at]
+                place = pl.ds(i * chip_rows, chip_rows)
+                block[j, place, :] = jnp.where(index < live[of_block], value + delta, 0.0).astype(out_ref.dtype)
+                copies.append(
+                    pltpu.make_async_copy(
+                        block.at[j, place, :],
+                        out_ref.at[pl.ds(pl.multiple_of(first, chip_rows), chip_rows), pl.ds(j * columns, columns)],
+                        sems.at[j, i],
+                    )
                 )
-            )
-            copies[-1].start()
+                copies[-1].start()
     for copy in copies:
         copy.wait()
 
 
 def finish(n, rows, groups, lookups, bases, last_pair, weight, sums, up, after):
-    (rank, width), depth = up.shape[1:], weight.shape[0]
+    (deep, width), depth, rank = up.shape, weight.shape[0], sums[0].shape[1] // 2
     total, columns = 2 * n * rows, tile_width(width)
     arrays = [*bases, *last_pair, weight, *sums, up]
     held = full_rows(2 * rows)
@@ -372,6 +391,7 @@
         scratch_shapes=[
             pltpu.VMEM((held, depth), jnp.bfloat16),
             pltpu.VMEM((n, 2 * rows, rank), jnp.bfloat16),
+            pltpu.VMEM((total, deep), jnp.bfloat16),
             pltpu.VMEM((width // columns, total, columns), jnp.bfloat16),
             *(pltpu.SMEM(x.shape, x.dtype) for x in lookups),
             pltpu.SemaphoreType.DMA((width // columns, n)),
@@ -422,7 +442,7 @@
     weights = [weight]
     near_swapped = swap_cores(near_rows, n)
     mine = core_rows(near_rows, len(near), rows, weights, [])
-    (up,) = call(cast_kernel, [up], [mine], [(up.shape, bf16)])
+    (up,) = call(cast_kernel, [up], [mine], [((up.shape[0] * rank, up.shape[2]), bf16)])
     arrived = []
     for _ in range(2, last - 1):
         up_way, down_way = ring_hop(up_way, down_way, n)
@@ -437,7 +457,8 @@
         [
             pltpu.SMEM(adapters.shape, jnp.int32),
             pltpu.VMEM((n * rows, window.size), bf16),
-            pltpu.VMEM((2 * held, n * rows, rank), jnp.float32),
+            pltpu.VMEM((2 * held * rank, window.size), bf16),
+            pltpu.VMEM((n * rows, 2 * held * rank), jnp.float32),
             pltpu.VMEM((n, rows, rank), jnp.float32),
             pltpu.SemaphoreType.DMA,
         ],

time: 55.1 us -> 55.1 us (level)
  no operation moved by 1% of the time
where the time goes in v14:
time: 55.1 us; the launch traced here: 55 us
  starting transfers between devices  27.4 us (50%)
  Pallas kernels  19.9 us (36%)
  waiting for transfers between devices  7.23 us (13%)
    pallas_call x12, Pallas kernels, call(): pl.pallas_call(body, out_shape=[pltpu.VMEM(shape, dtype) for shape, dtype...  13.4 us
    ppermute x3, starting transfers between devices, on_device(): lax.ppermute(x, AXES, ring_perm(n, d))  8.88 us
    ppermute x5, starting transfers between devices, ring_hop(): lax.ppermute(x, AXES, ring_perm(n, -1))  7.11 us
    ppermute x3, starting transfers between devices, on_device(): lax.ppermute(rounded, AXES, z_perm(n, shift))  5.84 us
    pallas_call x1, Pallas kernels, finish(): pl.pallas_call(functools.partial(finish_kernel, n, rows, groups, len(afte...  5.25 us
    ppermute x3, waiting for transfers between devices, on_device(): lax.ppermute(x, AXES, ring_perm(n, d))  4.39 us
    ppermute x5, starting transfers between devices, ring_hop(): lax.ppermute(x, AXES, ring_perm(n, 1))  3.42 us
    pallas_call x1, Pallas kernels, prepare(): pl.pallas_call(body, out_shape=[pltpu.VMEM(shape, dtype) for shape, dtype...  1.31 us
  transfers between devices with their start and end apart: 22, of which 5 were waited for; matrix products, arithmetic and copies ran while one was open for 0% of the time, Pallas kernels for 26%

profile of v14, /device:TPU:0, one launch (start us, length us, event | category | flops | bytes accessed | tf_op | source)
XLA Modules:
  0.0 55.0 jit_solution(7609502067281752672)
XLA Ops:
  0.0 3.0 %collective-permute-start.1 = (bf16[32,4608]{1,0:T(8,128)(2,1)}, bf16[32,4608]{1,0:T(8,128)(2,1)S(1)}, u32[]{:S(2)}, u32[]{:S(2)}) collective-permute-start(bf16[32,4608]{1,0:T(8,128)(2,1)} %refs_0_.4), channel_id=1, source_target_pairs={{0,2},{1,3},{4,0},{5,1},{8,4},{9,5},{12,8},{13,9},{14,12},{15,13},... | collective-permute-start | bytes 884744 | tf_op jit(solution)/shard_map/ppermute | solution.py:55
  3.0 1.3 %shard_map.64 = (bf16[2,64,640]{2,1,0:T(8,128)(2,1)S(1)}, bf16[32,640]{1,0:T(8,128)(2,1)S(1)}, bf16[32,640]{1,0:T(8,128)(2,1)S(1)}, bf16[32,640]{1,0:T(8,128)(2,1)S(1)}) custom-call(bf16[32,4608]{1,0:T(8,128)(2,1)} %refs_0_.4, f32[2,64,576]{2,1,0:T(8,128)} %bitcast.4, bf16[4608,2304]{1,0:T(8,128)(2,1)} %refs_4_.1, f32[4,64,2304]{2,1,0:T(8,128)} %refs_0_.5), custom_call_target="tpu_custom_call" | custom-call | tf_op jit(solution)/shard_map/pallas_call | solution.py:280
  4.3 4.0 %collective-permute-start.2 = (bf16[32,640]{1,0:T(8,128)(2,1)S(1)}, bf16[32,640]{1,0:T(8,128)(2,1)S(1)}, u32[]{:S(2)}, u32[]{:S(2)}) collective-permute-start(bf16[32,640]{1,0:T(8,128)(2,1)S(1)} %get-tuple-element.23), channel_id=1, source_target_pairs={{0,10},{1,11},{4,6},{5,7},{8,2},{9,3},{12,0},{13,1},{14,4},{15,5},... | collective-permute-start | bytes 122888 | tf_op jit(solution)/shard_map/ppermute | solution.py:431
  8.5 4.7 %collective-permute-start.4 = (bf16[32,640]{1,0:T(8,128)(2,1)S(1)}, bf16[32,640]{1,0:T(8,128)(2,1)S(1)}, u32[]{:S(2)}, u32[]{:S(2)}) collective-permute-start(bf16[32,640]{1,0:T(8,128)(2,1)S(1)} %get-tuple-element.25), channel_id=1, source_target_pairs={{0,14},{1,15},{4,10},{5,11},{8,6},{9,7},{12,2},{13,3},{14,0},{15,1... | collective-permute-start | bytes 122888 | tf_op jit(solution)/shard_map/ppermute | solution.py:431
  13.2 1.1 %collective-permute-done.2.refs_4_.refs_2_ = bf16[32,640]{1,0:T(8,128)(2,1)S(1)} collective-permute-done((bf16[32,640]{1,0:T(8,128)(2,1)S(1)}, bf16[32,640]{1,0:T(8,128)(2,1)S(1)}, u32[]{:S(2)}, u32[]{:S(2)}) %collective-permute-start.2) | collective-permute-done | bytes 40992 | tf_op jit(solution)/shard_map/ppermute | solution.py:431
  14.3 3.3 %collective-permute-done.3.refs_5_.refs_3_ = bf16[32,640]{1,0:T(8,128)(2,1)S(1)} collective-permute-done((bf16[32,640]{1,0:T(8,128)(2,1)S(1)}, bf16[32,640]{1,0:T(8,128)(2,1)S(1)}, u32[]{:S(2)}, u32[]{:S(2)}) %collective-permute-start.3) | collective-permute-done | bytes 40992 | tf_op jit(solution)/shard_map/ppermute | solution.py:431
  17.9 1.0 %collective-permute-start.6 = (bf16[32,2304]{1,0:T(8,128)(2,1)S(1)}, bf16[32,2304]{1,0:T(8,128)(2,1)S(1)}, u32[]{:S(2)}, u32[]{:S(2)}) collective-permute-start(bf16[32,2304]{1,0:T(8,128)(2,1)S(1)} %get-tuple-element.27), channel_id=1, source_target_pairs={{0,4},{1,5},{4,8},{5,9},{8,12},{9,13},{12,14},{13,15},{14,10},{15,... | collective-permute-start | bytes 442376 | tf_op jit(solution)/shard_map/ppermute | solution.py:55
  19.2 1.7 %collective-permute-start.8 = (bf16[32,2304]{1,0:T(8,128)(2,1)S(1)}, bf16[32,2304]{1,0:T(8,128)(2,1)S(1)}, u32[]{:S(2)}, u32[]{:S(2)}) collective-permute-start(bf16[32,2304]{1,0:T(8,128)(2,1)S(1)} %get-tuple-element.29), channel_id=1, source_target_pairs={{0,2},{1,3},{4,0},{5,1},{8,4},{9,5},{12,8},{13,9},{14,12},{15,13},... | collective-permute-start | bytes 442376 | tf_op jit(solution)/shard_map/ppermute | solution.py:55
  20.9 1.0 %collective-permute-start.9 = (bf16[32,2304]{1,0:T(8,128)(2,1)S(1)}, bf16[32,2304]{1,0:T(8,128)(2,1)S(1)}, u32[]{:S(2)}, u32[]{:S(2)}) collective-permute-start(bf16[32,2304]{1,0:T(8,128)(2,1)S(1)} %get-tuple-element.30), channel_id=1, source_target_pairs={{0,2},{1,3},{4,0},{5,1},{8,4},{9,5},{12,8},{13,9},{14,12},{15,13},... | collective-permute-start | bytes 442376 | tf_op jit(solution)/shard_map/ppermute | solution.py:55
  22.0 3.0 %shard_map.66.refs_1_.refs_4_ = f32[96,2304]{1,0:T(8,128)S(1)} custom-call(bf16[256,2304]{1,0:T(8,128)(2,1)S(1)} %get-tuple-element.26.refs_0_, bf16[4608,2304]{1,0:T(8,128)(2,1)S(1)} %copy-done), custom_call_target="tpu_custom_call" | custom-call | flops 2038431744 | tf_op jit(solution)/shard_map/pallas_call | solution.py:98
  25.1 1.0 %collective-permute-start.10 = (bf16[32,2304]{1,0:T(8,128)(2,1)S(1)}, bf16[32,2304]{1,0:T(8,128)(2,1)S(1)}, u32[]{:S(2)}, u32[]{:S(2)}) collective-permute-start(bf16[32,2304]{1,0:T(8,128)(2,1)S(1)} %collective-permute-done.6.refs_0_), channel_id=1, source_target_pairs={{0,4},{1,5},{4,8},{5,9},{8,12},{9,13},{12,14},{13,15},{14,10},{15,... | collective-permute-start | bytes 442376 | tf_op jit(solution)/shard_map/ppermute | solution.py:55
  26.2 1.2 %collective-permute-done.7.refs_1_ = bf16[32,2304]{1,0:T(8,128)(2,1)S(1)} collective-permute-done((bf16[32,2304]{1,0:T(8,128)(2,1)S(1)}, bf16[32,2304]{1,0:T(8,128)(2,1)S(1)}, u32[]{:S(2)}, u32[]{:S(2)}) %collective-permute-start.7) | collective-permute-done | bytes 147488 | tf_op jit(solution)/shard_map/ppermute | solution.py:55
  27.4 1.0 %collective-permute-start.11 = (bf16[32,2304]{1,0:T(8,128)(2,1)S(1)}, bf16[32,2304]{1,0:T(8,128)(2,1)S(1)}, u32[]{:S(2)}, u32[]{:S(2)}) collective-permute-start(bf16[32,2304]{1,0:T(8,128)(2,1)S(1)} %collective-permute-done.7.refs_1_), channel_id=1, source_target_pairs={{0,4},{1,5},{4,8},{5,9},{8,12},{9,13},{12,14},{13,15},{14,10},{15,... | collective-permute-start | bytes 442376 | tf_op jit(solution)/shard_map/ppermute | solution.py:55
  28.4 1.0 %collective-permute-start.12 = (bf16[32,2304]{1,0:T(8,128)(2,1)S(1)}, bf16[32,2304]{1,0:T(8,128)(2,1)S(1)}, u32[]{:S(2)}, u32[]{:S(2)}) collective-permute-start(bf16[32,2304]{1,0:T(8,128)(2,1)S(1)} %collective-permute-done.8.refs_2_), channel_id=1, source_target_pairs={{0,2},{1,3},{4,0},{5,1},{8,4},{9,5},{12,8},{13,9},{14,12},{15,13},... | collective-permute-start | bytes 442376 | tf_op jit(solution)/shard_map/ppermute | solution.py:55
  29.8 1.0 %shard_map.69 = (f32[128,128]{1,0:T(8,128)S(1)}, bf16[128,128]{1,0:T(8,128)(2,1)S(1)}) custom-call(bf16[256,2304]{1,0:T(8,128)(2,1)S(1)} %get-tuple-element.26.refs_0_, bf16[128,2304]{1,0:T(8,128)(2,1)S(1)} %shard_map.68.refs_1_.refs_0_, bf16[32,640]{1,0:T(8,128)(2,1)S(1)} %collective-permute-done.2.refs_4_.refs_2_, ...), custom_call_target="tpu_custom_call" | custom-call | tf_op jit(solution)/shard_map/pallas_call | solution.py:98
  30.8 1.1 %collective-permute-start.14 = (bf16[128,128]{1,0:T(8,128)(2,1)S(1)}, bf16[128,128]{1,0:T(8,128)(2,1)S(1)}, u32[]{:S(2)}, u32[]{:S(2)}) collective-permute-start(bf16[128,128]{1,0:T(8,128)(2,1)S(1)} %get-tuple-element.31.refs_3_), channel_id=1, source_target_pairs={{0,2},{1,3},{2,0},{3,1},{4,6},{5,7},{6,4},{7,5},{8,10},{9,11},{10,... | collective-permute-start | bytes 98312 | tf_op jit(solution)/shard_map/ppermute | solution.py:468
  31.9 3.0 %shard_map.70.refs_6_.refs_0_ = f32[192,2304]{1,0:T(8,128)S(1)} custom-call(bf16[256,2304]{1,0:T(8,128)(2,1)S(1)} %collective-permute-done.5.refs_6_.refs_0_, f32[96,2304]{1,0:T(8,128)S(1)} %shard_map.66.refs_1_.refs_4_, bf16[4608,2304]{1,0:T(8,128)(2,1)S(1)} %copy-done, bf16[128,128]{1,0:T(8,128)(2,1)S(1)} %get-tuple-element.31.refs_3_), custom_call_target="tpu_custom_call" | custom-call | flops 2038431744 | tf_op jit(solution)/shard_map/pallas_call | solution.py:98
  34.9 0.9 %collective-permute-done.14.refs_1_ = bf16[128,128]{1,0:T(8,128)(2,1)S(1)} collective-permute-done((bf16[128,128]{1,0:T(8,128)(2,1)S(1)}, bf16[128,128]{1,0:T(8,128)(2,1)S(1)}, u32[]{:S(2)}, u32[]{:S(2)}) %collective-permute-start.14) | collective-permute-done | bytes 32800 | tf_op jit(solution)/shard_map/ppermute | solution.py:468
  37.1 1.3 %collective-permute-start.19 = (bf16[128,128]{1,0:T(8,128)(2,1)S(1)}, bf16[128,128]{1,0:T(8,128)(2,1)S(1)}, u32[]{:S(2)}, u32[]{:S(2)}) collective-permute-start(bf16[128,128]{1,0:T(8,128)(2,1)S(1)} %get-tuple-element.33.refs_5_), channel_id=1, source_target_pairs={{0,4},{1,5},{2,6},{3,7},{4,8},{5,9},{6,10},{7,11},{8,12},{9,13},{1... | collective-permute-start | bytes 98312 | tf_op jit(solution)/shard_map/ppermute | solution.py:477
  38.4 1.7 %collective-permute-start.18 = (bf16[128,128]{1,0:T(8,128)(2,1)S(1)}, bf16[128,128]{1,0:T(8,128)(2,1)S(1)}, u32[]{:S(2)}, u32[]{:S(2)}) collective-permute-start(bf16[128,128]{1,0:T(8,128)(2,1)S(1)} %get-tuple-element.33.refs_5_), channel_id=1, source_target_pairs={{0,8},{1,9},{2,10},{3,11},{4,12},{5,13},{6,14},{7,15},{8,0},{9,1},... | collective-permute-start | bytes 98312 | tf_op jit(solution)/shard_map/ppermute | solution.py:477
  40.1 2.8 %collective-permute-start.17 = (bf16[128,128]{1,0:T(8,128)(2,1)S(1)}, bf16[128,128]{1,0:T(8,128)(2,1)S(1)}, u32[]{:S(2)}, u32[]{:S(2)}) collective-permute-start(bf16[128,128]{1,0:T(8,128)(2,1)S(1)} %get-tuple-element.33.refs_5_), channel_id=1, source_target_pairs={{0,12},{1,13},{2,14},{3,15},{4,0},{5,1},{6,2},{7,3},{8,4},{9,5},{1... | collective-permute-start | bytes 98312 | tf_op jit(solution)/shard_map/ppermute | solution.py:477
  42.9 2.9 %shard_map.73.refs_2_.refs_1_ = f32[128,2304]{1,0:T(8,128)S(1)} custom-call(bf16[256,2304]{1,0:T(8,128)(2,1)S(1)} %get-tuple-element.34.refs_0_, bf16[4608,2304]{1,0:T(8,128)(2,1)S(1)} %copy-done), custom_call_target="tpu_custom_call" | custom-call | flops 2717908992 | tf_op jit(solution)/shard_map/pallas_call | solution.py:98
  46.6 3.0 %shard_map.76.refs_1_ = f32[256,2304]{1,0:T(8,128)S(1)} custom-call(bf16[256,2304]{1,0:T(8,128)(2,1)S(1)} %collective-permute-done.15.refs_0_, f32[128,2304]{1,0:T(8,128)S(1)} %shard_map.73.refs_2_.refs_1_, bf16[4608,2304]{1,0:T(8,128)(2,1)S(1)} %copy-done, bf16[64,2304]{1,0:T(8,128)(2,1)S(1)} %shard_map.75.refs_3_.refs_2_), custom_call_target="tpu_custom_call" | custom-call | flops 2717908992 | tf_op jit(solution)/shard_map/pallas_call | solution.py:98
  49.6 5.3 %shard_map.77 = bf16[512,2304]{1,0:T(8,128)(2,1)} custom-call(f32[192,2304]{1,0:T(8,128)S(1)} %shard_map.70.refs_6_.refs_0_, f32[256,2304]{1,0:T(8,128)S(1)} %shard_map.76.refs_1_, bf16[64,2304]{1,0:T(8,128)(2,1)S(1)} %shard_map.75.refs_3_.refs_2_, bf16[64,2304]{1,0:T(8,128)(2,1)S(1)} %collective-permute-done.20.refs_3_, bf16[4608,2304]{1,0:T(8,128)(2,1)S(1)} %copy-done, ...), custom_call_target="tpu_custom_call" | custom-call | flops 2717908992 | bytes 2359296 | tf_op jit(solution)/shard_map/pallas_call | solution.py:386
  (44 shorter events, 3.0 us)
Async XLA Ops:
  0.0 17.6 %collective-permute-start.1 = (bf16[32,4608]{1,0:T(8,128)(2,1)}, bf16[32,4608]{1,0:T(8,128)(2,1)S(1)}, u32[]{:S(2)}, u32[]{:S(2)}) collective-permute-start(bf16[32,4608]{1,0:T(8,128)(2,1)} %refs_0_.4), channel_id=1, source_target_pairs={{0,2},{1,3},{4,0},{5,1},{8,4},{9,5},{12,8},{13,9},{14,12},{15,13},... | collective-permute-start | bytes 884744 | tf_op jit(solution)/shard_map/ppermute | solution.py:55
  3.0 14.7 %collective-permute-start = (bf16[32,4608]{1,0:T(8,128)(2,1)}, bf16[32,4608]{1,0:T(8,128)(2,1)S(1)}, u32[]{:S(2)}, u32[]{:S(2)}) collective-permute-start(bf16[32,4608]{1,0:T(8,128)(2,1)} %refs_0_.4), channel_id=1, source_target_pairs={{0,4},{1,5},{4,8},{5,9},{8,12},{9,13},{12,14},{13,15},{14,10},{15,... | collective-permute-start | bytes 884744 | tf_op jit(solution)/shard_map/ppermute | solution.py:55
  3.0 14.6 %copy-start.2 = (bf16[32,4608]{1,0:T(8,128)(2,1)S(1)}, bf16[32,4608]{1,0:T(8,128)(2,1)}, u32[]{:S(2)}) copy-start(bf16[32,4608]{1,0:T(8,128)(2,1)} %refs_0_.4) | copy-start | bytes 884740
  3.0 18.9 %copy-start = (bf16[4608,2304]{1,0:T(8,128)(2,1)S(1)}, bf16[4608,2304]{1,0:T(8,128)(2,1)}, u32[]{:S(2)}) copy-start(bf16[4608,2304]{1,0:T(8,128)(2,1)} %refs_4_.1) | copy-start | bytes 63700996
  4.3 9.9 %collective-permute-start.2 = (bf16[32,640]{1,0:T(8,128)(2,1)S(1)}, bf16[32,640]{1,0:T(8,128)(2,1)S(1)}, u32[]{:S(2)}, u32[]{:S(2)}) collective-permute-start(bf16[32,640]{1,0:T(8,128)(2,1)S(1)} %get-tuple-element.23), channel_id=1, source_target_pairs={{0,10},{1,11},{4,6},{5,7},{8,2},{9,3},{12,0},{13,1},{14,4},{15,5},... | collective-permute-start | bytes 122888 | tf_op jit(solution)/shard_map/ppermute | solution.py:431
  8.4 9.2 %collective-permute-start.3 = (bf16[32,640]{1,0:T(8,128)(2,1)S(1)}, bf16[32,640]{1,0:T(8,128)(2,1)S(1)}, u32[]{:S(2)}, u32[]{:S(2)}) collective-permute-start(bf16[32,640]{1,0:T(8,128)(2,1)S(1)} %get-tuple-element.24), channel_id=1, source_target_pairs={{0,12},{1,13},{4,14},{5,15},{8,10},{9,11},{12,6},{13,7},{14,2},{15... | collective-permute-start | bytes 122888 | tf_op jit(solution)/shard_map/ppermute | solution.py:431
  8.5 9.1 %collective-permute-start.4 = (bf16[32,640]{1,0:T(8,128)(2,1)S(1)}, bf16[32,640]{1,0:T(8,128)(2,1)S(1)}, u32[]{:S(2)}, u32[]{:S(2)}) collective-permute-start(bf16[32,640]{1,0:T(8,128)(2,1)S(1)} %get-tuple-element.25), channel_id=1, source_target_pairs={{0,14},{1,15},{4,10},{5,11},{8,6},{9,7},{12,2},{13,3},{14,0},{15,1... | collective-permute-start | bytes 122888 | tf_op jit(solution)/shard_map/ppermute | solution.py:431
  17.8 12.0 %collective-permute-start.5 = (bf16[256,2304]{1,0:T(8,128)(2,1)S(1)}, bf16[256,2304]{1,0:T(8,128)(2,1)S(1)}, u32[]{:S(2)}, u32[]{:S(2)}) collective-permute-start(bf16[256,2304]{1,0:T(8,128)(2,1)S(1)} %get-tuple-element.26.refs_0_), channel_id=1, source_target_pairs={{0,1},{1,0},{2,3},{3,2},{4,5},{5,4},{6,7},{7,6},{8,9},{9,8},{10,11... | collective-permute-start | bytes 3538952 | tf_op jit(solution)/shard_map/ppermute | solution.py:22
  17.9 7.3 %collective-permute-start.6 = (bf16[32,2304]{1,0:T(8,128)(2,1)S(1)}, bf16[32,2304]{1,0:T(8,128)(2,1)S(1)}, u32[]{:S(2)}, u32[]{:S(2)}) collective-permute-start(bf16[32,2304]{1,0:T(8,128)(2,1)S(1)} %get-tuple-element.27), channel_id=1, source_target_pairs={{0,4},{1,5},{4,8},{5,9},{8,12},{9,13},{12,14},{13,15},{14,10},{15,... | collective-permute-start | bytes 442376 | tf_op jit(solution)/shard_map/ppermute | solution.py:55
  18.9 8.5 %collective-permute-start.7 = (bf16[32,2304]{1,0:T(8,128)(2,1)S(1)}, bf16[32,2304]{1,0:T(8,128)(2,1)S(1)}, u32[]{:S(2)}, u32[]{:S(2)}) collective-permute-start(bf16[32,2304]{1,0:T(8,128)(2,1)S(1)} %get-tuple-element.28), channel_id=1, source_target_pairs={{0,4},{1,5},{4,8},{5,9},{8,12},{9,13},{12,14},{13,15},{14,10},{15,... | collective-permute-start | bytes 442376 | tf_op jit(solution)/shard_map/ppermute | solution.py:55
  19.2 9.2 %collective-permute-start.8 = (bf16[32,2304]{1,0:T(8,128)(2,1)S(1)}, bf16[32,2304]{1,0:T(8,128)(2,1)S(1)}, u32[]{:S(2)}, u32[]{:S(2)}) collective-permute-start(bf16[32,2304]{1,0:T(8,128)(2,1)S(1)} %get-tuple-element.29), channel_id=1, source_target_pairs={{0,2},{1,3},{4,0},{5,1},{8,4},{9,5},{12,8},{13,9},{14,12},{15,13},... | collective-permute-start | bytes 442376 | tf_op jit(solution)/shard_map/ppermute | solution.py:55
  20.9 8.5 %collective-permute-start.9 = (bf16[32,2304]{1,0:T(8,128)(2,1)S(1)}, bf16[32,2304]{1,0:T(8,128)(2,1)S(1)}, u32[]{:S(2)}, u32[]{:S(2)}) collective-permute-start(bf16[32,2304]{1,0:T(8,128)(2,1)S(1)} %get-tuple-element.30), channel_id=1, source_target_pairs={{0,2},{1,3},{4,0},{5,1},{8,4},{9,5},{12,8},{13,9},{14,12},{15,13},... | collective-permute-start | bytes 442376 | tf_op jit(solution)/shard_map/ppermute | solution.py:55
  25.1 10.7 %collective-permute-start.10 = (bf16[32,2304]{1,0:T(8,128)(2,1)S(1)}, bf16[32,2304]{1,0:T(8,128)(2,1)S(1)}, u32[]{:S(2)}, u32[]{:S(2)}) collective-permute-start(bf16[32,2304]{1,0:T(8,128)(2,1)S(1)} %collective-permute-done.6.refs_0_), channel_id=1, source_target_pairs={{0,4},{1,5},{4,8},{5,9},{8,12},{9,13},{12,14},{13,15},{14,10},{15,... | collective-permute-start | bytes 442376 | tf_op jit(solution)/shard_map/ppermute | solution.py:55
  27.4 8.5 %collective-permute-start.11 = (bf16[32,2304]{1,0:T(8,128)(2,1)S(1)}, bf16[32,2304]{1,0:T(8,128)(2,1)S(1)}, u32[]{:S(2)}, u32[]{:S(2)}) collective-permute-start(bf16[32,2304]{1,0:T(8,128)(2,1)S(1)} %collective-permute-done.7.refs_1_), channel_id=1, source_target_pairs={{0,4},{1,5},{4,8},{5,9},{8,12},{9,13},{12,14},{13,15},{14,10},{15,... | collective-permute-start | bytes 442376 | tf_op jit(solution)/shard_map/ppermute | solution.py:55
  28.4 7.5 %collective-permute-start.12 = (bf16[32,2304]{1,0:T(8,128)(2,1)S(1)}, bf16[32,2304]{1,0:T(8,128)(2,1)S(1)}, u32[]{:S(2)}, u32[]{:S(2)}) collective-permute-start(bf16[32,2304]{1,0:T(8,128)(2,1)S(1)} %collective-permute-done.8.refs_2_), channel_id=1, source_target_pairs={{0,2},{1,3},{4,0},{5,1},{8,4},{9,5},{12,8},{13,9},{14,12},{15,13},... | collective-permute-start | bytes 442376 | tf_op jit(solution)/shard_map/ppermute | solution.py:55
  29.4 7.2 %collective-permute-start.13 = (bf16[32,2304]{1,0:T(8,128)(2,1)S(1)}, bf16[32,2304]{1,0:T(8,128)(2,1)S(1)}, u32[]{:S(2)}, u32[]{:S(2)}) collective-permute-start(bf16[32,2304]{1,0:T(8,128)(2,1)S(1)} %collective-permute-done.9.refs_3_), channel_id=1, source_target_pairs={{0,2},{1,3},{4,0},{5,1},{8,4},{9,5},{12,8},{13,9},{14,12},{15,13},... | collective-permute-start | bytes 442376 | tf_op jit(solution)/shard_map/ppermute | solution.py:55
  30.8 5.0 %collective-permute-start.14 = (bf16[128,128]{1,0:T(8,128)(2,1)S(1)}, bf16[128,128]{1,0:T(8,128)(2,1)S(1)}, u32[]{:S(2)}, u32[]{:S(2)}) collective-permute-start(bf16[128,128]{1,0:T(8,128)(2,1)S(1)} %get-tuple-element.31.refs_3_), channel_id=1, source_target_pairs={{0,2},{1,3},{2,0},{3,1},{4,6},{5,7},{6,4},{7,5},{8,10},{9,11},{10,... | collective-permute-start | bytes 98312 | tf_op jit(solution)/shard_map/ppermute | solution.py:468
  36.7 9.9 %collective-permute-start.15 = (bf16[256,2304]{1,0:T(8,128)(2,1)S(1)}, bf16[256,2304]{1,0:T(8,128)(2,1)S(1)}, u32[]{:S(2)}, u32[]{:S(2)}) collective-permute-start(bf16[256,2304]{1,0:T(8,128)(2,1)S(1)} %get-tuple-element.34.refs_0_), channel_id=1, source_target_pairs={{0,1},{1,0},{2,3},{3,2},{4,5},{5,4},{6,7},{7,6},{8,9},{9,8},{10,11... | collective-permute-start | bytes 3538952 | tf_op jit(solution)/shard_map/ppermute | solution.py:22
  36.7 9.2 %collective-permute-start.16 = (bf16[64,2304]{1,0:T(8,128)(2,1)S(1)}, bf16[64,2304]{1,0:T(8,128)(2,1)S(1)}, u32[]{:S(2)}, u32[]{:S(2)}) collective-permute-start(bf16[64,2304]{1,0:T(8,128)(2,1)S(1)} %get-tuple-element.35), channel_id=1, source_target_pairs={{0,4},{1,3},{4,8},{5,1},{8,12},{9,5},{12,14},{13,9},{14,10},{15,13... | collective-permute-start | bytes 884744 | tf_op jit(solution)/shard_map/ppermute | solution.py:481
  37.1 8.8 %collective-permute-start.19 = (bf16[128,128]{1,0:T(8,128)(2,1)S(1)}, bf16[128,128]{1,0:T(8,128)(2,1)S(1)}, u32[]{:S(2)}, u32[]{:S(2)}) collective-permute-start(bf16[128,128]{1,0:T(8,128)(2,1)S(1)} %get-tuple-element.33.refs_5_), channel_id=1, source_target_pairs={{0,4},{1,5},{2,6},{3,7},{4,8},{5,9},{6,10},{7,11},{8,12},{9,13},{1... | collective-permute-start | bytes 98312 | tf_op jit(solution)/shard_map/ppermute | solution.py:477
  38.4 7.5 %collective-permute-start.18 = (bf16[128,128]{1,0:T(8,128)(2,1)S(1)}, bf16[128,128]{1,0:T(8,128)(2,1)S(1)}, u32[]{:S(2)}, u32[]{:S(2)}) collective-permute-start(bf16[128,128]{1,0:T(8,128)(2,1)S(1)} %get-tuple-element.33.refs_5_), channel_id=1, source_target_pairs={{0,8},{1,9},{2,10},{3,11},{4,12},{5,13},{6,14},{7,15},{8,0},{9,1},... | collective-permute-start | bytes 98312 | tf_op jit(solution)/shard_map/ppermute | solution.py:477
  40.1 5.8 %collective-permute-start.17 = (bf16[128,128]{1,0:T(8,128)(2,1)S(1)}, bf16[128,128]{1,0:T(8,128)(2,1)S(1)}, u32[]{:S(2)}, u32[]{:S(2)}) collective-permute-start(bf16[128,128]{1,0:T(8,128)(2,1)S(1)} %get-tuple-element.33.refs_5_), channel_id=1, source_target_pairs={{0,12},{1,13},{2,14},{3,15},{4,0},{5,1},{6,2},{7,3},{8,4},{9,5},{1... | collective-permute-start | bytes 98312 | tf_op jit(solution)/shard_map/ppermute | solution.py:477
  46.0 3.6 %collective-permute-start.20 = (bf16[64,2304]{1,0:T(8,128)(2,1)S(1)}, bf16[64,2304]{1,0:T(8,128)(2,1)S(1)}, u32[]{:S(2)}, u32[]{:S(2)}) collective-permute-start(bf16[64,2304]{1,0:T(8,128)(2,1)S(1)} %shard_map.75.refs_3_.refs_2_), channel_id=1, source_target_pairs={{0,1},{1,0},{2,3},{3,2},{4,5},{5,4},{6,7},{7,6},{8,9},{9,8},{10,11... | collective-permute-start | bytes 884744 | tf_op jit(solution)/shard_map/ppermute | solution.py:22
  46.1 3.5 %collective-permute-start.21 = (bf16[128,128]{1,0:T(8,128)(2,1)S(1)}, bf16[128,128]{1,0:T(8,128)(2,1)S(1)}, u32[]{:S(2)}, u32[]{:S(2)}) collective-permute-start(bf16[128,128]{1,0:T(8,128)(2,1)S(1)} %get-tuple-element.37.refs_1_), channel_id=1, source_target_pairs={{0,1},{1,0},{2,3},{3,2},{4,5},{5,4},{6,7},{7,6},{8,9},{9,8},{10,11... | collective-permute-start | bytes 98312 | tf_op jit(solution)/shard_map/ppermute | solution.py:22
  (3 other events, 11.3 us)

commit v15 on v11

--- a/solution.py
+++ b/solution.py
@@ -322,6 +322,7 @@
     chip_rows, rank = 2 * rows, up_ref.shape[1]
     tiles, _, columns = block.shape
     assemble([(mine, others)], [1], rows, held)
+    last = multiply(held, [weight], slice(0, columns))
     for t in range(n):
         i, k = t % (n // 2), t // (n // 2)
         for ref, core in ((own, c), (other, 1 - c)):
@@ -337,7 +338,8 @@
     copies = []
     for j in range(tiles):
         at = slice(j * columns, (j + 1) * columns)
-        last = multiply(held, [weight], at)
+        if j:
+            last = multiply(held, [weight], at)
         for i, (distance, base, row) in enumerate(places):
             chip = chip_at(distance, n)
             first = chip * chip_rows

time: 55.1 us -> 55.1 us (level)
  no operation moved by 1% of the time
where the time goes in v15:
time: 55.1 us; the launch traced here: 54.9 us
  starting transfers between devices  27.4 us (50%)
  Pallas kernels  19.6 us (36%)
  waiting for transfers between devices  7.44 us (14%)
    pallas_call x12, Pallas kernels, call(): pl.pallas_call(body, out_shape=[pltpu.VMEM(shape, dtype) for shape, dtype...  13.1 us
    ppermute x3, starting transfers between devices, on_device(): lax.ppermute(x, AXES, ring_perm(n, d))  8.88 us
    ppermute x5, starting transfers between devices, ring_hop(): lax.ppermute(x, AXES, ring_perm(n, -1))  7.11 us
    ppermute x3, starting transfers between devices, on_device(): lax.ppermute(rounded, AXES, z_perm(n, shift))  5.84 us
    pallas_call x1, Pallas kernels, finish(): pl.pallas_call(functools.partial(finish_kernel, n, rows, groups, len(afte...  5.16 us
    ppermute x3, waiting for transfers between devices, on_device(): lax.ppermute(x, AXES, ring_perm(n, d))  4.39 us
    ppermute x5, starting transfers between devices, ring_hop(): lax.ppermute(x, AXES, ring_perm(n, 1))  3.42 us
    pallas_call x1, Pallas kernels, prepare(): pl.pallas_call(body, out_shape=[pltpu.VMEM(shape, dtype) for shape, dtype...  1.31 us
  transfers between devices with their start and end apart: 22, of which 5 were waited for; matrix products, arithmetic and copies ran while one was open for 0% of the time, Pallas kernels for 26%

profile of v15, /device:TPU:0, one launch (start us, length us, event | category | flops | bytes accessed | tf_op | source)
XLA Modules:
  0.0 54.9 jit_solution(10694580286072596005)
XLA Ops:
  0.0 3.0 %collective-permute-start.1 = (bf16[32,4608]{1,0:T(8,128)(2,1)}, bf16[32,4608]{1,0:T(8,128)(2,1)S(1)}, u32[]{:S(2)}, u32[]{:S(2)}) collective-permute-start(bf16[32,4608]{1,0:T(8,128)(2,1)} %refs_0_.4), channel_id=1, source_target_pairs={{0,2},{1,3},{4,0},{5,1},{8,4},{9,5},{12,8},{13,9},{14,12},{15,13},... | collective-permute-start | bytes 884744 | tf_op jit(solution)/shard_map/ppermute | solution.py:55
  3.0 1.3 %shard_map.64 = (bf16[2,64,640]{2,1,0:T(8,128)(2,1)S(1)}, bf16[32,640]{1,0:T(8,128)(2,1)S(1)}, bf16[32,640]{1,0:T(8,128)(2,1)S(1)}, bf16[32,640]{1,0:T(8,128)(2,1)S(1)}) custom-call(bf16[32,4608]{1,0:T(8,128)(2,1)} %refs_0_.4, f32[2,64,576]{2,1,0:T(8,128)} %bitcast.4, bf16[4608,2304]{1,0:T(8,128)(2,1)} %refs_4_.1, f32[4,64,2304]{2,1,0:T(8,128)} %refs_0_.5), custom_call_target="tpu_custom_call" | custom-call | tf_op jit(solution)/shard_map/pallas_call | solution.py:272
  4.3 4.0 %collective-permute-start.2 = (bf16[32,640]{1,0:T(8,128)(2,1)S(1)}, bf16[32,640]{1,0:T(8,128)(2,1)S(1)}, u32[]{:S(2)}, u32[]{:S(2)}) collective-permute-start(bf16[32,640]{1,0:T(8,128)(2,1)S(1)} %get-tuple-element.23), channel_id=1, source_target_pairs={{0,10},{1,11},{4,6},{5,7},{8,2},{9,3},{12,0},{13,1},{14,4},{15,5},... | collective-permute-start | bytes 122888 | tf_op jit(solution)/shard_map/ppermute | solution.py:413
  8.5 4.7 %collective-permute-start.4 = (bf16[32,640]{1,0:T(8,128)(2,1)S(1)}, bf16[32,640]{1,0:T(8,128)(2,1)S(1)}, u32[]{:S(2)}, u32[]{:S(2)}) collective-permute-start(bf16[32,640]{1,0:T(8,128)(2,1)S(1)} %get-tuple-element.25), channel_id=1, source_target_pairs={{0,14},{1,15},{4,10},{5,11},{8,6},{9,7},{12,2},{13,3},{14,0},{15,1... | collective-permute-start | bytes 122888 | tf_op jit(solution)/shard_map/ppermute | solution.py:413
  13.2 1.1 %collective-permute-done.2.refs_4_.refs_2_ = bf16[32,640]{1,0:T(8,128)(2,1)S(1)} collective-permute-done((bf16[32,640]{1,0:T(8,128)(2,1)S(1)}, bf16[32,640]{1,0:T(8,128)(2,1)S(1)}, u32[]{:S(2)}, u32[]{:S(2)}) %collective-permute-start.2) | collective-permute-done | bytes 40992 | tf_op jit(solution)/shard_map/ppermute | solution.py:413
  14.3 3.3 %collective-permute-done.3.refs_5_.refs_3_ = bf16[32,640]{1,0:T(8,128)(2,1)S(1)} collective-permute-done((bf16[32,640]{1,0:T(8,128)(2,1)S(1)}, bf16[32,640]{1,0:T(8,128)(2,1)S(1)}, u32[]{:S(2)}, u32[]{:S(2)}) %collective-permute-start.3) | collective-permute-done | bytes 40992 | tf_op jit(solution)/shard_map/ppermute | solution.py:413
  17.9 1.0 %collective-permute-start.6 = (bf16[32,2304]{1,0:T(8,128)(2,1)S(1)}, bf16[32,2304]{1,0:T(8,128)(2,1)S(1)}, u32[]{:S(2)}, u32[]{:S(2)}) collective-permute-start(bf16[32,2304]{1,0:T(8,128)(2,1)S(1)} %get-tuple-element.27), channel_id=1, source_target_pairs={{0,4},{1,5},{4,8},{5,9},{8,12},{9,13},{12,14},{13,15},{14,10},{15,... | collective-permute-start | bytes 442376 | tf_op jit(solution)/shard_map/ppermute | solution.py:55
  19.2 1.7 %collective-permute-start.8 = (bf16[32,2304]{1,0:T(8,128)(2,1)S(1)}, bf16[32,2304]{1,0:T(8,128)(2,1)S(1)}, u32[]{:S(2)}, u32[]{:S(2)}) collective-permute-start(bf16[32,2304]{1,0:T(8,128)(2,1)S(1)} %get-tuple-element.29), channel_id=1, source_target_pairs={{0,2},{1,3},{4,0},{5,1},{8,4},{9,5},{12,8},{13,9},{14,12},{15,13},... | collective-permute-start | bytes 442376 | tf_op jit(solution)/shard_map/ppermute | solution.py:55
  20.9 1.0 %collective-permute-start.9 = (bf16[32,2304]{1,0:T(8,128)(2,1)S(1)}, bf16[32,2304]{1,0:T(8,128)(2,1)S(1)}, u32[]{:S(2)}, u32[]{:S(2)}) collective-permute-start(bf16[32,2304]{1,0:T(8,128)(2,1)S(1)} %get-tuple-element.30), channel_id=1, source_target_pairs={{0,2},{1,3},{4,0},{5,1},{8,4},{9,5},{12,8},{13,9},{14,12},{15,13},... | collective-permute-start | bytes 442376 | tf_op jit(solution)/shard_map/ppermute | solution.py:55
  22.0 3.0 %shard_map.66.refs_1_.refs_4_ = f32[96,2304]{1,0:T(8,128)S(1)} custom-call(bf16[256,2304]{1,0:T(8,128)(2,1)S(1)} %get-tuple-element.26.refs_0_, bf16[4608,2304]{1,0:T(8,128)(2,1)S(1)} %copy-done), custom_call_target="tpu_custom_call" | custom-call | flops 2038431744 | tf_op jit(solution)/shard_map/pallas_call | solution.py:98
  25.1 1.0 %collective-permute-start.10 = (bf16[32,2304]{1,0:T(8,128)(2,1)S(1)}, bf16[32,2304]{1,0:T(8,128)(2,1)S(1)}, u32[]{:S(2)}, u32[]{:S(2)}) collective-permute-start(bf16[32,2304]{1,0:T(8,128)(2,1)S(1)} %collective-permute-done.6.refs_0_), channel_id=1, source_target_pairs={{0,4},{1,5},{4,8},{5,9},{8,12},{9,13},{12,14},{13,15},{14,10},{15,... | collective-permute-start | bytes 442376 | tf_op jit(solution)/shard_map/ppermute | solution.py:55
  26.2 1.2 %collective-permute-done.7.refs_1_ = bf16[32,2304]{1,0:T(8,128)(2,1)S(1)} collective-permute-done((bf16[32,2304]{1,0:T(8,128)(2,1)S(1)}, bf16[32,2304]{1,0:T(8,128)(2,1)S(1)}, u32[]{:S(2)}, u32[]{:S(2)}) %collective-permute-start.7) | collective-permute-done | bytes 147488 | tf_op jit(solution)/shard_map/ppermute | solution.py:55
  27.4 1.0 %collective-permute-start.11 = (bf16[32,2304]{1,0:T(8,128)(2,1)S(1)}, bf16[32,2304]{1,0:T(8,128)(2,1)S(1)}, u32[]{:S(2)}, u32[]{:S(2)}) collective-permute-start(bf16[32,2304]{1,0:T(8,128)(2,1)S(1)} %collective-permute-done.7.refs_1_), channel_id=1, source_target_pairs={{0,4},{1,5},{4,8},{5,9},{8,12},{9,13},{12,14},{13,15},{14,10},{15,... | collective-permute-start | bytes 442376 | tf_op jit(solution)/shard_map/ppermute | solution.py:55
  28.4 1.0 %collective-permute-start.12 = (bf16[32,2304]{1,0:T(8,128)(2,1)S(1)}, bf16[32,2304]{1,0:T(8,128)(2,1)S(1)}, u32[]{:S(2)}, u32[]{:S(2)}) collective-permute-start(bf16[32,2304]{1,0:T(8,128)(2,1)S(1)} %collective-permute-done.8.refs_2_), channel_id=1, source_target_pairs={{0,2},{1,3},{4,0},{5,1},{8,4},{9,5},{12,8},{13,9},{14,12},{15,13},... | collective-permute-start | bytes 442376 | tf_op jit(solution)/shard_map/ppermute | solution.py:55
  29.8 0.8 %shard_map.69 = (f32[128,128]{1,0:T(8,128)S(1)}, bf16[128,128]{1,0:T(8,128)(2,1)S(1)}) custom-call(bf16[256,2304]{1,0:T(8,128)(2,1)S(1)} %get-tuple-element.26.refs_0_, bf16[128,2304]{1,0:T(8,128)(2,1)S(1)} %shard_map.68.refs_1_.refs_0_, bf16[32,640]{1,0:T(8,128)(2,1)S(1)} %collective-permute-done.2.refs_4_.refs_2_, ...), custom_call_target="tpu_custom_call" | custom-call | tf_op jit(solution)/shard_map/pallas_call | solution.py:98
  30.6 1.1 %collective-permute-start.14 = (bf16[128,128]{1,0:T(8,128)(2,1)S(1)}, bf16[128,128]{1,0:T(8,128)(2,1)S(1)}, u32[]{:S(2)}, u32[]{:S(2)}) collective-permute-start(bf16[128,128]{1,0:T(8,128)(2,1)S(1)} %get-tuple-element.31.refs_3_), channel_id=1, source_target_pairs={{0,2},{1,3},{2,0},{3,1},{4,6},{5,7},{6,4},{7,5},{8,10},{9,11},{10,... | collective-permute-start | bytes 98312 | tf_op jit(solution)/shard_map/ppermute | solution.py:449
  31.7 3.0 %shard_map.70.refs_6_.refs_0_ = f32[192,2304]{1,0:T(8,128)S(1)} custom-call(bf16[256,2304]{1,0:T(8,128)(2,1)S(1)} %collective-permute-done.5.refs_6_.refs_0_, f32[96,2304]{1,0:T(8,128)S(1)} %shard_map.66.refs_1_.refs_4_, bf16[4608,2304]{1,0:T(8,128)(2,1)S(1)} %copy-done, bf16[128,128]{1,0:T(8,128)(2,1)S(1)} %get-tuple-element.31.refs_3_), custom_call_target="tpu_custom_call" | custom-call | flops 2038431744 | tf_op jit(solution)/shard_map/pallas_call | solution.py:98
  34.7 1.1 %collective-permute-done.14.refs_1_ = bf16[128,128]{1,0:T(8,128)(2,1)S(1)} collective-permute-done((bf16[128,128]{1,0:T(8,128)(2,1)S(1)}, bf16[128,128]{1,0:T(8,128)(2,1)S(1)}, u32[]{:S(2)}, u32[]{:S(2)}) %collective-permute-start.14) | collective-permute-done | bytes 32800 | tf_op jit(solution)/shard_map/ppermute | solution.py:449
  37.1 1.3 %collective-permute-start.19 = (bf16[128,128]{1,0:T(8,128)(2,1)S(1)}, bf16[128,128]{1,0:T(8,128)(2,1)S(1)}, u32[]{:S(2)}, u32[]{:S(2)}) collective-permute-start(bf16[128,128]{1,0:T(8,128)(2,1)S(1)} %get-tuple-element.33.refs_5_), channel_id=1, source_target_pairs={{0,4},{1,5},{2,6},{3,7},{4,8},{5,9},{6,10},{7,11},{8,12},{9,13},{1... | collective-permute-start | bytes 98312 | tf_op jit(solution)/shard_map/ppermute | solution.py:458
  38.4 1.7 %collective-permute-start.18 = (bf16[128,128]{1,0:T(8,128)(2,1)S(1)}, bf16[128,128]{1,0:T(8,128)(2,1)S(1)}, u32[]{:S(2)}, u32[]{:S(2)}) collective-permute-start(bf16[128,128]{1,0:T(8,128)(2,1)S(1)} %get-tuple-element.33.refs_5_), channel_id=1, source_target_pairs={{0,8},{1,9},{2,10},{3,11},{4,12},{5,13},{6,14},{7,15},{8,0},{9,1},... | collective-permute-start | bytes 98312 | tf_op jit(solution)/shard_map/ppermute | solution.py:458
  40.1 2.8 %collective-permute-start.17 = (bf16[128,128]{1,0:T(8,128)(2,1)S(1)}, bf16[128,128]{1,0:T(8,128)(2,1)S(1)}, u32[]{:S(2)}, u32[]{:S(2)}) collective-permute-start(bf16[128,128]{1,0:T(8,128)(2,1)S(1)} %get-tuple-element.33.refs_5_), channel_id=1, source_target_pairs={{0,12},{1,13},{2,14},{3,15},{4,0},{5,1},{6,2},{7,3},{8,4},{9,5},{1... | collective-permute-start | bytes 98312 | tf_op jit(solution)/shard_map/ppermute | solution.py:458
  42.9 2.9 %shard_map.73.refs_2_.refs_1_ = f32[128,2304]{1,0:T(8,128)S(1)} custom-call(bf16[256,2304]{1,0:T(8,128)(2,1)S(1)} %get-tuple-element.34.refs_0_, bf16[4608,2304]{1,0:T(8,128)(2,1)S(1)} %copy-done), custom_call_target="tpu_custom_call" | custom-call | flops 2717908992 | tf_op jit(solution)/shard_map/pallas_call | solution.py:98
  46.6 3.0 %shard_map.76.refs_1_ = f32[256,2304]{1,0:T(8,128)S(1)} custom-call(bf16[256,2304]{1,0:T(8,128)(2,1)S(1)} %collective-permute-done.15.refs_0_, f32[128,2304]{1,0:T(8,128)S(1)} %shard_map.73.refs_2_.refs_1_, bf16[4608,2304]{1,0:T(8,128)(2,1)S(1)} %copy-done, bf16[64,2304]{1,0:T(8,128)(2,1)S(1)} %shard_map.75.refs_3_.refs_2_), custom_call_target="tpu_custom_call" | custom-call | flops 2717908992 | tf_op jit(solution)/shard_map/pallas_call | solution.py:98
  49.6 5.2 %shard_map.77 = bf16[512,2304]{1,0:T(8,128)(2,1)} custom-call(f32[192,2304]{1,0:T(8,128)S(1)} %shard_map.70.refs_6_.refs_0_, f32[256,2304]{1,0:T(8,128)S(1)} %shard_map.76.refs_1_, bf16[64,2304]{1,0:T(8,128)(2,1)S(1)} %shard_map.75.refs_3_.refs_2_, bf16[64,2304]{1,0:T(8,128)(2,1)S(1)} %collective-permute-done.20.refs_3_, bf16[4608,2304]{1,0:T(8,128)(2,1)S(1)} %copy-done, ...), custom_call_target="tpu_custom_call" | custom-call | flops 2717908992 | bytes 2359296 | tf_op jit(solution)/shard_map/pallas_call | solution.py:369
  (44 shorter events, 3.0 us)
Async XLA Ops:
  0.0 17.6 %collective-permute-start.1 = (bf16[32,4608]{1,0:T(8,128)(2,1)}, bf16[32,4608]{1,0:T(8,128)(2,1)S(1)}, u32[]{:S(2)}, u32[]{:S(2)}) collective-permute-start(bf16[32,4608]{1,0:T(8,128)(2,1)} %refs_0_.4), channel_id=1, source_target_pairs={{0,2},{1,3},{4,0},{5,1},{8,4},{9,5},{12,8},{13,9},{14,12},{15,13},... | collective-permute-start | bytes 884744 | tf_op jit(solution)/shard_map/ppermute | solution.py:55
  3.0 14.7 %collective-permute-start = (bf16[32,4608]{1,0:T(8,128)(2,1)}, bf16[32,4608]{1,0:T(8,128)(2,1)S(1)}, u32[]{:S(2)}, u32[]{:S(2)}) collective-permute-start(bf16[32,4608]{1,0:T(8,128)(2,1)} %refs_0_.4), channel_id=1, source_target_pairs={{0,4},{1,5},{4,8},{5,9},{8,12},{9,13},{12,14},{13,15},{14,10},{15,... | collective-permute-start | bytes 884744 | tf_op jit(solution)/shard_map/ppermute | solution.py:55
  3.0 14.6 %copy-start.2 = (bf16[32,4608]{1,0:T(8,128)(2,1)S(1)}, bf16[32,4608]{1,0:T(8,128)(2,1)}, u32[]{:S(2)}) copy-start(bf16[32,4608]{1,0:T(8,128)(2,1)} %refs_0_.4) | copy-start | bytes 884740
  3.0 18.9 %copy-start = (bf16[4608,2304]{1,0:T(8,128)(2,1)S(1)}, bf16[4608,2304]{1,0:T(8,128)(2,1)}, u32[]{:S(2)}) copy-start(bf16[4608,2304]{1,0:T(8,128)(2,1)} %refs_4_.1) | copy-start | bytes 63700996
  4.3 9.9 %collective-permute-start.2 = (bf16[32,640]{1,0:T(8,128)(2,1)S(1)}, bf16[32,640]{1,0:T(8,128)(2,1)S(1)}, u32[]{:S(2)}, u32[]{:S(2)}) collective-permute-start(bf16[32,640]{1,0:T(8,128)(2,1)S(1)} %get-tuple-element.23), channel_id=1, source_target_pairs={{0,10},{1,11},{4,6},{5,7},{8,2},{9,3},{12,0},{13,1},{14,4},{15,5},... | collective-permute-start | bytes 122888 | tf_op jit(solution)/shard_map/ppermute | solution.py:413
  8.4 9.2 %collective-permute-start.3 = (bf16[32,640]{1,0:T(8,128)(2,1)S(1)}, bf16[32,640]{1,0:T(8,128)(2,1)S(1)}, u32[]{:S(2)}, u32[]{:S(2)}) collective-permute-start(bf16[32,640]{1,0:T(8,128)(2,1)S(1)} %get-tuple-element.24), channel_id=1, source_target_pairs={{0,12},{1,13},{4,14},{5,15},{8,10},{9,11},{12,6},{13,7},{14,2},{15... | collective-permute-start | bytes 122888 | tf_op jit(solution)/shard_map/ppermute | solution.py:413
  8.5 9.1 %collective-permute-start.4 = (bf16[32,640]{1,0:T(8,128)(2,1)S(1)}, bf16[32,640]{1,0:T(8,128)(2,1)S(1)}, u32[]{:S(2)}, u32[]{:S(2)}) collective-permute-start(bf16[32,640]{1,0:T(8,128)(2,1)S(1)} %get-tuple-element.25), channel_id=1, source_target_pairs={{0,14},{1,15},{4,10},{5,11},{8,6},{9,7},{12,2},{13,3},{14,0},{15,1... | collective-permute-start | bytes 122888 | tf_op jit(solution)/shard_map/ppermute | solution.py:413
  17.8 12.0 %collective-permute-start.5 = (bf16[256,2304]{1,0:T(8,128)(2,1)S(1)}, bf16[256,2304]{1,0:T(8,128)(2,1)S(1)}, u32[]{:S(2)}, u32[]{:S(2)}) collective-permute-start(bf16[256,2304]{1,0:T(8,128)(2,1)S(1)} %get-tuple-element.26.refs_0_), channel_id=1, source_target_pairs={{0,1},{1,0},{2,3},{3,2},{4,5},{5,4},{6,7},{7,6},{8,9},{9,8},{10,11... | collective-permute-start | bytes 3538952 | tf_op jit(solution)/shard_map/ppermute | solution.py:22
  17.9 7.3 %collective-permute-start.6 = (bf16[32,2304]{1,0:T(8,128)(2,1)S(1)}, bf16[32,2304]{1,0:T(8,128)(2,1)S(1)}, u32[]{:S(2)}, u32[]{:S(2)}) collective-permute-start(bf16[32,2304]{1,0:T(8,128)(2,1)S(1)} %get-tuple-element.27), channel_id=1, source_target_pairs={{0,4},{1,5},{4,8},{5,9},{8,12},{9,13},{12,14},{13,15},{14,10},{15,... | collective-permute-start | bytes 442376 | tf_op jit(solution)/shard_map/ppermute | solution.py:55
  18.9 8.5 %collective-permute-start.7 = (bf16[32,2304]{1,0:T(8,128)(2,1)S(1)}, bf16[32,2304]{1,0:T(8,128)(2,1)S(1)}, u32[]{:S(2)}, u32[]{:S(2)}) collective-permute-start(bf16[32,2304]{1,0:T(8,128)(2,1)S(1)} %get-tuple-element.28), channel_id=1, source_target_pairs={{0,4},{1,5},{4,8},{5,9},{8,12},{9,13},{12,14},{13,15},{14,10},{15,... | collective-permute-start | bytes 442376 | tf_op jit(solution)/shard_map/ppermute | solution.py:55
  19.2 9.2 %collective-permute-start.8 = (bf16[32,2304]{1,0:T(8,128)(2,1)S(1)}, bf16[32,2304]{1,0:T(8,128)(2,1)S(1)}, u32[]{:S(2)}, u32[]{:S(2)}) collective-permute-start(bf16[32,2304]{1,0:T(8,128)(2,1)S(1)} %get-tuple-element.29), channel_id=1, source_target_pairs={{0,2},{1,3},{4,0},{5,1},{8,4},{9,5},{12,8},{13,9},{14,12},{15,13},... | collective-permute-start | bytes 442376 | tf_op jit(solution)/shard_map/ppermute | solution.py:55
  20.9 8.5 %collective-permute-start.9 = (bf16[32,2304]{1,0:T(8,128)(2,1)S(1)}, bf16[32,2304]{1,0:T(8,128)(2,1)S(1)}, u32[]{:S(2)}, u32[]{:S(2)}) collective-permute-start(bf16[32,2304]{1,0:T(8,128)(2,1)S(1)} %get-tuple-element.30), channel_id=1, source_target_pairs={{0,2},{1,3},{4,0},{5,1},{8,4},{9,5},{12,8},{13,9},{14,12},{15,13},... | collective-permute-start | bytes 442376 | tf_op jit(solution)/shard_map/ppermute | solution.py:55
  25.1 10.7 %collective-permute-start.10 = (bf16[32,2304]{1,0:T(8,128)(2,1)S(1)}, bf16[32,2304]{1,0:T(8,128)(2,1)S(1)}, u32[]{:S(2)}, u32[]{:S(2)}) collective-permute-start(bf16[32,2304]{1,0:T(8,128)(2,1)S(1)} %collective-permute-done.6.refs_0_), channel_id=1, source_target_pairs={{0,4},{1,5},{4,8},{5,9},{8,12},{9,13},{12,14},{13,15},{14,10},{15,... | collective-permute-start | bytes 442376 | tf_op jit(solution)/shard_map/ppermute | solution.py:55
  27.4 8.5 %collective-permute-start.11 = (bf16[32,2304]{1,0:T(8,128)(2,1)S(1)}, bf16[32,2304]{1,0:T(8,128)(2,1)S(1)}, u32[]{:S(2)}, u32[]{:S(2)}) collective-permute-start(bf16[32,2304]{1,0:T(8,128)(2,1)S(1)} %collective-permute-done.7.refs_1_), channel_id=1, source_target_pairs={{0,4},{1,5},{4,8},{5,9},{8,12},{9,13},{12,14},{13,15},{14,10},{15,... | collective-permute-start | bytes 442376 | tf_op jit(solution)/shard_map/ppermute | solution.py:55
  28.4 7.5 %collective-permute-start.12 = (bf16[32,2304]{1,0:T(8,128)(2,1)S(1)}, bf16[32,2304]{1,0:T(8,128)(2,1)S(1)}, u32[]{:S(2)}, u32[]{:S(2)}) collective-permute-start(bf16[32,2304]{1,0:T(8,128)(2,1)S(1)} %collective-permute-done.8.refs_2_), channel_id=1, source_target_pairs={{0,2},{1,3},{4,0},{5,1},{8,4},{9,5},{12,8},{13,9},{14,12},{15,13},... | collective-permute-start | bytes 442376 | tf_op jit(solution)/shard_map/ppermute | solution.py:55
  29.4 7.2 %collective-permute-start.13 = (bf16[32,2304]{1,0:T(8,128)(2,1)S(1)}, bf16[32,2304]{1,0:T(8,128)(2,1)S(1)}, u32[]{:S(2)}, u32[]{:S(2)}) collective-permute-start(bf16[32,2304]{1,0:T(8,128)(2,1)S(1)} %collective-permute-done.9.refs_3_), channel_id=1, source_target_pairs={{0,2},{1,3},{4,0},{5,1},{8,4},{9,5},{12,8},{13,9},{14,12},{15,13},... | collective-permute-start | bytes 442376 | tf_op jit(solution)/shard_map/ppermute | solution.py:55
  30.6 5.2 %collective-permute-start.14 = (bf16[128,128]{1,0:T(8,128)(2,1)S(1)}, bf16[128,128]{1,0:T(8,128)(2,1)S(1)}, u32[]{:S(2)}, u32[]{:S(2)}) collective-permute-start(bf16[128,128]{1,0:T(8,128)(2,1)S(1)} %get-tuple-element.31.refs_3_), channel_id=1, source_target_pairs={{0,2},{1,3},{2,0},{3,1},{4,6},{5,7},{6,4},{7,5},{8,10},{9,11},{10,... | collective-permute-start | bytes 98312 | tf_op jit(solution)/shard_map/ppermute | solution.py:449
  36.7 9.9 %collective-permute-start.15 = (bf16[256,2304]{1,0:T(8,128)(2,1)S(1)}, bf16[256,2304]{1,0:T(8,128)(2,1)S(1)}, u32[]{:S(2)}, u32[]{:S(2)}) collective-permute-start(bf16[256,2304]{1,0:T(8,128)(2,1)S(1)} %get-tuple-element.34.refs_0_), channel_id=1, source_target_pairs={{0,1},{1,0},{2,3},{3,2},{4,5},{5,4},{6,7},{7,6},{8,9},{9,8},{10,11... | collective-permute-start | bytes 3538952 | tf_op jit(solution)/shard_map/ppermute | solution.py:22
  36.7 9.2 %collective-permute-start.16 = (bf16[64,2304]{1,0:T(8,128)(2,1)S(1)}, bf16[64,2304]{1,0:T(8,128)(2,1)S(1)}, u32[]{:S(2)}, u32[]{:S(2)}) collective-permute-start(bf16[64,2304]{1,0:T(8,128)(2,1)S(1)} %get-tuple-element.35), channel_id=1, source_target_pairs={{0,4},{1,3},{4,8},{5,1},{8,12},{9,5},{12,14},{13,9},{14,10},{15,13... | collective-permute-start | bytes 884744 | tf_op jit(solution)/shard_map/ppermute | solution.py:462
  37.1 8.8 %collective-permute-start.19 = (bf16[128,128]{1,0:T(8,128)(2,1)S(1)}, bf16[128,128]{1,0:T(8,128)(2,1)S(1)}, u32[]{:S(2)}, u32[]{:S(2)}) collective-permute-start(bf16[128,128]{1,0:T(8,128)(2,1)S(1)} %get-tuple-element.33.refs_5_), channel_id=1, source_target_pairs={{0,4},{1,5},{2,6},{3,7},{4,8},{5,9},{6,10},{7,11},{8,12},{9,13},{1... | collective-permute-start | bytes 98312 | tf_op jit(solution)/shard_map/ppermute | solution.py:458
  38.4 7.5 %collective-permute-start.18 = (bf16[128,128]{1,0:T(8,128)(2,1)S(1)}, bf16[128,128]{1,0:T(8,128)(2,1)S(1)}, u32[]{:S(2)}, u32[]{:S(2)}) collective-permute-start(bf16[128,128]{1,0:T(8,128)(2,1)S(1)} %get-tuple-element.33.refs_5_), channel_id=1, source_target_pairs={{0,8},{1,9},{2,10},{3,11},{4,12},{5,13},{6,14},{7,15},{8,0},{9,1},... | collective-permute-start | bytes 98312 | tf_op jit(solution)/shard_map/ppermute | solution.py:458
  40.1 5.8 %collective-permute-start.17 = (bf16[128,128]{1,0:T(8,128)(2,1)S(1)}, bf16[128,128]{1,0:T(8,128)(2,1)S(1)}, u32[]{:S(2)}, u32[]{:S(2)}) collective-permute-start(bf16[128,128]{1,0:T(8,128)(2,1)S(1)} %get-tuple-element.33.refs_5_), channel_id=1, source_target_pairs={{0,12},{1,13},{2,14},{3,15},{4,0},{5,1},{6,2},{7,3},{8,4},{9,5},{1... | collective-permute-start | bytes 98312 | tf_op jit(solution)/shard_map/ppermute | solution.py:458
  46.0 3.6 %collective-permute-start.20 = (bf16[64,2304]{1,0:T(8,128)(2,1)S(1)}, bf16[64,2304]{1,0:T(8,128)(2,1)S(1)}, u32[]{:S(2)}, u32[]{:S(2)}) collective-permute-start(bf16[64,2304]{1,0:T(8,128)(2,1)S(1)} %shard_map.75.refs_3_.refs_2_), channel_id=1, source_target_pairs={{0,1},{1,0},{2,3},{3,2},{4,5},{5,4},{6,7},{7,6},{8,9},{9,8},{10,11... | collective-permute-start | bytes 884744 | tf_op jit(solution)/shard_map/ppermute | solution.py:22
  46.1 3.5 %collective-permute-start.21 = (bf16[128,128]{1,0:T(8,128)(2,1)S(1)}, bf16[128,128]{1,0:T(8,128)(2,1)S(1)}, u32[]{:S(2)}, u32[]{:S(2)}) collective-permute-start(bf16[128,128]{1,0:T(8,128)(2,1)S(1)} %get-tuple-element.37.refs_1_), channel_id=1, source_target_pairs={{0,1},{1,0},{2,3},{3,2},{4,5},{5,4},{6,7},{7,6},{8,9},{9,8},{10,11... | collective-permute-start | bytes 98312 | tf_op jit(solution)/shard_map/ppermute | solution.py:22
  (3 other events, 11.3 us)

commit v16 on v11

--- a/solution.py
+++ b/solution.py
@@ -335,6 +335,7 @@
     for lookup in lookups:
         lookup.wait()
     copies = []
+    piece = 256 if columns % 256 == 0 else columns
     for j in range(tiles):
         at = slice(j * columns, (j + 1) * columns)
         last = multiply(held, [weight], at)
@@ -342,11 +343,15 @@
             chip = chip_at(distance, n)
             first = chip * chip_rows
             of_block = first // BLOCK
-            delta = jnp.dot(shrink[chip], up_ref[adapters[of_block], :, at], preferred_element_type=jnp.float32)
-            index = lax.broadcasted_iota(jnp.int32, delta.shape, 0) + (first - of_block * BLOCK)
-            value = last[:chip_rows] if base is None else base[row : row + chip_rows, at]
             place = pl.ds(i * chip_rows, chip_rows)
-            block[j, place, :] = jnp.where(index < live[of_block], value + delta, 0.0).astype(out_ref.dtype)
+            mine_shrink, adapter = shrink[chip], adapters[of_block]
+            index = lax.broadcasted_iota(jnp.int32, (chip_rows, piece), 0) + (first - of_block * BLOCK)
+            on = index < live[of_block]
+            for k in range(0, columns, piece):
+                cut = slice(j * columns + k, j * columns + k + piece)
+                delta = jnp.dot(mine_shrink, up_ref[adapter, :, cut], preferred_element_type=jnp.float32)
+                value = last[:chip_rows, k : k + piece] if base is None else base[row : row + chip_rows, cut]
+                block[j, place, k : k + piece] = jnp.where(on, value + delta, 0.0).astype(out_ref.dtype)
             copies.append(
                 pltpu.make_async_copy(
                     block.at[j, place, :],

time: 55.1 us -> 55.1 us (level)
  no operation moved by 1% of the time
where the time goes in v16:
time: 55.1 us; the launch traced here: 55 us
  starting transfers between devices  27.4 us (50%)
  Pallas kernels  19.7 us (36%)
  waiting for transfers between devices  7.44 us (14%)
    pallas_call x12, Pallas kernels, call(): pl.pallas_call(body, out_shape=[pltpu.VMEM(shape, dtype) for shape, dtype...  13.1 us
    ppermute x3, starting transfers between devices, on_device(): lax.ppermute(x, AXES, ring_perm(n, d))  8.88 us
    ppermute x5, starting transfers between devices, ring_hop(): lax.ppermute(x, AXES, ring_perm(n, -1))  7.11 us
    ppermute x3, starting transfers between devices, on_device(): lax.ppermute(rounded, AXES, z_perm(n, shift))  5.84 us
    pallas_call x1, Pallas kernels, finish(): pl.pallas_call(functools.partial(finish_kernel, n, rows, groups, len(afte...  5.22 us
    ppermute x3, waiting for transfers between devices, on_device(): lax.ppermute(x, AXES, ring_perm(n, d))  4.39 us
    ppermute x5, starting transfers between devices, ring_hop(): lax.ppermute(x, AXES, ring_perm(n, 1))  3.42 us
    pallas_call x1, Pallas kernels, prepare(): pl.pallas_call(body, out_shape=[pltpu.VMEM(shape, dtype) for shape, dtype...  1.31 us
  transfers between devices with their start and end apart: 22, of which 5 were waited for; matrix products, arithmetic and copies ran while one was open for 0% of the time, Pallas kernels for 26%

profile of v16, /device:TPU:0, one launch (start us, length us, event | category | flops | bytes accessed | tf_op | source)
XLA Modules:
  0.0 55.0 jit_solution(210700938812997093)
XLA Ops:
  0.0 3.0 %collective-permute-start.1 = (bf16[32,4608]{1,0:T(8,128)(2,1)}, bf16[32,4608]{1,0:T(8,128)(2,1)S(1)}, u32[]{:S(2)}, u32[]{:S(2)}) collective-permute-start(bf16[32,4608]{1,0:T(8,128)(2,1)} %refs_0_.4), channel_id=1, source_target_pairs={{0,2},{1,3},{4,0},{5,1},{8,4},{9,5},{12,8},{13,9},{14,12},{15,13},... | collective-permute-start | bytes 884744 | tf_op jit(solution)/shard_map/ppermute | solution.py:55
  3.0 1.3 %shard_map.64 = (bf16[2,64,640]{2,1,0:T(8,128)(2,1)S(1)}, bf16[32,640]{1,0:T(8,128)(2,1)S(1)}, bf16[32,640]{1,0:T(8,128)(2,1)S(1)}, bf16[32,640]{1,0:T(8,128)(2,1)S(1)}) custom-call(bf16[32,4608]{1,0:T(8,128)(2,1)} %refs_0_.4, f32[2,64,576]{2,1,0:T(8,128)} %bitcast.4, bf16[4608,2304]{1,0:T(8,128)(2,1)} %refs_4_.1, f32[4,64,2304]{2,1,0:T(8,128)} %refs_0_.5), custom_call_target="tpu_custom_call" | custom-call | tf_op jit(solution)/shard_map/pallas_call | solution.py:272
  4.3 4.0 %collective-permute-start.2 = (bf16[32,640]{1,0:T(8,128)(2,1)S(1)}, bf16[32,640]{1,0:T(8,128)(2,1)S(1)}, u32[]{:S(2)}, u32[]{:S(2)}) collective-permute-start(bf16[32,640]{1,0:T(8,128)(2,1)S(1)} %get-tuple-element.23), channel_id=1, source_target_pairs={{0,10},{1,11},{4,6},{5,7},{8,2},{9,3},{12,0},{13,1},{14,4},{15,5},... | collective-permute-start | bytes 122888 | tf_op jit(solution)/shard_map/ppermute | solution.py:416
  8.5 4.7 %collective-permute-start.4 = (bf16[32,640]{1,0:T(8,128)(2,1)S(1)}, bf16[32,640]{1,0:T(8,128)(2,1)S(1)}, u32[]{:S(2)}, u32[]{:S(2)}) collective-permute-start(bf16[32,640]{1,0:T(8,128)(2,1)S(1)} %get-tuple-element.25), channel_id=1, source_target_pairs={{0,14},{1,15},{4,10},{5,11},{8,6},{9,7},{12,2},{13,3},{14,0},{15,1... | collective-permute-start | bytes 122888 | tf_op jit(solution)/shard_map/ppermute | solution.py:416
  13.2 1.1 %collective-permute-done.2.refs_4_.refs_2_ = bf16[32,640]{1,0:T(8,128)(2,1)S(1)} collective-permute-done((bf16[32,640]{1,0:T(8,128)(2,1)S(1)}, bf16[32,640]{1,0:T(8,128)(2,1)S(1)}, u32[]{:S(2)}, u32[]{:S(2)}) %collective-permute-start.2) | collective-permute-done | bytes 40992 | tf_op jit(solution)/shard_map/ppermute | solution.py:416
  14.3 3.3 %collective-permute-done.3.refs_5_.refs_3_ = bf16[32,640]{1,0:T(8,128)(2,1)S(1)} collective-permute-done((bf16[32,640]{1,0:T(8,128)(2,1)S(1)}, bf16[32,640]{1,0:T(8,128)(2,1)S(1)}, u32[]{:S(2)}, u32[]{:S(2)}) %collective-permute-start.3) | collective-permute-done | bytes 40992 | tf_op jit(solution)/shard_map/ppermute | solution.py:416
  17.9 1.0 %collective-permute-start.6 = (bf16[32,2304]{1,0:T(8,128)(2,1)S(1)}, bf16[32,2304]{1,0:T(8,128)(2,1)S(1)}, u32[]{:S(2)}, u32[]{:S(2)}) collective-permute-start(bf16[32,2304]{1,0:T(8,128)(2,1)S(1)} %get-tuple-element.27), channel_id=1, source_target_pairs={{0,4},{1,5},{4,8},{5,9},{8,12},{9,13},{12,14},{13,15},{14,10},{15,... | collective-permute-start | bytes 442376 | tf_op jit(solution)/shard_map/ppermute | solution.py:55
  19.2 1.7 %collective-permute-start.8 = (bf16[32,2304]{1,0:T(8,128)(2,1)S(1)}, bf16[32,2304]{1,0:T(8,128)(2,1)S(1)}, u32[]{:S(2)}, u32[]{:S(2)}) collective-permute-start(bf16[32,2304]{1,0:T(8,128)(2,1)S(1)} %get-tuple-element.29), channel_id=1, source_target_pairs={{0,2},{1,3},{4,0},{5,1},{8,4},{9,5},{12,8},{13,9},{14,12},{15,13},... | collective-permute-start | bytes 442376 | tf_op jit(solution)/shard_map/ppermute | solution.py:55
  20.9 1.0 %collective-permute-start.9 = (bf16[32,2304]{1,0:T(8,128)(2,1)S(1)}, bf16[32,2304]{1,0:T(8,128)(2,1)S(1)}, u32[]{:S(2)}, u32[]{:S(2)}) collective-permute-start(bf16[32,2304]{1,0:T(8,128)(2,1)S(1)} %get-tuple-element.30), channel_id=1, source_target_pairs={{0,2},{1,3},{4,0},{5,1},{8,4},{9,5},{12,8},{13,9},{14,12},{15,13},... | collective-permute-start | bytes 442376 | tf_op jit(solution)/shard_map/ppermute | solution.py:55
  22.0 3.0 %shard_map.66.refs_1_.refs_4_ = f32[96,2304]{1,0:T(8,128)S(1)} custom-call(bf16[256,2304]{1,0:T(8,128)(2,1)S(1)} %get-tuple-element.26.refs_0_, bf16[4608,2304]{1,0:T(8,128)(2,1)S(1)} %copy-done), custom_call_target="tpu_custom_call" | custom-call | flops 2038431744 | tf_op jit(solution)/shard_map/pallas_call | solution.py:98
  25.1 1.0 %collective-permute-start.10 = (bf16[32,2304]{1,0:T(8,128)(2,1)S(1)}, bf16[32,2304]{1,0:T(8,128)(2,1)S(1)}, u32[]{:S(2)}, u32[]{:S(2)}) collective-permute-start(bf16[32,2304]{1,0:T(8,128)(2,1)S(1)} %collective-permute-done.6.refs_0_), channel_id=1, source_target_pairs={{0,4},{1,5},{4,8},{5,9},{8,12},{9,13},{12,14},{13,15},{14,10},{15,... | collective-permute-start | bytes 442376 | tf_op jit(solution)/shard_map/ppermute | solution.py:55
  26.2 1.2 %collective-permute-done.7.refs_1_ = bf16[32,2304]{1,0:T(8,128)(2,1)S(1)} collective-permute-done((bf16[32,2304]{1,0:T(8,128)(2,1)S(1)}, bf16[32,2304]{1,0:T(8,128)(2,1)S(1)}, u32[]{:S(2)}, u32[]{:S(2)}) %collective-permute-start.7) | collective-permute-done | bytes 147488 | tf_op jit(solution)/shard_map/ppermute | solution.py:55
  27.4 1.0 %collective-permute-start.11 = (bf16[32,2304]{1,0:T(8,128)(2,1)S(1)}, bf16[32,2304]{1,0:T(8,128)(2,1)S(1)}, u32[]{:S(2)}, u32[]{:S(2)}) collective-permute-start(bf16[32,2304]{1,0:T(8,128)(2,1)S(1)} %collective-permute-done.7.refs_1_), channel_id=1, source_target_pairs={{0,4},{1,5},{4,8},{5,9},{8,12},{9,13},{12,14},{13,15},{14,10},{15,... | collective-permute-start | bytes 442376 | tf_op jit(solution)/shard_map/ppermute | solution.py:55
  28.4 1.0 %collective-permute-start.12 = (bf16[32,2304]{1,0:T(8,128)(2,1)S(1)}, bf16[32,2304]{1,0:T(8,128)(2,1)S(1)}, u32[]{:S(2)}, u32[]{:S(2)}) collective-permute-start(bf16[32,2304]{1,0:T(8,128)(2,1)S(1)} %collective-permute-done.8.refs_2_), channel_id=1, source_target_pairs={{0,2},{1,3},{4,0},{5,1},{8,4},{9,5},{12,8},{13,9},{14,12},{15,13},... | collective-permute-start | bytes 442376 | tf_op jit(solution)/shard_map/ppermute | solution.py:55
  29.8 0.8 %shard_map.69 = (f32[128,128]{1,0:T(8,128)S(1)}, bf16[128,128]{1,0:T(8,128)(2,1)S(1)}) custom-call(bf16[256,2304]{1,0:T(8,128)(2,1)S(1)} %get-tuple-element.26.refs_0_, bf16[128,2304]{1,0:T(8,128)(2,1)S(1)} %shard_map.68.refs_1_.refs_0_, bf16[32,640]{1,0:T(8,128)(2,1)S(1)} %collective-permute-done.2.refs_4_.refs_2_, ...), custom_call_target="tpu_custom_call" | custom-call | tf_op jit(solution)/shard_map/pallas_call | solution.py:98
  30.6 1.1 %collective-permute-start.14 = (bf16[128,128]{1,0:T(8,128)(2,1)S(1)}, bf16[128,128]{1,0:T(8,128)(2,1)S(1)}, u32[]{:S(2)}, u32[]{:S(2)}) collective-permute-start(bf16[128,128]{1,0:T(8,128)(2,1)S(1)} %get-tuple-element.31.refs_3_), channel_id=1, source_target_pairs={{0,2},{1,3},{2,0},{3,1},{4,6},{5,7},{6,4},{7,5},{8,10},{9,11},{10,... | collective-permute-start | bytes 98312 | tf_op jit(solution)/shard_map/ppermute | solution.py:452
  31.7 3.0 %shard_map.70.refs_6_.refs_0_ = f32[192,2304]{1,0:T(8,128)S(1)} custom-call(bf16[256,2304]{1,0:T(8,128)(2,1)S(1)} %collective-permute-done.5.refs_6_.refs_0_, f32[96,2304]{1,0:T(8,128)S(1)} %shard_map.66.refs_1_.refs_4_, bf16[4608,2304]{1,0:T(8,128)(2,1)S(1)} %copy-done, bf16[128,128]{1,0:T(8,128)(2,1)S(1)} %get-tuple-element.31.refs_3_), custom_call_target="tpu_custom_call" | custom-call | flops 2038431744 | tf_op jit(solution)/shard_map/pallas_call | solution.py:98
  34.7 1.1 %collective-permute-done.14.refs_1_ = bf16[128,128]{1,0:T(8,128)(2,1)S(1)} collective-permute-done((bf16[128,128]{1,0:T(8,128)(2,1)S(1)}, bf16[128,128]{1,0:T(8,128)(2,1)S(1)}, u32[]{:S(2)}, u32[]{:S(2)}) %collective-permute-start.14) | collective-permute-done | bytes 32800 | tf_op jit(solution)/shard_map/ppermute | solution.py:452
  37.1 1.3 %collective-permute-start.19 = (bf16[128,128]{1,0:T(8,128)(2,1)S(1)}, bf16[128,128]{1,0:T(8,128)(2,1)S(1)}, u32[]{:S(2)}, u32[]{:S(2)}) collective-permute-start(bf16[128,128]{1,0:T(8,128)(2,1)S(1)} %get-tuple-element.33.refs_5_), channel_id=1, source_target_pairs={{0,4},{1,5},{2,6},{3,7},{4,8},{5,9},{6,10},{7,11},{8,12},{9,13},{1... | collective-permute-start | bytes 98312 | tf_op jit(solution)/shard_map/ppermute | solution.py:461
  38.4 1.7 %collective-permute-start.18 = (bf16[128,128]{1,0:T(8,128)(2,1)S(1)}, bf16[128,128]{1,0:T(8,128)(2,1)S(1)}, u32[]{:S(2)}, u32[]{:S(2)}) collective-permute-start(bf16[128,128]{1,0:T(8,128)(2,1)S(1)} %get-tuple-element.33.refs_5_), channel_id=1, source_target_pairs={{0,8},{1,9},{2,10},{3,11},{4,12},{5,13},{6,14},{7,15},{8,0},{9,1},... | collective-permute-start | bytes 98312 | tf_op jit(solution)/shard_map/ppermute | solution.py:461
  40.1 2.8 %collective-permute-start.17 = (bf16[128,128]{1,0:T(8,128)(2,1)S(1)}, bf16[128,128]{1,0:T(8,128)(2,1)S(1)}, u32[]{:S(2)}, u32[]{:S(2)}) collective-permute-start(bf16[128,128]{1,0:T(8,128)(2,1)S(1)} %get-tuple-element.33.refs_5_), channel_id=1, source_target_pairs={{0,12},{1,13},{2,14},{3,15},{4,0},{5,1},{6,2},{7,3},{8,4},{9,5},{1... | collective-permute-start | bytes 98312 | tf_op jit(solution)/shard_map/ppermute | solution.py:461
  42.9 2.9 %shard_map.73.refs_2_.refs_1_ = f32[128,2304]{1,0:T(8,128)S(1)} custom-call(bf16[256,2304]{1,0:T(8,128)(2,1)S(1)} %get-tuple-element.34.refs_0_, bf16[4608,2304]{1,0:T(8,128)(2,1)S(1)} %copy-done), custom_call_target="tpu_custom_call" | custom-call | flops 2717908992 | tf_op jit(solution)/shard_map/pallas_call | solution.py:98
  46.6 3.0 %shard_map.76.refs_1_ = f32[256,2304]{1,0:T(8,128)S(1)} custom-call(bf16[256,2304]{1,0:T(8,128)(2,1)S(1)} %collective-permute-done.15.refs_0_, f32[128,2304]{1,0:T(8,128)S(1)} %shard_map.73.refs_2_.refs_1_, bf16[4608,2304]{1,0:T(8,128)(2,1)S(1)} %copy-done, bf16[64,2304]{1,0:T(8,128)(2,1)S(1)} %shard_map.75.refs_3_.refs_2_), custom_call_target="tpu_custom_call" | custom-call | flops 2717908992 | tf_op jit(solution)/shard_map/pallas_call | solution.py:98
  49.6 5.2 %shard_map.77 = bf16[512,2304]{1,0:T(8,128)(2,1)} custom-call(f32[192,2304]{1,0:T(8,128)S(1)} %shard_map.70.refs_6_.refs_0_, f32[256,2304]{1,0:T(8,128)S(1)} %shard_map.76.refs_1_, bf16[64,2304]{1,0:T(8,128)(2,1)S(1)} %shard_map.75.refs_3_.refs_2_, bf16[64,2304]{1,0:T(8,128)(2,1)S(1)} %collective-permute-done.20.refs_3_, bf16[4608,2304]{1,0:T(8,128)(2,1)S(1)} %copy-done, ...), custom_call_target="tpu_custom_call" | custom-call | flops 2717908992 | bytes 2359296 | tf_op jit(solution)/shard_map/pallas_call | solution.py:372
  (44 shorter events, 3.0 us)
Async XLA Ops:
  0.0 17.6 %collective-permute-start.1 = (bf16[32,4608]{1,0:T(8,128)(2,1)}, bf16[32,4608]{1,0:T(8,128)(2,1)S(1)}, u32[]{:S(2)}, u32[]{:S(2)}) collective-permute-start(bf16[32,4608]{1,0:T(8,128)(2,1)} %refs_0_.4), channel_id=1, source_target_pairs={{0,2},{1,3},{4,0},{5,1},{8,4},{9,5},{12,8},{13,9},{14,12},{15,13},... | collective-permute-start | bytes 884744 | tf_op jit(solution)/shard_map/ppermute | solution.py:55
  3.0 14.7 %collective-permute-start = (bf16[32,4608]{1,0:T(8,128)(2,1)}, bf16[32,4608]{1,0:T(8,128)(2,1)S(1)}, u32[]{:S(2)}, u32[]{:S(2)}) collective-permute-start(bf16[32,4608]{1,0:T(8,128)(2,1)} %refs_0_.4), channel_id=1, source_target_pairs={{0,4},{1,5},{4,8},{5,9},{8,12},{9,13},{12,14},{13,15},{14,10},{15,... | collective-permute-start | bytes 884744 | tf_op jit(solution)/shard_map/ppermute | solution.py:55
  3.0 14.6 %copy-start.2 = (bf16[32,4608]{1,0:T(8,128)(2,1)S(1)}, bf16[32,4608]{1,0:T(8,128)(2,1)}, u32[]{:S(2)}) copy-start(bf16[32,4608]{1,0:T(8,128)(2,1)} %refs_0_.4) | copy-start | bytes 884740
  3.0 18.9 %copy-start = (bf16[4608,2304]{1,0:T(8,128)(2,1)S(1)}, bf16[4608,2304]{1,0:T(8,128)(2,1)}, u32[]{:S(2)}) copy-start(bf16[4608,2304]{1,0:T(8,128)(2,1)} %refs_4_.1) | copy-start | bytes 63700996
  4.3 9.9 %collective-permute-start.2 = (bf16[32,640]{1,0:T(8,128)(2,1)S(1)}, bf16[32,640]{1,0:T(8,128)(2,1)S(1)}, u32[]{:S(2)}, u32[]{:S(2)}) collective-permute-start(bf16[32,640]{1,0:T(8,128)(2,1)S(1)} %get-tuple-element.23), channel_id=1, source_target_pairs={{0,10},{1,11},{4,6},{5,7},{8,2},{9,3},{12,0},{13,1},{14,4},{15,5},... | collective-permute-start | bytes 122888 | tf_op jit(solution)/shard_map/ppermute | solution.py:416
  8.4 9.2 %collective-permute-start.3 = (bf16[32,640]{1,0:T(8,128)(2,1)S(1)}, bf16[32,640]{1,0:T(8,128)(2,1)S(1)}, u32[]{:S(2)}, u32[]{:S(2)}) collective-permute-start(bf16[32,640]{1,0:T(8,128)(2,1)S(1)} %get-tuple-element.24), channel_id=1, source_target_pairs={{0,12},{1,13},{4,14},{5,15},{8,10},{9,11},{12,6},{13,7},{14,2},{15... | collective-permute-start | bytes 122888 | tf_op jit(solution)/shard_map/ppermute | solution.py:416
  8.5 9.1 %collective-permute-start.4 = (bf16[32,640]{1,0:T(8,128)(2,1)S(1)}, bf16[32,640]{1,0:T(8,128)(2,1)S(1)}, u32[]{:S(2)}, u32[]{:S(2)}) collective-permute-start(bf16[32,640]{1,0:T(8,128)(2,1)S(1)} %get-tuple-element.25), channel_id=1, source_target_pairs={{0,14},{1,15},{4,10},{5,11},{8,6},{9,7},{12,2},{13,3},{14,0},{15,1... | collective-permute-start | bytes 122888 | tf_op jit(solution)/shard_map/ppermute | solution.py:416
  17.8 12.0 %collective-permute-start.5 = (bf16[256,2304]{1,0:T(8,128)(2,1)S(1)}, bf16[256,2304]{1,0:T(8,128)(2,1)S(1)}, u32[]{:S(2)}, u32[]{:S(2)}) collective-permute-start(bf16[256,2304]{1,0:T(8,128)(2,1)S(1)} %get-tuple-element.26.refs_0_), channel_id=1, source_target_pairs={{0,1},{1,0},{2,3},{3,2},{4,5},{5,4},{6,7},{7,6},{8,9},{9,8},{10,11... | collective-permute-start | bytes 3538952 | tf_op jit(solution)/shard_map/ppermute | solution.py:22
  17.9 7.3 %collective-permute-start.6 = (bf16[32,2304]{1,0:T(8,128)(2,1)S(1)}, bf16[32,2304]{1,0:T(8,128)(2,1)S(1)}, u32[]{:S(2)}, u32[]{:S(2)}) collective-permute-start(bf16[32,2304]{1,0:T(8,128)(2,1)S(1)} %get-tuple-element.27), channel_id=1, source_target_pairs={{0,4},{1,5},{4,8},{5,9},{8,12},{9,13},{12,14},{13,15},{14,10},{15,... | collective-permute-start | bytes 442376 | tf_op jit(solution)/shard_map/ppermute | solution.py:55
  18.9 8.5 %collective-permute-start.7 = (bf16[32,2304]{1,0:T(8,128)(2,1)S(1)}, bf16[32,2304]{1,0:T(8,128)(2,1)S(1)}, u32[]{:S(2)}, u32[]{:S(2)}) collective-permute-start(bf16[32,2304]{1,0:T(8,128)(2,1)S(1)} %get-tuple-element.28), channel_id=1, source_target_pairs={{0,4},{1,5},{4,8},{5,9},{8,12},{9,13},{12,14},{13,15},{14,10},{15,... | collective-permute-start | bytes 442376 | tf_op jit(solution)/shard_map/ppermute | solution.py:55
  19.2 9.2 %collective-permute-start.8 = (bf16[32,2304]{1,0:T(8,128)(2,1)S(1)}, bf16[32,2304]{1,0:T(8,128)(2,1)S(1)}, u32[]{:S(2)}, u32[]{:S(2)}) collective-permute-start(bf16[32,2304]{1,0:T(8,128)(2,1)S(1)} %get-tuple-element.29), channel_id=1, source_target_pairs={{0,2},{1,3},{4,0},{5,1},{8,4},{9,5},{12,8},{13,9},{14,12},{15,13},... | collective-permute-start | bytes 442376 | tf_op jit(solution)/shard_map/ppermute | solution.py:55
  20.9 8.5 %collective-permute-start.9 = (bf16[32,2304]{1,0:T(8,128)(2,1)S(1)}, bf16[32,2304]{1,0:T(8,128)(2,1)S(1)}, u32[]{:S(2)}, u32[]{:S(2)}) collective-permute-start(bf16[32,2304]{1,0:T(8,128)(2,1)S(1)} %get-tuple-element.30), channel_id=1, source_target_pairs={{0,2},{1,3},{4,0},{5,1},{8,4},{9,5},{12,8},{13,9},{14,12},{15,13},... | collective-permute-start | bytes 442376 | tf_op jit(solution)/shard_map/ppermute | solution.py:55
  25.1 10.7 %collective-permute-start.10 = (bf16[32,2304]{1,0:T(8,128)(2,1)S(1)}, bf16[32,2304]{1,0:T(8,128)(2,1)S(1)}, u32[]{:S(2)}, u32[]{:S(2)}) collective-permute-start(bf16[32,2304]{1,0:T(8,128)(2,1)S(1)} %collective-permute-done.6.refs_0_), channel_id=1, source_target_pairs={{0,4},{1,5},{4,8},{5,9},{8,12},{9,13},{12,14},{13,15},{14,10},{15,... | collective-permute-start | bytes 442376 | tf_op jit(solution)/shard_map/ppermute | solution.py:55
  27.4 8.5 %collective-permute-start.11 = (bf16[32,2304]{1,0:T(8,128)(2,1)S(1)}, bf16[32,2304]{1,0:T(8,128)(2,1)S(1)}, u32[]{:S(2)}, u32[]{:S(2)}) collective-permute-start(bf16[32,2304]{1,0:T(8,128)(2,1)S(1)} %collective-permute-done.7.refs_1_), channel_id=1, source_target_pairs={{0,4},{1,5},{4,8},{5,9},{8,12},{9,13},{12,14},{13,15},{14,10},{15,... | collective-permute-start | bytes 442376 | tf_op jit(solution)/shard_map/ppermute | solution.py:55
  28.4 7.5 %collective-permute-start.12 = (bf16[32,2304]{1,0:T(8,128)(2,1)S(1)}, bf16[32,2304]{1,0:T(8,128)(2,1)S(1)}, u32[]{:S(2)}, u32[]{:S(2)}) collective-permute-start(bf16[32,2304]{1,0:T(8,128)(2,1)S(1)} %collective-permute-done.8.refs_2_), channel_id=1, source_target_pairs={{0,2},{1,3},{4,0},{5,1},{8,4},{9,5},{12,8},{13,9},{14,12},{15,13},... | collective-permute-start | bytes 442376 | tf_op jit(solution)/shard_map/ppermute | solution.py:55
  29.4 7.2 %collective-permute-start.13 = (bf16[32,2304]{1,0:T(8,128)(2,1)S(1)}, bf16[32,2304]{1,0:T(8,128)(2,1)S(1)}, u32[]{:S(2)}, u32[]{:S(2)}) collective-permute-start(bf16[32,2304]{1,0:T(8,128)(2,1)S(1)} %collective-permute-done.9.refs_3_), channel_id=1, source_target_pairs={{0,2},{1,3},{4,0},{5,1},{8,4},{9,5},{12,8},{13,9},{14,12},{15,13},... | collective-permute-start | bytes 442376 | tf_op jit(solution)/shard_map/ppermute | solution.py:55
  30.6 5.2 %collective-permute-start.14 = (bf16[128,128]{1,0:T(8,128)(2,1)S(1)}, bf16[128,128]{1,0:T(8,128)(2,1)S(1)}, u32[]{:S(2)}, u32[]{:S(2)}) collective-permute-start(bf16[128,128]{1,0:T(8,128)(2,1)S(1)} %get-tuple-element.31.refs_3_), channel_id=1, source_target_pairs={{0,2},{1,3},{2,0},{3,1},{4,6},{5,7},{6,4},{7,5},{8,10},{9,11},{10,... | collective-permute-start | bytes 98312 | tf_op jit(solution)/shard_map/ppermute | solution.py:452
  36.7 9.9 %collective-permute-start.15 = (bf16[256,2304]{1,0:T(8,128)(2,1)S(1)}, bf16[256,2304]{1,0:T(8,128)(2,1)S(1)}, u32[]{:S(2)}, u32[]{:S(2)}) collective-permute-start(bf16[256,2304]{1,0:T(8,128)(2,1)S(1)} %get-tuple-element.34.refs_0_), channel_id=1, source_target_pairs={{0,1},{1,0},{2,3},{3,2},{4,5},{5,4},{6,7},{7,6},{8,9},{9,8},{10,11... | collective-permute-start | bytes 3538952 | tf_op jit(solution)/shard_map/ppermute | solution.py:22
  36.7 9.2 %collective-permute-start.16 = (bf16[64,2304]{1,0:T(8,128)(2,1)S(1)}, bf16[64,2304]{1,0:T(8,128)(2,1)S(1)}, u32[]{:S(2)}, u32[]{:S(2)}) collective-permute-start(bf16[64,2304]{1,0:T(8,128)(2,1)S(1)} %get-tuple-element.35), channel_id=1, source_target_pairs={{0,4},{1,3},{4,8},{5,1},{8,12},{9,5},{12,14},{13,9},{14,10},{15,13... | collective-permute-start | bytes 884744 | tf_op jit(solution)/shard_map/ppermute | solution.py:465
  37.1 8.8 %collective-permute-start.19 = (bf16[128,128]{1,0:T(8,128)(2,1)S(1)}, bf16[128,128]{1,0:T(8,128)(2,1)S(1)}, u32[]{:S(2)}, u32[]{:S(2)}) collective-permute-start(bf16[128,128]{1,0:T(8,128)(2,1)S(1)} %get-tuple-element.33.refs_5_), channel_id=1, source_target_pairs={{0,4},{1,5},{2,6},{3,7},{4,8},{5,9},{6,10},{7,11},{8,12},{9,13},{1... | collective-permute-start | bytes 98312 | tf_op jit(solution)/shard_map/ppermute | solution.py:461
  38.4 7.5 %collective-permute-start.18 = (bf16[128,128]{1,0:T(8,128)(2,1)S(1)}, bf16[128,128]{1,0:T(8,128)(2,1)S(1)}, u32[]{:S(2)}, u32[]{:S(2)}) collective-permute-start(bf16[128,128]{1,0:T(8,128)(2,1)S(1)} %get-tuple-element.33.refs_5_), channel_id=1, source_target_pairs={{0,8},{1,9},{2,10},{3,11},{4,12},{5,13},{6,14},{7,15},{8,0},{9,1},... | collective-permute-start | bytes 98312 | tf_op jit(solution)/shard_map/ppermute | solution.py:461
  40.1 5.8 %collective-permute-start.17 = (bf16[128,128]{1,0:T(8,128)(2,1)S(1)}, bf16[128,128]{1,0:T(8,128)(2,1)S(1)}, u32[]{:S(2)}, u32[]{:S(2)}) collective-permute-start(bf16[128,128]{1,0:T(8,128)(2,1)S(1)} %get-tuple-element.33.refs_5_), channel_id=1, source_target_pairs={{0,12},{1,13},{2,14},{3,15},{4,0},{5,1},{6,2},{7,3},{8,4},{9,5},{1... | collective-permute-start | bytes 98312 | tf_op jit(solution)/shard_map/ppermute | solution.py:461
  46.0 3.6 %collective-permute-start.20 = (bf16[64,2304]{1,0:T(8,128)(2,1)S(1)}, bf16[64,2304]{1,0:T(8,128)(2,1)S(1)}, u32[]{:S(2)}, u32[]{:S(2)}) collective-permute-start(bf16[64,2304]{1,0:T(8,128)(2,1)S(1)} %shard_map.75.refs_3_.refs_2_), channel_id=1, source_target_pairs={{0,1},{1,0},{2,3},{3,2},{4,5},{5,4},{6,7},{7,6},{8,9},{9,8},{10,11... | collective-permute-start | bytes 884744 | tf_op jit(solution)/shard_map/ppermute | solution.py:22
  46.1 3.5 %collective-permute-start.21 = (bf16[128,128]{1,0:T(8,128)(2,1)S(1)}, bf16[128,128]{1,0:T(8,128)(2,1)S(1)}, u32[]{:S(2)}, u32[]{:S(2)}) collective-permute-start(bf16[128,128]{1,0:T(8,128)(2,1)S(1)} %get-tuple-element.37.refs_1_), channel_id=1, source_target_pairs={{0,1},{1,0},{2,3},{3,2},{4,5},{5,4},{6,7},{7,6},{8,9},{9,8},{10,11... | collective-permute-start | bytes 98312 | tf_op jit(solution)/shard_map/ppermute | solution.py:22
  (3 other events, 11.3 us)

commit v17 on v12

--- a/solution.py
+++ b/solution.py
@@ -228,7 +228,7 @@
 def core_kernel(rows, ref, *refs):
     *weights, base, held = refs
     assemble_core(ref, base.shape[0] // rows, rows, held)
-    columns = tile_width(base.shape[1])
+    columns = narrow_width(base.shape[1])
     for j in range(0, base.shape[1], columns):
         at = slice(j, j + columns)
         base[:, at] = multiply(held, weights, at)[: base.shape[0]]
@@ -237,7 +237,7 @@
 def near_base_kernel(rows, near, mid, swapped, mine, mid_rows, weight, base, mid_base, held):
     assemble_core(swapped, near, rows, held)
     assemble_core(mid_rows, mid, rows, held, 0, near * rows)
-    columns = tile_width(base.shape[1])
+    columns = narrow_width(base.shape[1])
     for j in range(0, base.shape[1], columns):
         at = slice(j, j + columns)
         tile = multiply(held, [weight], at)
@@ -247,7 +247,7 @@
 
 def late_base_kernel(rows, mid, far, swapped, mine, weight, base, far_base, held):
     assemble_core(swapped, mid + far, rows, held)
-    columns = tile_width(base.shape[1])
+    columns = narrow_width(base.shape[1])
     for j in range(0, base.shape[1], columns):
         at = slice(j, j + columns)
         tile = multiply(held, [weight], at)
@@ -305,6 +305,10 @@
                     row = pl.multiple_of(first + core * rows, rows)
                     held[pl.ds(row, rows), k * depth : (k + 1) * depth] = ref[at : at + rows, :]
             first += 2 * rows
+
+
+def narrow_width(width):
+    return 256 if width % 256 == 0 else width
 
 
 def tile_width(width):

time: 54.6 us -> 54.6 us (level)
  no operation moved by 1% of the time
where the time goes in v17:
time: 54.6 us; the launch traced here: 54.4 us
  starting transfers between devices  27.4 us (50%)
  Pallas kernels  17.8 us (33%)
  waiting for transfers between devices  8.9 us (16%)
    pallas_call x11, Pallas kernels, call(): pl.pallas_call(body, out_shape=[pltpu.VMEM(shape, dtype) for shape, dtype...  10.8 us
    ppermute x3, starting transfers between devices, on_device(): lax.ppermute(x, AXES, ring_perm(n, d))  8.88 us
    ppermute x5, starting transfers between devices, ring_hop(): lax.ppermute(x, AXES, ring_perm(n, -1))  7.06 us
    ppermute x3, starting transfers between devices, on_device(): lax.ppermute(rounded, AXES, z_perm(n, shift))  5.84 us
    pallas_call x1, Pallas kernels, finish(): pl.pallas_call(functools.partial(finish_kernel, n, rows, groups), out_sha...  5.66 us
    ppermute x3, waiting for transfers between devices, on_device(): lax.ppermute(x, AXES, ring_perm(n, d))  4.39 us
    ppermute x5, starting transfers between devices, ring_hop(): lax.ppermute(x, AXES, ring_perm(n, 1))  3.42 us
    ppermute x3, waiting for transfers between devices, on_device(): lax.ppermute(rounded, AXES, z_perm(n, shift))  2.06 us
  transfers between devices with their start and end apart: 22, of which 8 were waited for; matrix products, arithmetic and copies ran while one was open for 0% of the time, Pallas kernels for 22%

profile of v17, /device:TPU:0, one launch (start us, length us, event | category | flops | bytes accessed | tf_op | source)
XLA Modules:
  0.0 54.4 jit_solution(854018396232265974)
XLA Ops:
  0.0 3.0 %collective-permute-start.1 = (bf16[32,4608]{1,0:T(8,128)(2,1)}, bf16[32,4608]{1,0:T(8,128)(2,1)S(1)}, u32[]{:S(2)}, u32[]{:S(2)}) collective-permute-start(bf16[32,4608]{1,0:T(8,128)(2,1)} %refs_0_.4), channel_id=1, source_target_pairs={{0,2},{1,3},{4,0},{5,1},{8,4},{9,5},{12,8},{13,9},{14,12},{15,13},... | collective-permute-start | bytes 884744 | tf_op jit(solution)/shard_map/ppermute | solution.py:55
  3.0 1.3 %shard_map.64 = (bf16[2,64,640]{2,1,0:T(8,128)(2,1)S(1)}, bf16[32,640]{1,0:T(8,128)(2,1)S(1)}, bf16[32,640]{1,0:T(8,128)(2,1)S(1)}, bf16[32,640]{1,0:T(8,128)(2,1)S(1)}) custom-call(bf16[32,4608]{1,0:T(8,128)(2,1)} %refs_0_.4, f32[2,64,576]{2,1,0:T(8,128)} %bitcast.4, bf16[4608,2304]{1,0:T(8,128)(2,1)} %refs_6_.1, f32[4,64,2304]{2,1,0:T(8,128)} %refs_0_.5), custom_call_target="tpu_custom_call" | custom-call | tf_op jit(solution)/shard_map/pallas_call | solution.py:285
  4.3 4.0 %collective-permute-start.2 = (bf16[32,640]{1,0:T(8,128)(2,1)S(1)}, bf16[32,640]{1,0:T(8,128)(2,1)S(1)}, u32[]{:S(2)}, u32[]{:S(2)}) collective-permute-start(bf16[32,640]{1,0:T(8,128)(2,1)S(1)} %get-tuple-element.27), channel_id=1, source_target_pairs={{0,10},{1,11},{4,6},{5,7},{8,2},{9,3},{12,0},{13,1},{14,4},{15,5},... | collective-permute-start | bytes 122888 | tf_op jit(solution)/shard_map/ppermute | solution.py:458
  8.5 4.7 %collective-permute-start.4 = (bf16[32,640]{1,0:T(8,128)(2,1)S(1)}, bf16[32,640]{1,0:T(8,128)(2,1)S(1)}, u32[]{:S(2)}, u32[]{:S(2)}) collective-permute-start(bf16[32,640]{1,0:T(8,128)(2,1)S(1)} %get-tuple-element.29), channel_id=1, source_target_pairs={{0,14},{1,15},{4,10},{5,11},{8,6},{9,7},{12,2},{13,3},{14,0},{15,1... | collective-permute-start | bytes 122888 | tf_op jit(solution)/shard_map/ppermute | solution.py:458
  13.2 1.1 %collective-permute-done.2.refs_4_.refs_2_ = bf16[32,640]{1,0:T(8,128)(2,1)S(1)} collective-permute-done((bf16[32,640]{1,0:T(8,128)(2,1)S(1)}, bf16[32,640]{1,0:T(8,128)(2,1)S(1)}, u32[]{:S(2)}, u32[]{:S(2)}) %collective-permute-start.2) | collective-permute-done | bytes 40992 | tf_op jit(solution)/shard_map/ppermute | solution.py:458
  14.3 3.3 %collective-permute-done.3.refs_5_.refs_3_ = bf16[32,640]{1,0:T(8,128)(2,1)S(1)} collective-permute-done((bf16[32,640]{1,0:T(8,128)(2,1)S(1)}, bf16[32,640]{1,0:T(8,128)(2,1)S(1)}, u32[]{:S(2)}, u32[]{:S(2)}) %collective-permute-start.3) | collective-permute-done | bytes 40992 | tf_op jit(solution)/shard_map/ppermute | solution.py:458
  17.9 1.0 %collective-permute-start.6 = (bf16[32,2304]{1,0:T(8,128)(2,1)S(1)}, bf16[32,2304]{1,0:T(8,128)(2,1)S(1)}, u32[]{:S(2)}, u32[]{:S(2)}) collective-permute-start(bf16[32,2304]{1,0:T(8,128)(2,1)S(1)} %get-tuple-element.31), channel_id=1, source_target_pairs={{0,4},{1,5},{4,8},{5,9},{8,12},{9,13},{12,14},{13,15},{14,10},{15,... | collective-permute-start | bytes 442376 | tf_op jit(solution)/shard_map/ppermute | solution.py:55
  19.2 1.7 %collective-permute-start.8 = (bf16[32,2304]{1,0:T(8,128)(2,1)S(1)}, bf16[32,2304]{1,0:T(8,128)(2,1)S(1)}, u32[]{:S(2)}, u32[]{:S(2)}) collective-permute-start(bf16[32,2304]{1,0:T(8,128)(2,1)S(1)} %get-tuple-element.33), channel_id=1, source_target_pairs={{0,2},{1,3},{4,0},{5,1},{8,4},{9,5},{12,8},{13,9},{14,12},{15,13},... | collective-permute-start | bytes 442376 | tf_op jit(solution)/shard_map/ppermute | solution.py:55
  20.9 1.0 %collective-permute-start.9 = (bf16[32,2304]{1,0:T(8,128)(2,1)S(1)}, bf16[32,2304]{1,0:T(8,128)(2,1)S(1)}, u32[]{:S(2)}, u32[]{:S(2)}) collective-permute-start(bf16[32,2304]{1,0:T(8,128)(2,1)S(1)} %get-tuple-element.34), channel_id=1, source_target_pairs={{0,2},{1,3},{4,0},{5,1},{8,4},{9,5},{12,8},{13,9},{14,12},{15,13},... | collective-permute-start | bytes 442376 | tf_op jit(solution)/shard_map/ppermute | solution.py:55
  22.0 3.0 %shard_map.66.refs_1_.refs_4_ = f32[96,2304]{1,0:T(8,128)S(1)} custom-call(bf16[256,2304]{1,0:T(8,128)(2,1)S(1)} %get-tuple-element.30.refs_0_, bf16[4608,2304]{1,0:T(8,128)(2,1)S(1)} %copy-done), custom_call_target="tpu_custom_call" | custom-call | flops 2717908992 | tf_op jit(solution)/shard_map/pallas_call | solution.py:98
  25.1 1.0 %collective-permute-start.10 = (bf16[32,2304]{1,0:T(8,128)(2,1)S(1)}, bf16[32,2304]{1,0:T(8,128)(2,1)S(1)}, u32[]{:S(2)}, u32[]{:S(2)}) collective-permute-start(bf16[32,2304]{1,0:T(8,128)(2,1)S(1)} %collective-permute-done.6.refs_0_), channel_id=1, source_target_pairs={{0,4},{1,5},{4,8},{5,9},{8,12},{9,13},{12,14},{13,15},{14,10},{15,... | collective-permute-start | bytes 442376 | tf_op jit(solution)/shard_map/ppermute | solution.py:55
  26.1 1.3 %collective-permute-done.7.refs_1_ = bf16[32,2304]{1,0:T(8,128)(2,1)S(1)} collective-permute-done((bf16[32,2304]{1,0:T(8,128)(2,1)S(1)}, bf16[32,2304]{1,0:T(8,128)(2,1)S(1)}, u32[]{:S(2)}, u32[]{:S(2)}) %collective-permute-start.7) | collective-permute-done | bytes 147488 | tf_op jit(solution)/shard_map/ppermute | solution.py:55
  27.4 1.0 %collective-permute-start.11 = (bf16[32,2304]{1,0:T(8,128)(2,1)S(1)}, bf16[32,2304]{1,0:T(8,128)(2,1)S(1)}, u32[]{:S(2)}, u32[]{:S(2)}) collective-permute-start(bf16[32,2304]{1,0:T(8,128)(2,1)S(1)} %collective-permute-done.7.refs_1_), channel_id=1, source_target_pairs={{0,4},{1,5},{4,8},{5,9},{8,12},{9,13},{12,14},{13,15},{14,10},{15,... | collective-permute-start | bytes 442376 | tf_op jit(solution)/shard_map/ppermute | solution.py:55
  28.4 1.0 %collective-permute-start.12 = (bf16[32,2304]{1,0:T(8,128)(2,1)S(1)}, bf16[32,2304]{1,0:T(8,128)(2,1)S(1)}, u32[]{:S(2)}, u32[]{:S(2)}) collective-permute-start(bf16[32,2304]{1,0:T(8,128)(2,1)S(1)} %collective-permute-done.8.refs_2_), channel_id=1, source_target_pairs={{0,2},{1,3},{4,0},{5,1},{8,4},{9,5},{12,8},{13,9},{14,12},{15,13},... | collective-permute-start | bytes 442376 | tf_op jit(solution)/shard_map/ppermute | solution.py:55
  29.8 0.8 %shard_map.69 = (f32[128,128]{1,0:T(8,128)S(1)}, bf16[128,128]{1,0:T(8,128)(2,1)S(1)}) custom-call(bf16[256,2304]{1,0:T(8,128)(2,1)S(1)} %get-tuple-element.30.refs_0_, bf16[128,2304]{1,0:T(8,128)(2,1)S(1)} %shard_map.68.refs_1_.refs_2_.refs_0_, bf16[32,640]{1,0:T(8,128)(2,1)S(1)} %collective-permute-done.2.refs_4_.refs_2_, ...), custom_call_target="tpu_custom_call" | custom-call | tf_op jit(solution)/shard_map/pallas_call | solution.py:98
  30.6 1.1 %collective-permute-start.14 = (bf16[128,128]{1,0:T(8,128)(2,1)S(1)}, bf16[128,128]{1,0:T(8,128)(2,1)S(1)}, u32[]{:S(2)}, u32[]{:S(2)}) collective-permute-start(bf16[128,128]{1,0:T(8,128)(2,1)S(1)} %get-tuple-element.35.refs_4_), channel_id=1, source_target_pairs={{0,2},{1,3},{2,0},{3,1},{4,6},{5,7},{6,4},{7,5},{8,10},{9,11},{10,... | collective-permute-start | bytes 98312 | tf_op jit(solution)/shard_map/ppermute | solution.py:501
  31.7 3.7 %shard_map.70 = (f32[192,2304]{1,0:T(8,128)S(1)}, f32[64,2304]{1,0:T(8,128)S(1)}) custom-call(bf16[256,2304]{1,0:T(8,128)(2,1)S(1)} %collective-permute-done.5.refs_6_.refs_0_, f32[96,2304]{1,0:T(8,128)S(1)} %shard_map.66.refs_1_.refs_4_, bf16[128,2304]{1,0:T(8,128)(2,1)S(1)} %shard_map.68.refs_1_.refs_2_.refs_0_, bf16[4608,2304]{1,0:T(8,128)(2,1)S(1)} %copy-done, ...), custom_call_target="tpu_custom_call" | custom-call | flops 3397386240 | tf_op jit(solution)/shard_map/pallas_call | solution.py:98
  35.9 0.7 %collective-permute-done.13.refs_4_ = bf16[32,2304]{1,0:T(8,128)(2,1)S(1)} collective-permute-done((bf16[32,2304]{1,0:T(8,128)(2,1)S(1)}, bf16[32,2304]{1,0:T(8,128)(2,1)S(1)}, u32[]{:S(2)}, u32[]{:S(2)}) %collective-permute-start.13) | collective-permute-done | bytes 147488 | tf_op jit(solution)/shard_map/ppermute | solution.py:55
  37.1 1.3 %collective-permute-start.19 = (bf16[128,128]{1,0:T(8,128)(2,1)S(1)}, bf16[128,128]{1,0:T(8,128)(2,1)S(1)}, u32[]{:S(2)}, u32[]{:S(2)}) collective-permute-start(bf16[128,128]{1,0:T(8,128)(2,1)S(1)} %get-tuple-element.38.refs_5_), channel_id=1, source_target_pairs={{0,4},{1,5},{2,6},{3,7},{4,8},{5,9},{6,10},{7,11},{8,12},{9,13},{1... | collective-permute-start | bytes 98312 | tf_op jit(solution)/shard_map/ppermute | solution.py:508
  38.4 1.7 %collective-permute-start.18 = (bf16[128,128]{1,0:T(8,128)(2,1)S(1)}, bf16[128,128]{1,0:T(8,128)(2,1)S(1)}, u32[]{:S(2)}, u32[]{:S(2)}) collective-permute-start(bf16[128,128]{1,0:T(8,128)(2,1)S(1)} %get-tuple-element.38.refs_5_), channel_id=1, source_target_pairs={{0,8},{1,9},{2,10},{3,11},{4,12},{5,13},{6,14},{7,15},{8,0},{9,1},... | collective-permute-start | bytes 98312 | tf_op jit(solution)/shard_map/ppermute | solution.py:508
  40.1 2.8 %collective-permute-start.17 = (bf16[128,128]{1,0:T(8,128)(2,1)S(1)}, bf16[128,128]{1,0:T(8,128)(2,1)S(1)}, u32[]{:S(2)}, u32[]{:S(2)}) collective-permute-start(bf16[128,128]{1,0:T(8,128)(2,1)S(1)} %get-tuple-element.38.refs_5_), channel_id=1, source_target_pairs={{0,12},{1,13},{2,14},{3,15},{4,0},{5,1},{6,2},{7,3},{8,4},{9,5},{1... | collective-permute-start | bytes 98312 | tf_op jit(solution)/shard_map/ppermute | solution.py:508
  43.9 1.1 %collective-permute-done.17.refs_1_ = bf16[128,128]{1,0:T(8,128)(2,1)S(1)} collective-permute-done((bf16[128,128]{1,0:T(8,128)(2,1)S(1)}, bf16[128,128]{1,0:T(8,128)(2,1)S(1)}, u32[]{:S(2)}, u32[]{:S(2)}) %collective-permute-start.17) | collective-permute-done | bytes 32800 | tf_op jit(solution)/shard_map/ppermute | solution.py:508
  45.6 3.0 %shard_map.75 = (f32[128,2304]{1,0:T(8,128)S(1)}, f32[64,2304]{1,0:T(8,128)S(1)}) custom-call(bf16[256,2304]{1,0:T(8,128)(2,1)S(1)} %collective-permute-done.15.refs_0_, f32[64,2304]{1,0:T(8,128)S(1)} %get-tuple-element.40.refs_1_, bf16[4608,2304]{1,0:T(8,128)(2,1)S(1)} %copy-done, bf16[64,2304]{1,0:T(8,128)(2,1)S(1)} %shard_map.74.refs_3_.refs_4_), custom_call_target="tpu_custom_call" | custom-call | flops 2717908992 | tf_op jit(solution)/shard_map/pallas_call | solution.py:98
  48.6 5.7 %shard_map.76 = bf16[512,2304]{1,0:T(8,128)(2,1)} custom-call(f32[192,2304]{1,0:T(8,128)S(1)} %get-tuple-element.36.refs_6_.refs_0_, f32[128,2304]{1,0:T(8,128)S(1)} %get-tuple-element.44.refs_1_, f32[64,2304]{1,0:T(8,128)S(1)} %get-tuple-element.45.refs_2_, bf16[256,2304]{1,0:T(8,128)(2,1)S(1)} %get-tuple-element.39.refs_3_, ...), custom_call_target="tpu_custom_call" | custom-call | flops 2717908992 | bytes 2359296 | tf_op jit(solution)/shard_map/pallas_call | solution.py:413
  (43 shorter events, 3.7 us)
Async XLA Ops:
  0.0 17.6 %collective-permute-start.1 = (bf16[32,4608]{1,0:T(8,128)(2,1)}, bf16[32,4608]{1,0:T(8,128)(2,1)S(1)}, u32[]{:S(2)}, u32[]{:S(2)}) collective-permute-start(bf16[32,4608]{1,0:T(8,128)(2,1)} %refs_0_.4), channel_id=1, source_target_pairs={{0,2},{1,3},{4,0},{5,1},{8,4},{9,5},{12,8},{13,9},{14,12},{15,13},... | collective-permute-start | bytes 884744 | tf_op jit(solution)/shard_map/ppermute | solution.py:55
  3.0 14.7 %collective-permute-start = (bf16[32,4608]{1,0:T(8,128)(2,1)}, bf16[32,4608]{1,0:T(8,128)(2,1)S(1)}, u32[]{:S(2)}, u32[]{:S(2)}) collective-permute-start(bf16[32,4608]{1,0:T(8,128)(2,1)} %refs_0_.4), channel_id=1, source_target_pairs={{0,4},{1,5},{4,8},{5,9},{8,12},{9,13},{12,14},{13,15},{14,10},{15,... | collective-permute-start | bytes 884744 | tf_op jit(solution)/shard_map/ppermute | solution.py:55
  3.0 14.6 %copy-start.2 = (bf16[32,4608]{1,0:T(8,128)(2,1)S(1)}, bf16[32,4608]{1,0:T(8,128)(2,1)}, u32[]{:S(2)}) copy-start(bf16[32,4608]{1,0:T(8,128)(2,1)} %refs_0_.4) | copy-start | bytes 884740
  3.0 18.9 %copy-start = (bf16[4608,2304]{1,0:T(8,128)(2,1)S(1)}, bf16[4608,2304]{1,0:T(8,128)(2,1)}, u32[]{:S(2)}) copy-start(bf16[4608,2304]{1,0:T(8,128)(2,1)} %refs_6_.1) | copy-start | bytes 63700996
  4.3 9.9 %collective-permute-start.2 = (bf16[32,640]{1,0:T(8,128)(2,1)S(1)}, bf16[32,640]{1,0:T(8,128)(2,1)S(1)}, u32[]{:S(2)}, u32[]{:S(2)}) collective-permute-start(bf16[32,640]{1,0:T(8,128)(2,1)S(1)} %get-tuple-element.27), channel_id=1, source_target_pairs={{0,10},{1,11},{4,6},{5,7},{8,2},{9,3},{12,0},{13,1},{14,4},{15,5},... | collective-permute-start | bytes 122888 | tf_op jit(solution)/shard_map/ppermute | solution.py:458
  8.4 9.2 %collective-permute-start.3 = (bf16[32,640]{1,0:T(8,128)(2,1)S(1)}, bf16[32,640]{1,0:T(8,128)(2,1)S(1)}, u32[]{:S(2)}, u32[]{:S(2)}) collective-permute-start(bf16[32,640]{1,0:T(8,128)(2,1)S(1)} %get-tuple-element.28), channel_id=1, source_target_pairs={{0,12},{1,13},{4,14},{5,15},{8,10},{9,11},{12,6},{13,7},{14,2},{15... | collective-permute-start | bytes 122888 | tf_op jit(solution)/shard_map/ppermute | solution.py:458
  8.5 9.1 %collective-permute-start.4 = (bf16[32,640]{1,0:T(8,128)(2,1)S(1)}, bf16[32,640]{1,0:T(8,128)(2,1)S(1)}, u32[]{:S(2)}, u32[]{:S(2)}) collective-permute-start(bf16[32,640]{1,0:T(8,128)(2,1)S(1)} %get-tuple-element.29), channel_id=1, source_target_pairs={{0,14},{1,15},{4,10},{5,11},{8,6},{9,7},{12,2},{13,3},{14,0},{15,1... | collective-permute-start | bytes 122888 | tf_op jit(solution)/shard_map/ppermute | solution.py:458
  17.8 12.0 %collective-permute-start.5 = (bf16[256,2304]{1,0:T(8,128)(2,1)S(1)}, bf16[256,2304]{1,0:T(8,128)(2,1)S(1)}, u32[]{:S(2)}, u32[]{:S(2)}) collective-permute-start(bf16[256,2304]{1,0:T(8,128)(2,1)S(1)} %get-tuple-element.30.refs_0_), channel_id=1, source_target_pairs={{0,1},{1,0},{2,3},{3,2},{4,5},{5,4},{6,7},{7,6},{8,9},{9,8},{10,11... | collective-permute-start | bytes 3538952 | tf_op jit(solution)/shard_map/ppermute | solution.py:22
  17.9 7.2 %collective-permute-start.6 = (bf16[32,2304]{1,0:T(8,128)(2,1)S(1)}, bf16[32,2304]{1,0:T(8,128)(2,1)S(1)}, u32[]{:S(2)}, u32[]{:S(2)}) collective-permute-start(bf16[32,2304]{1,0:T(8,128)(2,1)S(1)} %get-tuple-element.31), channel_id=1, source_target_pairs={{0,4},{1,5},{4,8},{5,9},{8,12},{9,13},{12,14},{13,15},{14,10},{15,... | collective-permute-start | bytes 442376 | tf_op jit(solution)/shard_map/ppermute | solution.py:55
  18.9 8.5 %collective-permute-start.7 = (bf16[32,2304]{1,0:T(8,128)(2,1)S(1)}, bf16[32,2304]{1,0:T(8,128)(2,1)S(1)}, u32[]{:S(2)}, u32[]{:S(2)}) collective-permute-start(bf16[32,2304]{1,0:T(8,128)(2,1)S(1)} %get-tuple-element.32), channel_id=1, source_target_pairs={{0,4},{1,5},{4,8},{5,9},{8,12},{9,13},{12,14},{13,15},{14,10},{15,... | collective-permute-start | bytes 442376 | tf_op jit(solution)/shard_map/ppermute | solution.py:55
  19.2 9.2 %collective-permute-start.8 = (bf16[32,2304]{1,0:T(8,128)(2,1)S(1)}, bf16[32,2304]{1,0:T(8,128)(2,1)S(1)}, u32[]{:S(2)}, u32[]{:S(2)}) collective-permute-start(bf16[32,2304]{1,0:T(8,128)(2,1)S(1)} %get-tuple-element.33), channel_id=1, source_target_pairs={{0,2},{1,3},{4,0},{5,1},{8,4},{9,5},{12,8},{13,9},{14,12},{15,13},... | collective-permute-start | bytes 442376 | tf_op jit(solution)/shard_map/ppermute | solution.py:55
  20.9 8.5 %collective-permute-start.9 = (bf16[32,2304]{1,0:T(8,128)(2,1)S(1)}, bf16[32,2304]{1,0:T(8,128)(2,1)S(1)}, u32[]{:S(2)}, u32[]{:S(2)}) collective-permute-start(bf16[32,2304]{1,0:T(8,128)(2,1)S(1)} %get-tuple-element.34), channel_id=1, source_target_pairs={{0,2},{1,3},{4,0},{5,1},{8,4},{9,5},{12,8},{13,9},{14,12},{15,13},... | collective-permute-start | bytes 442376 | tf_op jit(solution)/shard_map/ppermute | solution.py:55
  25.1 10.7 %collective-permute-start.10 = (bf16[32,2304]{1,0:T(8,128)(2,1)S(1)}, bf16[32,2304]{1,0:T(8,128)(2,1)S(1)}, u32[]{:S(2)}, u32[]{:S(2)}) collective-permute-start(bf16[32,2304]{1,0:T(8,128)(2,1)S(1)} %collective-permute-done.6.refs_0_), channel_id=1, source_target_pairs={{0,4},{1,5},{4,8},{5,9},{8,12},{9,13},{12,14},{13,15},{14,10},{15,... | collective-permute-start | bytes 442376 | tf_op jit(solution)/shard_map/ppermute | solution.py:55
  27.4 8.4 %collective-permute-start.11 = (bf16[32,2304]{1,0:T(8,128)(2,1)S(1)}, bf16[32,2304]{1,0:T(8,128)(2,1)S(1)}, u32[]{:S(2)}, u32[]{:S(2)}) collective-permute-start(bf16[32,2304]{1,0:T(8,128)(2,1)S(1)} %collective-permute-done.7.refs_1_), channel_id=1, source_target_pairs={{0,4},{1,5},{4,8},{5,9},{8,12},{9,13},{12,14},{13,15},{14,10},{15,... | collective-permute-start | bytes 442376 | tf_op jit(solution)/shard_map/ppermute | solution.py:55
  28.4 7.4 %collective-permute-start.12 = (bf16[32,2304]{1,0:T(8,128)(2,1)S(1)}, bf16[32,2304]{1,0:T(8,128)(2,1)S(1)}, u32[]{:S(2)}, u32[]{:S(2)}) collective-permute-start(bf16[32,2304]{1,0:T(8,128)(2,1)S(1)} %collective-permute-done.8.refs_2_), channel_id=1, source_target_pairs={{0,2},{1,3},{4,0},{5,1},{8,4},{9,5},{12,8},{13,9},{14,12},{15,13},... | collective-permute-start | bytes 442376 | tf_op jit(solution)/shard_map/ppermute | solution.py:55
  29.4 7.1 %collective-permute-start.13 = (bf16[32,2304]{1,0:T(8,128)(2,1)S(1)}, bf16[32,2304]{1,0:T(8,128)(2,1)S(1)}, u32[]{:S(2)}, u32[]{:S(2)}) collective-permute-start(bf16[32,2304]{1,0:T(8,128)(2,1)S(1)} %collective-permute-done.9.refs_3_), channel_id=1, source_target_pairs={{0,2},{1,3},{4,0},{5,1},{8,4},{9,5},{12,8},{13,9},{14,12},{15,13},... | collective-permute-start | bytes 442376 | tf_op jit(solution)/shard_map/ppermute | solution.py:55
  30.6 5.2 %collective-permute-start.14 = (bf16[128,128]{1,0:T(8,128)(2,1)S(1)}, bf16[128,128]{1,0:T(8,128)(2,1)S(1)}, u32[]{:S(2)}, u32[]{:S(2)}) collective-permute-start(bf16[128,128]{1,0:T(8,128)(2,1)S(1)} %get-tuple-element.35.refs_4_), channel_id=1, source_target_pairs={{0,2},{1,3},{2,0},{3,1},{4,6},{5,7},{6,4},{7,5},{8,10},{9,11},{10,... | collective-permute-start | bytes 98312 | tf_op jit(solution)/shard_map/ppermute | solution.py:501
  36.7 9.0 %collective-permute-start.15 = (bf16[256,2304]{1,0:T(8,128)(2,1)S(1)}, bf16[256,2304]{1,0:T(8,128)(2,1)S(1)}, u32[]{:S(2)}, u32[]{:S(2)}) collective-permute-start(bf16[256,2304]{1,0:T(8,128)(2,1)S(1)} %get-tuple-element.39.refs_3_), channel_id=1, source_target_pairs={{0,1},{1,0},{2,3},{3,2},{4,5},{5,4},{6,7},{7,6},{8,9},{9,8},{10,11... | collective-permute-start | bytes 3538952 | tf_op jit(solution)/shard_map/ppermute | solution.py:22
  36.7 8.3 %collective-permute-start.16 = (bf16[64,2304]{1,0:T(8,128)(2,1)S(1)}, bf16[64,2304]{1,0:T(8,128)(2,1)S(1)}, u32[]{:S(2)}, u32[]{:S(2)}) collective-permute-start(bf16[64,2304]{1,0:T(8,128)(2,1)S(1)} %get-tuple-element.41), channel_id=1, source_target_pairs={{0,4},{1,3},{4,8},{5,1},{8,12},{9,5},{12,14},{13,9},{14,10},{15,13... | collective-permute-start | bytes 884744 | tf_op jit(solution)/shard_map/ppermute | solution.py:512
  37.1 6.2 %collective-permute-start.19 = (bf16[128,128]{1,0:T(8,128)(2,1)S(1)}, bf16[128,128]{1,0:T(8,128)(2,1)S(1)}, u32[]{:S(2)}, u32[]{:S(2)}) collective-permute-start(bf16[128,128]{1,0:T(8,128)(2,1)S(1)} %get-tuple-element.38.refs_5_), channel_id=1, source_target_pairs={{0,4},{1,5},{2,6},{3,7},{4,8},{5,9},{6,10},{7,11},{8,12},{9,13},{1... | collective-permute-start | bytes 98312 | tf_op jit(solution)/shard_map/ppermute | solution.py:508
  38.4 5.5 %collective-permute-start.18 = (bf16[128,128]{1,0:T(8,128)(2,1)S(1)}, bf16[128,128]{1,0:T(8,128)(2,1)S(1)}, u32[]{:S(2)}, u32[]{:S(2)}) collective-permute-start(bf16[128,128]{1,0:T(8,128)(2,1)S(1)} %get-tuple-element.38.refs_5_), channel_id=1, source_target_pairs={{0,8},{1,9},{2,10},{3,11},{4,12},{5,13},{6,14},{7,15},{8,0},{9,1},... | collective-permute-start | bytes 98312 | tf_op jit(solution)/shard_map/ppermute | solution.py:508
  40.1 4.9 %collective-permute-start.17 = (bf16[128,128]{1,0:T(8,128)(2,1)S(1)}, bf16[128,128]{1,0:T(8,128)(2,1)S(1)}, u32[]{:S(2)}, u32[]{:S(2)}) collective-permute-start(bf16[128,128]{1,0:T(8,128)(2,1)S(1)} %get-tuple-element.38.refs_5_), channel_id=1, source_target_pairs={{0,12},{1,13},{2,14},{3,15},{4,0},{5,1},{6,2},{7,3},{8,4},{9,5},{1... | collective-permute-start | bytes 98312 | tf_op jit(solution)/shard_map/ppermute | solution.py:508
  45.0 3.6 %collective-permute-start.20 = (bf16[64,2304]{1,0:T(8,128)(2,1)S(1)}, bf16[64,2304]{1,0:T(8,128)(2,1)S(1)}, u32[]{:S(2)}, u32[]{:S(2)}) collective-permute-start(bf16[64,2304]{1,0:T(8,128)(2,1)S(1)} %shard_map.74.refs_3_.refs_4_), channel_id=1, source_target_pairs={{0,1},{1,0},{2,3},{3,2},{4,5},{5,4},{6,7},{7,6},{8,9},{9,8},{10,11... | collective-permute-start | bytes 884744 | tf_op jit(solution)/shard_map/ppermute | solution.py:22
  45.2 3.4 %collective-permute-start.21 = (bf16[128,128]{1,0:T(8,128)(2,1)S(1)}, bf16[128,128]{1,0:T(8,128)(2,1)S(1)}, u32[]{:S(2)}, u32[]{:S(2)}) collective-permute-start(bf16[128,128]{1,0:T(8,128)(2,1)S(1)} %get-tuple-element.43.refs_1_), channel_id=1, source_target_pairs={{0,1},{1,0},{2,3},{3,2},{4,5},{5,4},{6,7},{7,6},{8,9},{9,8},{10,11... | collective-permute-start | bytes 98312 | tf_op jit(solution)/shard_map/ppermute | solution.py:22
  (3 other events, 10.7 us)

commit v18 on v12

--- a/solution.py
+++ b/solution.py
@@ -499,24 +499,24 @@
     late_rows, turned = join([mid_rows, *up_way, *down_way], [rounded, near_base], 1)
 
     late_swapped = swap_cores(late_rows, n)
-    total, rounded = call(
-        add_kernel,
-        [total] + [lax.ppermute(rounded, AXES, z_perm(n, shift)) for shift in range(1, n // 2)],
-        [],
-        sums,
-    )
-    (last_rows,) = join([lax.ppermute(turned, AXES, ring_perm(n, 1, -1))], [rounded])
-    last_pair = (last_rows, swap_cores(last_rows, n))
-
     late = len(mid) + len(far)
     mid_base, far_base = product(
         functools.partial(late_base_kernel, rows, len(mid), len(far)),
         [late_swapped, mine],
         weight,
-        [last_rows],
+        [],
         late * rows,
         [2 * len(mid) * rows, len(far) * rows],
     )
+    total, rounded = call(
+        add_kernel,
+        [total] + [lax.ppermute(rounded, AXES, z_perm(n, shift)) for shift in range(1, n // 2)],
+        [mid_base],
+        sums,
+    )
+    (last_rows,) = join([lax.ppermute(turned, AXES, ring_perm(n, 1, -1))], [rounded])
+    last_pair = (last_rows, swap_cores(last_rows, n))
+
     return finish(
         n,
         rows,

time: 54.6 us -> 53.7 us (0.984)
  waiting for transfers between devices: 8.82 us -> 7.88 us
    ppermute x3, waiting for transfers between devices: 2.06 us -> 0.01 us  [on_device(): lax.ppermute(rounded, AXES, z_perm(n, shift))]
    ppermute x4, waiting for transfers between devices: 0.01 us -> 1.13 us  [swap_cores(): lax.ppermute(x, AXES, [(2 * s + c, 2 * s + 1 - c) for s in range(n) for c...]
  transfers between devices with their start and end apart: 22 -> 22, of which waited for: 8 -> 6; matrix products, arithmetic and copies ran while one was open for 0% -> 0% of each run, Pallas kernels for 22% -> 22%
where the time goes in v18:
time: 53.7 us; the launch traced here: 53.5 us
  starting transfers between devices  27.4 us (51%)
  Pallas kernels  17.8 us (33%)
  waiting for transfers between devices  7.88 us (15%)
    pallas_call x11, Pallas kernels, call(): pl.pallas_call(body, out_shape=[pltpu.VMEM(shape, dtype) for shape, dtype...  10.9 us
    ppermute x3, starting transfers between devices, on_device(): lax.ppermute(x, AXES, ring_perm(n, d))  8.88 us
    ppermute x5, starting transfers between devices, ring_hop(): lax.ppermute(x, AXES, ring_perm(n, -1))  7.11 us
    ppermute x3, starting transfers between devices, on_device(): lax.ppermute(rounded, AXES, z_perm(n, shift))  5.84 us
    pallas_call x1, Pallas kernels, finish(): pl.pallas_call(functools.partial(finish_kernel, n, rows, groups), out_sha...  5.65 us
    ppermute x3, waiting for transfers between devices, on_device(): lax.ppermute(x, AXES, ring_perm(n, d))  4.39 us
    ppermute x5, starting transfers between devices, ring_hop(): lax.ppermute(x, AXES, ring_perm(n, 1))  3.42 us
    pallas_call x1, Pallas kernels, prepare(): pl.pallas_call(body, out_shape=[pltpu.VMEM(shape, dtype) for shape, dtype...  1.31 us
  transfers between devices with their start and end apart: 22, of which 6 were waited for; matrix products, arithmetic and copies ran while one was open for 0% of the time, Pallas kernels for 22%

profile of v18, /device:TPU:0, one launch (start us, length us, event | category | flops | bytes accessed | tf_op | source)
XLA Modules:
  0.0 53.5 jit_solution(13384428619472487912)
XLA Ops:
  0.0 3.0 %collective-permute-start.1 = (bf16[32,4608]{1,0:T(8,128)(2,1)}, bf16[32,4608]{1,0:T(8,128)(2,1)S(1)}, u32[]{:S(2)}, u32[]{:S(2)}) collective-permute-start(bf16[32,4608]{1,0:T(8,128)(2,1)} %refs_0_.4), channel_id=1, source_target_pairs={{0,2},{1,3},{4,0},{5,1},{8,4},{9,5},{12,8},{13,9},{14,12},{15,13},... | collective-permute-start | bytes 884744 | tf_op jit(solution)/shard_map/ppermute | solution.py:55
  3.0 1.3 %shard_map.64 = (bf16[2,64,640]{2,1,0:T(8,128)(2,1)S(1)}, bf16[32,640]{1,0:T(8,128)(2,1)S(1)}, bf16[32,640]{1,0:T(8,128)(2,1)S(1)}, bf16[32,640]{1,0:T(8,128)(2,1)S(1)}) custom-call(bf16[32,4608]{1,0:T(8,128)(2,1)} %refs_0_.4, f32[2,64,576]{2,1,0:T(8,128)} %bitcast.4, bf16[4608,2304]{1,0:T(8,128)(2,1)} %refs_6_.1, f32[4,64,2304]{2,1,0:T(8,128)} %refs_0_.5), custom_call_target="tpu_custom_call" | custom-call | tf_op jit(solution)/shard_map/pallas_call | solution.py:285
  4.3 4.0 %collective-permute-start.2 = (bf16[32,640]{1,0:T(8,128)(2,1)S(1)}, bf16[32,640]{1,0:T(8,128)(2,1)S(1)}, u32[]{:S(2)}, u32[]{:S(2)}) collective-permute-start(bf16[32,640]{1,0:T(8,128)(2,1)S(1)} %get-tuple-element.27), channel_id=1, source_target_pairs={{0,10},{1,11},{4,6},{5,7},{8,2},{9,3},{12,0},{13,1},{14,4},{15,5},... | collective-permute-start | bytes 122888 | tf_op jit(solution)/shard_map/ppermute | solution.py:454
  8.5 4.7 %collective-permute-start.4 = (bf16[32,640]{1,0:T(8,128)(2,1)S(1)}, bf16[32,640]{1,0:T(8,128)(2,1)S(1)}, u32[]{:S(2)}, u32[]{:S(2)}) collective-permute-start(bf16[32,640]{1,0:T(8,128)(2,1)S(1)} %get-tuple-element.29), channel_id=1, source_target_pairs={{0,14},{1,15},{4,10},{5,11},{8,6},{9,7},{12,2},{13,3},{14,0},{15,1... | collective-permute-start | bytes 122888 | tf_op jit(solution)/shard_map/ppermute | solution.py:454
  13.2 1.1 %collective-permute-done.2.refs_4_.refs_2_ = bf16[32,640]{1,0:T(8,128)(2,1)S(1)} collective-permute-done((bf16[32,640]{1,0:T(8,128)(2,1)S(1)}, bf16[32,640]{1,0:T(8,128)(2,1)S(1)}, u32[]{:S(2)}, u32[]{:S(2)}) %collective-permute-start.2) | collective-permute-done | bytes 40992 | tf_op jit(solution)/shard_map/ppermute | solution.py:454
  14.3 3.3 %collective-permute-done.3.refs_5_.refs_3_ = bf16[32,640]{1,0:T(8,128)(2,1)S(1)} collective-permute-done((bf16[32,640]{1,0:T(8,128)(2,1)S(1)}, bf16[32,640]{1,0:T(8,128)(2,1)S(1)}, u32[]{:S(2)}, u32[]{:S(2)}) %collective-permute-start.3) | collective-permute-done | bytes 40992 | tf_op jit(solution)/shard_map/ppermute | solution.py:454
  17.9 1.0 %collective-permute-start.6 = (bf16[32,2304]{1,0:T(8,128)(2,1)S(1)}, bf16[32,2304]{1,0:T(8,128)(2,1)S(1)}, u32[]{:S(2)}, u32[]{:S(2)}) collective-permute-start(bf16[32,2304]{1,0:T(8,128)(2,1)S(1)} %get-tuple-element.31), channel_id=1, source_target_pairs={{0,4},{1,5},{4,8},{5,9},{8,12},{9,13},{12,14},{13,15},{14,10},{15,... | collective-permute-start | bytes 442376 | tf_op jit(solution)/shard_map/ppermute | solution.py:55
  19.2 1.7 %collective-permute-start.8 = (bf16[32,2304]{1,0:T(8,128)(2,1)S(1)}, bf16[32,2304]{1,0:T(8,128)(2,1)S(1)}, u32[]{:S(2)}, u32[]{:S(2)}) collective-permute-start(bf16[32,2304]{1,0:T(8,128)(2,1)S(1)} %get-tuple-element.33), channel_id=1, source_target_pairs={{0,2},{1,3},{4,0},{5,1},{8,4},{9,5},{12,8},{13,9},{14,12},{15,13},... | collective-permute-start | bytes 442376 | tf_op jit(solution)/shard_map/ppermute | solution.py:55
  20.9 1.0 %collective-permute-start.9 = (bf16[32,2304]{1,0:T(8,128)(2,1)S(1)}, bf16[32,2304]{1,0:T(8,128)(2,1)S(1)}, u32[]{:S(2)}, u32[]{:S(2)}) collective-permute-start(bf16[32,2304]{1,0:T(8,128)(2,1)S(1)} %get-tuple-element.34), channel_id=1, source_target_pairs={{0,2},{1,3},{4,0},{5,1},{8,4},{9,5},{12,8},{13,9},{14,12},{15,13},... | collective-permute-start | bytes 442376 | tf_op jit(solution)/shard_map/ppermute | solution.py:55
  22.0 3.0 %shard_map.66.refs_1_.refs_4_ = f32[96,2304]{1,0:T(8,128)S(1)} custom-call(bf16[256,2304]{1,0:T(8,128)(2,1)S(1)} %get-tuple-element.30.refs_0_, bf16[4608,2304]{1,0:T(8,128)(2,1)S(1)} %copy-done), custom_call_target="tpu_custom_call" | custom-call | flops 2717908992 | tf_op jit(solution)/shard_map/pallas_call | solution.py:98
  25.1 1.0 %collective-permute-start.10 = (bf16[32,2304]{1,0:T(8,128)(2,1)S(1)}, bf16[32,2304]{1,0:T(8,128)(2,1)S(1)}, u32[]{:S(2)}, u32[]{:S(2)}) collective-permute-start(bf16[32,2304]{1,0:T(8,128)(2,1)S(1)} %collective-permute-done.6.refs_0_), channel_id=1, source_target_pairs={{0,4},{1,5},{4,8},{5,9},{8,12},{9,13},{12,14},{13,15},{14,10},{15,... | collective-permute-start | bytes 442376 | tf_op jit(solution)/shard_map/ppermute | solution.py:55
  26.2 1.2 %collective-permute-done.7.refs_1_ = bf16[32,2304]{1,0:T(8,128)(2,1)S(1)} collective-permute-done((bf16[32,2304]{1,0:T(8,128)(2,1)S(1)}, bf16[32,2304]{1,0:T(8,128)(2,1)S(1)}, u32[]{:S(2)}, u32[]{:S(2)}) %collective-permute-start.7) | collective-permute-done | bytes 147488 | tf_op jit(solution)/shard_map/ppermute | solution.py:55
  27.4 1.0 %collective-permute-start.11 = (bf16[32,2304]{1,0:T(8,128)(2,1)S(1)}, bf16[32,2304]{1,0:T(8,128)(2,1)S(1)}, u32[]{:S(2)}, u32[]{:S(2)}) collective-permute-start(bf16[32,2304]{1,0:T(8,128)(2,1)S(1)} %collective-permute-done.7.refs_1_), channel_id=1, source_target_pairs={{0,4},{1,5},{4,8},{5,9},{8,12},{9,13},{12,14},{13,15},{14,10},{15,... | collective-permute-start | bytes 442376 | tf_op jit(solution)/shard_map/ppermute | solution.py:55
  28.4 1.0 %collective-permute-start.12 = (bf16[32,2304]{1,0:T(8,128)(2,1)S(1)}, bf16[32,2304]{1,0:T(8,128)(2,1)S(1)}, u32[]{:S(2)}, u32[]{:S(2)}) collective-permute-start(bf16[32,2304]{1,0:T(8,128)(2,1)S(1)} %collective-permute-done.8.refs_2_), channel_id=1, source_target_pairs={{0,2},{1,3},{4,0},{5,1},{8,4},{9,5},{12,8},{13,9},{14,12},{15,13},... | collective-permute-start | bytes 442376 | tf_op jit(solution)/shard_map/ppermute | solution.py:55
  29.8 0.8 %shard_map.69 = (f32[128,128]{1,0:T(8,128)S(1)}, bf16[128,128]{1,0:T(8,128)(2,1)S(1)}) custom-call(bf16[256,2304]{1,0:T(8,128)(2,1)S(1)} %get-tuple-element.30.refs_0_, bf16[128,2304]{1,0:T(8,128)(2,1)S(1)} %shard_map.68.refs_1_.refs_2_.refs_0_, bf16[32,640]{1,0:T(8,128)(2,1)S(1)} %collective-permute-done.2.refs_4_.refs_2_, ...), custom_call_target="tpu_custom_call" | custom-call | tf_op jit(solution)/shard_map/pallas_call | solution.py:98
  30.6 1.1 %collective-permute-start.14 = (bf16[128,128]{1,0:T(8,128)(2,1)S(1)}, bf16[128,128]{1,0:T(8,128)(2,1)S(1)}, u32[]{:S(2)}, u32[]{:S(2)}) collective-permute-start(bf16[128,128]{1,0:T(8,128)(2,1)S(1)} %get-tuple-element.35.refs_4_), channel_id=1, source_target_pairs={{0,2},{1,3},{2,0},{3,1},{4,6},{5,7},{6,4},{7,5},{8,10},{9,11},{10,... | collective-permute-start | bytes 98312 | tf_op jit(solution)/shard_map/ppermute | solution.py:497
  31.7 3.7 %shard_map.70 = (f32[192,2304]{1,0:T(8,128)S(1)}, f32[64,2304]{1,0:T(8,128)S(1)}) custom-call(bf16[256,2304]{1,0:T(8,128)(2,1)S(1)} %collective-permute-done.5.refs_6_.refs_0_, f32[96,2304]{1,0:T(8,128)S(1)} %shard_map.66.refs_1_.refs_4_, bf16[128,2304]{1,0:T(8,128)(2,1)S(1)} %shard_map.68.refs_1_.refs_2_.refs_0_, bf16[4608,2304]{1,0:T(8,128)(2,1)S(1)} %copy-done, ...), custom_call_target="tpu_custom_call" | custom-call | flops 3397386240 | tf_op jit(solution)/shard_map/pallas_call | solution.py:98
  35.9 0.7 %collective-permute-done.13.refs_4_ = bf16[32,2304]{1,0:T(8,128)(2,1)S(1)} collective-permute-done((bf16[32,2304]{1,0:T(8,128)(2,1)S(1)}, bf16[32,2304]{1,0:T(8,128)(2,1)S(1)}, u32[]{:S(2)}, u32[]{:S(2)}) %collective-permute-start.13) | collective-permute-done | bytes 147488 | tf_op jit(solution)/shard_map/ppermute | solution.py:55
  37.1 1.3 %collective-permute-start.19 = (bf16[128,128]{1,0:T(8,128)(2,1)S(1)}, bf16[128,128]{1,0:T(8,128)(2,1)S(1)}, u32[]{:S(2)}, u32[]{:S(2)}) collective-permute-start(bf16[128,128]{1,0:T(8,128)(2,1)S(1)} %get-tuple-element.38.refs_5_), channel_id=1, source_target_pairs={{0,4},{1,5},{2,6},{3,7},{4,8},{5,9},{6,10},{7,11},{8,12},{9,13},{1... | collective-permute-start | bytes 98312 | tf_op jit(solution)/shard_map/ppermute | solution.py:513
  38.4 1.7 %collective-permute-start.18 = (bf16[128,128]{1,0:T(8,128)(2,1)S(1)}, bf16[128,128]{1,0:T(8,128)(2,1)S(1)}, u32[]{:S(2)}, u32[]{:S(2)}) collective-permute-start(bf16[128,128]{1,0:T(8,128)(2,1)S(1)} %get-tuple-element.38.refs_5_), channel_id=1, source_target_pairs={{0,8},{1,9},{2,10},{3,11},{4,12},{5,13},{6,14},{7,15},{8,0},{9,1},... | collective-permute-start | bytes 98312 | tf_op jit(solution)/shard_map/ppermute | solution.py:513
  40.1 2.8 %collective-permute-start.17 = (bf16[128,128]{1,0:T(8,128)(2,1)S(1)}, bf16[128,128]{1,0:T(8,128)(2,1)S(1)}, u32[]{:S(2)}, u32[]{:S(2)}) collective-permute-start(bf16[128,128]{1,0:T(8,128)(2,1)S(1)} %get-tuple-element.38.refs_5_), channel_id=1, source_target_pairs={{0,12},{1,13},{2,14},{3,15},{4,0},{5,1},{6,2},{7,3},{8,4},{9,5},{1... | collective-permute-start | bytes 98312 | tf_op jit(solution)/shard_map/ppermute | solution.py:513
  42.9 3.0 %shard_map.73 = (f32[128,2304]{1,0:T(8,128)S(1)}, f32[64,2304]{1,0:T(8,128)S(1)}) custom-call(bf16[256,2304]{1,0:T(8,128)(2,1)S(1)} %collective-permute-done.15.refs_0_, f32[64,2304]{1,0:T(8,128)S(1)} %get-tuple-element.40.refs_1_, bf16[4608,2304]{1,0:T(8,128)(2,1)S(1)} %copy-done), custom_call_target="tpu_custom_call" | custom-call | flops 2717908992 | tf_op jit(solution)/shard_map/pallas_call | solution.py:98
  46.6 1.1 %collective-permute-done.21.refs_8_ = bf16[128,128]{1,0:T(8,128)(2,1)S(1)} collective-permute-done((bf16[128,128]{1,0:T(8,128)(2,1)S(1)}, bf16[128,128]{1,0:T(8,128)(2,1)S(1)}, u32[]{:S(2)}, u32[]{:S(2)}) %collective-permute-start.21) | collective-permute-done | bytes 32800 | tf_op jit(solution)/shard_map/ppermute | solution.py:22
  47.7 5.6 %shard_map.76 = bf16[512,2304]{1,0:T(8,128)(2,1)} custom-call(f32[192,2304]{1,0:T(8,128)S(1)} %get-tuple-element.36.refs_6_.refs_0_, f32[128,2304]{1,0:T(8,128)S(1)} %get-tuple-element.41.refs_4_.refs_1_, f32[64,2304]{1,0:T(8,128)S(1)} %get-tuple-element.42.refs_2_, bf16[256,2304]{1,0:T(8,128)(2,1)S(1)} %get-tuple-element.39.refs_3_, ...), custom_call_target="tpu_custom_call" | custom-call | flops 2717908992 | bytes 2359296 | tf_op jit(solution)/shard_map/pallas_call | solution.py:409
  (43 shorter events, 2.8 us)
Async XLA Ops:
  0.0 17.6 %collective-permute-start.1 = (bf16[32,4608]{1,0:T(8,128)(2,1)}, bf16[32,4608]{1,0:T(8,128)(2,1)S(1)}, u32[]{:S(2)}, u32[]{:S(2)}) collective-permute-start(bf16[32,4608]{1,0:T(8,128)(2,1)} %refs_0_.4), channel_id=1, source_target_pairs={{0,2},{1,3},{4,0},{5,1},{8,4},{9,5},{12,8},{13,9},{14,12},{15,13},... | collective-permute-start | bytes 884744 | tf_op jit(solution)/shard_map/ppermute | solution.py:55
  3.0 14.7 %collective-permute-start = (bf16[32,4608]{1,0:T(8,128)(2,1)}, bf16[32,4608]{1,0:T(8,128)(2,1)S(1)}, u32[]{:S(2)}, u32[]{:S(2)}) collective-permute-start(bf16[32,4608]{1,0:T(8,128)(2,1)} %refs_0_.4), channel_id=1, source_target_pairs={{0,4},{1,5},{4,8},{5,9},{8,12},{9,13},{12,14},{13,15},{14,10},{15,... | collective-permute-start | bytes 884744 | tf_op jit(solution)/shard_map/ppermute | solution.py:55
  3.0 14.6 %copy-start.2 = (bf16[32,4608]{1,0:T(8,128)(2,1)S(1)}, bf16[32,4608]{1,0:T(8,128)(2,1)}, u32[]{:S(2)}) copy-start(bf16[32,4608]{1,0:T(8,128)(2,1)} %refs_0_.4) | copy-start | bytes 884740
  3.0 18.9 %copy-start = (bf16[4608,2304]{1,0:T(8,128)(2,1)S(1)}, bf16[4608,2304]{1,0:T(8,128)(2,1)}, u32[]{:S(2)}) copy-start(bf16[4608,2304]{1,0:T(8,128)(2,1)} %refs_6_.1) | copy-start | bytes 63700996
  4.3 9.9 %collective-permute-start.2 = (bf16[32,640]{1,0:T(8,128)(2,1)S(1)}, bf16[32,640]{1,0:T(8,128)(2,1)S(1)}, u32[]{:S(2)}, u32[]{:S(2)}) collective-permute-start(bf16[32,640]{1,0:T(8,128)(2,1)S(1)} %get-tuple-element.27), channel_id=1, source_target_pairs={{0,10},{1,11},{4,6},{5,7},{8,2},{9,3},{12,0},{13,1},{14,4},{15,5},... | collective-permute-start | bytes 122888 | tf_op jit(solution)/shard_map/ppermute | solution.py:454
  8.4 9.2 %collective-permute-start.3 = (bf16[32,640]{1,0:T(8,128)(2,1)S(1)}, bf16[32,640]{1,0:T(8,128)(2,1)S(1)}, u32[]{:S(2)}, u32[]{:S(2)}) collective-permute-start(bf16[32,640]{1,0:T(8,128)(2,1)S(1)} %get-tuple-element.28), channel_id=1, source_target_pairs={{0,12},{1,13},{4,14},{5,15},{8,10},{9,11},{12,6},{13,7},{14,2},{15... | collective-permute-start | bytes 122888 | tf_op jit(solution)/shard_map/ppermute | solution.py:454
  8.5 9.1 %collective-permute-start.4 = (bf16[32,640]{1,0:T(8,128)(2,1)S(1)}, bf16[32,640]{1,0:T(8,128)(2,1)S(1)}, u32[]{:S(2)}, u32[]{:S(2)}) collective-permute-start(bf16[32,640]{1,0:T(8,128)(2,1)S(1)} %get-tuple-element.29), channel_id=1, source_target_pairs={{0,14},{1,15},{4,10},{5,11},{8,6},{9,7},{12,2},{13,3},{14,0},{15,1... | collective-permute-start | bytes 122888 | tf_op jit(solution)/shard_map/ppermute | solution.py:454
  17.8 12.0 %collective-permute-start.5 = (bf16[256,2304]{1,0:T(8,128)(2,1)S(1)}, bf16[256,2304]{1,0:T(8,128)(2,1)S(1)}, u32[]{:S(2)}, u32[]{:S(2)}) collective-permute-start(bf16[256,2304]{1,0:T(8,128)(2,1)S(1)} %get-tuple-element.30.refs_0_), channel_id=1, source_target_pairs={{0,1},{1,0},{2,3},{3,2},{4,5},{5,4},{6,7},{7,6},{8,9},{9,8},{10,11... | collective-permute-start | bytes 3538952 | tf_op jit(solution)/shard_map/ppermute | solution.py:22
  17.9 7.3 %collective-permute-start.6 = (bf16[32,2304]{1,0:T(8,128)(2,1)S(1)}, bf16[32,2304]{1,0:T(8,128)(2,1)S(1)}, u32[]{:S(2)}, u32[]{:S(2)}) collective-permute-start(bf16[32,2304]{1,0:T(8,128)(2,1)S(1)} %get-tuple-element.31), channel_id=1, source_target_pairs={{0,4},{1,5},{4,8},{5,9},{8,12},{9,13},{12,14},{13,15},{14,10},{15,... | collective-permute-start | bytes 442376 | tf_op jit(solution)/shard_map/ppermute | solution.py:55
  18.9 8.5 %collective-permute-start.7 = (bf16[32,2304]{1,0:T(8,128)(2,1)S(1)}, bf16[32,2304]{1,0:T(8,128)(2,1)S(1)}, u32[]{:S(2)}, u32[]{:S(2)}) collective-permute-start(bf16[32,2304]{1,0:T(8,128)(2,1)S(1)} %get-tuple-element.32), channel_id=1, source_target_pairs={{0,4},{1,5},{4,8},{5,9},{8,12},{9,13},{12,14},{13,15},{14,10},{15,... | collective-permute-start | bytes 442376 | tf_op jit(solution)/shard_map/ppermute | solution.py:55
  19.2 9.2 %collective-permute-start.8 = (bf16[32,2304]{1,0:T(8,128)(2,1)S(1)}, bf16[32,2304]{1,0:T(8,128)(2,1)S(1)}, u32[]{:S(2)}, u32[]{:S(2)}) collective-permute-start(bf16[32,2304]{1,0:T(8,128)(2,1)S(1)} %get-tuple-element.33), channel_id=1, source_target_pairs={{0,2},{1,3},{4,0},{5,1},{8,4},{9,5},{12,8},{13,9},{14,12},{15,13},... | collective-permute-start | bytes 442376 | tf_op jit(solution)/shard_map/ppermute | solution.py:55
  20.9 8.5 %collective-permute-start.9 = (bf16[32,2304]{1,0:T(8,128)(2,1)S(1)}, bf16[32,2304]{1,0:T(8,128)(2,1)S(1)}, u32[]{:S(2)}, u32[]{:S(2)}) collective-permute-start(bf16[32,2304]{1,0:T(8,128)(2,1)S(1)} %get-tuple-element.34), channel_id=1, source_target_pairs={{0,2},{1,3},{4,0},{5,1},{8,4},{9,5},{12,8},{13,9},{14,12},{15,13},... | collective-permute-start | bytes 442376 | tf_op jit(solution)/shard_map/ppermute | solution.py:55
  25.1 10.7 %collective-permute-start.10 = (bf16[32,2304]{1,0:T(8,128)(2,1)S(1)}, bf16[32,2304]{1,0:T(8,128)(2,1)S(1)}, u32[]{:S(2)}, u32[]{:S(2)}) collective-permute-start(bf16[32,2304]{1,0:T(8,128)(2,1)S(1)} %collective-permute-done.6.refs_0_), channel_id=1, source_target_pairs={{0,4},{1,5},{4,8},{5,9},{8,12},{9,13},{12,14},{13,15},{14,10},{15,... | collective-permute-start | bytes 442376 | tf_op jit(solution)/shard_map/ppermute | solution.py:55
  27.4 8.5 %collective-permute-start.11 = (bf16[32,2304]{1,0:T(8,128)(2,1)S(1)}, bf16[32,2304]{1,0:T(8,128)(2,1)S(1)}, u32[]{:S(2)}, u32[]{:S(2)}) collective-permute-start(bf16[32,2304]{1,0:T(8,128)(2,1)S(1)} %collective-permute-done.7.refs_1_), channel_id=1, source_target_pairs={{0,4},{1,5},{4,8},{5,9},{8,12},{9,13},{12,14},{13,15},{14,10},{15,... | collective-permute-start | bytes 442376 | tf_op jit(solution)/shard_map/ppermute | solution.py:55
  28.4 7.5 %collective-permute-start.12 = (bf16[32,2304]{1,0:T(8,128)(2,1)S(1)}, bf16[32,2304]{1,0:T(8,128)(2,1)S(1)}, u32[]{:S(2)}, u32[]{:S(2)}) collective-permute-start(bf16[32,2304]{1,0:T(8,128)(2,1)S(1)} %collective-permute-done.8.refs_2_), channel_id=1, source_target_pairs={{0,2},{1,3},{4,0},{5,1},{8,4},{9,5},{12,8},{13,9},{14,12},{15,13},... | collective-permute-start | bytes 442376 | tf_op jit(solution)/shard_map/ppermute | solution.py:55
  29.4 7.2 %collective-permute-start.13 = (bf16[32,2304]{1,0:T(8,128)(2,1)S(1)}, bf16[32,2304]{1,0:T(8,128)(2,1)S(1)}, u32[]{:S(2)}, u32[]{:S(2)}) collective-permute-start(bf16[32,2304]{1,0:T(8,128)(2,1)S(1)} %collective-permute-done.9.refs_3_), channel_id=1, source_target_pairs={{0,2},{1,3},{4,0},{5,1},{8,4},{9,5},{12,8},{13,9},{14,12},{15,13},... | collective-permute-start | bytes 442376 | tf_op jit(solution)/shard_map/ppermute | solution.py:55
  30.6 5.2 %collective-permute-start.14 = (bf16[128,128]{1,0:T(8,128)(2,1)S(1)}, bf16[128,128]{1,0:T(8,128)(2,1)S(1)}, u32[]{:S(2)}, u32[]{:S(2)}) collective-permute-start(bf16[128,128]{1,0:T(8,128)(2,1)S(1)} %get-tuple-element.35.refs_4_), channel_id=1, source_target_pairs={{0,2},{1,3},{2,0},{3,1},{4,6},{5,7},{6,4},{7,5},{8,10},{9,11},{10,... | collective-permute-start | bytes 98312 | tf_op jit(solution)/shard_map/ppermute | solution.py:497
  36.7 6.3 %collective-permute-start.15 = (bf16[256,2304]{1,0:T(8,128)(2,1)S(1)}, bf16[256,2304]{1,0:T(8,128)(2,1)S(1)}, u32[]{:S(2)}, u32[]{:S(2)}) collective-permute-start(bf16[256,2304]{1,0:T(8,128)(2,1)S(1)} %get-tuple-element.39.refs_3_), channel_id=1, source_target_pairs={{0,1},{1,0},{2,3},{3,2},{4,5},{5,4},{6,7},{7,6},{8,9},{9,8},{10,11... | collective-permute-start | bytes 3538952 | tf_op jit(solution)/shard_map/ppermute | solution.py:22
  36.7 9.2 %collective-permute-start.16 = (bf16[64,2304]{1,0:T(8,128)(2,1)S(1)}, bf16[64,2304]{1,0:T(8,128)(2,1)S(1)}, u32[]{:S(2)}, u32[]{:S(2)}) collective-permute-start(bf16[64,2304]{1,0:T(8,128)(2,1)S(1)} %get-tuple-element.43), channel_id=1, source_target_pairs={{0,4},{1,3},{4,8},{5,1},{8,12},{9,5},{12,14},{13,9},{14,10},{15,13... | collective-permute-start | bytes 884744 | tf_op jit(solution)/shard_map/ppermute | solution.py:517
  37.1 8.8 %collective-permute-start.19 = (bf16[128,128]{1,0:T(8,128)(2,1)S(1)}, bf16[128,128]{1,0:T(8,128)(2,1)S(1)}, u32[]{:S(2)}, u32[]{:S(2)}) collective-permute-start(bf16[128,128]{1,0:T(8,128)(2,1)S(1)} %get-tuple-element.38.refs_5_), channel_id=1, source_target_pairs={{0,4},{1,5},{2,6},{3,7},{4,8},{5,9},{6,10},{7,11},{8,12},{9,13},{1... | collective-permute-start | bytes 98312 | tf_op jit(solution)/shard_map/ppermute | solution.py:513
  38.4 7.5 %collective-permute-start.18 = (bf16[128,128]{1,0:T(8,128)(2,1)S(1)}, bf16[128,128]{1,0:T(8,128)(2,1)S(1)}, u32[]{:S(2)}, u32[]{:S(2)}) collective-permute-start(bf16[128,128]{1,0:T(8,128)(2,1)S(1)} %get-tuple-element.38.refs_5_), channel_id=1, source_target_pairs={{0,8},{1,9},{2,10},{3,11},{4,12},{5,13},{6,14},{7,15},{8,0},{9,1},... | collective-permute-start | bytes 98312 | tf_op jit(solution)/shard_map/ppermute | solution.py:513
  40.1 5.8 %collective-permute-start.17 = (bf16[128,128]{1,0:T(8,128)(2,1)S(1)}, bf16[128,128]{1,0:T(8,128)(2,1)S(1)}, u32[]{:S(2)}, u32[]{:S(2)}) collective-permute-start(bf16[128,128]{1,0:T(8,128)(2,1)S(1)} %get-tuple-element.38.refs_5_), channel_id=1, source_target_pairs={{0,12},{1,13},{2,14},{3,15},{4,0},{5,1},{6,2},{7,3},{8,4},{9,5},{1... | collective-permute-start | bytes 98312 | tf_op jit(solution)/shard_map/ppermute | solution.py:513
  46.0 1.7 %collective-permute-start.20 = (bf16[64,2304]{1,0:T(8,128)(2,1)S(1)}, bf16[64,2304]{1,0:T(8,128)(2,1)S(1)}, u32[]{:S(2)}, u32[]{:S(2)}) collective-permute-start(bf16[64,2304]{1,0:T(8,128)(2,1)S(1)} %shard_map.75.refs_4_), channel_id=1, source_target_pairs={{0,1},{1,0},{2,3},{3,2},{4,5},{5,4},{6,7},{7,6},{8,9},{9,8},{10,11... | collective-permute-start | bytes 884744 | tf_op jit(solution)/shard_map/ppermute | solution.py:22
  46.1 1.6 %collective-permute-start.21 = (bf16[128,128]{1,0:T(8,128)(2,1)S(1)}, bf16[128,128]{1,0:T(8,128)(2,1)S(1)}, u32[]{:S(2)}, u32[]{:S(2)}) collective-permute-start(bf16[128,128]{1,0:T(8,128)(2,1)S(1)} %get-tuple-element.45.refs_1_), channel_id=1, source_target_pairs={{0,1},{1,0},{2,3},{3,2},{4,5},{5,4},{6,7},{7,6},{8,9},{9,8},{10,11... | collective-permute-start | bytes 98312 | tf_op jit(solution)/shard_map/ppermute | solution.py:22
  (3 other events, 9.5 us)

commit v19 on v18

--- a/solution.py
+++ b/solution.py
@@ -376,26 +376,20 @@
         base, k = early[i]
         return base[k * chip_rows : (k + 1) * chip_rows, at]
 
-    begun, rest = range(len(early)), range(len(early), n)
-    tile = None
-    for j in range(tiles + 1):
-        done, tile = tile, multiply(held, [weight], slice(j * columns, (j + 1) * columns)) if j < tiles else None
-        if j < tiles:
-            put(j, begun, early_value)
-        if done is not None:
-            at = slice((j - 1) * columns, j * columns)
-            own_far = done[chip_rows : chip_rows + far * rows]
-            interleave(rows, far, own_far, far_base[:, at], far_rows, slice(0, columns))
-
-            def rest_value(i, at, done=done):
-                k = i - len(early)
-                return far_rows[k * chip_rows : (k + 1) * chip_rows, :] if k < far else done[:chip_rows]
-
-            put(j - 1, rest, rest_value)
-        if j < tiles:
-            send(j, begun)
-        if done is not None:
-            send(j - 1, rest)
+    for j in range(tiles):
+        at = slice(j * columns, (j + 1) * columns)
+        tile = multiply(held, [weight], at)
+        interleave(rows, far, tile[chip_rows : chip_rows + far * rows], far_base[:, at], far_rows, slice(0, columns))
+
+        def value_of(i, at, tile=tile):
+            if i < len(early):
+                return early_value(i, at)
+            k = i - len(early)
+            return far_rows[k * chip_rows : (k + 1) * chip_rows, :] if k < far else tile[:chip_rows]
+
+        for i in range(n):
+            put(j, [i], value_of)
+            send(j, [i])
     for copy in copies:
         copy.wait()
 

time: 53.7 us -> 53.4 us (level)
  no operation moved by 1% of the time
where the time goes in v19:
time: 53.4 us; the launch traced here: 53.2 us
  starting transfers between devices  27.4 us (51%)
  Pallas kernels  17.5 us (33%)
  waiting for transfers between devices  7.88 us (15%)
    pallas_call x11, Pallas kernels, call(): pl.pallas_call(body, out_shape=[pltpu.VMEM(shape, dtype) for shape, dtype...  10.9 us
    ppermute x3, starting transfers between devices, on_device(): lax.ppermute(x, AXES, ring_perm(n, d))  8.88 us
    ppermute x5, starting transfers between devices, ring_hop(): lax.ppermute(x, AXES, ring_perm(n, -1))  7.11 us
    ppermute x3, starting transfers between devices, on_device(): lax.ppermute(rounded, AXES, z_perm(n, shift))  5.84 us
    pallas_call x1, Pallas kernels, finish(): pl.pallas_call(functools.partial(finish_kernel, n, rows, groups), out_sha...  5.35 us
    ppermute x3, waiting for transfers between devices, on_device(): lax.ppermute(x, AXES, ring_perm(n, d))  4.39 us
    ppermute x5, starting transfers between devices, ring_hop(): lax.ppermute(x, AXES, ring_perm(n, 1))  3.42 us
    pallas_call x1, Pallas kernels, prepare(): pl.pallas_call(body, out_shape=[pltpu.VMEM(shape, dtype) for shape, dtype...  1.31 us
  transfers between devices with their start and end apart: 22, of which 6 were waited for; matrix products, arithmetic and copies ran while one was open for 0% of the time, Pallas kernels for 22%

profile of v19, /device:TPU:0, one launch (start us, length us, event | category | flops | bytes accessed | tf_op | source)
XLA Modules:
  0.0 53.2 jit_solution(5269840742817419104)
XLA Ops:
  0.0 3.0 %collective-permute-start.1 = (bf16[32,4608]{1,0:T(8,128)(2,1)}, bf16[32,4608]{1,0:T(8,128)(2,1)S(1)}, u32[]{:S(2)}, u32[]{:S(2)}) collective-permute-start(bf16[32,4608]{1,0:T(8,128)(2,1)} %refs_0_.4), channel_id=1, source_target_pairs={{0,2},{1,3},{4,0},{5,1},{8,4},{9,5},{12,8},{13,9},{14,12},{15,13},... | collective-permute-start | bytes 884744 | tf_op jit(solution)/shard_map/ppermute | solution.py:55
  3.0 1.3 %shard_map.64 = (bf16[2,64,640]{2,1,0:T(8,128)(2,1)S(1)}, bf16[32,640]{1,0:T(8,128)(2,1)S(1)}, bf16[32,640]{1,0:T(8,128)(2,1)S(1)}, bf16[32,640]{1,0:T(8,128)(2,1)S(1)}) custom-call(bf16[32,4608]{1,0:T(8,128)(2,1)} %refs_0_.4, f32[2,64,576]{2,1,0:T(8,128)} %bitcast.4, bf16[4608,2304]{1,0:T(8,128)(2,1)} %refs_6_.1, f32[4,64,2304]{2,1,0:T(8,128)} %refs_0_.5), custom_call_target="tpu_custom_call" | custom-call | tf_op jit(solution)/shard_map/pallas_call | solution.py:285
  4.3 4.0 %collective-permute-start.2 = (bf16[32,640]{1,0:T(8,128)(2,1)S(1)}, bf16[32,640]{1,0:T(8,128)(2,1)S(1)}, u32[]{:S(2)}, u32[]{:S(2)}) collective-permute-start(bf16[32,640]{1,0:T(8,128)(2,1)S(1)} %get-tuple-element.27), channel_id=1, source_target_pairs={{0,10},{1,11},{4,6},{5,7},{8,2},{9,3},{12,0},{13,1},{14,4},{15,5},... | collective-permute-start | bytes 122888 | tf_op jit(solution)/shard_map/ppermute | solution.py:448
  8.5 4.7 %collective-permute-start.4 = (bf16[32,640]{1,0:T(8,128)(2,1)S(1)}, bf16[32,640]{1,0:T(8,128)(2,1)S(1)}, u32[]{:S(2)}, u32[]{:S(2)}) collective-permute-start(bf16[32,640]{1,0:T(8,128)(2,1)S(1)} %get-tuple-element.29), channel_id=1, source_target_pairs={{0,14},{1,15},{4,10},{5,11},{8,6},{9,7},{12,2},{13,3},{14,0},{15,1... | collective-permute-start | bytes 122888 | tf_op jit(solution)/shard_map/ppermute | solution.py:448
  13.2 1.1 %collective-permute-done.2.refs_4_.refs_2_ = bf16[32,640]{1,0:T(8,128)(2,1)S(1)} collective-permute-done((bf16[32,640]{1,0:T(8,128)(2,1)S(1)}, bf16[32,640]{1,0:T(8,128)(2,1)S(1)}, u32[]{:S(2)}, u32[]{:S(2)}) %collective-permute-start.2) | collective-permute-done | bytes 40992 | tf_op jit(solution)/shard_map/ppermute | solution.py:448
  14.3 3.3 %collective-permute-done.3.refs_5_.refs_3_ = bf16[32,640]{1,0:T(8,128)(2,1)S(1)} collective-permute-done((bf16[32,640]{1,0:T(8,128)(2,1)S(1)}, bf16[32,640]{1,0:T(8,128)(2,1)S(1)}, u32[]{:S(2)}, u32[]{:S(2)}) %collective-permute-start.3) | collective-permute-done | bytes 40992 | tf_op jit(solution)/shard_map/ppermute | solution.py:448
  17.9 1.0 %collective-permute-start.6 = (bf16[32,2304]{1,0:T(8,128)(2,1)S(1)}, bf16[32,2304]{1,0:T(8,128)(2,1)S(1)}, u32[]{:S(2)}, u32[]{:S(2)}) collective-permute-start(bf16[32,2304]{1,0:T(8,128)(2,1)S(1)} %get-tuple-element.31), channel_id=1, source_target_pairs={{0,4},{1,5},{4,8},{5,9},{8,12},{9,13},{12,14},{13,15},{14,10},{15,... | collective-permute-start | bytes 442376 | tf_op jit(solution)/shard_map/ppermute | solution.py:55
  19.2 1.7 %collective-permute-start.8 = (bf16[32,2304]{1,0:T(8,128)(2,1)S(1)}, bf16[32,2304]{1,0:T(8,128)(2,1)S(1)}, u32[]{:S(2)}, u32[]{:S(2)}) collective-permute-start(bf16[32,2304]{1,0:T(8,128)(2,1)S(1)} %get-tuple-element.33), channel_id=1, source_target_pairs={{0,2},{1,3},{4,0},{5,1},{8,4},{9,5},{12,8},{13,9},{14,12},{15,13},... | collective-permute-start | bytes 442376 | tf_op jit(solution)/shard_map/ppermute | solution.py:55
  20.9 1.0 %collective-permute-start.9 = (bf16[32,2304]{1,0:T(8,128)(2,1)S(1)}, bf16[32,2304]{1,0:T(8,128)(2,1)S(1)}, u32[]{:S(2)}, u32[]{:S(2)}) collective-permute-start(bf16[32,2304]{1,0:T(8,128)(2,1)S(1)} %get-tuple-element.34), channel_id=1, source_target_pairs={{0,2},{1,3},{4,0},{5,1},{8,4},{9,5},{12,8},{13,9},{14,12},{15,13},... | collective-permute-start | bytes 442376 | tf_op jit(solution)/shard_map/ppermute | solution.py:55
  22.0 3.0 %shard_map.66.refs_1_.refs_4_ = f32[96,2304]{1,0:T(8,128)S(1)} custom-call(bf16[256,2304]{1,0:T(8,128)(2,1)S(1)} %get-tuple-element.30.refs_0_, bf16[4608,2304]{1,0:T(8,128)(2,1)S(1)} %copy-done), custom_call_target="tpu_custom_call" | custom-call | flops 2717908992 | tf_op jit(solution)/shard_map/pallas_call | solution.py:98
  25.1 1.0 %collective-permute-start.10 = (bf16[32,2304]{1,0:T(8,128)(2,1)S(1)}, bf16[32,2304]{1,0:T(8,128)(2,1)S(1)}, u32[]{:S(2)}, u32[]{:S(2)}) collective-permute-start(bf16[32,2304]{1,0:T(8,128)(2,1)S(1)} %collective-permute-done.6.refs_0_), channel_id=1, source_target_pairs={{0,4},{1,5},{4,8},{5,9},{8,12},{9,13},{12,14},{13,15},{14,10},{15,... | collective-permute-start | bytes 442376 | tf_op jit(solution)/shard_map/ppermute | solution.py:55
  26.2 1.2 %collective-permute-done.7.refs_1_ = bf16[32,2304]{1,0:T(8,128)(2,1)S(1)} collective-permute-done((bf16[32,2304]{1,0:T(8,128)(2,1)S(1)}, bf16[32,2304]{1,0:T(8,128)(2,1)S(1)}, u32[]{:S(2)}, u32[]{:S(2)}) %collective-permute-start.7) | collective-permute-done | bytes 147488 | tf_op jit(solution)/shard_map/ppermute | solution.py:55
  27.4 1.0 %collective-permute-start.11 = (bf16[32,2304]{1,0:T(8,128)(2,1)S(1)}, bf16[32,2304]{1,0:T(8,128)(2,1)S(1)}, u32[]{:S(2)}, u32[]{:S(2)}) collective-permute-start(bf16[32,2304]{1,0:T(8,128)(2,1)S(1)} %collective-permute-done.7.refs_1_), channel_id=1, source_target_pairs={{0,4},{1,5},{4,8},{5,9},{8,12},{9,13},{12,14},{13,15},{14,10},{15,... | collective-permute-start | bytes 442376 | tf_op jit(solution)/shard_map/ppermute | solution.py:55
  28.4 1.0 %collective-permute-start.12 = (bf16[32,2304]{1,0:T(8,128)(2,1)S(1)}, bf16[32,2304]{1,0:T(8,128)(2,1)S(1)}, u32[]{:S(2)}, u32[]{:S(2)}) collective-permute-start(bf16[32,2304]{1,0:T(8,128)(2,1)S(1)} %collective-permute-done.8.refs_2_), channel_id=1, source_target_pairs={{0,2},{1,3},{4,0},{5,1},{8,4},{9,5},{12,8},{13,9},{14,12},{15,13},... | collective-permute-start | bytes 442376 | tf_op jit(solution)/shard_map/ppermute | solution.py:55
  29.8 0.8 %shard_map.69 = (f32[128,128]{1,0:T(8,128)S(1)}, bf16[128,128]{1,0:T(8,128)(2,1)S(1)}) custom-call(bf16[256,2304]{1,0:T(8,128)(2,1)S(1)} %get-tuple-element.30.refs_0_, bf16[128,2304]{1,0:T(8,128)(2,1)S(1)} %shard_map.68.refs_1_.refs_2_.refs_0_, bf16[32,640]{1,0:T(8,128)(2,1)S(1)} %collective-permute-done.2.refs_4_.refs_2_, ...), custom_call_target="tpu_custom_call" | custom-call | tf_op jit(solution)/shard_map/pallas_call | solution.py:98
  30.6 1.1 %collective-permute-start.14 = (bf16[128,128]{1,0:T(8,128)(2,1)S(1)}, bf16[128,128]{1,0:T(8,128)(2,1)S(1)}, u32[]{:S(2)}, u32[]{:S(2)}) collective-permute-start(bf16[128,128]{1,0:T(8,128)(2,1)S(1)} %get-tuple-element.35.refs_4_), channel_id=1, source_target_pairs={{0,2},{1,3},{2,0},{3,1},{4,6},{5,7},{6,4},{7,5},{8,10},{9,11},{10,... | collective-permute-start | bytes 98312 | tf_op jit(solution)/shard_map/ppermute | solution.py:491
  31.7 3.7 %shard_map.70 = (f32[192,2304]{1,0:T(8,128)S(1)}, f32[64,2304]{1,0:T(8,128)S(1)}) custom-call(bf16[256,2304]{1,0:T(8,128)(2,1)S(1)} %collective-permute-done.5.refs_6_.refs_0_, f32[96,2304]{1,0:T(8,128)S(1)} %shard_map.66.refs_1_.refs_4_, bf16[128,2304]{1,0:T(8,128)(2,1)S(1)} %shard_map.68.refs_1_.refs_2_.refs_0_, bf16[4608,2304]{1,0:T(8,128)(2,1)S(1)} %copy-done, ...), custom_call_target="tpu_custom_call" | custom-call | flops 3397386240 | tf_op jit(solution)/shard_map/pallas_call | solution.py:98
  35.9 0.7 %collective-permute-done.13.refs_4_ = bf16[32,2304]{1,0:T(8,128)(2,1)S(1)} collective-permute-done((bf16[32,2304]{1,0:T(8,128)(2,1)S(1)}, bf16[32,2304]{1,0:T(8,128)(2,1)S(1)}, u32[]{:S(2)}, u32[]{:S(2)}) %collective-permute-start.13) | collective-permute-done | bytes 147488 | tf_op jit(solution)/shard_map/ppermute | solution.py:55
  37.1 1.3 %collective-permute-start.19 = (bf16[128,128]{1,0:T(8,128)(2,1)S(1)}, bf16[128,128]{1,0:T(8,128)(2,1)S(1)}, u32[]{:S(2)}, u32[]{:S(2)}) collective-permute-start(bf16[128,128]{1,0:T(8,128)(2,1)S(1)} %get-tuple-element.38.refs_5_), channel_id=1, source_target_pairs={{0,4},{1,5},{2,6},{3,7},{4,8},{5,9},{6,10},{7,11},{8,12},{9,13},{1... | collective-permute-start | bytes 98312 | tf_op jit(solution)/shard_map/ppermute | solution.py:507
  38.4 1.7 %collective-permute-start.18 = (bf16[128,128]{1,0:T(8,128)(2,1)S(1)}, bf16[128,128]{1,0:T(8,128)(2,1)S(1)}, u32[]{:S(2)}, u32[]{:S(2)}) collective-permute-start(bf16[128,128]{1,0:T(8,128)(2,1)S(1)} %get-tuple-element.38.refs_5_), channel_id=1, source_target_pairs={{0,8},{1,9},{2,10},{3,11},{4,12},{5,13},{6,14},{7,15},{8,0},{9,1},... | collective-permute-start | bytes 98312 | tf_op jit(solution)/shard_map/ppermute | solution.py:507
  40.1 2.8 %collective-permute-start.17 = (bf16[128,128]{1,0:T(8,128)(2,1)S(1)}, bf16[128,128]{1,0:T(8,128)(2,1)S(1)}, u32[]{:S(2)}, u32[]{:S(2)}) collective-permute-start(bf16[128,128]{1,0:T(8,128)(2,1)S(1)} %get-tuple-element.38.refs_5_), channel_id=1, source_target_pairs={{0,12},{1,13},{2,14},{3,15},{4,0},{5,1},{6,2},{7,3},{8,4},{9,5},{1... | collective-permute-start | bytes 98312 | tf_op jit(solution)/shard_map/ppermute | solution.py:507
  42.9 3.0 %shard_map.73 = (f32[128,2304]{1,0:T(8,128)S(1)}, f32[64,2304]{1,0:T(8,128)S(1)}) custom-call(bf16[256,2304]{1,0:T(8,128)(2,1)S(1)} %collective-permute-done.15.refs_0_, f32[64,2304]{1,0:T(8,128)S(1)} %get-tuple-element.40.refs_1_, bf16[4608,2304]{1,0:T(8,128)(2,1)S(1)} %copy-done), custom_call_target="tpu_custom_call" | custom-call | flops 2717908992 | tf_op jit(solution)/shard_map/pallas_call | solution.py:98
  46.6 1.1 %collective-permute-done.21.refs_8_ = bf16[128,128]{1,0:T(8,128)(2,1)S(1)} collective-permute-done((bf16[128,128]{1,0:T(8,128)(2,1)S(1)}, bf16[128,128]{1,0:T(8,128)(2,1)S(1)}, u32[]{:S(2)}, u32[]{:S(2)}) %collective-permute-start.21) | collective-permute-done | bytes 32800 | tf_op jit(solution)/shard_map/ppermute | solution.py:22
  47.7 5.3 %shard_map.76 = bf16[512,2304]{1,0:T(8,128)(2,1)} custom-call(f32[192,2304]{1,0:T(8,128)S(1)} %get-tuple-element.36.refs_6_.refs_0_, f32[128,2304]{1,0:T(8,128)S(1)} %get-tuple-element.41.refs_4_.refs_1_, f32[64,2304]{1,0:T(8,128)S(1)} %get-tuple-element.42.refs_2_, bf16[256,2304]{1,0:T(8,128)(2,1)S(1)} %get-tuple-element.39.refs_3_, ...), custom_call_target="tpu_custom_call" | custom-call | flops 2717908992 | bytes 2359296 | tf_op jit(solution)/shard_map/pallas_call | solution.py:403
  (43 shorter events, 2.8 us)
Async XLA Ops:
  0.0 17.6 %collective-permute-start.1 = (bf16[32,4608]{1,0:T(8,128)(2,1)}, bf16[32,4608]{1,0:T(8,128)(2,1)S(1)}, u32[]{:S(2)}, u32[]{:S(2)}) collective-permute-start(bf16[32,4608]{1,0:T(8,128)(2,1)} %refs_0_.4), channel_id=1, source_target_pairs={{0,2},{1,3},{4,0},{5,1},{8,4},{9,5},{12,8},{13,9},{14,12},{15,13},... | collective-permute-start | bytes 884744 | tf_op jit(solution)/shard_map/ppermute | solution.py:55
  3.0 14.7 %collective-permute-start = (bf16[32,4608]{1,0:T(8,128)(2,1)}, bf16[32,4608]{1,0:T(8,128)(2,1)S(1)}, u32[]{:S(2)}, u32[]{:S(2)}) collective-permute-start(bf16[32,4608]{1,0:T(8,128)(2,1)} %refs_0_.4), channel_id=1, source_target_pairs={{0,4},{1,5},{4,8},{5,9},{8,12},{9,13},{12,14},{13,15},{14,10},{15,... | collective-permute-start | bytes 884744 | tf_op jit(solution)/shard_map/ppermute | solution.py:55
  3.0 14.6 %copy-start.2 = (bf16[32,4608]{1,0:T(8,128)(2,1)S(1)}, bf16[32,4608]{1,0:T(8,128)(2,1)}, u32[]{:S(2)}) copy-start(bf16[32,4608]{1,0:T(8,128)(2,1)} %refs_0_.4) | copy-start | bytes 884740
  3.0 18.9 %copy-start = (bf16[4608,2304]{1,0:T(8,128)(2,1)S(1)}, bf16[4608,2304]{1,0:T(8,128)(2,1)}, u32[]{:S(2)}) copy-start(bf16[4608,2304]{1,0:T(8,128)(2,1)} %refs_6_.1) | copy-start | bytes 63700996
  4.3 9.9 %collective-permute-start.2 = (bf16[32,640]{1,0:T(8,128)(2,1)S(1)}, bf16[32,640]{1,0:T(8,128)(2,1)S(1)}, u32[]{:S(2)}, u32[]{:S(2)}) collective-permute-start(bf16[32,640]{1,0:T(8,128)(2,1)S(1)} %get-tuple-element.27), channel_id=1, source_target_pairs={{0,10},{1,11},{4,6},{5,7},{8,2},{9,3},{12,0},{13,1},{14,4},{15,5},... | collective-permute-start | bytes 122888 | tf_op jit(solution)/shard_map/ppermute | solution.py:448
  8.4 9.2 %collective-permute-start.3 = (bf16[32,640]{1,0:T(8,128)(2,1)S(1)}, bf16[32,640]{1,0:T(8,128)(2,1)S(1)}, u32[]{:S(2)}, u32[]{:S(2)}) collective-permute-start(bf16[32,640]{1,0:T(8,128)(2,1)S(1)} %get-tuple-element.28), channel_id=1, source_target_pairs={{0,12},{1,13},{4,14},{5,15},{8,10},{9,11},{12,6},{13,7},{14,2},{15... | collective-permute-start | bytes 122888 | tf_op jit(solution)/shard_map/ppermute | solution.py:448
  8.5 9.1 %collective-permute-start.4 = (bf16[32,640]{1,0:T(8,128)(2,1)S(1)}, bf16[32,640]{1,0:T(8,128)(2,1)S(1)}, u32[]{:S(2)}, u32[]{:S(2)}) collective-permute-start(bf16[32,640]{1,0:T(8,128)(2,1)S(1)} %get-tuple-element.29), channel_id=1, source_target_pairs={{0,14},{1,15},{4,10},{5,11},{8,6},{9,7},{12,2},{13,3},{14,0},{15,1... | collective-permute-start | bytes 122888 | tf_op jit(solution)/shard_map/ppermute | solution.py:448
  17.8 12.0 %collective-permute-start.5 = (bf16[256,2304]{1,0:T(8,128)(2,1)S(1)}, bf16[256,2304]{1,0:T(8,128)(2,1)S(1)}, u32[]{:S(2)}, u32[]{:S(2)}) collective-permute-start(bf16[256,2304]{1,0:T(8,128)(2,1)S(1)} %get-tuple-element.30.refs_0_), channel_id=1, source_target_pairs={{0,1},{1,0},{2,3},{3,2},{4,5},{5,4},{6,7},{7,6},{8,9},{9,8},{10,11... | collective-permute-start | bytes 3538952 | tf_op jit(solution)/shard_map/ppermute | solution.py:22
  17.9 7.3 %collective-permute-start.6 = (bf16[32,2304]{1,0:T(8,128)(2,1)S(1)}, bf16[32,2304]{1,0:T(8,128)(2,1)S(1)}, u32[]{:S(2)}, u32[]{:S(2)}) collective-permute-start(bf16[32,2304]{1,0:T(8,128)(2,1)S(1)} %get-tuple-element.31), channel_id=1, source_target_pairs={{0,4},{1,5},{4,8},{5,9},{8,12},{9,13},{12,14},{13,15},{14,10},{15,... | collective-permute-start | bytes 442376 | tf_op jit(solution)/shard_map/ppermute | solution.py:55
  18.9 8.5 %collective-permute-start.7 = (bf16[32,2304]{1,0:T(8,128)(2,1)S(1)}, bf16[32,2304]{1,0:T(8,128)(2,1)S(1)}, u32[]{:S(2)}, u32[]{:S(2)}) collective-permute-start(bf16[32,2304]{1,0:T(8,128)(2,1)S(1)} %get-tuple-element.32), channel_id=1, source_target_pairs={{0,4},{1,5},{4,8},{5,9},{8,12},{9,13},{12,14},{13,15},{14,10},{15,... | collective-permute-start | bytes 442376 | tf_op jit(solution)/shard_map/ppermute | solution.py:55
  19.2 9.2 %collective-permute-start.8 = (bf16[32,2304]{1,0:T(8,128)(2,1)S(1)}, bf16[32,2304]{1,0:T(8,128)(2,1)S(1)}, u32[]{:S(2)}, u32[]{:S(2)}) collective-permute-start(bf16[32,2304]{1,0:T(8,128)(2,1)S(1)} %get-tuple-element.33), channel_id=1, source_target_pairs={{0,2},{1,3},{4,0},{5,1},{8,4},{9,5},{12,8},{13,9},{14,12},{15,13},... | collective-permute-start | bytes 442376 | tf_op jit(solution)/shard_map/ppermute | solution.py:55
  20.9 8.5 %collective-permute-start.9 = (bf16[32,2304]{1,0:T(8,128)(2,1)S(1)}, bf16[32,2304]{1,0:T(8,128)(2,1)S(1)}, u32[]{:S(2)}, u32[]{:S(2)}) collective-permute-start(bf16[32,2304]{1,0:T(8,128)(2,1)S(1)} %get-tuple-element.34), channel_id=1, source_target_pairs={{0,2},{1,3},{4,0},{5,1},{8,4},{9,5},{12,8},{13,9},{14,12},{15,13},... | collective-permute-start | bytes 442376 | tf_op jit(solution)/shard_map/ppermute | solution.py:55
  25.1 10.7 %collective-permute-start.10 = (bf16[32,2304]{1,0:T(8,128)(2,1)S(1)}, bf16[32,2304]{1,0:T(8,128)(2,1)S(1)}, u32[]{:S(2)}, u32[]{:S(2)}) collective-permute-start(bf16[32,2304]{1,0:T(8,128)(2,1)S(1)} %collective-permute-done.6.refs_0_), channel_id=1, source_target_pairs={{0,4},{1,5},{4,8},{5,9},{8,12},{9,13},{12,14},{13,15},{14,10},{15,... | collective-permute-start | bytes 442376 | tf_op jit(solution)/shard_map/ppermute | solution.py:55
  27.4 8.5 %collective-permute-start.11 = (bf16[32,2304]{1,0:T(8,128)(2,1)S(1)}, bf16[32,2304]{1,0:T(8,128)(2,1)S(1)}, u32[]{:S(2)}, u32[]{:S(2)}) collective-permute-start(bf16[32,2304]{1,0:T(8,128)(2,1)S(1)} %collective-permute-done.7.refs_1_), channel_id=1, source_target_pairs={{0,4},{1,5},{4,8},{5,9},{8,12},{9,13},{12,14},{13,15},{14,10},{15,... | collective-permute-start | bytes 442376 | tf_op jit(solution)/shard_map/ppermute | solution.py:55
  28.4 7.5 %collective-permute-start.12 = (bf16[32,2304]{1,0:T(8,128)(2,1)S(1)}, bf16[32,2304]{1,0:T(8,128)(2,1)S(1)}, u32[]{:S(2)}, u32[]{:S(2)}) collective-permute-start(bf16[32,2304]{1,0:T(8,128)(2,1)S(1)} %collective-permute-done.8.refs_2_), channel_id=1, source_target_pairs={{0,2},{1,3},{4,0},{5,1},{8,4},{9,5},{12,8},{13,9},{14,12},{15,13},... | collective-permute-start | bytes 442376 | tf_op jit(solution)/shard_map/ppermute | solution.py:55
  29.4 7.2 %collective-permute-start.13 = (bf16[32,2304]{1,0:T(8,128)(2,1)S(1)}, bf16[32,2304]{1,0:T(8,128)(2,1)S(1)}, u32[]{:S(2)}, u32[]{:S(2)}) collective-permute-start(bf16[32,2304]{1,0:T(8,128)(2,1)S(1)} %collective-permute-done.9.refs_3_), channel_id=1, source_target_pairs={{0,2},{1,3},{4,0},{5,1},{8,4},{9,5},{12,8},{13,9},{14,12},{15,13},... | collective-permute-start | bytes 442376 | tf_op jit(solution)/shard_map/ppermute | solution.py:55
  30.6 5.2 %collective-permute-start.14 = (bf16[128,128]{1,0:T(8,128)(2,1)S(1)}, bf16[128,128]{1,0:T(8,128)(2,1)S(1)}, u32[]{:S(2)}, u32[]{:S(2)}) collective-permute-start(bf16[128,128]{1,0:T(8,128)(2,1)S(1)} %get-tuple-element.35.refs_4_), channel_id=1, source_target_pairs={{0,2},{1,3},{2,0},{3,1},{4,6},{5,7},{6,4},{7,5},{8,10},{9,11},{10,... | collective-permute-start | bytes 98312 | tf_op jit(solution)/shard_map/ppermute | solution.py:491
  36.7 6.3 %collective-permute-start.15 = (bf16[256,2304]{1,0:T(8,128)(2,1)S(1)}, bf16[256,2304]{1,0:T(8,128)(2,1)S(1)}, u32[]{:S(2)}, u32[]{:S(2)}) collective-permute-start(bf16[256,2304]{1,0:T(8,128)(2,1)S(1)} %get-tuple-element.39.refs_3_), channel_id=1, source_target_pairs={{0,1},{1,0},{2,3},{3,2},{4,5},{5,4},{6,7},{7,6},{8,9},{9,8},{10,11... | collective-permute-start | bytes 3538952 | tf_op jit(solution)/shard_map/ppermute | solution.py:22
  36.7 9.2 %collective-permute-start.16 = (bf16[64,2304]{1,0:T(8,128)(2,1)S(1)}, bf16[64,2304]{1,0:T(8,128)(2,1)S(1)}, u32[]{:S(2)}, u32[]{:S(2)}) collective-permute-start(bf16[64,2304]{1,0:T(8,128)(2,1)S(1)} %get-tuple-element.43), channel_id=1, source_target_pairs={{0,4},{1,3},{4,8},{5,1},{8,12},{9,5},{12,14},{13,9},{14,10},{15,13... | collective-permute-start | bytes 884744 | tf_op jit(solution)/shard_map/ppermute | solution.py:511
  37.1 8.8 %collective-permute-start.19 = (bf16[128,128]{1,0:T(8,128)(2,1)S(1)}, bf16[128,128]{1,0:T(8,128)(2,1)S(1)}, u32[]{:S(2)}, u32[]{:S(2)}) collective-permute-start(bf16[128,128]{1,0:T(8,128)(2,1)S(1)} %get-tuple-element.38.refs_5_), channel_id=1, source_target_pairs={{0,4},{1,5},{2,6},{3,7},{4,8},{5,9},{6,10},{7,11},{8,12},{9,13},{1... | collective-permute-start | bytes 98312 | tf_op jit(solution)/shard_map/ppermute | solution.py:507
  38.4 7.5 %collective-permute-start.18 = (bf16[128,128]{1,0:T(8,128)(2,1)S(1)}, bf16[128,128]{1,0:T(8,128)(2,1)S(1)}, u32[]{:S(2)}, u32[]{:S(2)}) collective-permute-start(bf16[128,128]{1,0:T(8,128)(2,1)S(1)} %get-tuple-element.38.refs_5_), channel_id=1, source_target_pairs={{0,8},{1,9},{2,10},{3,11},{4,12},{5,13},{6,14},{7,15},{8,0},{9,1},... | collective-permute-start | bytes 98312 | tf_op jit(solution)/shard_map/ppermute | solution.py:507
  40.1 5.8 %collective-permute-start.17 = (bf16[128,128]{1,0:T(8,128)(2,1)S(1)}, bf16[128,128]{1,0:T(8,128)(2,1)S(1)}, u32[]{:S(2)}, u32[]{:S(2)}) collective-permute-start(bf16[128,128]{1,0:T(8,128)(2,1)S(1)} %get-tuple-element.38.refs_5_), channel_id=1, source_target_pairs={{0,12},{1,13},{2,14},{3,15},{4,0},{5,1},{6,2},{7,3},{8,4},{9,5},{1... | collective-permute-start | bytes 98312 | tf_op jit(solution)/shard_map/ppermute | solution.py:507
  46.0 1.7 %collective-permute-start.20 = (bf16[64,2304]{1,0:T(8,128)(2,1)S(1)}, bf16[64,2304]{1,0:T(8,128)(2,1)S(1)}, u32[]{:S(2)}, u32[]{:S(2)}) collective-permute-start(bf16[64,2304]{1,0:T(8,128)(2,1)S(1)} %shard_map.75.refs_4_), channel_id=1, source_target_pairs={{0,1},{1,0},{2,3},{3,2},{4,5},{5,4},{6,7},{7,6},{8,9},{9,8},{10,11... | collective-permute-start | bytes 884744 | tf_op jit(solution)/shard_map/ppermute | solution.py:22
  46.1 1.6 %collective-permute-start.21 = (bf16[128,128]{1,0:T(8,128)(2,1)S(1)}, bf16[128,128]{1,0:T(8,128)(2,1)S(1)}, u32[]{:S(2)}, u32[]{:S(2)}) collective-permute-start(bf16[128,128]{1,0:T(8,128)(2,1)S(1)} %get-tuple-element.45.refs_1_), channel_id=1, source_target_pairs={{0,1},{1,0},{2,3},{3,2},{4,5},{5,4},{6,7},{7,6},{8,9},{9,8},{10,11... | collective-permute-start | bytes 98312 | tf_op jit(solution)/shard_map/ppermute | solution.py:22
  (3 other events, 9.5 us)

commit v20 on v19

--- a/solution.py
+++ b/solution.py
@@ -396,7 +396,7 @@
 
 def finish(n, rows, groups, lookups, bases, late, weight, sums, up):
     (rank, width), depth = up.shape[1:], weight.shape[0]
-    total, columns = 2 * n * rows, tile_width(width)
+    total, columns = 2 * n * rows, 256 if width % 256 == 0 else width
     arrays = [*bases, *late, weight, *sums, up]
     far = len(groups[2])
     held = full_rows((2 + far) * rows)

time: 53.4 us -> 54 us (1.011)
  Pallas kernels: 17.5 us -> 18.1 us
    pallas_call x1, Pallas kernels: 5.35 us -> 5.95 us  [finish(): pl.pallas_call(functools.partial(finish_kernel, n, rows, groups), out_sha...]
where the time goes in v20:
time: 54 us; the launch traced here: 53.8 us
  starting transfers between devices  27.4 us (51%)
  Pallas kernels  18.1 us (34%)
  waiting for transfers between devices  7.88 us (15%)
    pallas_call x11, Pallas kernels, call(): pl.pallas_call(body, out_shape=[pltpu.VMEM(shape, dtype) for shape, dtype...  10.9 us
    ppermute x3, starting transfers between devices, on_device(): lax.ppermute(x, AXES, ring_perm(n, d))  8.88 us
    ppermute x5, starting transfers between devices, ring_hop(): lax.ppermute(x, AXES, ring_perm(n, -1))  7.11 us
    pallas_call x1, Pallas kernels, finish(): pl.pallas_call(functools.partial(finish_kernel, n, rows, groups), out_sha...  5.95 us
    ppermute x3, starting transfers between devices, on_device(): lax.ppermute(rounded, AXES, z_perm(n, shift))  5.84 us
    ppermute x3, waiting for transfers between devices, on_device(): lax.ppermute(x, AXES, ring_perm(n, d))  4.39 us
    ppermute x5, starting transfers between devices, ring_hop(): lax.ppermute(x, AXES, ring_perm(n, 1))  3.42 us
    pallas_call x1, Pallas kernels, prepare(): pl.pallas_call(body, out_shape=[pltpu.VMEM(shape, dtype) for shape, dtype...  1.31 us
  transfers between devices with their start and end apart: 22, of which 6 were waited for; matrix products, arithmetic and copies ran while one was open for 0% of the time, Pallas kernels for 22%

profile of v20, /device:TPU:0, one launch (start us, length us, event | category | flops | bytes accessed | tf_op | source)
XLA Modules:
  0.0 53.8 jit_solution(3205188265215516651)
XLA Ops:
  0.0 3.0 %collective-permute-start.1 = (bf16[32,4608]{1,0:T(8,128)(2,1)}, bf16[32,4608]{1,0:T(8,128)(2,1)S(1)}, u32[]{:S(2)}, u32[]{:S(2)}) collective-permute-start(bf16[32,4608]{1,0:T(8,128)(2,1)} %refs_0_.4), channel_id=1, source_target_pairs={{0,2},{1,3},{4,0},{5,1},{8,4},{9,5},{12,8},{13,9},{14,12},{15,13},... | collective-permute-start | bytes 884744 | tf_op jit(solution)/shard_map/ppermute | solution.py:55
  3.0 1.3 %shard_map.64 = (bf16[2,64,640]{2,1,0:T(8,128)(2,1)S(1)}, bf16[32,640]{1,0:T(8,128)(2,1)S(1)}, bf16[32,640]{1,0:T(8,128)(2,1)S(1)}, bf16[32,640]{1,0:T(8,128)(2,1)S(1)}) custom-call(bf16[32,4608]{1,0:T(8,128)(2,1)} %refs_0_.4, f32[2,64,576]{2,1,0:T(8,128)} %bitcast.4, bf16[4608,2304]{1,0:T(8,128)(2,1)} %refs_6_.1, f32[4,64,2304]{2,1,0:T(8,128)} %refs_0_.5), custom_call_target="tpu_custom_call" | custom-call | tf_op jit(solution)/shard_map/pallas_call | solution.py:285
  4.3 4.0 %collective-permute-start.2 = (bf16[32,640]{1,0:T(8,128)(2,1)S(1)}, bf16[32,640]{1,0:T(8,128)(2,1)S(1)}, u32[]{:S(2)}, u32[]{:S(2)}) collective-permute-start(bf16[32,640]{1,0:T(8,128)(2,1)S(1)} %get-tuple-element.27), channel_id=1, source_target_pairs={{0,10},{1,11},{4,6},{5,7},{8,2},{9,3},{12,0},{13,1},{14,4},{15,5},... | collective-permute-start | bytes 122888 | tf_op jit(solution)/shard_map/ppermute | solution.py:448
  8.5 4.7 %collective-permute-start.4 = (bf16[32,640]{1,0:T(8,128)(2,1)S(1)}, bf16[32,640]{1,0:T(8,128)(2,1)S(1)}, u32[]{:S(2)}, u32[]{:S(2)}) collective-permute-start(bf16[32,640]{1,0:T(8,128)(2,1)S(1)} %get-tuple-element.29), channel_id=1, source_target_pairs={{0,14},{1,15},{4,10},{5,11},{8,6},{9,7},{12,2},{13,3},{14,0},{15,1... | collective-permute-start | bytes 122888 | tf_op jit(solution)/shard_map/ppermute | solution.py:448
  13.2 1.1 %collective-permute-done.2.refs_4_.refs_2_ = bf16[32,640]{1,0:T(8,128)(2,1)S(1)} collective-permute-done((bf16[32,640]{1,0:T(8,128)(2,1)S(1)}, bf16[32,640]{1,0:T(8,128)(2,1)S(1)}, u32[]{:S(2)}, u32[]{:S(2)}) %collective-permute-start.2) | collective-permute-done | bytes 40992 | tf_op jit(solution)/shard_map/ppermute | solution.py:448
  14.3 3.3 %collective-permute-done.3.refs_5_.refs_3_ = bf16[32,640]{1,0:T(8,128)(2,1)S(1)} collective-permute-done((bf16[32,640]{1,0:T(8,128)(2,1)S(1)}, bf16[32,640]{1,0:T(8,128)(2,1)S(1)}, u32[]{:S(2)}, u32[]{:S(2)}) %collective-permute-start.3) | collective-permute-done | bytes 40992 | tf_op jit(solution)/shard_map/ppermute | solution.py:448
  17.9 1.0 %collective-permute-start.6 = (bf16[32,2304]{1,0:T(8,128)(2,1)S(1)}, bf16[32,2304]{1,0:T(8,128)(2,1)S(1)}, u32[]{:S(2)}, u32[]{:S(2)}) collective-permute-start(bf16[32,2304]{1,0:T(8,128)(2,1)S(1)} %get-tuple-element.31), channel_id=1, source_target_pairs={{0,4},{1,5},{4,8},{5,9},{8,12},{9,13},{12,14},{13,15},{14,10},{15,... | collective-permute-start | bytes 442376 | tf_op jit(solution)/shard_map/ppermute | solution.py:55
  19.2 1.7 %collective-permute-start.8 = (bf16[32,2304]{1,0:T(8,128)(2,1)S(1)}, bf16[32,2304]{1,0:T(8,128)(2,1)S(1)}, u32[]{:S(2)}, u32[]{:S(2)}) collective-permute-start(bf16[32,2304]{1,0:T(8,128)(2,1)S(1)} %get-tuple-element.33), channel_id=1, source_target_pairs={{0,2},{1,3},{4,0},{5,1},{8,4},{9,5},{12,8},{13,9},{14,12},{15,13},... | collective-permute-start | bytes 442376 | tf_op jit(solution)/shard_map/ppermute | solution.py:55
  20.9 1.0 %collective-permute-start.9 = (bf16[32,2304]{1,0:T(8,128)(2,1)S(1)}, bf16[32,2304]{1,0:T(8,128)(2,1)S(1)}, u32[]{:S(2)}, u32[]{:S(2)}) collective-permute-start(bf16[32,2304]{1,0:T(8,128)(2,1)S(1)} %get-tuple-element.34), channel_id=1, source_target_pairs={{0,2},{1,3},{4,0},{5,1},{8,4},{9,5},{12,8},{13,9},{14,12},{15,13},... | collective-permute-start | bytes 442376 | tf_op jit(solution)/shard_map/ppermute | solution.py:55
  22.0 3.0 %shard_map.66.refs_1_.refs_4_ = f32[96,2304]{1,0:T(8,128)S(1)} custom-call(bf16[256,2304]{1,0:T(8,128)(2,1)S(1)} %get-tuple-element.30.refs_0_, bf16[4608,2304]{1,0:T(8,128)(2,1)S(1)} %copy-done), custom_call_target="tpu_custom_call" | custom-call | flops 2717908992 | tf_op jit(solution)/shard_map/pallas_call | solution.py:98
  25.1 1.0 %collective-permute-start.10 = (bf16[32,2304]{1,0:T(8,128)(2,1)S(1)}, bf16[32,2304]{1,0:T(8,128)(2,1)S(1)}, u32[]{:S(2)}, u32[]{:S(2)}) collective-permute-start(bf16[32,2304]{1,0:T(8,128)(2,1)S(1)} %collective-permute-done.6.refs_0_), channel_id=1, source_target_pairs={{0,4},{1,5},{4,8},{5,9},{8,12},{9,13},{12,14},{13,15},{14,10},{15,... | collective-permute-start | bytes 442376 | tf_op jit(solution)/shard_map/ppermute | solution.py:55
  26.2 1.2 %collective-permute-done.7.refs_1_ = bf16[32,2304]{1,0:T(8,128)(2,1)S(1)} collective-permute-done((bf16[32,2304]{1,0:T(8,128)(2,1)S(1)}, bf16[32,2304]{1,0:T(8,128)(2,1)S(1)}, u32[]{:S(2)}, u32[]{:S(2)}) %collective-permute-start.7) | collective-permute-done | bytes 147488 | tf_op jit(solution)/shard_map/ppermute | solution.py:55
  27.4 1.0 %collective-permute-start.11 = (bf16[32,2304]{1,0:T(8,128)(2,1)S(1)}, bf16[32,2304]{1,0:T(8,128)(2,1)S(1)}, u32[]{:S(2)}, u32[]{:S(2)}) collective-permute-start(bf16[32,2304]{1,0:T(8,128)(2,1)S(1)} %collective-permute-done.7.refs_1_), channel_id=1, source_target_pairs={{0,4},{1,5},{4,8},{5,9},{8,12},{9,13},{12,14},{13,15},{14,10},{15,... | collective-permute-start | bytes 442376 | tf_op jit(solution)/shard_map/ppermute | solution.py:55
  28.4 1.0 %collective-permute-start.12 = (bf16[32,2304]{1,0:T(8,128)(2,1)S(1)}, bf16[32,2304]{1,0:T(8,128)(2,1)S(1)}, u32[]{:S(2)}, u32[]{:S(2)}) collective-permute-start(bf16[32,2304]{1,0:T(8,128)(2,1)S(1)} %collective-permute-done.8.refs_2_), channel_id=1, source_target_pairs={{0,2},{1,3},{4,0},{5,1},{8,4},{9,5},{12,8},{13,9},{14,12},{15,13},... | collective-permute-start | bytes 442376 | tf_op jit(solution)/shard_map/ppermute | solution.py:55
  29.8 0.8 %shard_map.69 = (f32[128,128]{1,0:T(8,128)S(1)}, bf16[128,128]{1,0:T(8,128)(2,1)S(1)}) custom-call(bf16[256,2304]{1,0:T(8,128)(2,1)S(1)} %get-tuple-element.30.refs_0_, bf16[128,2304]{1,0:T(8,128)(2,1)S(1)} %shard_map.68.refs_1_.refs_2_.refs_0_, bf16[32,640]{1,0:T(8,128)(2,1)S(1)} %collective-permute-done.2.refs_4_.refs_2_, ...), custom_call_target="tpu_custom_call" | custom-call | tf_op jit(solution)/shard_map/pallas_call | solution.py:98
  30.6 1.1 %collective-permute-start.14 = (bf16[128,128]{1,0:T(8,128)(2,1)S(1)}, bf16[128,128]{1,0:T(8,128)(2,1)S(1)}, u32[]{:S(2)}, u32[]{:S(2)}) collective-permute-start(bf16[128,128]{1,0:T(8,128)(2,1)S(1)} %get-tuple-element.35.refs_4_), channel_id=1, source_target_pairs={{0,2},{1,3},{2,0},{3,1},{4,6},{5,7},{6,4},{7,5},{8,10},{9,11},{10,... | collective-permute-start | bytes 98312 | tf_op jit(solution)/shard_map/ppermute | solution.py:491
  31.7 3.7 %shard_map.70 = (f32[192,2304]{1,0:T(8,128)S(1)}, f32[64,2304]{1,0:T(8,128)S(1)}) custom-call(bf16[256,2304]{1,0:T(8,128)(2,1)S(1)} %collective-permute-done.5.refs_6_.refs_0_, f32[96,2304]{1,0:T(8,128)S(1)} %shard_map.66.refs_1_.refs_4_, bf16[128,2304]{1,0:T(8,128)(2,1)S(1)} %shard_map.68.refs_1_.refs_2_.refs_0_, bf16[4608,2304]{1,0:T(8,128)(2,1)S(1)} %copy-done, ...), custom_call_target="tpu_custom_call" | custom-call | flops 3397386240 | tf_op jit(solution)/shard_map/pallas_call | solution.py:98
  35.9 0.7 %collective-permute-done.13.refs_4_ = bf16[32,2304]{1,0:T(8,128)(2,1)S(1)} collective-permute-done((bf16[32,2304]{1,0:T(8,128)(2,1)S(1)}, bf16[32,2304]{1,0:T(8,128)(2,1)S(1)}, u32[]{:S(2)}, u32[]{:S(2)}) %collective-permute-start.13) | collective-permute-done | bytes 147488 | tf_op jit(solution)/shard_map/ppermute | solution.py:55
  37.1 1.3 %collective-permute-start.19 = (bf16[128,128]{1,0:T(8,128)(2,1)S(1)}, bf16[128,128]{1,0:T(8,128)(2,1)S(1)}, u32[]{:S(2)}, u32[]{:S(2)}) collective-permute-start(bf16[128,128]{1,0:T(8,128)(2,1)S(1)} %get-tuple-element.38.refs_5_), channel_id=1, source_target_pairs={{0,4},{1,5},{2,6},{3,7},{4,8},{5,9},{6,10},{7,11},{8,12},{9,13},{1... | collective-permute-start | bytes 98312 | tf_op jit(solution)/shard_map/ppermute | solution.py:507
  38.4 1.7 %collective-permute-start.18 = (bf16[128,128]{1,0:T(8,128)(2,1)S(1)}, bf16[128,128]{1,0:T(8,128)(2,1)S(1)}, u32[]{:S(2)}, u32[]{:S(2)}) collective-permute-start(bf16[128,128]{1,0:T(8,128)(2,1)S(1)} %get-tuple-element.38.refs_5_), channel_id=1, source_target_pairs={{0,8},{1,9},{2,10},{3,11},{4,12},{5,13},{6,14},{7,15},{8,0},{9,1},... | collective-permute-start | bytes 98312 | tf_op jit(solution)/shard_map/ppermute | solution.py:507
  40.1 2.8 %collective-permute-start.17 = (bf16[128,128]{1,0:T(8,128)(2,1)S(1)}, bf16[128,128]{1,0:T(8,128)(2,1)S(1)}, u32[]{:S(2)}, u32[]{:S(2)}) collective-permute-start(bf16[128,128]{1,0:T(8,128)(2,1)S(1)} %get-tuple-element.38.refs_5_), channel_id=1, source_target_pairs={{0,12},{1,13},{2,14},{3,15},{4,0},{5,1},{6,2},{7,3},{8,4},{9,5},{1... | collective-permute-start | bytes 98312 | tf_op jit(solution)/shard_map/ppermute | solution.py:507
  42.9 3.0 %shard_map.73 = (f32[128,2304]{1,0:T(8,128)S(1)}, f32[64,2304]{1,0:T(8,128)S(1)}) custom-call(bf16[256,2304]{1,0:T(8,128)(2,1)S(1)} %collective-permute-done.15.refs_0_, f32[64,2304]{1,0:T(8,128)S(1)} %get-tuple-element.40.refs_1_, bf16[4608,2304]{1,0:T(8,128)(2,1)S(1)} %copy-done), custom_call_target="tpu_custom_call" | custom-call | flops 2717908992 | tf_op jit(solution)/shard_map/pallas_call | solution.py:98
  46.6 1.1 %collective-permute-done.21.refs_8_ = bf16[128,128]{1,0:T(8,128)(2,1)S(1)} collective-permute-done((bf16[128,128]{1,0:T(8,128)(2,1)S(1)}, bf16[128,128]{1,0:T(8,128)(2,1)S(1)}, u32[]{:S(2)}, u32[]{:S(2)}) %collective-permute-start.21) | collective-permute-done | bytes 32800 | tf_op jit(solution)/shard_map/ppermute | solution.py:22
  47.7 5.9 %shard_map.76 = bf16[512,2304]{1,0:T(8,128)(2,1)} custom-call(f32[192,2304]{1,0:T(8,128)S(1)} %get-tuple-element.36.refs_6_.refs_0_, f32[128,2304]{1,0:T(8,128)S(1)} %get-tuple-element.41.refs_4_.refs_1_, f32[64,2304]{1,0:T(8,128)S(1)} %get-tuple-element.42.refs_2_, bf16[256,2304]{1,0:T(8,128)(2,1)S(1)} %get-tuple-element.39.refs_3_, ...), custom_call_target="tpu_custom_call" | custom-call | flops 2717908992 | bytes 2359296 | tf_op jit(solution)/shard_map/pallas_call | solution.py:403
  (43 shorter events, 2.8 us)
Async XLA Ops:
  0.0 17.6 %collective-permute-start.1 = (bf16[32,4608]{1,0:T(8,128)(2,1)}, bf16[32,4608]{1,0:T(8,128)(2,1)S(1)}, u32[]{:S(2)}, u32[]{:S(2)}) collective-permute-start(bf16[32,4608]{1,0:T(8,128)(2,1)} %refs_0_.4), channel_id=1, source_target_pairs={{0,2},{1,3},{4,0},{5,1},{8,4},{9,5},{12,8},{13,9},{14,12},{15,13},... | collective-permute-start | bytes 884744 | tf_op jit(solution)/shard_map/ppermute | solution.py:55
  3.0 14.7 %collective-permute-start = (bf16[32,4608]{1,0:T(8,128)(2,1)}, bf16[32,4608]{1,0:T(8,128)(2,1)S(1)}, u32[]{:S(2)}, u32[]{:S(2)}) collective-permute-start(bf16[32,4608]{1,0:T(8,128)(2,1)} %refs_0_.4), channel_id=1, source_target_pairs={{0,4},{1,5},{4,8},{5,9},{8,12},{9,13},{12,14},{13,15},{14,10},{15,... | collective-permute-start | bytes 884744 | tf_op jit(solution)/shard_map/ppermute | solution.py:55
  3.0 14.6 %copy-start.2 = (bf16[32,4608]{1,0:T(8,128)(2,1)S(1)}, bf16[32,4608]{1,0:T(8,128)(2,1)}, u32[]{:S(2)}) copy-start(bf16[32,4608]{1,0:T(8,128)(2,1)} %refs_0_.4) | copy-start | bytes 884740
  3.0 18.9 %copy-start = (bf16[4608,2304]{1,0:T(8,128)(2,1)S(1)}, bf16[4608,2304]{1,0:T(8,128)(2,1)}, u32[]{:S(2)}) copy-start(bf16[4608,2304]{1,0:T(8,128)(2,1)} %refs_6_.1) | copy-start | bytes 63700996
  4.3 9.9 %collective-permute-start.2 = (bf16[32,640]{1,0:T(8,128)(2,1)S(1)}, bf16[32,640]{1,0:T(8,128)(2,1)S(1)}, u32[]{:S(2)}, u32[]{:S(2)}) collective-permute-start(bf16[32,640]{1,0:T(8,128)(2,1)S(1)} %get-tuple-element.27), channel_id=1, source_target_pairs={{0,10},{1,11},{4,6},{5,7},{8,2},{9,3},{12,0},{13,1},{14,4},{15,5},... | collective-permute-start | bytes 122888 | tf_op jit(solution)/shard_map/ppermute | solution.py:448
  8.4 9.2 %collective-permute-start.3 = (bf16[32,640]{1,0:T(8,128)(2,1)S(1)}, bf16[32,640]{1,0:T(8,128)(2,1)S(1)}, u32[]{:S(2)}, u32[]{:S(2)}) collective-permute-start(bf16[32,640]{1,0:T(8,128)(2,1)S(1)} %get-tuple-element.28), channel_id=1, source_target_pairs={{0,12},{1,13},{4,14},{5,15},{8,10},{9,11},{12,6},{13,7},{14,2},{15... | collective-permute-start | bytes 122888 | tf_op jit(solution)/shard_map/ppermute | solution.py:448
  8.5 9.1 %collective-permute-start.4 = (bf16[32,640]{1,0:T(8,128)(2,1)S(1)}, bf16[32,640]{1,0:T(8,128)(2,1)S(1)}, u32[]{:S(2)}, u32[]{:S(2)}) collective-permute-start(bf16[32,640]{1,0:T(8,128)(2,1)S(1)} %get-tuple-element.29), channel_id=1, source_target_pairs={{0,14},{1,15},{4,10},{5,11},{8,6},{9,7},{12,2},{13,3},{14,0},{15,1... | collective-permute-start | bytes 122888 | tf_op jit(solution)/shard_map/ppermute | solution.py:448
  17.8 12.0 %collective-permute-start.5 = (bf16[256,2304]{1,0:T(8,128)(2,1)S(1)}, bf16[256,2304]{1,0:T(8,128)(2,1)S(1)}, u32[]{:S(2)}, u32[]{:S(2)}) collective-permute-start(bf16[256,2304]{1,0:T(8,128)(2,1)S(1)} %get-tuple-element.30.refs_0_), channel_id=1, source_target_pairs={{0,1},{1,0},{2,3},{3,2},{4,5},{5,4},{6,7},{7,6},{8,9},{9,8},{10,11... | collective-permute-start | bytes 3538952 | tf_op jit(solution)/shard_map/ppermute | solution.py:22
  17.9 7.3 %collective-permute-start.6 = (bf16[32,2304]{1,0:T(8,128)(2,1)S(1)}, bf16[32,2304]{1,0:T(8,128)(2,1)S(1)}, u32[]{:S(2)}, u32[]{:S(2)}) collective-permute-start(bf16[32,2304]{1,0:T(8,128)(2,1)S(1)} %get-tuple-element.31), channel_id=1, source_target_pairs={{0,4},{1,5},{4,8},{5,9},{8,12},{9,13},{12,14},{13,15},{14,10},{15,... | collective-permute-start | bytes 442376 | tf_op jit(solution)/shard_map/ppermute | solution.py:55
  18.9 8.5 %collective-permute-start.7 = (bf16[32,2304]{1,0:T(8,128)(2,1)S(1)}, bf16[32,2304]{1,0:T(8,128)(2,1)S(1)}, u32[]{:S(2)}, u32[]{:S(2)}) collective-permute-start(bf16[32,2304]{1,0:T(8,128)(2,1)S(1)} %get-tuple-element.32), channel_id=1, source_target_pairs={{0,4},{1,5},{4,8},{5,9},{8,12},{9,13},{12,14},{13,15},{14,10},{15,... | collective-permute-start | bytes 442376 | tf_op jit(solution)/shard_map/ppermute | solution.py:55
  19.2 9.2 %collective-permute-start.8 = (bf16[32,2304]{1,0:T(8,128)(2,1)S(1)}, bf16[32,2304]{1,0:T(8,128)(2,1)S(1)}, u32[]{:S(2)}, u32[]{:S(2)}) collective-permute-start(bf16[32,2304]{1,0:T(8,128)(2,1)S(1)} %get-tuple-element.33), channel_id=1, source_target_pairs={{0,2},{1,3},{4,0},{5,1},{8,4},{9,5},{12,8},{13,9},{14,12},{15,13},... | collective-permute-start | bytes 442376 | tf_op jit(solution)/shard_map/ppermute | solution.py:55
  20.9 8.5 %collective-permute-start.9 = (bf16[32,2304]{1,0:T(8,128)(2,1)S(1)}, bf16[32,2304]{1,0:T(8,128)(2,1)S(1)}, u32[]{:S(2)}, u32[]{:S(2)}) collective-permute-start(bf16[32,2304]{1,0:T(8,128)(2,1)S(1)} %get-tuple-element.34), channel_id=1, source_target_pairs={{0,2},{1,3},{4,0},{5,1},{8,4},{9,5},{12,8},{13,9},{14,12},{15,13},... | collective-permute-start | bytes 442376 | tf_op jit(solution)/shard_map/ppermute | solution.py:55
  25.1 10.7 %collective-permute-start.10 = (bf16[32,2304]{1,0:T(8,128)(2,1)S(1)}, bf16[32,2304]{1,0:T(8,128)(2,1)S(1)}, u32[]{:S(2)}, u32[]{:S(2)}) collective-permute-start(bf16[32,2304]{1,0:T(8,128)(2,1)S(1)} %collective-permute-done.6.refs_0_), channel_id=1, source_target_pairs={{0,4},{1,5},{4,8},{5,9},{8,12},{9,13},{12,14},{13,15},{14,10},{15,... | collective-permute-start | bytes 442376 | tf_op jit(solution)/shard_map/ppermute | solution.py:55
  27.4 8.5 %collective-permute-start.11 = (bf16[32,2304]{1,0:T(8,128)(2,1)S(1)}, bf16[32,2304]{1,0:T(8,128)(2,1)S(1)}, u32[]{:S(2)}, u32[]{:S(2)}) collective-permute-start(bf16[32,2304]{1,0:T(8,128)(2,1)S(1)} %collective-permute-done.7.refs_1_), channel_id=1, source_target_pairs={{0,4},{1,5},{4,8},{5,9},{8,12},{9,13},{12,14},{13,15},{14,10},{15,... | collective-permute-start | bytes 442376 | tf_op jit(solution)/shard_map/ppermute | solution.py:55
  28.4 7.5 %collective-permute-start.12 = (bf16[32,2304]{1,0:T(8,128)(2,1)S(1)}, bf16[32,2304]{1,0:T(8,128)(2,1)S(1)}, u32[]{:S(2)}, u32[]{:S(2)}) collective-permute-start(bf16[32,2304]{1,0:T(8,128)(2,1)S(1)} %collective-permute-done.8.refs_2_), channel_id=1, source_target_pairs={{0,2},{1,3},{4,0},{5,1},{8,4},{9,5},{12,8},{13,9},{14,12},{15,13},... | collective-permute-start | bytes 442376 | tf_op jit(solution)/shard_map/ppermute | solution.py:55
  29.4 7.2 %collective-permute-start.13 = (bf16[32,2304]{1,0:T(8,128)(2,1)S(1)}, bf16[32,2304]{1,0:T(8,128)(2,1)S(1)}, u32[]{:S(2)}, u32[]{:S(2)}) collective-permute-start(bf16[32,2304]{1,0:T(8,128)(2,1)S(1)} %collective-permute-done.9.refs_3_), channel_id=1, source_target_pairs={{0,2},{1,3},{4,0},{5,1},{8,4},{9,5},{12,8},{13,9},{14,12},{15,13},... | collective-permute-start | bytes 442376 | tf_op jit(solution)/shard_map/ppermute | solution.py:55
  30.6 5.2 %collective-permute-start.14 = (bf16[128,128]{1,0:T(8,128)(2,1)S(1)}, bf16[128,128]{1,0:T(8,128)(2,1)S(1)}, u32[]{:S(2)}, u32[]{:S(2)}) collective-permute-start(bf16[128,128]{1,0:T(8,128)(2,1)S(1)} %get-tuple-element.35.refs_4_), channel_id=1, source_target_pairs={{0,2},{1,3},{2,0},{3,1},{4,6},{5,7},{6,4},{7,5},{8,10},{9,11},{10,... | collective-permute-start | bytes 98312 | tf_op jit(solution)/shard_map/ppermute | solution.py:491
  36.7 6.3 %collective-permute-start.15 = (bf16[256,2304]{1,0:T(8,128)(2,1)S(1)}, bf16[256,2304]{1,0:T(8,128)(2,1)S(1)}, u32[]{:S(2)}, u32[]{:S(2)}) collective-permute-start(bf16[256,2304]{1,0:T(8,128)(2,1)S(1)} %get-tuple-element.39.refs_3_), channel_id=1, source_target_pairs={{0,1},{1,0},{2,3},{3,2},{4,5},{5,4},{6,7},{7,6},{8,9},{9,8},{10,11... | collective-permute-start | bytes 3538952 | tf_op jit(solution)/shard_map/ppermute | solution.py:22
  36.7 9.2 %collective-permute-start.16 = (bf16[64,2304]{1,0:T(8,128)(2,1)S(1)}, bf16[64,2304]{1,0:T(8,128)(2,1)S(1)}, u32[]{:S(2)}, u32[]{:S(2)}) collective-permute-start(bf16[64,2304]{1,0:T(8,128)(2,1)S(1)} %get-tuple-element.43), channel_id=1, source_target_pairs={{0,4},{1,3},{4,8},{5,1},{8,12},{9,5},{12,14},{13,9},{14,10},{15,13... | collective-permute-start | bytes 884744 | tf_op jit(solution)/shard_map/ppermute | solution.py:511
  37.1 8.8 %collective-permute-start.19 = (bf16[128,128]{1,0:T(8,128)(2,1)S(1)}, bf16[128,128]{1,0:T(8,128)(2,1)S(1)}, u32[]{:S(2)}, u32[]{:S(2)}) collective-permute-start(bf16[128,128]{1,0:T(8,128)(2,1)S(1)} %get-tuple-element.38.refs_5_), channel_id=1, source_target_pairs={{0,4},{1,5},{2,6},{3,7},{4,8},{5,9},{6,10},{7,11},{8,12},{9,13},{1... | collective-permute-start | bytes 98312 | tf_op jit(solution)/shard_map/ppermute | solution.py:507
  38.4 7.5 %collective-permute-start.18 = (bf16[128,128]{1,0:T(8,128)(2,1)S(1)}, bf16[128,128]{1,0:T(8,128)(2,1)S(1)}, u32[]{:S(2)}, u32[]{:S(2)}) collective-permute-start(bf16[128,128]{1,0:T(8,128)(2,1)S(1)} %get-tuple-element.38.refs_5_), channel_id=1, source_target_pairs={{0,8},{1,9},{2,10},{3,11},{4,12},{5,13},{6,14},{7,15},{8,0},{9,1},... | collective-permute-start | bytes 98312 | tf_op jit(solution)/shard_map/ppermute | solution.py:507
  40.1 5.8 %collective-permute-start.17 = (bf16[128,128]{1,0:T(8,128)(2,1)S(1)}, bf16[128,128]{1,0:T(8,128)(2,1)S(1)}, u32[]{:S(2)}, u32[]{:S(2)}) collective-permute-start(bf16[128,128]{1,0:T(8,128)(2,1)S(1)} %get-tuple-element.38.refs_5_), channel_id=1, source_target_pairs={{0,12},{1,13},{2,14},{3,15},{4,0},{5,1},{6,2},{7,3},{8,4},{9,5},{1... | collective-permute-start | bytes 98312 | tf_op jit(solution)/shard_map/ppermute | solution.py:507
  46.0 1.7 %collective-permute-start.20 = (bf16[64,2304]{1,0:T(8,128)(2,1)S(1)}, bf16[64,2304]{1,0:T(8,128)(2,1)S(1)}, u32[]{:S(2)}, u32[]{:S(2)}) collective-permute-start(bf16[64,2304]{1,0:T(8,128)(2,1)S(1)} %shard_map.75.refs_4_), channel_id=1, source_target_pairs={{0,1},{1,0},{2,3},{3,2},{4,5},{5,4},{6,7},{7,6},{8,9},{9,8},{10,11... | collective-permute-start | bytes 884744 | tf_op jit(solution)/shard_map/ppermute | solution.py:22
  46.1 1.6 %collective-permute-start.21 = (bf16[128,128]{1,0:T(8,128)(2,1)S(1)}, bf16[128,128]{1,0:T(8,128)(2,1)S(1)}, u32[]{:S(2)}, u32[]{:S(2)}) collective-permute-start(bf16[128,128]{1,0:T(8,128)(2,1)S(1)} %get-tuple-element.45.refs_1_), channel_id=1, source_target_pairs={{0,1},{1,0},{2,3},{3,2},{4,5},{5,4},{6,7},{7,6},{8,9},{9,8},{10,11... | collective-permute-start | bytes 98312 | tf_op jit(solution)/shard_map/ppermute | solution.py:22
  (3 other events, 9.5 us)
